TPU v7x, 32 devices: a whole 2x2x4 slice. The times are simulated.
32 devices in a mesh: walk: 2 (over x), chol: 16 (over z, y, core).
Axes of the slice: x: 2, y: 2, z: 4, core: 2. Of those that a mesh axis runs over, the one named last changes fastest.
Arguments:
- walkers: bfloat16 [16, 2048, 256], P('walk', 'chol'), may hold values from -2.5 to 2.5
- trial: bfloat16 [2048, 256], P('chol'), may hold values from -1.05 to 1.05
- cholesky: bfloat16 [32, 2048, 2048], P(None, 'chol'), may hold values from -0.125 to 0.125
- rotated: bfloat16 [32, 2048, 256], P(None, 'chol'), may hold values from -0.09375 to 0.09375
- fields: float32 [16, 32], P('walk'), may hold values from -4 to 4
- source: int32 [16], replicated, may hold values from 0 to 15, as said below
Outputs:
- propagated: bfloat16 [16, 2048, 256], P('walk', 'chol')
- force_bias: float32 [16, 32], P('walk')
Inputs may be any that keep to these rules, and one draw needn't show every extreme that they name: source is a permutation of the walkers. New slots g * 8 to (g + 1) * 8 - 1 form group g, as do the old walkers. Of the old walkers of one group at most 4 fill slots of any one new group, and in every draw some group sends exactly 4 to some group.
All inputs are finite; a program needn't handle non-finite values.
Results may differ from a plain program's by a relative error of at most 0.0051.
Values may be sent and summed in bfloat16 or wider, within the bound.
No kernel may reach another device: no remote copies, remote signals or barrier semaphores. Data moves between devices by JAX's collectives and lax.ppermute only.
A program may use at most 128 MiB of HBM per device.

v0:
```python
import jax
import jax.numpy as jnp
from jax import lax
from jax.sharding import PartitionSpec as P

ITERS = 3


TAU_ROOT = 0.1


def newton_inverse(intersections):
    identity = jnp.eye(intersections.shape[-1], dtype=jnp.float32)
    estimate = jnp.broadcast_to(identity, intersections.shape)
    for sweep_index in range(ITERS):
        product = jnp.einsum(
            "wij,wjk->wik", intersections, estimate, precision=lax.Precision.HIGHEST
        )
        estimate = jnp.einsum(
            "wij,wjk->wik", estimate, 2.0 * identity - product, precision=lax.Precision.HIGHEST
        )
    return estimate


def column_fold(potential, shard_piece):
    return jnp.einsum("wpq,wqi->wpi", potential, shard_piece, preferred_element_type=jnp.float32)


def shards(walkers, trial, cholesky, rotated, fields, source):
    per_group = walkers.shape[0]
    row_count = walkers.shape[1]
    electrons = walkers.shape[2]
    group_index = lax.axis_index("walk")
    group_count = lax.axis_size("walk")
    capacity = per_group // 2
    anchor = (source // per_group).reshape(group_count, per_group)
    local_slot = (source % per_group).reshape(group_count, per_group)
    from_here = (anchor == group_index).astype(jnp.int32)
    before = jnp.cumsum(from_here, axis=1) - from_here
    slot_match = (from_here[:, None, :] == 1) & (
        before[:, None, :] == jnp.arange(capacity)[None, :, None]
    )
    picked = jnp.sum(jnp.where(slot_match, local_slot[:, None, :], 0), axis=2)
    filled = jnp.any(slot_match, axis=2)
    outgoing = jnp.take(walkers, picked.reshape(-1), axis=0).reshape(
        group_count, capacity, row_count, electrons
    )
    outgoing = jnp.where(filled[:, :, None, None], outgoing, jnp.zeros_like(outgoing))
    arrived = lax.all_to_all(outgoing, "walk", split_axis=0, concat_axis=0, tiled=True)
    arrived = arrived.reshape(group_count * capacity, row_count, electrons)
    incoming_groups = (
        lax.dynamic_slice_in_dim(source, group_index * per_group, per_group) // per_group
    )
    positions = jnp.arange(per_group)
    same_anchor = (incoming_groups[:, None] == incoming_groups[None, :]) & (
        positions[None, :] < positions[:, None]
    )
    order_rank = jnp.sum(same_anchor.astype(jnp.int32), axis=1)
    migrated = jnp.take(arrived, incoming_groups * capacity + order_rank, axis=0)
    partial_intersection = jnp.einsum(
        "pi,wpj->wij", trial, migrated, preferred_element_type=jnp.float32
    )
    intersections = lax.psum(partial_intersection, "chol")
    inverse = newton_inverse(intersections).astype(jnp.bfloat16)
    greens = jnp.einsum(
        "wpj,wji->wpi", migrated, inverse, preferred_element_type=jnp.float32
    ).astype(jnp.bfloat16)
    vectors = rotated.shape[0]
    partial_bias = lax.dot_general(
        greens.reshape(per_group, -1),
        rotated.reshape(vectors, -1),
        (((1,), (1,)), ((), ())),
        preferred_element_type=jnp.float32,
    )
    force_bias = TAU_ROOT * lax.psum(partial_bias, "chol")
    shifted = (fields - force_bias).astype(jnp.bfloat16)
    potential = (
        TAU_ROOT
        * jnp.dot(shifted, cholesky.reshape(vectors, -1), preferred_element_type=jnp.float32)
    ).astype(jnp.bfloat16)
    potential = potential.reshape(per_group, row_count, -1)
    first_term = column_fold(potential, lax.all_gather(migrated, "chol", axis=1, tiled=True))
    second_term = column_fold(
        potential, lax.all_gather(first_term.astype(jnp.bfloat16), "chol", axis=1, tiled=True)
    )
    propagated = (migrated.astype(jnp.float32) + first_term + 0.5 * second_term).astype(
        jnp.bfloat16
    )
    return (propagated, force_bias)


def solution(mesh):
    in_specs = (
        P("walk", "chol", None),
        P("chol", None),
        P(None, "chol", None),
        P(None, "chol", None),
        P("walk", None),
        P(),
    )
    out_specs = (P("walk", "chol", None), P("walk", None))
    return jax.shard_map(shards, mesh=mesh, in_specs=in_specs, out_specs=out_specs, check_vma=False)
```

profile of v0, /device:TPU:0, one launch (start us, length us, event | category | flops | bytes accessed | tf_op | source)
XLA Modules:
  0.0 300.7 jit_solution(4115162217148224863)
XLA Ops:
  7.2 0.0 copy-start
  7.2 0.8 and_select_fusion.1
  8.0 0.7 compare_convert_fusion
  8.7 0.1 reshape.71
  8.8 0.2 reduce_window_sum.11
  8.9 0.1 broadcast_in_dim.51
  9.0 0.1 select_reduce_fusion
  9.2 0.1 reshape.66
  9.3 0.1 fusion.39
  9.4 0.0 copy-start.8
  9.5 1.6 gather_fusion
  11.1 0.1 broadcast_select_fusion.1
  11.2 0.0 copy-start.5
  11.2 0.9 broadcast_select_fusion.2
  12.1 4.2 %all-to-all-start = ((bf16[2,4,128,256]{3,2,1,0:T(8,128)(2,1)}), bf16[2,4,128,256]{3,2,1,0:T(8,128)(2,1)S(1)}, u32[]{:S(2)}, u32[]{:S(2)}) async-start(bf16[2,4,128,256]{3,2,1,0:T(8,128)(2,1)} %broadcast_select_fusion.2), calls=%async_computation | async-start | bytes 1048576 | tf_op jit(solution)/shard_map/all_to_all | solution.py:49
  16.3 0.0 all-reduce.2.cloned.1.call-start
  16.3 0.0 copy-done.8
  16.3 0.1 and_select_fusion
  16.4 0.2 convert_reduce_fusion
  16.6 0.1 compare_and_fusion
  16.7 8.4 %all-to-all-done = bf16[2,4,128,256]{3,2,1,0:T(8,128)(2,1)S(1)} async-done(((bf16[2,4,128,256]{3,2,1,0:T(8,128)(2,1)}), bf16[2,4,128,256]{3,2,1,0:T(8,128)(2,1)S(1)}, u32[]{:S(2)}, u32[]{:S(2)}) %all-to-all-start) | async-done | bytes 524320 | tf_op jit(solution)/shard_map/all_to_all | solution.py:49
  25.1 0.6 gather_fusion.1
  25.6 0.1 broadcast_select_fusion
  25.8 0.0 copy-start.3
  25.8 0.0 copy-done.5
  25.8 1.8 convolution_bitcast_fusion
  27.6 0.0 all-reduce.2.cloned.1.call-update
  27.6 0.0 copy-done.3
  27.6 0.0 all-gather.3.cloned.1.call-start
  27.6 0.7 all-gather.3.cloned.1.call-update
  28.3 0.0 all-gather.5.cloned.1.call-start
  28.4 18.7 %copy.18 = bf16[4,8,128,2048]{3,1,2,0:T(8,128)(2,1)} copy(bf16[4,8,128,2048]{3,2,1,0:T(8,128)(2,1)} %bitcast.26) | data formatting | bytes 33554432
  47.2 79.0 %all-reduce.2.cloned.1.call-done = f32[8,256,256]{1,2,0:T(8,128)} async-done(((f32[8,256,256]{1,2,0:T(8,128)}), f32[8,256,256]{1,2,0:T(8,128)}) %all-reduce.2.cloned.1.call-update) | async-done | bytes 2097168 | tf_op jit(solution)/shard_map/psum | solution.py:63
  126.1 5.1 %fusion.32 = f32[8,256,256]{2,1,0:T(8,128)S(1)} fusion(f32[8,256,256]{1,2,0:T(8,128)} %all-reduce.2.cloned.1.call-done, f32[256,256]{1,0:T(8,128)S(1)} %fusion.35), kind=kOutput, calls=%fused_computation.27 | convolution fusion | flops 1610612736 | bytes 4456448 | tf_op jit(solution)/shard_map/wij,wjk->wik/dot_general | solution.py:16
  131.2 0.0 copy-start.2
  131.2 1.9 fusion.11
  133.2 0.0 copy-done.2
  133.2 3.6 %fusion.41 = f32[8,256,256]{2,1,0:T(8,128)S(1)} fusion(f32[8,256,256]{1,2,0:T(8,128)S(1)} %copy-done.2, f32[8,256,256]{2,1,0:T(8,128)S(1)} %fusion.11), kind=kOutput, calls=%fused_computation.63 | convolution fusion | flops 1610612736 | bytes 6291456 | tf_op jit(solution)/shard_map/wij,wjk->wik/dot_general | solution.py:16
  136.8 2.3 fusion.9
  139.1 3.8 %fusion.42 = f32[8,256,256]{2,1,0:T(8,128)S(1)} fusion(f32[8,256,256]{1,2,0:T(8,128)S(1)} %copy-done.2, f32[8,256,256]{2,1,0:T(8,128)S(1)} %fusion.9), kind=kOutput, calls=%fused_computation.64 | convolution fusion | flops 1610612736 | bytes 6291456 | tf_op jit(solution)/shard_map/wij,wjk->wik/dot_general | solution.py:16
  142.9 0.0 copy-start.4
  142.9 2.2 fusion.13
  145.1 0.0 copy-done.4
  145.1 0.0 copy-start.7
  145.1 0.3 fusion.43
  145.5 0.0 copy-done
  145.5 1.5 fusion.25
  146.9 31.6 %psum.15 = f32[8,32]{1,0:T(8,128)S(1)} all-reduce(f32[8,32]{1,0:T(8,128)S(1)} %fusion.25), channel_id=1, replica_groups=mesh['walk'=2,'chol'=16] {'chol'}, use_global_device_ids=true, to_apply=%region_5.7 | all-reduce | flops 256 | bytes 2048 | tf_op jit(solution)/shard_map/psum | solution.py:75
  178.6 0.0 copy-start.6
  178.6 0.0 copy-done.7
  178.6 10.1 %fusion = bf16[8,262144]{1,0:T(8,128)(2,1)} fusion(bf16[32,262144]{1,0:T(8,128)(2,1)} %bitcast.25, f32[8,32]{1,0:T(8,128)S(1)} %copy-done.7, f32[8,32]{1,0:T(8,128)S(1)} %broadcast_multiply_fusion), kind=kOutput, calls=%fused_computation.3 | convolution fusion | flops 138412544 | bytes 20973568 | tf_op jit(solution)/shard_map/dot_general | solution.py:79
  188.7 0.0 copy-done.6
  188.7 14.9 %all-gather.3.cloned.1.call-done = bf16[8,2048,256]{2,1,0:T(8,128)(2,1)} async-done(((bf16[8,128,256]{2,1,0:T(8,128)(2,1)}), bf16[8,2048,256]{2,1,0:T(8,128)(2,1)}) %all-gather.3.cloned.1.call-update) | async-done | bytes 8388624 | tf_op jit(solution)/shard_map/all_gather | solution.py:82
  203.6 8.6 %fusion.40 = (bf16[8,128,256]{2,1,0:T(8,128)(2,1)}, f32[8,128,256]{2,1,0:T(8,128)}) fusion(bf16[8,2048,256]{2,1,0:T(8,128)(2,1)} %all-gather.3.cloned.1.call-done, bf16[8,128,2048]{2,0,1:T(8,128)(2,1)} %bitcast.27), kind=kOutput, calls=%fused_computation.62 | convolution fusion | flops 1074003968 | bytes 14155776 | tf_op jit(solution)/shard_map/wpq,wqi->wpi/dot_general | solution.py:26
  212.2 0.0 all-gather.5.cloned.1.call-update
  212.2 73.3 %all-gather.5.cloned.1.call-done = bf16[8,2048,256]{2,1,0:T(8,128)(2,1)} async-done(((bf16[8,128,256]{2,1,0:T(8,128)(2,1)}), bf16[8,2048,256]{2,1,0:T(8,128)(2,1)}) %all-gather.5.cloned.1.call-update) | async-done | bytes 8388624 | tf_op jit(solution)/shard_map/all_gather | solution.py:84
  285.6 0.0 copy-start.1
  285.6 8.6 %fusion.22 = bf16[8,128,256]{2,1,0:T(8,128)(2,1)} fusion(bf16[8,2048,256]{2,1,0:T(8,128)(2,1)} %all-gather.5.cloned.1.call-done, bf16[8,128,2048]{2,0,1:T(8,128)(2,1)} %bitcast.28, f32[8,128,256]{2,1,0:T(8,128)} %get-tuple-element.6, bf16[8,128,256]{2,1,0:T(8,128)(2,1)S(1)} %copy-done.4), kind=kOutput, calls=%fused_computation.20 | convolution fusion | flops 1075052544 | bytes 14680064 | tf_op jit(solution)/shard_map/wpq,wqi->wpi/dot_general | solution.py:26
  294.1 0.0 copy-done.1
  (9 shorter events, 0.1 us)
Async XLA Ops:
  7.2 138.3 %copy-start = (bf16[32,128,256]{2,1,0:T(8,128)(2,1)S(1)}, bf16[32,128,256]{2,1,0:T(8,128)(2,1)}, u32[]{:S(2)}) copy-start(bf16[32,128,256]{2,1,0:T(8,128)(2,1)} %param.11) | copy-start | bytes 6291460
  9.4 6.9 %copy-start.8 = (s32[16]{0:T(128)S(1)}, s32[16]{0:T(128)}, u32[]{:S(2)}) copy-start(s32[16]{0:T(128)} %param.13) | copy-start | bytes 196
  11.2 14.6 %copy-start.5 = (bf16[128,256]{1,0:T(8,128)(2,1)S(1)}, bf16[128,256]{1,0:T(8,128)(2,1)}, u32[]{:S(2)}) copy-start(bf16[128,256]{1,0:T(8,128)(2,1)} %param.9) | copy-start | bytes 196612
  12.1 12.9 %all-to-all-start = ((bf16[2,4,128,256]{3,2,1,0:T(8,128)(2,1)}), bf16[2,4,128,256]{3,2,1,0:T(8,128)(2,1)S(1)}, u32[]{:S(2)}, u32[]{:S(2)}) async-start(bf16[2,4,128,256]{3,2,1,0:T(8,128)(2,1)} %broadcast_select_fusion.2), calls=%async_computation | async-start | bytes 1048576 | tf_op jit(solution)/shard_map/all_to_all | solution.py:49
  16.3 109.8 %all-reduce.2.cloned.1.call-start = ((), (), s32[]{:S(2)}) async-start(), calls=%async_computation.1 | async-start | bytes 4194304 | tf_op jit(solution)/shard_map/psum | solution.py:63
  25.8 1.8 copy-start.3
  27.6 176.0 %all-gather.3.cloned.1.call-start = ((), (), s32[]{:S(2)}) async-start(), calls=%async_computation.2 | async-start | bytes 8912896 | tf_op jit(solution)/shard_map/all_gather | solution.py:82
  28.3 257.2 %all-gather.5.cloned.1.call-start = ((), (), s32[]{:S(2)}) async-start(), calls=%async_computation.3 | async-start | bytes 8912896 | tf_op jit(solution)/shard_map/all_gather | solution.py:84
  131.2 1.9 copy-start.2
  142.9 2.2 copy-start.4
  145.1 33.5 %copy-start.7 = (f32[8,32]{1,0:T(8,128)S(1)}, f32[8,32]{1,0:T(8,128)}, u32[]{:S(2)}) copy-start(f32[8,32]{1,0:T(8,128)} %param.12) | copy-start | bytes 3076
  178.6 10.1 %copy-start.6 = (f32[8,32]{1,0:T(8,128)}, f32[8,32]{1,0:T(8,128)S(1)}, u32[]{:S(2)}) copy-start(f32[8,32]{1,0:T(8,128)S(1)} %broadcast_multiply_fusion) | copy-start | bytes 3076
  285.6 8.6 %copy-start.1 = (bf16[32,128,256]{2,1,0:T(8,128)(2,1)S(1)}, bf16[32,128,256]{2,1,0:T(8,128)(2,1)}, u32[]{:S(2)}) copy-start(bf16[32,128,256]{2,1,0:T(8,128)(2,1)} %param.11) | copy-start | bytes 6291460
Sparse Core Ops, SparseCore 0:
  27.7 98.3 all-reduce.1
  129.1 74.4 all-gather.2
  212.4 73.1 all-gather.4
where the time goes:
time: 301 us
  waiting for transfers between devices  176 us (58%)
  matrix products  49.7 us (17%)
  blocking collectives  31.6 us (10%)
  local copies, waits for them, and re-layouts  21.2 us (7%)
  between operations  14 us (5%)
  starting transfers between devices  4.29 us (1%)
  other arithmetic  3.52 us (1%)
    psum x1, waiting for transfers between devices, shards(): intersections = lax.psum(partial_intersection, 'chol')  79 us
    all_gather x1, waiting for transfers between devices, shards(): lax.all_gather(first_term.astype(jnp.bfloat16), 'chol', axis=1, tiled=True)  73.3 us
    psum x1, blocking collectives, shards(): force_bias = TAU_ROOT * lax.psum(partial_bias, 'chol')  31.6 us
    unnamed x19, local copies, waits for them, and re-layouts  18.8 us
    dot_general x2, matrix products, column_fold(): jnp.einsum('wpq,wqi->wpi', potential, shard_piece, preferred_element_type...  17.2 us
    all_gather x1, waiting for transfers between devices, shards(): lax.all_gather(migrated, 'chol', axis=1, tiled=True)  14.9 us
    dot_general x3, matrix products, newton_inverse(): jnp.einsum('wij,wjk->wik', intersections, estimate, precision=lax.Precisi...  12.5 us
    dot_general x1, matrix products, shards(): jnp.dot(shifted, cholesky.reshape(vectors, -1), preferred_element_type=jn...  10.1 us
  transfers between devices with their start and end apart: 4, of which 4 were waited for; matrix products, arithmetic and copies ran while one was open for 17% of the time, Pallas kernels for 0%

commit v1 on v0

v1 whole, which is shorter than its diff:
```python
import functools

import jax
import jax.numpy as jnp
from jax import lax
from jax.experimental import pallas as pl
from jax.experimental.pallas import tpu as pltpu
from jax.sharding import PartitionSpec as P

ITERS = 3
TAU_ROOT = 0.1
BLOCK = 16
HIGHEST = lax.Precision.HIGHEST
VMEM_LIMIT = 48 * 1024 * 1024

F32 = jnp.float32
BF16 = jnp.bfloat16


def params(limit=VMEM_LIMIT):
    return pltpu.CompilerParams(vmem_limit_bytes=limit)


def vmem_specs(count):
    return [pl.BlockSpec(memory_space=pltpu.VMEM)] * count


class Layout:
    def __init__(self, walk_size, chol_size):
        self.walk = walk_size
        self.chol = chol_size
        self.z = chol_size // 4

    def shift(self, array, dz=0, dy=0, db=0):
        pairs = []
        for index in range(self.chol):
            z, y, b = index // 4, (index // 2) % 2, index % 2
            target = (((z + dz) % self.z) * 2 + (y ^ dy)) * 2 + (b ^ db)
            pairs.append((index, target))
        return lax.ppermute(array, "chol", pairs)

    def shift_all(self, array, dw=0, dy=0, db=0):
        pairs = []
        for group in range(self.walk):
            for index in range(self.chol):
                z, y, b = index // 4, (index // 2) % 2, index % 2
                target = (z * 2 + (y ^ dy)) * 2 + (b ^ db)
                pairs.append(
                    (group * self.chol + index, ((group + dw) % self.walk) * self.chol + target)
                )
        return lax.ppermute(array, ("walk", "chol"), pairs)

    def gather(self, piece):
        along_z = [piece]
        for _ in range(self.z - 1):
            along_z.append(self.shift(along_z[-1], dz=1))
        chips = []
        for dz, array in enumerate(along_z):
            chips.append((array, dz, 0))
            chips.append((self.shift(array, dy=1), dz, 1))
        pieces = []
        for array, dz, dy in chips:
            pieces.append((array, dz, dy, 0))
            pieces.append((self.shift(array, db=1), dz, dy, 1))
        return pieces


def intersection_kernel(places, mine, theirs, trial_mine, trial_theirs, *outs):
    count = mine.shape[0]
    first = trial_mine[...].T
    second = trial_theirs[...].T
    z = lax.rem(lax.axis_index("chol") // 4, count)
    for step in range(count):
        walker = lax.rem(z + step, count) if places else step
        total = jnp.dot(first, mine[walker], preferred_element_type=F32)
        total += jnp.dot(second, theirs[walker], preferred_element_type=F32)
        outs[step][...] = total.astype(outs[step].dtype)


def intersections_of(mine, theirs, trial_mine, trial_theirs, places):
    count, _, electrons = mine.shape
    kinds = [F32] + [BF16 if places else F32] * (count - 1)
    return pl.pallas_call(
        functools.partial(intersection_kernel, places),
        out_shape=[jax.ShapeDtypeStruct((electrons, electrons), kind) for kind in kinds],
        in_specs=vmem_specs(4),
        out_specs=vmem_specs(count),
        compiler_params=params(),
    )(mine, theirs, trial_mine, trial_theirs)


def newton_kernel(*refs):
    parts, out = refs[:-1], refs[-1]
    matrix = parts[0][...]
    for part in parts[1:]:
        matrix = matrix + part[...].astype(F32)
    shape = matrix.shape
    twice = jnp.where(
        lax.broadcasted_iota(jnp.int32, shape, 0) == lax.broadcasted_iota(jnp.int32, shape, 1),
        2.0,
        0.0,
    ).astype(F32)
    estimate = twice - matrix
    for _ in range(ITERS - 1):
        product = jnp.dot(matrix, estimate, precision=HIGHEST, preferred_element_type=F32)
        estimate = jnp.dot(
            estimate, twice - product, precision=HIGHEST, preferred_element_type=F32
        )
    out[...] = estimate.astype(out.dtype)


def newton_of(parts):
    return pl.pallas_call(
        newton_kernel,
        out_shape=jax.ShapeDtypeStruct(parts[0].shape, BF16),
        in_specs=vmem_specs(len(parts)),
        out_specs=pl.BlockSpec(memory_space=pltpu.VMEM),
        compiler_params=params(),
    )(*parts)


def bias_kernel(places, count, mine, theirs, rot_mine, rot_theirs, *refs):
    inverses, out, total = refs[:count], refs[count], refs[count + 1]
    step = pl.program_id(0)
    z = lax.axis_index("chol") // 4

    @pl.when(step == 0)
    def _():
        total[...] = jnp.zeros_like(total)

    rows, electrons = mine.shape[1], mine.shape[2]
    vectors = rot_mine.shape[0]
    both = []
    for index in range(count):
        walker = lax.rem(z + (count - index), count) if places else index
        walker_rows = jnp.concatenate([mine[walker], theirs[walker]], axis=0)
        both.append(
            jnp.dot(walker_rows, inverses[index][...], preferred_element_type=F32).astype(BF16)
        )
    for half, rot in enumerate((rot_mine, rot_theirs)):
        greens = jnp.concatenate([g[half * rows : (half + 1) * rows] for g in both], axis=0)
        total[...] += lax.dot_general(
            greens,
            rot[...].reshape(vectors * rows, electrons),
            (((1,), (1,)), ((), ())),
            preferred_element_type=F32,
        )

    @pl.when(step == pl.num_programs(0) - 1)
    def _():
        shape = total.shape
        same = lax.rem(lax.broadcasted_iota(jnp.int32, shape, 0), rows) == lax.rem(
            lax.broadcasted_iota(jnp.int32, shape, 1), rows
        )
        kept = jnp.where(same, total[...], 0.0)
        summed = jnp.sum(kept.reshape(count, rows, shape[1]), axis=1)
        wide = (vectors * rows, vectors)
        pick = (
            lax.broadcasted_iota(jnp.int32, wide, 0) // rows
            == lax.broadcasted_iota(jnp.int32, wide, 1)
        ).astype(F32)
        result = jnp.dot(summed, pick, precision=HIGHEST, preferred_element_type=F32)
        row = lax.broadcasted_iota(jnp.int32, (count, 1), 0)
        ordered = jnp.zeros_like(result)
        for index in range(count):
            walker = lax.rem(z + (count - index), count) if places else index
            ordered += jnp.where(row == walker, result[index : index + 1], 0.0)
        out[...] = ordered


def bias_of(mine, theirs, rot_mine, rot_theirs, inverses, places):
    count, rows, electrons = mine.shape
    vectors = rot_mine.shape[0]
    walker_spec = pl.BlockSpec((count, BLOCK, electrons), lambda step: (0, step, 0))
    rot_spec = pl.BlockSpec((vectors, BLOCK, electrons), lambda step: (0, step, 0))
    whole = pl.BlockSpec((electrons, electrons), lambda step: (0, 0))
    return pl.pallas_call(
        functools.partial(bias_kernel, places, count),
        grid=(rows // BLOCK,),
        out_shape=jax.ShapeDtypeStruct((count, vectors), F32),
        in_specs=[walker_spec, walker_spec, rot_spec, rot_spec] + [whole] * count,
        out_specs=pl.BlockSpec((count, vectors), lambda step: (0, 0)),
        scratch_shapes=[pltpu.VMEM((count * BLOCK, vectors * BLOCK), F32)],
        compiler_params=params(),
        cost_estimate=pl.CostEstimate(
            flops=4 * count * rows * electrons * (electrons + vectors * BLOCK),
            bytes_accessed=4 * (vectors + count) * rows * electrons,
            transcendentals=0,
        ),
    )(mine, theirs, rot_mine, rot_theirs, *inverses)


def potential_kernel(origins, layout, fields, source, position, *refs):
    pieces = refs[: len(origins)]
    cholesky, bias_out, potential, weights = refs[len(origins) :]
    per_group, vectors = fields.shape
    half = pieces[0].shape[0]
    step = pl.program_id(0)

    @pl.when(step == 0)
    def _():
        group = lax.axis_index("walk")
        b = lax.rem(lax.axis_index("chol"), 2)
        wanted = source[...]
        bias = jnp.zeros((per_group, vectors), F32)
        for (dw, db), piece in zip(origins, pieces):
            from_group = lax.rem(group + (layout.walk - dw), layout.walk)
            from_b = b + db - 2 * b * db
            base = from_group * per_group + from_b * half
            for row in range(half):
                bias += jnp.where(wanted == base + row, piece[row : row + 1, :], 0.0)
        bias = TAU_ROOT * bias
        bias_out[...] = bias
        shifted = (fields[...] - bias).astype(BF16)
        tall = (per_group * BLOCK, per_group)
        rows = (
            lax.broadcasted_iota(jnp.int32, tall, 0) // BLOCK == position[...]
        ).astype(BF16)
        wide = (vectors, vectors * BLOCK)
        columns = (
            lax.broadcasted_iota(jnp.int32, wide, 1) // BLOCK
            == lax.broadcasted_iota(jnp.int32, wide, 0)
        ).astype(BF16)
        spread = jnp.dot(rows, shifted, preferred_element_type=F32).astype(BF16)
        spread = jnp.dot(spread, columns, preferred_element_type=F32)
        same = lax.rem(lax.broadcasted_iota(jnp.int32, spread.shape, 0), BLOCK) == lax.rem(
            lax.broadcasted_iota(jnp.int32, spread.shape, 1), BLOCK
        )
        weights[...] = jnp.where(same, spread, 0.0).astype(BF16)

    block = cholesky[...].reshape(vectors * BLOCK, cholesky.shape[2])
    result = TAU_ROOT * jnp.dot(weights[...], block, preferred_element_type=F32)
    potential[...] = result.astype(BF16).reshape(potential.shape)


def potential_of(layout, fields, source, position, pieces, cholesky):
    per_group, vectors = fields.shape
    rows, orbitals = cholesky.shape[1], cholesky.shape[2]
    origins = [origin for origin, _ in pieces]
    arrays = [array for _, array in pieces]

    def whole(array):
        return pl.BlockSpec(array.shape, lambda step: (0, 0))

    return pl.pallas_call(
        functools.partial(potential_kernel, origins, layout),
        grid=(rows // BLOCK,),
        out_shape=[
            jax.ShapeDtypeStruct((per_group, vectors), F32),
            jax.ShapeDtypeStruct((per_group, rows, orbitals), BF16),
        ],
        in_specs=[whole(a) for a in (fields, source, position, *arrays)]
        + [pl.BlockSpec((vectors, BLOCK, orbitals), lambda step: (0, step, 0))],
        out_specs=[
            pl.BlockSpec((per_group, vectors), lambda step: (0, 0)),
            pl.BlockSpec((per_group, BLOCK, orbitals), lambda step: (0, step, 0)),
        ],
        scratch_shapes=[pltpu.VMEM((per_group * BLOCK, vectors * BLOCK), BF16)],
        compiler_params=params(),
        cost_estimate=pl.CostEstimate(
            flops=2 * per_group * vectors * rows * BLOCK * orbitals,
            bytes_accessed=2 * (vectors + per_group) * rows * orbitals,
            transcendentals=0,
        ),
    )(fields, source, position, *arrays, cholesky)


def load_pieces(layout, places, pieces, buffer, semaphores):
    index = lax.axis_index("chol")
    z, y, b = index // 4, lax.rem(index // 2, 2), lax.rem(index, 2)
    rows = pieces[0].shape[1]
    copies = []
    for number, ((dz, dy, db), piece) in enumerate(zip(places, pieces)):
        from_z = lax.rem(z + (layout.z - dz), layout.z)
        from_y = y + dy - 2 * y * dy
        from_b = b + db - 2 * b * db
        owner = (from_z * 2 + from_y) * 2 + from_b
        copies.append(
            pltpu.make_async_copy(
                piece,
                buffer.at[:, pl.ds(pl.multiple_of(owner * rows, rows), rows), :],
                semaphores.at[number],
            )
        )
    return copies


def first_kernel(layout, places, potential, *refs):
    pieces = refs[: len(places)]
    rounded, base, buffer, semaphores = refs[len(places) :]
    step = pl.program_id(0)

    @pl.when(step == 0)
    def _():
        copies = load_pieces(layout, places, pieces, buffer, semaphores)
        for copy in copies:
            copy.start()
        for copy in copies:
            copy.wait()

    rows = base.shape[1]
    own = pl.ds(pl.multiple_of(lax.axis_index("chol") * rows, rows), rows)
    term = jnp.dot(potential[0], buffer[step], preferred_element_type=F32)
    rounded[0] = term.astype(BF16)
    base[0] = buffer[step, own, :].astype(F32) + term


def second_kernel(layout, places, order, potential, base, *refs):
    del order
    pieces = refs[: len(places)]
    out, buffer, semaphores = refs[-3:]
    step = pl.program_id(0)

    @pl.when(step == 0)
    def _():
        copies = load_pieces(layout, places, pieces, buffer, semaphores)
        for copy in copies:
            copy.start()
        for copy in copies:
            copy.wait()

    term = jnp.dot(potential[0], buffer[step], preferred_element_type=F32)
    out[0] = (base[0] + 0.5 * term).astype(BF16)


def fold_cost(count, rows, orbitals, electrons):
    return pl.CostEstimate(
        flops=2 * count * rows * orbitals * electrons,
        bytes_accessed=2 * count * orbitals * (rows + electrons),
        transcendentals=0,
    )


def first_of(layout, part, potential, gathered):
    places = [piece[1:] for piece in gathered]
    arrays = [piece[0] for piece in gathered]
    count, rows, electrons = arrays[0].shape
    orbitals = potential.shape[2]
    out_spec = pl.BlockSpec((1, rows, electrons), lambda step: (step, 0, 0))
    return pl.pallas_call(
        functools.partial(first_kernel, layout, places),
        grid=(count,),
        out_shape=[
            jax.ShapeDtypeStruct((count, rows, electrons), BF16),
            jax.ShapeDtypeStruct((count, rows, electrons), F32),
        ],
        in_specs=[pl.BlockSpec((1, rows, orbitals), lambda step: (part * count + step, 0, 0))]
        + [pl.BlockSpec(memory_space=pl.ANY)] * len(arrays),
        out_specs=[out_spec, out_spec],
        scratch_shapes=[
            pltpu.VMEM((count, orbitals, electrons), BF16),
            pltpu.SemaphoreType.DMA((len(arrays),)),
        ],
        compiler_params=params(),
        cost_estimate=fold_cost(count, rows, orbitals, electrons),
    )(potential, *arrays)


def second_of(layout, part, potential, base, gathered, order, previous):
    places = [piece[1:] for piece in gathered]
    arrays = [piece[0] for piece in gathered]
    count, rows, electrons = arrays[0].shape
    per_group, _, orbitals = potential.shape
    extra = [] if previous is None else [previous]
    inputs = [order, potential, base, *arrays, *extra]
    return pl.pallas_call(
        functools.partial(second_kernel, layout, places),
        out_shape=jax.ShapeDtypeStruct((per_group, rows, electrons), BF16),
        grid_spec=pltpu.PrefetchScalarGridSpec(
            num_scalar_prefetch=1,
            grid=(count,),
            in_specs=[
                pl.BlockSpec((1, rows, orbitals), lambda step, order: (part * count + step, 0, 0)),
                pl.BlockSpec((1, rows, electrons), lambda step, order: (step, 0, 0)),
            ]
            + [pl.BlockSpec(memory_space=pl.ANY)] * (len(arrays) + len(extra)),
            out_specs=pl.BlockSpec(
                (1, rows, electrons), lambda step, order: (order[part * count + step], 0, 0)
            ),
            scratch_shapes=[
                pltpu.VMEM((count, orbitals, electrons), BF16),
                pltpu.SemaphoreType.DMA((len(arrays),)),
            ],
        ),
        input_output_aliases={} if previous is None else {len(inputs) - 1: 0},
        compiler_params=params(),
        cost_estimate=fold_cost(count, rows, orbitals, electrons),
    )(*inputs)


def ranks(flags):
    count = flags.shape[-1]
    before = jnp.arange(count)[None, :] < jnp.arange(count)[:, None]
    return jnp.sum(jnp.where(before & flags[..., None, :], 1, 0), axis=-1)


def migrate(layout, walkers, source):
    per_group = walkers.shape[0]
    half = per_group // 2
    group = lax.axis_index("walk")
    table = source.reshape(layout.walk, per_group)
    incoming = lax.dynamic_index_in_dim(table, group, 0, keepdims=False)
    incoming_groups = incoming // per_group

    def outgoing(distance):
        row = lax.dynamic_index_in_dim(table, (group + distance) % layout.walk, 0, keepdims=False)
        local = row - group * per_group
        here = (local >= 0) & (local < per_group)
        match = here[None, :] & (ranks(here)[None, :] == jnp.arange(half)[:, None])
        return jnp.take(walkers, jnp.sum(jnp.where(match, local[None, :], 0), axis=1), axis=0)

    arrived = []
    for distance in range(layout.walk):
        block = outgoing(distance)
        if distance:
            pairs = [(g, (g + distance) % layout.walk) for g in range(layout.walk)]
            block = lax.ppermute(block, "walk", pairs)
        arrived.append(block)
    slots = jnp.arange(per_group)
    if layout.walk == 2:
        stays = incoming_groups == group
        position = jnp.where(stays, ranks(stays), half + ranks(~stays))
        hit = position[None, :] == slots[:, None]
        order = jnp.sum(jnp.where(hit, slots[None, :], 0), axis=1)
        return arrived, position.astype(jnp.int32), order.astype(jnp.int32)
    same = (incoming_groups[:, None] == incoming_groups[None, :]) & (slots[None, :] < slots[:, None])
    rank = jnp.sum(same.astype(jnp.int32), axis=1)
    distance = (group - incoming_groups) % layout.walk
    migrated = jnp.take(jnp.concatenate(arrived, axis=0), distance * half + rank, axis=0)
    slots = slots.astype(jnp.int32)
    return [migrated[:half], migrated[half:]], slots, slots


def shards(layout, walkers, trial, cholesky, rotated, fields, source):
    per_group = walkers.shape[0]
    half = per_group // 2
    group = lax.axis_index("walk")
    b = lax.axis_index("chol") % 2

    trial_theirs = layout.shift(trial, db=1)
    mine = lax.dynamic_slice_in_dim(walkers, b * half, half, 0)
    theirs = layout.shift(lax.dynamic_slice_in_dim(walkers, (1 - b) * half, half, 0), db=1)
    rot_theirs = layout.shift(rotated, db=1)
    halves, position, order = migrate(layout, walkers, source)
    places = layout.z == half
    partial = intersections_of(mine, theirs, trial, trial_theirs, places)
    if places:
        total = partial[0]
        for dz in range(1, half):
            total = total + layout.shift(partial[dz], dz=dz).astype(F32)
        other = layout.shift(total.astype(BF16), dy=1)
        inverse = newton_of([total, other])
        inverses = [inverse] + [layout.shift(inverse, dz=dz) for dz in range(1, half)]
    else:
        spread = jnp.zeros((2 * half,) + partial[0].shape, F32)
        spread = lax.dynamic_update_slice_in_dim(spread, jnp.stack(partial), b * half, 0)
        summed = lax.dynamic_slice_in_dim(lax.psum(spread, "chol"), b * half, half, 0)
        inverses = [newton_of([summed[index]]) for index in range(half)]
    bias = bias_of(mine, theirs, rotated, rot_theirs, inverses, places)
    parts = [bias] + [layout.shift(bias, dz=dz) for dz in range(1, layout.z)]
    while len(parts) > 1:
        far = (len(parts) + 1) // 2
        parts = [sum(parts[at::far][1:], parts[at]) for at in range(far)]
    total = parts[0]
    pieces = []
    for dw in range(layout.walk):
        for dy in range(2):
            for db in range(2):
                moved = total if dw + dy + db == 0 else layout.shift_all(total, dw, dy, db)
                pieces.append(((dw, db), moved))

    wanted = lax.dynamic_slice_in_dim(source, group * per_group, per_group)[:, None]
    force_bias, potential = potential_of(
        layout, fields, wanted, position[None, :], pieces, cholesky
    )

    bases, seconds = [], []
    gathered = [layout.gather(piece) for piece in halves]
    for part in range(2):
        rounded, base = first_of(layout, part, potential, gathered[part])
        bases.append(base)
        seconds.append(layout.gather(rounded))
    out = None
    for part in range(2):
        out = second_of(layout, part, potential, bases[part], seconds[part], order, out)
    return out, force_bias


def solution(mesh):
    in_specs = (
        P("walk", "chol", None),
        P("chol", None),
        P(None, "chol", None),
        P(None, "chol", None),
        P("walk", None),
        P(),
    )
    out_specs = (P("walk", "chol", None), P("walk", None))
    layout = Layout(mesh.shape["walk"], mesh.shape["chol"])
    return jax.shard_map(
        functools.partial(shards, layout),
        mesh=mesh,
        in_specs=in_specs,
        out_specs=out_specs,
        check_vma=False,
    )
```

time: 301 us -> 196 us (0.65)
  waiting for transfers between devices: 176 us -> 77.8 us
  starting transfers between devices: 4.29 us -> 59.7 us
  matrix products: 49.7 us -> 0 us
  Pallas kernels: 0 us -> 39.1 us
  blocking collectives: 31.6 us -> 0 us
  between operations: 14 us -> 1.31 us
  local copies, waits for them, and re-layouts: 21.2 us -> 16.3 us
    all_gather x2 -> x0, waiting for transfers between devices: 88.2 us -> none  [the longest x1 73.3 us: shards(): lax.all_gather(first_term.astype(jnp.bfloat16), 'chol', axis=1, tiled=True)]
    psum x1 -> x0, waiting for transfers between devices: 79 us -> none  [shards(): intersections = lax.psum(partial_intersection, 'chol')]
    ppermute x0 -> x81, waiting for transfers between devices: none -> 77.8 us  [the longest x73 75.1 us: shift(): return lax.ppermute(array, 'chol', pairs)]
    ppermute x0 -> x81, starting transfers between devices: none -> 59.7 us  [the longest x73 53.2 us: shift(): return lax.ppermute(array, 'chol', pairs)]
    dot_general x12 -> x0, matrix products: 49.7 us -> none  [the longest x2 17.2 us: column_fold(): jnp.einsum('wpq,wqi->wpi', potential, shard_piece, preferred_element_type...]
    pallas_call x0 -> x8, Pallas kernels: none -> 39.1 us  [the longest x1 10.4 us: potential_of(): pl.pallas_call(functools.partial(potential_kernel, origins, layout), grid...]
    psum x1 -> x0, blocking collectives: 31.6 us -> none  [shards(): force_bias = TAU_ROOT * lax.psum(partial_bias, 'chol')]
    unnamed x19 -> x86, local copies, waits for them, and re-layouts: 18.8 us -> 10.3 us
  transfers between devices with their start and end apart: 4 -> 81, of which waited for: 4 -> 25; matrix products, arithmetic and copies ran while one was open for 17% -> 3% of each run, Pallas kernels for 0% -> 17%
where the time goes in v1:
time: 196 us; the launch traced here: 195 us
  waiting for transfers between devices  77.8 us (40%)
  starting transfers between devices  59.7 us (30%)
  Pallas kernels  39.1 us (20%)
  local copies, waits for them, and re-layouts  16.3 us (8%)
    ppermute x73, waiting for transfers between devices, shift(): return lax.ppermute(array, 'chol', pairs)  75.1 us
    ppermute x73, starting transfers between devices, shift(): return lax.ppermute(array, 'chol', pairs)  53.2 us
    pallas_call x1, Pallas kernels, potential_of(): pl.pallas_call(functools.partial(potential_kernel, origins, layout), grid...  10.4 us
    unnamed x86, local copies, waits for them, and re-layouts  10.3 us
    pallas_call x2, Pallas kernels, second_of(): pl.pallas_call(functools.partial(second_kernel, layout, places), out_shap...  10.1 us
    pallas_call x2, Pallas kernels, first_of(): pl.pallas_call(functools.partial(first_kernel, layout, places), grid=(cou...  9.66 us
    pallas_call x1, Pallas kernels, bias_of(): pl.pallas_call(functools.partial(bias_kernel, places, count), grid=(rows...  6.29 us
    ppermute x7, starting transfers between devices, shift_all(): return lax.ppermute(array, ('walk', 'chol'), pairs)  5.03 us
  transfers between devices with their start and end apart: 81, of which 25 were waited for; matrix products, arithmetic and copies ran while one was open for 3% of the time, Pallas kernels for 17%

profile of v1, /device:TPU:0, one launch (start us, length us, event | category | flops | bytes accessed | tf_op | source)
XLA Modules:
  0.0 195.3 jit_solution(10778452690299480510)
XLA Ops:
  0.7 1.9 constant_dynamic-slice_fusion.2
  3.5 0.7 reshape.24
  4.7 1.6 gather_fusion.1
  6.4 2.6 %collective-permute-start.54 = (bf16[4,128,256]{2,1,0:T(8,128)(2,1)S(1)}, bf16[4,128,256]{2,1,0:T(8,128)(2,1)S(1)}, u32[]{:S(2)}, u32[]{:S(2)}) collective-permute-start(bf16[4,128,256]{2,1,0:T(8,128)(2,1)S(1)} %broadcast_select_fusion.refs_0_), channel_id=1, source_target_pairs={{0,4},{1,5},{2,6},{3,7},{4,8},{5,9},{6,10},{7,11},{8,12},{9,13},{1... | collective-permute-start | bytes 786440 | tf_op jit(solution)/shard_map/ppermute | solution.py:40
  9.1 1.6 gather_fusion
  10.8 0.8 copy-done.40
  12.1 1.6 collective-permute-start.3
  13.7 1.1 collective-permute-start.4
  14.8 2.8 %collective-permute-start.5 = (bf16[256,256]{1,0:T(8,128)(2,1)S(1)}, bf16[256,256]{1,0:T(8,128)(2,1)S(1)}, u32[]{:S(2)}, u32[]{:S(2)}) collective-permute-start(bf16[256,256]{1,0:T(8,128)(2,1)S(1)} %get-tuple-element.16), channel_id=1, source_target_pairs={{0,12},{1,13},{2,14},{3,15},{4,0},{5,1},{6,2},{7,3},{8,4},{9,5},{1... | collective-permute-start | bytes 393224 | tf_op jit(solution)/shard_map/ppermute | solution.py:40
  18.5 1.6 collective-permute-start.52
  20.1 1.1 collective-permute-done.3
  21.2 5.4 %collective-permute-done.4 = bf16[256,256]{1,0:T(8,128)(2,1)S(1)} collective-permute-done((bf16[256,256]{1,0:T(8,128)(2,1)S(1)}, bf16[256,256]{1,0:T(8,128)(2,1)S(1)}, u32[]{:S(2)}, u32[]{:S(2)}) %collective-permute-start.4) | collective-permute-done | bytes 131104 | tf_op jit(solution)/shard_map/ppermute | solution.py:40
  26.6 1.5 collective-permute-start.20
  28.1 1.8 collective-permute-start.58
  30.0 1.6 collective-permute-start.56
  33.0 1.8 collective-permute-done.20.refs_0_
  34.8 1.5 collective-permute-start.6
  36.3 4.5 %collective-permute-done.6.refs_1_ = bf16[256,256]{1,0:T(8,128)(2,1)S(1)} collective-permute-done((bf16[256,256]{1,0:T(8,128)(2,1)S(1)}, bf16[256,256]{1,0:T(8,128)(2,1)S(1)}, u32[]{:S(2)}, u32[]{:S(2)}) %collective-permute-start.6) | collective-permute-done | bytes 131104 | tf_op jit(solution)/shard_map/ppermute | solution.py:40
  41.2 1.5 collective-permute-start.22
  43.4 2.8 %collective-permute-start.62 = (bf16[4,128,256]{2,1,0:T(8,128)(2,1)S(1)}, bf16[4,128,256]{2,1,0:T(8,128)(2,1)S(1)}, u32[]{:S(2)}, u32[]{:S(2)}) collective-permute-start(bf16[4,128,256]{2,1,0:T(8,128)(2,1)S(1)} %collective-permute-done.58.refs_8_), channel_id=1, source_target_pairs={{0,4},{1,5},{2,6},{3,7},{4,8},{5,9},{6,10},{7,11},{8,12},{9,13},{1... | collective-permute-start | bytes 786440 | tf_op jit(solution)/shard_map/ppermute | solution.py:40
  46.2 2.2 %shard_map.78.refs_0_ = bf16[256,256]{1,0:T(8,128)(2,1)S(1)} custom-call(f32[256,256]{1,0:T(8,128)S(1)} %get-tuple-element.24.refs_0_, bf16[256,256]{1,0:T(8,128)(2,1)S(1)} %collective-permute-done.6.refs_1_), custom_call_target="tpu_custom_call" | custom-call | tf_op jit(solution)/shard_map/pallas_call | solution.py:113
  48.4 3.3 %collective-permute-done.24.refs_4_ = bf16[4,128,256]{2,1,0:T(8,128)(2,1)S(1)} collective-permute-done((bf16[4,128,256]{2,1,0:T(8,128)(2,1)S(1)}, bf16[4,128,256]{2,1,0:T(8,128)(2,1)S(1)}, u32[]{:S(2)}, u32[]{:S(2)}) %collective-permute-start.24) | collective-permute-done | bytes 262176 | tf_op jit(solution)/shard_map/ppermute | solution.py:40
  51.8 1.8 collective-permute-start.8
  53.6 2.1 %collective-permute-start.9 = (bf16[256,256]{1,0:T(8,128)(2,1)S(1)}, bf16[256,256]{1,0:T(8,128)(2,1)S(1)}, u32[]{:S(2)}, u32[]{:S(2)}) collective-permute-start(bf16[256,256]{1,0:T(8,128)(2,1)S(1)} %shard_map.78.refs_0_), channel_id=1, source_target_pairs={{0,12},{1,13},{2,14},{3,15},{4,0},{5,1},{6,2},{7,3},{8,4},{9,5},{1... | collective-permute-start | bytes 393224 | tf_op jit(solution)/shard_map/ppermute | solution.py:40
  55.7 4.7 %collective-permute-done.7.refs_1_ = bf16[256,256]{1,0:T(8,128)(2,1)S(1)} collective-permute-done((bf16[256,256]{1,0:T(8,128)(2,1)S(1)}, bf16[256,256]{1,0:T(8,128)(2,1)S(1)}, u32[]{:S(2)}, u32[]{:S(2)}) %collective-permute-start.7) | collective-permute-done | bytes 131104 | tf_op jit(solution)/shard_map/ppermute | solution.py:40
  60.4 1.5 collective-permute-start.60
  61.9 3.6 %collective-permute-done.8.refs_2_ = bf16[256,256]{1,0:T(8,128)(2,1)S(1)} collective-permute-done((bf16[256,256]{1,0:T(8,128)(2,1)S(1)}, bf16[256,256]{1,0:T(8,128)(2,1)S(1)}, u32[]{:S(2)}, u32[]{:S(2)}) %collective-permute-start.8) | collective-permute-done | bytes 131104 | tf_op jit(solution)/shard_map/ppermute | solution.py:40
  66.0 2.8 %collective-permute-start.28 = (bf16[4,128,256]{2,1,0:T(8,128)(2,1)S(1)}, bf16[4,128,256]{2,1,0:T(8,128)(2,1)}, u32[]{:S(2)}, u32[]{:S(2)}) collective-permute-start(bf16[4,128,256]{2,1,0:T(8,128)(2,1)S(1)} %collective-permute-done.24.refs_4_), channel_id=1, source_target_pairs={{0,4},{1,5},{2,6},{3,7},{4,8},{5,9},{6,10},{7,11},{8,12},{9,13},{1... | collective-permute-start | bytes 786440 | tf_op jit(solution)/shard_map/ppermute | solution.py:40
  68.9 1.5 collective-permute-start.26
  72.3 4.7 %collective-permute-done.28.refs_8_ = bf16[4,128,256]{2,1,0:T(8,128)(2,1)} collective-permute-done((bf16[4,128,256]{2,1,0:T(8,128)(2,1)S(1)}, bf16[4,128,256]{2,1,0:T(8,128)(2,1)}, u32[]{:S(2)}, u32[]{:S(2)}) %collective-permute-start.28) | collective-permute-done | bytes 262176 | tf_op jit(solution)/shard_map/ppermute | solution.py:40
  77.0 1.5 collective-permute-start.64
  79.2 6.3 %shard_map.79 = f32[4,32]{1,0:T(4,128)S(1)} custom-call(bf16[4,128,256]{2,1,0:T(8,128)(2,1)S(1)} %get-tuple-element.28.mine, bf16[4,128,256]{2,1,0:T(8,128)(2,1)S(1)} %collective-permute-done.theirs, bf16[32,128,256]{2,1,0:T(8,128)(2,1)S(1)} %copy-done.1, bf16[32,128,256]{2,1,0:T(8,128)(2,1)} %collective-permute-done.1.rot_theirs, ...), custom_call_target="tpu_custom_call" | custom-call | flops 402653184 | bytes 4718592 | tf_op jit(solution)/shard_map/pallas_call | solution.py:177
  85.6 0.7 copy-done.24
  87.5 1.6 collective-permute-start.10
  89.1 2.1 %collective-permute-start.11 = (f32[4,32]{1,0:T(4,128)S(1)}, f32[4,32]{1,0:T(4,128)S(1)}, u32[]{:S(2)}, u32[]{:S(2)}) collective-permute-start(f32[4,32]{1,0:T(4,128)S(1)} %shard_map.79), channel_id=1, source_target_pairs={{0,4},{1,5},{2,6},{3,7},{4,8},{5,9},{6,10},{7,11},{8,12},{9,13},{1... | collective-permute-start | bytes 1544 | tf_op jit(solution)/shard_map/ppermute | solution.py:40
  91.3 1.8 collective-permute-start.12
  93.8 0.8 collective-permute-done.11
  97.0 1.4 collective-permute-start.14
  98.4 4.5 %collective-permute-done.30.refs_10_ = bf16[4,128,256]{2,1,0:T(8,128)(2,1)} collective-permute-done((bf16[4,128,256]{2,1,0:T(8,128)(2,1)}, bf16[4,128,256]{2,1,0:T(8,128)(2,1)}, u32[]{:S(2)}, u32[]{:S(2)}) %collective-permute-start.30) | collective-permute-done | bytes 262176 | tf_op jit(solution)/shard_map/ppermute | solution.py:40
  103.5 3.2 %collective-permute-done.34.refs_14_ = bf16[4,128,256]{2,1,0:T(8,128)(2,1)} collective-permute-done((bf16[4,128,256]{2,1,0:T(8,128)(2,1)}, bf16[4,128,256]{2,1,0:T(8,128)(2,1)}, u32[]{:S(2)}, u32[]{:S(2)}) %collective-permute-start.34) | collective-permute-done | bytes 262176 | tf_op jit(solution)/shard_map/ppermute | solution.py:40
  107.2 2.4 %collective-permute-start.19 = (f32[4,32]{1,0:T(4,128)S(1)}, f32[4,32]{1,0:T(4,128)S(1)}, u32[]{:S(2)}, u32[]{:S(2)}) collective-permute-start(f32[4,32]{1,0:T(4,128)S(1)} %add_add_fusion.refs_0_), channel_id=1, source_target_pairs={{0,19},{1,18},{2,17},{3,16},{4,23},{5,22},{6,21},{7,20},{8,27},{9,... | collective-permute-start | bytes 1544 | tf_op jit(solution)/shard_map/ppermute | solution.py:51
  110.3 0.9 collective-permute-done.18.refs_6_
  111.2 1.2 collective-permute-start.35
  112.7 10.4 %shard_map.80 = (f32[8,32]{1,0:T(8,128)}, bf16[8,128,2048]{2,1,0:T(8,128)(2,1)S(1)}) custom-call(f32[8,32]{1,0:T(8,128)S(1)} %copy-done.41, s32[8,1]{1,0:T(8,128)S(1)} %copy.10.source, s32[1,8]{1,0:T(1,128)S(1)} %bitcast_select_fusion.position, f32[4,32]{1,0:T(4,128)S(1)} %add_add_fusion.refs_0_, f32[4,32]{1,0:T(4,128)S(1)} %collective-permute-done.13.refs_1_, ...), custom_call_target="tpu_custom_call" | custom-call | flops 2147483648 | bytes 20971520 | tf_op jit(solution)/shard_map/pallas_call | solution.py:245
  123.1 2.0 %copy-done = bf16[8,128,2048]{2,1,0:T(8,128)(2,1)} copy-done((bf16[8,128,2048]{2,1,0:T(8,128)(2,1)}, bf16[8,128,2048]{2,1,0:T(8,128)(2,1)S(1)}, u32[]{:S(2)}) %copy-start) | copy-done | bytes 4194328
  125.3 0.9 copy-done.39
  126.2 4.6 %shard_map.82 = (bf16[4,128,256]{2,1,0:T(8,128)(2,1)S(1)}, f32[4,128,256]{2,1,0:T(8,128)S(1)}) custom-call(bf16[8,128,2048]{2,1,0:T(8,128)(2,1)} %copy-done, bf16[4,128,256]{2,1,0:T(8,128)(2,1)S(1)} %broadcast_select_fusion.refs_0_, bf16[4,128,256]{2,1,0:T(8,128)(2,1)S(1)} %copy-done.5, bf16[4,128,256]{2,1,0:T(8,128)(2,1)S(1)} %copy-done.3, ...), custom_call_target="tpu_custom_call" | custom-call | flops 536870912 | bytes 6291456 | tf_op jit(solution)/shard_map/pallas_call | solution.py:340
  131.2 1.5 collective-permute-start.67
  132.8 5.0 %shard_map.81 = (bf16[4,128,256]{2,1,0:T(8,128)(2,1)S(1)}, f32[4,128,256]{2,1,0:T(8,128)S(1)}) custom-call(bf16[8,128,2048]{2,1,0:T(8,128)(2,1)} %copy-done, bf16[4,128,256]{2,1,0:T(8,128)(2,1)S(1)} %collective-permute-done.20.refs_0_, bf16[4,128,256]{2,1,0:T(8,128)(2,1)S(1)} %copy-done.15, bf16[4,128,256]{2,1,0:T(8,128)(2,1)S(1)} %copy-done.11, ...), custom_call_target="tpu_custom_call" | custom-call | flops 536870912 | bytes 6291456 | tf_op jit(solution)/shard_map/pallas_call | solution.py:340
  138.7 2.2 %collective-permute-done.69.refs_4_ = bf16[4,128,256]{2,1,0:T(8,128)(2,1)S(1)} collective-permute-done((bf16[4,128,256]{2,1,0:T(8,128)(2,1)S(1)}, bf16[4,128,256]{2,1,0:T(8,128)(2,1)S(1)}, u32[]{:S(2)}, u32[]{:S(2)}) %collective-permute-start.69) | collective-permute-done | bytes 262176 | tf_op jit(solution)/shard_map/ppermute | solution.py:40
  141.0 1.6 collective-permute-start.71
  142.6 6.2 %collective-permute-done.39.refs_4_ = bf16[4,128,256]{2,1,0:T(8,128)(2,1)S(1)} collective-permute-done((bf16[4,128,256]{2,1,0:T(8,128)(2,1)S(1)}, bf16[4,128,256]{2,1,0:T(8,128)(2,1)S(1)}, u32[]{:S(2)}, u32[]{:S(2)}) %collective-permute-start.39) | collective-permute-done | bytes 262176 | tf_op jit(solution)/shard_map/ppermute | solution.py:40
  149.4 4.8 %collective-permute-done.73.refs_8_ = bf16[4,128,256]{2,1,0:T(8,128)(2,1)S(1)} collective-permute-done((bf16[4,128,256]{2,1,0:T(8,128)(2,1)S(1)}, bf16[4,128,256]{2,1,0:T(8,128)(2,1)S(1)}, u32[]{:S(2)}, u32[]{:S(2)}) %collective-permute-start.73) | collective-permute-done | bytes 262176 | tf_op jit(solution)/shard_map/ppermute | solution.py:40
  155.3 4.4 %collective-permute-done.43.refs_8_ = bf16[4,128,256]{2,1,0:T(8,128)(2,1)S(1)} collective-permute-done((bf16[4,128,256]{2,1,0:T(8,128)(2,1)S(1)}, bf16[4,128,256]{2,1,0:T(8,128)(2,1)S(1)}, u32[]{:S(2)}, u32[]{:S(2)}) %collective-permute-start.43) | collective-permute-done | bytes 262176 | tf_op jit(solution)/shard_map/ppermute | solution.py:40
  160.2 2.0 %collective-permute-done.41.refs_6_ = bf16[4,128,256]{2,1,0:T(8,128)(2,1)S(1)} collective-permute-done((bf16[4,128,256]{2,1,0:T(8,128)(2,1)S(1)}, bf16[4,128,256]{2,1,0:T(8,128)(2,1)S(1)}, u32[]{:S(2)}, u32[]{:S(2)}) %collective-permute-start.41) | collective-permute-done | bytes 262176 | tf_op jit(solution)/shard_map/ppermute | solution.py:40
  162.7 2.7 %collective-permute-done.77.refs_12_ = bf16[4,128,256]{2,1,0:T(8,128)(2,1)S(1)} collective-permute-done((bf16[4,128,256]{2,1,0:T(8,128)(2,1)S(1)}, bf16[4,128,256]{2,1,0:T(8,128)(2,1)S(1)}, u32[]{:S(2)}, u32[]{:S(2)}) %collective-permute-start.77) | collective-permute-done | bytes 262176 | tf_op jit(solution)/shard_map/ppermute | solution.py:40
  165.3 1.5 collective-permute-start.79
  166.9 1.1 collective-permute-done.75.refs_10_
  168.6 4.1 %collective-permute-done.47.refs_12_ = bf16[4,128,256]{2,1,0:T(8,128)(2,1)S(1)} collective-permute-done((bf16[4,128,256]{2,1,0:T(8,128)(2,1)S(1)}, bf16[4,128,256]{2,1,0:T(8,128)(2,1)S(1)}, u32[]{:S(2)}, u32[]{:S(2)}) %collective-permute-start.47) | collective-permute-done | bytes 262176 | tf_op jit(solution)/shard_map/ppermute | solution.py:40
  173.2 1.4 collective-permute-done.79.refs_14_
  174.6 5.6 %collective-permute-done.45.refs_10_ = bf16[4,128,256]{2,1,0:T(8,128)(2,1)S(1)} collective-permute-done((bf16[4,128,256]{2,1,0:T(8,128)(2,1)S(1)}, bf16[4,128,256]{2,1,0:T(8,128)(2,1)S(1)}, u32[]{:S(2)}, u32[]{:S(2)}) %collective-permute-start.45) | collective-permute-done | bytes 262176 | tf_op jit(solution)/shard_map/ppermute | solution.py:40
  180.8 3.6 %collective-permute-done.49.refs_14_ = bf16[4,128,256]{2,1,0:T(8,128)(2,1)S(1)} collective-permute-done((bf16[4,128,256]{2,1,0:T(8,128)(2,1)S(1)}, bf16[4,128,256]{2,1,0:T(8,128)(2,1)S(1)}, u32[]{:S(2)}, u32[]{:S(2)}) %collective-permute-start.49) | collective-permute-done | bytes 262176 | tf_op jit(solution)/shard_map/ppermute | solution.py:40
  185.1 5.1 %shard_map.83.refs_16_ = bf16[8,128,256]{2,1,0:T(8,128)(2,1)} custom-call(s32[8]{0:T(128)S(1)} %select_reduce_fusion.2.order, bf16[8,128,2048]{2,1,0:T(8,128)(2,1)} %copy-done, f32[4,128,256]{2,1,0:T(8,128)S(1)} %get-tuple-element.20.base, bf16[4,128,256]{2,1,0:T(8,128)(2,1)S(1)} %get-tuple-element.21.refs_0_, ...), custom_call_target="tpu_custom_call" | custom-call | flops 536870912 | bytes 6291456 | tf_op jit(solution)/shard_map/pallas_call | solution.py:366
  190.2 5.1 %shard_map.84 = bf16[8,128,256]{2,1,0:T(8,128)(2,1)} custom-call(s32[8]{0:T(128)S(1)} %select_reduce_fusion.2.order, bf16[8,128,2048]{2,1,0:T(8,128)(2,1)} %copy-done, f32[4,128,256]{2,1,0:T(8,128)S(1)} %get-tuple-element.18.base, bf16[4,128,256]{2,1,0:T(8,128)(2,1)S(1)} %get-tuple-element.19.refs_0_, ...), custom_call_target="tpu_custom_call", output_to_operand_aliasing={{}: (19, {})} | custom-call | flops 536870912 | bytes 6291456 | tf_op jit(solution)/shard_map/pallas_call | solution.py:366
  (216 shorter events, 21.2 us)
Async XLA Ops:
  2.6 8.2 %collective-permute-start = (bf16[4,128,256]{2,1,0:T(8,128)(2,1)}, bf16[4,128,256]{2,1,0:T(8,128)(2,1)S(1)}, u32[]{:S(2)}, u32[]{:S(2)}) collective-permute-start(bf16[4,128,256]{2,1,0:T(8,128)(2,1)} %get-tuple-element.27), channel_id=1, source_target_pairs={{0,1},{1,0},{2,3},{3,2},{4,5},{5,4},{6,7},{7,6},{8,9},{9,8},{10,11... | collective-permute-start | bytes 786440 | tf_op jit(solution)/shard_map/ppermute | solution.py:40
  3.0 7.7 %collective-permute-start.2 = (bf16[128,256]{1,0:T(8,128)(2,1)}, bf16[128,256]{1,0:T(8,128)(2,1)S(1)}, u32[]{:S(2)}, u32[]{:S(2)}) collective-permute-start(bf16[128,256]{1,0:T(8,128)(2,1)} %trial_mine.1), channel_id=1, source_target_pairs={{0,1},{1,0},{2,3},{3,2},{4,5},{5,4},{6,7},{7,6},{8,9},{9,8},{10,11... | collective-permute-start | bytes 196616 | tf_op jit(solution)/shard_map/ppermute | solution.py:40
  3.1 75.4 %collective-permute-start.1 = (bf16[32,128,256]{2,1,0:T(8,128)(2,1)}, bf16[32,128,256]{2,1,0:T(8,128)(2,1)}, u32[]{:S(2)}, u32[]{:S(2)}) collective-permute-start(bf16[32,128,256]{2,1,0:T(8,128)(2,1)} %rot_mine.1), channel_id=1, source_target_pairs={{0,1},{1,0},{2,3},{3,2},{4,5},{5,4},{6,7},{7,6},{8,9},{9,8},{10,11... | collective-permute-start | bytes 6291464 | tf_op jit(solution)/shard_map/ppermute | solution.py:40
  6.4 12.0 %collective-permute-start.54 = (bf16[4,128,256]{2,1,0:T(8,128)(2,1)S(1)}, bf16[4,128,256]{2,1,0:T(8,128)(2,1)S(1)}, u32[]{:S(2)}, u32[]{:S(2)}) collective-permute-start(bf16[4,128,256]{2,1,0:T(8,128)(2,1)S(1)} %broadcast_select_fusion.refs_0_), channel_id=1, source_target_pairs={{0,4},{1,5},{2,6},{3,7},{4,8},{5,9},{6,10},{7,11},{8,12},{9,13},{1... | collective-permute-start | bytes 786440 | tf_op jit(solution)/shard_map/ppermute | solution.py:40
  12.1 9.1 %collective-permute-start.3 = (bf16[256,256]{1,0:T(8,128)(2,1)S(1)}, bf16[256,256]{1,0:T(8,128)(2,1)S(1)}, u32[]{:S(2)}, u32[]{:S(2)}) collective-permute-start(bf16[256,256]{1,0:T(8,128)(2,1)S(1)} %get-tuple-element.14), channel_id=1, source_target_pairs={{0,4},{1,5},{2,6},{3,7},{4,8},{5,9},{6,10},{7,11},{8,12},{9,13},{1... | collective-permute-start | bytes 393224 | tf_op jit(solution)/shard_map/ppermute | solution.py:40
  13.7 12.9 %collective-permute-start.4 = (bf16[256,256]{1,0:T(8,128)(2,1)S(1)}, bf16[256,256]{1,0:T(8,128)(2,1)S(1)}, u32[]{:S(2)}, u32[]{:S(2)}) collective-permute-start(bf16[256,256]{1,0:T(8,128)(2,1)S(1)} %get-tuple-element.15), channel_id=1, source_target_pairs={{0,8},{1,9},{2,10},{3,11},{4,12},{5,13},{6,14},{7,15},{8,0},{9,1},... | collective-permute-start | bytes 393224 | tf_op jit(solution)/shard_map/ppermute | solution.py:40
  14.8 13.3 %collective-permute-start.5 = (bf16[256,256]{1,0:T(8,128)(2,1)S(1)}, bf16[256,256]{1,0:T(8,128)(2,1)S(1)}, u32[]{:S(2)}, u32[]{:S(2)}) collective-permute-start(bf16[256,256]{1,0:T(8,128)(2,1)S(1)} %get-tuple-element.16), channel_id=1, source_target_pairs={{0,12},{1,13},{2,14},{3,15},{4,0},{5,1},{6,2},{7,3},{8,4},{9,5},{1... | collective-permute-start | bytes 393224 | tf_op jit(solution)/shard_map/ppermute | solution.py:40
  18.5 11.5 %collective-permute-start.52 = (bf16[4,128,256]{2,1,0:T(8,128)(2,1)S(1)}, bf16[4,128,256]{2,1,0:T(8,128)(2,1)S(1)}, u32[]{:S(2)}, u32[]{:S(2)}) collective-permute-start(bf16[4,128,256]{2,1,0:T(8,128)(2,1)S(1)} %broadcast_select_fusion.refs_0_), channel_id=1, source_target_pairs={{0,2},{1,3},{2,0},{3,1},{4,6},{5,7},{6,4},{7,5},{8,10},{9,11},{10,... | collective-permute-start | bytes 786440 | tf_op jit(solution)/shard_map/ppermute | solution.py:40
  21.2 10.4 %collective-permute-start.51 = (bf16[4,128,256]{2,1,0:T(8,128)(2,1)S(1)}, bf16[4,128,256]{2,1,0:T(8,128)(2,1)S(1)}, u32[]{:S(2)}, u32[]{:S(2)}) collective-permute-start(bf16[4,128,256]{2,1,0:T(8,128)(2,1)S(1)} %broadcast_select_fusion.refs_0_), channel_id=1, source_target_pairs={{0,1},{1,0},{2,3},{3,2},{4,5},{5,4},{6,7},{7,6},{8,9},{9,8},{10,11... | collective-permute-start | bytes 786440 | tf_op jit(solution)/shard_map/ppermute | solution.py:40
  26.6 8.1 %collective-permute-start.20 = (bf16[4,128,256]{2,1,0:T(8,128)(2,1)S(1)}, bf16[4,128,256]{2,1,0:T(8,128)(2,1)S(1)}, u32[]{:S(2)}, u32[]{:S(2)}) collective-permute-start(bf16[4,128,256]{2,1,0:T(8,128)(2,1)S(1)} %broadcast_select_fusion.1), channel_id=1, source_target_pairs={{0,16},{16,0},{1,17},{17,1},{2,18},{18,2},{3,19},{19,3},{4,20},{20... | collective-permute-start | bytes 786440 | tf_op jit(solution)/shard_map/ppermute | solution.py:417
  28.1 12.7 %collective-permute-start.58 = (bf16[4,128,256]{2,1,0:T(8,128)(2,1)S(1)}, bf16[4,128,256]{2,1,0:T(8,128)(2,1)S(1)}, u32[]{:S(2)}, u32[]{:S(2)}) collective-permute-start(bf16[4,128,256]{2,1,0:T(8,128)(2,1)S(1)} %collective-permute-done.54.refs_4_), channel_id=1, source_target_pairs={{0,4},{1,5},{2,6},{3,7},{4,8},{5,9},{6,10},{7,11},{8,12},{9,13},{1... | collective-permute-start | bytes 786440 | tf_op jit(solution)/shard_map/ppermute | solution.py:40
  30.0 11.2 %collective-permute-start.56 = (bf16[4,128,256]{2,1,0:T(8,128)(2,1)S(1)}, bf16[4,128,256]{2,1,0:T(8,128)(2,1)S(1)}, u32[]{:S(2)}, u32[]{:S(2)}) collective-permute-start(bf16[4,128,256]{2,1,0:T(8,128)(2,1)S(1)} %collective-permute-done.54.refs_4_), channel_id=1, source_target_pairs={{0,2},{1,3},{2,0},{3,1},{4,6},{5,7},{6,4},{7,5},{8,10},{9,11},{10,... | collective-permute-start | bytes 786440 | tf_op jit(solution)/shard_map/ppermute | solution.py:40
  32.3 10.4 %collective-permute-start.53 = (bf16[4,128,256]{2,1,0:T(8,128)(2,1)S(1)}, bf16[4,128,256]{2,1,0:T(8,128)(2,1)S(1)}, u32[]{:S(2)}, u32[]{:S(2)}) collective-permute-start(bf16[4,128,256]{2,1,0:T(8,128)(2,1)S(1)} %collective-permute-done.52.refs_2_), channel_id=1, source_target_pairs={{0,1},{1,0},{2,3},{3,2},{4,5},{5,4},{6,7},{7,6},{8,9},{9,8},{10,11... | collective-permute-start | bytes 786440 | tf_op jit(solution)/shard_map/ppermute | solution.py:40
  40.8 11.0 %collective-permute-start.24 = (bf16[4,128,256]{2,1,0:T(8,128)(2,1)S(1)}, bf16[4,128,256]{2,1,0:T(8,128)(2,1)S(1)}, u32[]{:S(2)}, u32[]{:S(2)}) collective-permute-start(bf16[4,128,256]{2,1,0:T(8,128)(2,1)S(1)} %collective-permute-done.20.refs_0_), channel_id=1, source_target_pairs={{0,4},{1,5},{2,6},{3,7},{4,8},{5,9},{6,10},{7,11},{8,12},{9,13},{1... | collective-permute-start | bytes 786440 | tf_op jit(solution)/shard_map/ppermute | solution.py:40
  41.2 10.6 %collective-permute-start.22 = (bf16[4,128,256]{2,1,0:T(8,128)(2,1)S(1)}, bf16[4,128,256]{2,1,0:T(8,128)(2,1)S(1)}, u32[]{:S(2)}, u32[]{:S(2)}) collective-permute-start(bf16[4,128,256]{2,1,0:T(8,128)(2,1)S(1)} %collective-permute-done.20.refs_0_), channel_id=1, source_target_pairs={{0,2},{1,3},{2,0},{3,1},{4,6},{5,7},{6,4},{7,5},{8,10},{9,11},{10,... | collective-permute-start | bytes 786440 | tf_op jit(solution)/shard_map/ppermute | solution.py:40
  43.4 10.2 %collective-permute-start.21 = (bf16[4,128,256]{2,1,0:T(8,128)(2,1)S(1)}, bf16[4,128,256]{2,1,0:T(8,128)(2,1)S(1)}, u32[]{:S(2)}, u32[]{:S(2)}) collective-permute-start(bf16[4,128,256]{2,1,0:T(8,128)(2,1)S(1)} %collective-permute-done.20.refs_0_), channel_id=1, source_target_pairs={{0,1},{1,0},{2,3},{3,2},{4,5},{5,4},{6,7},{7,6},{8,9},{9,8},{10,11... | collective-permute-start | bytes 786440 | tf_op jit(solution)/shard_map/ppermute | solution.py:40
  43.4 22.6 %collective-permute-start.62 = (bf16[4,128,256]{2,1,0:T(8,128)(2,1)S(1)}, bf16[4,128,256]{2,1,0:T(8,128)(2,1)S(1)}, u32[]{:S(2)}, u32[]{:S(2)}) collective-permute-start(bf16[4,128,256]{2,1,0:T(8,128)(2,1)S(1)} %collective-permute-done.58.refs_8_), channel_id=1, source_target_pairs={{0,4},{1,5},{2,6},{3,7},{4,8},{5,9},{6,10},{7,11},{8,12},{9,13},{1... | collective-permute-start | bytes 786440 | tf_op jit(solution)/shard_map/ppermute | solution.py:40
  51.8 8.6 %collective-permute-start.7 = (bf16[256,256]{1,0:T(8,128)(2,1)S(1)}, bf16[256,256]{1,0:T(8,128)(2,1)S(1)}, u32[]{:S(2)}, u32[]{:S(2)}) collective-permute-start(bf16[256,256]{1,0:T(8,128)(2,1)S(1)} %shard_map.78.refs_0_), channel_id=1, source_target_pairs={{0,4},{1,5},{2,6},{3,7},{4,8},{5,9},{6,10},{7,11},{8,12},{9,13},{1... | collective-permute-start | bytes 393224 | tf_op jit(solution)/shard_map/ppermute | solution.py:40
  51.8 13.7 %collective-permute-start.8 = (bf16[256,256]{1,0:T(8,128)(2,1)S(1)}, bf16[256,256]{1,0:T(8,128)(2,1)S(1)}, u32[]{:S(2)}, u32[]{:S(2)}) collective-permute-start(bf16[256,256]{1,0:T(8,128)(2,1)S(1)} %shard_map.78.refs_0_), channel_id=1, source_target_pairs={{0,8},{1,9},{2,10},{3,11},{4,12},{5,13},{6,14},{7,15},{8,0},{9,1},... | collective-permute-start | bytes 393224 | tf_op jit(solution)/shard_map/ppermute | solution.py:40
  53.6 11.9 %collective-permute-start.9 = (bf16[256,256]{1,0:T(8,128)(2,1)S(1)}, bf16[256,256]{1,0:T(8,128)(2,1)S(1)}, u32[]{:S(2)}, u32[]{:S(2)}) collective-permute-start(bf16[256,256]{1,0:T(8,128)(2,1)S(1)} %shard_map.78.refs_0_), channel_id=1, source_target_pairs={{0,12},{1,13},{2,14},{3,15},{4,0},{5,1},{6,2},{7,3},{8,4},{9,5},{1... | collective-permute-start | bytes 393224 | tf_op jit(solution)/shard_map/ppermute | solution.py:40
  60.4 8.5 %collective-permute-start.60 = (bf16[4,128,256]{2,1,0:T(8,128)(2,1)S(1)}, bf16[4,128,256]{2,1,0:T(8,128)(2,1)S(1)}, u32[]{:S(2)}, u32[]{:S(2)}) collective-permute-start(bf16[4,128,256]{2,1,0:T(8,128)(2,1)S(1)} %collective-permute-done.58.refs_8_), channel_id=1, source_target_pairs={{0,2},{1,3},{2,0},{3,1},{4,6},{5,7},{6,4},{7,5},{8,10},{9,11},{10,... | collective-permute-start | bytes 786440 | tf_op jit(solution)/shard_map/ppermute | solution.py:40
  66.0 10.9 %collective-permute-start.28 = (bf16[4,128,256]{2,1,0:T(8,128)(2,1)S(1)}, bf16[4,128,256]{2,1,0:T(8,128)(2,1)}, u32[]{:S(2)}, u32[]{:S(2)}) collective-permute-start(bf16[4,128,256]{2,1,0:T(8,128)(2,1)S(1)} %collective-permute-done.24.refs_4_), channel_id=1, source_target_pairs={{0,4},{1,5},{2,6},{3,7},{4,8},{5,9},{6,10},{7,11},{8,12},{9,13},{1... | collective-permute-start | bytes 786440 | tf_op jit(solution)/shard_map/ppermute | solution.py:40
  68.9 16.6 %collective-permute-start.26 = (bf16[4,128,256]{2,1,0:T(8,128)(2,1)S(1)}, bf16[4,128,256]{2,1,0:T(8,128)(2,1)S(1)}, u32[]{:S(2)}, u32[]{:S(2)}) collective-permute-start(bf16[4,128,256]{2,1,0:T(8,128)(2,1)S(1)} %collective-permute-done.24.refs_4_), channel_id=1, source_target_pairs={{0,2},{1,3},{2,0},{3,1},{4,6},{5,7},{6,4},{7,5},{8,10},{9,11},{10,... | collective-permute-start | bytes 786440 | tf_op jit(solution)/shard_map/ppermute | solution.py:40
  71.1 14.5 %collective-permute-start.23 = (bf16[4,128,256]{2,1,0:T(8,128)(2,1)S(1)}, bf16[4,128,256]{2,1,0:T(8,128)(2,1)S(1)}, u32[]{:S(2)}, u32[]{:S(2)}) collective-permute-start(bf16[4,128,256]{2,1,0:T(8,128)(2,1)S(1)} %collective-permute-done.22.refs_2_), channel_id=1, source_target_pairs={{0,1},{1,0},{2,3},{3,2},{4,5},{5,4},{6,7},{7,6},{8,9},{9,8},{10,11... | collective-permute-start | bytes 786440 | tf_op jit(solution)/shard_map/ppermute | solution.py:40
  71.8 15.0 %collective-permute-start.25 = (bf16[4,128,256]{2,1,0:T(8,128)(2,1)S(1)}, bf16[4,128,256]{2,1,0:T(8,128)(2,1)S(1)}, u32[]{:S(2)}, u32[]{:S(2)}) collective-permute-start(bf16[4,128,256]{2,1,0:T(8,128)(2,1)S(1)} %collective-permute-done.24.refs_4_), channel_id=1, source_target_pairs={{0,1},{1,0},{2,3},{3,2},{4,5},{5,4},{6,7},{7,6},{8,9},{9,8},{10,11... | collective-permute-start | bytes 786440 | tf_op jit(solution)/shard_map/ppermute | solution.py:40
  77.0 12.2 %collective-permute-start.64 = (bf16[4,128,256]{2,1,0:T(8,128)(2,1)S(1)}, bf16[4,128,256]{2,1,0:T(8,128)(2,1)}, u32[]{:S(2)}, u32[]{:S(2)}) collective-permute-start(bf16[4,128,256]{2,1,0:T(8,128)(2,1)S(1)} %collective-permute-done.62.refs_12_), channel_id=1, source_target_pairs={{0,2},{1,3},{2,0},{3,1},{4,6},{5,7},{6,4},{7,5},{8,10},{9,11},{10,... | collective-permute-start | bytes 786440 | tf_op jit(solution)/shard_map/ppermute | solution.py:40
  78.5 12.8 %collective-permute-start.32 = (bf16[4,128,256]{2,1,0:T(8,128)(2,1)}, bf16[4,128,256]{2,1,0:T(8,128)(2,1)}, u32[]{:S(2)}, u32[]{:S(2)}) collective-permute-start(bf16[4,128,256]{2,1,0:T(8,128)(2,1)} %collective-permute-done.28.refs_8_), channel_id=1, source_target_pairs={{0,4},{1,5},{2,6},{3,7},{4,8},{5,9},{6,10},{7,11},{8,12},{9,13},{1... | collective-permute-start | bytes 786440 | tf_op jit(solution)/shard_map/ppermute | solution.py:40
  85.5 10.8 %collective-permute-start.63 = (bf16[4,128,256]{2,1,0:T(8,128)(2,1)S(1)}, bf16[4,128,256]{2,1,0:T(8,128)(2,1)S(1)}, u32[]{:S(2)}, u32[]{:S(2)}) collective-permute-start(bf16[4,128,256]{2,1,0:T(8,128)(2,1)S(1)} %collective-permute-done.62.refs_12_), channel_id=1, source_target_pairs={{0,1},{1,0},{2,3},{3,2},{4,5},{5,4},{6,7},{7,6},{8,9},{9,8},{10,11... | collective-permute-start | bytes 786440 | tf_op jit(solution)/shard_map/ppermute | solution.py:40
  86.3 9.1 %collective-permute-start.61 = (bf16[4,128,256]{2,1,0:T(8,128)(2,1)S(1)}, bf16[4,128,256]{2,1,0:T(8,128)(2,1)S(1)}, u32[]{:S(2)}, u32[]{:S(2)}) collective-permute-start(bf16[4,128,256]{2,1,0:T(8,128)(2,1)S(1)} %collective-permute-done.60.refs_10_), channel_id=1, source_target_pairs={{0,1},{1,0},{2,3},{3,2},{4,5},{5,4},{6,7},{7,6},{8,9},{9,8},{10,11... | collective-permute-start | bytes 786440 | tf_op jit(solution)/shard_map/ppermute | solution.py:40
  93.2 9.6 %collective-permute-start.30 = (bf16[4,128,256]{2,1,0:T(8,128)(2,1)}, bf16[4,128,256]{2,1,0:T(8,128)(2,1)}, u32[]{:S(2)}, u32[]{:S(2)}) collective-permute-start(bf16[4,128,256]{2,1,0:T(8,128)(2,1)} %collective-permute-done.28.refs_8_), channel_id=1, source_target_pairs={{0,2},{1,3},{2,0},{3,1},{4,6},{5,7},{6,4},{7,5},{8,10},{9,11},{10,... | collective-permute-start | bytes 786440 | tf_op jit(solution)/shard_map/ppermute | solution.py:40
  94.6 8.3 %collective-permute-start.65 = (bf16[4,128,256]{2,1,0:T(8,128)(2,1)}, bf16[4,128,256]{2,1,0:T(8,128)(2,1)S(1)}, u32[]{:S(2)}, u32[]{:S(2)}) collective-permute-start(bf16[4,128,256]{2,1,0:T(8,128)(2,1)} %collective-permute-done.64.refs_14_), channel_id=1, source_target_pairs={{0,1},{1,0},{2,3},{3,2},{4,5},{5,4},{6,7},{7,6},{8,9},{9,8},{10,11... | collective-permute-start | bytes 786440 | tf_op jit(solution)/shard_map/ppermute | solution.py:40
  94.9 11.8 %collective-permute-start.34 = (bf16[4,128,256]{2,1,0:T(8,128)(2,1)}, bf16[4,128,256]{2,1,0:T(8,128)(2,1)}, u32[]{:S(2)}, u32[]{:S(2)}) collective-permute-start(bf16[4,128,256]{2,1,0:T(8,128)(2,1)} %collective-permute-done.32.refs_12_), channel_id=1, source_target_pairs={{0,2},{1,3},{2,0},{3,1},{4,6},{5,7},{6,4},{7,5},{8,10},{9,11},{10,... | collective-permute-start | bytes 786440 | tf_op jit(solution)/shard_map/ppermute | solution.py:40
  96.2 10.6 %collective-permute-start.13 = (f32[4,32]{1,0:T(4,128)S(1)}, f32[4,32]{1,0:T(4,128)S(1)}, u32[]{:S(2)}, u32[]{:S(2)}) collective-permute-start(f32[4,32]{1,0:T(4,128)S(1)} %add_add_fusion.refs_0_), channel_id=1, source_target_pairs={{0,1},{1,0},{2,3},{3,2},{4,5},{5,4},{6,7},{7,6},{8,9},{9,8},{10,11... | collective-permute-start | bytes 1544 | tf_op jit(solution)/shard_map/ppermute | solution.py:51
  97.0 10.2 %collective-permute-start.14 = (f32[4,32]{1,0:T(4,128)S(1)}, f32[4,32]{1,0:T(4,128)S(1)}, u32[]{:S(2)}, u32[]{:S(2)}) collective-permute-start(f32[4,32]{1,0:T(4,128)S(1)} %add_add_fusion.refs_0_), channel_id=1, source_target_pairs={{0,2},{1,3},{2,0},{3,1},{4,6},{5,7},{6,4},{7,5},{8,10},{9,11},{10,... | collective-permute-start | bytes 1544 | tf_op jit(solution)/shard_map/ppermute | solution.py:51
  102.9 6.9 %collective-permute-start.16 = (f32[4,32]{1,0:T(4,128)S(1)}, f32[4,32]{1,0:T(4,128)S(1)}, u32[]{:S(2)}, u32[]{:S(2)}) collective-permute-start(f32[4,32]{1,0:T(4,128)S(1)} %add_add_fusion.refs_0_), channel_id=1, source_target_pairs={{0,16},{1,17},{2,18},{3,19},{4,20},{5,21},{6,22},{7,23},{8,24},{9,... | collective-permute-start | bytes 1544 | tf_op jit(solution)/shard_map/ppermute | solution.py:51
  109.6 21.6 %collective-permute-start.29 = (bf16[4,128,256]{2,1,0:T(8,128)(2,1)}, bf16[4,128,256]{2,1,0:T(8,128)(2,1)}, u32[]{:S(2)}, u32[]{:S(2)}) collective-permute-start(bf16[4,128,256]{2,1,0:T(8,128)(2,1)} %collective-permute-done.28.refs_8_), channel_id=1, source_target_pairs={{0,1},{1,0},{2,3},{3,2},{4,5},{5,4},{6,7},{7,6},{8,9},{9,8},{10,11... | collective-permute-start | bytes 786440 | tf_op jit(solution)/shard_map/ppermute | solution.py:40
  109.8 21.1 %collective-permute-start.27 = (bf16[4,128,256]{2,1,0:T(8,128)(2,1)}, bf16[4,128,256]{2,1,0:T(8,128)(2,1)}, u32[]{:S(2)}, u32[]{:S(2)}) collective-permute-start(bf16[4,128,256]{2,1,0:T(8,128)(2,1)} %copy-done.22), channel_id=1, source_target_pairs={{0,1},{1,0},{2,3},{3,2},{4,5},{5,4},{6,7},{7,6},{8,9},{9,8},{10,11... | collective-permute-start | bytes 786440 | tf_op jit(solution)/shard_map/ppermute | solution.py:40
  110.2 22.6 %collective-permute-start.33 = (bf16[4,128,256]{2,1,0:T(8,128)(2,1)}, bf16[4,128,256]{2,1,0:T(8,128)(2,1)}, u32[]{:S(2)}, u32[]{:S(2)}) collective-permute-start(bf16[4,128,256]{2,1,0:T(8,128)(2,1)} %collective-permute-done.32.refs_12_), channel_id=1, source_target_pairs={{0,1},{1,0},{2,3},{3,2},{4,5},{5,4},{6,7},{7,6},{8,9},{9,8},{10,11... | collective-permute-start | bytes 786440 | tf_op jit(solution)/shard_map/ppermute | solution.py:40
  111.2 21.5 %collective-permute-start.31 = (bf16[4,128,256]{2,1,0:T(8,128)(2,1)}, bf16[4,128,256]{2,1,0:T(8,128)(2,1)}, u32[]{:S(2)}, u32[]{:S(2)}) collective-permute-start(bf16[4,128,256]{2,1,0:T(8,128)(2,1)} %collective-permute-done.30.refs_10_), channel_id=1, source_target_pairs={{0,1},{1,0},{2,3},{3,2},{4,5},{5,4},{6,7},{7,6},{8,9},{9,8},{10,11... | collective-permute-start | bytes 786440 | tf_op jit(solution)/shard_map/ppermute | solution.py:40
  111.2 21.5 %collective-permute-start.35 = (bf16[4,128,256]{2,1,0:T(8,128)(2,1)}, bf16[4,128,256]{2,1,0:T(8,128)(2,1)}, u32[]{:S(2)}, u32[]{:S(2)}) collective-permute-start(bf16[4,128,256]{2,1,0:T(8,128)(2,1)} %collective-permute-done.34.refs_14_), channel_id=1, source_target_pairs={{0,1},{1,0},{2,3},{3,2},{4,5},{5,4},{6,7},{7,6},{8,9},{9,8},{10,11... | collective-permute-start | bytes 786440 | tf_op jit(solution)/shard_map/ppermute | solution.py:40
  130.9 10.1 %collective-permute-start.69 = (bf16[4,128,256]{2,1,0:T(8,128)(2,1)S(1)}, bf16[4,128,256]{2,1,0:T(8,128)(2,1)S(1)}, u32[]{:S(2)}, u32[]{:S(2)}) collective-permute-start(bf16[4,128,256]{2,1,0:T(8,128)(2,1)S(1)} %get-tuple-element.21.refs_0_), channel_id=1, source_target_pairs={{0,4},{1,5},{2,6},{3,7},{4,8},{5,9},{6,10},{7,11},{8,12},{9,13},{1... | collective-permute-start | bytes 786440 | tf_op jit(solution)/shard_map/ppermute | solution.py:40
  131.2 9.7 %collective-permute-start.67 = (bf16[4,128,256]{2,1,0:T(8,128)(2,1)S(1)}, bf16[4,128,256]{2,1,0:T(8,128)(2,1)S(1)}, u32[]{:S(2)}, u32[]{:S(2)}) collective-permute-start(bf16[4,128,256]{2,1,0:T(8,128)(2,1)S(1)} %get-tuple-element.21.refs_0_), channel_id=1, source_target_pairs={{0,2},{1,3},{2,0},{3,1},{4,6},{5,7},{6,4},{7,5},{8,10},{9,11},{10,... | collective-permute-start | bytes 786440 | tf_op jit(solution)/shard_map/ppermute | solution.py:40
  132.8 8.2 %collective-permute-start.66 = (bf16[4,128,256]{2,1,0:T(8,128)(2,1)S(1)}, bf16[4,128,256]{2,1,0:T(8,128)(2,1)S(1)}, u32[]{:S(2)}, u32[]{:S(2)}) collective-permute-start(bf16[4,128,256]{2,1,0:T(8,128)(2,1)S(1)} %get-tuple-element.21.refs_0_), channel_id=1, source_target_pairs={{0,1},{1,0},{2,3},{3,2},{4,5},{5,4},{6,7},{7,6},{8,9},{9,8},{10,11... | collective-permute-start | bytes 786440 | tf_op jit(solution)/shard_map/ppermute | solution.py:40
  137.9 11.0 %collective-permute-start.39 = (bf16[4,128,256]{2,1,0:T(8,128)(2,1)S(1)}, bf16[4,128,256]{2,1,0:T(8,128)(2,1)S(1)}, u32[]{:S(2)}, u32[]{:S(2)}) collective-permute-start(bf16[4,128,256]{2,1,0:T(8,128)(2,1)S(1)} %get-tuple-element.19.refs_0_), channel_id=1, source_target_pairs={{0,4},{1,5},{2,6},{3,7},{4,8},{5,9},{6,10},{7,11},{8,12},{9,13},{1... | collective-permute-start | bytes 786440 | tf_op jit(solution)/shard_map/ppermute | solution.py:40
  138.2 10.6 %collective-permute-start.37 = (bf16[4,128,256]{2,1,0:T(8,128)(2,1)S(1)}, bf16[4,128,256]{2,1,0:T(8,128)(2,1)S(1)}, u32[]{:S(2)}, u32[]{:S(2)}) collective-permute-start(bf16[4,128,256]{2,1,0:T(8,128)(2,1)S(1)} %get-tuple-element.19.refs_0_), channel_id=1, source_target_pairs={{0,2},{1,3},{2,0},{3,1},{4,6},{5,7},{6,4},{7,5},{8,10},{9,11},{10,... | collective-permute-start | bytes 786440 | tf_op jit(solution)/shard_map/ppermute | solution.py:40
  141.0 8.4 %collective-permute-start.36 = (bf16[4,128,256]{2,1,0:T(8,128)(2,1)S(1)}, bf16[4,128,256]{2,1,0:T(8,128)(2,1)S(1)}, u32[]{:S(2)}, u32[]{:S(2)}) collective-permute-start(bf16[4,128,256]{2,1,0:T(8,128)(2,1)S(1)} %get-tuple-element.19.refs_0_), channel_id=1, source_target_pairs={{0,1},{1,0},{2,3},{3,2},{4,5},{5,4},{6,7},{7,6},{8,9},{9,8},{10,11... | collective-permute-start | bytes 786440 | tf_op jit(solution)/shard_map/ppermute | solution.py:40
  141.0 13.3 %collective-permute-start.73 = (bf16[4,128,256]{2,1,0:T(8,128)(2,1)S(1)}, bf16[4,128,256]{2,1,0:T(8,128)(2,1)S(1)}, u32[]{:S(2)}, u32[]{:S(2)}) collective-permute-start(bf16[4,128,256]{2,1,0:T(8,128)(2,1)S(1)} %collective-permute-done.69.refs_4_), channel_id=1, source_target_pairs={{0,4},{1,5},{2,6},{3,7},{4,8},{5,9},{6,10},{7,11},{8,12},{9,13},{1... | collective-permute-start | bytes 786440 | tf_op jit(solution)/shard_map/ppermute | solution.py:40
  141.0 13.8 %collective-permute-start.71 = (bf16[4,128,256]{2,1,0:T(8,128)(2,1)S(1)}, bf16[4,128,256]{2,1,0:T(8,128)(2,1)S(1)}, u32[]{:S(2)}, u32[]{:S(2)}) collective-permute-start(bf16[4,128,256]{2,1,0:T(8,128)(2,1)S(1)} %collective-permute-done.69.refs_4_), channel_id=1, source_target_pairs={{0,2},{1,3},{2,0},{3,1},{4,6},{5,7},{6,4},{7,5},{8,10},{9,11},{10,... | collective-permute-start | bytes 786440 | tf_op jit(solution)/shard_map/ppermute | solution.py:40
  149.3 10.3 %collective-permute-start.43 = (bf16[4,128,256]{2,1,0:T(8,128)(2,1)S(1)}, bf16[4,128,256]{2,1,0:T(8,128)(2,1)S(1)}, u32[]{:S(2)}, u32[]{:S(2)}) collective-permute-start(bf16[4,128,256]{2,1,0:T(8,128)(2,1)S(1)} %collective-permute-done.39.refs_4_), channel_id=1, source_target_pairs={{0,4},{1,5},{2,6},{3,7},{4,8},{5,9},{6,10},{7,11},{8,12},{9,13},{1... | collective-permute-start | bytes 786440 | tf_op jit(solution)/shard_map/ppermute | solution.py:40
  154.2 7.9 %collective-permute-start.41 = (bf16[4,128,256]{2,1,0:T(8,128)(2,1)S(1)}, bf16[4,128,256]{2,1,0:T(8,128)(2,1)S(1)}, u32[]{:S(2)}, u32[]{:S(2)}) collective-permute-start(bf16[4,128,256]{2,1,0:T(8,128)(2,1)S(1)} %collective-permute-done.39.refs_4_), channel_id=1, source_target_pairs={{0,2},{1,3},{2,0},{3,1},{4,6},{5,7},{6,4},{7,5},{8,10},{9,11},{10,... | collective-permute-start | bytes 786440 | tf_op jit(solution)/shard_map/ppermute | solution.py:40
  154.7 7.4 %collective-permute-start.38 = (bf16[4,128,256]{2,1,0:T(8,128)(2,1)S(1)}, bf16[4,128,256]{2,1,0:T(8,128)(2,1)S(1)}, u32[]{:S(2)}, u32[]{:S(2)}) collective-permute-start(bf16[4,128,256]{2,1,0:T(8,128)(2,1)S(1)} %collective-permute-done.37.refs_2_), channel_id=1, source_target_pairs={{0,1},{1,0},{2,3},{3,2},{4,5},{5,4},{6,7},{7,6},{8,9},{9,8},{10,11... | collective-permute-start | bytes 786440 | tf_op jit(solution)/shard_map/ppermute | solution.py:40
  154.8 7.9 %collective-permute-start.40 = (bf16[4,128,256]{2,1,0:T(8,128)(2,1)S(1)}, bf16[4,128,256]{2,1,0:T(8,128)(2,1)S(1)}, u32[]{:S(2)}, u32[]{:S(2)}) collective-permute-start(bf16[4,128,256]{2,1,0:T(8,128)(2,1)S(1)} %collective-permute-done.39.refs_4_), channel_id=1, source_target_pairs={{0,1},{1,0},{2,3},{3,2},{4,5},{5,4},{6,7},{7,6},{8,9},{9,8},{10,11... | collective-permute-start | bytes 786440 | tf_op jit(solution)/shard_map/ppermute | solution.py:40
  155.3 10.1 %collective-permute-start.77 = (bf16[4,128,256]{2,1,0:T(8,128)(2,1)S(1)}, bf16[4,128,256]{2,1,0:T(8,128)(2,1)S(1)}, u32[]{:S(2)}, u32[]{:S(2)}) collective-permute-start(bf16[4,128,256]{2,1,0:T(8,128)(2,1)S(1)} %collective-permute-done.73.refs_8_), channel_id=1, source_target_pairs={{0,4},{1,5},{2,6},{3,7},{4,8},{5,9},{6,10},{7,11},{8,12},{9,13},{1... | collective-permute-start | bytes 786440 | tf_op jit(solution)/shard_map/ppermute | solution.py:40
  159.7 8.3 %collective-permute-start.75 = (bf16[4,128,256]{2,1,0:T(8,128)(2,1)S(1)}, bf16[4,128,256]{2,1,0:T(8,128)(2,1)S(1)}, u32[]{:S(2)}, u32[]{:S(2)}) collective-permute-start(bf16[4,128,256]{2,1,0:T(8,128)(2,1)S(1)} %collective-permute-done.73.refs_8_), channel_id=1, source_target_pairs={{0,2},{1,3},{2,0},{3,1},{4,6},{5,7},{6,4},{7,5},{8,10},{9,11},{10,... | collective-permute-start | bytes 786440 | tf_op jit(solution)/shard_map/ppermute | solution.py:40
  162.7 10.1 %collective-permute-start.47 = (bf16[4,128,256]{2,1,0:T(8,128)(2,1)S(1)}, bf16[4,128,256]{2,1,0:T(8,128)(2,1)S(1)}, u32[]{:S(2)}, u32[]{:S(2)}) collective-permute-start(bf16[4,128,256]{2,1,0:T(8,128)(2,1)S(1)} %collective-permute-done.43.refs_8_), channel_id=1, source_target_pairs={{0,4},{1,5},{2,6},{3,7},{4,8},{5,9},{6,10},{7,11},{8,12},{9,13},{1... | collective-permute-start | bytes 786440 | tf_op jit(solution)/shard_map/ppermute | solution.py:40
  165.3 9.2 %collective-permute-start.79 = (bf16[4,128,256]{2,1,0:T(8,128)(2,1)S(1)}, bf16[4,128,256]{2,1,0:T(8,128)(2,1)S(1)}, u32[]{:S(2)}, u32[]{:S(2)}) collective-permute-start(bf16[4,128,256]{2,1,0:T(8,128)(2,1)S(1)} %collective-permute-done.77.refs_12_), channel_id=1, source_target_pairs={{0,2},{1,3},{2,0},{3,1},{4,6},{5,7},{6,4},{7,5},{8,10},{9,11},{10,... | collective-permute-start | bytes 786440 | tf_op jit(solution)/shard_map/ppermute | solution.py:40
  167.9 12.3 %collective-permute-start.45 = (bf16[4,128,256]{2,1,0:T(8,128)(2,1)S(1)}, bf16[4,128,256]{2,1,0:T(8,128)(2,1)S(1)}, u32[]{:S(2)}, u32[]{:S(2)}) collective-permute-start(bf16[4,128,256]{2,1,0:T(8,128)(2,1)S(1)} %collective-permute-done.43.refs_8_), channel_id=1, source_target_pairs={{0,2},{1,3},{2,0},{3,1},{4,6},{5,7},{6,4},{7,5},{8,10},{9,11},{10,... | collective-permute-start | bytes 786440 | tf_op jit(solution)/shard_map/ppermute | solution.py:40
  168.1 12.1 %collective-permute-start.76 = (bf16[4,128,256]{2,1,0:T(8,128)(2,1)S(1)}, bf16[4,128,256]{2,1,0:T(8,128)(2,1)S(1)}, u32[]{:S(2)}, u32[]{:S(2)}) collective-permute-start(bf16[4,128,256]{2,1,0:T(8,128)(2,1)S(1)} %collective-permute-done.75.refs_10_), channel_id=1, source_target_pairs={{0,1},{1,0},{2,3},{3,2},{4,5},{5,4},{6,7},{7,6},{8,9},{9,8},{10,11... | collective-permute-start | bytes 786440 | tf_op jit(solution)/shard_map/ppermute | solution.py:40
  168.1 12.6 %collective-permute-start.78 = (bf16[4,128,256]{2,1,0:T(8,128)(2,1)S(1)}, bf16[4,128,256]{2,1,0:T(8,128)(2,1)S(1)}, u32[]{:S(2)}, u32[]{:S(2)}) collective-permute-start(bf16[4,128,256]{2,1,0:T(8,128)(2,1)S(1)} %collective-permute-done.77.refs_12_), channel_id=1, source_target_pairs={{0,1},{1,0},{2,3},{3,2},{4,5},{5,4},{6,7},{7,6},{8,9},{9,8},{10,11... | collective-permute-start | bytes 786440 | tf_op jit(solution)/shard_map/ppermute | solution.py:40
  172.7 11.7 %collective-permute-start.49 = (bf16[4,128,256]{2,1,0:T(8,128)(2,1)S(1)}, bf16[4,128,256]{2,1,0:T(8,128)(2,1)S(1)}, u32[]{:S(2)}, u32[]{:S(2)}) collective-permute-start(bf16[4,128,256]{2,1,0:T(8,128)(2,1)S(1)} %collective-permute-done.47.refs_12_), channel_id=1, source_target_pairs={{0,2},{1,3},{2,0},{3,1},{4,6},{5,7},{6,4},{7,5},{8,10},{9,11},{10,... | collective-permute-start | bytes 786440 | tf_op jit(solution)/shard_map/ppermute | solution.py:40
  174.6 9.9 %collective-permute-start.80 = (bf16[4,128,256]{2,1,0:T(8,128)(2,1)S(1)}, bf16[4,128,256]{2,1,0:T(8,128)(2,1)S(1)}, u32[]{:S(2)}, u32[]{:S(2)}) collective-permute-start(bf16[4,128,256]{2,1,0:T(8,128)(2,1)S(1)} %collective-permute-done.79.refs_14_), channel_id=1, source_target_pairs={{0,1},{1,0},{2,3},{3,2},{4,5},{5,4},{6,7},{7,6},{8,9},{9,8},{10,11... | collective-permute-start | bytes 786440 | tf_op jit(solution)/shard_map/ppermute | solution.py:40
  180.2 9.9 %collective-permute-start.44 = (bf16[4,128,256]{2,1,0:T(8,128)(2,1)S(1)}, bf16[4,128,256]{2,1,0:T(8,128)(2,1)S(1)}, u32[]{:S(2)}, u32[]{:S(2)}) collective-permute-start(bf16[4,128,256]{2,1,0:T(8,128)(2,1)S(1)} %collective-permute-done.43.refs_8_), channel_id=1, source_target_pairs={{0,1},{1,0},{2,3},{3,2},{4,5},{5,4},{6,7},{7,6},{8,9},{9,8},{10,11... | collective-permute-start | bytes 786440 | tf_op jit(solution)/shard_map/ppermute | solution.py:40
  180.2 9.9 %collective-permute-start.42 = (bf16[4,128,256]{2,1,0:T(8,128)(2,1)S(1)}, bf16[4,128,256]{2,1,0:T(8,128)(2,1)S(1)}, u32[]{:S(2)}, u32[]{:S(2)}) collective-permute-start(bf16[4,128,256]{2,1,0:T(8,128)(2,1)S(1)} %collective-permute-done.41.refs_6_), channel_id=1, source_target_pairs={{0,1},{1,0},{2,3},{3,2},{4,5},{5,4},{6,7},{7,6},{8,9},{9,8},{10,11... | collective-permute-start | bytes 786440 | tf_op jit(solution)/shard_map/ppermute | solution.py:40
  180.7 9.4 %collective-permute-start.48 = (bf16[4,128,256]{2,1,0:T(8,128)(2,1)S(1)}, bf16[4,128,256]{2,1,0:T(8,128)(2,1)S(1)}, u32[]{:S(2)}, u32[]{:S(2)}) collective-permute-start(bf16[4,128,256]{2,1,0:T(8,128)(2,1)S(1)} %collective-permute-done.47.refs_12_), channel_id=1, source_target_pairs={{0,1},{1,0},{2,3},{3,2},{4,5},{5,4},{6,7},{7,6},{8,9},{9,8},{10,11... | collective-permute-start | bytes 786440 | tf_op jit(solution)/shard_map/ppermute | solution.py:40
  (60 other events, 904.5 us)

commit v2 on v1

v2 whole, which is shorter than its diff:
```python
import functools

import jax
import jax.numpy as jnp
from jax import lax
from jax.experimental import pallas as pl
from jax.experimental.pallas import tpu as pltpu
from jax.sharding import PartitionSpec as P

ITERS = 3
TAU_ROOT = 0.1
BLOCK = 16
HIGHEST = lax.Precision.HIGHEST
MIB = 1024 * 1024

F32 = jnp.float32
BF16 = jnp.bfloat16


def params(mebibytes):
    return pltpu.CompilerParams(vmem_limit_bytes=mebibytes * MIB)


def vmem_specs(count):
    return [pl.BlockSpec(memory_space=pltpu.VMEM)] * count


class Layout:
    def __init__(self, walk_size, chol_size):
        self.walk = walk_size
        self.chol = chol_size
        self.z = chol_size // 4

    def shift(self, array, dz=0, dy=0, db=0):
        pairs = []
        for index in range(self.chol):
            z, y, b = index // 4, (index // 2) % 2, index % 2
            target = (((z + dz) % self.z) * 2 + (y ^ dy)) * 2 + (b ^ db)
            pairs.append((index, target))
        return lax.ppermute(array, "chol", pairs)

    def shift_all(self, array, dw, db):
        pairs = []
        for group in range(self.walk):
            for index in range(self.chol):
                target = ((group + dw) % self.walk) * self.chol + (index ^ db)
                pairs.append((group * self.chol + index, target))
        return lax.ppermute(array, ("walk", "chol"), pairs)

    def swap(self, array, distance):
        pairs = [(i, (((i // 4) ^ distance) * 4) + i % 4) for i in range(self.chol)]
        return lax.ppermute(array, "chol", pairs)

    def gather_plane(self, piece):
        planes = [[i for i in range(self.chol) if i % 2 == b] for b in range(2)]
        return lax.all_gather(piece, "chol", axis_index_groups=planes, axis=1, tiled=True)

    def with_sibling(self, plane, rows):
        both = (plane, self.shift(plane, db=1))
        shape = (plane.shape[0], self.chol // 2, rows, plane.shape[2])
        return [array.reshape(shape) for array in both]


def intersection_kernel(places, mine, theirs, trial_mine, trial_theirs, *outs):
    count = mine.shape[0] // 2
    first = trial_mine[...].T
    second = trial_theirs[...].T
    index = lax.axis_index("chol")
    z, base = index // 4, lax.rem(index, 2) * count
    for step in range(count):
        walker = base + (lax.rem(z + step, count) if places else step)
        total = jnp.dot(first, mine[walker], preferred_element_type=F32)
        total += jnp.dot(second, theirs[walker], preferred_element_type=F32)
        outs[step][...] = total.astype(outs[step].dtype)


def intersections_of(mine, theirs, trial_mine, trial_theirs, places):
    per_group, _, electrons = mine.shape
    count = per_group // 2
    kinds = [F32] + [BF16 if places else F32] * (count - 1)
    return pl.pallas_call(
        functools.partial(intersection_kernel, places),
        out_shape=[jax.ShapeDtypeStruct((electrons, electrons), kind) for kind in kinds],
        in_specs=vmem_specs(4),
        out_specs=vmem_specs(count),
        compiler_params=params(8),
    )(mine, theirs, trial_mine, trial_theirs)


def newton_kernel(*refs):
    parts, out = refs[:-1], refs[-1]
    matrix = parts[0][...]
    for part in parts[1:]:
        matrix = matrix + part[...].astype(F32)
    shape = matrix.shape
    twice = jnp.where(
        lax.broadcasted_iota(jnp.int32, shape, 0) == lax.broadcasted_iota(jnp.int32, shape, 1),
        2.0,
        0.0,
    ).astype(F32)
    estimate = twice - matrix
    for _ in range(ITERS - 1):
        product = jnp.dot(matrix, estimate, precision=HIGHEST, preferred_element_type=F32)
        estimate = jnp.dot(
            estimate, twice - product, precision=HIGHEST, preferred_element_type=F32
        )
    out[...] = estimate.astype(out.dtype)


def newton_of(parts):
    return pl.pallas_call(
        newton_kernel,
        out_shape=jax.ShapeDtypeStruct(parts[0].shape, BF16),
        in_specs=vmem_specs(len(parts)),
        out_specs=pl.BlockSpec(memory_space=pltpu.VMEM),
        compiler_params=params(8),
    )(*parts)


def bias_kernel(places, mine, theirs, rot_mine, rot_theirs, *refs):
    inverses, out, greens = refs[:-2], refs[-2], refs[-1]
    count = len(inverses)
    rows, electrons = mine.shape[1], mine.shape[2]
    vectors = rot_mine.shape[0]
    index = lax.axis_index("chol")
    z, base = index // 4, lax.rem(index, 2) * count
    for at in range(count):
        walker = base + (lax.rem(z + (count - at), count) if places else at)
        both = jnp.concatenate([mine[walker], theirs[walker]], axis=0)
        product = jnp.dot(both, inverses[at][...], preferred_element_type=F32).astype(BF16)
        greens[:, :, at] = product.reshape(2, rows // BLOCK, BLOCK, electrons)
    total = jnp.zeros((vectors * BLOCK, count * BLOCK), F32)
    for half, rot in enumerate((rot_mine, rot_theirs)):
        for block in range(rows // BLOCK):
            total += lax.dot_general(
                rot[:, block * BLOCK : (block + 1) * BLOCK, :].reshape(vectors * BLOCK, electrons),
                greens[half, block].reshape(count * BLOCK, electrons),
                (((1,), (1,)), ((), ())),
                preferred_element_type=F32,
            )
    same = lax.rem(lax.broadcasted_iota(jnp.int32, total.shape, 0), BLOCK) == lax.rem(
        lax.broadcasted_iota(jnp.int32, total.shape, 1), BLOCK
    )
    summed = jnp.sum(
        jnp.where(same, total, 0.0).reshape(vectors, BLOCK, count * BLOCK), axis=1
    )
    shape = (count, count * BLOCK)
    walker = lax.broadcasted_iota(jnp.int32, shape, 0)
    place = lax.rem(lax.rem(z, count) + (count - walker), count) if places else walker
    pick = (lax.broadcasted_iota(jnp.int32, shape, 1) // BLOCK == place).astype(F32)
    out[...] = lax.dot_general(
        pick, summed, (((1,), (1,)), ((), ())), precision=HIGHEST, preferred_element_type=F32
    )


def bias_of(mine, theirs, rot_mine, rot_theirs, inverses, places):
    _, rows, electrons = mine.shape
    count = len(inverses)
    vectors = rot_mine.shape[0]
    return pl.pallas_call(
        functools.partial(bias_kernel, places),
        out_shape=jax.ShapeDtypeStruct((count, vectors), F32),
        in_specs=vmem_specs(4 + count),
        out_specs=pl.BlockSpec(memory_space=pltpu.VMEM),
        scratch_shapes=[pltpu.VMEM((2, rows // BLOCK, count, BLOCK, electrons), BF16)],
        compiler_params=params(12),
        cost_estimate=pl.CostEstimate(
            flops=4 * count * rows * electrons * (electrons + vectors * BLOCK),
            bytes_accessed=4 * (vectors + count) * rows * electrons,
            transcendentals=0,
        ),
    )(mine, theirs, rot_mine, rot_theirs, *inverses)


def potential_kernel(origins, layout, order, fields, source, *refs):
    pieces = refs[: len(origins)]
    cholesky, bias_out, potential, weights = refs[len(origins) :]
    per_group, vectors = fields.shape
    half = pieces[0].shape[0]
    step = pl.program_id(0)

    @pl.when(step == 0)
    def _():
        group = lax.axis_index("walk")
        b = lax.rem(lax.axis_index("chol"), 2)
        wanted = source[...]
        bias = jnp.zeros((per_group, vectors), F32)
        for (dw, db), piece in zip(origins, pieces):
            from_group = lax.rem(group + (layout.walk - dw), layout.walk)
            from_b = b + db - 2 * b * db
            base = from_group * per_group + from_b * half
            for row in range(half):
                bias += jnp.where(wanted == base + row, piece[row : row + 1, :], 0.0)
        bias = TAU_ROOT * bias
        bias_out[...] = bias
        shifted = (fields[...] - bias).astype(BF16)
        tall = (per_group * BLOCK, per_group)
        slot = jnp.zeros((per_group * BLOCK, 1), jnp.int32)
        place = lax.broadcasted_iota(jnp.int32, slot.shape, 0) // BLOCK
        for at in range(per_group):
            slot = jnp.where(place == at, order[at], slot)
        rows = (lax.broadcasted_iota(jnp.int32, tall, 1) == slot).astype(BF16)
        wide = (vectors, vectors * BLOCK)
        columns = (
            lax.broadcasted_iota(jnp.int32, wide, 1) // BLOCK
            == lax.broadcasted_iota(jnp.int32, wide, 0)
        ).astype(BF16)
        spread = jnp.dot(rows, shifted, preferred_element_type=F32).astype(BF16)
        spread = jnp.dot(spread, columns, preferred_element_type=F32)
        same = lax.rem(lax.broadcasted_iota(jnp.int32, spread.shape, 0), BLOCK) == lax.rem(
            lax.broadcasted_iota(jnp.int32, spread.shape, 1), BLOCK
        )
        weights[...] = jnp.where(same, spread, 0.0).astype(BF16)

    block = cholesky[...].reshape(vectors * BLOCK, cholesky.shape[2])
    result = TAU_ROOT * jnp.dot(weights[...], block, preferred_element_type=F32)
    potential[...] = result.astype(BF16).reshape(potential.shape)


def potential_of(layout, order, fields, source, pieces, cholesky):
    per_group, vectors = fields.shape
    rows, orbitals = cholesky.shape[1], cholesky.shape[2]
    origins = [origin for origin, _ in pieces]
    arrays = [array for _, array in pieces]

    def whole(array):
        return pl.BlockSpec(array.shape, lambda step: (0, 0))

    return pl.pallas_call(
        functools.partial(potential_kernel, origins, layout),
        grid=(rows // BLOCK,),
        out_shape=[
            jax.ShapeDtypeStruct((per_group, vectors), F32),
            jax.ShapeDtypeStruct((per_group, rows, orbitals), BF16),
        ],
        in_specs=[pl.BlockSpec(memory_space=pltpu.SMEM)]
        + [whole(a) for a in (fields, source, *arrays)]
        + [pl.BlockSpec((vectors, BLOCK, orbitals), lambda step: (0, step, 0))],
        out_specs=[
            pl.BlockSpec((per_group, vectors), lambda step: (0, 0)),
            pl.BlockSpec((per_group, BLOCK, orbitals), lambda step: (0, step, 0)),
        ],
        scratch_shapes=[pltpu.VMEM((per_group * BLOCK, vectors * BLOCK), BF16)],
        compiler_params=params(12),
        cost_estimate=pl.CostEstimate(
            flops=2 * per_group * vectors * rows * BLOCK * orbitals,
            bytes_accessed=2 * (vectors + per_group) * rows * orbitals,
            transcendentals=0,
        ),
    )(order, fields, source, *arrays, cholesky)


def plane_copies(planes, buffer, semaphores, walker):
    b = lax.rem(lax.axis_index("chol"), 2)
    return [
        pltpu.make_async_copy(
            plane.at[walker], buffer.at[walker, :, core], semaphores.at[number, walker]
        )
        for number, (plane, core) in enumerate(zip(planes, (b, 1 - b)))
    ]


def gathered_walker(planes, buffer, semaphores):
    step = pl.program_id(0)

    @pl.when(step == 0)
    def _():
        for walker in range(buffer.shape[0]):
            for copy in plane_copies(planes, buffer, semaphores, walker):
                copy.start()

    for copy in plane_copies(planes, buffer, semaphores, step):
        copy.wait()
    walker = buffer[step]
    return walker.reshape(-1, walker.shape[-1])


def first_kernel(potential, *refs):
    planes, (rounded, base, buffer, semaphores) = refs[:2], refs[2:]
    walker = gathered_walker(planes, buffer, semaphores)
    term = jnp.dot(potential[0], walker, preferred_element_type=F32)
    index = lax.axis_index("chol")
    own = buffer[pl.program_id(0), index // 2, lax.rem(index, 2)]
    rounded[0] = term.astype(BF16)
    base[0] = own.astype(F32) + term


def second_kernel(order, potential, base, *refs):
    del order
    planes, (out, buffer, semaphores) = refs[:2], refs[-3:]
    walker = gathered_walker(planes, buffer, semaphores)
    term = jnp.dot(potential[0], walker, preferred_element_type=F32)
    out[0] = (base[0] + 0.5 * term).astype(BF16)


def fold_cost(count, rows, orbitals, electrons):
    return pl.CostEstimate(
        flops=2 * count * rows * orbitals * electrons,
        bytes_accessed=2 * count * orbitals * (rows + electrons),
        transcendentals=0,
    )


def first_of(part, potential, planes):
    count, _, rows, electrons = planes[0].shape
    orbitals = potential.shape[2]
    out_spec = pl.BlockSpec((1, rows, electrons), lambda step: (step, 0, 0))
    return pl.pallas_call(
        first_kernel,
        grid=(count,),
        out_shape=[
            jax.ShapeDtypeStruct((count, rows, electrons), BF16),
            jax.ShapeDtypeStruct((count, rows, electrons), F32),
        ],
        in_specs=[pl.BlockSpec((1, rows, orbitals), lambda step: (part * count + step, 0, 0))]
        + [pl.BlockSpec(memory_space=pl.ANY)] * 2,
        out_specs=[out_spec, out_spec],
        scratch_shapes=[
            pltpu.VMEM((count, orbitals // (2 * rows), 2, rows, electrons), BF16),
            pltpu.SemaphoreType.DMA((2, count)),
        ],
        compiler_params=params(10),
        cost_estimate=fold_cost(count, rows, orbitals, electrons),
    )(potential, *planes)


def second_of(part, potential, base, planes, order, previous):
    count, _, rows, electrons = planes[0].shape
    per_group, _, orbitals = potential.shape
    extra = [] if previous is None else [previous]
    inputs = [order, potential, base, *planes, *extra]
    return pl.pallas_call(
        second_kernel,
        out_shape=jax.ShapeDtypeStruct((per_group, rows, electrons), BF16),
        grid_spec=pltpu.PrefetchScalarGridSpec(
            num_scalar_prefetch=1,
            grid=(count,),
            in_specs=[
                pl.BlockSpec((1, rows, orbitals), lambda step, order: (part * count + step, 0, 0)),
                pl.BlockSpec((1, rows, electrons), lambda step, order: (step, 0, 0)),
            ]
            + [pl.BlockSpec(memory_space=pl.ANY)] * (2 + len(extra)),
            out_specs=pl.BlockSpec(
                (1, rows, electrons), lambda step, order: (order[part * count + step], 0, 0)
            ),
            scratch_shapes=[
                pltpu.VMEM((count, orbitals // (2 * rows), 2, rows, electrons), BF16),
                pltpu.SemaphoreType.DMA((2, count)),
            ],
        ),
        input_output_aliases={} if previous is None else {len(inputs) - 1: 0},
        compiler_params=params(10),
        cost_estimate=fold_cost(count, rows, orbitals, electrons),
    )(*inputs)


def split_kernel(source, walkers, staying, leaving, order, picked, semaphores):
    per_group = walkers.shape[0]
    half = per_group // 2
    group = lax.axis_index("walk")
    counts = [jnp.int32(0), jnp.int32(0)]
    for slot in range(per_group):
        local = source[group * per_group + slot] - group * per_group
        stays = ((local >= 0) & (local < per_group)).astype(jnp.int32)
        place = jnp.where(stays == 1, counts[0], half + counts[1])
        place = jnp.minimum(place, per_group - 1)
        order[place] = jnp.int32(slot)
        picked[place] = jnp.where(stays == 1, local, 0)
        counts = [counts[0] + stays, counts[1] + 1 - stays]
    sent = jnp.int32(0)
    for slot in range(per_group):
        local = source[(1 - group) * per_group + slot] - group * per_group
        goes = ((local >= 0) & (local < per_group)).astype(jnp.int32)
        place = jnp.where(goes == 1, half + jnp.minimum(sent, half - 1), per_group)
        picked[place] = local
        sent = sent + goes
    copies = []
    for place in range(per_group):
        target = (leaving if place >= half else staying).at[place % half]
        copies.append(
            pltpu.make_async_copy(walkers.at[picked[place]], target, semaphores.at[place])
        )
    for copy in copies[half:] + copies[:half]:
        copy.start()
    for copy in copies:
        copy.wait()


def split_walkers(walkers, source):
    per_group, rows, electrons = walkers.shape
    half = jax.ShapeDtypeStruct((per_group // 2, rows, electrons), walkers.dtype)
    return pl.pallas_call(
        split_kernel,
        out_shape=[half, half, jax.ShapeDtypeStruct((per_group,), jnp.int32)],
        in_specs=[pl.BlockSpec(memory_space=pltpu.SMEM), pl.BlockSpec(memory_space=pl.ANY)],
        out_specs=[pl.BlockSpec(memory_space=pl.ANY)] * 2
        + [pl.BlockSpec(memory_space=pltpu.SMEM)],
        scratch_shapes=[
            pltpu.SMEM((per_group + 1,), jnp.int32),
            pltpu.SemaphoreType.DMA((per_group,)),
        ],
        compiler_params=params(4),
    )(source, walkers)


def ranks(flags):
    count = flags.shape[-1]
    before = jnp.arange(count)[None, :] < jnp.arange(count)[:, None]
    return jnp.sum(jnp.where(before & flags[..., None, :], 1, 0), axis=-1)


def migrate(layout, walkers, source):
    per_group = walkers.shape[0]
    half = per_group // 2
    group = lax.axis_index("walk")
    if layout.walk == 2:
        staying, leaving, order = split_walkers(walkers, source)
        return [staying, lax.ppermute(leaving, "walk", [(0, 1), (1, 0)])], order
    table = source.reshape(layout.walk, per_group)
    incoming = lax.dynamic_index_in_dim(table, group, 0, keepdims=False)
    incoming_groups = incoming // per_group

    def outgoing(distance):
        row = lax.dynamic_index_in_dim(table, (group + distance) % layout.walk, 0, keepdims=False)
        local = row - group * per_group
        here = (local >= 0) & (local < per_group)
        match = here[None, :] & (ranks(here)[None, :] == jnp.arange(half)[:, None])
        return jnp.take(walkers, jnp.sum(jnp.where(match, local[None, :], 0), axis=1), axis=0)

    arrived = [outgoing(0)]
    for distance in range(1, layout.walk):
        pairs = [(g, (g + distance) % layout.walk) for g in range(layout.walk)]
        arrived.append(lax.ppermute(outgoing(distance), "walk", pairs))
    slots = jnp.arange(per_group)
    same = (incoming_groups[:, None] == incoming_groups[None, :]) & (slots[None, :] < slots[:, None])
    rank = jnp.sum(same.astype(jnp.int32), axis=1)
    distance = (group - incoming_groups) % layout.walk
    migrated = jnp.take(jnp.concatenate(arrived, axis=0), distance * half + rank, axis=0)
    return [migrated[:half], migrated[half:]], slots.astype(jnp.int32)


def shards(layout, walkers, trial, cholesky, rotated, fields, source):
    per_group = walkers.shape[0]
    half = per_group // 2
    group = lax.axis_index("walk")

    trial_theirs = layout.shift(trial, db=1)
    theirs = layout.shift(walkers, db=1)
    rot_theirs = layout.shift(rotated, db=1)
    halves, order = migrate(layout, walkers, source)
    places = layout.z == half
    partial = intersections_of(walkers, theirs, trial, trial_theirs, places)
    if places:
        total = partial[0]
        for dz in range(1, half):
            total = total + layout.shift(partial[dz], dz=dz).astype(F32)
        total, halves[1] = lax.optimization_barrier((total, halves[1]))
        other = layout.shift(total.astype(BF16), dy=1)
        inverse = newton_of([total, other])
        inverses = [inverse] + [layout.shift(inverse, dz=dz) for dz in range(1, half)]
    else:
        b = lax.axis_index("chol") % 2
        spread = jnp.zeros((per_group,) + partial[0].shape, F32)
        spread = lax.dynamic_update_slice_in_dim(spread, jnp.stack(partial), b * half, 0)
        summed = lax.dynamic_slice_in_dim(lax.psum(spread, "chol"), b * half, half, 0)
        inverses = [newton_of([summed[index]]) for index in range(half)]
    total = bias_of(walkers, theirs, rotated, rot_theirs, inverses, places)
    distance = layout.z // 2
    while distance:
        total = total + layout.swap(total, distance)
        distance //= 2
    total = total + layout.shift(total, dy=1)
    planes = [layout.gather_plane(piece) for piece in halves]
    total, planes[0] = lax.optimization_barrier((total, planes[0]))
    pieces = []
    for dw in range(layout.walk):
        for db in range(2):
            moved = layout.shift_all(total, dw, db) if dw + db else total
            pieces.append(((dw, db), moved))

    wanted = lax.dynamic_slice_in_dim(source, group * per_group, per_group)[:, None]
    force_bias, potential = potential_of(layout, order, fields, wanted, pieces, cholesky)

    rows = walkers.shape[1]
    bases, seconds = [], []
    for part in range(2):
        both = layout.with_sibling(planes[part], rows)
        rounded, base = first_of(part, potential, both)
        bases.append(base)
        seconds.append(layout.gather_plane(rounded))
    out = None
    for part in range(2):
        both = layout.with_sibling(seconds[part], rows)
        out = second_of(part, potential, bases[part], both, order, out)
    return out, force_bias


def solution(mesh):
    in_specs = (
        P("walk", "chol", None),
        P("chol", None),
        P(None, "chol", None),
        P(None, "chol", None),
        P("walk", None),
        P(),
    )
    out_specs = (P("walk", "chol", None), P("walk", None))
    layout = Layout(mesh.shape["walk"], mesh.shape["chol"])
    return jax.shard_map(
        functools.partial(shards, layout),
        mesh=mesh,
        in_specs=in_specs,
        out_specs=out_specs,
        check_vma=False,
    )
```

time: 196 us -> 245 us (1.25)
  waiting for transfers between devices: 77.8 us -> 165 us
  starting transfers between devices: 59.7 us -> 22.4 us
  Pallas kernels: 39.1 us -> 26.4 us
  between operations: 1.31 us -> 13.9 us
    all_gather x0 -> x4, waiting for transfers between devices: none -> 108 us  [gather_plane(): lax.all_gather(piece, 'chol', axis_index_groups=planes, axis=1, tiled=True)]
    ppermute x73 -> x15, starting transfers between devices: 53.2 us -> 18.5 us  [shift(): return lax.ppermute(array, 'chol', pairs)]
    ppermute x73 -> x15, waiting for transfers between devices: 75.1 us -> 46.3 us  [shift(): return lax.ppermute(array, 'chol', pairs)]
    pallas_call x5 -> x6, Pallas kernels: 26.1 us -> 17.4 us  [the longest x2 6.34 us: second_of(): pl.pallas_call(second_kernel, out_shape=jax.ShapeDtypeStruct((per_group,...]
    unnamed x86 -> x32, local copies, waits for them, and re-layouts: 10.3 us -> 17 us
    ppermute x1 -> x3, waiting for transfers between devices: 1.8 us -> 8.07 us  [the longest x2 8.06 us: swap(): return lax.ppermute(array, 'chol', pairs)]
    pallas_call x1, Pallas kernels: 10.4 us -> 6.36 us  [potential_of(): pl.pallas_call(functools.partial(potential_kernel, origins, layout), grid...]
    gather x2 -> x0, local copies, waits for them, and re-layouts: 3.22 us -> none  [outgoing(): jnp.take(walkers, jnp.sum(jnp.where(match, local[None, :], 0), axis=1), a...]
  transfers between devices with their start and end apart: 81 -> 25, of which waited for: 25 -> 17; matrix products, arithmetic and copies ran while one was open for 3% -> 0% of each run, Pallas kernels for 17% -> 9%
where the time goes in v2:
time: 245 us
  waiting for transfers between devices  165 us (67%)
  Pallas kernels  26.4 us (11%)
  starting transfers between devices  22.4 us (9%)
  local copies, waits for them, and re-layouts  17.2 us (7%)
  between operations  13.9 us (6%)
    all_gather x4, waiting for transfers between devices, gather_plane(): lax.all_gather(piece, 'chol', axis_index_groups=planes, axis=1, tiled=True)  108 us
    ppermute x15, waiting for transfers between devices, shift(): return lax.ppermute(array, 'chol', pairs)  46.3 us
    ppermute x15, starting transfers between devices, shift(): return lax.ppermute(array, 'chol', pairs)  18.5 us
    unnamed x32, local copies, waits for them, and re-layouts  17 us
    ppermute x2, waiting for transfers between devices, swap(): return lax.ppermute(array, 'chol', pairs)  8.06 us
    pallas_call x1, Pallas kernels, potential_of(): pl.pallas_call(functools.partial(potential_kernel, origins, layout), grid...  6.36 us
    pallas_call x2, Pallas kernels, second_of(): pl.pallas_call(second_kernel, out_shape=jax.ShapeDtypeStruct((per_group,...  6.34 us
    pallas_call x2, Pallas kernels, first_of(): pl.pallas_call(first_kernel, grid=(count,), out_shape=[jax.ShapeDtypeStru...  5.75 us
  transfers between devices with their start and end apart: 25, of which 17 were waited for; matrix products, arithmetic and copies ran while one was open for 0% of the time, Pallas kernels for 9%

profile of v2, /device:TPU:0, one launch (start us, length us, event | category | flops | bytes accessed | tf_op | source)
XLA Modules:
  0.0 244.9 jit_solution(9944550575811563154)
XLA Ops:
  7.2 0.0 all-gather.5.cloned.1.call-start
  7.2 0.0 copy-start.4
  7.2 1.0 copy-done.4
  8.3 0.7 copy-done.14
  8.9 2.1 shard_map.77
  11.0 0.0 all-gather.5.cloned.1.call-update
  11.0 0.0 all-gather.7.cloned.1.call-start
  11.1 0.5 collective-permute-start
  11.6 0.1 collective-permute-start.1
  11.7 0.4 collective-permute-start.2
  12.1 1.4 collective-permute-done.2.trial_theirs
  13.5 1.0 copy-done.5
  14.6 0.8 copy-done.12
  15.4 0.5 shard_map.78
  15.9 3.0 %collective-permute-start.3 = (bf16[256,256]{1,0:T(8,128)(2,1)S(1)}, bf16[256,256]{1,0:T(8,128)(2,1)S(1)}, u32[]{:S(2)}, u32[]{:S(2)}) collective-permute-start(bf16[256,256]{1,0:T(8,128)(2,1)S(1)} %get-tuple-element.21), channel_id=1, source_target_pairs={{0,4},{1,5},{2,6},{3,7},{4,8},{5,9},{6,10},{7,11},{8,12},{9,13},{1... | collective-permute-start | bytes 393224 | tf_op jit(solution)/shard_map/ppermute | solution.py:40
  18.9 2.6 %collective-permute-start.4 = (bf16[256,256]{1,0:T(8,128)(2,1)S(1)}, bf16[256,256]{1,0:T(8,128)(2,1)S(1)}, u32[]{:S(2)}, u32[]{:S(2)}) collective-permute-start(bf16[256,256]{1,0:T(8,128)(2,1)S(1)} %get-tuple-element.22), channel_id=1, source_target_pairs={{0,8},{1,9},{2,10},{3,11},{4,12},{5,13},{6,14},{7,15},{8,0},{9,1},... | collective-permute-start | bytes 393224 | tf_op jit(solution)/shard_map/ppermute | solution.py:40
  21.4 1.3 collective-permute-start.5
  22.8 1.5 collective-permute-start.6
  24.3 1.0 collective-permute-done.3
  25.3 10.0 %collective-permute-done.4 = bf16[256,256]{1,0:T(8,128)(2,1)S(1)} collective-permute-done((bf16[256,256]{1,0:T(8,128)(2,1)S(1)}, bf16[256,256]{1,0:T(8,128)(2,1)S(1)}, u32[]{:S(2)}, u32[]{:S(2)}) %collective-permute-start.4) | collective-permute-done | bytes 131104 | tf_op jit(solution)/shard_map/ppermute | solution.py:40
  35.3 0.0 collective-permute-done.5
  35.3 0.1 convert_add_fusion.refs_0_
  35.4 0.0 all-gather.7.cloned.1.call-update
  35.4 0.0 all-gather.11.cloned.1.call-start
  35.5 2.0 collective-permute-start.7
  37.5 3.3 %collective-permute-done.7.refs_1_ = bf16[256,256]{1,0:T(8,128)(2,1)S(1)} collective-permute-done((bf16[256,256]{1,0:T(8,128)(2,1)S(1)}, bf16[256,256]{1,0:T(8,128)(2,1)S(1)}, u32[]{:S(2)}, u32[]{:S(2)}) %collective-permute-start.7) | collective-permute-done | bytes 131104 | tf_op jit(solution)/shard_map/ppermute | solution.py:40
  40.8 2.2 shard_map.79.refs_0_
  43.0 0.0 copy-start.15
  43.0 0.0 copy-start.13
  43.0 6.9 %collective-permute-start.10 = (bf16[256,256]{1,0:T(8,128)(2,1)S(1)}, bf16[256,256]{1,0:T(8,128)(2,1)S(1)}, u32[]{:S(2)}, u32[]{:S(2)}) collective-permute-start(bf16[256,256]{1,0:T(8,128)(2,1)S(1)} %shard_map.79.refs_0_), channel_id=1, source_target_pairs={{0,12},{1,13},{2,14},{3,15},{4,0},{5,1},{6,2},{7,3},{8,4},{9,5},{1... | collective-permute-start | bytes 393224 | tf_op jit(solution)/shard_map/ppermute | solution.py:40
  49.9 0.0 collective-permute-start.8
  49.9 0.6 collective-permute-start.9
  50.6 6.2 %collective-permute-done.10.refs_3_ = bf16[256,256]{1,0:T(8,128)(2,1)S(1)} collective-permute-done((bf16[256,256]{1,0:T(8,128)(2,1)S(1)}, bf16[256,256]{1,0:T(8,128)(2,1)S(1)}, u32[]{:S(2)}, u32[]{:S(2)}) %collective-permute-start.10) | collective-permute-done | bytes 131104 | tf_op jit(solution)/shard_map/ppermute | solution.py:40
  56.7 4.6 %collective-permute-done.8.refs_1_ = bf16[256,256]{1,0:T(8,128)(2,1)S(1)} collective-permute-done((bf16[256,256]{1,0:T(8,128)(2,1)S(1)}, bf16[256,256]{1,0:T(8,128)(2,1)S(1)}, u32[]{:S(2)}, u32[]{:S(2)}) %collective-permute-start.8) | collective-permute-done | bytes 131104 | tf_op jit(solution)/shard_map/ppermute | solution.py:40
  61.4 12.8 %collective-permute-done.9.refs_2_ = bf16[256,256]{1,0:T(8,128)(2,1)S(1)} collective-permute-done((bf16[256,256]{1,0:T(8,128)(2,1)S(1)}, bf16[256,256]{1,0:T(8,128)(2,1)S(1)}, u32[]{:S(2)}, u32[]{:S(2)}) %collective-permute-start.9) | collective-permute-done | bytes 131104 | tf_op jit(solution)/shard_map/ppermute | solution.py:40
  74.1 3.2 %shard_map.80 = f32[4,32]{1,0:T(4,128)S(1)} custom-call(bf16[8,128,256]{2,1,0:T(8,128)(2,1)S(1)} %copy-done.6, bf16[8,128,256]{2,1,0:T(8,128)(2,1)S(1)} %collective-permute-done.theirs, bf16[32,128,256]{2,1,0:T(8,128)(2,1)S(1)} %copy-done.9, bf16[32,128,256]{2,1,0:T(8,128)(2,1)} %collective-permute-done.1.rot_theirs, ...), custom_call_target="tpu_custom_call" | custom-call | flops 402653184 | bytes 4718592 | tf_op jit(solution)/shard_map/pallas_call | solution.py:160
  77.4 4.5 %collective-permute-done.11 = f32[4,32]{1,0:T(4,128)S(1)} collective-permute-done((f32[4,32]{1,0:T(4,128)S(1)}, f32[4,32]{1,0:T(4,128)S(1)}, u32[]{:S(2)}, u32[]{:S(2)}) %collective-permute-start.11) | collective-permute-done | bytes 544 | tf_op jit(solution)/shard_map/ppermute | solution.py:52
  81.9 3.6 %collective-permute-done.12 = f32[4,32]{1,0:T(4,128)S(1)} collective-permute-done((f32[4,32]{1,0:T(4,128)S(1)}, f32[4,32]{1,0:T(4,128)S(1)}, u32[]{:S(2)}, u32[]{:S(2)}) %collective-permute-start.12) | collective-permute-done | bytes 544 | tf_op jit(solution)/shard_map/ppermute | solution.py:52
  85.5 1.0 collective-permute-start.13
  86.5 2.6 %collective-permute-done.13 = f32[4,32]{1,0:T(4,128)S(1)} collective-permute-done((f32[4,32]{1,0:T(4,128)S(1)}, f32[4,32]{1,0:T(4,128)S(1)}, u32[]{:S(2)}, u32[]{:S(2)}) %collective-permute-start.13) | collective-permute-done | bytes 544 | tf_op jit(solution)/shard_map/ppermute | solution.py:40
  89.1 0.5 collective-permute-start.14
  89.6 1.7 collective-permute-start.15
  91.3 0.1 dynamic-slice_bitcast_fusion
  91.3 0.1 copy.9.source
  91.4 1.4 collective-permute-done.14.refs_1_
  92.8 0.3 collective-permute-done.15.refs_2_
  93.2 1.1 collective-permute-done.16.refs_3_
  94.3 5.8 %copy-done.3 = bf16[32,128,2048]{2,1,0:T(8,128)(2,1)S(1)} copy-done((bf16[32,128,2048]{2,1,0:T(8,128)(2,1)S(1)}, bf16[32,128,2048]{2,1,0:T(8,128)(2,1)}, u32[]{:S(2)}) %copy-start.3) | copy-done | bytes 16777240
  100.1 6.4 %shard_map.81 = (f32[8,32]{1,0:T(8,128)}, bf16[8,128,2048]{2,1,0:T(8,128)(2,1)S(1)}) custom-call(s32[8]{0:T(128)S(1)} %get-tuple-element.19.order, f32[8,32]{1,0:T(8,128)S(1)} %copy-done.13, s32[8,1]{1,0:T(8,128)S(1)} %copy.9.source, f32[4,32]{1,0:T(4,128)S(1)} %add.27.refs_0_, f32[4,32]{1,0:T(4,128)S(1)} %collective-permute-done.14.refs_1_, ...), custom_call_target="tpu_custom_call" | custom-call | flops 2147483648 | bytes 20971520 | tf_op jit(solution)/shard_map/pallas_call | solution.py:229
  106.5 3.1 %shard_map.83 = (bf16[4,128,256]{2,1,0:T(8,128)(2,1)}, f32[4,128,256]{2,1,0:T(8,128)S(1)}) custom-call(bf16[8,128,2048]{2,1,0:T(8,128)(2,1)S(1)} %get-tuple-element.28.potential, bf16[4,8,128,256]{3,2,1,0:T(8,128)(2,1)S(1)} %bitcast.14, bf16[4,8,128,256]{3,2,1,0:T(8,128)(2,1)S(1)} %bitcast.16), custom_call_target="tpu_custom_call" | custom-call | flops 536870912 | bytes 6291456 | tf_op jit(solution)/shard_map/pallas_call | solution.py:308
  109.6 0.0 all-gather.11.cloned.1.call-update
  109.7 0.0 all-gather.9.cloned.1.call-start
  109.7 18.1 %all-gather.7.cloned.1.call-done = bf16[4,1024,256]{2,1,0:T(8,128)(2,1)} async-done(((bf16[4,128,256]{2,1,0:T(8,128)(2,1)}), bf16[4,1024,256]{2,1,0:T(8,128)(2,1)}) %all-gather.7.cloned.1.call-update) | async-done | bytes 2097168 | tf_op jit(solution)/shard_map/all_gather | solution.py:56
  127.8 4.4 %collective-permute-done.17 = bf16[4,1024,256]{2,1,0:T(8,128)(2,1)S(1)} collective-permute-done((bf16[4,1024,256]{2,1,0:T(8,128)(2,1)}, bf16[4,1024,256]{2,1,0:T(8,128)(2,1)S(1)}, u32[]{:S(2)}, u32[]{:S(2)}) %collective-permute-start.17) | collective-permute-done | bytes 2097184 | tf_op jit(solution)/shard_map/ppermute | solution.py:40
  132.2 2.2 copy-done.1
  134.4 1.7 copy-done.11
  136.0 2.6 %shard_map.82 = (bf16[4,128,256]{2,1,0:T(8,128)(2,1)}, f32[4,128,256]{2,1,0:T(8,128)S(1)}) custom-call(bf16[8,128,2048]{2,1,0:T(8,128)(2,1)S(1)} %copy-done.1, bf16[4,8,128,256]{3,2,1,0:T(8,128)(2,1)S(1)} %bitcast.15, bf16[4,8,128,256]{3,2,1,0:T(8,128)(2,1)S(1)} %bitcast.17), custom_call_target="tpu_custom_call" | custom-call | flops 536870912 | bytes 6291456 | tf_op jit(solution)/shard_map/pallas_call | solution.py:308
  138.7 0.0 all-gather.9.cloned.1.call-update
  138.7 39.1 %all-gather.11.cloned.1.call-done = bf16[4,1024,256]{2,1,0:T(8,128)(2,1)} async-done(((bf16[4,128,256]{2,1,0:T(8,128)(2,1)}), bf16[4,1024,256]{2,1,0:T(8,128)(2,1)}) %all-gather.11.cloned.1.call-update) | async-done | bytes 2097168 | tf_op jit(solution)/shard_map/all_gather | solution.py:56
  177.8 50.4 %all-gather.9.cloned.1.call-done = bf16[4,1024,256]{2,1,0:T(8,128)(2,1)} async-done(((bf16[4,128,256]{2,1,0:T(8,128)(2,1)}), bf16[4,1024,256]{2,1,0:T(8,128)(2,1)}) %all-gather.9.cloned.1.call-update) | async-done | bytes 2097168 | tf_op jit(solution)/shard_map/all_gather | solution.py:56
  228.2 2.2 copy-done.2
  230.4 1.6 copy-done.7
  232.0 3.2 %shard_map.84.refs_2_ = bf16[8,128,256]{2,1,0:T(8,128)(2,1)} custom-call(s32[8]{0:T(128)S(1)} %get-tuple-element.19.order, bf16[8,128,2048]{2,1,0:T(8,128)(2,1)S(1)} %copy-done.2, f32[4,128,256]{2,1,0:T(8,128)S(1)} %get-tuple-element.33.base, bf16[4,8,128,256]{3,2,1,0:T(8,128)(2,1)S(1)} %bitcast.10, bf16[4,8,128,256]{3,2,1,0:T(8,128)(2,1)S(1)} %bitcast.13), custom_call_target="tpu_custom_call" | custom-call | flops 536870912 | bytes 6291456 | tf_op jit(solution)/shard_map/pallas_call | solution.py:332
  235.2 3.2 %shard_map.85 = bf16[8,128,256]{2,1,0:T(8,128)(2,1)} custom-call(s32[8]{0:T(128)S(1)} %get-tuple-element.19.order, bf16[8,128,2048]{2,1,0:T(8,128)(2,1)S(1)} %copy-done.2, f32[4,128,256]{2,1,0:T(8,128)S(1)} %get-tuple-element.30.base, bf16[4,8,128,256]{3,2,1,0:T(8,128)(2,1)S(1)} %bitcast.11, ...), custom_call_target="tpu_custom_call", output_to_operand_aliasing={{}: (5, {})} | custom-call | flops 536870912 | bytes 6291456 | tf_op jit(solution)/shard_map/pallas_call | solution.py:332
  (38 shorter events, 0.1 us)
Async XLA Ops:
  7.2 81.9 %all-gather.5.cloned.1.call-start = ((), (), s32[]{:S(2)}) async-start(), calls=%async_computation | async-start | bytes 2359296 | tf_op jit(solution)/shard_map/all_gather | solution.py:56
  7.2 1.0 copy-start.4
  8.3 0.7 copy-start.14
  8.9 65.2 %copy-start.6 = (bf16[8,128,256]{2,1,0:T(8,128)(2,1)S(1)}, bf16[8,128,256]{2,1,0:T(8,128)(2,1)}, u32[]{:S(2)}) copy-start(bf16[8,128,256]{2,1,0:T(8,128)(2,1)} %mine.3) | copy-start | bytes 1572868
  11.0 116.8 %all-gather.7.cloned.1.call-start = ((), (), s32[]{:S(2)}) async-start(), calls=%async_computation.1 | async-start | bytes 2359296 | tf_op jit(solution)/shard_map/all_gather | solution.py:56
  11.1 2.5 %collective-permute-start = (bf16[8,128,256]{2,1,0:T(8,128)(2,1)}, bf16[8,128,256]{2,1,0:T(8,128)(2,1)S(1)}, u32[]{:S(2)}, u32[]{:S(2)}) collective-permute-start(bf16[8,128,256]{2,1,0:T(8,128)(2,1)} %mine.3), channel_id=1, source_target_pairs={{0,1},{1,0},{2,3},{3,2},{4,5},{5,4},{6,7},{7,6},{8,9},{9,8},{10,11... | collective-permute-start | bytes 1572872 | tf_op jit(solution)/shard_map/ppermute | solution.py:40
  11.6 62.5 %collective-permute-start.1 = (bf16[32,128,256]{2,1,0:T(8,128)(2,1)}, bf16[32,128,256]{2,1,0:T(8,128)(2,1)}, u32[]{:S(2)}, u32[]{:S(2)}) collective-permute-start(bf16[32,128,256]{2,1,0:T(8,128)(2,1)} %rot_mine.1), channel_id=1, source_target_pairs={{0,1},{1,0},{2,3},{3,2},{4,5},{5,4},{6,7},{7,6},{8,9},{9,8},{10,11... | collective-permute-start | bytes 6291464 | tf_op jit(solution)/shard_map/ppermute | solution.py:40
  11.7 1.9 collective-permute-start.2
  13.5 1.0 copy-start.5
  14.6 0.8 copy-start.12
  15.4 58.7 %copy-start.9 = (bf16[32,128,256]{2,1,0:T(8,128)(2,1)S(1)}, bf16[32,128,256]{2,1,0:T(8,128)(2,1)}, u32[]{:S(2)}) copy-start(bf16[32,128,256]{2,1,0:T(8,128)(2,1)} %rot_mine.1) | copy-start | bytes 6291460
  15.9 9.4 %collective-permute-start.3 = (bf16[256,256]{1,0:T(8,128)(2,1)S(1)}, bf16[256,256]{1,0:T(8,128)(2,1)S(1)}, u32[]{:S(2)}, u32[]{:S(2)}) collective-permute-start(bf16[256,256]{1,0:T(8,128)(2,1)S(1)} %get-tuple-element.21), channel_id=1, source_target_pairs={{0,4},{1,5},{2,6},{3,7},{4,8},{5,9},{6,10},{7,11},{8,12},{9,13},{1... | collective-permute-start | bytes 393224 | tf_op jit(solution)/shard_map/ppermute | solution.py:40
  18.9 16.4 %collective-permute-start.4 = (bf16[256,256]{1,0:T(8,128)(2,1)S(1)}, bf16[256,256]{1,0:T(8,128)(2,1)S(1)}, u32[]{:S(2)}, u32[]{:S(2)}) collective-permute-start(bf16[256,256]{1,0:T(8,128)(2,1)S(1)} %get-tuple-element.22), channel_id=1, source_target_pairs={{0,8},{1,9},{2,10},{3,11},{4,12},{5,13},{6,14},{7,15},{8,0},{9,1},... | collective-permute-start | bytes 393224 | tf_op jit(solution)/shard_map/ppermute | solution.py:40
  21.4 13.9 %collective-permute-start.5 = (bf16[256,256]{1,0:T(8,128)(2,1)S(1)}, bf16[256,256]{1,0:T(8,128)(2,1)S(1)}, u32[]{:S(2)}, u32[]{:S(2)}) collective-permute-start(bf16[256,256]{1,0:T(8,128)(2,1)S(1)} %get-tuple-element.23), channel_id=1, source_target_pairs={{0,12},{1,13},{2,14},{3,15},{4,0},{5,1},{6,2},{7,3},{8,4},{9,5},{1... | collective-permute-start | bytes 393224 | tf_op jit(solution)/shard_map/ppermute | solution.py:40
  22.8 12.6 %collective-permute-start.6 = (bf16[4,128,256]{2,1,0:T(8,128)(2,1)}, bf16[4,128,256]{2,1,0:T(8,128)(2,1)}, u32[]{:S(2)}, u32[]{:S(2)}) collective-permute-start(bf16[4,128,256]{2,1,0:T(8,128)(2,1)} %get-tuple-element.24), channel_id=1, source_target_pairs={{0,16},{16,0},{1,17},{17,1},{2,18},{18,2},{3,19},{19,3},{4,20},{20... | collective-permute-start | bytes 786440 | tf_op jit(solution)/shard_map/ppermute | solution.py:418
  35.4 142.4 %all-gather.11.cloned.1.call-start = ((), (), s32[]{:S(2)}) async-start(), calls=%async_computation.3 | async-start | bytes 2359296 | tf_op jit(solution)/shard_map/all_gather | solution.py:56
  35.5 5.3 %collective-permute-start.7 = (bf16[256,256]{1,0:T(8,128)(2,1)S(1)}, bf16[256,256]{1,0:T(8,128)(2,1)S(1)}, u32[]{:S(2)}, u32[]{:S(2)}) collective-permute-start(bf16[256,256]{1,0:T(8,128)(2,1)S(1)} %convert_element_type.15), channel_id=1, source_target_pairs={{0,2},{1,3},{2,0},{3,1},{4,6},{5,7},{6,4},{7,5},{8,10},{9,11},{10,... | collective-permute-start | bytes 393224 | tf_op jit(solution)/shard_map/ppermute | solution.py:40
  43.0 48.3 %copy-start.15 = (s32[16]{0:T(128)S(1)}, s32[16]{0:T(128)}, u32[]{:S(2)}) copy-start(s32[16]{0:T(128)} %source.1) | copy-start | bytes 196
  43.0 51.3 %copy-start.13 = (f32[8,32]{1,0:T(8,128)S(1)}, f32[8,32]{1,0:T(8,128)}, u32[]{:S(2)}) copy-start(f32[8,32]{1,0:T(8,128)} %fields.1) | copy-start | bytes 3076
  43.0 13.7 %collective-permute-start.10 = (bf16[256,256]{1,0:T(8,128)(2,1)S(1)}, bf16[256,256]{1,0:T(8,128)(2,1)S(1)}, u32[]{:S(2)}, u32[]{:S(2)}) collective-permute-start(bf16[256,256]{1,0:T(8,128)(2,1)S(1)} %shard_map.79.refs_0_), channel_id=1, source_target_pairs={{0,12},{1,13},{2,14},{3,15},{4,0},{5,1},{6,2},{7,3},{8,4},{9,5},{1... | collective-permute-start | bytes 393224 | tf_op jit(solution)/shard_map/ppermute | solution.py:40
  49.9 11.4 %collective-permute-start.8 = (bf16[256,256]{1,0:T(8,128)(2,1)S(1)}, bf16[256,256]{1,0:T(8,128)(2,1)S(1)}, u32[]{:S(2)}, u32[]{:S(2)}) collective-permute-start(bf16[256,256]{1,0:T(8,128)(2,1)S(1)} %shard_map.79.refs_0_), channel_id=1, source_target_pairs={{0,4},{1,5},{2,6},{3,7},{4,8},{5,9},{6,10},{7,11},{8,12},{9,13},{1... | collective-permute-start | bytes 393224 | tf_op jit(solution)/shard_map/ppermute | solution.py:40
  49.9 24.2 %collective-permute-start.9 = (bf16[256,256]{1,0:T(8,128)(2,1)S(1)}, bf16[256,256]{1,0:T(8,128)(2,1)S(1)}, u32[]{:S(2)}, u32[]{:S(2)}) collective-permute-start(bf16[256,256]{1,0:T(8,128)(2,1)S(1)} %shard_map.79.refs_0_), channel_id=1, source_target_pairs={{0,8},{1,9},{2,10},{3,11},{4,12},{5,13},{6,14},{7,15},{8,0},{9,1},... | collective-permute-start | bytes 393224 | tf_op jit(solution)/shard_map/ppermute | solution.py:40
  77.4 4.5 %collective-permute-start.11 = (f32[4,32]{1,0:T(4,128)S(1)}, f32[4,32]{1,0:T(4,128)S(1)}, u32[]{:S(2)}, u32[]{:S(2)}) collective-permute-start(f32[4,32]{1,0:T(4,128)S(1)} %shard_map.80), channel_id=1, source_target_pairs={{0,8},{1,9},{2,10},{3,11},{4,12},{5,13},{6,14},{7,15},{8,0},{9,1},... | collective-permute-start | bytes 1544 | tf_op jit(solution)/shard_map/ppermute | solution.py:52
  81.9 3.6 %collective-permute-start.12 = (f32[4,32]{1,0:T(4,128)S(1)}, f32[4,32]{1,0:T(4,128)S(1)}, u32[]{:S(2)}, u32[]{:S(2)}) collective-permute-start(f32[4,32]{1,0:T(4,128)S(1)} %add.25), channel_id=1, source_target_pairs={{0,4},{1,5},{2,6},{3,7},{4,0},{5,1},{6,2},{7,3},{8,12},{9,13},{10,... | collective-permute-start | bytes 1544 | tf_op jit(solution)/shard_map/ppermute | solution.py:52
  85.5 3.6 %collective-permute-start.13 = (f32[4,32]{1,0:T(4,128)S(1)}, f32[4,32]{1,0:T(4,128)S(1)}, u32[]{:S(2)}, u32[]{:S(2)}) collective-permute-start(f32[4,32]{1,0:T(4,128)S(1)} %add.26), channel_id=1, source_target_pairs={{0,2},{1,3},{2,0},{3,1},{4,6},{5,7},{6,4},{7,5},{8,10},{9,11},{10,... | collective-permute-start | bytes 1544 | tf_op jit(solution)/shard_map/ppermute | solution.py:40
  89.1 17.4 %collective-permute-start.19 = (bf16[4,1024,256]{2,1,0:T(8,128)(2,1)}, bf16[4,1024,256]{2,1,0:T(8,128)(2,1)S(1)}, u32[]{:S(2)}, u32[]{:S(2)}) collective-permute-start(bf16[4,1024,256]{2,1,0:T(8,128)(2,1)} %all-gather.5.cloned.1.call-done), channel_id=1, source_target_pairs={{0,1},{1,0},{2,3},{3,2},{4,5},{5,4},{6,7},{7,6},{8,9},{9,8},{10,11... | collective-permute-start | bytes 6291464 | tf_op jit(solution)/shard_map/ppermute | solution.py:40
  89.1 3.8 %collective-permute-start.14 = (f32[4,32]{1,0:T(4,128)S(1)}, f32[4,32]{1,0:T(4,128)S(1)}, u32[]{:S(2)}, u32[]{:S(2)}) collective-permute-start(f32[4,32]{1,0:T(4,128)S(1)} %add.27.refs_0_), channel_id=1, source_target_pairs={{0,1},{1,0},{2,3},{3,2},{4,5},{5,4},{6,7},{7,6},{8,9},{9,8},{10,11... | collective-permute-start | bytes 1544 | tf_op jit(solution)/shard_map/ppermute | solution.py:48
  89.6 3.6 %collective-permute-start.15 = (f32[4,32]{1,0:T(4,128)S(1)}, f32[4,32]{1,0:T(4,128)S(1)}, u32[]{:S(2)}, u32[]{:S(2)}) collective-permute-start(f32[4,32]{1,0:T(4,128)S(1)} %add.27.refs_0_), channel_id=1, source_target_pairs={{0,16},{1,17},{2,18},{3,19},{4,20},{5,21},{6,22},{7,23},{8,24},{9,... | collective-permute-start | bytes 1544 | tf_op jit(solution)/shard_map/ppermute | solution.py:48
  91.3 3.0 %collective-permute-start.16 = (f32[4,32]{1,0:T(4,128)S(1)}, f32[4,32]{1,0:T(4,128)S(1)}, u32[]{:S(2)}, u32[]{:S(2)}) collective-permute-start(f32[4,32]{1,0:T(4,128)S(1)} %add.27.refs_0_), channel_id=1, source_target_pairs={{0,17},{1,16},{2,19},{3,18},{4,21},{5,20},{6,23},{7,22},{8,25},{9,... | collective-permute-start | bytes 1544 | tf_op jit(solution)/shard_map/ppermute | solution.py:48
  94.3 5.8 %copy-start.3 = (bf16[32,128,2048]{2,1,0:T(8,128)(2,1)S(1)}, bf16[32,128,2048]{2,1,0:T(8,128)(2,1)}, u32[]{:S(2)}) copy-start(bf16[32,128,2048]{2,1,0:T(8,128)(2,1)} %refs_4_.1) | copy-start | bytes 50331652
  100.1 6.4 %copy-start.10 = (bf16[4,1024,256]{2,1,0:T(8,128)(2,1)S(1)}, bf16[4,1024,256]{2,1,0:T(8,128)(2,1)}, u32[]{:S(2)}) copy-start(bf16[4,1024,256]{2,1,0:T(8,128)(2,1)} %all-gather.5.cloned.1.call-done) | copy-start | bytes 6291460
  106.5 3.2 %copy-start = (bf16[8,128,2048]{2,1,0:T(8,128)(2,1)}, bf16[8,128,2048]{2,1,0:T(8,128)(2,1)S(1)}, u32[]{:S(2)}) copy-start(bf16[8,128,2048]{2,1,0:T(8,128)(2,1)S(1)} %get-tuple-element.28.potential) | copy-start | bytes 12582916
  109.7 118.5 %all-gather.9.cloned.1.call-start = ((), (), s32[]{:S(2)}) async-start(), calls=%async_computation.2 | async-start | bytes 2359296 | tf_op jit(solution)/shard_map/all_gather | solution.py:56
  127.8 4.4 %collective-permute-start.17 = (bf16[4,1024,256]{2,1,0:T(8,128)(2,1)}, bf16[4,1024,256]{2,1,0:T(8,128)(2,1)S(1)}, u32[]{:S(2)}, u32[]{:S(2)}) collective-permute-start(bf16[4,1024,256]{2,1,0:T(8,128)(2,1)} %all-gather.7.cloned.1.call-done), channel_id=1, source_target_pairs={{0,1},{1,0},{2,3},{3,2},{4,5},{5,4},{6,7},{7,6},{8,9},{9,8},{10,11... | collective-permute-start | bytes 6291464 | tf_op jit(solution)/shard_map/ppermute | solution.py:40
  132.2 2.2 copy-start.1
  134.4 1.7 copy-start.11
  177.8 50.4 %collective-permute-start.20 = (bf16[4,1024,256]{2,1,0:T(8,128)(2,1)}, bf16[4,1024,256]{2,1,0:T(8,128)(2,1)S(1)}, u32[]{:S(2)}, u32[]{:S(2)}) collective-permute-start(bf16[4,1024,256]{2,1,0:T(8,128)(2,1)} %all-gather.11.cloned.1.call-done), channel_id=1, source_target_pairs={{0,1},{1,0},{2,3},{3,2},{4,5},{5,4},{6,7},{7,6},{8,9},{9,8},{10,11... | collective-permute-start | bytes 6291464 | tf_op jit(solution)/shard_map/ppermute | solution.py:40
  228.2 7.0 %collective-permute-start.18 = (bf16[4,1024,256]{2,1,0:T(8,128)(2,1)}, bf16[4,1024,256]{2,1,0:T(8,128)(2,1)S(1)}, u32[]{:S(2)}, u32[]{:S(2)}) collective-permute-start(bf16[4,1024,256]{2,1,0:T(8,128)(2,1)} %all-gather.9.cloned.1.call-done), channel_id=1, source_target_pairs={{0,1},{1,0},{2,3},{3,2},{4,5},{5,4},{6,7},{7,6},{8,9},{9,8},{10,11... | collective-permute-start | bytes 6291464 | tf_op jit(solution)/shard_map/ppermute | solution.py:40
  228.2 2.2 copy-start.2
  230.4 1.6 copy-start.7
  232.0 3.2 %copy-start.8 = (bf16[4,1024,256]{2,1,0:T(8,128)(2,1)S(1)}, bf16[4,1024,256]{2,1,0:T(8,128)(2,1)}, u32[]{:S(2)}) copy-start(bf16[4,1024,256]{2,1,0:T(8,128)(2,1)} %all-gather.9.cloned.1.call-done) | copy-start | bytes 6291460
Sparse Core Ops, SparseCore 0:
  11.1 66.2 all-gather.4
  79.6 48.1 all-gather.6
  130.0 47.7 all-gather.10
  180.4 47.7 all-gather.8

commit v3 on v2

v3 whole, which is shorter than its diff:
```python
import functools

import jax
import jax.numpy as jnp
from jax import lax
from jax.experimental import pallas as pl
from jax.experimental.pallas import tpu as pltpu
from jax.sharding import PartitionSpec as P

ITERS = 3
TAU_ROOT = 0.1
BLOCK = 16
HIGHEST = lax.Precision.HIGHEST
MIB = 1024 * 1024

F32 = jnp.float32
BF16 = jnp.bfloat16


def params(mebibytes):
    return pltpu.CompilerParams(vmem_limit_bytes=mebibytes * MIB)


def vmem_specs(count):
    return [pl.BlockSpec(memory_space=pltpu.VMEM)] * count


class Layout:
    def __init__(self, walk_size, chol_size):
        self.walk = walk_size
        self.chol = chol_size
        self.z = chol_size // 4

    def shift(self, array, dz=0, dy=0, db=0):
        pairs = []
        for index in range(self.chol):
            z, y, b = index // 4, (index // 2) % 2, index % 2
            target = (((z + dz) % self.z) * 2 + (y ^ dy)) * 2 + (b ^ db)
            pairs.append((index, target))
        return lax.ppermute(array, "chol", pairs)

    def shift_all(self, array, dw, db):
        pairs = []
        for group in range(self.walk):
            for index in range(self.chol):
                target = ((group + dw) % self.walk) * self.chol + (index ^ db)
                pairs.append((group * self.chol + index, target))
        return lax.ppermute(array, ("walk", "chol"), pairs)

    def swap(self, array, distance):
        pairs = [(i, (((i // 4) ^ distance) * 4) + i % 4) for i in range(self.chol)]
        return lax.ppermute(array, "chol", pairs)


class Stream:
    def __init__(self, layout, piece, walker=0):
        self.layout = layout
        self.walker = walker
        self.ring = [piece]
        self.across = []

    def advance(self, anchors=()):
        if len(self.across) == self.layout.z:
            return anchors
        latest = self.ring[-1]
        moved = [self.layout.shift(latest, dy=1)]
        last = len(self.ring) == self.layout.z
        if not last:
            moved.append(self.layout.shift(latest, dz=1))
        if anchors or not last:
            anchors, moved = lax.optimization_barrier((anchors, moved))
        self.across.append(moved[0])
        self.ring.extend(moved[1:])
        return anchors

    def pieces(self):
        ring = [(array, self.walker, dz, 0) for dz, array in enumerate(self.ring)]
        return ring + [(array, self.walker, dz, 1) for dz, array in enumerate(self.across)]


def diagonal(shape):
    return lax.broadcasted_iota(jnp.int32, shape, 0) == lax.broadcasted_iota(jnp.int32, shape, 1)


def to_message(total):
    rounded = total.astype(BF16)
    rest = jnp.where(diagonal(total.shape), total - rounded.astype(F32), 0.0)
    rest = jnp.broadcast_to(jnp.sum(rest, axis=0, keepdims=True), (BLOCK, total.shape[1]))
    return jnp.concatenate([rounded, rest.astype(BF16)], axis=0)


def from_message(message):
    size = message.shape[1]
    matrix = message[:size].astype(F32)
    rest = message[size:].astype(F32)[:1]
    return matrix + jnp.where(diagonal(matrix.shape), rest, 0.0)


def intersection_kernel(places, mine, theirs, trial_mine, trial_theirs, *outs):
    count = mine.shape[0] // 2
    first = trial_mine[...].T
    second = trial_theirs[...].T
    index = lax.axis_index("chol")
    z, base = index // 4, lax.rem(index, 2) * count
    for step in range(count):
        walker = base + (lax.rem(z + step, count) if places else step)
        total = jnp.dot(first, mine[walker], preferred_element_type=F32)
        total += jnp.dot(second, theirs[walker], preferred_element_type=F32)
        outs[step][...] = to_message(total) if places and step else total


def intersections_of(mine, theirs, trial_mine, trial_theirs, places):
    per_group, _, electrons = mine.shape
    count = per_group // 2
    whole = jax.ShapeDtypeStruct((electrons, electrons), F32)
    message = jax.ShapeDtypeStruct((electrons + BLOCK, electrons), BF16)
    return pl.pallas_call(
        functools.partial(intersection_kernel, places),
        out_shape=[whole] + [message if places else whole] * (count - 1),
        in_specs=vmem_specs(4),
        out_specs=vmem_specs(count),
        compiler_params=params(8),
    )(mine, theirs, trial_mine, trial_theirs)


def sum_kernel(own, *refs):
    messages, (total_out, message_out) = refs[:-2], refs[-2:]
    total = own[...]
    for message in messages:
        total = total + from_message(message[...])
    total_out[...] = total
    message_out[...] = to_message(total)


def sum_of(own, messages):
    return pl.pallas_call(
        sum_kernel,
        out_shape=[
            jax.ShapeDtypeStruct(own.shape, F32),
            jax.ShapeDtypeStruct(messages[0].shape, BF16),
        ],
        in_specs=vmem_specs(1 + len(messages)),
        out_specs=vmem_specs(2),
        compiler_params=params(8),
    )(own, *messages)


def newton_kernel(own, *refs):
    messages, out = refs[:-1], refs[-1]
    matrix = own[...]
    for message in messages:
        matrix = matrix + from_message(message[...])
    twice = jnp.where(diagonal(matrix.shape), 2.0, 0.0).astype(F32)
    estimate = twice - matrix
    for _ in range(ITERS - 1):
        product = jnp.dot(matrix, estimate, precision=HIGHEST, preferred_element_type=F32)
        estimate = jnp.dot(
            estimate, twice - product, precision=HIGHEST, preferred_element_type=F32
        )
    out[...] = estimate.astype(out.dtype)


def newton_of(own, messages=()):
    return pl.pallas_call(
        newton_kernel,
        out_shape=jax.ShapeDtypeStruct(own.shape, BF16),
        in_specs=vmem_specs(1 + len(messages)),
        out_specs=pl.BlockSpec(memory_space=pltpu.VMEM),
        compiler_params=params(8),
    )(own, *messages)


def bias_kernel(places, mine, theirs, rot_mine, rot_theirs, *refs):
    inverses, out, greens = refs[:-2], refs[-2], refs[-1]
    count = len(inverses)
    rows, electrons = mine.shape[1], mine.shape[2]
    vectors = rot_mine.shape[0]
    index = lax.axis_index("chol")
    z, base = index // 4, lax.rem(index, 2) * count
    for at in range(count):
        walker = base + (lax.rem(z + (count - at), count) if places else at)
        both = jnp.concatenate([mine[walker], theirs[walker]], axis=0)
        product = jnp.dot(both, inverses[at][...], preferred_element_type=F32).astype(BF16)
        greens[:, :, at] = product.reshape(2, rows // BLOCK, BLOCK, electrons)
    total = jnp.zeros((vectors * BLOCK, count * BLOCK), F32)
    for half, rot in enumerate((rot_mine, rot_theirs)):
        for block in range(rows // BLOCK):
            total += lax.dot_general(
                rot[:, block * BLOCK : (block + 1) * BLOCK, :].reshape(vectors * BLOCK, electrons),
                greens[half, block].reshape(count * BLOCK, electrons),
                (((1,), (1,)), ((), ())),
                preferred_element_type=F32,
            )
    same = lax.rem(lax.broadcasted_iota(jnp.int32, total.shape, 0), BLOCK) == lax.rem(
        lax.broadcasted_iota(jnp.int32, total.shape, 1), BLOCK
    )
    summed = jnp.sum(
        jnp.where(same, total, 0.0).reshape(vectors, BLOCK, count * BLOCK), axis=1
    )
    shape = (count, count * BLOCK)
    walker = lax.broadcasted_iota(jnp.int32, shape, 0)
    place = lax.rem(lax.rem(z, count) + (count - walker), count) if places else walker
    pick = (lax.broadcasted_iota(jnp.int32, shape, 1) // BLOCK == place).astype(F32)
    out[...] = lax.dot_general(
        pick, summed, (((1,), (1,)), ((), ())), precision=HIGHEST, preferred_element_type=F32
    )


def bias_of(mine, theirs, rot_mine, rot_theirs, inverses, places):
    _, rows, electrons = mine.shape
    count = len(inverses)
    vectors = rot_mine.shape[0]
    return pl.pallas_call(
        functools.partial(bias_kernel, places),
        out_shape=jax.ShapeDtypeStruct((count, vectors), F32),
        in_specs=vmem_specs(4 + count),
        out_specs=pl.BlockSpec(memory_space=pltpu.VMEM),
        scratch_shapes=[pltpu.VMEM((2, rows // BLOCK, count, BLOCK, electrons), BF16)],
        compiler_params=params(12),
        cost_estimate=pl.CostEstimate(
            flops=4 * count * rows * electrons * (electrons + vectors * BLOCK),
            bytes_accessed=4 * (vectors + count) * rows * electrons,
            transcendentals=0,
        ),
    )(mine, theirs, rot_mine, rot_theirs, *inverses)


def weights_kernel(origins, layout, order, fields, source, *refs):
    pieces, (bias_out, weights) = refs[:-2], refs[-2:]
    per_group, vectors = fields.shape
    half = pieces[0].shape[0]
    group = lax.axis_index("walk")
    b = lax.rem(lax.axis_index("chol"), 2)
    wanted = source[...]
    bias = jnp.zeros((per_group, vectors), F32)
    for (dw, db), piece in zip(origins, pieces):
        from_group = lax.rem(group + (layout.walk - dw), layout.walk)
        from_b = b + db - 2 * b * db
        base = from_group * per_group + from_b * half
        for row in range(half):
            bias += jnp.where(wanted == base + row, piece[row : row + 1, :], 0.0)
    bias = TAU_ROOT * bias
    bias_out[...] = bias
    shifted = (fields[...] - bias).astype(BF16)
    slot = jnp.zeros((per_group * BLOCK, 1), jnp.int32)
    place = lax.broadcasted_iota(jnp.int32, slot.shape, 0) // BLOCK
    for at in range(per_group):
        slot = jnp.where(place == at, order[lax.rem(at + b * half, per_group)], slot)
    tall = (per_group * BLOCK, per_group)
    rows = (lax.broadcasted_iota(jnp.int32, tall, 1) == slot).astype(BF16)
    wide = (vectors, vectors * BLOCK)
    columns = (
        lax.broadcasted_iota(jnp.int32, wide, 1) // BLOCK
        == lax.broadcasted_iota(jnp.int32, wide, 0)
    ).astype(BF16)
    spread = jnp.dot(rows, shifted, preferred_element_type=F32).astype(BF16)
    spread = jnp.dot(spread, columns, preferred_element_type=F32)
    same = lax.rem(lax.broadcasted_iota(jnp.int32, spread.shape, 0), BLOCK) == lax.rem(
        lax.broadcasted_iota(jnp.int32, spread.shape, 1), BLOCK
    )
    weights[...] = jnp.where(same, spread, 0.0).astype(BF16)


def weights_of(layout, order, fields, source, pieces):
    per_group, vectors = fields.shape
    origins = [origin for origin, _ in pieces]
    arrays = [array for _, array in pieces]
    return pl.pallas_call(
        functools.partial(weights_kernel, origins, layout),
        out_shape=[
            jax.ShapeDtypeStruct((per_group, vectors), F32),
            jax.ShapeDtypeStruct((per_group * BLOCK, vectors * BLOCK), BF16),
        ],
        in_specs=[pl.BlockSpec(memory_space=pltpu.SMEM)] + vmem_specs(2 + len(arrays)),
        out_specs=vmem_specs(2),
        compiler_params=params(8),
    )(order, fields, source, *arrays)


def potential_kernel(start, weights, cholesky, kept, sent, blocks, semaphores):
    vectors, orbitals = cholesky.shape[0], cholesky.shape[2]
    half = kept.shape[0]
    copies = []
    for at in range(blocks.shape[0]):
        rows = pl.ds(start + at * BLOCK, BLOCK)
        copies.append(
            pltpu.make_async_copy(cholesky.at[:, rows, :], blocks.at[at], semaphores.at[at])
        )
    for copy in copies:
        copy.start()
    for at, copy in enumerate(copies):
        copy.wait()
        block = blocks[at].reshape(vectors * BLOCK, orbitals)
        result = TAU_ROOT * jnp.dot(weights[...], block, preferred_element_type=F32)
        result = result.astype(BF16).reshape(2 * half, BLOCK, orbitals)
        kept[:, at * BLOCK : (at + 1) * BLOCK, :] = result[:half]
        sent[:, at * BLOCK : (at + 1) * BLOCK, :] = result[half:]


def potential_of(weights, cholesky, part, parts):
    vectors, rows, orbitals = cholesky.shape
    half = weights.shape[0] // BLOCK // 2
    rows = rows // parts
    out = jax.ShapeDtypeStruct((half, rows, orbitals), BF16)
    return pl.pallas_call(
        functools.partial(potential_kernel, part * rows),
        out_shape=[out, out],
        in_specs=vmem_specs(1) + [pl.BlockSpec(memory_space=pltpu.HBM)],
        out_specs=vmem_specs(2),
        scratch_shapes=[
            pltpu.VMEM((rows // BLOCK, vectors, BLOCK, orbitals), BF16),
            pltpu.SemaphoreType.DMA((rows // BLOCK,)),
        ],
        compiler_params=params(48),
    )(weights, cholesky)


def fold(layout, places, kept, theirs, pieces, buffer, walker):
    index = lax.axis_index("chol")
    z, y = index // 4, lax.rem(index // 2, 2)
    for piece, (count, first, dz, dy) in zip(pieces, places):
        if first <= walker < first + count:
            chip = lax.rem(z + (layout.z - dz), layout.z) * 2 + (y + dy - 2 * y * dy)
            buffer[walker, chip] = piece[walker - first]
    rows = jnp.concatenate([part[walker] for part in (*kept, *theirs)], axis=0)
    full = buffer[walker]
    return jnp.dot(rows, full.reshape(-1, full.shape[-1]), preferred_element_type=F32)


def first_kernel(layout, places, parts, sizes, *refs):
    kept, theirs, refs = refs[:parts], refs[parts : 2 * parts], refs[2 * parts :]
    base, buffer = refs[-2:]
    outs = refs[-2 - len(sizes) : -2]
    pieces = refs[: -2 - len(sizes)]
    b = lax.rem(lax.axis_index("chol"), 2)
    own_chip = lax.axis_index("chol") // 2
    number, walker = 0, 0
    for number, size in enumerate(sizes):
        for at in range(size):
            term = fold(layout, places, kept, theirs, pieces, buffer, walker)
            rows = term.shape[0] // 2
            for block, value in ((b, term[:rows]), (1 - b, term[rows:])):
                outs[number][at, block] = value.astype(BF16)
                base[walker, block] = buffer[walker, own_chip, block].astype(F32) + value
            walker += 1


def second_kernel(layout, places, parts, *refs):
    kept, theirs, refs = refs[:parts], refs[parts : 2 * parts], refs[2 * parts :]
    base, pieces, (mine, sent, buffer) = refs[0], refs[1:-3], refs[-3:]
    b = lax.rem(lax.axis_index("chol"), 2)
    for walker in range(base.shape[0]):
        term = fold(layout, places, kept, theirs, pieces, buffer, walker)
        rows = term.shape[0] // 2
        mine[walker] = (base[walker, b] + 0.5 * term[:rows]).astype(BF16)
        sent[walker] = (base[walker, 1 - b] + 0.5 * term[rows:]).astype(BF16)


def operands_of(pieces):
    arrays = [piece[0] for piece in pieces]
    return arrays, [(piece[0].shape[0], *piece[1:]) for piece in pieces]


def fold_cost(half, rows, orbitals, electrons):
    return pl.CostEstimate(
        flops=4 * half * rows * orbitals * electrons,
        bytes_accessed=2 * half * orbitals * (2 * rows + electrons),
        transcendentals=0,
    )


def first_of(layout, kept, theirs, pieces, sizes):
    arrays, places = operands_of(pieces)
    half, _, orbitals = kept[0].shape
    _, rows, electrons = arrays[0].shape[-3:]
    return pl.pallas_call(
        functools.partial(first_kernel, layout, places, len(kept), sizes),
        out_shape=[jax.ShapeDtypeStruct((size, 2, rows, electrons), BF16) for size in sizes]
        + [jax.ShapeDtypeStruct((half, 2, rows, electrons), F32)],
        in_specs=vmem_specs(2 * len(kept) + len(arrays)),
        out_specs=vmem_specs(len(sizes) + 1),
        scratch_shapes=[pltpu.VMEM((half, orbitals // (2 * rows), 2, rows, electrons), BF16)],
        compiler_params=params(16),
        cost_estimate=fold_cost(half, rows, orbitals, electrons),
    )(*kept, *theirs, *arrays)


def second_of(layout, kept, theirs, base, pieces):
    arrays, places = operands_of(pieces)
    half, _, orbitals = kept[0].shape
    _, rows, electrons = arrays[0].shape[-3:]
    out = jax.ShapeDtypeStruct((half, rows, electrons), BF16)
    return pl.pallas_call(
        functools.partial(second_kernel, layout, places, len(kept)),
        out_shape=[out, out],
        in_specs=vmem_specs(2 * len(kept) + 1 + len(arrays)),
        out_specs=vmem_specs(2),
        scratch_shapes=[pltpu.VMEM((half, orbitals // (2 * rows), 2, rows, electrons), BF16)],
        compiler_params=params(16),
        cost_estimate=fold_cost(half, rows, orbitals, electrons),
    )(*kept, *theirs, base, *arrays)


def place_kernel(order, mine, theirs, out):
    half = mine.shape[0]
    b = lax.rem(lax.axis_index("chol"), 2)
    for walker in range(half):
        out[order[b * half + walker]] = mine[walker]
        out[order[(1 - b) * half + walker]] = theirs[walker]


def place(order, mine, theirs):
    half, rows, electrons = mine.shape
    return pl.pallas_call(
        place_kernel,
        out_shape=jax.ShapeDtypeStruct((2 * half, rows, electrons), BF16),
        in_specs=[pl.BlockSpec(memory_space=pltpu.SMEM)] + vmem_specs(2),
        out_specs=pl.BlockSpec(memory_space=pltpu.VMEM),
        compiler_params=params(8),
    )(order, mine, theirs)


def split_kernel(source, walkers, first, second, order, picked, semaphores):
    per_group = walkers.shape[0]
    half = per_group // 2
    group = lax.axis_index("walk")
    b = lax.rem(lax.axis_index("chol"), 2)
    stayed, arrived, sent = jnp.int32(0), jnp.int32(0), jnp.int32(0)
    for slot in range(per_group):
        local = source[group * per_group + slot] - group * per_group
        stays = ((local >= 0) & (local < per_group)).astype(jnp.int32)
        at = jnp.where(stays == 1, jnp.minimum(stayed, half - 1), per_group)
        picked[at] = local
        at = jnp.where(stays == 1, stayed, half + arrived)
        order[jnp.minimum(at, per_group - 1)] = jnp.int32(slot)
        stayed, arrived = stayed + stays, arrived + 1 - stays
        local = source[(1 - group) * per_group + slot] - group * per_group
        goes = ((local >= 0) & (local < per_group)).astype(jnp.int32)
        at = jnp.where(goes == 1, half + jnp.minimum(sent, half - 1), per_group)
        picked[at] = local
        sent = sent + goes
    copies = []
    for target, offset in ((second, (1 - b) * half), (first, b * half)):
        for walker in range(half):
            copies.append(
                pltpu.make_async_copy(
                    walkers.at[picked[offset + walker]],
                    target.at[walker],
                    semaphores.at[len(copies)],
                )
            )
    for copy in copies:
        copy.start()
    for copy in copies:
        copy.wait()


def split_walkers(walkers, source):
    per_group, rows, electrons = walkers.shape
    half = jax.ShapeDtypeStruct((per_group // 2, rows, electrons), walkers.dtype)
    return pl.pallas_call(
        split_kernel,
        out_shape=[half, half, jax.ShapeDtypeStruct((per_group,), jnp.int32)],
        in_specs=[pl.BlockSpec(memory_space=pltpu.SMEM), pl.BlockSpec(memory_space=pltpu.HBM)],
        out_specs=[pl.BlockSpec(memory_space=pl.ANY)] * 2
        + [pl.BlockSpec(memory_space=pltpu.SMEM)],
        scratch_shapes=[
            pltpu.SMEM((per_group + 1,), jnp.int32),
            pltpu.SemaphoreType.DMA((per_group,)),
        ],
        compiler_params=params(4),
    )(source, walkers)


def ranks(flags):
    count = flags.shape[-1]
    before = jnp.arange(count)[None, :] < jnp.arange(count)[:, None]
    return jnp.sum(jnp.where(before & flags[..., None, :], 1, 0), axis=-1)


def migrate(layout, walkers, source):
    per_group = walkers.shape[0]
    half = per_group // 2
    group = lax.axis_index("walk")
    if layout.walk == 2:
        first, second, order = split_walkers(walkers, source)
        near, cross = [], []
        for index in range(2 * layout.chol):
            across = (index + layout.chol) % (2 * layout.chol)
            if index % 2 == 0:
                near.append((index, index))
                cross.append((index, across + 1))
            else:
                near.append((index, across))
                cross.append((index, index - 1))
        axes = ("walk", "chol")
        return lax.ppermute(first, axes, near), lax.ppermute(second, axes, cross), order
    table = source.reshape(layout.walk, per_group)
    incoming = lax.dynamic_index_in_dim(table, group, 0, keepdims=False)
    incoming_groups = incoming // per_group

    def outgoing(distance):
        row = lax.dynamic_index_in_dim(table, (group + distance) % layout.walk, 0, keepdims=False)
        local = row - group * per_group
        here = (local >= 0) & (local < per_group)
        match = here[None, :] & (ranks(here)[None, :] == jnp.arange(half)[:, None])
        return jnp.take(walkers, jnp.sum(jnp.where(match, local[None, :], 0), axis=1), axis=0)

    arrived = [outgoing(0)]
    for distance in range(1, layout.walk):
        pairs = [(g, (g + distance) % layout.walk) for g in range(layout.walk)]
        arrived.append(lax.ppermute(outgoing(distance), "walk", pairs))
    slots = jnp.arange(per_group)
    same = (incoming_groups[:, None] == incoming_groups[None, :]) & (slots[None, :] < slots[:, None])
    rank = jnp.sum(same.astype(jnp.int32), axis=1)
    distance = (group - incoming_groups) % layout.walk
    migrated = jnp.take(jnp.concatenate(arrived, axis=0), distance * half + rank, axis=0)
    b = lax.axis_index("chol") % 2
    mine = lax.dynamic_slice_in_dim(migrated, b * half, half, 0)
    theirs = lax.dynamic_slice_in_dim(migrated, (1 - b) * half, half, 0)
    return mine, layout.shift(theirs, db=1), slots.astype(jnp.int32)


def shards(layout, walkers, trial, cholesky, rotated, fields, source):
    per_group = walkers.shape[0]
    half = per_group // 2
    group = lax.axis_index("walk")
    b = lax.axis_index("chol") % 2
    own, other, order = migrate(layout, walkers, source)
    trial_theirs = layout.shift(trial, db=1)
    theirs = layout.shift(walkers, db=1)
    rot_theirs = layout.shift(rotated, db=1)
    places = layout.z == half
    partial = intersections_of(walkers, theirs, trial, trial_theirs, places)
    if places:
        messages = [layout.shift(partial[dz], dz=dz) for dz in range(1, half)]
        messages, own, other = lax.optimization_barrier((messages, own, other))
        total, message = sum_of(partial[0], messages)
        inverse = newton_of(total, [layout.shift(message, dy=1)])
    chunk = jnp.stack([jnp.where(b == 0, own, other), jnp.where(b == 0, other, own)], axis=1)
    migrated = Stream(layout, chunk)
    if places:
        (inverse,) = migrated.advance((inverse,))
        inverses = [inverse] + [layout.shift(inverse, dz=dz) for dz in range(1, half)]
    else:
        spread = jnp.zeros((per_group,) + partial[0].shape, F32)
        spread = lax.dynamic_update_slice_in_dim(spread, jnp.stack(partial), b * half, 0)
        summed = lax.dynamic_slice_in_dim(lax.psum(spread, "chol"), b * half, half, 0)
        inverses = [newton_of(summed[index]) for index in range(half)]
    inverses = migrated.advance(inverses)

    total = bias_of(walkers, theirs, rotated, rot_theirs, inverses, places)
    distance = layout.z // 2
    while distance:
        total = total + layout.swap(total, distance)
        distance //= 2
    total = total + layout.shift(total, dy=1)
    pieces = []
    for dw in range(layout.walk):
        for db in range(2):
            moved = layout.shift_all(total, dw, db) if dw + db else total
            pieces.append(((dw, db), moved))

    wanted = lax.dynamic_slice_in_dim(source, group * per_group, per_group)[:, None]
    force_bias, weights = weights_of(layout, order, fields, wanted, pieces)
    (weights,) = migrated.advance((weights,))
    kept, received = [], []
    for part in range(2):
        mine, sent = potential_of(weights, cholesky, part, 2)
        kept.append(mine)
        received.append(layout.shift(sent, db=1))

    while len(migrated.across) < layout.z:
        migrated.advance()
    sizes = (half // 2, half - half // 2)
    *firsts, base = first_of(layout, kept, received, migrated.pieces(), sizes)
    streams = [Stream(layout, first, at * sizes[0]) for at, first in enumerate(firsts)]
    for _ in range(layout.z):
        for stream in streams:
            stream.advance()
    gathered = [piece for stream in streams for piece in stream.pieces()]
    mine, sent = second_of(layout, kept, received, base, gathered)
    return place(order, mine, layout.shift(sent, db=1)), force_bias


def solution(mesh):
    in_specs = (
        P("walk", "chol", None),
        P("chol", None),
        P(None, "chol", None),
        P(None, "chol", None),
        P("walk", None),
        P(),
    )
    out_specs = (P("walk", "chol", None), P("walk", None))
    layout = Layout(mesh.shape["walk"], mesh.shape["chol"])
    return jax.shard_map(
        functools.partial(shards, layout),
        mesh=mesh,
        in_specs=in_specs,
        out_specs=out_specs,
        check_vma=False,
    )
```

time: 245 us -> 187 us (0.76)
  waiting for transfers between devices: 165 us -> 111 us
  starting transfers between devices: 22.4 us -> 42.5 us
  between operations: 13.9 us -> 0.89 us
  local copies, waits for them, and re-layouts: 17.2 us -> 6.85 us
    all_gather x4 -> x0, waiting for transfers between devices: 108 us -> none  [gather_plane(): lax.all_gather(piece, 'chol', axis_index_groups=planes, axis=1, tiled=True)]
    ppermute x15 -> x35, waiting for transfers between devices: 46.3 us -> 101 us  [shift(): return lax.ppermute(array, 'chol', pairs)]
    ppermute x15 -> x35, starting transfers between devices: 18.5 us -> 35.4 us  [shift(): return lax.ppermute(array, 'chol', pairs)]
    unnamed x32 -> x34, local copies, waits for them, and re-layouts: 17 us -> 6.69 us
    ppermute x2, starting transfers between devices: 0.01 us -> 4.52 us  [swap(): return lax.ppermute(array, 'chol', pairs)]
    pallas_call x6 -> x8, Pallas kernels: 20.6 us -> 18.4 us  [the longest x2 8.04 us: potential_of(): pl.pallas_call(functools.partial(potential_kernel, part * rows), out_shap...]
  transfers between devices with their start and end apart: 25 -> 42, of which waited for: 17 -> 27; matrix products, arithmetic and copies ran while one was open for 0% -> 1% of each run, Pallas kernels for 9% -> 6%
where the time goes in v3:
time: 187 us
  waiting for transfers between devices  111 us (59%)
  starting transfers between devices  42.5 us (23%)
  Pallas kernels  24.9 us (13%)
  local copies, waits for them, and re-layouts  6.85 us (4%)
    ppermute x35, waiting for transfers between devices, shift(): return lax.ppermute(array, 'chol', pairs)  101 us
    ppermute x35, starting transfers between devices, shift(): return lax.ppermute(array, 'chol', pairs)  35.4 us
    ppermute x2, waiting for transfers between devices, swap(): return lax.ppermute(array, 'chol', pairs)  8.68 us
    pallas_call x2, Pallas kernels, potential_of(): pl.pallas_call(functools.partial(potential_kernel, part * rows), out_shap...  8.04 us
    unnamed x34, local copies, waits for them, and re-layouts  6.69 us
    ppermute x2, starting transfers between devices, swap(): return lax.ppermute(array, 'chol', pairs)  4.52 us
  transfers between devices with their start and end apart: 42, of which 27 were waited for; matrix products, arithmetic and copies ran while one was open for 1% of the time, Pallas kernels for 6%

profile of v3, /device:TPU:0, one launch (start us, length us, event | category | flops | bytes accessed | tf_op | source)
XLA Modules:
  0.0 187.1 jit_solution(1178635329594275199)
XLA Ops:
  1.1 1.0 copy-done
  2.2 0.7 copy-done.14
  2.8 2.0 %shard_map.77 = (bf16[4,128,256]{2,1,0:T(8,128)(2,1)S(1)}, bf16[4,128,256]{2,1,0:T(8,128)(2,1)}, s32[8]{0:T(128)S(1)}) custom-call(s32[16]{0:T(128)S(1)} %copy-done.14, bf16[8,128,256]{2,1,0:T(8,128)(2,1)S(1)} %copy-done), custom_call_target="tpu_custom_call" | custom-call | tf_op jit(solution)/shard_map/pallas_call | solution.py:461
  4.9 0.7 collective-permute-start.6
  5.5 4.0 %collective-permute-start.1 = (bf16[32,128,256]{2,1,0:T(8,128)(2,1)}, bf16[32,128,256]{2,1,0:T(8,128)(2,1)}, u32[]{:S(2)}, u32[]{:S(2)}) collective-permute-start(bf16[32,128,256]{2,1,0:T(8,128)(2,1)} %rot_mine.1), channel_id=1, source_target_pairs={{0,1},{1,0},{2,3},{3,2},{4,5},{5,4},{6,7},{7,6},{8,9},{9,8},{10,11... | collective-permute-start | bytes 6291464 | tf_op jit(solution)/shard_map/ppermute | solution.py:40
  10.1 3.6 %collective-permute-done.2.trial_theirs = bf16[128,256]{1,0:T(8,128)(2,1)S(1)} collective-permute-done((bf16[128,256]{1,0:T(8,128)(2,1)}, bf16[128,256]{1,0:T(8,128)(2,1)S(1)}, u32[]{:S(2)}, u32[]{:S(2)}) %collective-permute-start.2) | collective-permute-done | bytes 65568 | tf_op jit(solution)/shard_map/ppermute | solution.py:40
  13.7 1.0 copy-done.1
  14.7 0.8 copy-done.12
  15.5 1.2 shard_map.78
  16.7 1.6 collective-permute-start.3
  18.3 2.6 %collective-permute-start.4 = (bf16[272,256]{1,0:T(8,128)(2,1)}, bf16[272,256]{1,0:T(8,128)(2,1)}, u32[]{:S(2)}, u32[]{:S(2)}) collective-permute-start(bf16[272,256]{1,0:T(8,128)(2,1)} %get-tuple-element.54), channel_id=1, source_target_pairs={{0,8},{1,9},{2,10},{3,11},{4,12},{5,13},{6,14},{7,15},{8,0},{9,1},... | collective-permute-start | bytes 417800 | tf_op jit(solution)/shard_map/ppermute | solution.py:40
  20.9 0.7 copy-done.16
  21.6 1.3 collective-permute-start.5
  22.9 2.4 %collective-permute-done.3.refs_0_ = bf16[272,256]{1,0:T(8,128)(2,1)S(1)} collective-permute-done((bf16[272,256]{1,0:T(8,128)(2,1)}, bf16[272,256]{1,0:T(8,128)(2,1)S(1)}, u32[]{:S(2)}, u32[]{:S(2)}) %collective-permute-start.3) | collective-permute-done | bytes 139296 | tf_op jit(solution)/shard_map/ppermute | solution.py:40
  25.3 5.6 %collective-permute-done.4.refs_1_ = bf16[272,256]{1,0:T(8,128)(2,1)} collective-permute-done((bf16[272,256]{1,0:T(8,128)(2,1)}, bf16[272,256]{1,0:T(8,128)(2,1)}, u32[]{:S(2)}, u32[]{:S(2)}) %collective-permute-start.4) | collective-permute-done | bytes 139296 | tf_op jit(solution)/shard_map/ppermute | solution.py:40
  30.9 1.1 select_bitcast_fusion.1
  32.0 3.5 %collective-permute-start.10 = (bf16[4,2,128,256]{3,2,1,0:T(8,128)(2,1)S(1)}, bf16[4,2,128,256]{3,2,1,0:T(8,128)(2,1)S(1)}, u32[]{:S(2)}, u32[]{:S(2)}) collective-permute-start(bf16[4,2,128,256]{3,2,1,0:T(8,128)(2,1)S(1)} %pad_maximum_fusion.refs_4_), channel_id=1, source_target_pairs={{0,4},{1,5},{2,6},{3,7},{4,8},{5,9},{6,10},{7,11},{8,12},{9,13},{1... | collective-permute-start | bytes 1572872 | tf_op jit(solution)/shard_map/ppermute | solution.py:40
  35.6 1.5 collective-permute-start.9
  37.1 1.1 shard_map.79
  38.8 13.4 %collective-permute-done.8.refs_0_ = bf16[272,256]{1,0:T(8,128)(2,1)S(1)} collective-permute-done((bf16[272,256]{1,0:T(8,128)(2,1)S(1)}, bf16[272,256]{1,0:T(8,128)(2,1)S(1)}, u32[]{:S(2)}, u32[]{:S(2)}) %collective-permute-start.8) | collective-permute-done | bytes 139296 | tf_op jit(solution)/shard_map/ppermute | solution.py:40
  52.1 2.2 %shard_map.80.refs_0_ = bf16[256,256]{1,0:T(8,128)(2,1)S(1)} custom-call(f32[256,256]{1,0:T(8,128)S(1)} %get-tuple-element.61.own, bf16[272,256]{1,0:T(8,128)(2,1)S(1)} %collective-permute-done.8.refs_0_), custom_call_target="tpu_custom_call" | custom-call | tf_op jit(solution)/shard_map/pallas_call | solution.py:164
  54.4 0.8 copy-done.8
  55.5 1.5 collective-permute-start.14
  57.0 0.8 copy-done.6
  57.8 3.5 %collective-permute-start.13 = (bf16[256,256]{1,0:T(8,128)(2,1)S(1)}, bf16[256,256]{1,0:T(8,128)(2,1)S(1)}, u32[]{:S(2)}, u32[]{:S(2)}) collective-permute-start(bf16[256,256]{1,0:T(8,128)(2,1)S(1)} %shard_map.80.refs_0_), channel_id=1, source_target_pairs={{0,12},{1,13},{2,14},{3,15},{4,0},{5,1},{6,2},{7,3},{8,4},{9,5},{1... | collective-permute-start | bytes 393224 | tf_op jit(solution)/shard_map/ppermute | solution.py:40
  61.3 11.2 %collective-permute-done.13.refs_3_ = bf16[256,256]{1,0:T(8,128)(2,1)S(1)} collective-permute-done((bf16[256,256]{1,0:T(8,128)(2,1)S(1)}, bf16[256,256]{1,0:T(8,128)(2,1)S(1)}, u32[]{:S(2)}, u32[]{:S(2)}) %collective-permute-start.13) | collective-permute-done | bytes 131104 | tf_op jit(solution)/shard_map/ppermute | solution.py:40
  72.5 2.1 %collective-permute-start.11 = (bf16[256,256]{1,0:T(8,128)(2,1)S(1)}, bf16[256,256]{1,0:T(8,128)(2,1)S(1)}, u32[]{:S(2)}, u32[]{:S(2)}) collective-permute-start(bf16[256,256]{1,0:T(8,128)(2,1)S(1)} %shard_map.80.refs_0_), channel_id=1, source_target_pairs={{0,4},{1,5},{2,6},{3,7},{4,8},{5,9},{6,10},{7,11},{8,12},{9,13},{1... | collective-permute-start | bytes 393224 | tf_op jit(solution)/shard_map/ppermute | solution.py:40
  74.5 6.4 %collective-permute-done.12.refs_2_ = bf16[256,256]{1,0:T(8,128)(2,1)S(1)} collective-permute-done((bf16[256,256]{1,0:T(8,128)(2,1)S(1)}, bf16[256,256]{1,0:T(8,128)(2,1)S(1)}, u32[]{:S(2)}, u32[]{:S(2)}) %collective-permute-start.12) | collective-permute-done | bytes 131104 | tf_op jit(solution)/shard_map/ppermute | solution.py:40
  80.9 0.8 copy-done.10
  81.7 1.6 collective-permute-start.22
  83.3 3.2 %shard_map.81 = f32[4,32]{1,0:T(4,128)S(1)} custom-call(bf16[8,128,256]{2,1,0:T(8,128)(2,1)S(1)} %copy-done.2, bf16[8,128,256]{2,1,0:T(8,128)(2,1)S(1)} %copy-done.5, bf16[32,128,256]{2,1,0:T(8,128)(2,1)S(1)} %copy-done.3, bf16[32,128,256]{2,1,0:T(8,128)(2,1)} %collective-permute-done.1.rot_theirs, bf16[256,256]{1,0:T(8,128)(2,1)S(1)} %shard_map.80.refs_0_, ...), custom_call_target="tpu_custom_call" | custom-call | flops 402653184 | bytes 4718592 | tf_op jit(solution)/shard_map/pallas_call | solution.py:213
  86.6 7.1 %collective-permute-done.16 = f32[4,32]{1,0:T(4,128)S(1)} collective-permute-done((f32[4,32]{1,0:T(4,128)S(1)}, f32[4,32]{1,0:T(4,128)S(1)}, u32[]{:S(2)}, u32[]{:S(2)}) %collective-permute-start.16) | collective-permute-done | bytes 544 | tf_op jit(solution)/shard_map/ppermute | solution.py:52
  93.7 4.5 %collective-permute-start.17 = (f32[4,32]{1,0:T(4,128)S(1)}, f32[4,32]{1,0:T(4,128)S(1)}, u32[]{:S(2)}, u32[]{:S(2)}) collective-permute-start(f32[4,32]{1,0:T(4,128)S(1)} %add.18), channel_id=1, source_target_pairs={{0,4},{1,5},{2,6},{3,7},{4,0},{5,1},{6,2},{7,3},{8,12},{9,13},{10,... | collective-permute-start | bytes 1544 | tf_op jit(solution)/shard_map/ppermute | solution.py:52
  98.2 1.6 collective-permute-done.17
  99.8 0.6 collective-permute-start.18
  100.4 2.9 %collective-permute-done.18 = f32[4,32]{1,0:T(4,128)S(1)} collective-permute-done((f32[4,32]{1,0:T(4,128)S(1)}, f32[4,32]{1,0:T(4,128)S(1)}, u32[]{:S(2)}, u32[]{:S(2)}) %collective-permute-start.18) | collective-permute-done | bytes 544 | tf_op jit(solution)/shard_map/ppermute | solution.py:40
  103.9 1.3 collective-permute-start.19
  105.4 1.0 collective-permute-done.21.refs_3_
  107.0 1.2 shard_map.82
  108.3 4.0 %shard_map.84 = (bf16[4,64,2048]{2,1,0:T(8,128)(2,1)S(1)}, bf16[4,64,2048]{2,1,0:T(8,128)(2,1)S(1)}) custom-call(bf16[128,512]{1,0:T(8,128)(2,1)S(1)} %get-tuple-element.73.weights, bf16[32,128,2048]{2,1,0:T(8,128)(2,1)} %cholesky.3), custom_call_target="tpu_custom_call" | custom-call | tf_op jit(solution)/shard_map/pallas_call | solution.py:305
  112.3 4.1 %shard_map.83 = (bf16[4,64,2048]{2,1,0:T(8,128)(2,1)S(1)}, bf16[4,64,2048]{2,1,0:T(8,128)(2,1)S(1)}) custom-call(bf16[128,512]{1,0:T(8,128)(2,1)S(1)} %get-tuple-element.73.weights, bf16[32,128,2048]{2,1,0:T(8,128)(2,1)} %cholesky.3), custom_call_target="tpu_custom_call" | custom-call | tf_op jit(solution)/shard_map/pallas_call | solution.py:305
  116.9 0.6 collective-permute-start.26
  117.6 13.5 %collective-permute-done.26.refs_11_ = bf16[4,2,128,256]{3,2,1,0:T(8,128)(2,1)S(1)} collective-permute-done((bf16[4,2,128,256]{3,2,1,0:T(8,128)(2,1)}, bf16[4,2,128,256]{3,2,1,0:T(8,128)(2,1)S(1)}, u32[]{:S(2)}, u32[]{:S(2)}) %collective-permute-start.26) | collective-permute-done | bytes 524320 | tf_op jit(solution)/shard_map/ppermute | solution.py:40
  131.1 2.9 %shard_map.85 = (bf16[2,2,128,256]{3,2,1,0:T(8,128)(2,1)S(1)}, bf16[2,2,128,256]{3,2,1,0:T(8,128)(2,1)S(1)}, f32[4,2,128,256]{3,2,1,0:T(8,128)S(1)}) custom-call(bf16[4,64,2048]{2,1,0:T(8,128)(2,1)S(1)} %get-tuple-element.74.refs_0_, bf16[4,64,2048]{2,1,0:T(8,128)(2,1)S(1)} %get-tuple-element.75.refs_1_, ...), custom_call_target="tpu_custom_call" | custom-call | flops 1073741824 | bytes 8388608 | tf_op jit(solution)/shard_map/pallas_call | solution.py:376
  134.0 2.1 %collective-permute-start.28 = (bf16[2,2,128,256]{3,2,1,0:T(8,128)(2,1)S(1)}, bf16[2,2,128,256]{3,2,1,0:T(8,128)(2,1)S(1)}, u32[]{:S(2)}, u32[]{:S(2)}) collective-permute-start(bf16[2,2,128,256]{3,2,1,0:T(8,128)(2,1)S(1)} %get-tuple-element.83.refs_5_), channel_id=1, source_target_pairs={{0,4},{1,5},{2,6},{3,7},{4,8},{5,9},{6,10},{7,11},{8,12},{9,13},{1... | collective-permute-start | bytes 786440 | tf_op jit(solution)/shard_map/ppermute | solution.py:40
  136.1 0.6 collective-permute-start.27
  136.8 1.4 collective-permute-start.34
  138.2 6.9 %collective-permute-done.28.refs_6_ = bf16[2,2,128,256]{3,2,1,0:T(8,128)(2,1)S(1)} collective-permute-done((bf16[2,2,128,256]{3,2,1,0:T(8,128)(2,1)S(1)}, bf16[2,2,128,256]{3,2,1,0:T(8,128)(2,1)S(1)}, u32[]{:S(2)}, u32[]{:S(2)}) %collective-permute-start.28) | collective-permute-done | bytes 262176 | tf_op jit(solution)/shard_map/ppermute | solution.py:40
  145.4 0.6 collective-permute-start.29
  146.0 4.7 %collective-permute-done.35.refs_14_ = bf16[2,2,128,256]{3,2,1,0:T(8,128)(2,1)S(1)} collective-permute-done((bf16[2,2,128,256]{3,2,1,0:T(8,128)(2,1)S(1)}, bf16[2,2,128,256]{3,2,1,0:T(8,128)(2,1)S(1)}, u32[]{:S(2)}, u32[]{:S(2)}) %collective-permute-start.35) | collective-permute-done | bytes 262176 | tf_op jit(solution)/shard_map/ppermute | solution.py:40
  151.0 0.6 collective-permute-start.36
  151.7 4.7 %collective-permute-done.30.refs_7_ = bf16[2,2,128,256]{3,2,1,0:T(8,128)(2,1)S(1)} collective-permute-done((bf16[2,2,128,256]{3,2,1,0:T(8,128)(2,1)S(1)}, bf16[2,2,128,256]{3,2,1,0:T(8,128)(2,1)S(1)}, u32[]{:S(2)}, u32[]{:S(2)}) %collective-permute-start.30) | collective-permute-done | bytes 262176 | tf_op jit(solution)/shard_map/ppermute | solution.py:40
  156.6 0.6 collective-permute-start.31
  157.3 4.7 %collective-permute-done.37.refs_15_ = bf16[2,2,128,256]{3,2,1,0:T(8,128)(2,1)S(1)} collective-permute-done((bf16[2,2,128,256]{3,2,1,0:T(8,128)(2,1)S(1)}, bf16[2,2,128,256]{3,2,1,0:T(8,128)(2,1)S(1)}, u32[]{:S(2)}, u32[]{:S(2)}) %collective-permute-start.37) | collective-permute-done | bytes 262176 | tf_op jit(solution)/shard_map/ppermute | solution.py:40
  162.3 0.6 collective-permute-start.38
  162.9 4.7 %collective-permute-done.32.refs_8_ = bf16[2,2,128,256]{3,2,1,0:T(8,128)(2,1)S(1)} collective-permute-done((bf16[2,2,128,256]{3,2,1,0:T(8,128)(2,1)S(1)}, bf16[2,2,128,256]{3,2,1,0:T(8,128)(2,1)S(1)}, u32[]{:S(2)}, u32[]{:S(2)}) %collective-permute-start.32) | collective-permute-done | bytes 262176 | tf_op jit(solution)/shard_map/ppermute | solution.py:40
  167.8 0.6 collective-permute-start.33
  168.4 3.0 %collective-permute-done.39.refs_16_ = bf16[2,2,128,256]{3,2,1,0:T(8,128)(2,1)S(1)} collective-permute-done((bf16[2,2,128,256]{3,2,1,0:T(8,128)(2,1)S(1)}, bf16[2,2,128,256]{3,2,1,0:T(8,128)(2,1)S(1)}, u32[]{:S(2)}, u32[]{:S(2)}) %collective-permute-start.39) | collective-permute-done | bytes 262176 | tf_op jit(solution)/shard_map/ppermute | solution.py:40
  171.4 2.0 %collective-permute-done.38.refs_19_ = bf16[2,2,128,256]{3,2,1,0:T(8,128)(2,1)S(1)} collective-permute-done((bf16[2,2,128,256]{3,2,1,0:T(8,128)(2,1)S(1)}, bf16[2,2,128,256]{3,2,1,0:T(8,128)(2,1)S(1)}, u32[]{:S(2)}, u32[]{:S(2)}) %collective-permute-start.38) | collective-permute-done | bytes 262176 | tf_op jit(solution)/shard_map/ppermute | solution.py:40
  174.1 5.0 %collective-permute-done.33.refs_12_ = bf16[2,2,128,256]{3,2,1,0:T(8,128)(2,1)S(1)} collective-permute-done((bf16[2,2,128,256]{3,2,1,0:T(8,128)(2,1)S(1)}, bf16[2,2,128,256]{3,2,1,0:T(8,128)(2,1)S(1)}, u32[]{:S(2)}, u32[]{:S(2)}) %collective-permute-start.33) | collective-permute-done | bytes 262176 | tf_op jit(solution)/shard_map/ppermute | solution.py:40
  179.0 3.5 %collective-permute-done.40.refs_20_ = bf16[2,2,128,256]{3,2,1,0:T(8,128)(2,1)S(1)} collective-permute-done((bf16[2,2,128,256]{3,2,1,0:T(8,128)(2,1)S(1)}, bf16[2,2,128,256]{3,2,1,0:T(8,128)(2,1)S(1)}, u32[]{:S(2)}, u32[]{:S(2)}) %collective-permute-start.40) | collective-permute-done | bytes 262176 | tf_op jit(solution)/shard_map/ppermute | solution.py:40
  182.6 1.5 shard_map.86
  184.2 1.5 collective-permute-done.41.theirs
  185.7 1.4 shard_map.87
  (72 shorter events, 6.2 us)
Async XLA Ops:
  0.6 13.0 %collective-permute-start = (bf16[8,128,256]{2,1,0:T(8,128)(2,1)}, bf16[8,128,256]{2,1,0:T(8,128)(2,1)S(1)}, u32[]{:S(2)}, u32[]{:S(2)}) collective-permute-start(bf16[8,128,256]{2,1,0:T(8,128)(2,1)} %mine.3), channel_id=1, source_target_pairs={{0,1},{1,0},{2,3},{3,2},{4,5},{5,4},{6,7},{7,6},{8,9},{9,8},{10,11... | collective-permute-start | bytes 1572872 | tf_op jit(solution)/shard_map/ppermute | solution.py:40
  1.1 1.0 copy-start
  2.2 0.7 copy-start.14
  4.9 16.0 %collective-permute-start.6 = (bf16[4,128,256]{2,1,0:T(8,128)(2,1)S(1)}, bf16[4,128,256]{2,1,0:T(8,128)(2,1)S(1)}, u32[]{:S(2)}, u32[]{:S(2)}) collective-permute-start(bf16[4,128,256]{2,1,0:T(8,128)(2,1)S(1)} %get-tuple-element.56), channel_id=1, source_target_pairs={{0,0},{1,17},{2,2},{3,19},{4,4},{5,21},{6,6},{7,23},{8,8},{9,25},{... | collective-permute-start | bytes 786440 | tf_op jit(solution)/shard_map/ppermute | solution.py:497
  5.5 77.8 %collective-permute-start.1 = (bf16[32,128,256]{2,1,0:T(8,128)(2,1)}, bf16[32,128,256]{2,1,0:T(8,128)(2,1)}, u32[]{:S(2)}, u32[]{:S(2)}) collective-permute-start(bf16[32,128,256]{2,1,0:T(8,128)(2,1)} %rot_mine.1), channel_id=1, source_target_pairs={{0,1},{1,0},{2,3},{3,2},{4,5},{5,4},{6,7},{7,6},{8,9},{9,8},{10,11... | collective-permute-start | bytes 6291464 | tf_op jit(solution)/shard_map/ppermute | solution.py:40
  9.6 13.4 %collective-permute-start.7 = (bf16[4,128,256]{2,1,0:T(8,128)(2,1)}, bf16[4,128,256]{2,1,0:T(8,128)(2,1)}, u32[]{:S(2)}, u32[]{:S(2)}) collective-permute-start(bf16[4,128,256]{2,1,0:T(8,128)(2,1)} %get-tuple-element.57), channel_id=1, source_target_pairs={{0,17},{1,0},{2,19},{3,2},{4,21},{5,4},{6,23},{7,6},{8,25},{9,8},{... | collective-permute-start | bytes 786440 | tf_op jit(solution)/shard_map/ppermute | solution.py:497
  9.6 4.1 %collective-permute-start.2 = (bf16[128,256]{1,0:T(8,128)(2,1)}, bf16[128,256]{1,0:T(8,128)(2,1)S(1)}, u32[]{:S(2)}, u32[]{:S(2)}) collective-permute-start(bf16[128,256]{1,0:T(8,128)(2,1)} %trial_mine.1), channel_id=1, source_target_pairs={{0,1},{1,0},{2,3},{3,2},{4,5},{5,4},{6,7},{7,6},{8,9},{9,8},{10,11... | collective-permute-start | bytes 196616 | tf_op jit(solution)/shard_map/ppermute | solution.py:40
  13.6 1.0 copy-start.1
  14.7 0.8 copy-start.12
  15.5 16.4 %copy-start.4 = (bf16[8,128,256]{2,1,0:T(8,128)(2,1)}, bf16[8,128,256]{2,1,0:T(8,128)(2,1)S(1)}, u32[]{:S(2)}) copy-start(bf16[8,128,256]{2,1,0:T(8,128)(2,1)S(1)} %collective-permute-done.theirs) | copy-start | bytes 1572868
  15.5 67.8 %copy-start.2 = (bf16[8,128,256]{2,1,0:T(8,128)(2,1)S(1)}, bf16[8,128,256]{2,1,0:T(8,128)(2,1)}, u32[]{:S(2)}) copy-start(bf16[8,128,256]{2,1,0:T(8,128)(2,1)} %mine.3) | copy-start | bytes 1572868
  15.5 67.8 %copy-start.3 = (bf16[32,128,256]{2,1,0:T(8,128)(2,1)S(1)}, bf16[32,128,256]{2,1,0:T(8,128)(2,1)}, u32[]{:S(2)}) copy-start(bf16[32,128,256]{2,1,0:T(8,128)(2,1)} %rot_mine.1) | copy-start | bytes 6291460
  16.7 8.6 %collective-permute-start.3 = (bf16[272,256]{1,0:T(8,128)(2,1)}, bf16[272,256]{1,0:T(8,128)(2,1)S(1)}, u32[]{:S(2)}, u32[]{:S(2)}) collective-permute-start(bf16[272,256]{1,0:T(8,128)(2,1)} %get-tuple-element.53), channel_id=1, source_target_pairs={{0,4},{1,5},{2,6},{3,7},{4,8},{5,9},{6,10},{7,11},{8,12},{9,13},{1... | collective-permute-start | bytes 417800 | tf_op jit(solution)/shard_map/ppermute | solution.py:40
  18.3 12.6 %collective-permute-start.4 = (bf16[272,256]{1,0:T(8,128)(2,1)}, bf16[272,256]{1,0:T(8,128)(2,1)}, u32[]{:S(2)}, u32[]{:S(2)}) collective-permute-start(bf16[272,256]{1,0:T(8,128)(2,1)} %get-tuple-element.54), channel_id=1, source_target_pairs={{0,8},{1,9},{2,10},{3,11},{4,12},{5,13},{6,14},{7,15},{8,0},{9,1},... | collective-permute-start | bytes 417800 | tf_op jit(solution)/shard_map/ppermute | solution.py:40
  20.9 0.7 copy-start.16
  21.6 9.3 %collective-permute-start.5 = (bf16[272,256]{1,0:T(8,128)(2,1)}, bf16[272,256]{1,0:T(8,128)(2,1)}, u32[]{:S(2)}, u32[]{:S(2)}) collective-permute-start(bf16[272,256]{1,0:T(8,128)(2,1)} %get-tuple-element.55), channel_id=1, source_target_pairs={{0,12},{1,13},{2,14},{3,15},{4,0},{5,1},{6,2},{7,3},{8,4},{9,5},{1... | collective-permute-start | bytes 417800 | tf_op jit(solution)/shard_map/ppermute | solution.py:40
  32.0 51.3 %copy-start.5 = (bf16[8,128,256]{2,1,0:T(8,128)(2,1)S(1)}, bf16[8,128,256]{2,1,0:T(8,128)(2,1)}, u32[]{:S(2)}) copy-start(bf16[8,128,256]{2,1,0:T(8,128)(2,1)} %copy-done.4) | copy-start | bytes 1572868
  32.0 22.3 %collective-permute-start.10 = (bf16[4,2,128,256]{3,2,1,0:T(8,128)(2,1)S(1)}, bf16[4,2,128,256]{3,2,1,0:T(8,128)(2,1)S(1)}, u32[]{:S(2)}, u32[]{:S(2)}) collective-permute-start(bf16[4,2,128,256]{3,2,1,0:T(8,128)(2,1)S(1)} %pad_maximum_fusion.refs_4_), channel_id=1, source_target_pairs={{0,4},{1,5},{2,6},{3,7},{4,8},{5,9},{6,10},{7,11},{8,12},{9,13},{1... | collective-permute-start | bytes 1572872 | tf_op jit(solution)/shard_map/ppermute | solution.py:40
  35.6 18.8 %collective-permute-start.9 = (bf16[4,2,128,256]{3,2,1,0:T(8,128)(2,1)S(1)}, bf16[4,2,128,256]{3,2,1,0:T(8,128)(2,1)S(1)}, u32[]{:S(2)}, u32[]{:S(2)}) collective-permute-start(bf16[4,2,128,256]{3,2,1,0:T(8,128)(2,1)S(1)} %pad_maximum_fusion.refs_4_), channel_id=1, source_target_pairs={{0,2},{1,3},{2,0},{3,1},{4,6},{5,7},{6,4},{7,5},{8,10},{9,11},{10,... | collective-permute-start | bytes 1572872 | tf_op jit(solution)/shard_map/ppermute | solution.py:40
  38.2 13.9 %collective-permute-start.8 = (bf16[272,256]{1,0:T(8,128)(2,1)S(1)}, bf16[272,256]{1,0:T(8,128)(2,1)S(1)}, u32[]{:S(2)}, u32[]{:S(2)}) collective-permute-start(bf16[272,256]{1,0:T(8,128)(2,1)S(1)} %get-tuple-element.62), channel_id=1, source_target_pairs={{0,2},{1,3},{2,0},{3,1},{4,6},{5,7},{6,4},{7,5},{8,10},{9,11},{10,... | collective-permute-start | bytes 417800 | tf_op jit(solution)/shard_map/ppermute | solution.py:40
  54.3 50.9 %copy-start.15 = (s32[16]{0:T(128)S(1)}, s32[16]{0:T(128)}, u32[]{:S(2)}) copy-start(s32[16]{0:T(128)} %source.1) | copy-start | bytes 196
  54.3 52.7 %copy-start.13 = (f32[8,32]{1,0:T(8,128)S(1)}, f32[8,32]{1,0:T(8,128)}, u32[]{:S(2)}) copy-start(f32[8,32]{1,0:T(8,128)} %fields.1) | copy-start | bytes 3076
  54.4 0.8 copy-start.8
  55.2 25.7 %collective-permute-start.15 = (bf16[4,2,128,256]{3,2,1,0:T(8,128)(2,1)S(1)}, bf16[4,2,128,256]{3,2,1,0:T(8,128)(2,1)}, u32[]{:S(2)}, u32[]{:S(2)}) collective-permute-start(bf16[4,2,128,256]{3,2,1,0:T(8,128)(2,1)S(1)} %collective-permute-done.10.refs_5_), channel_id=1, source_target_pairs={{0,4},{1,5},{2,6},{3,7},{4,8},{5,9},{6,10},{7,11},{8,12},{9,13},{1... | collective-permute-start | bytes 1572872 | tf_op jit(solution)/shard_map/ppermute | solution.py:40
  55.5 25.4 %collective-permute-start.14 = (bf16[4,2,128,256]{3,2,1,0:T(8,128)(2,1)S(1)}, bf16[4,2,128,256]{3,2,1,0:T(8,128)(2,1)S(1)}, u32[]{:S(2)}, u32[]{:S(2)}) collective-permute-start(bf16[4,2,128,256]{3,2,1,0:T(8,128)(2,1)S(1)} %collective-permute-done.10.refs_5_), channel_id=1, source_target_pairs={{0,2},{1,3},{2,0},{3,1},{4,6},{5,7},{6,4},{7,5},{8,10},{9,11},{10,... | collective-permute-start | bytes 1572872 | tf_op jit(solution)/shard_map/ppermute | solution.py:40
  57.0 0.8 copy-start.6
  57.8 14.6 %collective-permute-start.13 = (bf16[256,256]{1,0:T(8,128)(2,1)S(1)}, bf16[256,256]{1,0:T(8,128)(2,1)S(1)}, u32[]{:S(2)}, u32[]{:S(2)}) collective-permute-start(bf16[256,256]{1,0:T(8,128)(2,1)S(1)} %shard_map.80.refs_0_), channel_id=1, source_target_pairs={{0,12},{1,13},{2,14},{3,15},{4,0},{5,1},{6,2},{7,3},{8,4},{9,5},{1... | collective-permute-start | bytes 393224 | tf_op jit(solution)/shard_map/ppermute | solution.py:40
  61.3 19.6 %collective-permute-start.12 = (bf16[256,256]{1,0:T(8,128)(2,1)S(1)}, bf16[256,256]{1,0:T(8,128)(2,1)S(1)}, u32[]{:S(2)}, u32[]{:S(2)}) collective-permute-start(bf16[256,256]{1,0:T(8,128)(2,1)S(1)} %shard_map.80.refs_0_), channel_id=1, source_target_pairs={{0,8},{1,9},{2,10},{3,11},{4,12},{5,13},{6,14},{7,15},{8,0},{9,1},... | collective-permute-start | bytes 393224 | tf_op jit(solution)/shard_map/ppermute | solution.py:40
  72.5 8.4 %collective-permute-start.11 = (bf16[256,256]{1,0:T(8,128)(2,1)S(1)}, bf16[256,256]{1,0:T(8,128)(2,1)S(1)}, u32[]{:S(2)}, u32[]{:S(2)}) collective-permute-start(bf16[256,256]{1,0:T(8,128)(2,1)S(1)} %shard_map.80.refs_0_), channel_id=1, source_target_pairs={{0,4},{1,5},{2,6},{3,7},{4,8},{5,9},{6,10},{7,11},{8,12},{9,13},{1... | collective-permute-start | bytes 393224 | tf_op jit(solution)/shard_map/ppermute | solution.py:40
  80.9 0.8 copy-start.10
  81.7 26.5 %collective-permute-start.23 = (bf16[4,2,128,256]{3,2,1,0:T(8,128)(2,1)}, bf16[4,2,128,256]{3,2,1,0:T(8,128)(2,1)}, u32[]{:S(2)}, u32[]{:S(2)}) collective-permute-start(bf16[4,2,128,256]{3,2,1,0:T(8,128)(2,1)} %collective-permute-done.15.refs_6_), channel_id=1, source_target_pairs={{0,4},{1,5},{2,6},{3,7},{4,8},{5,9},{6,10},{7,11},{8,12},{9,13},{1... | collective-permute-start | bytes 1572872 | tf_op jit(solution)/shard_map/ppermute | solution.py:40
  81.7 26.5 %collective-permute-start.22 = (bf16[4,2,128,256]{3,2,1,0:T(8,128)(2,1)}, bf16[4,2,128,256]{3,2,1,0:T(8,128)(2,1)}, u32[]{:S(2)}, u32[]{:S(2)}) collective-permute-start(bf16[4,2,128,256]{3,2,1,0:T(8,128)(2,1)} %collective-permute-done.15.refs_6_), channel_id=1, source_target_pairs={{0,2},{1,3},{2,0},{3,1},{4,6},{5,7},{6,4},{7,5},{8,10},{9,11},{10,... | collective-permute-start | bytes 1572872 | tf_op jit(solution)/shard_map/ppermute | solution.py:40
  86.6 7.1 %collective-permute-start.16 = (f32[4,32]{1,0:T(4,128)S(1)}, f32[4,32]{1,0:T(4,128)S(1)}, u32[]{:S(2)}, u32[]{:S(2)}) collective-permute-start(f32[4,32]{1,0:T(4,128)S(1)} %shard_map.81), channel_id=1, source_target_pairs={{0,8},{1,9},{2,10},{3,11},{4,12},{5,13},{6,14},{7,15},{8,0},{9,1},... | collective-permute-start | bytes 1544 | tf_op jit(solution)/shard_map/ppermute | solution.py:52
  93.7 6.1 %collective-permute-start.17 = (f32[4,32]{1,0:T(4,128)S(1)}, f32[4,32]{1,0:T(4,128)S(1)}, u32[]{:S(2)}, u32[]{:S(2)}) collective-permute-start(f32[4,32]{1,0:T(4,128)S(1)} %add.18), channel_id=1, source_target_pairs={{0,4},{1,5},{2,6},{3,7},{4,0},{5,1},{6,2},{7,3},{8,12},{9,13},{10,... | collective-permute-start | bytes 1544 | tf_op jit(solution)/shard_map/ppermute | solution.py:52
  99.8 3.6 %collective-permute-start.18 = (f32[4,32]{1,0:T(4,128)S(1)}, f32[4,32]{1,0:T(4,128)S(1)}, u32[]{:S(2)}, u32[]{:S(2)}) collective-permute-start(f32[4,32]{1,0:T(4,128)S(1)} %add.19), channel_id=1, source_target_pairs={{0,2},{1,3},{2,0},{3,1},{4,6},{5,7},{6,4},{7,5},{8,10},{9,11},{10,... | collective-permute-start | bytes 1544 | tf_op jit(solution)/shard_map/ppermute | solution.py:40
  103.4 3.0 %collective-permute-start.21 = (f32[4,32]{1,0:T(4,128)S(1)}, f32[4,32]{1,0:T(4,128)S(1)}, u32[]{:S(2)}, u32[]{:S(2)}) collective-permute-start(f32[4,32]{1,0:T(4,128)S(1)} %add.20.refs_0_), channel_id=1, source_target_pairs={{0,17},{1,16},{2,19},{3,18},{4,21},{5,20},{6,23},{7,22},{8,25},{9,... | collective-permute-start | bytes 1544 | tf_op jit(solution)/shard_map/ppermute | solution.py:48
  103.4 3.6 %collective-permute-start.20 = (f32[4,32]{1,0:T(4,128)S(1)}, f32[4,32]{1,0:T(4,128)S(1)}, u32[]{:S(2)}, u32[]{:S(2)}) collective-permute-start(f32[4,32]{1,0:T(4,128)S(1)} %add.20.refs_0_), channel_id=1, source_target_pairs={{0,16},{1,17},{2,18},{3,19},{4,20},{5,21},{6,22},{7,23},{8,24},{9,... | collective-permute-start | bytes 1544 | tf_op jit(solution)/shard_map/ppermute | solution.py:48
  103.9 3.1 %collective-permute-start.19 = (f32[4,32]{1,0:T(4,128)S(1)}, f32[4,32]{1,0:T(4,128)S(1)}, u32[]{:S(2)}, u32[]{:S(2)}) collective-permute-start(f32[4,32]{1,0:T(4,128)S(1)} %add.20.refs_0_), channel_id=1, source_target_pairs={{0,1},{1,0},{2,3},{3,2},{4,5},{5,4},{6,7},{7,6},{8,9},{9,8},{10,11... | collective-permute-start | bytes 1544 | tf_op jit(solution)/shard_map/ppermute | solution.py:48
  112.2 18.8 %copy-start.7 = (bf16[4,2,128,256]{3,2,1,0:T(8,128)(2,1)S(1)}, bf16[4,2,128,256]{3,2,1,0:T(8,128)(2,1)}, u32[]{:S(2)}) copy-start(bf16[4,2,128,256]{3,2,1,0:T(8,128)(2,1)} %copy-done.6) | copy-start | bytes 1572868
  112.2 18.8 %copy-start.9 = (bf16[4,2,128,256]{3,2,1,0:T(8,128)(2,1)S(1)}, bf16[4,2,128,256]{3,2,1,0:T(8,128)(2,1)}, u32[]{:S(2)}) copy-start(bf16[4,2,128,256]{3,2,1,0:T(8,128)(2,1)} %copy-done.8) | copy-start | bytes 1572868
  112.2 18.8 %copy-start.11 = (bf16[4,2,128,256]{3,2,1,0:T(8,128)(2,1)S(1)}, bf16[4,2,128,256]{3,2,1,0:T(8,128)(2,1)}, u32[]{:S(2)}) copy-start(bf16[4,2,128,256]{3,2,1,0:T(8,128)(2,1)} %copy-done.10) | copy-start | bytes 1572868
  116.3 14.7 %collective-permute-start.25 = (bf16[4,64,2048]{2,1,0:T(8,128)(2,1)S(1)}, bf16[4,64,2048]{2,1,0:T(8,128)(2,1)S(1)}, u32[]{:S(2)}, u32[]{:S(2)}) collective-permute-start(bf16[4,64,2048]{2,1,0:T(8,128)(2,1)S(1)} %get-tuple-element.77), channel_id=1, source_target_pairs={{0,1},{1,0},{2,3},{3,2},{4,5},{5,4},{6,7},{7,6},{8,9},{9,8},{10,11... | collective-permute-start | bytes 3145736 | tf_op jit(solution)/shard_map/ppermute | solution.py:40
  116.4 14.6 %collective-permute-start.24 = (bf16[4,64,2048]{2,1,0:T(8,128)(2,1)S(1)}, bf16[4,64,2048]{2,1,0:T(8,128)(2,1)S(1)}, u32[]{:S(2)}, u32[]{:S(2)}) collective-permute-start(bf16[4,64,2048]{2,1,0:T(8,128)(2,1)S(1)} %get-tuple-element.76), channel_id=1, source_target_pairs={{0,1},{1,0},{2,3},{3,2},{4,5},{5,4},{6,7},{7,6},{8,9},{9,8},{10,11... | collective-permute-start | bytes 3145736 | tf_op jit(solution)/shard_map/ppermute | solution.py:40
  116.9 14.1 %collective-permute-start.26 = (bf16[4,2,128,256]{3,2,1,0:T(8,128)(2,1)}, bf16[4,2,128,256]{3,2,1,0:T(8,128)(2,1)S(1)}, u32[]{:S(2)}, u32[]{:S(2)}) collective-permute-start(bf16[4,2,128,256]{3,2,1,0:T(8,128)(2,1)} %collective-permute-done.23.refs_7_), channel_id=1, source_target_pairs={{0,2},{1,3},{2,0},{3,1},{4,6},{5,7},{6,4},{7,5},{8,10},{9,11},{10,... | collective-permute-start | bytes 1572872 | tf_op jit(solution)/shard_map/ppermute | solution.py:40
  134.0 11.1 %collective-permute-start.28 = (bf16[2,2,128,256]{3,2,1,0:T(8,128)(2,1)S(1)}, bf16[2,2,128,256]{3,2,1,0:T(8,128)(2,1)S(1)}, u32[]{:S(2)}, u32[]{:S(2)}) collective-permute-start(bf16[2,2,128,256]{3,2,1,0:T(8,128)(2,1)S(1)} %get-tuple-element.83.refs_5_), channel_id=1, source_target_pairs={{0,4},{1,5},{2,6},{3,7},{4,8},{5,9},{6,10},{7,11},{8,12},{9,13},{1... | collective-permute-start | bytes 786440 | tf_op jit(solution)/shard_map/ppermute | solution.py:40
  136.1 9.2 %collective-permute-start.27 = (bf16[2,2,128,256]{3,2,1,0:T(8,128)(2,1)S(1)}, bf16[2,2,128,256]{3,2,1,0:T(8,128)(2,1)S(1)}, u32[]{:S(2)}, u32[]{:S(2)}) collective-permute-start(bf16[2,2,128,256]{3,2,1,0:T(8,128)(2,1)S(1)} %get-tuple-element.83.refs_5_), channel_id=1, source_target_pairs={{0,2},{1,3},{2,0},{3,1},{4,6},{5,7},{6,4},{7,5},{8,10},{9,11},{10,... | collective-permute-start | bytes 786440 | tf_op jit(solution)/shard_map/ppermute | solution.py:40
  136.7 14.0 %collective-permute-start.35 = (bf16[2,2,128,256]{3,2,1,0:T(8,128)(2,1)S(1)}, bf16[2,2,128,256]{3,2,1,0:T(8,128)(2,1)S(1)}, u32[]{:S(2)}, u32[]{:S(2)}) collective-permute-start(bf16[2,2,128,256]{3,2,1,0:T(8,128)(2,1)S(1)} %get-tuple-element.90.refs_13_), channel_id=1, source_target_pairs={{0,4},{1,5},{2,6},{3,7},{4,8},{5,9},{6,10},{7,11},{8,12},{9,13},{1... | collective-permute-start | bytes 786440 | tf_op jit(solution)/shard_map/ppermute | solution.py:40
  136.8 14.1 %collective-permute-start.34 = (bf16[2,2,128,256]{3,2,1,0:T(8,128)(2,1)S(1)}, bf16[2,2,128,256]{3,2,1,0:T(8,128)(2,1)S(1)}, u32[]{:S(2)}, u32[]{:S(2)}) collective-permute-start(bf16[2,2,128,256]{3,2,1,0:T(8,128)(2,1)S(1)} %get-tuple-element.90.refs_13_), channel_id=1, source_target_pairs={{0,2},{1,3},{2,0},{3,1},{4,6},{5,7},{6,4},{7,5},{8,10},{9,11},{10,... | collective-permute-start | bytes 786440 | tf_op jit(solution)/shard_map/ppermute | solution.py:40
  145.3 11.0 %collective-permute-start.30 = (bf16[2,2,128,256]{3,2,1,0:T(8,128)(2,1)S(1)}, bf16[2,2,128,256]{3,2,1,0:T(8,128)(2,1)S(1)}, u32[]{:S(2)}, u32[]{:S(2)}) collective-permute-start(bf16[2,2,128,256]{3,2,1,0:T(8,128)(2,1)S(1)} %collective-permute-done.28.refs_6_), channel_id=1, source_target_pairs={{0,4},{1,5},{2,6},{3,7},{4,8},{5,9},{6,10},{7,11},{8,12},{9,13},{1... | collective-permute-start | bytes 786440 | tf_op jit(solution)/shard_map/ppermute | solution.py:40
  145.4 11.2 %collective-permute-start.29 = (bf16[2,2,128,256]{3,2,1,0:T(8,128)(2,1)S(1)}, bf16[2,2,128,256]{3,2,1,0:T(8,128)(2,1)S(1)}, u32[]{:S(2)}, u32[]{:S(2)}) collective-permute-start(bf16[2,2,128,256]{3,2,1,0:T(8,128)(2,1)S(1)} %collective-permute-done.28.refs_6_), channel_id=1, source_target_pairs={{0,2},{1,3},{2,0},{3,1},{4,6},{5,7},{6,4},{7,5},{8,10},{9,11},{10,... | collective-permute-start | bytes 786440 | tf_op jit(solution)/shard_map/ppermute | solution.py:40
  150.9 11.0 %collective-permute-start.37 = (bf16[2,2,128,256]{3,2,1,0:T(8,128)(2,1)S(1)}, bf16[2,2,128,256]{3,2,1,0:T(8,128)(2,1)S(1)}, u32[]{:S(2)}, u32[]{:S(2)}) collective-permute-start(bf16[2,2,128,256]{3,2,1,0:T(8,128)(2,1)S(1)} %collective-permute-done.35.refs_14_), channel_id=1, source_target_pairs={{0,4},{1,5},{2,6},{3,7},{4,8},{5,9},{6,10},{7,11},{8,12},{9,13},{1... | collective-permute-start | bytes 786440 | tf_op jit(solution)/shard_map/ppermute | solution.py:40
  151.0 11.2 %collective-permute-start.36 = (bf16[2,2,128,256]{3,2,1,0:T(8,128)(2,1)S(1)}, bf16[2,2,128,256]{3,2,1,0:T(8,128)(2,1)S(1)}, u32[]{:S(2)}, u32[]{:S(2)}) collective-permute-start(bf16[2,2,128,256]{3,2,1,0:T(8,128)(2,1)S(1)} %collective-permute-done.35.refs_14_), channel_id=1, source_target_pairs={{0,2},{1,3},{2,0},{3,1},{4,6},{5,7},{6,4},{7,5},{8,10},{9,11},{10,... | collective-permute-start | bytes 786440 | tf_op jit(solution)/shard_map/ppermute | solution.py:40
  156.6 11.0 %collective-permute-start.32 = (bf16[2,2,128,256]{3,2,1,0:T(8,128)(2,1)S(1)}, bf16[2,2,128,256]{3,2,1,0:T(8,128)(2,1)S(1)}, u32[]{:S(2)}, u32[]{:S(2)}) collective-permute-start(bf16[2,2,128,256]{3,2,1,0:T(8,128)(2,1)S(1)} %collective-permute-done.30.refs_7_), channel_id=1, source_target_pairs={{0,4},{1,5},{2,6},{3,7},{4,8},{5,9},{6,10},{7,11},{8,12},{9,13},{1... | collective-permute-start | bytes 786440 | tf_op jit(solution)/shard_map/ppermute | solution.py:40
  156.6 11.2 %collective-permute-start.31 = (bf16[2,2,128,256]{3,2,1,0:T(8,128)(2,1)S(1)}, bf16[2,2,128,256]{3,2,1,0:T(8,128)(2,1)S(1)}, u32[]{:S(2)}, u32[]{:S(2)}) collective-permute-start(bf16[2,2,128,256]{3,2,1,0:T(8,128)(2,1)S(1)} %collective-permute-done.30.refs_7_), channel_id=1, source_target_pairs={{0,2},{1,3},{2,0},{3,1},{4,6},{5,7},{6,4},{7,5},{8,10},{9,11},{10,... | collective-permute-start | bytes 786440 | tf_op jit(solution)/shard_map/ppermute | solution.py:40
  162.2 9.2 %collective-permute-start.39 = (bf16[2,2,128,256]{3,2,1,0:T(8,128)(2,1)S(1)}, bf16[2,2,128,256]{3,2,1,0:T(8,128)(2,1)S(1)}, u32[]{:S(2)}, u32[]{:S(2)}) collective-permute-start(bf16[2,2,128,256]{3,2,1,0:T(8,128)(2,1)S(1)} %collective-permute-done.37.refs_15_), channel_id=1, source_target_pairs={{0,4},{1,5},{2,6},{3,7},{4,8},{5,9},{6,10},{7,11},{8,12},{9,13},{1... | collective-permute-start | bytes 786440 | tf_op jit(solution)/shard_map/ppermute | solution.py:40
  162.3 11.2 %collective-permute-start.38 = (bf16[2,2,128,256]{3,2,1,0:T(8,128)(2,1)S(1)}, bf16[2,2,128,256]{3,2,1,0:T(8,128)(2,1)S(1)}, u32[]{:S(2)}, u32[]{:S(2)}) collective-permute-start(bf16[2,2,128,256]{3,2,1,0:T(8,128)(2,1)S(1)} %collective-permute-done.37.refs_15_), channel_id=1, source_target_pairs={{0,2},{1,3},{2,0},{3,1},{4,6},{5,7},{6,4},{7,5},{8,10},{9,11},{10,... | collective-permute-start | bytes 786440 | tf_op jit(solution)/shard_map/ppermute | solution.py:40
  167.8 11.2 %collective-permute-start.33 = (bf16[2,2,128,256]{3,2,1,0:T(8,128)(2,1)S(1)}, bf16[2,2,128,256]{3,2,1,0:T(8,128)(2,1)S(1)}, u32[]{:S(2)}, u32[]{:S(2)}) collective-permute-start(bf16[2,2,128,256]{3,2,1,0:T(8,128)(2,1)S(1)} %collective-permute-done.32.refs_8_), channel_id=1, source_target_pairs={{0,2},{1,3},{2,0},{3,1},{4,6},{5,7},{6,4},{7,5},{8,10},{9,11},{10,... | collective-permute-start | bytes 786440 | tf_op jit(solution)/shard_map/ppermute | solution.py:40
  173.4 9.2 %collective-permute-start.40 = (bf16[2,2,128,256]{3,2,1,0:T(8,128)(2,1)S(1)}, bf16[2,2,128,256]{3,2,1,0:T(8,128)(2,1)S(1)}, u32[]{:S(2)}, u32[]{:S(2)}) collective-permute-start(bf16[2,2,128,256]{3,2,1,0:T(8,128)(2,1)S(1)} %collective-permute-done.39.refs_16_), channel_id=1, source_target_pairs={{0,2},{1,3},{2,0},{3,1},{4,6},{5,7},{6,4},{7,5},{8,10},{9,11},{10,... | collective-permute-start | bytes 786440 | tf_op jit(solution)/shard_map/ppermute | solution.py:40
  184.1 1.6 collective-permute-start.41

commit v4 on v3

--- a/solution.py
+++ b/solution.py
@@ -38,14 +38,6 @@
             target = (((z + dz) % self.z) * 2 + (y ^ dy)) * 2 + (b ^ db)
             pairs.append((index, target))
         return lax.ppermute(array, "chol", pairs)
-
-    def shift_all(self, array, dw, db):
-        pairs = []
-        for group in range(self.walk):
-            for index in range(self.chol):
-                target = ((group + dw) % self.walk) * self.chol + (index ^ db)
-                pairs.append((group * self.chol + index, target))
-        return lax.ppermute(array, ("walk", "chol"), pairs)
 
     def swap(self, array, distance):
         pairs = [(i, (((i // 4) ^ distance) * 4) + i % 4) for i in range(self.chol)]
@@ -78,112 +70,93 @@
         return ring + [(array, self.walker, dz, 1) for dz, array in enumerate(self.across)]
 
 
-def diagonal(shape):
-    return lax.broadcasted_iota(jnp.int32, shape, 0) == lax.broadcasted_iota(jnp.int32, shape, 1)
-
-
-def to_message(total):
-    rounded = total.astype(BF16)
-    rest = jnp.where(diagonal(total.shape), total - rounded.astype(F32), 0.0)
-    rest = jnp.broadcast_to(jnp.sum(rest, axis=0, keepdims=True), (BLOCK, total.shape[1]))
-    return jnp.concatenate([rounded, rest.astype(BF16)], axis=0)
-
-
-def from_message(message):
-    size = message.shape[1]
-    matrix = message[:size].astype(F32)
-    rest = message[size:].astype(F32)[:1]
-    return matrix + jnp.where(diagonal(matrix.shape), rest, 0.0)
-
-
-def intersection_kernel(places, mine, theirs, trial_mine, trial_theirs, *outs):
-    count = mine.shape[0] // 2
-    first = trial_mine[...].T
-    second = trial_theirs[...].T
+def gathered(layout, dz, dy):
     index = lax.axis_index("chol")
-    z, base = index // 4, lax.rem(index, 2) * count
-    for step in range(count):
-        walker = base + (lax.rem(z + step, count) if places else step)
-        total = jnp.dot(first, mine[walker], preferred_element_type=F32)
-        total += jnp.dot(second, theirs[walker], preferred_element_type=F32)
-        outs[step][...] = to_message(total) if places and step else total
-
-
-def intersections_of(mine, theirs, trial_mine, trial_theirs, places):
-    per_group, _, electrons = mine.shape
-    count = per_group // 2
-    whole = jax.ShapeDtypeStruct((electrons, electrons), F32)
-    message = jax.ShapeDtypeStruct((electrons + BLOCK, electrons), BF16)
-    return pl.pallas_call(
-        functools.partial(intersection_kernel, places),
-        out_shape=[whole] + [message if places else whole] * (count - 1),
-        in_specs=vmem_specs(4),
-        out_specs=vmem_specs(count),
+    z, y = index // 4, lax.rem(index // 2, 2)
+    return lax.rem(z + (layout.z - dz), layout.z) * 2 + (y + dy - 2 * y * dy)
+
+
+def transpose_kernel(layout, mine, theirs, out, buffer):
+    b = lax.rem(lax.axis_index("chol"), 2)
+    for dz in range(layout.z):
+        for dy in range(2):
+            chip = gathered(layout, dz, dy)
+            buffer[chip, b] = mine[dz, dy]
+            buffer[chip, 1 - b] = theirs[dz, dy]
+    out[...] = buffer[...].reshape(-1, buffer.shape[-1]).T
+
+
+def transposed(layout, mine, theirs):
+    _, _, rows, electrons = mine.shape
+    chips = layout.chol // 2
+    return pl.pallas_call(
+        functools.partial(transpose_kernel, layout),
+        out_shape=jax.ShapeDtypeStruct((electrons, layout.chol * rows), BF16),
+        in_specs=vmem_specs(2),
+        out_specs=pl.BlockSpec(memory_space=pltpu.VMEM),
+        scratch_shapes=[pltpu.VMEM((chips, 2, rows, electrons), BF16)],
         compiler_params=params(8),
-    )(mine, theirs, trial_mine, trial_theirs)
-
-
-def sum_kernel(own, *refs):
-    messages, (total_out, message_out) = refs[:-2], refs[-2:]
-    total = own[...]
-    for message in messages:
-        total = total + from_message(message[...])
-    total_out[...] = total
-    message_out[...] = to_message(total)
-
-
-def sum_of(own, messages):
-    return pl.pallas_call(
-        sum_kernel,
-        out_shape=[
-            jax.ShapeDtypeStruct(own.shape, F32),
-            jax.ShapeDtypeStruct(messages[0].shape, BF16),
-        ],
-        in_specs=vmem_specs(1 + len(messages)),
-        out_specs=vmem_specs(2),
-        compiler_params=params(8),
-    )(own, *messages)
-
-
-def newton_kernel(own, *refs):
-    messages, out = refs[:-1], refs[-1]
-    matrix = own[...]
-    for message in messages:
-        matrix = matrix + from_message(message[...])
-    twice = jnp.where(diagonal(matrix.shape), 2.0, 0.0).astype(F32)
-    estimate = twice - matrix
+    )(mine, theirs)
+
+
+def newton_inverses(matrices):
+    shape = matrices[0].shape
+    same = lax.broadcasted_iota(jnp.int32, shape, 0) == lax.broadcasted_iota(jnp.int32, shape, 1)
+    twice = jnp.where(same, 2.0, 0.0).astype(F32)
+    estimates = [twice - matrix for matrix in matrices]
     for _ in range(ITERS - 1):
-        product = jnp.dot(matrix, estimate, precision=HIGHEST, preferred_element_type=F32)
-        estimate = jnp.dot(
-            estimate, twice - product, precision=HIGHEST, preferred_element_type=F32
-        )
-    out[...] = estimate.astype(out.dtype)
-
-
-def newton_of(own, messages=()):
-    return pl.pallas_call(
-        newton_kernel,
-        out_shape=jax.ShapeDtypeStruct(own.shape, BF16),
-        in_specs=vmem_specs(1 + len(messages)),
+        products = [
+            jnp.dot(matrix, estimate, precision=HIGHEST, preferred_element_type=F32)
+            for matrix, estimate in zip(matrices, estimates)
+        ]
+        estimates = [
+            jnp.dot(estimate, twice - product, precision=HIGHEST, preferred_element_type=F32)
+            for estimate, product in zip(estimates, products)
+        ]
+    return estimates
+
+
+def inverse_kernel(layout, places, trial, *refs):
+    pieces, (out, buffer) = refs[:-2], refs[-2:]
+    matrices = []
+    for walker in range(out.shape[0]):
+        for piece, (dz, dy) in zip(pieces, places):
+            buffer[walker, gathered(layout, dz, dy)] = piece[walker]
+        full = buffer[walker]
+        full = full.reshape(-1, full.shape[-1])
+        matrices.append(jnp.dot(trial[...], full, preferred_element_type=F32))
+    for walker, inverse in enumerate(newton_inverses(matrices)):
+        out[walker] = inverse.astype(out.dtype)
+
+
+def inverses_of(layout, trial, stream):
+    arrays = [piece[0] for piece in stream.pieces()]
+    places = [piece[2:] for piece in stream.pieces()]
+    count, _, rows, electrons = arrays[0].shape
+    return pl.pallas_call(
+        functools.partial(inverse_kernel, layout, places),
+        out_shape=jax.ShapeDtypeStruct((count, electrons, electrons), BF16),
+        in_specs=vmem_specs(1 + len(arrays)),
         out_specs=pl.BlockSpec(memory_space=pltpu.VMEM),
-        compiler_params=params(8),
-    )(own, *messages)
-
-
-def bias_kernel(places, mine, theirs, rot_mine, rot_theirs, *refs):
-    inverses, out, greens = refs[:-2], refs[-2], refs[-1]
-    count = len(inverses)
-    rows, electrons = mine.shape[1], mine.shape[2]
-    vectors = rot_mine.shape[0]
-    index = lax.axis_index("chol")
-    z, base = index // 4, lax.rem(index, 2) * count
-    for at in range(count):
-        walker = base + (lax.rem(z + (count - at), count) if places else at)
-        both = jnp.concatenate([mine[walker], theirs[walker]], axis=0)
-        product = jnp.dot(both, inverses[at][...], preferred_element_type=F32).astype(BF16)
-        greens[:, :, at] = product.reshape(2, rows // BLOCK, BLOCK, electrons)
+        scratch_shapes=[pltpu.VMEM((count, layout.chol // 2, 2, rows, electrons), BF16)],
+        compiler_params=params(16),
+    )(trial, *arrays)
+
+
+def bias_kernel(sizes, rot_mine, rot_theirs, *refs):
+    streams = len(sizes)
+    chunks, inverses, (out, greens) = refs[:streams], refs[streams : 2 * streams], refs[-2:]
+    vectors, rows, electrons = rot_mine.shape
+    b = lax.rem(lax.axis_index("chol"), 2)
+    count = 0
+    for chunk, inverse, size in zip(chunks, inverses, sizes):
+        for walker in range(size):
+            both = chunk[walker].reshape(2 * rows, electrons)
+            product = jnp.dot(both, inverse[walker], preferred_element_type=F32).astype(BF16)
+            greens[:, :, count] = product.reshape(2, rows // BLOCK, BLOCK, electrons)
+            count += 1
     total = jnp.zeros((vectors * BLOCK, count * BLOCK), F32)
-    for half, rot in enumerate((rot_mine, rot_theirs)):
+    for half, rot in ((b, rot_mine), (1 - b, rot_theirs)):
         for block in range(rows // BLOCK):
             total += lax.dot_general(
                 rot[:, block * BLOCK : (block + 1) * BLOCK, :].reshape(vectors * BLOCK, electrons),
@@ -198,22 +171,23 @@
         jnp.where(same, total, 0.0).reshape(vectors, BLOCK, count * BLOCK), axis=1
     )
     shape = (count, count * BLOCK)
-    walker = lax.broadcasted_iota(jnp.int32, shape, 0)
-    place = lax.rem(lax.rem(z, count) + (count - walker), count) if places else walker
-    pick = (lax.broadcasted_iota(jnp.int32, shape, 1) // BLOCK == place).astype(F32)
+    pick = (
+        lax.broadcasted_iota(jnp.int32, shape, 1) // BLOCK
+        == lax.broadcasted_iota(jnp.int32, shape, 0)
+    ).astype(F32)
     out[...] = lax.dot_general(
         pick, summed, (((1,), (1,)), ((), ())), precision=HIGHEST, preferred_element_type=F32
     )
 
 
-def bias_of(mine, theirs, rot_mine, rot_theirs, inverses, places):
-    _, rows, electrons = mine.shape
-    count = len(inverses)
-    vectors = rot_mine.shape[0]
-    return pl.pallas_call(
-        functools.partial(bias_kernel, places),
+def bias_of(chunks, inverses, rot_mine, rot_theirs):
+    vectors, rows, electrons = rot_mine.shape
+    sizes = [chunk.shape[0] for chunk in chunks]
+    count = sum(sizes)
+    return pl.pallas_call(
+        functools.partial(bias_kernel, sizes),
         out_shape=jax.ShapeDtypeStruct((count, vectors), F32),
-        in_specs=vmem_specs(4 + count),
+        in_specs=vmem_specs(2 + 2 * len(sizes)),
         out_specs=pl.BlockSpec(memory_space=pltpu.VMEM),
         scratch_shapes=[pltpu.VMEM((2, rows // BLOCK, count, BLOCK, electrons), BF16)],
         compiler_params=params(12),
@@ -222,23 +196,19 @@
             bytes_accessed=4 * (vectors + count) * rows * electrons,
             transcendentals=0,
         ),
-    )(mine, theirs, rot_mine, rot_theirs, *inverses)
-
-
-def weights_kernel(origins, layout, order, fields, source, *refs):
-    pieces, (bias_out, weights) = refs[:-2], refs[-2:]
+    )(rot_mine, rot_theirs, *chunks, *inverses)
+
+
+def weights_kernel(order, fields, mine, theirs, bias_out, weights):
     per_group, vectors = fields.shape
-    half = pieces[0].shape[0]
-    group = lax.axis_index("walk")
-    b = lax.rem(lax.axis_index("chol"), 2)
-    wanted = source[...]
+    half = mine.shape[0]
+    b = lax.rem(lax.axis_index("chol"), 2)
+    row = lax.broadcasted_iota(jnp.int32, (per_group, vectors), 0)
     bias = jnp.zeros((per_group, vectors), F32)
-    for (dw, db), piece in zip(origins, pieces):
-        from_group = lax.rem(group + (layout.walk - dw), layout.walk)
-        from_b = b + db - 2 * b * db
-        base = from_group * per_group + from_b * half
-        for row in range(half):
-            bias += jnp.where(wanted == base + row, piece[row : row + 1, :], 0.0)
+    for walker in range(half):
+        for part, core in ((mine, b), (theirs, 1 - b)):
+            slot = order[core * half + walker]
+            bias += jnp.where(row == slot, part[walker : walker + 1, :], 0.0)
     bias = TAU_ROOT * bias
     bias_out[...] = bias
     shifted = (fields[...] - bias).astype(BF16)
@@ -261,20 +231,18 @@
     weights[...] = jnp.where(same, spread, 0.0).astype(BF16)
 
 
-def weights_of(layout, order, fields, source, pieces):
+def weights_of(order, fields, mine, theirs):
     per_group, vectors = fields.shape
-    origins = [origin for origin, _ in pieces]
-    arrays = [array for _, array in pieces]
-    return pl.pallas_call(
-        functools.partial(weights_kernel, origins, layout),
+    return pl.pallas_call(
+        weights_kernel,
         out_shape=[
             jax.ShapeDtypeStruct((per_group, vectors), F32),
             jax.ShapeDtypeStruct((per_group * BLOCK, vectors * BLOCK), BF16),
         ],
-        in_specs=[pl.BlockSpec(memory_space=pltpu.SMEM)] + vmem_specs(2 + len(arrays)),
+        in_specs=[pl.BlockSpec(memory_space=pltpu.SMEM)] + vmem_specs(3),
         out_specs=vmem_specs(2),
         compiler_params=params(8),
-    )(order, fields, source, *arrays)
+    )(order, fields, mine, theirs)
 
 
 def potential_kernel(start, weights, cholesky, kept, sent, blocks, semaphores):
@@ -316,12 +284,9 @@
 
 
 def fold(layout, places, kept, theirs, pieces, buffer, walker):
-    index = lax.axis_index("chol")
-    z, y = index // 4, lax.rem(index // 2, 2)
     for piece, (count, first, dz, dy) in zip(pieces, places):
         if first <= walker < first + count:
-            chip = lax.rem(z + (layout.z - dz), layout.z) * 2 + (y + dy - 2 * y * dy)
-            buffer[walker, chip] = piece[walker - first]
+            buffer[walker, gathered(layout, dz, dy)] = piece[walker - first]
     rows = jnp.concatenate([part[walker] for part in (*kept, *theirs)], axis=0)
     full = buffer[walker]
     return jnp.dot(rows, full.reshape(-1, full.shape[-1]), preferred_element_type=F32)
@@ -522,64 +487,60 @@
 
 
 def shards(layout, walkers, trial, cholesky, rotated, fields, source):
-    per_group = walkers.shape[0]
-    half = per_group // 2
-    group = lax.axis_index("walk")
+    half = walkers.shape[0] // 2
+    sizes = (half // 2, half - half // 2)
     b = lax.axis_index("chol") % 2
+
+    pairs = [jnp.stack([trial, layout.shift(trial, dy=1)])]
     own, other, order = migrate(layout, walkers, source)
-    trial_theirs = layout.shift(trial, db=1)
-    theirs = layout.shift(walkers, db=1)
-    rot_theirs = layout.shift(rotated, db=1)
-    places = layout.z == half
-    partial = intersections_of(walkers, theirs, trial, trial_theirs, places)
-    if places:
-        messages = [layout.shift(partial[dz], dz=dz) for dz in range(1, half)]
-        messages, own, other = lax.optimization_barrier((messages, own, other))
-        total, message = sum_of(partial[0], messages)
-        inverse = newton_of(total, [layout.shift(message, dy=1)])
+    for _ in range(layout.z // 2):
+        pairs.append(layout.shift(pairs[-1], dz=1))
+    own, other, pairs = lax.optimization_barrier((own, other, pairs))
+    for _ in range(layout.z - len(pairs)):
+        pairs.append(layout.shift(pairs[-1], dz=1))
     chunk = jnp.stack([jnp.where(b == 0, own, other), jnp.where(b == 0, other, own)], axis=1)
-    migrated = Stream(layout, chunk)
-    if places:
-        (inverse,) = migrated.advance((inverse,))
-        inverses = [inverse] + [layout.shift(inverse, dz=dz) for dz in range(1, half)]
-    else:
-        spread = jnp.zeros((per_group,) + partial[0].shape, F32)
-        spread = lax.dynamic_update_slice_in_dim(spread, jnp.stack(partial), b * half, 0)
-        summed = lax.dynamic_slice_in_dim(lax.psum(spread, "chol"), b * half, half, 0)
-        inverses = [newton_of(summed[index]) for index in range(half)]
-    inverses = migrated.advance(inverses)
-
-    total = bias_of(walkers, theirs, rotated, rot_theirs, inverses, places)
+    chunks = [chunk[: sizes[0]], chunk[sizes[0] :]]
+    streams = [Stream(layout, chunks[0]), Stream(layout, chunks[1], sizes[0])]
+    for stage in range(layout.z):
+        if stage == 0:
+            pairs = streams[0].advance(pairs)
+            streams[1].advance()
+            planes = jnp.stack(pairs)
+            planes_theirs = layout.shift(planes, db=1)
+            rot_theirs = layout.shift(rotated, db=1)
+        elif stage == 1:
+            planes_theirs, rot_theirs = streams[0].advance((planes_theirs, rot_theirs))
+            streams[1].advance()
+            turned = transposed(layout, planes, planes_theirs)
+        elif stage == 2:
+            (turned,) = streams[0].advance((turned,))
+            streams[1].advance()
+        else:
+            for stream in streams:
+                stream.advance()
+
+    inverses = [inverses_of(layout, turned, stream) for stream in streams]
+    total = bias_of(chunks, inverses, rotated, rot_theirs)
     distance = layout.z // 2
     while distance:
         total = total + layout.swap(total, distance)
         distance //= 2
     total = total + layout.shift(total, dy=1)
-    pieces = []
-    for dw in range(layout.walk):
-        for db in range(2):
-            moved = layout.shift_all(total, dw, db) if dw + db else total
-            pieces.append(((dw, db), moved))
-
-    wanted = lax.dynamic_slice_in_dim(source, group * per_group, per_group)[:, None]
-    force_bias, weights = weights_of(layout, order, fields, wanted, pieces)
-    (weights,) = migrated.advance((weights,))
+    force_bias, weights = weights_of(order, fields, total, layout.shift(total, db=1))
     kept, received = [], []
     for part in range(2):
         mine, sent = potential_of(weights, cholesky, part, 2)
         kept.append(mine)
         received.append(layout.shift(sent, db=1))
 
-    while len(migrated.across) < layout.z:
-        migrated.advance()
-    sizes = (half // 2, half - half // 2)
-    *firsts, base = first_of(layout, kept, received, migrated.pieces(), sizes)
-    streams = [Stream(layout, first, at * sizes[0]) for at, first in enumerate(firsts)]
+    pieces = [piece for stream in streams for piece in stream.pieces()]
+    *firsts, base = first_of(layout, kept, received, pieces, sizes)
+    streams = [Stream(layout, firsts[0]), Stream(layout, firsts[1], sizes[0])]
     for _ in range(layout.z):
         for stream in streams:
             stream.advance()
-    gathered = [piece for stream in streams for piece in stream.pieces()]
-    mine, sent = second_of(layout, kept, received, base, gathered)
+    pieces = [piece for stream in streams for piece in stream.pieces()]
+    mine, sent = second_of(layout, kept, received, base, pieces)
     return place(order, mine, layout.shift(sent, db=1)), force_bias
 
 

time: 187 us -> 168 us (0.90)
  starting transfers between devices: 42.5 us -> 24.9 us
  local copies, waits for them, and re-layouts: 6.85 us -> 1.71 us
  waiting for transfers between devices: 111 us -> 114 us
    ppermute x35 -> x39, starting transfers between devices: 35.4 us -> 21.4 us  [shift(): return lax.ppermute(array, 'chol', pairs)]
    ppermute x35 -> x39, waiting for transfers between devices: 101 us -> 106 us  [shift(): return lax.ppermute(array, 'chol', pairs)]
    unnamed x34 -> x8, local copies, waits for them, and re-layouts: 6.69 us -> 1.71 us
    ppermute x2, starting transfers between devices: 4.52 us -> 0.01 us  [swap(): return lax.ppermute(array, 'chol', pairs)]
    ppermute x1, starting transfers between devices: 0.01 us -> 2.8 us  [migrate(): lax.ppermute(second, axes, cross)]
  transfers between devices with their start and end apart: 42 -> 43, of which waited for: 27 -> 29; matrix products, arithmetic and copies ran while one was open for 1% -> 1% of each run, Pallas kernels for 6% -> 3%
where the time goes in v4:
time: 168 us; the launch traced here: 167 us
  waiting for transfers between devices  114 us (68%)
  starting transfers between devices  24.9 us (15%)
  Pallas kernels  24.4 us (15%)
  local copies, waits for them, and re-layouts  1.71 us (1%)
    ppermute x39, waiting for transfers between devices, shift(): return lax.ppermute(array, 'chol', pairs)  106 us
    ppermute x39, starting transfers between devices, shift(): return lax.ppermute(array, 'chol', pairs)  21.4 us
    ppermute x2, waiting for transfers between devices, swap(): return lax.ppermute(array, 'chol', pairs)  8.09 us
    pallas_call x2, Pallas kernels, potential_of(): pl.pallas_call(functools.partial(potential_kernel, part * rows), out_shap...  7.92 us
    pallas_call x2, Pallas kernels, inverses_of(): pl.pallas_call(functools.partial(inverse_kernel, layout, places), out_sha...  6.58 us
  transfers between devices with their start and end apart: 43, of which 29 were waited for; matrix products, arithmetic and copies ran while one was open for 1% of the time, Pallas kernels for 3%

profile of v4, /device:TPU:0, one launch (start us, length us, event | category | flops | bytes accessed | tf_op | source)
XLA Modules:
  0.0 167.3 jit_solution(10642831477629499038)
XLA Ops:
  0.6 0.5 collective-permute-start.9
  1.1 2.6 %collective-permute-start.2 = (bf16[128,256]{1,0:T(8,128)(2,1)}, bf16[128,256]{1,0:T(8,128)(2,1)S(1)}, u32[]{:S(2)}, u32[]{:S(2)}) collective-permute-start(bf16[128,256]{1,0:T(8,128)(2,1)} %param.7), channel_id=1, source_target_pairs={{0,2},{1,3},{2,0},{3,1},{4,6},{5,7},{6,4},{7,5},{8,10},{9,11},{10,... | collective-permute-start | bytes 196616 | tf_op jit(solution)/shard_map/ppermute | solution.py:40
  3.7 1.0 copy-done.1
  4.8 0.7 copy-done.3
  5.4 2.0 %shard_map.77 = (bf16[4,128,256]{2,1,0:T(8,128)(2,1)S(1)}, bf16[4,128,256]{2,1,0:T(8,128)(2,1)S(1)}, s32[8]{0:T(128)S(1)}) custom-call(s32[16]{0:T(128)S(1)} %copy-done.3, bf16[8,128,256]{2,1,0:T(8,128)(2,1)S(1)} %copy-done.1), custom_call_target="tpu_custom_call" | custom-call | tf_op jit(solution)/shard_map/pallas_call | solution.py:426
  7.4 0.7 collective-permute-start
  8.1 2.8 %collective-permute-start.1 = (bf16[4,128,256]{2,1,0:T(8,128)(2,1)S(1)}, bf16[4,128,256]{2,1,0:T(8,128)(2,1)S(1)}, u32[]{:S(2)}, u32[]{:S(2)}) collective-permute-start(bf16[4,128,256]{2,1,0:T(8,128)(2,1)S(1)} %get-tuple-element.54), channel_id=1, source_target_pairs={{0,17},{1,0},{2,19},{3,2},{4,21},{5,4},{6,23},{7,6},{8,25},{9,8},{... | collective-permute-start | bytes 786440 | tf_op jit(solution)/shard_map/ppermute | solution.py:462
  10.9 0.9 pad_maximum_fusion.2
  11.8 1.6 collective-permute-start.3
  13.4 5.6 %collective-permute-done.3 = bf16[2,128,256]{2,1,0:T(8,128)(2,1)S(1)} collective-permute-done((bf16[2,128,256]{2,1,0:T(8,128)(2,1)S(1)}, bf16[2,128,256]{2,1,0:T(8,128)(2,1)S(1)}, u32[]{:S(2)}, u32[]{:S(2)}) %collective-permute-start.3) | collective-permute-done | bytes 131104 | tf_op jit(solution)/shard_map/ppermute | solution.py:40
  19.0 6.8 %collective-permute-done.4 = bf16[2,128,256]{2,1,0:T(8,128)(2,1)S(1)} collective-permute-done((bf16[2,128,256]{2,1,0:T(8,128)(2,1)S(1)}, bf16[2,128,256]{2,1,0:T(8,128)(2,1)S(1)}, u32[]{:S(2)}, u32[]{:S(2)}) %collective-permute-start.4) | collective-permute-done | bytes 131104 | tf_op jit(solution)/shard_map/ppermute | solution.py:40
  25.9 0.6 collective-permute-start.15
  26.5 1.5 collective-permute-start.6
  28.0 8.9 %collective-permute-done.16.refs_1_.refs_13_ = bf16[2,2,128,256]{3,2,1,0:T(8,128)(2,1)S(1)} collective-permute-done((bf16[2,2,128,256]{3,2,1,0:T(8,128)(2,1)S(1)}, bf16[2,2,128,256]{3,2,1,0:T(8,128)(2,1)S(1)}, u32[]{:S(2)}, u32[]{:S(2)}) %collective-permute-start.16) | collective-permute-done | bytes 262176 | tf_op jit(solution)/shard_map/ppermute | solution.py:40
  37.0 8.1 %collective-permute-done.5 = bf16[2,128,256]{2,1,0:T(8,128)(2,1)S(1)} collective-permute-done((bf16[2,128,256]{2,1,0:T(8,128)(2,1)S(1)}, bf16[2,128,256]{2,1,0:T(8,128)(2,1)S(1)}, u32[]{:S(2)}, u32[]{:S(2)}) %collective-permute-start.5) | collective-permute-done | bytes 131104 | tf_op jit(solution)/shard_map/ppermute | solution.py:40
  45.2 0.8 collective-permute-start.17
  46.1 1.8 %collective-permute-done.18.refs_2_.refs_14_ = bf16[2,2,128,256]{3,2,1,0:T(8,128)(2,1)S(1)} collective-permute-done((bf16[2,2,128,256]{3,2,1,0:T(8,128)(2,1)S(1)}, bf16[2,2,128,256]{3,2,1,0:T(8,128)(2,1)S(1)}, u32[]{:S(2)}, u32[]{:S(2)}) %collective-permute-start.18) | collective-permute-done | bytes 262176 | tf_op jit(solution)/shard_map/ppermute | solution.py:40
  47.9 0.8 collective-permute-start.10
  48.6 5.8 %collective-permute-done.17.refs_5_.refs_17_ = bf16[2,2,128,256]{3,2,1,0:T(8,128)(2,1)S(1)} collective-permute-done((bf16[2,2,128,256]{3,2,1,0:T(8,128)(2,1)S(1)}, bf16[2,2,128,256]{3,2,1,0:T(8,128)(2,1)S(1)}, u32[]{:S(2)}, u32[]{:S(2)}) %collective-permute-start.17) | collective-permute-done | bytes 262176 | tf_op jit(solution)/shard_map/ppermute | solution.py:40
  54.4 1.8 %collective-permute-done.11.refs_2_.refs_6_ = bf16[2,2,128,256]{3,2,1,0:T(8,128)(2,1)S(1)} collective-permute-done((bf16[2,2,128,256]{3,2,1,0:T(8,128)(2,1)S(1)}, bf16[2,2,128,256]{3,2,1,0:T(8,128)(2,1)S(1)}, u32[]{:S(2)}, u32[]{:S(2)}) %collective-permute-start.11) | collective-permute-done | bytes 262176 | tf_op jit(solution)/shard_map/ppermute | solution.py:40
  56.2 1.3 collective-permute-start.19
  57.5 2.5 %collective-permute-done.10.refs_5_.refs_9_ = bf16[2,2,128,256]{3,2,1,0:T(8,128)(2,1)S(1)} collective-permute-done((bf16[2,2,128,256]{3,2,1,0:T(8,128)(2,1)S(1)}, bf16[2,2,128,256]{3,2,1,0:T(8,128)(2,1)S(1)}, u32[]{:S(2)}, u32[]{:S(2)}) %collective-permute-start.10) | collective-permute-done | bytes 262176 | tf_op jit(solution)/shard_map/ppermute | solution.py:40
  60.0 0.8 collective-permute-start.12
  60.9 2.8 %collective-permute-done.20.refs_3_.refs_15_ = bf16[2,2,128,256]{3,2,1,0:T(8,128)(2,1)S(1)} collective-permute-done((bf16[2,2,128,256]{3,2,1,0:T(8,128)(2,1)S(1)}, bf16[2,2,128,256]{3,2,1,0:T(8,128)(2,1)S(1)}, u32[]{:S(2)}, u32[]{:S(2)}) %collective-permute-start.20) | collective-permute-done | bytes 262176 | tf_op jit(solution)/shard_map/ppermute | solution.py:40
  63.6 2.0 %collective-permute-done.19.refs_6_.refs_18_ = bf16[2,2,128,256]{3,2,1,0:T(8,128)(2,1)S(1)} collective-permute-done((bf16[2,2,128,256]{3,2,1,0:T(8,128)(2,1)S(1)}, bf16[2,2,128,256]{3,2,1,0:T(8,128)(2,1)S(1)}, u32[]{:S(2)}, u32[]{:S(2)}) %collective-permute-start.19) | collective-permute-done | bytes 262176 | tf_op jit(solution)/shard_map/ppermute | solution.py:40
  65.6 1.1 collective-permute-start.21
  67.2 2.1 %collective-permute-done.13.refs_3_.refs_7_ = bf16[2,2,128,256]{3,2,1,0:T(8,128)(2,1)S(1)} collective-permute-done((bf16[2,2,128,256]{3,2,1,0:T(8,128)(2,1)S(1)}, bf16[2,2,128,256]{3,2,1,0:T(8,128)(2,1)S(1)}, u32[]{:S(2)}, u32[]{:S(2)}) %collective-permute-start.13) | collective-permute-done | bytes 262176 | tf_op jit(solution)/shard_map/ppermute | solution.py:40
  69.3 2.0 %collective-permute-done.12.refs_6_.refs_10_ = bf16[2,2,128,256]{3,2,1,0:T(8,128)(2,1)S(1)} collective-permute-done((bf16[2,2,128,256]{3,2,1,0:T(8,128)(2,1)S(1)}, bf16[2,2,128,256]{3,2,1,0:T(8,128)(2,1)S(1)}, u32[]{:S(2)}, u32[]{:S(2)}) %collective-permute-start.12) | collective-permute-done | bytes 262176 | tf_op jit(solution)/shard_map/ppermute | solution.py:40
  71.3 1.1 collective-permute-start.14
  72.4 4.5 %collective-permute-done.21.refs_7_.refs_19_ = bf16[2,2,128,256]{3,2,1,0:T(8,128)(2,1)S(1)} collective-permute-done((bf16[2,2,128,256]{3,2,1,0:T(8,128)(2,1)S(1)}, bf16[2,2,128,256]{3,2,1,0:T(8,128)(2,1)S(1)}, u32[]{:S(2)}, u32[]{:S(2)}) %collective-permute-start.21) | collective-permute-done | bytes 262176 | tf_op jit(solution)/shard_map/ppermute | solution.py:40
  76.9 3.3 %shard_map.80.refs_3_ = bf16[2,256,256]{2,1,0:T(8,128)(2,1)S(1)} custom-call(bf16[256,2048]{1,0:T(8,128)(2,1)S(1)} %shard_map.78.trial, bf16[2,2,128,256]{3,2,1,0:T(8,128)(2,1)S(1)} %get-tuple-element.102.refs_0_.refs_1_.refs_12_, bf16[2,2,128,256]{3,2,1,0:T(8,128)(2,1)S(1)} %collective-permute-done.16.refs_1_.refs_13_, ...), custom_call_target="tpu_custom_call" | custom-call | tf_op jit(solution)/shard_map/pallas_call | solution.py:136
  80.2 1.9 %collective-permute-done.14.refs_7_.refs_11_ = bf16[2,2,128,256]{3,2,1,0:T(8,128)(2,1)S(1)} collective-permute-done((bf16[2,2,128,256]{3,2,1,0:T(8,128)(2,1)S(1)}, bf16[2,2,128,256]{3,2,1,0:T(8,128)(2,1)S(1)}, u32[]{:S(2)}, u32[]{:S(2)}) %collective-permute-start.14) | collective-permute-done | bytes 262176 | tf_op jit(solution)/shard_map/ppermute | solution.py:40
  82.1 3.3 %shard_map.79.refs_2_ = bf16[2,256,256]{2,1,0:T(8,128)(2,1)S(1)} custom-call(bf16[256,2048]{1,0:T(8,128)(2,1)S(1)} %shard_map.78.trial, bf16[2,2,128,256]{3,2,1,0:T(8,128)(2,1)S(1)} %get-tuple-element.103.refs_0_.refs_4_, bf16[2,2,128,256]{3,2,1,0:T(8,128)(2,1)S(1)} %collective-permute-done.7.refs_1_.refs_5_, ...), custom_call_target="tpu_custom_call" | custom-call | tf_op jit(solution)/shard_map/pallas_call | solution.py:136
  85.4 1.7 %shard_map.81 = f32[4,32]{1,0:T(4,128)S(1)} custom-call(bf16[32,128,256]{2,1,0:T(8,128)(2,1)S(1)} %copy-done, bf16[32,128,256]{2,1,0:T(8,128)(2,1)S(1)} %collective-permute-done.9.rot_theirs, bf16[2,2,128,256]{3,2,1,0:T(8,128)(2,1)S(1)} %get-tuple-element.103.refs_0_.refs_4_, bf16[2,2,128,256]{3,2,1,0:T(8,128)(2,1)S(1)} %get-tuple-element.102.refs_0_.refs_1_.refs_12_, ...), custom_call_target="tpu_custom_call" | custom-call | flops 402653184 | bytes 4718592 | tf_op jit(solution)/shard_map/pallas_call | solution.py:187
  87.1 4.5 %collective-permute-done.22 = f32[4,32]{1,0:T(4,128)S(1)} collective-permute-done((f32[4,32]{1,0:T(4,128)S(1)}, f32[4,32]{1,0:T(4,128)S(1)}, u32[]{:S(2)}, u32[]{:S(2)}) %collective-permute-start.22) | collective-permute-done | bytes 544 | tf_op jit(solution)/shard_map/ppermute | solution.py:44
  91.6 3.6 %collective-permute-done.23 = f32[4,32]{1,0:T(4,128)S(1)} collective-permute-done((f32[4,32]{1,0:T(4,128)S(1)}, f32[4,32]{1,0:T(4,128)S(1)}, u32[]{:S(2)}, u32[]{:S(2)}) %collective-permute-start.23) | collective-permute-done | bytes 544 | tf_op jit(solution)/shard_map/ppermute | solution.py:44
  95.2 0.8 collective-permute-start.24
  95.9 2.8 %collective-permute-done.24 = f32[4,32]{1,0:T(4,128)S(1)} collective-permute-done((f32[4,32]{1,0:T(4,128)S(1)}, f32[4,32]{1,0:T(4,128)S(1)}, u32[]{:S(2)}, u32[]{:S(2)}) %collective-permute-start.24) | collective-permute-done | bytes 544 | tf_op jit(solution)/shard_map/ppermute | solution.py:40
  98.8 1.2 collective-permute-done.25.theirs
  99.9 1.2 shard_map.82
  101.1 4.0 %shard_map.84 = (bf16[4,64,2048]{2,1,0:T(8,128)(2,1)S(1)}, bf16[4,64,2048]{2,1,0:T(8,128)(2,1)S(1)}) custom-call(bf16[128,512]{1,0:T(8,128)(2,1)S(1)} %get-tuple-element.79.weights, bf16[32,128,2048]{2,1,0:T(8,128)(2,1)} %cholesky.3), custom_call_target="tpu_custom_call" | custom-call | tf_op jit(solution)/shard_map/pallas_call | solution.py:273
  105.1 4.0 %shard_map.83 = (bf16[4,64,2048]{2,1,0:T(8,128)(2,1)S(1)}, bf16[4,64,2048]{2,1,0:T(8,128)(2,1)S(1)}) custom-call(bf16[128,512]{1,0:T(8,128)(2,1)S(1)} %get-tuple-element.79.weights, bf16[32,128,2048]{2,1,0:T(8,128)(2,1)} %cholesky.3), custom_call_target="tpu_custom_call" | custom-call | tf_op jit(solution)/shard_map/pallas_call | solution.py:273
  109.6 2.1 %collective-permute-done.27.refs_3_ = bf16[4,64,2048]{2,1,0:T(8,128)(2,1)S(1)} collective-permute-done((bf16[4,64,2048]{2,1,0:T(8,128)(2,1)S(1)}, bf16[4,64,2048]{2,1,0:T(8,128)(2,1)S(1)}, u32[]{:S(2)}, u32[]{:S(2)}) %collective-permute-start.27) | collective-permute-done | bytes 1048608 | tf_op jit(solution)/shard_map/ppermute | solution.py:40
  111.8 1.5 collective-permute-done.26.refs_2_
  113.3 1.7 %shard_map.85 = (bf16[2,2,128,256]{3,2,1,0:T(8,128)(2,1)S(1)}, bf16[2,2,128,256]{3,2,1,0:T(8,128)(2,1)S(1)}, f32[4,2,128,256]{3,2,1,0:T(8,128)S(1)}) custom-call(bf16[4,64,2048]{2,1,0:T(8,128)(2,1)S(1)} %get-tuple-element.80.refs_0_, bf16[4,64,2048]{2,1,0:T(8,128)(2,1)S(1)} %get-tuple-element.81.refs_1_, ...), custom_call_target="tpu_custom_call" | custom-call | flops 1073741824 | bytes 8388608 | tf_op jit(solution)/shard_map/pallas_call | solution.py:341
  115.0 0.8 collective-permute-start.28
  116.4 1.3 collective-permute-start.35
  117.6 8.3 %collective-permute-done.29.refs_6_ = bf16[2,2,128,256]{3,2,1,0:T(8,128)(2,1)S(1)} collective-permute-done((bf16[2,2,128,256]{3,2,1,0:T(8,128)(2,1)S(1)}, bf16[2,2,128,256]{3,2,1,0:T(8,128)(2,1)S(1)}, u32[]{:S(2)}, u32[]{:S(2)}) %collective-permute-start.29) | collective-permute-done | bytes 262176 | tf_op jit(solution)/shard_map/ppermute | solution.py:40
  126.0 0.8 collective-permute-start.30
  126.7 4.9 %collective-permute-done.36.refs_14_ = bf16[2,2,128,256]{3,2,1,0:T(8,128)(2,1)S(1)} collective-permute-done((bf16[2,2,128,256]{3,2,1,0:T(8,128)(2,1)S(1)}, bf16[2,2,128,256]{3,2,1,0:T(8,128)(2,1)S(1)}, u32[]{:S(2)}, u32[]{:S(2)}) %collective-permute-start.36) | collective-permute-done | bytes 262176 | tf_op jit(solution)/shard_map/ppermute | solution.py:40
  131.6 0.8 collective-permute-start.37
  132.4 4.9 %collective-permute-done.31.refs_7_ = bf16[2,2,128,256]{3,2,1,0:T(8,128)(2,1)S(1)} collective-permute-done((bf16[2,2,128,256]{3,2,1,0:T(8,128)(2,1)S(1)}, bf16[2,2,128,256]{3,2,1,0:T(8,128)(2,1)S(1)}, u32[]{:S(2)}, u32[]{:S(2)}) %collective-permute-start.31) | collective-permute-done | bytes 262176 | tf_op jit(solution)/shard_map/ppermute | solution.py:40
  137.2 0.8 collective-permute-start.32
  138.0 4.9 %collective-permute-done.38.refs_15_ = bf16[2,2,128,256]{3,2,1,0:T(8,128)(2,1)S(1)} collective-permute-done((bf16[2,2,128,256]{3,2,1,0:T(8,128)(2,1)S(1)}, bf16[2,2,128,256]{3,2,1,0:T(8,128)(2,1)S(1)}, u32[]{:S(2)}, u32[]{:S(2)}) %collective-permute-start.38) | collective-permute-done | bytes 262176 | tf_op jit(solution)/shard_map/ppermute | solution.py:40
  142.8 0.8 collective-permute-start.39
  143.6 4.9 %collective-permute-done.33.refs_8_ = bf16[2,2,128,256]{3,2,1,0:T(8,128)(2,1)S(1)} collective-permute-done((bf16[2,2,128,256]{3,2,1,0:T(8,128)(2,1)S(1)}, bf16[2,2,128,256]{3,2,1,0:T(8,128)(2,1)S(1)}, u32[]{:S(2)}, u32[]{:S(2)}) %collective-permute-start.33) | collective-permute-done | bytes 262176 | tf_op jit(solution)/shard_map/ppermute | solution.py:40
  148.5 0.8 collective-permute-start.34
  149.2 4.1 %collective-permute-done.40.refs_16_ = bf16[2,2,128,256]{3,2,1,0:T(8,128)(2,1)S(1)} collective-permute-done((bf16[2,2,128,256]{3,2,1,0:T(8,128)(2,1)S(1)}, bf16[2,2,128,256]{3,2,1,0:T(8,128)(2,1)S(1)}, u32[]{:S(2)}, u32[]{:S(2)}) %collective-permute-start.40) | collective-permute-done | bytes 262176 | tf_op jit(solution)/shard_map/ppermute | solution.py:40
  153.3 0.8 collective-permute-start.41
  154.1 3.9 %collective-permute-done.34.refs_12_ = bf16[2,2,128,256]{3,2,1,0:T(8,128)(2,1)S(1)} collective-permute-done((bf16[2,2,128,256]{3,2,1,0:T(8,128)(2,1)S(1)}, bf16[2,2,128,256]{3,2,1,0:T(8,128)(2,1)S(1)}, u32[]{:S(2)}, u32[]{:S(2)}) %collective-permute-start.34) | collective-permute-done | bytes 262176 | tf_op jit(solution)/shard_map/ppermute | solution.py:40
  158.0 4.9 %collective-permute-done.41.refs_20_ = bf16[2,2,128,256]{3,2,1,0:T(8,128)(2,1)S(1)} collective-permute-done((bf16[2,2,128,256]{3,2,1,0:T(8,128)(2,1)S(1)}, bf16[2,2,128,256]{3,2,1,0:T(8,128)(2,1)S(1)}, u32[]{:S(2)}, u32[]{:S(2)}) %collective-permute-start.41) | collective-permute-done | bytes 262176 | tf_op jit(solution)/shard_map/ppermute | solution.py:40
  162.8 1.5 shard_map.86
  164.4 1.5 collective-permute-done.42.theirs
  165.9 1.4 shard_map.87
  (48 shorter events, 2.0 us)
Async XLA Ops:
  0.6 59.4 %collective-permute-start.9 = (bf16[32,128,256]{2,1,0:T(8,128)(2,1)}, bf16[32,128,256]{2,1,0:T(8,128)(2,1)S(1)}, u32[]{:S(2)}, u32[]{:S(2)}) collective-permute-start(bf16[32,128,256]{2,1,0:T(8,128)(2,1)} %rot_mine.1), channel_id=1, source_target_pairs={{0,1},{1,0},{2,3},{3,2},{4,5},{5,4},{6,7},{7,6},{8,9},{9,8},{10,11... | collective-permute-start | bytes 6291464 | tf_op jit(solution)/shard_map/ppermute | solution.py:40
  1.1 9.8 %collective-permute-start.2 = (bf16[128,256]{1,0:T(8,128)(2,1)}, bf16[128,256]{1,0:T(8,128)(2,1)S(1)}, u32[]{:S(2)}, u32[]{:S(2)}) collective-permute-start(bf16[128,256]{1,0:T(8,128)(2,1)} %param.7), channel_id=1, source_target_pairs={{0,2},{1,3},{2,0},{3,1},{4,6},{5,7},{6,4},{7,5},{8,10},{9,11},{10,... | collective-permute-start | bytes 196616 | tf_op jit(solution)/shard_map/ppermute | solution.py:40
  3.7 1.0 copy-start.1
  4.8 0.7 copy-start.3
  7.4 11.5 %collective-permute-start = (bf16[4,128,256]{2,1,0:T(8,128)(2,1)S(1)}, bf16[4,128,256]{2,1,0:T(8,128)(2,1)S(1)}, u32[]{:S(2)}, u32[]{:S(2)}) collective-permute-start(bf16[4,128,256]{2,1,0:T(8,128)(2,1)S(1)} %get-tuple-element.53), channel_id=1, source_target_pairs={{0,0},{1,17},{2,2},{3,19},{4,4},{5,21},{6,6},{7,23},{8,8},{9,25},{... | collective-permute-start | bytes 786440 | tf_op jit(solution)/shard_map/ppermute | solution.py:462
  8.1 10.9 %collective-permute-start.1 = (bf16[4,128,256]{2,1,0:T(8,128)(2,1)S(1)}, bf16[4,128,256]{2,1,0:T(8,128)(2,1)S(1)}, u32[]{:S(2)}, u32[]{:S(2)}) collective-permute-start(bf16[4,128,256]{2,1,0:T(8,128)(2,1)S(1)} %get-tuple-element.54), channel_id=1, source_target_pairs={{0,17},{1,0},{2,19},{3,2},{4,21},{5,4},{6,23},{7,6},{8,25},{9,8},{... | collective-permute-start | bytes 786440 | tf_op jit(solution)/shard_map/ppermute | solution.py:462
  11.8 7.2 %collective-permute-start.3 = (bf16[2,128,256]{2,1,0:T(8,128)(2,1)S(1)}, bf16[2,128,256]{2,1,0:T(8,128)(2,1)S(1)}, u32[]{:S(2)}, u32[]{:S(2)}) collective-permute-start(bf16[2,128,256]{2,1,0:T(8,128)(2,1)S(1)} %pad_maximum_fusion.2), channel_id=1, source_target_pairs={{0,4},{1,5},{2,6},{3,7},{4,8},{5,9},{6,10},{7,11},{8,12},{9,13},{1... | collective-permute-start | bytes 393224 | tf_op jit(solution)/shard_map/ppermute | solution.py:40
  19.0 6.8 %collective-permute-start.4 = (bf16[2,128,256]{2,1,0:T(8,128)(2,1)S(1)}, bf16[2,128,256]{2,1,0:T(8,128)(2,1)S(1)}, u32[]{:S(2)}, u32[]{:S(2)}) collective-permute-start(bf16[2,128,256]{2,1,0:T(8,128)(2,1)S(1)} %collective-permute-done.3), channel_id=1, source_target_pairs={{0,4},{1,5},{2,6},{3,7},{4,8},{5,9},{6,10},{7,11},{8,12},{9,13},{1... | collective-permute-start | bytes 393224 | tf_op jit(solution)/shard_map/ppermute | solution.py:40
  25.8 11.1 %collective-permute-start.16 = (bf16[2,2,128,256]{3,2,1,0:T(8,128)(2,1)S(1)}, bf16[2,2,128,256]{3,2,1,0:T(8,128)(2,1)S(1)}, u32[]{:S(2)}, u32[]{:S(2)}) collective-permute-start(bf16[2,2,128,256]{3,2,1,0:T(8,128)(2,1)S(1)} %get-tuple-element.102.refs_0_.refs_1_.refs_12_), channel_id=1, source_target_pairs={{0,4},{1,5},{2,6},{3,7},{4,8},{5,9},{6,10},{7,11},{8,12},{9,13},{1... | collective-permute-start | bytes 786440 | tf_op jit(solution)/shard_map/ppermute | solution.py:40
  25.9 11.0 %collective-permute-start.15 = (bf16[2,2,128,256]{3,2,1,0:T(8,128)(2,1)S(1)}, bf16[2,2,128,256]{3,2,1,0:T(8,128)(2,1)S(1)}, u32[]{:S(2)}, u32[]{:S(2)}) collective-permute-start(bf16[2,2,128,256]{3,2,1,0:T(8,128)(2,1)S(1)} %get-tuple-element.102.refs_0_.refs_1_.refs_12_), channel_id=1, source_target_pairs={{0,2},{1,3},{2,0},{3,1},{4,6},{5,7},{6,4},{7,5},{8,10},{9,11},{10,... | collective-permute-start | bytes 786440 | tf_op jit(solution)/shard_map/ppermute | solution.py:40
  26.5 18.6 %collective-permute-start.7 = (bf16[2,2,128,256]{3,2,1,0:T(8,128)(2,1)S(1)}, bf16[2,2,128,256]{3,2,1,0:T(8,128)(2,1)S(1)}, u32[]{:S(2)}, u32[]{:S(2)}) collective-permute-start(bf16[2,2,128,256]{3,2,1,0:T(8,128)(2,1)S(1)} %get-tuple-element.103.refs_0_.refs_4_), channel_id=1, source_target_pairs={{0,4},{1,5},{2,6},{3,7},{4,8},{5,9},{6,10},{7,11},{8,12},{9,13},{1... | collective-permute-start | bytes 786440 | tf_op jit(solution)/shard_map/ppermute | solution.py:40
  26.5 18.6 %collective-permute-start.6 = (bf16[2,2,128,256]{3,2,1,0:T(8,128)(2,1)S(1)}, bf16[2,2,128,256]{3,2,1,0:T(8,128)(2,1)S(1)}, u32[]{:S(2)}, u32[]{:S(2)}) collective-permute-start(bf16[2,2,128,256]{3,2,1,0:T(8,128)(2,1)S(1)} %get-tuple-element.103.refs_0_.refs_4_), channel_id=1, source_target_pairs={{0,2},{1,3},{2,0},{3,1},{4,6},{5,7},{6,4},{7,5},{8,10},{9,11},{10,... | collective-permute-start | bytes 786440 | tf_op jit(solution)/shard_map/ppermute | solution.py:40
  36.9 8.1 %collective-permute-start.5 = (bf16[2,128,256]{2,1,0:T(8,128)(2,1)S(1)}, bf16[2,128,256]{2,1,0:T(8,128)(2,1)S(1)}, u32[]{:S(2)}, u32[]{:S(2)}) collective-permute-start(bf16[2,128,256]{2,1,0:T(8,128)(2,1)S(1)} %collective-permute-done.4), channel_id=1, source_target_pairs={{0,4},{1,5},{2,6},{3,7},{4,8},{5,9},{6,10},{7,11},{8,12},{9,13},{1... | collective-permute-start | bytes 393224 | tf_op jit(solution)/shard_map/ppermute | solution.py:40
  36.9 10.9 %collective-permute-start.18 = (bf16[2,2,128,256]{3,2,1,0:T(8,128)(2,1)S(1)}, bf16[2,2,128,256]{3,2,1,0:T(8,128)(2,1)S(1)}, u32[]{:S(2)}, u32[]{:S(2)}) collective-permute-start(bf16[2,2,128,256]{3,2,1,0:T(8,128)(2,1)S(1)} %collective-permute-done.16.refs_1_.refs_13_), channel_id=1, source_target_pairs={{0,4},{1,5},{2,6},{3,7},{4,8},{5,9},{6,10},{7,11},{8,12},{9,13},{1... | collective-permute-start | bytes 786440 | tf_op jit(solution)/shard_map/ppermute | solution.py:40
  45.2 14.9 %collective-permute-start.8 = (bf16[4,2,128,256]{3,2,1,0:T(8,128)(2,1)S(1)}, bf16[4,2,128,256]{3,2,1,0:T(8,128)(2,1)S(1)}, u32[]{:S(2)}, u32[]{:S(2)}) collective-permute-start(bf16[4,2,128,256]{3,2,1,0:T(8,128)(2,1)S(1)} %pad_maximum_fusion.mine), channel_id=1, source_target_pairs={{0,1},{1,0},{2,3},{3,2},{4,5},{5,4},{6,7},{7,6},{8,9},{9,8},{10,11... | collective-permute-start | bytes 1572872 | tf_op jit(solution)/shard_map/ppermute | solution.py:40
  45.2 9.2 %collective-permute-start.17 = (bf16[2,2,128,256]{3,2,1,0:T(8,128)(2,1)S(1)}, bf16[2,2,128,256]{3,2,1,0:T(8,128)(2,1)S(1)}, u32[]{:S(2)}, u32[]{:S(2)}) collective-permute-start(bf16[2,2,128,256]{3,2,1,0:T(8,128)(2,1)S(1)} %collective-permute-done.16.refs_1_.refs_13_), channel_id=1, source_target_pairs={{0,2},{1,3},{2,0},{3,1},{4,6},{5,7},{6,4},{7,5},{8,10},{9,11},{10,... | collective-permute-start | bytes 786440 | tf_op jit(solution)/shard_map/ppermute | solution.py:40
  46.1 10.2 %collective-permute-start.11 = (bf16[2,2,128,256]{3,2,1,0:T(8,128)(2,1)S(1)}, bf16[2,2,128,256]{3,2,1,0:T(8,128)(2,1)S(1)}, u32[]{:S(2)}, u32[]{:S(2)}) collective-permute-start(bf16[2,2,128,256]{3,2,1,0:T(8,128)(2,1)S(1)} %collective-permute-done.7.refs_1_.refs_5_), channel_id=1, source_target_pairs={{0,4},{1,5},{2,6},{3,7},{4,8},{5,9},{6,10},{7,11},{8,12},{9,13},{1... | collective-permute-start | bytes 786440 | tf_op jit(solution)/shard_map/ppermute | solution.py:40
  47.9 12.1 %collective-permute-start.10 = (bf16[2,2,128,256]{3,2,1,0:T(8,128)(2,1)S(1)}, bf16[2,2,128,256]{3,2,1,0:T(8,128)(2,1)S(1)}, u32[]{:S(2)}, u32[]{:S(2)}) collective-permute-start(bf16[2,2,128,256]{3,2,1,0:T(8,128)(2,1)S(1)} %collective-permute-done.7.refs_1_.refs_5_), channel_id=1, source_target_pairs={{0,2},{1,3},{2,0},{3,1},{4,6},{5,7},{6,4},{7,5},{8,10},{9,11},{10,... | collective-permute-start | bytes 786440 | tf_op jit(solution)/shard_map/ppermute | solution.py:40
  54.4 9.2 %collective-permute-start.20 = (bf16[2,2,128,256]{3,2,1,0:T(8,128)(2,1)S(1)}, bf16[2,2,128,256]{3,2,1,0:T(8,128)(2,1)S(1)}, u32[]{:S(2)}, u32[]{:S(2)}) collective-permute-start(bf16[2,2,128,256]{3,2,1,0:T(8,128)(2,1)S(1)} %collective-permute-done.18.refs_2_.refs_14_), channel_id=1, source_target_pairs={{0,4},{1,5},{2,6},{3,7},{4,8},{5,9},{6,10},{7,11},{8,12},{9,13},{1... | collective-permute-start | bytes 786440 | tf_op jit(solution)/shard_map/ppermute | solution.py:40
  56.2 9.4 %collective-permute-start.19 = (bf16[2,2,128,256]{3,2,1,0:T(8,128)(2,1)S(1)}, bf16[2,2,128,256]{3,2,1,0:T(8,128)(2,1)S(1)}, u32[]{:S(2)}, u32[]{:S(2)}) collective-permute-start(bf16[2,2,128,256]{3,2,1,0:T(8,128)(2,1)S(1)} %collective-permute-done.18.refs_2_.refs_14_), channel_id=1, source_target_pairs={{0,2},{1,3},{2,0},{3,1},{4,6},{5,7},{6,4},{7,5},{8,10},{9,11},{10,... | collective-permute-start | bytes 786440 | tf_op jit(solution)/shard_map/ppermute | solution.py:40
  60.0 9.2 %collective-permute-start.13 = (bf16[2,2,128,256]{3,2,1,0:T(8,128)(2,1)S(1)}, bf16[2,2,128,256]{3,2,1,0:T(8,128)(2,1)S(1)}, u32[]{:S(2)}, u32[]{:S(2)}) collective-permute-start(bf16[2,2,128,256]{3,2,1,0:T(8,128)(2,1)S(1)} %collective-permute-done.11.refs_2_.refs_6_), channel_id=1, source_target_pairs={{0,4},{1,5},{2,6},{3,7},{4,8},{5,9},{6,10},{7,11},{8,12},{9,13},{1... | collective-permute-start | bytes 786440 | tf_op jit(solution)/shard_map/ppermute | solution.py:40
  60.0 11.2 %collective-permute-start.12 = (bf16[2,2,128,256]{3,2,1,0:T(8,128)(2,1)S(1)}, bf16[2,2,128,256]{3,2,1,0:T(8,128)(2,1)S(1)}, u32[]{:S(2)}, u32[]{:S(2)}) collective-permute-start(bf16[2,2,128,256]{3,2,1,0:T(8,128)(2,1)S(1)} %collective-permute-done.11.refs_2_.refs_6_), channel_id=1, source_target_pairs={{0,2},{1,3},{2,0},{3,1},{4,6},{5,7},{6,4},{7,5},{8,10},{9,11},{10,... | collective-permute-start | bytes 786440 | tf_op jit(solution)/shard_map/ppermute | solution.py:40
  65.6 11.2 %collective-permute-start.21 = (bf16[2,2,128,256]{3,2,1,0:T(8,128)(2,1)S(1)}, bf16[2,2,128,256]{3,2,1,0:T(8,128)(2,1)S(1)}, u32[]{:S(2)}, u32[]{:S(2)}) collective-permute-start(bf16[2,2,128,256]{3,2,1,0:T(8,128)(2,1)S(1)} %collective-permute-done.20.refs_3_.refs_15_), channel_id=1, source_target_pairs={{0,2},{1,3},{2,0},{3,1},{4,6},{5,7},{6,4},{7,5},{8,10},{9,11},{10,... | collective-permute-start | bytes 786440 | tf_op jit(solution)/shard_map/ppermute | solution.py:40
  71.3 10.8 %collective-permute-start.14 = (bf16[2,2,128,256]{3,2,1,0:T(8,128)(2,1)S(1)}, bf16[2,2,128,256]{3,2,1,0:T(8,128)(2,1)S(1)}, u32[]{:S(2)}, u32[]{:S(2)}) collective-permute-start(bf16[2,2,128,256]{3,2,1,0:T(8,128)(2,1)S(1)} %collective-permute-done.13.refs_3_.refs_7_), channel_id=1, source_target_pairs={{0,2},{1,3},{2,0},{3,1},{4,6},{5,7},{6,4},{7,5},{8,10},{9,11},{10,... | collective-permute-start | bytes 786440 | tf_op jit(solution)/shard_map/ppermute | solution.py:40
  80.2 5.2 %copy-start = (bf16[32,128,256]{2,1,0:T(8,128)(2,1)S(1)}, bf16[32,128,256]{2,1,0:T(8,128)(2,1)}, u32[]{:S(2)}) copy-start(bf16[32,128,256]{2,1,0:T(8,128)(2,1)} %rot_mine.1) | copy-start | bytes 6291460
  85.4 14.6 %copy-start.2 = (f32[8,32]{1,0:T(8,128)S(1)}, f32[8,32]{1,0:T(8,128)}, u32[]{:S(2)}) copy-start(f32[8,32]{1,0:T(8,128)} %fields.1) | copy-start | bytes 3076
  87.1 4.5 %collective-permute-start.22 = (f32[4,32]{1,0:T(4,128)S(1)}, f32[4,32]{1,0:T(4,128)S(1)}, u32[]{:S(2)}, u32[]{:S(2)}) collective-permute-start(f32[4,32]{1,0:T(4,128)S(1)} %shard_map.81), channel_id=1, source_target_pairs={{0,8},{1,9},{2,10},{3,11},{4,12},{5,13},{6,14},{7,15},{8,0},{9,1},... | collective-permute-start | bytes 1544 | tf_op jit(solution)/shard_map/ppermute | solution.py:44
  91.6 3.6 %collective-permute-start.23 = (f32[4,32]{1,0:T(4,128)S(1)}, f32[4,32]{1,0:T(4,128)S(1)}, u32[]{:S(2)}, u32[]{:S(2)}) collective-permute-start(f32[4,32]{1,0:T(4,128)S(1)} %add.14), channel_id=1, source_target_pairs={{0,4},{1,5},{2,6},{3,7},{4,0},{5,1},{6,2},{7,3},{8,12},{9,13},{10,... | collective-permute-start | bytes 1544 | tf_op jit(solution)/shard_map/ppermute | solution.py:44
  95.2 3.6 %collective-permute-start.24 = (f32[4,32]{1,0:T(4,128)S(1)}, f32[4,32]{1,0:T(4,128)S(1)}, u32[]{:S(2)}, u32[]{:S(2)}) collective-permute-start(f32[4,32]{1,0:T(4,128)S(1)} %add.15), channel_id=1, source_target_pairs={{0,2},{1,3},{2,0},{3,1},{4,6},{5,7},{6,4},{7,5},{8,10},{9,11},{10,... | collective-permute-start | bytes 1544 | tf_op jit(solution)/shard_map/ppermute | solution.py:40
  98.8 1.2 collective-permute-start.25
  109.0 2.7 %collective-permute-start.27 = (bf16[4,64,2048]{2,1,0:T(8,128)(2,1)S(1)}, bf16[4,64,2048]{2,1,0:T(8,128)(2,1)S(1)}, u32[]{:S(2)}, u32[]{:S(2)}) collective-permute-start(bf16[4,64,2048]{2,1,0:T(8,128)(2,1)S(1)} %get-tuple-element.83), channel_id=1, source_target_pairs={{0,1},{1,0},{2,3},{3,2},{4,5},{5,4},{6,7},{7,6},{8,9},{9,8},{10,11... | collective-permute-start | bytes 3145736 | tf_op jit(solution)/shard_map/ppermute | solution.py:40
  109.3 4.0 %collective-permute-start.26 = (bf16[4,64,2048]{2,1,0:T(8,128)(2,1)S(1)}, bf16[4,64,2048]{2,1,0:T(8,128)(2,1)S(1)}, u32[]{:S(2)}, u32[]{:S(2)}) collective-permute-start(bf16[4,64,2048]{2,1,0:T(8,128)(2,1)S(1)} %get-tuple-element.82), channel_id=1, source_target_pairs={{0,1},{1,0},{2,3},{3,2},{4,5},{5,4},{6,7},{7,6},{8,9},{9,8},{10,11... | collective-permute-start | bytes 3145736 | tf_op jit(solution)/shard_map/ppermute | solution.py:40
  115.0 11.0 %collective-permute-start.29 = (bf16[2,2,128,256]{3,2,1,0:T(8,128)(2,1)S(1)}, bf16[2,2,128,256]{3,2,1,0:T(8,128)(2,1)S(1)}, u32[]{:S(2)}, u32[]{:S(2)}) collective-permute-start(bf16[2,2,128,256]{3,2,1,0:T(8,128)(2,1)S(1)} %get-tuple-element.85.refs_5_), channel_id=1, source_target_pairs={{0,4},{1,5},{2,6},{3,7},{4,8},{5,9},{6,10},{7,11},{8,12},{9,13},{1... | collective-permute-start | bytes 786440 | tf_op jit(solution)/shard_map/ppermute | solution.py:40
  115.0 10.9 %collective-permute-start.28 = (bf16[2,2,128,256]{3,2,1,0:T(8,128)(2,1)S(1)}, bf16[2,2,128,256]{3,2,1,0:T(8,128)(2,1)S(1)}, u32[]{:S(2)}, u32[]{:S(2)}) collective-permute-start(bf16[2,2,128,256]{3,2,1,0:T(8,128)(2,1)S(1)} %get-tuple-element.85.refs_5_), channel_id=1, source_target_pairs={{0,2},{1,3},{2,0},{3,1},{4,6},{5,7},{6,4},{7,5},{8,10},{9,11},{10,... | collective-permute-start | bytes 786440 | tf_op jit(solution)/shard_map/ppermute | solution.py:40
  115.9 15.7 %collective-permute-start.36 = (bf16[2,2,128,256]{3,2,1,0:T(8,128)(2,1)S(1)}, bf16[2,2,128,256]{3,2,1,0:T(8,128)(2,1)S(1)}, u32[]{:S(2)}, u32[]{:S(2)}) collective-permute-start(bf16[2,2,128,256]{3,2,1,0:T(8,128)(2,1)S(1)} %get-tuple-element.92.refs_13_), channel_id=1, source_target_pairs={{0,4},{1,5},{2,6},{3,7},{4,8},{5,9},{6,10},{7,11},{8,12},{9,13},{1... | collective-permute-start | bytes 786440 | tf_op jit(solution)/shard_map/ppermute | solution.py:40
  116.4 15.2 %collective-permute-start.35 = (bf16[2,2,128,256]{3,2,1,0:T(8,128)(2,1)S(1)}, bf16[2,2,128,256]{3,2,1,0:T(8,128)(2,1)S(1)}, u32[]{:S(2)}, u32[]{:S(2)}) collective-permute-start(bf16[2,2,128,256]{3,2,1,0:T(8,128)(2,1)S(1)} %get-tuple-element.92.refs_13_), channel_id=1, source_target_pairs={{0,2},{1,3},{2,0},{3,1},{4,6},{5,7},{6,4},{7,5},{8,10},{9,11},{10,... | collective-permute-start | bytes 786440 | tf_op jit(solution)/shard_map/ppermute | solution.py:40
  126.0 11.2 %collective-permute-start.31 = (bf16[2,2,128,256]{3,2,1,0:T(8,128)(2,1)S(1)}, bf16[2,2,128,256]{3,2,1,0:T(8,128)(2,1)S(1)}, u32[]{:S(2)}, u32[]{:S(2)}) collective-permute-start(bf16[2,2,128,256]{3,2,1,0:T(8,128)(2,1)S(1)} %collective-permute-done.29.refs_6_), channel_id=1, source_target_pairs={{0,4},{1,5},{2,6},{3,7},{4,8},{5,9},{6,10},{7,11},{8,12},{9,13},{1... | collective-permute-start | bytes 786440 | tf_op jit(solution)/shard_map/ppermute | solution.py:40
  126.0 11.2 %collective-permute-start.30 = (bf16[2,2,128,256]{3,2,1,0:T(8,128)(2,1)S(1)}, bf16[2,2,128,256]{3,2,1,0:T(8,128)(2,1)S(1)}, u32[]{:S(2)}, u32[]{:S(2)}) collective-permute-start(bf16[2,2,128,256]{3,2,1,0:T(8,128)(2,1)S(1)} %collective-permute-done.29.refs_6_), channel_id=1, source_target_pairs={{0,2},{1,3},{2,0},{3,1},{4,6},{5,7},{6,4},{7,5},{8,10},{9,11},{10,... | collective-permute-start | bytes 786440 | tf_op jit(solution)/shard_map/ppermute | solution.py:40
  131.6 11.2 %collective-permute-start.38 = (bf16[2,2,128,256]{3,2,1,0:T(8,128)(2,1)S(1)}, bf16[2,2,128,256]{3,2,1,0:T(8,128)(2,1)S(1)}, u32[]{:S(2)}, u32[]{:S(2)}) collective-permute-start(bf16[2,2,128,256]{3,2,1,0:T(8,128)(2,1)S(1)} %collective-permute-done.36.refs_14_), channel_id=1, source_target_pairs={{0,4},{1,5},{2,6},{3,7},{4,8},{5,9},{6,10},{7,11},{8,12},{9,13},{1... | collective-permute-start | bytes 786440 | tf_op jit(solution)/shard_map/ppermute | solution.py:40
  131.6 11.2 %collective-permute-start.37 = (bf16[2,2,128,256]{3,2,1,0:T(8,128)(2,1)S(1)}, bf16[2,2,128,256]{3,2,1,0:T(8,128)(2,1)S(1)}, u32[]{:S(2)}, u32[]{:S(2)}) collective-permute-start(bf16[2,2,128,256]{3,2,1,0:T(8,128)(2,1)S(1)} %collective-permute-done.36.refs_14_), channel_id=1, source_target_pairs={{0,2},{1,3},{2,0},{3,1},{4,6},{5,7},{6,4},{7,5},{8,10},{9,11},{10,... | collective-permute-start | bytes 786440 | tf_op jit(solution)/shard_map/ppermute | solution.py:40
  137.2 11.2 %collective-permute-start.33 = (bf16[2,2,128,256]{3,2,1,0:T(8,128)(2,1)S(1)}, bf16[2,2,128,256]{3,2,1,0:T(8,128)(2,1)S(1)}, u32[]{:S(2)}, u32[]{:S(2)}) collective-permute-start(bf16[2,2,128,256]{3,2,1,0:T(8,128)(2,1)S(1)} %collective-permute-done.31.refs_7_), channel_id=1, source_target_pairs={{0,4},{1,5},{2,6},{3,7},{4,8},{5,9},{6,10},{7,11},{8,12},{9,13},{1... | collective-permute-start | bytes 786440 | tf_op jit(solution)/shard_map/ppermute | solution.py:40
  137.2 11.2 %collective-permute-start.32 = (bf16[2,2,128,256]{3,2,1,0:T(8,128)(2,1)S(1)}, bf16[2,2,128,256]{3,2,1,0:T(8,128)(2,1)S(1)}, u32[]{:S(2)}, u32[]{:S(2)}) collective-permute-start(bf16[2,2,128,256]{3,2,1,0:T(8,128)(2,1)S(1)} %collective-permute-done.31.refs_7_), channel_id=1, source_target_pairs={{0,2},{1,3},{2,0},{3,1},{4,6},{5,7},{6,4},{7,5},{8,10},{9,11},{10,... | collective-permute-start | bytes 786440 | tf_op jit(solution)/shard_map/ppermute | solution.py:40
  142.8 10.5 %collective-permute-start.40 = (bf16[2,2,128,256]{3,2,1,0:T(8,128)(2,1)S(1)}, bf16[2,2,128,256]{3,2,1,0:T(8,128)(2,1)S(1)}, u32[]{:S(2)}, u32[]{:S(2)}) collective-permute-start(bf16[2,2,128,256]{3,2,1,0:T(8,128)(2,1)S(1)} %collective-permute-done.38.refs_15_), channel_id=1, source_target_pairs={{0,4},{1,5},{2,6},{3,7},{4,8},{5,9},{6,10},{7,11},{8,12},{9,13},{1... | collective-permute-start | bytes 786440 | tf_op jit(solution)/shard_map/ppermute | solution.py:40
  142.8 10.5 %collective-permute-start.39 = (bf16[2,2,128,256]{3,2,1,0:T(8,128)(2,1)S(1)}, bf16[2,2,128,256]{3,2,1,0:T(8,128)(2,1)S(1)}, u32[]{:S(2)}, u32[]{:S(2)}) collective-permute-start(bf16[2,2,128,256]{3,2,1,0:T(8,128)(2,1)S(1)} %collective-permute-done.38.refs_15_), channel_id=1, source_target_pairs={{0,2},{1,3},{2,0},{3,1},{4,6},{5,7},{6,4},{7,5},{8,10},{9,11},{10,... | collective-permute-start | bytes 786440 | tf_op jit(solution)/shard_map/ppermute | solution.py:40
  148.5 9.5 %collective-permute-start.34 = (bf16[2,2,128,256]{3,2,1,0:T(8,128)(2,1)S(1)}, bf16[2,2,128,256]{3,2,1,0:T(8,128)(2,1)S(1)}, u32[]{:S(2)}, u32[]{:S(2)}) collective-permute-start(bf16[2,2,128,256]{3,2,1,0:T(8,128)(2,1)S(1)} %collective-permute-done.33.refs_8_), channel_id=1, source_target_pairs={{0,2},{1,3},{2,0},{3,1},{4,6},{5,7},{6,4},{7,5},{8,10},{9,11},{10,... | collective-permute-start | bytes 786440 | tf_op jit(solution)/shard_map/ppermute | solution.py:40
  153.3 9.5 %collective-permute-start.41 = (bf16[2,2,128,256]{3,2,1,0:T(8,128)(2,1)S(1)}, bf16[2,2,128,256]{3,2,1,0:T(8,128)(2,1)S(1)}, u32[]{:S(2)}, u32[]{:S(2)}) collective-permute-start(bf16[2,2,128,256]{3,2,1,0:T(8,128)(2,1)S(1)} %collective-permute-done.40.refs_16_), channel_id=1, source_target_pairs={{0,2},{1,3},{2,0},{3,1},{4,6},{5,7},{6,4},{7,5},{8,10},{9,11},{10,... | collective-permute-start | bytes 786440 | tf_op jit(solution)/shard_map/ppermute | solution.py:40
  164.3 1.6 collective-permute-start.42

commit v5 on v4

--- a/solution.py
+++ b/solution.py
@@ -39,15 +39,10 @@
             pairs.append((index, target))
         return lax.ppermute(array, "chol", pairs)
 
-    def swap(self, array, distance):
-        pairs = [(i, (((i // 4) ^ distance) * 4) + i % 4) for i in range(self.chol)]
-        return lax.ppermute(array, "chol", pairs)
-
 
 class Stream:
-    def __init__(self, layout, piece, walker=0):
+    def __init__(self, layout, piece):
         self.layout = layout
-        self.walker = walker
         self.ring = [piece]
         self.across = []
 
@@ -66,8 +61,8 @@
         return anchors
 
     def pieces(self):
-        ring = [(array, self.walker, dz, 0) for dz, array in enumerate(self.ring)]
-        return ring + [(array, self.walker, dz, 1) for dz, array in enumerate(self.across)]
+        ring = [(array, dz, 0) for dz, array in enumerate(self.ring)]
+        return ring + [(array, dz, 1) for dz, array in enumerate(self.across)]
 
 
 def gathered(layout, dz, dy):
@@ -117,29 +112,30 @@
 
 
 def inverse_kernel(layout, places, trial, *refs):
-    pieces, (out, buffer) = refs[:-2], refs[-2:]
+    pieces, (full, out) = refs[:-2], refs[-2:]
     matrices = []
     for walker in range(out.shape[0]):
         for piece, (dz, dy) in zip(pieces, places):
-            buffer[walker, gathered(layout, dz, dy)] = piece[walker]
-        full = buffer[walker]
-        full = full.reshape(-1, full.shape[-1])
-        matrices.append(jnp.dot(trial[...], full, preferred_element_type=F32))
+            full[walker, gathered(layout, dz, dy)] = piece[walker]
+        rows = full[walker].reshape(-1, full.shape[-1])
+        matrices.append(jnp.dot(trial[...], rows, preferred_element_type=F32))
     for walker, inverse in enumerate(newton_inverses(matrices)):
         out[walker] = inverse.astype(out.dtype)
 
 
 def inverses_of(layout, trial, stream):
-    arrays = [piece[0] for piece in stream.pieces()]
-    places = [piece[2:] for piece in stream.pieces()]
+    arrays = [array for array, _, _ in stream.pieces()]
+    places = [place for _, *place in stream.pieces()]
     count, _, rows, electrons = arrays[0].shape
     return pl.pallas_call(
         functools.partial(inverse_kernel, layout, places),
-        out_shape=jax.ShapeDtypeStruct((count, electrons, electrons), BF16),
+        out_shape=[
+            jax.ShapeDtypeStruct((count, layout.chol // 2, 2, rows, electrons), BF16),
+            jax.ShapeDtypeStruct((count, electrons, electrons), BF16),
+        ],
         in_specs=vmem_specs(1 + len(arrays)),
-        out_specs=pl.BlockSpec(memory_space=pltpu.VMEM),
-        scratch_shapes=[pltpu.VMEM((count, layout.chol // 2, 2, rows, electrons), BF16)],
-        compiler_params=params(16),
+        out_specs=vmem_specs(2),
+        compiler_params=params(8),
     )(trial, *arrays)
 
 
@@ -199,14 +195,15 @@
     )(rot_mine, rot_theirs, *chunks, *inverses)
 
 
-def weights_kernel(order, fields, mine, theirs, bias_out, weights):
+def weights_kernel(order, fields, mine, mine_across, theirs, theirs_across, bias_out, weights):
     per_group, vectors = fields.shape
     half = mine.shape[0]
+    sums = (mine[...] + mine_across[...], theirs[...] + theirs_across[...])
     b = lax.rem(lax.axis_index("chol"), 2)
     row = lax.broadcasted_iota(jnp.int32, (per_group, vectors), 0)
     bias = jnp.zeros((per_group, vectors), F32)
     for walker in range(half):
-        for part, core in ((mine, b), (theirs, 1 - b)):
+        for part, core in zip(sums, (b, 1 - b)):
             slot = order[core * half + walker]
             bias += jnp.where(row == slot, part[walker : walker + 1, :], 0.0)
     bias = TAU_ROOT * bias
@@ -231,7 +228,7 @@
     weights[...] = jnp.where(same, spread, 0.0).astype(BF16)
 
 
-def weights_of(order, fields, mine, theirs):
+def weights_of(order, fields, parts):
     per_group, vectors = fields.shape
     return pl.pallas_call(
         weights_kernel,
@@ -239,10 +236,10 @@
             jax.ShapeDtypeStruct((per_group, vectors), F32),
             jax.ShapeDtypeStruct((per_group * BLOCK, vectors * BLOCK), BF16),
         ],
-        in_specs=[pl.BlockSpec(memory_space=pltpu.SMEM)] + vmem_specs(3),
+        in_specs=[pl.BlockSpec(memory_space=pltpu.SMEM)] + vmem_specs(5),
         out_specs=vmem_specs(2),
         compiler_params=params(8),
-    )(order, fields, mine, theirs)
+    )(order, fields, *parts)
 
 
 def potential_kernel(start, weights, cholesky, kept, sent, blocks, semaphores):
@@ -283,87 +280,78 @@
     )(weights, cholesky)
 
 
-def fold(layout, places, kept, theirs, pieces, buffer, walker):
-    for piece, (count, first, dz, dy) in zip(pieces, places):
-        if first <= walker < first + count:
-            buffer[walker, gathered(layout, dz, dy)] = piece[walker - first]
-    rows = jnp.concatenate([part[walker] for part in (*kept, *theirs)], axis=0)
-    full = buffer[walker]
-    return jnp.dot(rows, full.reshape(-1, full.shape[-1]), preferred_element_type=F32)
-
-
-def first_kernel(layout, places, parts, sizes, *refs):
-    kept, theirs, refs = refs[:parts], refs[parts : 2 * parts], refs[2 * parts :]
-    base, buffer = refs[-2:]
-    outs = refs[-2 - len(sizes) : -2]
-    pieces = refs[: -2 - len(sizes)]
-    b = lax.rem(lax.axis_index("chol"), 2)
-    own_chip = lax.axis_index("chol") // 2
-    number, walker = 0, 0
-    for number, size in enumerate(sizes):
-        for at in range(size):
-            term = fold(layout, places, kept, theirs, pieces, buffer, walker)
-            rows = term.shape[0] // 2
-            for block, value in ((b, term[:rows]), (1 - b, term[rows:])):
-                outs[number][at, block] = value.astype(BF16)
-                base[walker, block] = buffer[walker, own_chip, block].astype(F32) + value
-            walker += 1
+def first_kernel(sibling, parts, *refs):
+    potential, fulls, (rounded, base) = refs[:parts], refs[parts:-2], refs[-2:]
+    b = lax.rem(lax.axis_index("chol"), 2)
+    chip = lax.axis_index("chol") // 2
+    count = 0
+    for full in fulls:
+        for walker in range(full.shape[0]):
+            rows = jnp.concatenate([part[count] for part in potential], axis=0)
+            columns = full[walker].reshape(-1, full.shape[-1])
+            term = jnp.dot(rows, columns, preferred_element_type=F32)
+            rounded[count] = term.astype(BF16)
+            own = full[walker, chip, 1 - b if sibling else b]
+            base[count] = own.astype(F32) + term
+            count += 1
+
+
+def first_of(potential, fulls, sibling):
+    half, _, orbitals = potential[0].shape
+    rows, electrons = fulls[0].shape[-2:]
+    shape = (half, rows, electrons)
+    return pl.pallas_call(
+        functools.partial(first_kernel, sibling, len(potential)),
+        out_shape=[jax.ShapeDtypeStruct(shape, BF16), jax.ShapeDtypeStruct(shape, F32)],
+        in_specs=vmem_specs(len(potential) + len(fulls)),
+        out_specs=vmem_specs(2),
+        compiler_params=params(8),
+        cost_estimate=pl.CostEstimate(
+            flops=2 * half * rows * orbitals * electrons,
+            bytes_accessed=2 * half * orbitals * (rows + electrons),
+            transcendentals=0,
+        ),
+    )(*potential, *fulls)
 
 
 def second_kernel(layout, places, parts, *refs):
     kept, theirs, refs = refs[:parts], refs[parts : 2 * parts], refs[2 * parts :]
-    base, pieces, (mine, sent, buffer) = refs[0], refs[1:-3], refs[-3:]
-    b = lax.rem(lax.axis_index("chol"), 2)
-    for walker in range(base.shape[0]):
-        term = fold(layout, places, kept, theirs, pieces, buffer, walker)
-        rows = term.shape[0] // 2
-        mine[walker] = (base[walker, b] + 0.5 * term[:rows]).astype(BF16)
-        sent[walker] = (base[walker, 1 - b] + 0.5 * term[rows:]).astype(BF16)
-
-
-def operands_of(pieces):
-    arrays = [piece[0] for piece in pieces]
-    return arrays, [(piece[0].shape[0], *piece[1:]) for piece in pieces]
-
-
-def fold_cost(half, rows, orbitals, electrons):
-    return pl.CostEstimate(
-        flops=4 * half * rows * orbitals * electrons,
-        bytes_accessed=2 * half * orbitals * (2 * rows + electrons),
-        transcendentals=0,
-    )
-
-
-def first_of(layout, kept, theirs, pieces, sizes):
-    arrays, places = operands_of(pieces)
-    half, _, orbitals = kept[0].shape
-    _, rows, electrons = arrays[0].shape[-3:]
-    return pl.pallas_call(
-        functools.partial(first_kernel, layout, places, len(kept), sizes),
-        out_shape=[jax.ShapeDtypeStruct((size, 2, rows, electrons), BF16) for size in sizes]
-        + [jax.ShapeDtypeStruct((half, 2, rows, electrons), F32)],
-        in_specs=vmem_specs(2 * len(kept) + len(arrays)),
-        out_specs=vmem_specs(len(sizes) + 1),
-        scratch_shapes=[pltpu.VMEM((half, orbitals // (2 * rows), 2, rows, electrons), BF16)],
-        compiler_params=params(16),
-        cost_estimate=fold_cost(half, rows, orbitals, electrons),
-    )(*kept, *theirs, *arrays)
-
-
-def second_of(layout, kept, theirs, base, pieces):
-    arrays, places = operands_of(pieces)
-    half, _, orbitals = kept[0].shape
-    _, rows, electrons = arrays[0].shape[-3:]
+    bases, pieces, (mine, sent, buffer) = refs[:2], refs[2:-3], refs[-3:]
+    b = lax.rem(lax.axis_index("chol"), 2)
+    for walker in range(mine.shape[0]):
+        for piece, (sibling, dz, dy) in zip(pieces, places):
+            block = 1 - b if sibling else b
+            buffer[walker, gathered(layout, dz, dy), block] = piece[walker]
+        rows = jnp.concatenate([part[walker] for part in (*kept, *theirs)], axis=0)
+        columns = buffer[walker].reshape(-1, buffer.shape[-1])
+        term = jnp.dot(rows, columns, preferred_element_type=F32)
+        count = term.shape[0] // 2
+        mine[walker] = (bases[0][walker] + 0.5 * term[:count]).astype(BF16)
+        sent[walker] = (bases[1][walker] + 0.5 * term[count:]).astype(BF16)
+
+
+def second_of(layout, kept, theirs, bases, streams):
+    arrays, places = [], []
+    for sibling, stream in enumerate(streams):
+        for array, dz, dy in stream.pieces():
+            arrays.append(array)
+            places.append((sibling, dz, dy))
+    orbitals = kept[0].shape[2]
+    half, rows, electrons = arrays[0].shape
     out = jax.ShapeDtypeStruct((half, rows, electrons), BF16)
     return pl.pallas_call(
         functools.partial(second_kernel, layout, places, len(kept)),
         out_shape=[out, out],
-        in_specs=vmem_specs(2 * len(kept) + 1 + len(arrays)),
+        in_specs=vmem_specs(2 * len(kept) + 2 + len(arrays)),
         out_specs=vmem_specs(2),
-        scratch_shapes=[pltpu.VMEM((half, orbitals // (2 * rows), 2, rows, electrons), BF16)],
+        scratch_shapes=[pltpu.VMEM((half, layout.chol // 2, 2, rows, electrons), BF16)],
         compiler_params=params(16),
-        cost_estimate=fold_cost(half, rows, orbitals, electrons),
-    )(*kept, *theirs, base, *arrays)
+        cost_estimate=pl.CostEstimate(
+            flops=4 * half * rows * orbitals * electrons,
+            bytes_accessed=2 * half * orbitals * (2 * rows + electrons),
+            transcendentals=0,
+        ),
+    )(*kept, *theirs, *bases, *arrays)
 
 
 def place_kernel(order, mine, theirs, out):
@@ -443,12 +431,13 @@
     return jnp.sum(jnp.where(before & flags[..., None, :], 1, 0), axis=-1)
 
 
-def migrate(layout, walkers, source):
+def migrate(layout, walkers, source, trial):
     per_group = walkers.shape[0]
     half = per_group // 2
     group = lax.axis_index("walk")
     if layout.walk == 2:
         first, second, order = split_walkers(walkers, source)
+        first, second, trial = lax.optimization_barrier((first, second, trial))
         near, cross = [], []
         for index in range(2 * layout.chol):
             across = (index + layout.chol) % (2 * layout.chol)
@@ -459,7 +448,7 @@
                 near.append((index, across))
                 cross.append((index, index - 1))
         axes = ("walk", "chol")
-        return lax.ppermute(first, axes, near), lax.ppermute(second, axes, cross), order
+        return lax.ppermute(first, axes, near), lax.ppermute(second, axes, cross), order, trial
     table = source.reshape(layout.walk, per_group)
     incoming = lax.dynamic_index_in_dim(table, group, 0, keepdims=False)
     incoming_groups = incoming // per_group
@@ -483,7 +472,7 @@
     b = lax.axis_index("chol") % 2
     mine = lax.dynamic_slice_in_dim(migrated, b * half, half, 0)
     theirs = lax.dynamic_slice_in_dim(migrated, (1 - b) * half, half, 0)
-    return mine, layout.shift(theirs, db=1), slots.astype(jnp.int32)
+    return mine, layout.shift(theirs, db=1), slots.astype(jnp.int32), trial
 
 
 def shards(layout, walkers, trial, cholesky, rotated, fields, source):
@@ -491,26 +480,25 @@
     sizes = (half // 2, half - half // 2)
     b = lax.axis_index("chol") % 2
 
+    own, other, order, trial = migrate(layout, walkers, source, trial)
     pairs = [jnp.stack([trial, layout.shift(trial, dy=1)])]
-    own, other, order = migrate(layout, walkers, source)
-    for _ in range(layout.z // 2):
-        pairs.append(layout.shift(pairs[-1], dz=1))
+    pairs.append(layout.shift(pairs[0], dz=1))
     own, other, pairs = lax.optimization_barrier((own, other, pairs))
-    for _ in range(layout.z - len(pairs)):
+    while len(pairs) < layout.z:
         pairs.append(layout.shift(pairs[-1], dz=1))
     chunk = jnp.stack([jnp.where(b == 0, own, other), jnp.where(b == 0, other, own)], axis=1)
     chunks = [chunk[: sizes[0]], chunk[sizes[0] :]]
-    streams = [Stream(layout, chunks[0]), Stream(layout, chunks[1], sizes[0])]
+    streams = [Stream(layout, chunk) for chunk in chunks]
     for stage in range(layout.z):
         if stage == 0:
-            pairs = streams[0].advance(pairs)
-            streams[1].advance()
+            pairs[:3] = streams[0].advance(pairs[:3])
+            pairs[3:] = streams[1].advance(pairs[3:])
             planes = jnp.stack(pairs)
             planes_theirs = layout.shift(planes, db=1)
             rot_theirs = layout.shift(rotated, db=1)
         elif stage == 1:
-            planes_theirs, rot_theirs = streams[0].advance((planes_theirs, rot_theirs))
-            streams[1].advance()
+            streams[0].advance()
+            planes_theirs, rot_theirs = streams[1].advance((planes_theirs, rot_theirs))
             turned = transposed(layout, planes, planes_theirs)
         elif stage == 2:
             (turned,) = streams[0].advance((turned,))
@@ -519,28 +507,27 @@
             for stream in streams:
                 stream.advance()
 
-    inverses = [inverses_of(layout, turned, stream) for stream in streams]
+    fulls, inverses = zip(*[inverses_of(layout, turned, stream) for stream in streams])
     total = bias_of(chunks, inverses, rotated, rot_theirs)
-    distance = layout.z // 2
-    while distance:
-        total = total + layout.swap(total, distance)
-        distance //= 2
-    total = total + layout.shift(total, dy=1)
-    force_bias, weights = weights_of(order, fields, total, layout.shift(total, db=1))
+    parts = [total] + [layout.shift(total, dz=dz) for dz in range(1, layout.z)]
+    while len(parts) > 1:
+        far = len(parts) // 2
+        parts = [parts[at] + parts[at + far] for at in range(far)]
+    parts = [parts[0]] + [layout.shift(parts[0], dy=dy, db=db) for dy, db in ((1, 0), (0, 1), (1, 1))]
+    force_bias, weights = weights_of(order, fields, parts)
     kept, received = [], []
     for part in range(2):
         mine, sent = potential_of(weights, cholesky, part, 2)
         kept.append(mine)
         received.append(layout.shift(sent, db=1))
 
-    pieces = [piece for stream in streams for piece in stream.pieces()]
-    *firsts, base = first_of(layout, kept, received, pieces, sizes)
-    streams = [Stream(layout, firsts[0]), Stream(layout, firsts[1], sizes[0])]
+    rounded, base = first_of(kept, fulls, 0)
+    rounded_theirs, base_theirs = first_of(received, fulls, 1)
+    streams = [Stream(layout, rounded), Stream(layout, rounded_theirs)]
     for _ in range(layout.z):
         for stream in streams:
             stream.advance()
-    pieces = [piece for stream in streams for piece in stream.pieces()]
-    mine, sent = second_of(layout, kept, received, base, pieces)
+    mine, sent = second_of(layout, kept, received, (base, base_theirs), streams)
     return place(order, mine, layout.shift(sent, db=1)), force_bias
 
 

time: 168 us -> 159 us (0.946)
  waiting for transfers between devices: 114 us -> 97.5 us
  starting transfers between devices: 24.9 us -> 33.9 us
    ppermute x39 -> x43, starting transfers between devices: 21.4 us -> 30.4 us  [shift(): return lax.ppermute(array, 'chol', pairs)]
    ppermute x39 -> x43, waiting for transfers between devices: 106 us -> 97.4 us  [shift(): return lax.ppermute(array, 'chol', pairs)]
    ppermute x2 -> x0, waiting for transfers between devices: 8.09 us -> none  [swap(): return lax.ppermute(array, 'chol', pairs)]
  transfers between devices with their start and end apart: 43 -> 45, of which waited for: 29 -> 36; matrix products, arithmetic and copies ran while one was open for 1% -> 1% of each run, Pallas kernels for 3% -> 4%
where the time goes in v5:
time: 159 us
  waiting for transfers between devices  97.5 us (61%)
  starting transfers between devices  33.9 us (21%)
  Pallas kernels  24.1 us (15%)
  local copies, waits for them, and re-layouts  1.71 us (1%)
    ppermute x43, waiting for transfers between devices, shift(): return lax.ppermute(array, 'chol', pairs)  97.4 us
    ppermute x43, starting transfers between devices, shift(): return lax.ppermute(array, 'chol', pairs)  30.4 us
    pallas_call x2, Pallas kernels, potential_of(): pl.pallas_call(functools.partial(potential_kernel, part * rows), out_shap...  7.92 us
    pallas_call x2, Pallas kernels, inverses_of(): pl.pallas_call(functools.partial(inverse_kernel, layout, places), out_sha...  6.58 us
  transfers between devices with their start and end apart: 45, of which 36 were waited for; matrix products, arithmetic and copies ran while one was open for 1% of the time, Pallas kernels for 4%

profile of v5, /device:TPU:0, one launch (start us, length us, event | category | flops | bytes accessed | tf_op | source)
XLA Modules:
  0.0 159.0 jit_solution(2510047512422901355)
XLA Ops:
  1.1 1.0 copy-done.1
  2.8 2.0 %shard_map.77 = (bf16[4,128,256]{2,1,0:T(8,128)(2,1)S(1)}, bf16[4,128,256]{2,1,0:T(8,128)(2,1)S(1)}, s32[8]{0:T(128)S(1)}) custom-call(s32[16]{0:T(128)S(1)} %copy-done.3, bf16[8,128,256]{2,1,0:T(8,128)(2,1)S(1)} %copy-done.1), custom_call_target="tpu_custom_call" | custom-call | tf_op jit(solution)/shard_map/pallas_call | solution.py:414
  4.8 2.6 %collective-permute-start.2 = (bf16[128,256]{1,0:T(8,128)(2,1)}, bf16[128,256]{1,0:T(8,128)(2,1)S(1)}, u32[]{:S(2)}, u32[]{:S(2)}) collective-permute-start(bf16[128,256]{1,0:T(8,128)(2,1)} %param.7), channel_id=1, source_target_pairs={{0,2},{1,3},{2,0},{3,1},{4,6},{5,7},{6,4},{7,5},{8,10},{9,11},{10,... | collective-permute-start | bytes 196616 | tf_op jit(solution)/shard_map/ppermute | solution.py:40
  8.1 2.8 %collective-permute-start.1 = (bf16[4,128,256]{2,1,0:T(8,128)(2,1)S(1)}, bf16[4,128,256]{2,1,0:T(8,128)(2,1)S(1)}, u32[]{:S(2)}, u32[]{:S(2)}) collective-permute-start(bf16[4,128,256]{2,1,0:T(8,128)(2,1)S(1)} %get-tuple-element.63), channel_id=1, source_target_pairs={{0,17},{1,0},{2,19},{3,2},{4,21},{5,4},{6,23},{7,6},{8,25},{9,8},{... | collective-permute-start | bytes 786440 | tf_op jit(solution)/shard_map/ppermute | solution.py:451
  11.0 0.9 pad_maximum_fusion.2
  11.8 1.6 %collective-permute-start.3 = (bf16[2,128,256]{2,1,0:T(8,128)(2,1)S(1)}, bf16[2,128,256]{2,1,0:T(8,128)(2,1)S(1)}, u32[]{:S(2)}, u32[]{:S(2)}) collective-permute-start(bf16[2,128,256]{2,1,0:T(8,128)(2,1)S(1)} %pad_maximum_fusion.2), channel_id=1, source_target_pairs={{0,4},{1,5},{2,6},{3,7},{4,8},{5,9},{6,10},{7,11},{8,12},{9,13},{1... | collective-permute-start | bytes 393224 | tf_op jit(solution)/shard_map/ppermute | solution.py:40
  13.4 5.6 %collective-permute-done.3 = bf16[2,128,256]{2,1,0:T(8,128)(2,1)S(1)} collective-permute-done((bf16[2,128,256]{2,1,0:T(8,128)(2,1)S(1)}, bf16[2,128,256]{2,1,0:T(8,128)(2,1)S(1)}, u32[]{:S(2)}, u32[]{:S(2)}) %collective-permute-start.3) | collective-permute-done | bytes 131104 | tf_op jit(solution)/shard_map/ppermute | solution.py:40
  19.0 6.7 %collective-permute-done.4 = bf16[2,128,256]{2,1,0:T(8,128)(2,1)S(1)} collective-permute-done((bf16[2,128,256]{2,1,0:T(8,128)(2,1)S(1)}, bf16[2,128,256]{2,1,0:T(8,128)(2,1)S(1)}, u32[]{:S(2)}, u32[]{:S(2)}) %collective-permute-start.4) | collective-permute-done | bytes 131104 | tf_op jit(solution)/shard_map/ppermute | solution.py:40
  25.9 1.1 collective-permute-start.8
  27.0 1.3 collective-permute-start.5
  28.3 5.4 %collective-permute-done.7 = bf16[2,128,256]{2,1,0:T(8,128)(2,1)S(1)} collective-permute-done((bf16[2,128,256]{2,1,0:T(8,128)(2,1)S(1)}, bf16[2,128,256]{2,1,0:T(8,128)(2,1)S(1)}, u32[]{:S(2)}, u32[]{:S(2)}) %collective-permute-start.7) | collective-permute-done | bytes 131104 | tf_op jit(solution)/shard_map/ppermute | solution.py:40
  33.7 1.2 collective-permute-done.8.refs_4_
  34.9 4.4 %collective-permute-done.9.refs_1_ = bf16[2,2,128,256]{3,2,1,0:T(8,128)(2,1)S(1)} collective-permute-done((bf16[2,2,128,256]{3,2,1,0:T(8,128)(2,1)S(1)}, bf16[2,2,128,256]{3,2,1,0:T(8,128)(2,1)S(1)}, u32[]{:S(2)}, u32[]{:S(2)}) %collective-permute-start.9) | collective-permute-done | bytes 262176 | tf_op jit(solution)/shard_map/ppermute | solution.py:40
  39.3 2.9 %collective-permute-done.6.refs_1_ = bf16[2,2,128,256]{3,2,1,0:T(8,128)(2,1)S(1)} collective-permute-done((bf16[2,2,128,256]{3,2,1,0:T(8,128)(2,1)S(1)}, bf16[2,2,128,256]{3,2,1,0:T(8,128)(2,1)S(1)}, u32[]{:S(2)}, u32[]{:S(2)}) %collective-permute-start.6) | collective-permute-done | bytes 262176 | tf_op jit(solution)/shard_map/ppermute | solution.py:40
  43.2 1.3 collective-permute-start.12
  44.5 6.4 %collective-permute-done.14.refs_5_ = bf16[2,2,128,256]{3,2,1,0:T(8,128)(2,1)S(1)} collective-permute-done((bf16[2,2,128,256]{3,2,1,0:T(8,128)(2,1)S(1)}, bf16[2,2,128,256]{3,2,1,0:T(8,128)(2,1)S(1)}, u32[]{:S(2)}, u32[]{:S(2)}) %collective-permute-start.14) | collective-permute-done | bytes 262176 | tf_op jit(solution)/shard_map/ppermute | solution.py:40
  50.9 3.2 %collective-permute-done.15.refs_2_ = bf16[2,2,128,256]{3,2,1,0:T(8,128)(2,1)S(1)} collective-permute-done((bf16[2,2,128,256]{3,2,1,0:T(8,128)(2,1)S(1)}, bf16[2,2,128,256]{3,2,1,0:T(8,128)(2,1)S(1)}, u32[]{:S(2)}, u32[]{:S(2)}) %collective-permute-start.15) | collective-permute-done | bytes 262176 | tf_op jit(solution)/shard_map/ppermute | solution.py:40
  54.1 1.2 collective-permute-start.16
  55.3 4.5 %collective-permute-done.13.refs_2_ = bf16[2,2,128,256]{3,2,1,0:T(8,128)(2,1)S(1)} collective-permute-done((bf16[2,2,128,256]{3,2,1,0:T(8,128)(2,1)S(1)}, bf16[2,2,128,256]{3,2,1,0:T(8,128)(2,1)S(1)}, u32[]{:S(2)}, u32[]{:S(2)}) %collective-permute-start.13) | collective-permute-done | bytes 262176 | tf_op jit(solution)/shard_map/ppermute | solution.py:40
  59.8 1.6 %collective-permute-start.19 = (bf16[2,2,128,256]{3,2,1,0:T(8,128)(2,1)S(1)}, bf16[2,2,128,256]{3,2,1,0:T(8,128)(2,1)S(1)}, u32[]{:S(2)}, u32[]{:S(2)}) collective-permute-start(bf16[2,2,128,256]{3,2,1,0:T(8,128)(2,1)S(1)} %collective-permute-done.13.refs_2_), channel_id=1, source_target_pairs={{0,2},{1,3},{2,0},{3,1},{4,6},{5,7},{6,4},{7,5},{8,10},{9,11},{10,... | collective-permute-start | bytes 786440 | tf_op jit(solution)/shard_map/ppermute | solution.py:40
  61.9 1.5 collective-permute-done.16.refs_6_
  63.3 3.0 %collective-permute-done.17.refs_3_ = bf16[2,2,128,256]{3,2,1,0:T(8,128)(2,1)S(1)} collective-permute-done((bf16[2,2,128,256]{3,2,1,0:T(8,128)(2,1)S(1)}, bf16[2,2,128,256]{3,2,1,0:T(8,128)(2,1)S(1)}, u32[]{:S(2)}, u32[]{:S(2)}) %collective-permute-start.17) | collective-permute-done | bytes 262176 | tf_op jit(solution)/shard_map/ppermute | solution.py:40
  67.2 0.9 collective-permute-done.19.refs_6_
  68.1 2.4 %collective-permute-done.20.refs_3_ = bf16[2,2,128,256]{3,2,1,0:T(8,128)(2,1)S(1)} collective-permute-done((bf16[2,2,128,256]{3,2,1,0:T(8,128)(2,1)S(1)}, bf16[2,2,128,256]{3,2,1,0:T(8,128)(2,1)S(1)}, u32[]{:S(2)}, u32[]{:S(2)}) %collective-permute-start.20) | collective-permute-done | bytes 262176 | tf_op jit(solution)/shard_map/ppermute | solution.py:40
  70.5 1.2 collective-permute-start.21
  71.7 2.3 %collective-permute-done.18.refs_7_ = bf16[2,2,128,256]{3,2,1,0:T(8,128)(2,1)S(1)} collective-permute-done((bf16[2,2,128,256]{3,2,1,0:T(8,128)(2,1)S(1)}, bf16[2,2,128,256]{3,2,1,0:T(8,128)(2,1)S(1)}, u32[]{:S(2)}, u32[]{:S(2)}) %collective-permute-start.18) | collective-permute-done | bytes 262176 | tf_op jit(solution)/shard_map/ppermute | solution.py:40
  74.0 3.3 %shard_map.79 = (bf16[2,8,2,128,256]{4,3,2,1,0:T(8,128)(2,1)S(1)}, bf16[2,256,256]{2,1,0:T(8,128)(2,1)S(1)}) custom-call(bf16[256,2048]{1,0:T(8,128)(2,1)S(1)} %shard_map.78.trial, bf16[2,2,128,256]{3,2,1,0:T(8,128)(2,1)S(1)} %get-tuple-element.116.refs_0_, bf16[2,2,128,256]{3,2,1,0:T(8,128)(2,1)S(1)} %collective-permute-done.6.refs_1_, ...), custom_call_target="tpu_custom_call" | custom-call | tf_op jit(solution)/shard_map/pallas_call | solution.py:130
  77.3 1.1 collective-permute-done.21.refs_7_
  78.4 3.3 %shard_map.80 = (bf16[2,8,2,128,256]{4,3,2,1,0:T(8,128)(2,1)S(1)}, bf16[2,256,256]{2,1,0:T(8,128)(2,1)S(1)}) custom-call(bf16[256,2048]{1,0:T(8,128)(2,1)S(1)} %shard_map.78.trial, bf16[2,2,128,256]{3,2,1,0:T(8,128)(2,1)S(1)} %get-tuple-element.117.refs_0_.refs_1_, bf16[2,2,128,256]{3,2,1,0:T(8,128)(2,1)S(1)} %collective-permute-done.9.refs_1_, ...), custom_call_target="tpu_custom_call" | custom-call | tf_op jit(solution)/shard_map/pallas_call | solution.py:130
  81.7 1.7 %shard_map.81 = f32[4,32]{1,0:T(4,128)S(1)} custom-call(bf16[32,128,256]{2,1,0:T(8,128)(2,1)S(1)} %copy-done, bf16[32,128,256]{2,1,0:T(8,128)(2,1)S(1)} %collective-permute-done.11.rot_theirs, bf16[2,2,128,256]{3,2,1,0:T(8,128)(2,1)S(1)} %get-tuple-element.116.refs_0_, bf16[2,2,128,256]{3,2,1,0:T(8,128)(2,1)S(1)} %get-tuple-element.117.refs_0_.refs_1_, ...), custom_call_target="tpu_custom_call" | custom-call | flops 402653184 | bytes 4718592 | tf_op jit(solution)/shard_map/pallas_call | solution.py:183
  83.4 3.9 %collective-permute-start.24 = (f32[4,32]{1,0:T(4,128)S(1)}, f32[4,32]{1,0:T(4,128)S(1)}, u32[]{:S(2)}, u32[]{:S(2)}) collective-permute-start(f32[4,32]{1,0:T(4,128)S(1)} %shard_map.81), channel_id=1, source_target_pairs={{0,12},{1,13},{2,14},{3,15},{4,0},{5,1},{6,2},{7,3},{8,4},{9,5},{1... | collective-permute-start | bytes 1544 | tf_op jit(solution)/shard_map/ppermute | solution.py:40
  87.3 1.6 collective-permute-done.23
  88.8 2.9 %collective-permute-done.22 = f32[4,32]{1,0:T(4,128)S(1)} collective-permute-done((f32[4,32]{1,0:T(4,128)S(1)}, f32[4,32]{1,0:T(4,128)S(1)}, u32[]{:S(2)}, u32[]{:S(2)}) %collective-permute-start.22) | collective-permute-done | bytes 544 | tf_op jit(solution)/shard_map/ppermute | solution.py:40
  91.7 1.2 collective-permute-start.25
  93.0 0.9 collective-permute-start.27
  93.9 1.4 collective-permute-done.25.mine_across
  96.0 1.2 shard_map.82
  97.1 4.0 %shard_map.83 = (bf16[4,64,2048]{2,1,0:T(8,128)(2,1)S(1)}, bf16[4,64,2048]{2,1,0:T(8,128)(2,1)S(1)}) custom-call(bf16[128,512]{1,0:T(8,128)(2,1)S(1)} %get-tuple-element.90.weights, bf16[32,128,2048]{2,1,0:T(8,128)(2,1)} %cholesky.3), custom_call_target="tpu_custom_call" | custom-call | tf_op jit(solution)/shard_map/pallas_call | solution.py:270
  101.1 4.0 %shard_map.84 = (bf16[4,64,2048]{2,1,0:T(8,128)(2,1)S(1)}, bf16[4,64,2048]{2,1,0:T(8,128)(2,1)S(1)}) custom-call(bf16[128,512]{1,0:T(8,128)(2,1)S(1)} %get-tuple-element.90.weights, bf16[32,128,2048]{2,1,0:T(8,128)(2,1)} %cholesky.3), custom_call_target="tpu_custom_call" | custom-call | tf_op jit(solution)/shard_map/pallas_call | solution.py:270
  106.4 0.9 collective-permute-start.30
  107.9 1.5 collective-permute-done.29.refs_1_.refs_3_
  110.2 0.9 collective-permute-start.37
  111.0 4.6 %collective-permute-done.30.refs_10_ = bf16[4,128,256]{2,1,0:T(8,128)(2,1)S(1)} collective-permute-done((bf16[4,128,256]{2,1,0:T(8,128)(2,1)S(1)}, bf16[4,128,256]{2,1,0:T(8,128)(2,1)S(1)}, u32[]{:S(2)}, u32[]{:S(2)}) %collective-permute-start.30) | collective-permute-done | bytes 262176 | tf_op jit(solution)/shard_map/ppermute | solution.py:40
  115.6 2.7 %collective-permute-done.31.refs_7_ = bf16[4,128,256]{2,1,0:T(8,128)(2,1)S(1)} collective-permute-done((bf16[4,128,256]{2,1,0:T(8,128)(2,1)S(1)}, bf16[4,128,256]{2,1,0:T(8,128)(2,1)S(1)}, u32[]{:S(2)}, u32[]{:S(2)}) %collective-permute-start.31) | collective-permute-done | bytes 262176 | tf_op jit(solution)/shard_map/ppermute | solution.py:40
  118.3 1.2 collective-permute-start.32
  119.5 1.7 %collective-permute-done.37.refs_18_ = bf16[4,128,256]{2,1,0:T(8,128)(2,1)S(1)} collective-permute-done((bf16[4,128,256]{2,1,0:T(8,128)(2,1)S(1)}, bf16[4,128,256]{2,1,0:T(8,128)(2,1)S(1)}, u32[]{:S(2)}, u32[]{:S(2)}) %collective-permute-start.37) | collective-permute-done | bytes 262176 | tf_op jit(solution)/shard_map/ppermute | solution.py:40
  121.2 2.7 %collective-permute-done.38.refs_15_ = bf16[4,128,256]{2,1,0:T(8,128)(2,1)S(1)} collective-permute-done((bf16[4,128,256]{2,1,0:T(8,128)(2,1)S(1)}, bf16[4,128,256]{2,1,0:T(8,128)(2,1)S(1)}, u32[]{:S(2)}, u32[]{:S(2)}) %collective-permute-start.38) | collective-permute-done | bytes 262176 | tf_op jit(solution)/shard_map/ppermute | solution.py:40
  123.9 1.2 collective-permute-start.39
  125.1 2.4 %collective-permute-done.32.refs_11_ = bf16[4,128,256]{2,1,0:T(8,128)(2,1)S(1)} collective-permute-done((bf16[4,128,256]{2,1,0:T(8,128)(2,1)S(1)}, bf16[4,128,256]{2,1,0:T(8,128)(2,1)S(1)}, u32[]{:S(2)}, u32[]{:S(2)}) %collective-permute-start.32) | collective-permute-done | bytes 262176 | tf_op jit(solution)/shard_map/ppermute | solution.py:40
  127.5 2.1 %collective-permute-done.33.refs_8_ = bf16[4,128,256]{2,1,0:T(8,128)(2,1)S(1)} collective-permute-done((bf16[4,128,256]{2,1,0:T(8,128)(2,1)S(1)}, bf16[4,128,256]{2,1,0:T(8,128)(2,1)S(1)}, u32[]{:S(2)}, u32[]{:S(2)}) %collective-permute-start.33) | collective-permute-done | bytes 262176 | tf_op jit(solution)/shard_map/ppermute | solution.py:40
  129.6 1.6 %collective-permute-start.34 = (bf16[4,128,256]{2,1,0:T(8,128)(2,1)S(1)}, bf16[4,128,256]{2,1,0:T(8,128)(2,1)S(1)}, u32[]{:S(2)}, u32[]{:S(2)}) collective-permute-start(bf16[4,128,256]{2,1,0:T(8,128)(2,1)S(1)} %collective-permute-done.33.refs_8_), channel_id=1, source_target_pairs={{0,2},{1,3},{2,0},{3,1},{4,6},{5,7},{6,4},{7,5},{8,10},{9,11},{10,... | collective-permute-start | bytes 786440 | tf_op jit(solution)/shard_map/ppermute | solution.py:40
  131.2 1.9 %collective-permute-done.39.refs_19_ = bf16[4,128,256]{2,1,0:T(8,128)(2,1)S(1)} collective-permute-done((bf16[4,128,256]{2,1,0:T(8,128)(2,1)S(1)}, bf16[4,128,256]{2,1,0:T(8,128)(2,1)S(1)}, u32[]{:S(2)}, u32[]{:S(2)}) %collective-permute-start.39) | collective-permute-done | bytes 262176 | tf_op jit(solution)/shard_map/ppermute | solution.py:40
  133.1 2.7 %collective-permute-done.40.refs_16_ = bf16[4,128,256]{2,1,0:T(8,128)(2,1)S(1)} collective-permute-done((bf16[4,128,256]{2,1,0:T(8,128)(2,1)S(1)}, bf16[4,128,256]{2,1,0:T(8,128)(2,1)S(1)}, u32[]{:S(2)}, u32[]{:S(2)}) %collective-permute-start.40) | collective-permute-done | bytes 262176 | tf_op jit(solution)/shard_map/ppermute | solution.py:40
  135.9 1.1 collective-permute-start.41
  137.0 1.9 %collective-permute-done.34.refs_12_ = bf16[4,128,256]{2,1,0:T(8,128)(2,1)S(1)} collective-permute-done((bf16[4,128,256]{2,1,0:T(8,128)(2,1)S(1)}, bf16[4,128,256]{2,1,0:T(8,128)(2,1)S(1)}, u32[]{:S(2)}, u32[]{:S(2)}) %collective-permute-start.34) | collective-permute-done | bytes 262176 | tf_op jit(solution)/shard_map/ppermute | solution.py:40
  138.9 2.6 %collective-permute-done.35.refs_9_ = bf16[4,128,256]{2,1,0:T(8,128)(2,1)S(1)} collective-permute-done((bf16[4,128,256]{2,1,0:T(8,128)(2,1)S(1)}, bf16[4,128,256]{2,1,0:T(8,128)(2,1)S(1)}, u32[]{:S(2)}, u32[]{:S(2)}) %collective-permute-start.35) | collective-permute-done | bytes 262176 | tf_op jit(solution)/shard_map/ppermute | solution.py:40
  141.5 1.2 collective-permute-start.36
  142.7 2.4 %collective-permute-done.41.refs_20_ = bf16[4,128,256]{2,1,0:T(8,128)(2,1)S(1)} collective-permute-done((bf16[4,128,256]{2,1,0:T(8,128)(2,1)S(1)}, bf16[4,128,256]{2,1,0:T(8,128)(2,1)S(1)}, u32[]{:S(2)}, u32[]{:S(2)}) %collective-permute-start.41) | collective-permute-done | bytes 262176 | tf_op jit(solution)/shard_map/ppermute | solution.py:40
  145.6 1.2 collective-permute-start.43
  146.8 3.9 %collective-permute-done.36.refs_13_ = bf16[4,128,256]{2,1,0:T(8,128)(2,1)S(1)} collective-permute-done((bf16[4,128,256]{2,1,0:T(8,128)(2,1)S(1)}, bf16[4,128,256]{2,1,0:T(8,128)(2,1)S(1)}, u32[]{:S(2)}, u32[]{:S(2)}) %collective-permute-start.36) | collective-permute-done | bytes 262176 | tf_op jit(solution)/shard_map/ppermute | solution.py:40
  150.7 3.8 %collective-permute-done.43.refs_21_ = bf16[4,128,256]{2,1,0:T(8,128)(2,1)S(1)} collective-permute-done((bf16[4,128,256]{2,1,0:T(8,128)(2,1)S(1)}, bf16[4,128,256]{2,1,0:T(8,128)(2,1)S(1)}, u32[]{:S(2)}, u32[]{:S(2)}) %collective-permute-start.43) | collective-permute-done | bytes 262176 | tf_op jit(solution)/shard_map/ppermute | solution.py:40
  154.5 1.5 shard_map.87
  156.1 1.5 collective-permute-done.44.theirs
  157.6 1.4 shard_map.88
  (51 shorter events, 8.2 us)
Async XLA Ops:
  0.6 59.2 %collective-permute-start.11 = (bf16[32,128,256]{2,1,0:T(8,128)(2,1)}, bf16[32,128,256]{2,1,0:T(8,128)(2,1)S(1)}, u32[]{:S(2)}, u32[]{:S(2)}) collective-permute-start(bf16[32,128,256]{2,1,0:T(8,128)(2,1)} %rot_mine.1), channel_id=1, source_target_pairs={{0,1},{1,0},{2,3},{3,2},{4,5},{5,4},{6,7},{7,6},{8,9},{9,8},{10,11... | collective-permute-start | bytes 6291464 | tf_op jit(solution)/shard_map/ppermute | solution.py:40
  1.1 1.0 copy-start.1
  2.2 0.7 copy-start.3
  4.8 6.1 %collective-permute-start.2 = (bf16[128,256]{1,0:T(8,128)(2,1)}, bf16[128,256]{1,0:T(8,128)(2,1)S(1)}, u32[]{:S(2)}, u32[]{:S(2)}) collective-permute-start(bf16[128,256]{1,0:T(8,128)(2,1)} %param.7), channel_id=1, source_target_pairs={{0,2},{1,3},{2,0},{3,1},{4,6},{5,7},{6,4},{7,5},{8,10},{9,11},{10,... | collective-permute-start | bytes 196616 | tf_op jit(solution)/shard_map/ppermute | solution.py:40
  7.4 11.6 %collective-permute-start = (bf16[4,128,256]{2,1,0:T(8,128)(2,1)S(1)}, bf16[4,128,256]{2,1,0:T(8,128)(2,1)S(1)}, u32[]{:S(2)}, u32[]{:S(2)}) collective-permute-start(bf16[4,128,256]{2,1,0:T(8,128)(2,1)S(1)} %get-tuple-element.62), channel_id=1, source_target_pairs={{0,0},{1,17},{2,2},{3,19},{4,4},{5,21},{6,6},{7,23},{8,8},{9,25},{... | collective-permute-start | bytes 786440 | tf_op jit(solution)/shard_map/ppermute | solution.py:451
  8.1 10.9 %collective-permute-start.1 = (bf16[4,128,256]{2,1,0:T(8,128)(2,1)S(1)}, bf16[4,128,256]{2,1,0:T(8,128)(2,1)S(1)}, u32[]{:S(2)}, u32[]{:S(2)}) collective-permute-start(bf16[4,128,256]{2,1,0:T(8,128)(2,1)S(1)} %get-tuple-element.63), channel_id=1, source_target_pairs={{0,17},{1,0},{2,19},{3,2},{4,21},{5,4},{6,23},{7,6},{8,25},{9,8},{... | collective-permute-start | bytes 786440 | tf_op jit(solution)/shard_map/ppermute | solution.py:451
  11.8 7.2 %collective-permute-start.3 = (bf16[2,128,256]{2,1,0:T(8,128)(2,1)S(1)}, bf16[2,128,256]{2,1,0:T(8,128)(2,1)S(1)}, u32[]{:S(2)}, u32[]{:S(2)}) collective-permute-start(bf16[2,128,256]{2,1,0:T(8,128)(2,1)S(1)} %pad_maximum_fusion.2), channel_id=1, source_target_pairs={{0,4},{1,5},{2,6},{3,7},{4,8},{5,9},{6,10},{7,11},{8,12},{9,13},{1... | collective-permute-start | bytes 393224 | tf_op jit(solution)/shard_map/ppermute | solution.py:40
  19.0 6.8 %collective-permute-start.4 = (bf16[2,128,256]{2,1,0:T(8,128)(2,1)S(1)}, bf16[2,128,256]{2,1,0:T(8,128)(2,1)S(1)}, u32[]{:S(2)}, u32[]{:S(2)}) collective-permute-start(bf16[2,128,256]{2,1,0:T(8,128)(2,1)S(1)} %collective-permute-done.3), channel_id=1, source_target_pairs={{0,4},{1,5},{2,6},{3,7},{4,8},{5,9},{6,10},{7,11},{8,12},{9,13},{1... | collective-permute-start | bytes 393224 | tf_op jit(solution)/shard_map/ppermute | solution.py:40
  25.8 7.9 %collective-permute-start.7 = (bf16[2,128,256]{2,1,0:T(8,128)(2,1)S(1)}, bf16[2,128,256]{2,1,0:T(8,128)(2,1)S(1)}, u32[]{:S(2)}, u32[]{:S(2)}) collective-permute-start(bf16[2,128,256]{2,1,0:T(8,128)(2,1)S(1)} %collective-permute-done.4), channel_id=1, source_target_pairs={{0,4},{1,5},{2,6},{3,7},{4,8},{5,9},{6,10},{7,11},{8,12},{9,13},{1... | collective-permute-start | bytes 393224 | tf_op jit(solution)/shard_map/ppermute | solution.py:40
  25.9 9.0 %collective-permute-start.8 = (bf16[2,2,128,256]{3,2,1,0:T(8,128)(2,1)S(1)}, bf16[2,2,128,256]{3,2,1,0:T(8,128)(2,1)S(1)}, u32[]{:S(2)}, u32[]{:S(2)}) collective-permute-start(bf16[2,2,128,256]{3,2,1,0:T(8,128)(2,1)S(1)} %get-tuple-element.117.refs_0_.refs_1_), channel_id=1, source_target_pairs={{0,2},{1,3},{2,0},{3,1},{4,6},{5,7},{6,4},{7,5},{8,10},{9,11},{10,... | collective-permute-start | bytes 786440 | tf_op jit(solution)/shard_map/ppermute | solution.py:40
  27.0 12.3 %collective-permute-start.9 = (bf16[2,2,128,256]{3,2,1,0:T(8,128)(2,1)S(1)}, bf16[2,2,128,256]{3,2,1,0:T(8,128)(2,1)S(1)}, u32[]{:S(2)}, u32[]{:S(2)}) collective-permute-start(bf16[2,2,128,256]{3,2,1,0:T(8,128)(2,1)S(1)} %get-tuple-element.117.refs_0_.refs_1_), channel_id=1, source_target_pairs={{0,4},{1,5},{2,6},{3,7},{4,8},{5,9},{6,10},{7,11},{8,12},{9,13},{1... | collective-permute-start | bytes 786440 | tf_op jit(solution)/shard_map/ppermute | solution.py:40
  27.0 12.3 %collective-permute-start.5 = (bf16[2,2,128,256]{3,2,1,0:T(8,128)(2,1)S(1)}, bf16[2,2,128,256]{3,2,1,0:T(8,128)(2,1)S(1)}, u32[]{:S(2)}, u32[]{:S(2)}) collective-permute-start(bf16[2,2,128,256]{3,2,1,0:T(8,128)(2,1)S(1)} %get-tuple-element.116.refs_0_), channel_id=1, source_target_pairs={{0,2},{1,3},{2,0},{3,1},{4,6},{5,7},{6,4},{7,5},{8,10},{9,11},{10,... | collective-permute-start | bytes 786440 | tf_op jit(solution)/shard_map/ppermute | solution.py:40
  33.7 8.4 %collective-permute-start.6 = (bf16[2,2,128,256]{3,2,1,0:T(8,128)(2,1)S(1)}, bf16[2,2,128,256]{3,2,1,0:T(8,128)(2,1)S(1)}, u32[]{:S(2)}, u32[]{:S(2)}) collective-permute-start(bf16[2,2,128,256]{3,2,1,0:T(8,128)(2,1)S(1)} %get-tuple-element.116.refs_0_), channel_id=1, source_target_pairs={{0,4},{1,5},{2,6},{3,7},{4,8},{5,9},{6,10},{7,11},{8,12},{9,13},{1... | collective-permute-start | bytes 786440 | tf_op jit(solution)/shard_map/ppermute | solution.py:40
  42.2 8.8 %collective-permute-start.14 = (bf16[2,2,128,256]{3,2,1,0:T(8,128)(2,1)S(1)}, bf16[2,2,128,256]{3,2,1,0:T(8,128)(2,1)S(1)}, u32[]{:S(2)}, u32[]{:S(2)}) collective-permute-start(bf16[2,2,128,256]{3,2,1,0:T(8,128)(2,1)S(1)} %collective-permute-done.6.refs_1_), channel_id=1, source_target_pairs={{0,2},{1,3},{2,0},{3,1},{4,6},{5,7},{6,4},{7,5},{8,10},{9,11},{10,... | collective-permute-start | bytes 786440 | tf_op jit(solution)/shard_map/ppermute | solution.py:40
  43.1 16.8 %collective-permute-start.10 = (bf16[4,2,128,256]{3,2,1,0:T(8,128)(2,1)S(1)}, bf16[4,2,128,256]{3,2,1,0:T(8,128)(2,1)S(1)}, u32[]{:S(2)}, u32[]{:S(2)}) collective-permute-start(bf16[4,2,128,256]{3,2,1,0:T(8,128)(2,1)S(1)} %pad_maximum_fusion.mine), channel_id=1, source_target_pairs={{0,1},{1,0},{2,3},{3,2},{4,5},{5,4},{6,7},{7,6},{8,9},{9,8},{10,11... | collective-permute-start | bytes 1572872 | tf_op jit(solution)/shard_map/ppermute | solution.py:40
  43.1 11.0 %collective-permute-start.15 = (bf16[2,2,128,256]{3,2,1,0:T(8,128)(2,1)S(1)}, bf16[2,2,128,256]{3,2,1,0:T(8,128)(2,1)S(1)}, u32[]{:S(2)}, u32[]{:S(2)}) collective-permute-start(bf16[2,2,128,256]{3,2,1,0:T(8,128)(2,1)S(1)} %collective-permute-done.6.refs_1_), channel_id=1, source_target_pairs={{0,4},{1,5},{2,6},{3,7},{4,8},{5,9},{6,10},{7,11},{8,12},{9,13},{1... | collective-permute-start | bytes 786440 | tf_op jit(solution)/shard_map/ppermute | solution.py:40
  43.2 12.1 %collective-permute-start.12 = (bf16[2,2,128,256]{3,2,1,0:T(8,128)(2,1)S(1)}, bf16[2,2,128,256]{3,2,1,0:T(8,128)(2,1)S(1)}, u32[]{:S(2)}, u32[]{:S(2)}) collective-permute-start(bf16[2,2,128,256]{3,2,1,0:T(8,128)(2,1)S(1)} %collective-permute-done.9.refs_1_), channel_id=1, source_target_pairs={{0,2},{1,3},{2,0},{3,1},{4,6},{5,7},{6,4},{7,5},{8,10},{9,11},{10,... | collective-permute-start | bytes 786440 | tf_op jit(solution)/shard_map/ppermute | solution.py:40
  50.9 8.9 %collective-permute-start.13 = (bf16[2,2,128,256]{3,2,1,0:T(8,128)(2,1)S(1)}, bf16[2,2,128,256]{3,2,1,0:T(8,128)(2,1)S(1)}, u32[]{:S(2)}, u32[]{:S(2)}) collective-permute-start(bf16[2,2,128,256]{3,2,1,0:T(8,128)(2,1)S(1)} %collective-permute-done.9.refs_1_), channel_id=1, source_target_pairs={{0,4},{1,5},{2,6},{3,7},{4,8},{5,9},{6,10},{7,11},{8,12},{9,13},{1... | collective-permute-start | bytes 786440 | tf_op jit(solution)/shard_map/ppermute | solution.py:40
  54.1 9.2 %collective-permute-start.16 = (bf16[2,2,128,256]{3,2,1,0:T(8,128)(2,1)S(1)}, bf16[2,2,128,256]{3,2,1,0:T(8,128)(2,1)S(1)}, u32[]{:S(2)}, u32[]{:S(2)}) collective-permute-start(bf16[2,2,128,256]{3,2,1,0:T(8,128)(2,1)S(1)} %collective-permute-done.15.refs_2_), channel_id=1, source_target_pairs={{0,2},{1,3},{2,0},{3,1},{4,6},{5,7},{6,4},{7,5},{8,10},{9,11},{10,... | collective-permute-start | bytes 786440 | tf_op jit(solution)/shard_map/ppermute | solution.py:40
  55.3 11.0 %collective-permute-start.17 = (bf16[2,2,128,256]{3,2,1,0:T(8,128)(2,1)S(1)}, bf16[2,2,128,256]{3,2,1,0:T(8,128)(2,1)S(1)}, u32[]{:S(2)}, u32[]{:S(2)}) collective-permute-start(bf16[2,2,128,256]{3,2,1,0:T(8,128)(2,1)S(1)} %collective-permute-done.15.refs_2_), channel_id=1, source_target_pairs={{0,4},{1,5},{2,6},{3,7},{4,8},{5,9},{6,10},{7,11},{8,12},{9,13},{1... | collective-permute-start | bytes 786440 | tf_op jit(solution)/shard_map/ppermute | solution.py:40
  59.8 8.3 %collective-permute-start.19 = (bf16[2,2,128,256]{3,2,1,0:T(8,128)(2,1)S(1)}, bf16[2,2,128,256]{3,2,1,0:T(8,128)(2,1)S(1)}, u32[]{:S(2)}, u32[]{:S(2)}) collective-permute-start(bf16[2,2,128,256]{3,2,1,0:T(8,128)(2,1)S(1)} %collective-permute-done.13.refs_2_), channel_id=1, source_target_pairs={{0,2},{1,3},{2,0},{3,1},{4,6},{5,7},{6,4},{7,5},{8,10},{9,11},{10,... | collective-permute-start | bytes 786440 | tf_op jit(solution)/shard_map/ppermute | solution.py:40
  61.4 9.1 %collective-permute-start.20 = (bf16[2,2,128,256]{3,2,1,0:T(8,128)(2,1)S(1)}, bf16[2,2,128,256]{3,2,1,0:T(8,128)(2,1)S(1)}, u32[]{:S(2)}, u32[]{:S(2)}) collective-permute-start(bf16[2,2,128,256]{3,2,1,0:T(8,128)(2,1)S(1)} %collective-permute-done.13.refs_2_), channel_id=1, source_target_pairs={{0,4},{1,5},{2,6},{3,7},{4,8},{5,9},{6,10},{7,11},{8,12},{9,13},{1... | collective-permute-start | bytes 786440 | tf_op jit(solution)/shard_map/ppermute | solution.py:40
  66.3 7.6 %collective-permute-start.18 = (bf16[2,2,128,256]{3,2,1,0:T(8,128)(2,1)S(1)}, bf16[2,2,128,256]{3,2,1,0:T(8,128)(2,1)S(1)}, u32[]{:S(2)}, u32[]{:S(2)}) collective-permute-start(bf16[2,2,128,256]{3,2,1,0:T(8,128)(2,1)S(1)} %collective-permute-done.17.refs_3_), channel_id=1, source_target_pairs={{0,2},{1,3},{2,0},{3,1},{4,6},{5,7},{6,4},{7,5},{8,10},{9,11},{10,... | collective-permute-start | bytes 786440 | tf_op jit(solution)/shard_map/ppermute | solution.py:40
  70.5 7.9 %collective-permute-start.21 = (bf16[2,2,128,256]{3,2,1,0:T(8,128)(2,1)S(1)}, bf16[2,2,128,256]{3,2,1,0:T(8,128)(2,1)S(1)}, u32[]{:S(2)}, u32[]{:S(2)}) collective-permute-start(bf16[2,2,128,256]{3,2,1,0:T(8,128)(2,1)S(1)} %collective-permute-done.20.refs_3_), channel_id=1, source_target_pairs={{0,2},{1,3},{2,0},{3,1},{4,6},{5,7},{6,4},{7,5},{8,10},{9,11},{10,... | collective-permute-start | bytes 786440 | tf_op jit(solution)/shard_map/ppermute | solution.py:40
  77.3 4.4 %copy-start = (bf16[32,128,256]{2,1,0:T(8,128)(2,1)S(1)}, bf16[32,128,256]{2,1,0:T(8,128)(2,1)}, u32[]{:S(2)}) copy-start(bf16[32,128,256]{2,1,0:T(8,128)(2,1)} %rot_mine.1) | copy-start | bytes 6291460
  81.7 14.3 %copy-start.2 = (f32[8,32]{1,0:T(8,128)S(1)}, f32[8,32]{1,0:T(8,128)}, u32[]{:S(2)}) copy-start(f32[8,32]{1,0:T(8,128)} %fields.1) | copy-start | bytes 3076
  83.4 5.4 %collective-permute-start.23 = (f32[4,32]{1,0:T(4,128)S(1)}, f32[4,32]{1,0:T(4,128)S(1)}, u32[]{:S(2)}, u32[]{:S(2)}) collective-permute-start(f32[4,32]{1,0:T(4,128)S(1)} %shard_map.81), channel_id=1, source_target_pairs={{0,4},{1,5},{2,6},{3,7},{4,8},{5,9},{6,10},{7,11},{8,12},{9,13},{1... | collective-permute-start | bytes 1544 | tf_op jit(solution)/shard_map/ppermute | solution.py:40
  83.4 5.4 %collective-permute-start.24 = (f32[4,32]{1,0:T(4,128)S(1)}, f32[4,32]{1,0:T(4,128)S(1)}, u32[]{:S(2)}, u32[]{:S(2)}) collective-permute-start(f32[4,32]{1,0:T(4,128)S(1)} %shard_map.81), channel_id=1, source_target_pairs={{0,12},{1,13},{2,14},{3,15},{4,0},{5,1},{6,2},{7,3},{8,4},{9,5},{1... | collective-permute-start | bytes 1544 | tf_op jit(solution)/shard_map/ppermute | solution.py:40
  87.3 4.5 %collective-permute-start.22 = (f32[4,32]{1,0:T(4,128)S(1)}, f32[4,32]{1,0:T(4,128)S(1)}, u32[]{:S(2)}, u32[]{:S(2)}) collective-permute-start(f32[4,32]{1,0:T(4,128)S(1)} %shard_map.81), channel_id=1, source_target_pairs={{0,8},{1,9},{2,10},{3,11},{4,12},{5,13},{6,14},{7,15},{8,0},{9,1},... | collective-permute-start | bytes 1544 | tf_op jit(solution)/shard_map/ppermute | solution.py:40
  91.7 3.6 %collective-permute-start.25 = (f32[4,32]{1,0:T(4,128)S(1)}, f32[4,32]{1,0:T(4,128)S(1)}, u32[]{:S(2)}, u32[]{:S(2)}) collective-permute-start(f32[4,32]{1,0:T(4,128)S(1)} %add_add_fusion.mine), channel_id=1, source_target_pairs={{0,2},{1,3},{2,0},{3,1},{4,6},{5,7},{6,4},{7,5},{8,10},{9,11},{10,... | collective-permute-start | bytes 1544 | tf_op jit(solution)/shard_map/ppermute | solution.py:40
  93.0 2.4 %collective-permute-start.26 = (f32[4,32]{1,0:T(4,128)S(1)}, f32[4,32]{1,0:T(4,128)S(1)}, u32[]{:S(2)}, u32[]{:S(2)}) collective-permute-start(f32[4,32]{1,0:T(4,128)S(1)} %add_add_fusion.mine), channel_id=1, source_target_pairs={{0,1},{1,0},{2,3},{3,2},{4,5},{5,4},{6,7},{7,6},{8,9},{9,8},{10,11... | collective-permute-start | bytes 1544 | tf_op jit(solution)/shard_map/ppermute | solution.py:40
  93.0 3.0 %collective-permute-start.27 = (f32[4,32]{1,0:T(4,128)S(1)}, f32[4,32]{1,0:T(4,128)S(1)}, u32[]{:S(2)}, u32[]{:S(2)}) collective-permute-start(f32[4,32]{1,0:T(4,128)S(1)} %add_add_fusion.mine), channel_id=1, source_target_pairs={{0,3},{1,2},{2,1},{3,0},{4,7},{5,6},{6,5},{7,4},{8,11},{9,10},{10,... | collective-permute-start | bytes 1544 | tf_op jit(solution)/shard_map/ppermute | solution.py:40
  105.1 2.9 %collective-permute-start.28 = (bf16[4,64,2048]{2,1,0:T(8,128)(2,1)S(1)}, bf16[4,64,2048]{2,1,0:T(8,128)(2,1)S(1)}, u32[]{:S(2)}, u32[]{:S(2)}) collective-permute-start(bf16[4,64,2048]{2,1,0:T(8,128)(2,1)S(1)} %get-tuple-element.93), channel_id=1, source_target_pairs={{0,1},{1,0},{2,3},{3,2},{4,5},{5,4},{6,7},{7,6},{8,9},{9,8},{10,11... | collective-permute-start | bytes 3145736 | tf_op jit(solution)/shard_map/ppermute | solution.py:40
  105.6 3.8 %collective-permute-start.29 = (bf16[4,64,2048]{2,1,0:T(8,128)(2,1)S(1)}, bf16[4,64,2048]{2,1,0:T(8,128)(2,1)S(1)}, u32[]{:S(2)}, u32[]{:S(2)}) collective-permute-start(bf16[4,64,2048]{2,1,0:T(8,128)(2,1)S(1)} %get-tuple-element.94), channel_id=1, source_target_pairs={{0,1},{1,0},{2,3},{3,2},{4,5},{5,4},{6,7},{7,6},{8,9},{9,8},{10,11... | collective-permute-start | bytes 3145736 | tf_op jit(solution)/shard_map/ppermute | solution.py:40
  106.4 9.2 %collective-permute-start.30 = (bf16[4,128,256]{2,1,0:T(8,128)(2,1)S(1)}, bf16[4,128,256]{2,1,0:T(8,128)(2,1)S(1)}, u32[]{:S(2)}, u32[]{:S(2)}) collective-permute-start(bf16[4,128,256]{2,1,0:T(8,128)(2,1)S(1)} %get-tuple-element.99.refs_6_), channel_id=1, source_target_pairs={{0,2},{1,3},{2,0},{3,1},{4,6},{5,7},{6,4},{7,5},{8,10},{9,11},{10,... | collective-permute-start | bytes 786440 | tf_op jit(solution)/shard_map/ppermute | solution.py:40
  107.3 10.9 %collective-permute-start.31 = (bf16[4,128,256]{2,1,0:T(8,128)(2,1)S(1)}, bf16[4,128,256]{2,1,0:T(8,128)(2,1)S(1)}, u32[]{:S(2)}, u32[]{:S(2)}) collective-permute-start(bf16[4,128,256]{2,1,0:T(8,128)(2,1)S(1)} %get-tuple-element.99.refs_6_), channel_id=1, source_target_pairs={{0,4},{1,5},{2,6},{3,7},{4,8},{5,9},{6,10},{7,11},{8,12},{9,13},{1... | collective-permute-start | bytes 786440 | tf_op jit(solution)/shard_map/ppermute | solution.py:40
  110.2 11.1 %collective-permute-start.37 = (bf16[4,128,256]{2,1,0:T(8,128)(2,1)S(1)}, bf16[4,128,256]{2,1,0:T(8,128)(2,1)S(1)}, u32[]{:S(2)}, u32[]{:S(2)}) collective-permute-start(bf16[4,128,256]{2,1,0:T(8,128)(2,1)S(1)} %get-tuple-element.106.refs_14_), channel_id=1, source_target_pairs={{0,2},{1,3},{2,0},{3,1},{4,6},{5,7},{6,4},{7,5},{8,10},{9,11},{10,... | collective-permute-start | bytes 786440 | tf_op jit(solution)/shard_map/ppermute | solution.py:40
  111.0 12.8 %collective-permute-start.38 = (bf16[4,128,256]{2,1,0:T(8,128)(2,1)S(1)}, bf16[4,128,256]{2,1,0:T(8,128)(2,1)S(1)}, u32[]{:S(2)}, u32[]{:S(2)}) collective-permute-start(bf16[4,128,256]{2,1,0:T(8,128)(2,1)S(1)} %get-tuple-element.106.refs_14_), channel_id=1, source_target_pairs={{0,4},{1,5},{2,6},{3,7},{4,8},{5,9},{6,10},{7,11},{8,12},{9,13},{1... | collective-permute-start | bytes 786440 | tf_op jit(solution)/shard_map/ppermute | solution.py:40
  118.3 9.2 %collective-permute-start.32 = (bf16[4,128,256]{2,1,0:T(8,128)(2,1)S(1)}, bf16[4,128,256]{2,1,0:T(8,128)(2,1)S(1)}, u32[]{:S(2)}, u32[]{:S(2)}) collective-permute-start(bf16[4,128,256]{2,1,0:T(8,128)(2,1)S(1)} %collective-permute-done.31.refs_7_), channel_id=1, source_target_pairs={{0,2},{1,3},{2,0},{3,1},{4,6},{5,7},{6,4},{7,5},{8,10},{9,11},{10,... | collective-permute-start | bytes 786440 | tf_op jit(solution)/shard_map/ppermute | solution.py:40
  119.5 10.1 %collective-permute-start.33 = (bf16[4,128,256]{2,1,0:T(8,128)(2,1)S(1)}, bf16[4,128,256]{2,1,0:T(8,128)(2,1)S(1)}, u32[]{:S(2)}, u32[]{:S(2)}) collective-permute-start(bf16[4,128,256]{2,1,0:T(8,128)(2,1)S(1)} %collective-permute-done.31.refs_7_), channel_id=1, source_target_pairs={{0,4},{1,5},{2,6},{3,7},{4,8},{5,9},{6,10},{7,11},{8,12},{9,13},{1... | collective-permute-start | bytes 786440 | tf_op jit(solution)/shard_map/ppermute | solution.py:40
  123.9 9.2 %collective-permute-start.39 = (bf16[4,128,256]{2,1,0:T(8,128)(2,1)S(1)}, bf16[4,128,256]{2,1,0:T(8,128)(2,1)S(1)}, u32[]{:S(2)}, u32[]{:S(2)}) collective-permute-start(bf16[4,128,256]{2,1,0:T(8,128)(2,1)S(1)} %collective-permute-done.38.refs_15_), channel_id=1, source_target_pairs={{0,2},{1,3},{2,0},{3,1},{4,6},{5,7},{6,4},{7,5},{8,10},{9,11},{10,... | collective-permute-start | bytes 786440 | tf_op jit(solution)/shard_map/ppermute | solution.py:40
  125.1 10.7 %collective-permute-start.40 = (bf16[4,128,256]{2,1,0:T(8,128)(2,1)S(1)}, bf16[4,128,256]{2,1,0:T(8,128)(2,1)S(1)}, u32[]{:S(2)}, u32[]{:S(2)}) collective-permute-start(bf16[4,128,256]{2,1,0:T(8,128)(2,1)S(1)} %collective-permute-done.38.refs_15_), channel_id=1, source_target_pairs={{0,4},{1,5},{2,6},{3,7},{4,8},{5,9},{6,10},{7,11},{8,12},{9,13},{1... | collective-permute-start | bytes 786440 | tf_op jit(solution)/shard_map/ppermute | solution.py:40
  129.6 9.2 %collective-permute-start.34 = (bf16[4,128,256]{2,1,0:T(8,128)(2,1)S(1)}, bf16[4,128,256]{2,1,0:T(8,128)(2,1)S(1)}, u32[]{:S(2)}, u32[]{:S(2)}) collective-permute-start(bf16[4,128,256]{2,1,0:T(8,128)(2,1)S(1)} %collective-permute-done.33.refs_8_), channel_id=1, source_target_pairs={{0,2},{1,3},{2,0},{3,1},{4,6},{5,7},{6,4},{7,5},{8,10},{9,11},{10,... | collective-permute-start | bytes 786440 | tf_op jit(solution)/shard_map/ppermute | solution.py:40
  131.2 10.2 %collective-permute-start.35 = (bf16[4,128,256]{2,1,0:T(8,128)(2,1)S(1)}, bf16[4,128,256]{2,1,0:T(8,128)(2,1)S(1)}, u32[]{:S(2)}, u32[]{:S(2)}) collective-permute-start(bf16[4,128,256]{2,1,0:T(8,128)(2,1)S(1)} %collective-permute-done.33.refs_8_), channel_id=1, source_target_pairs={{0,4},{1,5},{2,6},{3,7},{4,8},{5,9},{6,10},{7,11},{8,12},{9,13},{1... | collective-permute-start | bytes 786440 | tf_op jit(solution)/shard_map/ppermute | solution.py:40
  135.9 9.2 %collective-permute-start.41 = (bf16[4,128,256]{2,1,0:T(8,128)(2,1)S(1)}, bf16[4,128,256]{2,1,0:T(8,128)(2,1)S(1)}, u32[]{:S(2)}, u32[]{:S(2)}) collective-permute-start(bf16[4,128,256]{2,1,0:T(8,128)(2,1)S(1)} %collective-permute-done.40.refs_16_), channel_id=1, source_target_pairs={{0,2},{1,3},{2,0},{3,1},{4,6},{5,7},{6,4},{7,5},{8,10},{9,11},{10,... | collective-permute-start | bytes 786440 | tf_op jit(solution)/shard_map/ppermute | solution.py:40
  137.0 8.6 %collective-permute-start.42 = (bf16[4,128,256]{2,1,0:T(8,128)(2,1)S(1)}, bf16[4,128,256]{2,1,0:T(8,128)(2,1)S(1)}, u32[]{:S(2)}, u32[]{:S(2)}) collective-permute-start(bf16[4,128,256]{2,1,0:T(8,128)(2,1)S(1)} %collective-permute-done.40.refs_16_), channel_id=1, source_target_pairs={{0,4},{1,5},{2,6},{3,7},{4,8},{5,9},{6,10},{7,11},{8,12},{9,13},{1... | collective-permute-start | bytes 786440 | tf_op jit(solution)/shard_map/ppermute | solution.py:40
  141.5 9.2 %collective-permute-start.36 = (bf16[4,128,256]{2,1,0:T(8,128)(2,1)S(1)}, bf16[4,128,256]{2,1,0:T(8,128)(2,1)S(1)}, u32[]{:S(2)}, u32[]{:S(2)}) collective-permute-start(bf16[4,128,256]{2,1,0:T(8,128)(2,1)S(1)} %collective-permute-done.35.refs_9_), channel_id=1, source_target_pairs={{0,2},{1,3},{2,0},{3,1},{4,6},{5,7},{6,4},{7,5},{8,10},{9,11},{10,... | collective-permute-start | bytes 786440 | tf_op jit(solution)/shard_map/ppermute | solution.py:40
  145.6 8.9 %collective-permute-start.43 = (bf16[4,128,256]{2,1,0:T(8,128)(2,1)S(1)}, bf16[4,128,256]{2,1,0:T(8,128)(2,1)S(1)}, u32[]{:S(2)}, u32[]{:S(2)}) collective-permute-start(bf16[4,128,256]{2,1,0:T(8,128)(2,1)S(1)} %collective-permute-done.42.refs_17_), channel_id=1, source_target_pairs={{0,2},{1,3},{2,0},{3,1},{4,6},{5,7},{6,4},{7,5},{8,10},{9,11},{10,... | collective-permute-start | bytes 786440 | tf_op jit(solution)/shard_map/ppermute | solution.py:40
  156.0 1.6 %collective-permute-start.44 = (bf16[4,128,256]{2,1,0:T(8,128)(2,1)S(1)}, bf16[4,128,256]{2,1,0:T(8,128)(2,1)S(1)}, u32[]{:S(2)}, u32[]{:S(2)}) collective-permute-start(bf16[4,128,256]{2,1,0:T(8,128)(2,1)S(1)} %get-tuple-element.114), channel_id=1, source_target_pairs={{0,1},{1,0},{2,3},{3,2},{4,5},{5,4},{6,7},{7,6},{8,9},{9,8},{10,11... | collective-permute-start | bytes 786440 | tf_op jit(solution)/shard_map/ppermute | solution.py:40

commit v6 on v5

--- a/solution.py
+++ b/solution.py
@@ -41,17 +41,19 @@
 
 
 class Stream:
-    def __init__(self, layout, piece):
+    def __init__(self, layout, piece, last_along_z=False):
         self.layout = layout
         self.ring = [piece]
         self.across = []
+        self.last_along_z = last_along_z
 
     def advance(self, anchors=()):
-        if len(self.across) == self.layout.z:
-            return anchors
         latest = self.ring[-1]
-        moved = [self.layout.shift(latest, dy=1)]
         last = len(self.ring) == self.layout.z
+        if last and self.last_along_z:
+            moved = [self.layout.shift(self.across[-1], dz=1)]
+        else:
+            moved = [self.layout.shift(latest, dy=1)]
         if not last:
             moved.append(self.layout.shift(latest, dz=1))
         if anchors or not last:
@@ -65,6 +67,22 @@
         return ring + [(array, dz, 1) for dz, array in enumerate(self.across)]
 
 
+class CrossFirst:
+    def __init__(self, layout, piece):
+        self.layout = layout
+        self.piece = piece
+        self.ring = []
+
+    def advance(self, anchors=()):
+        if self.ring:
+            moved = self.layout.shift(self.ring[-1], dz=1)
+        else:
+            moved = self.layout.shift(self.piece, dy=1)
+        anchors, moved = lax.optimization_barrier((anchors, moved))
+        self.ring.append(moved if self.ring else jnp.stack([self.piece, moved]))
+        return anchors
+
+
 def gathered(layout, dz, dy):
     index = lax.axis_index("chol")
     z, y = index // 4, lax.rem(index // 2, 2)
@@ -94,20 +112,25 @@
     )(mine, theirs)
 
 
+def product(left, right):
+    high, right_high = left.astype(BF16), right.astype(BF16)
+    low = (left - high.astype(F32)).astype(BF16)
+    right_low = (right - right_high.astype(F32)).astype(BF16)
+    return jnp.dot(
+        jnp.concatenate([high, high, low], axis=1),
+        jnp.concatenate([right_high, right_low, right_high], axis=0),
+        preferred_element_type=F32,
+    )
+
+
 def newton_inverses(matrices):
     shape = matrices[0].shape
     same = lax.broadcasted_iota(jnp.int32, shape, 0) == lax.broadcasted_iota(jnp.int32, shape, 1)
     twice = jnp.where(same, 2.0, 0.0).astype(F32)
     estimates = [twice - matrix for matrix in matrices]
     for _ in range(ITERS - 1):
-        products = [
-            jnp.dot(matrix, estimate, precision=HIGHEST, preferred_element_type=F32)
-            for matrix, estimate in zip(matrices, estimates)
-        ]
-        estimates = [
-            jnp.dot(estimate, twice - product, precision=HIGHEST, preferred_element_type=F32)
-            for estimate, product in zip(estimates, products)
-        ]
+        steps = [twice - product(a, x) for a, x in zip(matrices, estimates)]
+        estimates = [product(x, step) for x, step in zip(estimates, steps)]
     return estimates
 
 
@@ -116,7 +139,7 @@
     matrices = []
     for walker in range(out.shape[0]):
         for piece, (dz, dy) in zip(pieces, places):
-            full[walker, gathered(layout, dz, dy)] = piece[walker]
+            full[walker, gathered(layout, dz, dy)] = piece[:, walker]
         rows = full[walker].reshape(-1, full.shape[-1])
         matrices.append(jnp.dot(trial[...], rows, preferred_element_type=F32))
     for walker, inverse in enumerate(newton_inverses(matrices)):
@@ -124,9 +147,9 @@
 
 
 def inverses_of(layout, trial, stream):
-    arrays = [array for array, _, _ in stream.pieces()]
+    arrays = [array for array, *_ in stream.pieces()]
     places = [place for _, *place in stream.pieces()]
-    count, _, rows, electrons = arrays[0].shape
+    _, count, rows, electrons = arrays[0].shape
     return pl.pallas_call(
         functools.partial(inverse_kernel, layout, places),
         out_shape=[
@@ -136,6 +159,11 @@
         in_specs=vmem_specs(1 + len(arrays)),
         out_specs=vmem_specs(2),
         compiler_params=params(8),
+        cost_estimate=pl.CostEstimate(
+            flops=2 * count * electrons**2 * (trial.shape[1] + 6 * (ITERS - 1) * electrons),
+            bytes_accessed=4 * (count + 1) * trial.shape[1] * electrons,
+            transcendentals=0,
+        ),
     )(trial, *arrays)
 
 
@@ -147,7 +175,7 @@
     count = 0
     for chunk, inverse, size in zip(chunks, inverses, sizes):
         for walker in range(size):
-            both = chunk[walker].reshape(2 * rows, electrons)
+            both = chunk[:, walker].reshape(2 * rows, electrons)
             product = jnp.dot(both, inverse[walker], preferred_element_type=F32).astype(BF16)
             greens[:, :, count] = product.reshape(2, rows // BLOCK, BLOCK, electrons)
             count += 1
@@ -178,7 +206,7 @@
 
 def bias_of(chunks, inverses, rot_mine, rot_theirs):
     vectors, rows, electrons = rot_mine.shape
-    sizes = [chunk.shape[0] for chunk in chunks]
+    sizes = [chunk.shape[1] for chunk in chunks]
     count = sum(sizes)
     return pl.pallas_call(
         functools.partial(bias_kernel, sizes),
@@ -242,41 +270,29 @@
     )(order, fields, *parts)
 
 
-def potential_kernel(start, weights, cholesky, kept, sent, blocks, semaphores):
-    vectors, orbitals = cholesky.shape[0], cholesky.shape[2]
-    half = kept.shape[0]
-    copies = []
-    for at in range(blocks.shape[0]):
-        rows = pl.ds(start + at * BLOCK, BLOCK)
-        copies.append(
-            pltpu.make_async_copy(cholesky.at[:, rows, :], blocks.at[at], semaphores.at[at])
-        )
-    for copy in copies:
-        copy.start()
-    for at, copy in enumerate(copies):
-        copy.wait()
-        block = blocks[at].reshape(vectors * BLOCK, orbitals)
-        result = TAU_ROOT * jnp.dot(weights[...], block, preferred_element_type=F32)
+def potential_kernel(weights, cholesky, kept, *sent):
+    half, part = kept.shape[0], sent[0].shape[1]
+    vectors, rows, orbitals = cholesky.shape
+    for at in range(0, rows, BLOCK):
+        columns = cholesky[:, at : at + BLOCK, :].reshape(vectors * BLOCK, orbitals)
+        result = TAU_ROOT * jnp.dot(weights[...], columns, preferred_element_type=F32)
         result = result.astype(BF16).reshape(2 * half, BLOCK, orbitals)
-        kept[:, at * BLOCK : (at + 1) * BLOCK, :] = result[:half]
-        sent[:, at * BLOCK : (at + 1) * BLOCK, :] = result[half:]
-
-
-def potential_of(weights, cholesky, part, parts):
+        kept[:, at : at + BLOCK, :] = result[:half]
+        start = at % part
+        sent[at // part][:, start : start + BLOCK, :] = result[half:]
+
+
+def potential_of(weights, cholesky):
     vectors, rows, orbitals = cholesky.shape
     half = weights.shape[0] // BLOCK // 2
-    rows = rows // parts
-    out = jax.ShapeDtypeStruct((half, rows, orbitals), BF16)
-    return pl.pallas_call(
-        functools.partial(potential_kernel, part * rows),
-        out_shape=[out, out],
-        in_specs=vmem_specs(1) + [pl.BlockSpec(memory_space=pltpu.HBM)],
-        out_specs=vmem_specs(2),
-        scratch_shapes=[
-            pltpu.VMEM((rows // BLOCK, vectors, BLOCK, orbitals), BF16),
-            pltpu.SemaphoreType.DMA((rows // BLOCK,)),
-        ],
-        compiler_params=params(48),
+    kept = jax.ShapeDtypeStruct((half, rows, orbitals), BF16)
+    sent = jax.ShapeDtypeStruct((half, rows // 2, orbitals), BF16)
+    return pl.pallas_call(
+        potential_kernel,
+        out_shape=[kept, sent, sent],
+        in_specs=vmem_specs(2),
+        out_specs=vmem_specs(3),
+        compiler_params=params(12),
     )(weights, cholesky)
 
 
@@ -315,14 +331,14 @@
 
 
 def second_kernel(layout, places, parts, *refs):
-    kept, theirs, refs = refs[:parts], refs[parts : 2 * parts], refs[2 * parts :]
+    potential, refs = refs[:parts], refs[parts:]
     bases, pieces, (mine, sent, buffer) = refs[:2], refs[2:-3], refs[-3:]
     b = lax.rem(lax.axis_index("chol"), 2)
     for walker in range(mine.shape[0]):
         for piece, (sibling, dz, dy) in zip(pieces, places):
             block = 1 - b if sibling else b
             buffer[walker, gathered(layout, dz, dy), block] = piece[walker]
-        rows = jnp.concatenate([part[walker] for part in (*kept, *theirs)], axis=0)
+        rows = jnp.concatenate([part[walker] for part in potential], axis=0)
         columns = buffer[walker].reshape(-1, buffer.shape[-1])
         term = jnp.dot(rows, columns, preferred_element_type=F32)
         count = term.shape[0] // 2
@@ -330,19 +346,19 @@
         sent[walker] = (bases[1][walker] + 0.5 * term[count:]).astype(BF16)
 
 
-def second_of(layout, kept, theirs, bases, streams):
+def second_of(layout, potential, bases, streams):
     arrays, places = [], []
     for sibling, stream in enumerate(streams):
         for array, dz, dy in stream.pieces():
             arrays.append(array)
             places.append((sibling, dz, dy))
-    orbitals = kept[0].shape[2]
-    half, rows, electrons = arrays[0].shape
+    half, rows, orbitals = potential[0].shape
+    electrons = arrays[0].shape[-1]
     out = jax.ShapeDtypeStruct((half, rows, electrons), BF16)
     return pl.pallas_call(
-        functools.partial(second_kernel, layout, places, len(kept)),
+        functools.partial(second_kernel, layout, places, len(potential)),
         out_shape=[out, out],
-        in_specs=vmem_specs(2 * len(kept) + 2 + len(arrays)),
+        in_specs=vmem_specs(len(potential) + 2 + len(arrays)),
         out_specs=vmem_specs(2),
         scratch_shapes=[pltpu.VMEM((half, layout.chol // 2, 2, rows, electrons), BF16)],
         compiler_params=params(16),
@@ -351,7 +367,7 @@
             bytes_accessed=2 * half * orbitals * (2 * rows + electrons),
             transcendentals=0,
         ),
-    )(*kept, *theirs, *bases, *arrays)
+    )(*potential, *bases, *arrays)
 
 
 def place_kernel(order, mine, theirs, out):
@@ -373,28 +389,30 @@
     )(order, mine, theirs)
 
 
-def split_kernel(source, walkers, first, second, order, picked, semaphores):
+def split_kernel(source, walkers, *refs):
+    targets, (order, picked, semaphores) = refs[:4], refs[4:]
     per_group = walkers.shape[0]
     half = per_group // 2
+    share = half // 2
     group = lax.axis_index("walk")
     b = lax.rem(lax.axis_index("chol"), 2)
     stayed, arrived, sent = jnp.int32(0), jnp.int32(0), jnp.int32(0)
     for slot in range(per_group):
         local = source[group * per_group + slot] - group * per_group
         stays = ((local >= 0) & (local < per_group)).astype(jnp.int32)
-        at = jnp.where(stays == 1, jnp.minimum(stayed, half - 1), per_group)
-        picked[at] = local
-        at = jnp.where(stays == 1, stayed, half + arrived)
-        order[jnp.minimum(at, per_group - 1)] = jnp.int32(slot)
+        picked[jnp.where(stays == 1, jnp.minimum(stayed, half - 1), per_group)] = local
+        rank = jnp.minimum(jnp.where(stays == 1, stayed, arrived), half - 1)
+        core = rank // share
+        order[core * half + (1 - stays) * share + rank - core * share] = jnp.int32(slot)
         stayed, arrived = stayed + stays, arrived + 1 - stays
         local = source[(1 - group) * per_group + slot] - group * per_group
         goes = ((local >= 0) & (local < per_group)).astype(jnp.int32)
-        at = jnp.where(goes == 1, half + jnp.minimum(sent, half - 1), per_group)
-        picked[at] = local
+        picked[jnp.where(goes == 1, half + jnp.minimum(sent, half - 1), per_group)] = local
         sent = sent + goes
+    offsets = (b * share, (1 - b) * share, half + b * share, half + (1 - b) * share)
     copies = []
-    for target, offset in ((second, (1 - b) * half), (first, b * half)):
-        for walker in range(half):
+    for target, offset in reversed(list(zip(targets, offsets))):
+        for walker in range(share):
             copies.append(
                 pltpu.make_async_copy(
                     walkers.at[picked[offset + walker]],
@@ -410,12 +428,12 @@
 
 def split_walkers(walkers, source):
     per_group, rows, electrons = walkers.shape
-    half = jax.ShapeDtypeStruct((per_group // 2, rows, electrons), walkers.dtype)
+    share = jax.ShapeDtypeStruct((per_group // 4, rows, electrons), walkers.dtype)
     return pl.pallas_call(
         split_kernel,
-        out_shape=[half, half, jax.ShapeDtypeStruct((per_group,), jnp.int32)],
-        in_specs=[pl.BlockSpec(memory_space=pltpu.SMEM), pl.BlockSpec(memory_space=pltpu.HBM)],
-        out_specs=[pl.BlockSpec(memory_space=pl.ANY)] * 2
+        out_shape=[share] * 4 + [jax.ShapeDtypeStruct((per_group,), jnp.int32)],
+        in_specs=[pl.BlockSpec(memory_space=pltpu.SMEM), pl.BlockSpec(memory_space=pl.ANY)],
+        out_specs=[pl.BlockSpec(memory_space=pl.ANY)] * 4
         + [pl.BlockSpec(memory_space=pltpu.SMEM)],
         scratch_shapes=[
             pltpu.SMEM((per_group + 1,), jnp.int32),
@@ -431,24 +449,18 @@
     return jnp.sum(jnp.where(before & flags[..., None, :], 1, 0), axis=-1)
 
 
-def migrate(layout, walkers, source, trial):
+def migrate(layout, walkers, source):
     per_group = walkers.shape[0]
     half = per_group // 2
     group = lax.axis_index("walk")
-    if layout.walk == 2:
-        first, second, order = split_walkers(walkers, source)
-        first, second, trial = lax.optimization_barrier((first, second, trial))
-        near, cross = [], []
-        for index in range(2 * layout.chol):
-            across = (index + layout.chol) % (2 * layout.chol)
-            if index % 2 == 0:
-                near.append((index, index))
-                cross.append((index, across + 1))
-            else:
-                near.append((index, across))
-                cross.append((index, index - 1))
+    if layout.walk == 2 and half % 2 == 0:
+        stay, stay_sent, near, cross, order = split_walkers(walkers, source)
+        count = 2 * layout.chol
+        across = [(index + layout.chol) % count for index in range(count)]
         axes = ("walk", "chol")
-        return lax.ppermute(first, axes, near), lax.ppermute(second, axes, cross), order, trial
+        near = lax.ppermute(near, axes, list(enumerate(across)))
+        cross = lax.ppermute(cross, axes, [(i, j ^ 1) for i, j in enumerate(across)])
+        return [(stay, layout.shift(stay_sent, db=1)), (near, cross)], order
     table = source.reshape(layout.walk, per_group)
     incoming = lax.dynamic_index_in_dim(table, group, 0, keepdims=False)
     incoming_groups = incoming // per_group
@@ -472,41 +484,44 @@
     b = lax.axis_index("chol") % 2
     mine = lax.dynamic_slice_in_dim(migrated, b * half, half, 0)
     theirs = lax.dynamic_slice_in_dim(migrated, (1 - b) * half, half, 0)
-    return mine, layout.shift(theirs, db=1), slots.astype(jnp.int32), trial
+    theirs = layout.shift(theirs, db=1)
+    share = half // 2
+    shares = [(mine[:share], theirs[:share]), (mine[share:], theirs[share:])]
+    return shares, slots.astype(jnp.int32)
 
 
 def shards(layout, walkers, trial, cholesky, rotated, fields, source):
     half = walkers.shape[0] // 2
-    sizes = (half // 2, half - half // 2)
     b = lax.axis_index("chol") % 2
-
-    own, other, order, trial = migrate(layout, walkers, source, trial)
-    pairs = [jnp.stack([trial, layout.shift(trial, dy=1)])]
-    pairs.append(layout.shift(pairs[0], dz=1))
-    own, other, pairs = lax.optimization_barrier((own, other, pairs))
-    while len(pairs) < layout.z:
-        pairs.append(layout.shift(pairs[-1], dz=1))
-    chunk = jnp.stack([jnp.where(b == 0, own, other), jnp.where(b == 0, other, own)], axis=1)
-    chunks = [chunk[: sizes[0]], chunk[sizes[0] :]]
+    shares, order = migrate(layout, walkers, source)
+    chunks = [
+        jnp.stack([jnp.where(b == 0, own, other), jnp.where(b == 0, other, own)])
+        for own, other in shares
+    ]
     streams = [Stream(layout, chunk) for chunk in chunks]
+    pairs = CrossFirst(layout, trial)
+    rot_theirs = layout.shift(rotated, db=1)
     for stage in range(layout.z):
-        if stage == 0:
-            pairs[:3] = streams[0].advance(pairs[:3])
-            pairs[3:] = streams[1].advance(pairs[3:])
-            planes = jnp.stack(pairs)
-            planes_theirs = layout.shift(planes, db=1)
-            rot_theirs = layout.shift(rotated, db=1)
-        elif stage == 1:
-            streams[0].advance()
-            planes_theirs, rot_theirs = streams[1].advance((planes_theirs, rot_theirs))
+        last = stage == layout.z - 1
+        if stage < 2:
+            pairs.advance()
+            streams[0].advance(pairs.ring[-1:])
+            if stage == 1:
+                while len(pairs.ring) < layout.z:
+                    pairs.advance()
+            else:
+                pairs.advance()
+            streams[1].advance(pairs.ring[-1:])
+            if stage == 1:
+                planes = jnp.stack(pairs.ring)
+                planes_theirs = layout.shift(planes, db=1)
+        elif stage == 2:
+            planes_theirs, rot_theirs = streams[0].advance((planes_theirs, rot_theirs))
             turned = transposed(layout, planes, planes_theirs)
-        elif stage == 2:
-            (turned,) = streams[0].advance((turned,))
-            streams[1].advance()
+            (turned,) = streams[1].advance((turned,))
         else:
             for stream in streams:
                 stream.advance()
-
     fulls, inverses = zip(*[inverses_of(layout, turned, stream) for stream in streams])
     total = bias_of(chunks, inverses, rotated, rot_theirs)
     parts = [total] + [layout.shift(total, dz=dz) for dz in range(1, layout.z)]
@@ -515,19 +530,16 @@
         parts = [parts[at] + parts[at + far] for at in range(far)]
     parts = [parts[0]] + [layout.shift(parts[0], dy=dy, db=db) for dy, db in ((1, 0), (0, 1), (1, 1))]
     force_bias, weights = weights_of(order, fields, parts)
-    kept, received = [], []
-    for part in range(2):
-        mine, sent = potential_of(weights, cholesky, part, 2)
-        kept.append(mine)
-        received.append(layout.shift(sent, db=1))
-
-    rounded, base = first_of(kept, fulls, 0)
+    kept, *sent = potential_of(weights, cholesky)
+    received = [layout.shift(part, db=1) for part in sent]
+
+    rounded, base = first_of([kept], fulls, 0)
     rounded_theirs, base_theirs = first_of(received, fulls, 1)
-    streams = [Stream(layout, rounded), Stream(layout, rounded_theirs)]
+    streams = [Stream(layout, rounded), Stream(layout, rounded_theirs, last_along_z=True)]
     for _ in range(layout.z):
         for stream in streams:
             stream.advance()
-    mine, sent = second_of(layout, kept, received, (base, base_theirs), streams)
+    mine, sent = second_of(layout, (kept, *received), (base, base_theirs), streams)
     return place(order, mine, layout.shift(sent, db=1)), force_bias
 
 

time: 159 us -> 148 us (0.931)
  starting transfers between devices: 33.9 us -> 26 us
  Pallas kernels: 24.1 us -> 16.5 us
  waiting for transfers between devices: 97.5 us -> 102 us
    ppermute x43 -> x44, starting transfers between devices: 30.4 us -> 24.3 us  [shift(): return lax.ppermute(array, 'chol', pairs)]
    pallas_call x4 -> x3, Pallas kernels: 11.4 us -> 5.9 us  [the longest x1 2.36 us: potential_of(): pl.pallas_call(potential_kernel, out_shape=[kept, sent, sent], in_specs=v...]
    ppermute x43 -> x44, waiting for transfers between devices: 97.4 us -> 102 us  [shift(): return lax.ppermute(array, 'chol', pairs)]
    pallas_call x2, Pallas kernels: 6.58 us -> 4.45 us  [inverses_of(): pl.pallas_call(functools.partial(inverse_kernel, layout, places), out_sha...]
    ppermute x2, starting transfers between devices: 3.51 us -> 1.7 us  [the longest x1 1.49 us: migrate(): near = lax.ppermute(near, axes, list(enumerate(across)))]
  transfers between devices with their start and end apart: 45 -> 46, of which waited for: 36 -> 31; matrix products, arithmetic and copies ran while one was open for 1% -> 1% of each run, Pallas kernels for 4% -> 4%
where the time goes in v6:
time: 148 us
  waiting for transfers between devices  102 us (69%)
  starting transfers between devices  26 us (18%)
  Pallas kernels  16.5 us (11%)
  local copies, waits for them, and re-layouts  1.71 us (1%)
    ppermute x44, waiting for transfers between devices, shift(): return lax.ppermute(array, 'chol', pairs)  102 us
    ppermute x44, starting transfers between devices, shift(): return lax.ppermute(array, 'chol', pairs)  24.3 us
    pallas_call x2, Pallas kernels, inverses_of(): pl.pallas_call(functools.partial(inverse_kernel, layout, places), out_sha...  4.45 us
  transfers between devices with their start and end apart: 46, of which 31 were waited for; matrix products, arithmetic and copies ran while one was open for 1% of the time, Pallas kernels for 4%

profile of v6, /device:TPU:0, one launch (start us, length us, event | category | flops | bytes accessed | tf_op | source)
XLA Modules:
  0.0 147.9 jit_solution(3649351743149691525)
XLA Ops:
  1.1 2.6 %collective-permute-start = (bf16[128,256]{1,0:T(8,128)(2,1)}, bf16[128,256]{1,0:T(8,128)(2,1)S(1)}, u32[]{:S(2)}, u32[]{:S(2)}) collective-permute-start(bf16[128,256]{1,0:T(8,128)(2,1)} %param.7), channel_id=1, source_target_pairs={{0,2},{1,3},{2,0},{3,1},{4,6},{5,7},{6,4},{7,5},{8,10},{9,11},{10,... | collective-permute-start | bytes 196616 | tf_op jit(solution)/shard_map/ppermute | solution.py:40
  3.7 1.0 copy-done.2
  4.8 0.7 copy-done.4
  5.4 2.0 %shard_map.77 = (bf16[2,128,256]{2,1,0:T(8,128)(2,1)S(1)}, bf16[2,128,256]{2,1,0:T(8,128)(2,1)S(1)}, bf16[2,128,256]{2,1,0:T(8,128)(2,1)S(1)}, bf16[2,128,256]{2,1,0:T(8,128)(2,1)S(1)}, s32[8]{0:T(128)S(1)}) custom-call(s32[16]{0:T(128)S(1)} %copy-done.4, bf16[8,128,256]{2,1,0:T(8,128)(2,1)S(1)} %copy-done.2), custom_call_target="tpu_custom_call" | custom-call | tf_op jit(solution)/shard_map/pallas_call | solution.py:432
  7.7 1.5 %collective-permute-start.13 = (bf16[2,128,256]{2,1,0:T(8,128)(2,1)S(1)}, bf16[2,128,256]{2,1,0:T(8,128)(2,1)S(1)}, u32[]{:S(2)}, u32[]{:S(2)}) collective-permute-start(bf16[2,128,256]{2,1,0:T(8,128)(2,1)S(1)} %get-tuple-element.55), channel_id=1, source_target_pairs={{0,16},{1,17},{2,18},{3,19},{4,20},{5,21},{6,22},{7,23},{8,24},{9,... | collective-permute-start | bytes 393224 | tf_op jit(solution)/shard_map/ppermute | solution.py:461
  9.4 0.9 fusion
  10.3 1.6 %collective-permute-start.1 = (bf16[2,128,256]{2,1,0:T(8,128)(2,1)S(1)}, bf16[2,128,256]{2,1,0:T(8,128)(2,1)S(1)}, u32[]{:S(2)}, u32[]{:S(2)}) collective-permute-start(bf16[2,128,256]{2,1,0:T(8,128)(2,1)S(1)} %get-tuple-element.101), channel_id=1, source_target_pairs={{0,4},{1,5},{2,6},{3,7},{4,8},{5,9},{6,10},{7,11},{8,12},{9,13},{1... | collective-permute-start | bytes 393224 | tf_op jit(solution)/shard_map/ppermute | solution.py:40
  12.0 0.6 collective-permute-start.7
  12.6 5.5 %collective-permute-done.1 = bf16[2,128,256]{2,1,0:T(8,128)(2,1)S(1)} collective-permute-done((bf16[2,128,256]{2,1,0:T(8,128)(2,1)S(1)}, bf16[2,128,256]{2,1,0:T(8,128)(2,1)S(1)}, u32[]{:S(2)}, u32[]{:S(2)}) %collective-permute-start.1) | collective-permute-done | bytes 131104 | tf_op jit(solution)/shard_map/ppermute | solution.py:40
  18.1 1.3 collective-permute-start.2
  19.4 0.6 collective-permute-start.15
  20.0 10.6 %collective-permute-done.2 = bf16[2,128,256]{2,1,0:T(8,128)(2,1)S(1)} collective-permute-done((bf16[2,128,256]{2,1,0:T(8,128)(2,1)S(1)}, bf16[2,128,256]{2,1,0:T(8,128)(2,1)S(1)}, u32[]{:S(2)}, u32[]{:S(2)}) %collective-permute-start.2) | collective-permute-done | bytes 131104 | tf_op jit(solution)/shard_map/ppermute | solution.py:40
  30.6 0.7 collective-permute-start.9
  31.3 0.8 collective-permute-start.10
  32.1 9.5 %collective-permute-done.16.refs_1_ = bf16[2,2,128,256]{3,2,1,0:T(8,128)(2,1)S(1)} collective-permute-done((bf16[2,2,128,256]{3,2,1,0:T(8,128)(2,1)S(1)}, bf16[2,2,128,256]{3,2,1,0:T(8,128)(2,1)S(1)}, u32[]{:S(2)}, u32[]{:S(2)}) %collective-permute-start.16) | collective-permute-done | bytes 262176 | tf_op jit(solution)/shard_map/ppermute | solution.py:40
  41.6 0.6 collective-permute-start.17
  42.3 2.2 %collective-permute-done.3 = bf16[2,128,256]{2,1,0:T(8,128)(2,1)S(1)} collective-permute-done((bf16[2,128,256]{2,1,0:T(8,128)(2,1)S(1)}, bf16[2,128,256]{2,1,0:T(8,128)(2,1)S(1)}, u32[]{:S(2)}, u32[]{:S(2)}) %collective-permute-start.3) | collective-permute-done | bytes 131104 | tf_op jit(solution)/shard_map/ppermute | solution.py:40
  44.7 3.2 %collective-permute-done.10.refs_2_ = bf16[2,2,128,256]{3,2,1,0:T(8,128)(2,1)S(1)} collective-permute-done((bf16[2,2,128,256]{3,2,1,0:T(8,128)(2,1)S(1)}, bf16[2,2,128,256]{3,2,1,0:T(8,128)(2,1)S(1)}, u32[]{:S(2)}, u32[]{:S(2)}) %collective-permute-start.10) | collective-permute-done | bytes 262176 | tf_op jit(solution)/shard_map/ppermute | solution.py:40
  47.9 0.8 collective-permute-start.11
  48.6 6.9 %collective-permute-done.18.refs_2_ = bf16[2,2,128,256]{3,2,1,0:T(8,128)(2,1)S(1)} collective-permute-done((bf16[2,2,128,256]{3,2,1,0:T(8,128)(2,1)S(1)}, bf16[2,2,128,256]{3,2,1,0:T(8,128)(2,1)S(1)}, u32[]{:S(2)}, u32[]{:S(2)}) %collective-permute-start.18) | collective-permute-done | bytes 262176 | tf_op jit(solution)/shard_map/ppermute | solution.py:40
  55.6 0.6 collective-permute-start.19
  56.2 5.0 %collective-permute-done.12.refs_3_ = bf16[2,2,128,256]{3,2,1,0:T(8,128)(2,1)S(1)} collective-permute-done((bf16[2,2,128,256]{3,2,1,0:T(8,128)(2,1)S(1)}, bf16[2,2,128,256]{3,2,1,0:T(8,128)(2,1)S(1)}, u32[]{:S(2)}, u32[]{:S(2)}) %collective-permute-start.12) | collective-permute-done | bytes 262176 | tf_op jit(solution)/shard_map/ppermute | solution.py:40
  62.2 0.8 collective-permute-done.19.refs_6_
  63.0 3.4 %collective-permute-done.20.refs_3_ = bf16[2,2,128,256]{3,2,1,0:T(8,128)(2,1)S(1)} collective-permute-done((bf16[2,2,128,256]{3,2,1,0:T(8,128)(2,1)S(1)}, bf16[2,2,128,256]{3,2,1,0:T(8,128)(2,1)S(1)}, u32[]{:S(2)}, u32[]{:S(2)}) %collective-permute-start.20) | collective-permute-done | bytes 262176 | tf_op jit(solution)/shard_map/ppermute | solution.py:40
  66.3 0.6 collective-permute-start.22
  67.0 2.0 %collective-permute-done.21.refs_7_ = bf16[2,2,128,256]{3,2,1,0:T(8,128)(2,1)S(1)} collective-permute-done((bf16[2,2,128,256]{3,2,1,0:T(8,128)(2,1)S(1)}, bf16[2,2,128,256]{3,2,1,0:T(8,128)(2,1)S(1)}, u32[]{:S(2)}, u32[]{:S(2)}) %collective-permute-start.21) | collective-permute-done | bytes 262176 | tf_op jit(solution)/shard_map/ppermute | solution.py:40
  69.0 2.2 %shard_map.79 = (bf16[2,8,2,128,256]{4,3,2,1,0:T(8,128)(2,1)S(1)}, bf16[2,256,256]{2,1,0:T(8,128)(2,1)S(1)}) custom-call(bf16[256,2048]{1,0:T(8,128)(2,1)S(1)} %shard_map.78.trial, bf16[2,2,128,256]{3,2,1,0:T(8,128)(2,1)S(1)} %pad_maximum_fusion.1.refs_0_, bf16[2,2,128,256]{3,2,1,0:T(8,128)(2,1)S(1)} %collective-permute-done.8.refs_1_, ...), custom_call_target="tpu_custom_call" | custom-call | flops 1342177280 | bytes 6291456 | tf_op jit(solution)/shard_map/pallas_call | solution.py:153
  71.2 3.0 %collective-permute-done.22.refs_7_ = bf16[2,2,128,256]{3,2,1,0:T(8,128)(2,1)S(1)} collective-permute-done((bf16[2,2,128,256]{3,2,1,0:T(8,128)(2,1)S(1)}, bf16[2,2,128,256]{3,2,1,0:T(8,128)(2,1)S(1)}, u32[]{:S(2)}, u32[]{:S(2)}) %collective-permute-start.22) | collective-permute-done | bytes 262176 | tf_op jit(solution)/shard_map/ppermute | solution.py:40
  74.2 2.2 %shard_map.80 = (bf16[2,8,2,128,256]{4,3,2,1,0:T(8,128)(2,1)S(1)}, bf16[2,256,256]{2,1,0:T(8,128)(2,1)S(1)}) custom-call(bf16[256,2048]{1,0:T(8,128)(2,1)S(1)} %shard_map.78.trial, bf16[2,2,128,256]{3,2,1,0:T(8,128)(2,1)S(1)} %pad_maximum_fusion.2.refs_0_.refs_1_, bf16[2,2,128,256]{3,2,1,0:T(8,128)(2,1)S(1)} %collective-permute-done.16.refs_1_, ...), custom_call_target="tpu_custom_call" | custom-call | flops 1342177280 | bytes 6291456 | tf_op jit(solution)/shard_map/pallas_call | solution.py:153
  76.4 1.7 %shard_map.81 = f32[4,32]{1,0:T(4,128)S(1)} custom-call(bf16[32,128,256]{2,1,0:T(8,128)(2,1)S(1)} %copy-done.1, bf16[32,128,256]{2,1,0:T(8,128)(2,1)S(1)} %collective-permute-done.5.rot_theirs, bf16[2,2,128,256]{3,2,1,0:T(8,128)(2,1)S(1)} %pad_maximum_fusion.1.refs_0_, bf16[2,2,128,256]{3,2,1,0:T(8,128)(2,1)S(1)} %pad_maximum_fusion.2.refs_0_.refs_1_, ...), custom_call_target="tpu_custom_call" | custom-call | flops 402653184 | bytes 4718592 | tf_op jit(solution)/shard_map/pallas_call | solution.py:211
  78.2 3.8 %collective-permute-start.25 = (f32[4,32]{1,0:T(4,128)S(1)}, f32[4,32]{1,0:T(4,128)S(1)}, u32[]{:S(2)}, u32[]{:S(2)}) collective-permute-start(f32[4,32]{1,0:T(4,128)S(1)} %shard_map.81), channel_id=1, source_target_pairs={{0,12},{1,13},{2,14},{3,15},{4,0},{5,1},{6,2},{7,3},{8,4},{9,5},{1... | collective-permute-start | bytes 1544 | tf_op jit(solution)/shard_map/ppermute | solution.py:40
  82.0 1.6 %collective-permute-done.24 = f32[4,32]{1,0:T(4,128)S(1)} collective-permute-done((f32[4,32]{1,0:T(4,128)S(1)}, f32[4,32]{1,0:T(4,128)S(1)}, u32[]{:S(2)}, u32[]{:S(2)}) %collective-permute-start.24) | collective-permute-done | bytes 544 | tf_op jit(solution)/shard_map/ppermute | solution.py:40
  83.6 2.9 %collective-permute-done.23 = f32[4,32]{1,0:T(4,128)S(1)} collective-permute-done((f32[4,32]{1,0:T(4,128)S(1)}, f32[4,32]{1,0:T(4,128)S(1)}, u32[]{:S(2)}, u32[]{:S(2)}) %collective-permute-start.23) | collective-permute-done | bytes 544 | tf_op jit(solution)/shard_map/ppermute | solution.py:40
  86.5 0.6 collective-permute-start.26
  87.1 1.5 %collective-permute-start.28 = (f32[4,32]{1,0:T(4,128)S(1)}, f32[4,32]{1,0:T(4,128)S(1)}, u32[]{:S(2)}, u32[]{:S(2)}) collective-permute-start(f32[4,32]{1,0:T(4,128)S(1)} %add_add_fusion.mine), channel_id=1, source_target_pairs={{0,3},{1,2},{2,1},{3,0},{4,7},{5,6},{6,5},{7,4},{8,11},{9,10},{10,... | collective-permute-start | bytes 1544 | tf_op jit(solution)/shard_map/ppermute | solution.py:40
  88.6 1.4 collective-permute-done.26.mine_across
  90.1 1.2 shard_map.82
  91.3 2.4 %shard_map.83 = (bf16[4,128,2048]{2,1,0:T(8,128)(2,1)S(1)}, bf16[4,64,2048]{2,1,0:T(8,128)(2,1)S(1)}, bf16[4,64,2048]{2,1,0:T(8,128)(2,1)S(1)}) custom-call(bf16[128,512]{1,0:T(8,128)(2,1)S(1)} %get-tuple-element.71.weights, bf16[32,128,2048]{2,1,0:T(8,128)(2,1)S(1)} %copy-done), custom_call_target="tpu_custom_call" | custom-call | tf_op jit(solution)/shard_map/pallas_call | solution.py:290
  93.7 0.6 collective-permute-start.29
  94.3 0.8 shard_map.84
  95.1 1.5 collective-permute-start.31
  96.6 1.5 collective-permute-done.30.refs_1_.refs_2_
  98.0 0.8 shard_map.85
  98.8 1.5 collective-permute-start.38
  100.3 4.0 %collective-permute-done.31.refs_9_ = bf16[4,128,256]{2,1,0:T(8,128)(2,1)S(1)} collective-permute-done((bf16[4,128,256]{2,1,0:T(8,128)(2,1)S(1)}, bf16[4,128,256]{2,1,0:T(8,128)(2,1)S(1)}, u32[]{:S(2)}, u32[]{:S(2)}) %collective-permute-start.31) | collective-permute-done | bytes 262176 | tf_op jit(solution)/shard_map/ppermute | solution.py:40
  104.3 3.2 %collective-permute-done.32.refs_6_ = bf16[4,128,256]{2,1,0:T(8,128)(2,1)S(1)} collective-permute-done((bf16[4,128,256]{2,1,0:T(8,128)(2,1)S(1)}, bf16[4,128,256]{2,1,0:T(8,128)(2,1)S(1)}, u32[]{:S(2)}, u32[]{:S(2)}) %collective-permute-start.32) | collective-permute-done | bytes 262176 | tf_op jit(solution)/shard_map/ppermute | solution.py:40
  107.5 0.6 collective-permute-start.33
  108.1 1.7 %collective-permute-done.38.refs_17_ = bf16[4,128,256]{2,1,0:T(8,128)(2,1)S(1)} collective-permute-done((bf16[4,128,256]{2,1,0:T(8,128)(2,1)S(1)}, bf16[4,128,256]{2,1,0:T(8,128)(2,1)S(1)}, u32[]{:S(2)}, u32[]{:S(2)}) %collective-permute-start.38) | collective-permute-done | bytes 262176 | tf_op jit(solution)/shard_map/ppermute | solution.py:40
  109.9 3.2 %collective-permute-done.39.refs_14_ = bf16[4,128,256]{2,1,0:T(8,128)(2,1)S(1)} collective-permute-done((bf16[4,128,256]{2,1,0:T(8,128)(2,1)S(1)}, bf16[4,128,256]{2,1,0:T(8,128)(2,1)S(1)}, u32[]{:S(2)}, u32[]{:S(2)}) %collective-permute-start.39) | collective-permute-done | bytes 262176 | tf_op jit(solution)/shard_map/ppermute | solution.py:40
  113.1 0.6 collective-permute-start.40
  113.7 2.1 %collective-permute-done.33.refs_10_ = bf16[4,128,256]{2,1,0:T(8,128)(2,1)S(1)} collective-permute-done((bf16[4,128,256]{2,1,0:T(8,128)(2,1)S(1)}, bf16[4,128,256]{2,1,0:T(8,128)(2,1)S(1)}, u32[]{:S(2)}, u32[]{:S(2)}) %collective-permute-start.33) | collective-permute-done | bytes 262176 | tf_op jit(solution)/shard_map/ppermute | solution.py:40
  115.8 3.4 %collective-permute-done.34.refs_7_ = bf16[4,128,256]{2,1,0:T(8,128)(2,1)S(1)} collective-permute-done((bf16[4,128,256]{2,1,0:T(8,128)(2,1)S(1)}, bf16[4,128,256]{2,1,0:T(8,128)(2,1)S(1)}, u32[]{:S(2)}, u32[]{:S(2)}) %collective-permute-start.34) | collective-permute-done | bytes 262176 | tf_op jit(solution)/shard_map/ppermute | solution.py:40
  119.3 2.5 %collective-permute-done.40.refs_18_ = bf16[4,128,256]{2,1,0:T(8,128)(2,1)S(1)} collective-permute-done((bf16[4,128,256]{2,1,0:T(8,128)(2,1)S(1)}, bf16[4,128,256]{2,1,0:T(8,128)(2,1)S(1)}, u32[]{:S(2)}, u32[]{:S(2)}) %collective-permute-start.40) | collective-permute-done | bytes 262176 | tf_op jit(solution)/shard_map/ppermute | solution.py:40
  121.8 3.0 %collective-permute-done.41.refs_15_ = bf16[4,128,256]{2,1,0:T(8,128)(2,1)S(1)} collective-permute-done((bf16[4,128,256]{2,1,0:T(8,128)(2,1)S(1)}, bf16[4,128,256]{2,1,0:T(8,128)(2,1)S(1)}, u32[]{:S(2)}, u32[]{:S(2)}) %collective-permute-start.41) | collective-permute-done | bytes 262176 | tf_op jit(solution)/shard_map/ppermute | solution.py:40
  124.8 0.6 collective-permute-start.42
  125.4 2.1 %collective-permute-done.35.refs_11_ = bf16[4,128,256]{2,1,0:T(8,128)(2,1)S(1)} collective-permute-done((bf16[4,128,256]{2,1,0:T(8,128)(2,1)S(1)}, bf16[4,128,256]{2,1,0:T(8,128)(2,1)S(1)}, u32[]{:S(2)}, u32[]{:S(2)}) %collective-permute-start.35) | collective-permute-done | bytes 262176 | tf_op jit(solution)/shard_map/ppermute | solution.py:40
  127.4 3.0 %collective-permute-done.36.refs_8_ = bf16[4,128,256]{2,1,0:T(8,128)(2,1)S(1)} collective-permute-done((bf16[4,128,256]{2,1,0:T(8,128)(2,1)S(1)}, bf16[4,128,256]{2,1,0:T(8,128)(2,1)S(1)}, u32[]{:S(2)}, u32[]{:S(2)}) %collective-permute-start.36) | collective-permute-done | bytes 262176 | tf_op jit(solution)/shard_map/ppermute | solution.py:40
  131.0 2.1 %collective-permute-done.42.refs_19_ = bf16[4,128,256]{2,1,0:T(8,128)(2,1)S(1)} collective-permute-done((bf16[4,128,256]{2,1,0:T(8,128)(2,1)S(1)}, bf16[4,128,256]{2,1,0:T(8,128)(2,1)S(1)}, u32[]{:S(2)}, u32[]{:S(2)}) %collective-permute-start.42) | collective-permute-done | bytes 262176 | tf_op jit(solution)/shard_map/ppermute | solution.py:40
  133.0 1.8 %collective-permute-done.43.refs_16_ = bf16[4,128,256]{2,1,0:T(8,128)(2,1)S(1)} collective-permute-done((bf16[4,128,256]{2,1,0:T(8,128)(2,1)S(1)}, bf16[4,128,256]{2,1,0:T(8,128)(2,1)S(1)}, u32[]{:S(2)}, u32[]{:S(2)}) %collective-permute-start.43) | collective-permute-done | bytes 262176 | tf_op jit(solution)/shard_map/ppermute | solution.py:40
  134.8 2.7 %collective-permute-done.37.refs_12_ = bf16[4,128,256]{2,1,0:T(8,128)(2,1)S(1)} collective-permute-done((bf16[4,128,256]{2,1,0:T(8,128)(2,1)S(1)}, bf16[4,128,256]{2,1,0:T(8,128)(2,1)S(1)}, u32[]{:S(2)}, u32[]{:S(2)}) %collective-permute-start.37) | collective-permute-done | bytes 262176 | tf_op jit(solution)/shard_map/ppermute | solution.py:40
  137.5 5.8 %collective-permute-done.44.refs_20_ = bf16[4,128,256]{2,1,0:T(8,128)(2,1)S(1)} collective-permute-done((bf16[4,128,256]{2,1,0:T(8,128)(2,1)S(1)}, bf16[4,128,256]{2,1,0:T(8,128)(2,1)S(1)}, u32[]{:S(2)}, u32[]{:S(2)}) %collective-permute-start.44) | collective-permute-done | bytes 262176 | tf_op jit(solution)/shard_map/ppermute | solution.py:40
  143.4 1.5 %shard_map.86 = (bf16[4,128,256]{2,1,0:T(8,128)(2,1)S(1)}, bf16[4,128,256]{2,1,0:T(8,128)(2,1)S(1)}) custom-call(bf16[4,128,2048]{2,1,0:T(8,128)(2,1)S(1)} %get-tuple-element.72.refs_0_, bf16[4,64,2048]{2,1,0:T(8,128)(2,1)S(1)} %collective-permute-done.29.refs_0_.refs_1_, bf16[4,64,2048]{2,1,0:T(8,128)(2,1)S(1)} %collective-permute-done.30.refs_1_.refs_2_, ...), custom_call_target="tpu_custom_call" | custom-call | flops 1073741824 | bytes 8388608 | tf_op jit(solution)/shard_map/pallas_call | solution.py:358
  144.9 1.5 %collective-permute-done.45.theirs = bf16[4,128,256]{2,1,0:T(8,128)(2,1)S(1)} collective-permute-done((bf16[4,128,256]{2,1,0:T(8,128)(2,1)S(1)}, bf16[4,128,256]{2,1,0:T(8,128)(2,1)S(1)}, u32[]{:S(2)}, u32[]{:S(2)}) %collective-permute-start.45) | collective-permute-done | bytes 262176 | tf_op jit(solution)/shard_map/ppermute | solution.py:40
  146.5 1.4 shard_map.87
  (56 shorter events, 3.2 us)
Async XLA Ops:
  0.6 60.6 %collective-permute-start.5 = (bf16[32,128,256]{2,1,0:T(8,128)(2,1)}, bf16[32,128,256]{2,1,0:T(8,128)(2,1)S(1)}, u32[]{:S(2)}, u32[]{:S(2)}) collective-permute-start(bf16[32,128,256]{2,1,0:T(8,128)(2,1)} %rot_mine.1), channel_id=1, source_target_pairs={{0,1},{1,0},{2,3},{3,2},{4,5},{5,4},{6,7},{7,6},{8,9},{9,8},{10,11... | collective-permute-start | bytes 6291464 | tf_op jit(solution)/shard_map/ppermute | solution.py:40
  1.1 8.3 %collective-permute-start = (bf16[128,256]{1,0:T(8,128)(2,1)}, bf16[128,256]{1,0:T(8,128)(2,1)S(1)}, u32[]{:S(2)}, u32[]{:S(2)}) collective-permute-start(bf16[128,256]{1,0:T(8,128)(2,1)} %param.7), channel_id=1, source_target_pairs={{0,2},{1,3},{2,0},{3,1},{4,6},{5,7},{6,4},{7,5},{8,10},{9,11},{10,... | collective-permute-start | bytes 196616 | tf_op jit(solution)/shard_map/ppermute | solution.py:40
  3.7 1.0 copy-start.2
  4.8 0.7 copy-start.4
  7.5 4.4 %collective-permute-start.6 = (bf16[2,128,256]{2,1,0:T(8,128)(2,1)S(1)}, bf16[2,128,256]{2,1,0:T(8,128)(2,1)S(1)}, u32[]{:S(2)}, u32[]{:S(2)}) collective-permute-start(bf16[2,128,256]{2,1,0:T(8,128)(2,1)S(1)} %get-tuple-element.51), channel_id=1, source_target_pairs={{0,1},{1,0},{2,3},{3,2},{4,5},{5,4},{6,7},{7,6},{8,9},{9,8},{10,11... | collective-permute-start | bytes 393224 | tf_op jit(solution)/shard_map/ppermute | solution.py:40
  7.7 10.3 %collective-permute-start.13 = (bf16[2,128,256]{2,1,0:T(8,128)(2,1)S(1)}, bf16[2,128,256]{2,1,0:T(8,128)(2,1)S(1)}, u32[]{:S(2)}, u32[]{:S(2)}) collective-permute-start(bf16[2,128,256]{2,1,0:T(8,128)(2,1)S(1)} %get-tuple-element.55), channel_id=1, source_target_pairs={{0,16},{1,17},{2,18},{3,19},{4,20},{5,21},{6,22},{7,23},{8,24},{9,... | collective-permute-start | bytes 393224 | tf_op jit(solution)/shard_map/ppermute | solution.py:461
  9.2 10.1 %collective-permute-start.14 = (bf16[2,128,256]{2,1,0:T(8,128)(2,1)S(1)}, bf16[2,128,256]{2,1,0:T(8,128)(2,1)S(1)}, u32[]{:S(2)}, u32[]{:S(2)}) collective-permute-start(bf16[2,128,256]{2,1,0:T(8,128)(2,1)S(1)} %get-tuple-element.56), channel_id=1, source_target_pairs={{0,17},{1,16},{2,19},{3,18},{4,21},{5,20},{6,23},{7,22},{8,25},{9,... | collective-permute-start | bytes 393224 | tf_op jit(solution)/shard_map/ppermute | solution.py:462
  10.3 7.8 %collective-permute-start.1 = (bf16[2,128,256]{2,1,0:T(8,128)(2,1)S(1)}, bf16[2,128,256]{2,1,0:T(8,128)(2,1)S(1)}, u32[]{:S(2)}, u32[]{:S(2)}) collective-permute-start(bf16[2,128,256]{2,1,0:T(8,128)(2,1)S(1)} %get-tuple-element.101), channel_id=1, source_target_pairs={{0,4},{1,5},{2,6},{3,7},{4,8},{5,9},{6,10},{7,11},{8,12},{9,13},{1... | collective-permute-start | bytes 393224 | tf_op jit(solution)/shard_map/ppermute | solution.py:40
  12.0 18.6 %collective-permute-start.7 = (bf16[2,2,128,256]{3,2,1,0:T(8,128)(2,1)S(1)}, bf16[2,2,128,256]{3,2,1,0:T(8,128)(2,1)S(1)}, u32[]{:S(2)}, u32[]{:S(2)}) collective-permute-start(bf16[2,2,128,256]{3,2,1,0:T(8,128)(2,1)S(1)} %pad_maximum_fusion.1.refs_0_), channel_id=1, source_target_pairs={{0,2},{1,3},{2,0},{3,1},{4,6},{5,7},{6,4},{7,5},{8,10},{9,11},{10,... | collective-permute-start | bytes 786440 | tf_op jit(solution)/shard_map/ppermute | solution.py:40
  18.0 12.6 %collective-permute-start.8 = (bf16[2,2,128,256]{3,2,1,0:T(8,128)(2,1)S(1)}, bf16[2,2,128,256]{3,2,1,0:T(8,128)(2,1)S(1)}, u32[]{:S(2)}, u32[]{:S(2)}) collective-permute-start(bf16[2,2,128,256]{3,2,1,0:T(8,128)(2,1)S(1)} %pad_maximum_fusion.1.refs_0_), channel_id=1, source_target_pairs={{0,4},{1,5},{2,6},{3,7},{4,8},{5,9},{6,10},{7,11},{8,12},{9,13},{1... | collective-permute-start | bytes 786440 | tf_op jit(solution)/shard_map/ppermute | solution.py:40
  18.1 12.5 %collective-permute-start.2 = (bf16[2,128,256]{2,1,0:T(8,128)(2,1)S(1)}, bf16[2,128,256]{2,1,0:T(8,128)(2,1)S(1)}, u32[]{:S(2)}, u32[]{:S(2)}) collective-permute-start(bf16[2,128,256]{2,1,0:T(8,128)(2,1)S(1)} %collective-permute-done.1), channel_id=1, source_target_pairs={{0,4},{1,5},{2,6},{3,7},{4,8},{5,9},{6,10},{7,11},{8,12},{9,13},{1... | collective-permute-start | bytes 393224 | tf_op jit(solution)/shard_map/ppermute | solution.py:40
  19.4 57.1 %copy-start.1 = (bf16[32,128,256]{2,1,0:T(8,128)(2,1)S(1)}, bf16[32,128,256]{2,1,0:T(8,128)(2,1)}, u32[]{:S(2)}) copy-start(bf16[32,128,256]{2,1,0:T(8,128)(2,1)} %rot_mine.1) | copy-start | bytes 6291460
  19.4 11.9 %collective-permute-start.15 = (bf16[2,2,128,256]{3,2,1,0:T(8,128)(2,1)S(1)}, bf16[2,2,128,256]{3,2,1,0:T(8,128)(2,1)S(1)}, u32[]{:S(2)}, u32[]{:S(2)}) collective-permute-start(bf16[2,2,128,256]{3,2,1,0:T(8,128)(2,1)S(1)} %pad_maximum_fusion.2.refs_0_.refs_1_), channel_id=1, source_target_pairs={{0,2},{1,3},{2,0},{3,1},{4,6},{5,7},{6,4},{7,5},{8,10},{9,11},{10,... | collective-permute-start | bytes 786440 | tf_op jit(solution)/shard_map/ppermute | solution.py:40
  30.6 11.0 %collective-permute-start.16 = (bf16[2,2,128,256]{3,2,1,0:T(8,128)(2,1)S(1)}, bf16[2,2,128,256]{3,2,1,0:T(8,128)(2,1)S(1)}, u32[]{:S(2)}, u32[]{:S(2)}) collective-permute-start(bf16[2,2,128,256]{3,2,1,0:T(8,128)(2,1)S(1)} %pad_maximum_fusion.2.refs_0_.refs_1_), channel_id=1, source_target_pairs={{0,4},{1,5},{2,6},{3,7},{4,8},{5,9},{6,10},{7,11},{8,12},{9,13},{1... | collective-permute-start | bytes 786440 | tf_op jit(solution)/shard_map/ppermute | solution.py:40
  30.6 13.8 %collective-permute-start.3 = (bf16[2,128,256]{2,1,0:T(8,128)(2,1)S(1)}, bf16[2,128,256]{2,1,0:T(8,128)(2,1)S(1)}, u32[]{:S(2)}, u32[]{:S(2)}) collective-permute-start(bf16[2,128,256]{2,1,0:T(8,128)(2,1)S(1)} %collective-permute-done.2), channel_id=1, source_target_pairs={{0,4},{1,5},{2,6},{3,7},{4,8},{5,9},{6,10},{7,11},{8,12},{9,13},{1... | collective-permute-start | bytes 393224 | tf_op jit(solution)/shard_map/ppermute | solution.py:40
  30.6 14.0 %collective-permute-start.9 = (bf16[2,2,128,256]{3,2,1,0:T(8,128)(2,1)S(1)}, bf16[2,2,128,256]{3,2,1,0:T(8,128)(2,1)S(1)}, u32[]{:S(2)}, u32[]{:S(2)}) collective-permute-start(bf16[2,2,128,256]{3,2,1,0:T(8,128)(2,1)S(1)} %collective-permute-done.8.refs_1_), channel_id=1, source_target_pairs={{0,2},{1,3},{2,0},{3,1},{4,6},{5,7},{6,4},{7,5},{8,10},{9,11},{10,... | collective-permute-start | bytes 786440 | tf_op jit(solution)/shard_map/ppermute | solution.py:40
  31.3 16.6 %collective-permute-start.10 = (bf16[2,2,128,256]{3,2,1,0:T(8,128)(2,1)S(1)}, bf16[2,2,128,256]{3,2,1,0:T(8,128)(2,1)S(1)}, u32[]{:S(2)}, u32[]{:S(2)}) collective-permute-start(bf16[2,2,128,256]{3,2,1,0:T(8,128)(2,1)S(1)} %collective-permute-done.8.refs_1_), channel_id=1, source_target_pairs={{0,4},{1,5},{2,6},{3,7},{4,8},{5,9},{6,10},{7,11},{8,12},{9,13},{1... | collective-permute-start | bytes 786440 | tf_op jit(solution)/shard_map/ppermute | solution.py:40
  41.6 7.0 %collective-permute-start.17 = (bf16[2,2,128,256]{3,2,1,0:T(8,128)(2,1)S(1)}, bf16[2,2,128,256]{3,2,1,0:T(8,128)(2,1)S(1)}, u32[]{:S(2)}, u32[]{:S(2)}) collective-permute-start(bf16[2,2,128,256]{3,2,1,0:T(8,128)(2,1)S(1)} %collective-permute-done.16.refs_1_), channel_id=1, source_target_pairs={{0,2},{1,3},{2,0},{3,1},{4,6},{5,7},{6,4},{7,5},{8,10},{9,11},{10,... | collective-permute-start | bytes 786440 | tf_op jit(solution)/shard_map/ppermute | solution.py:40
  44.4 45.7 %copy-start.3 = (f32[8,32]{1,0:T(8,128)S(1)}, f32[8,32]{1,0:T(8,128)}, u32[]{:S(2)}) copy-start(f32[8,32]{1,0:T(8,128)} %fields.1) | copy-start | bytes 3076
  44.5 16.7 %collective-permute-start.4 = (bf16[4,2,128,256]{3,2,1,0:T(8,128)(2,1)S(1)}, bf16[4,2,128,256]{3,2,1,0:T(8,128)(2,1)S(1)}, u32[]{:S(2)}, u32[]{:S(2)}) collective-permute-start(bf16[4,2,128,256]{3,2,1,0:T(8,128)(2,1)S(1)} %pad_maximum_fusion.mine), channel_id=1, source_target_pairs={{0,1},{1,0},{2,3},{3,2},{4,5},{5,4},{6,7},{7,6},{8,9},{9,8},{10,11... | collective-permute-start | bytes 1572872 | tf_op jit(solution)/shard_map/ppermute | solution.py:40
  44.6 11.0 %collective-permute-start.18 = (bf16[2,2,128,256]{3,2,1,0:T(8,128)(2,1)S(1)}, bf16[2,2,128,256]{3,2,1,0:T(8,128)(2,1)S(1)}, u32[]{:S(2)}, u32[]{:S(2)}) collective-permute-start(bf16[2,2,128,256]{3,2,1,0:T(8,128)(2,1)S(1)} %collective-permute-done.16.refs_1_), channel_id=1, source_target_pairs={{0,4},{1,5},{2,6},{3,7},{4,8},{5,9},{6,10},{7,11},{8,12},{9,13},{1... | collective-permute-start | bytes 786440 | tf_op jit(solution)/shard_map/ppermute | solution.py:40
  47.9 8.3 %collective-permute-start.11 = (bf16[2,2,128,256]{3,2,1,0:T(8,128)(2,1)S(1)}, bf16[2,2,128,256]{3,2,1,0:T(8,128)(2,1)S(1)}, u32[]{:S(2)}, u32[]{:S(2)}) collective-permute-start(bf16[2,2,128,256]{3,2,1,0:T(8,128)(2,1)S(1)} %collective-permute-done.10.refs_2_), channel_id=1, source_target_pairs={{0,2},{1,3},{2,0},{3,1},{4,6},{5,7},{6,4},{7,5},{8,10},{9,11},{10,... | collective-permute-start | bytes 786440 | tf_op jit(solution)/shard_map/ppermute | solution.py:40
  48.6 12.6 %collective-permute-start.12 = (bf16[2,2,128,256]{3,2,1,0:T(8,128)(2,1)S(1)}, bf16[2,2,128,256]{3,2,1,0:T(8,128)(2,1)S(1)}, u32[]{:S(2)}, u32[]{:S(2)}) collective-permute-start(bf16[2,2,128,256]{3,2,1,0:T(8,128)(2,1)S(1)} %collective-permute-done.10.refs_2_), channel_id=1, source_target_pairs={{0,4},{1,5},{2,6},{3,7},{4,8},{5,9},{6,10},{7,11},{8,12},{9,13},{1... | collective-permute-start | bytes 786440 | tf_op jit(solution)/shard_map/ppermute | solution.py:40
  55.6 7.4 %collective-permute-start.19 = (bf16[2,2,128,256]{3,2,1,0:T(8,128)(2,1)S(1)}, bf16[2,2,128,256]{3,2,1,0:T(8,128)(2,1)S(1)}, u32[]{:S(2)}, u32[]{:S(2)}) collective-permute-start(bf16[2,2,128,256]{3,2,1,0:T(8,128)(2,1)S(1)} %collective-permute-done.18.refs_2_), channel_id=1, source_target_pairs={{0,2},{1,3},{2,0},{3,1},{4,6},{5,7},{6,4},{7,5},{8,10},{9,11},{10,... | collective-permute-start | bytes 786440 | tf_op jit(solution)/shard_map/ppermute | solution.py:40
  56.2 10.1 %collective-permute-start.20 = (bf16[2,2,128,256]{3,2,1,0:T(8,128)(2,1)S(1)}, bf16[2,2,128,256]{3,2,1,0:T(8,128)(2,1)S(1)}, u32[]{:S(2)}, u32[]{:S(2)}) collective-permute-start(bf16[2,2,128,256]{3,2,1,0:T(8,128)(2,1)S(1)} %collective-permute-done.18.refs_2_), channel_id=1, source_target_pairs={{0,4},{1,5},{2,6},{3,7},{4,8},{5,9},{6,10},{7,11},{8,12},{9,13},{1... | collective-permute-start | bytes 786440 | tf_op jit(solution)/shard_map/ppermute | solution.py:40
  61.2 7.8 %collective-permute-start.21 = (bf16[2,2,128,256]{3,2,1,0:T(8,128)(2,1)S(1)}, bf16[2,2,128,256]{3,2,1,0:T(8,128)(2,1)S(1)}, u32[]{:S(2)}, u32[]{:S(2)}) collective-permute-start(bf16[2,2,128,256]{3,2,1,0:T(8,128)(2,1)S(1)} %collective-permute-done.12.refs_3_), channel_id=1, source_target_pairs={{0,2},{1,3},{2,0},{3,1},{4,6},{5,7},{6,4},{7,5},{8,10},{9,11},{10,... | collective-permute-start | bytes 786440 | tf_op jit(solution)/shard_map/ppermute | solution.py:40
  61.7 29.6 %copy-start = (bf16[32,128,2048]{2,1,0:T(8,128)(2,1)S(1)}, bf16[32,128,2048]{2,1,0:T(8,128)(2,1)}, u32[]{:S(2)}) copy-start(bf16[32,128,2048]{2,1,0:T(8,128)(2,1)} %cholesky.1) | copy-start | bytes 50331652
  66.3 7.9 %collective-permute-start.22 = (bf16[2,2,128,256]{3,2,1,0:T(8,128)(2,1)S(1)}, bf16[2,2,128,256]{3,2,1,0:T(8,128)(2,1)S(1)}, u32[]{:S(2)}, u32[]{:S(2)}) collective-permute-start(bf16[2,2,128,256]{3,2,1,0:T(8,128)(2,1)S(1)} %collective-permute-done.20.refs_3_), channel_id=1, source_target_pairs={{0,2},{1,3},{2,0},{3,1},{4,6},{5,7},{6,4},{7,5},{8,10},{9,11},{10,... | collective-permute-start | bytes 786440 | tf_op jit(solution)/shard_map/ppermute | solution.py:40
  78.2 5.4 %collective-permute-start.24 = (f32[4,32]{1,0:T(4,128)S(1)}, f32[4,32]{1,0:T(4,128)S(1)}, u32[]{:S(2)}, u32[]{:S(2)}) collective-permute-start(f32[4,32]{1,0:T(4,128)S(1)} %shard_map.81), channel_id=1, source_target_pairs={{0,4},{1,5},{2,6},{3,7},{4,8},{5,9},{6,10},{7,11},{8,12},{9,13},{1... | collective-permute-start | bytes 1544 | tf_op jit(solution)/shard_map/ppermute | solution.py:40
  78.2 5.4 %collective-permute-start.25 = (f32[4,32]{1,0:T(4,128)S(1)}, f32[4,32]{1,0:T(4,128)S(1)}, u32[]{:S(2)}, u32[]{:S(2)}) collective-permute-start(f32[4,32]{1,0:T(4,128)S(1)} %shard_map.81), channel_id=1, source_target_pairs={{0,12},{1,13},{2,14},{3,15},{4,0},{5,1},{6,2},{7,3},{8,4},{9,5},{1... | collective-permute-start | bytes 1544 | tf_op jit(solution)/shard_map/ppermute | solution.py:40
  82.0 4.5 %collective-permute-start.23 = (f32[4,32]{1,0:T(4,128)S(1)}, f32[4,32]{1,0:T(4,128)S(1)}, u32[]{:S(2)}, u32[]{:S(2)}) collective-permute-start(f32[4,32]{1,0:T(4,128)S(1)} %shard_map.81), channel_id=1, source_target_pairs={{0,8},{1,9},{2,10},{3,11},{4,12},{5,13},{6,14},{7,15},{8,0},{9,1},... | collective-permute-start | bytes 1544 | tf_op jit(solution)/shard_map/ppermute | solution.py:40
  86.5 3.6 %collective-permute-start.26 = (f32[4,32]{1,0:T(4,128)S(1)}, f32[4,32]{1,0:T(4,128)S(1)}, u32[]{:S(2)}, u32[]{:S(2)}) collective-permute-start(f32[4,32]{1,0:T(4,128)S(1)} %add_add_fusion.mine), channel_id=1, source_target_pairs={{0,2},{1,3},{2,0},{3,1},{4,6},{5,7},{6,4},{7,5},{8,10},{9,11},{10,... | collective-permute-start | bytes 1544 | tf_op jit(solution)/shard_map/ppermute | solution.py:40
  87.1 3.0 %collective-permute-start.27 = (f32[4,32]{1,0:T(4,128)S(1)}, f32[4,32]{1,0:T(4,128)S(1)}, u32[]{:S(2)}, u32[]{:S(2)}) collective-permute-start(f32[4,32]{1,0:T(4,128)S(1)} %add_add_fusion.mine), channel_id=1, source_target_pairs={{0,1},{1,0},{2,3},{3,2},{4,5},{5,4},{6,7},{7,6},{8,9},{9,8},{10,11... | collective-permute-start | bytes 1544 | tf_op jit(solution)/shard_map/ppermute | solution.py:40
  87.1 3.0 %collective-permute-start.28 = (f32[4,32]{1,0:T(4,128)S(1)}, f32[4,32]{1,0:T(4,128)S(1)}, u32[]{:S(2)}, u32[]{:S(2)}) collective-permute-start(f32[4,32]{1,0:T(4,128)S(1)} %add_add_fusion.mine), channel_id=1, source_target_pairs={{0,3},{1,2},{2,1},{3,0},{4,7},{5,6},{6,5},{7,4},{8,11},{9,10},{10,... | collective-permute-start | bytes 1544 | tf_op jit(solution)/shard_map/ppermute | solution.py:40
  93.7 2.9 %collective-permute-start.29 = (bf16[4,64,2048]{2,1,0:T(8,128)(2,1)S(1)}, bf16[4,64,2048]{2,1,0:T(8,128)(2,1)S(1)}, u32[]{:S(2)}, u32[]{:S(2)}) collective-permute-start(bf16[4,64,2048]{2,1,0:T(8,128)(2,1)S(1)} %get-tuple-element.73), channel_id=1, source_target_pairs={{0,1},{1,0},{2,3},{3,2},{4,5},{5,4},{6,7},{7,6},{8,9},{9,8},{10,11... | collective-permute-start | bytes 3145736 | tf_op jit(solution)/shard_map/ppermute | solution.py:40
  94.2 3.8 %collective-permute-start.30 = (bf16[4,64,2048]{2,1,0:T(8,128)(2,1)S(1)}, bf16[4,64,2048]{2,1,0:T(8,128)(2,1)S(1)}, u32[]{:S(2)}, u32[]{:S(2)}) collective-permute-start(bf16[4,64,2048]{2,1,0:T(8,128)(2,1)S(1)} %get-tuple-element.74), channel_id=1, source_target_pairs={{0,1},{1,0},{2,3},{3,2},{4,5},{5,4},{6,7},{7,6},{8,9},{9,8},{10,11... | collective-permute-start | bytes 3145736 | tf_op jit(solution)/shard_map/ppermute | solution.py:40
  95.1 9.2 %collective-permute-start.31 = (bf16[4,128,256]{2,1,0:T(8,128)(2,1)S(1)}, bf16[4,128,256]{2,1,0:T(8,128)(2,1)S(1)}, u32[]{:S(2)}, u32[]{:S(2)}) collective-permute-start(bf16[4,128,256]{2,1,0:T(8,128)(2,1)S(1)} %get-tuple-element.79.refs_5_), channel_id=1, source_target_pairs={{0,2},{1,3},{2,0},{3,1},{4,6},{5,7},{6,4},{7,5},{8,10},{9,11},{10,... | collective-permute-start | bytes 786440 | tf_op jit(solution)/shard_map/ppermute | solution.py:40
  96.6 10.9 %collective-permute-start.32 = (bf16[4,128,256]{2,1,0:T(8,128)(2,1)S(1)}, bf16[4,128,256]{2,1,0:T(8,128)(2,1)S(1)}, u32[]{:S(2)}, u32[]{:S(2)}) collective-permute-start(bf16[4,128,256]{2,1,0:T(8,128)(2,1)S(1)} %get-tuple-element.79.refs_5_), channel_id=1, source_target_pairs={{0,4},{1,5},{2,6},{3,7},{4,8},{5,9},{6,10},{7,11},{8,12},{9,13},{1... | collective-permute-start | bytes 786440 | tf_op jit(solution)/shard_map/ppermute | solution.py:40
  98.8 11.1 %collective-permute-start.38 = (bf16[4,128,256]{2,1,0:T(8,128)(2,1)S(1)}, bf16[4,128,256]{2,1,0:T(8,128)(2,1)S(1)}, u32[]{:S(2)}, u32[]{:S(2)}) collective-permute-start(bf16[4,128,256]{2,1,0:T(8,128)(2,1)S(1)} %get-tuple-element.86.refs_13_), channel_id=1, source_target_pairs={{0,2},{1,3},{2,0},{3,1},{4,6},{5,7},{6,4},{7,5},{8,10},{9,11},{10,... | collective-permute-start | bytes 786440 | tf_op jit(solution)/shard_map/ppermute | solution.py:40
  100.3 12.8 %collective-permute-start.39 = (bf16[4,128,256]{2,1,0:T(8,128)(2,1)S(1)}, bf16[4,128,256]{2,1,0:T(8,128)(2,1)S(1)}, u32[]{:S(2)}, u32[]{:S(2)}) collective-permute-start(bf16[4,128,256]{2,1,0:T(8,128)(2,1)S(1)} %get-tuple-element.86.refs_13_), channel_id=1, source_target_pairs={{0,4},{1,5},{2,6},{3,7},{4,8},{5,9},{6,10},{7,11},{8,12},{9,13},{1... | collective-permute-start | bytes 786440 | tf_op jit(solution)/shard_map/ppermute | solution.py:40
  107.5 8.2 %collective-permute-start.33 = (bf16[4,128,256]{2,1,0:T(8,128)(2,1)S(1)}, bf16[4,128,256]{2,1,0:T(8,128)(2,1)S(1)}, u32[]{:S(2)}, u32[]{:S(2)}) collective-permute-start(bf16[4,128,256]{2,1,0:T(8,128)(2,1)S(1)} %collective-permute-done.32.refs_6_), channel_id=1, source_target_pairs={{0,2},{1,3},{2,0},{3,1},{4,6},{5,7},{6,4},{7,5},{8,10},{9,11},{10,... | collective-permute-start | bytes 786440 | tf_op jit(solution)/shard_map/ppermute | solution.py:40
  108.1 11.0 %collective-permute-start.34 = (bf16[4,128,256]{2,1,0:T(8,128)(2,1)S(1)}, bf16[4,128,256]{2,1,0:T(8,128)(2,1)S(1)}, u32[]{:S(2)}, u32[]{:S(2)}) collective-permute-start(bf16[4,128,256]{2,1,0:T(8,128)(2,1)S(1)} %collective-permute-done.32.refs_6_), channel_id=1, source_target_pairs={{0,4},{1,5},{2,6},{3,7},{4,8},{5,9},{6,10},{7,11},{8,12},{9,13},{1... | collective-permute-start | bytes 786440 | tf_op jit(solution)/shard_map/ppermute | solution.py:40
  113.1 8.7 %collective-permute-start.40 = (bf16[4,128,256]{2,1,0:T(8,128)(2,1)S(1)}, bf16[4,128,256]{2,1,0:T(8,128)(2,1)S(1)}, u32[]{:S(2)}, u32[]{:S(2)}) collective-permute-start(bf16[4,128,256]{2,1,0:T(8,128)(2,1)S(1)} %collective-permute-done.39.refs_14_), channel_id=1, source_target_pairs={{0,2},{1,3},{2,0},{3,1},{4,6},{5,7},{6,4},{7,5},{8,10},{9,11},{10,... | collective-permute-start | bytes 786440 | tf_op jit(solution)/shard_map/ppermute | solution.py:40
  113.7 11.1 %collective-permute-start.41 = (bf16[4,128,256]{2,1,0:T(8,128)(2,1)S(1)}, bf16[4,128,256]{2,1,0:T(8,128)(2,1)S(1)}, u32[]{:S(2)}, u32[]{:S(2)}) collective-permute-start(bf16[4,128,256]{2,1,0:T(8,128)(2,1)S(1)} %collective-permute-done.39.refs_14_), channel_id=1, source_target_pairs={{0,4},{1,5},{2,6},{3,7},{4,8},{5,9},{6,10},{7,11},{8,12},{9,13},{1... | collective-permute-start | bytes 786440 | tf_op jit(solution)/shard_map/ppermute | solution.py:40
  119.2 8.2 %collective-permute-start.35 = (bf16[4,128,256]{2,1,0:T(8,128)(2,1)S(1)}, bf16[4,128,256]{2,1,0:T(8,128)(2,1)S(1)}, u32[]{:S(2)}, u32[]{:S(2)}) collective-permute-start(bf16[4,128,256]{2,1,0:T(8,128)(2,1)S(1)} %collective-permute-done.34.refs_7_), channel_id=1, source_target_pairs={{0,2},{1,3},{2,0},{3,1},{4,6},{5,7},{6,4},{7,5},{8,10},{9,11},{10,... | collective-permute-start | bytes 786440 | tf_op jit(solution)/shard_map/ppermute | solution.py:40
  119.3 11.1 %collective-permute-start.36 = (bf16[4,128,256]{2,1,0:T(8,128)(2,1)S(1)}, bf16[4,128,256]{2,1,0:T(8,128)(2,1)S(1)}, u32[]{:S(2)}, u32[]{:S(2)}) collective-permute-start(bf16[4,128,256]{2,1,0:T(8,128)(2,1)S(1)} %collective-permute-done.34.refs_7_), channel_id=1, source_target_pairs={{0,4},{1,5},{2,6},{3,7},{4,8},{5,9},{6,10},{7,11},{8,12},{9,13},{1... | collective-permute-start | bytes 786440 | tf_op jit(solution)/shard_map/ppermute | solution.py:40
  124.8 8.2 %collective-permute-start.42 = (bf16[4,128,256]{2,1,0:T(8,128)(2,1)S(1)}, bf16[4,128,256]{2,1,0:T(8,128)(2,1)S(1)}, u32[]{:S(2)}, u32[]{:S(2)}) collective-permute-start(bf16[4,128,256]{2,1,0:T(8,128)(2,1)S(1)} %collective-permute-done.41.refs_15_), channel_id=1, source_target_pairs={{0,2},{1,3},{2,0},{3,1},{4,6},{5,7},{6,4},{7,5},{8,10},{9,11},{10,... | collective-permute-start | bytes 786440 | tf_op jit(solution)/shard_map/ppermute | solution.py:40
  125.3 9.5 %collective-permute-start.43 = (bf16[4,128,256]{2,1,0:T(8,128)(2,1)S(1)}, bf16[4,128,256]{2,1,0:T(8,128)(2,1)S(1)}, u32[]{:S(2)}, u32[]{:S(2)}) collective-permute-start(bf16[4,128,256]{2,1,0:T(8,128)(2,1)S(1)} %collective-permute-done.41.refs_15_), channel_id=1, source_target_pairs={{0,4},{1,5},{2,6},{3,7},{4,8},{5,9},{6,10},{7,11},{8,12},{9,13},{1... | collective-permute-start | bytes 786440 | tf_op jit(solution)/shard_map/ppermute | solution.py:40
  130.4 7.1 %collective-permute-start.37 = (bf16[4,128,256]{2,1,0:T(8,128)(2,1)S(1)}, bf16[4,128,256]{2,1,0:T(8,128)(2,1)S(1)}, u32[]{:S(2)}, u32[]{:S(2)}) collective-permute-start(bf16[4,128,256]{2,1,0:T(8,128)(2,1)S(1)} %collective-permute-done.36.refs_8_), channel_id=1, source_target_pairs={{0,2},{1,3},{2,0},{3,1},{4,6},{5,7},{6,4},{7,5},{8,10},{9,11},{10,... | collective-permute-start | bytes 786440 | tf_op jit(solution)/shard_map/ppermute | solution.py:40
  134.8 8.6 %collective-permute-start.44 = (bf16[4,128,256]{2,1,0:T(8,128)(2,1)S(1)}, bf16[4,128,256]{2,1,0:T(8,128)(2,1)S(1)}, u32[]{:S(2)}, u32[]{:S(2)}) collective-permute-start(bf16[4,128,256]{2,1,0:T(8,128)(2,1)S(1)} %collective-permute-done.42.refs_19_), channel_id=1, source_target_pairs={{0,4},{1,5},{2,6},{3,7},{4,8},{5,9},{6,10},{7,11},{8,12},{9,13},{1... | collective-permute-start | bytes 786440 | tf_op jit(solution)/shard_map/ppermute | solution.py:40
  144.9 1.6 %collective-permute-start.45 = (bf16[4,128,256]{2,1,0:T(8,128)(2,1)S(1)}, bf16[4,128,256]{2,1,0:T(8,128)(2,1)S(1)}, u32[]{:S(2)}, u32[]{:S(2)}) collective-permute-start(bf16[4,128,256]{2,1,0:T(8,128)(2,1)S(1)} %get-tuple-element.94), channel_id=1, source_target_pairs={{0,1},{1,0},{2,3},{3,2},{4,5},{5,4},{6,7},{7,6},{8,9},{9,8},{10,11... | collective-permute-start | bytes 786440 | tf_op jit(solution)/shard_map/ppermute | solution.py:40

commit v7 on v6

--- a/solution.py
+++ b/solution.py
@@ -39,6 +39,20 @@
             pairs.append((index, target))
         return lax.ppermute(array, "chol", pairs)
 
+    def step(self, array):
+        ring = [*range(0, self.z, 2), *reversed(range(1, self.z, 2))]
+        target = {z: ring[(at + 1) % self.z] for at, z in enumerate(ring)}
+        pairs = [(index, target[index // 4] * 4 + index % 4) for index in range(self.chol)]
+        return lax.ppermute(array, "chol", pairs)
+
+    def origin(self, steps, dy):
+        index = lax.axis_index("chol")
+        z, y = index // 4, lax.rem(index // 2, 2)
+        at = jnp.where(lax.rem(z, 2) == 0, z // 2, self.z - (z + 1) // 2)
+        at = lax.rem(at + (self.z - steps), self.z)
+        z = jnp.where(2 * at < self.z, 2 * at, 2 * (self.z - at) - 1)
+        return z * 2 + (y + dy - 2 * y * dy)
+
 
 class Stream:
     def __init__(self, layout, piece, last_along_z=False):
@@ -51,11 +65,11 @@
         latest = self.ring[-1]
         last = len(self.ring) == self.layout.z
         if last and self.last_along_z:
-            moved = [self.layout.shift(self.across[-1], dz=1)]
+            moved = [self.layout.step(self.across[-1])]
         else:
             moved = [self.layout.shift(latest, dy=1)]
         if not last:
-            moved.append(self.layout.shift(latest, dz=1))
+            moved.append(self.layout.step(latest))
         if anchors or not last:
             anchors, moved = lax.optimization_barrier((anchors, moved))
         self.across.append(moved[0])
@@ -63,53 +77,33 @@
         return anchors
 
     def pieces(self):
-        ring = [(array, dz, 0) for dz, array in enumerate(self.ring)]
-        return ring + [(array, dz, 1) for dz, array in enumerate(self.across)]
-
-
-class CrossFirst:
-    def __init__(self, layout, piece):
-        self.layout = layout
-        self.piece = piece
-        self.ring = []
-
-    def advance(self, anchors=()):
-        if self.ring:
-            moved = self.layout.shift(self.ring[-1], dz=1)
-        else:
-            moved = self.layout.shift(self.piece, dy=1)
-        anchors, moved = lax.optimization_barrier((anchors, moved))
-        self.ring.append(moved if self.ring else jnp.stack([self.piece, moved]))
-        return anchors
-
-
-def gathered(layout, dz, dy):
-    index = lax.axis_index("chol")
-    z, y = index // 4, lax.rem(index // 2, 2)
-    return lax.rem(z + (layout.z - dz), layout.z) * 2 + (y + dy - 2 * y * dy)
-
-
-def transpose_kernel(layout, mine, theirs, out, buffer):
-    b = lax.rem(lax.axis_index("chol"), 2)
-    for dz in range(layout.z):
-        for dy in range(2):
-            chip = gathered(layout, dz, dy)
-            buffer[chip, b] = mine[dz, dy]
-            buffer[chip, 1 - b] = theirs[dz, dy]
+        ring = [(array, steps, 0) for steps, array in enumerate(self.ring)]
+        return ring + [(array, steps, 1) for steps, array in enumerate(self.across)]
+
+
+def transpose_kernel(layout, places, *refs):
+    arrays, theirs, (out, buffer) = refs[: len(places)], refs[len(places) : -2], refs[-2:]
+    b = lax.rem(lax.axis_index("chol"), 2)
+    slabs = [(part, at) for part in theirs for at in range(part.shape[0])]
+    for array, (steps, dy), (part, at) in zip(arrays, places, slabs):
+        chip = layout.origin(steps, dy)
+        buffer[chip, b] = array[array.shape[0] - 1]
+        buffer[chip, 1 - b] = part[at]
     out[...] = buffer[...].reshape(-1, buffer.shape[-1]).T
 
 
-def transposed(layout, mine, theirs):
-    _, _, rows, electrons = mine.shape
-    chips = layout.chol // 2
-    return pl.pallas_call(
-        functools.partial(transpose_kernel, layout),
+def transposed(layout, stream, theirs):
+    arrays = [array for array, *_ in stream.pieces()]
+    places = [place for _, *place in stream.pieces()]
+    _, rows, electrons = arrays[0].shape
+    return pl.pallas_call(
+        functools.partial(transpose_kernel, layout, places),
         out_shape=jax.ShapeDtypeStruct((electrons, layout.chol * rows), BF16),
-        in_specs=vmem_specs(2),
+        in_specs=vmem_specs(len(arrays) + len(theirs)),
         out_specs=pl.BlockSpec(memory_space=pltpu.VMEM),
-        scratch_shapes=[pltpu.VMEM((chips, 2, rows, electrons), BF16)],
+        scratch_shapes=[pltpu.VMEM((layout.chol // 2, 2, rows, electrons), BF16)],
         compiler_params=params(8),
-    )(mine, theirs)
+    )(*arrays, *theirs)
 
 
 def product(left, right):
@@ -136,20 +130,23 @@
 
 def inverse_kernel(layout, places, trial, *refs):
     pieces, (full, out) = refs[:-2], refs[-2:]
+    count = out.shape[0]
     matrices = []
-    for walker in range(out.shape[0]):
-        for piece, (dz, dy) in zip(pieces, places):
-            full[walker, gathered(layout, dz, dy)] = piece[:, walker]
+    for walker in range(count):
+        for piece, (steps, dy) in zip(pieces, places):
+            chip = layout.origin(steps, dy)
+            for block in range(2):
+                full[walker, chip, block] = piece[block * count + walker]
         rows = full[walker].reshape(-1, full.shape[-1])
         matrices.append(jnp.dot(trial[...], rows, preferred_element_type=F32))
     for walker, inverse in enumerate(newton_inverses(matrices)):
         out[walker] = inverse.astype(out.dtype)
 
 
-def inverses_of(layout, trial, stream):
+def inverses_of(layout, trial, stream, count):
     arrays = [array for array, *_ in stream.pieces()]
     places = [place for _, *place in stream.pieces()]
-    _, count, rows, electrons = arrays[0].shape
+    _, rows, electrons = arrays[0].shape
     return pl.pallas_call(
         functools.partial(inverse_kernel, layout, places),
         out_shape=[
@@ -175,7 +172,7 @@
     count = 0
     for chunk, inverse, size in zip(chunks, inverses, sizes):
         for walker in range(size):
-            both = chunk[:, walker].reshape(2 * rows, electrons)
+            both = jnp.concatenate([chunk[walker], chunk[size + walker]], axis=0)
             product = jnp.dot(both, inverse[walker], preferred_element_type=F32).astype(BF16)
             greens[:, :, count] = product.reshape(2, rows // BLOCK, BLOCK, electrons)
             count += 1
@@ -206,7 +203,7 @@
 
 def bias_of(chunks, inverses, rot_mine, rot_theirs):
     vectors, rows, electrons = rot_mine.shape
-    sizes = [chunk.shape[1] for chunk in chunks]
+    sizes = [inverse.shape[0] for inverse in inverses]
     count = sum(sizes)
     return pl.pallas_call(
         functools.partial(bias_kernel, sizes),
@@ -223,9 +220,10 @@
     )(rot_mine, rot_theirs, *chunks, *inverses)
 
 
-def weights_kernel(order, fields, mine, mine_across, theirs, theirs_across, bias_out, weights):
+def potential_kernel(order, fields, mine, mine_across, theirs, theirs_across, cholesky, *refs):
+    bias_out, kept, *sent, weights = refs
     per_group, vectors = fields.shape
-    half = mine.shape[0]
+    half, piece = kept.shape[0], sent[0].shape[1]
     sums = (mine[...] + mine_across[...], theirs[...] + theirs_across[...])
     b = lax.rem(lax.axis_index("chol"), 2)
     row = lax.broadcasted_iota(jnp.int32, (per_group, vectors), 0)
@@ -254,46 +252,34 @@
         lax.broadcasted_iota(jnp.int32, spread.shape, 1), BLOCK
     )
     weights[...] = jnp.where(same, spread, 0.0).astype(BF16)
-
-
-def weights_of(order, fields, parts):
-    per_group, vectors = fields.shape
-    return pl.pallas_call(
-        weights_kernel,
-        out_shape=[
-            jax.ShapeDtypeStruct((per_group, vectors), F32),
-            jax.ShapeDtypeStruct((per_group * BLOCK, vectors * BLOCK), BF16),
-        ],
-        in_specs=[pl.BlockSpec(memory_space=pltpu.SMEM)] + vmem_specs(5),
-        out_specs=vmem_specs(2),
-        compiler_params=params(8),
-    )(order, fields, *parts)
-
-
-def potential_kernel(weights, cholesky, kept, *sent):
-    half, part = kept.shape[0], sent[0].shape[1]
-    vectors, rows, orbitals = cholesky.shape
+    rows, orbitals = cholesky.shape[1:]
     for at in range(0, rows, BLOCK):
         columns = cholesky[:, at : at + BLOCK, :].reshape(vectors * BLOCK, orbitals)
         result = TAU_ROOT * jnp.dot(weights[...], columns, preferred_element_type=F32)
         result = result.astype(BF16).reshape(2 * half, BLOCK, orbitals)
         kept[:, at : at + BLOCK, :] = result[:half]
-        start = at % part
-        sent[at // part][:, start : start + BLOCK, :] = result[half:]
-
-
-def potential_of(weights, cholesky):
-    vectors, rows, orbitals = cholesky.shape
-    half = weights.shape[0] // BLOCK // 2
-    kept = jax.ShapeDtypeStruct((half, rows, orbitals), BF16)
+        start = at % piece
+        sent[at // piece][:, start : start + BLOCK, :] = result[half:]
+
+
+def potential_of(order, fields, parts, cholesky):
+    per_group, vectors = fields.shape
+    half = per_group // 2
+    _, rows, orbitals = cholesky.shape
     sent = jax.ShapeDtypeStruct((half, rows // 2, orbitals), BF16)
     return pl.pallas_call(
         potential_kernel,
-        out_shape=[kept, sent, sent],
-        in_specs=vmem_specs(2),
-        out_specs=vmem_specs(3),
+        out_shape=[
+            jax.ShapeDtypeStruct((per_group, vectors), F32),
+            jax.ShapeDtypeStruct((half, rows, orbitals), BF16),
+            sent,
+            sent,
+        ],
+        in_specs=[pl.BlockSpec(memory_space=pltpu.SMEM)] + vmem_specs(6),
+        out_specs=vmem_specs(4),
+        scratch_shapes=[pltpu.VMEM((per_group * BLOCK, vectors * BLOCK), BF16)],
         compiler_params=params(12),
-    )(weights, cholesky)
+    )(order, fields, *parts, cholesky)
 
 
 def first_kernel(sibling, parts, *refs):
@@ -331,62 +317,109 @@
 
 
 def second_kernel(layout, places, parts, *refs):
-    potential, refs = refs[:parts], refs[parts:]
-    bases, pieces, (mine, sent, buffer) = refs[:2], refs[2:-3], refs[-3:]
-    b = lax.rem(lax.axis_index("chol"), 2)
-    for walker in range(mine.shape[0]):
-        for piece, (sibling, dz, dy) in zip(pieces, places):
+    potential, base, pieces = refs[:parts], refs[parts], refs[parts + 1 : -2]
+    out, full = refs[-2:]
+    b = lax.rem(lax.axis_index("chol"), 2)
+    for walker in range(out.shape[0]):
+        for piece, (sibling, steps, dy) in zip(pieces, places):
             block = 1 - b if sibling else b
-            buffer[walker, gathered(layout, dz, dy), block] = piece[walker]
+            full[walker, layout.origin(steps, dy), block] = piece[walker]
         rows = jnp.concatenate([part[walker] for part in potential], axis=0)
-        columns = buffer[walker].reshape(-1, buffer.shape[-1])
+        columns = full[walker].reshape(-1, full.shape[-1])
         term = jnp.dot(rows, columns, preferred_element_type=F32)
-        count = term.shape[0] // 2
-        mine[walker] = (bases[0][walker] + 0.5 * term[:count]).astype(BF16)
-        sent[walker] = (bases[1][walker] + 0.5 * term[count:]).astype(BF16)
-
-
-def second_of(layout, potential, bases, streams):
+        out[walker] = (base[walker] + 0.5 * term).astype(BF16)
+
+
+def second_of(layout, potential, base, streams):
     arrays, places = [], []
     for sibling, stream in enumerate(streams):
-        for array, dz, dy in stream.pieces():
+        for array, steps, dy in stream.pieces():
             arrays.append(array)
-            places.append((sibling, dz, dy))
-    half, rows, orbitals = potential[0].shape
-    electrons = arrays[0].shape[-1]
-    out = jax.ShapeDtypeStruct((half, rows, electrons), BF16)
+            places.append((sibling, steps, dy))
+    orbitals = potential[0].shape[2]
+    half, rows, electrons = base.shape
     return pl.pallas_call(
         functools.partial(second_kernel, layout, places, len(potential)),
-        out_shape=[out, out],
-        in_specs=vmem_specs(len(potential) + 2 + len(arrays)),
+        out_shape=[
+            jax.ShapeDtypeStruct((half, rows, electrons), BF16),
+            jax.ShapeDtypeStruct((half, layout.chol // 2, 2, rows, electrons), BF16),
+        ],
+        in_specs=vmem_specs(len(potential) + 1 + len(arrays)),
         out_specs=vmem_specs(2),
-        scratch_shapes=[pltpu.VMEM((half, layout.chol // 2, 2, rows, electrons), BF16)],
-        compiler_params=params(16),
+        compiler_params=params(8),
         cost_estimate=pl.CostEstimate(
-            flops=4 * half * rows * orbitals * electrons,
-            bytes_accessed=2 * half * orbitals * (2 * rows + electrons),
+            flops=2 * half * rows * orbitals * electrons,
+            bytes_accessed=2 * half * orbitals * (rows + 3 * electrons),
             transcendentals=0,
         ),
-    )(*potential, *bases, *arrays)
-
-
-def place_kernel(order, mine, theirs, out):
-    half = mine.shape[0]
-    b = lax.rem(lax.axis_index("chol"), 2)
+    )(*potential, base, *arrays)
+
+
+def finish_kernel(order, potential, base, full, out, results, semaphores):
+    half = base.shape[0]
+    b = lax.rem(lax.axis_index("chol"), 2)
+    copies = []
     for walker in range(half):
-        out[order[b * half + walker]] = mine[walker]
-        out[order[(1 - b) * half + walker]] = theirs[walker]
-
-
-def place(order, mine, theirs):
-    half, rows, electrons = mine.shape
+        columns = full[walker].reshape(-1, full.shape[-1])
+        term = jnp.dot(potential[walker], columns, preferred_element_type=F32)
+        results[walker] = (base[walker] + 0.5 * term).astype(BF16)
+        copies.append(
+            pltpu.make_async_copy(
+                results.at[walker], out.at[order[b * half + walker]], semaphores.at[walker]
+            )
+        )
+        copies[-1].start()
+    for copy in copies:
+        copy.wait()
+
+
+def finish(order, potential, base, full):
+    half, rows, electrons = base.shape
+    orbitals = potential.shape[2]
+    return pl.pallas_call(
+        finish_kernel,
+        out_shape=jax.ShapeDtypeStruct((2 * half, rows, electrons), BF16),
+        in_specs=[pl.BlockSpec(memory_space=pltpu.SMEM)] + vmem_specs(3),
+        out_specs=pl.BlockSpec(memory_space=pl.ANY),
+        scratch_shapes=[
+            pltpu.VMEM((half, rows, electrons), BF16),
+            pltpu.SemaphoreType.DMA((half,)),
+        ],
+        compiler_params=params(8),
+        cost_estimate=pl.CostEstimate(
+            flops=2 * half * rows * orbitals * electrons,
+            bytes_accessed=2 * half * orbitals * (rows + electrons),
+            transcendentals=0,
+        ),
+    )(order, potential, base, full)
+
+
+def place_kernel(order, theirs, _, out, semaphores):
+    half = theirs.shape[0]
+    b = lax.rem(lax.axis_index("chol"), 2)
+    copies = [
+        pltpu.make_async_copy(
+            theirs.at[walker], out.at[order[(1 - b) * half + walker]], semaphores.at[walker]
+        )
+        for walker in range(half)
+    ]
+    for copy in copies:
+        copy.start()
+    for copy in copies:
+        copy.wait()
+
+
+def place(order, theirs, out):
     return pl.pallas_call(
         place_kernel,
-        out_shape=jax.ShapeDtypeStruct((2 * half, rows, electrons), BF16),
-        in_specs=[pl.BlockSpec(memory_space=pltpu.SMEM)] + vmem_specs(2),
-        out_specs=pl.BlockSpec(memory_space=pltpu.VMEM),
-        compiler_params=params(8),
-    )(order, mine, theirs)
+        out_shape=jax.ShapeDtypeStruct(out.shape, out.dtype),
+        in_specs=[pl.BlockSpec(memory_space=pltpu.SMEM)] + vmem_specs(1)
+        + [pl.BlockSpec(memory_space=pl.ANY)],
+        out_specs=pl.BlockSpec(memory_space=pl.ANY),
+        scratch_shapes=[pltpu.SemaphoreType.DMA((theirs.shape[0],))],
+        input_output_aliases={2: 0},
+        compiler_params=params(4),
+    )(order, theirs, out)
 
 
 def split_kernel(source, walkers, *refs):
@@ -491,46 +524,34 @@
 
 
 def shards(layout, walkers, trial, cholesky, rotated, fields, source):
-    half = walkers.shape[0] // 2
     b = lax.axis_index("chol") % 2
     shares, order = migrate(layout, walkers, source)
+    sizes = [own.shape[0] for own, _ in shares]
     chunks = [
-        jnp.stack([jnp.where(b == 0, own, other), jnp.where(b == 0, other, own)])
-        for own, other in shares
+        jnp.concatenate([jnp.where(b == 0, own, other), jnp.where(b == 0, other, own), *extra])
+        for (own, other), extra in zip(shares, ([trial[None]], []))
     ]
-    streams = [Stream(layout, chunk) for chunk in chunks]
-    pairs = CrossFirst(layout, trial)
+    streams = [Stream(layout, chunks[0]), Stream(layout, chunks[1], last_along_z=True)]
     rot_theirs = layout.shift(rotated, db=1)
     for stage in range(layout.z):
-        last = stage == layout.z - 1
-        if stage < 2:
-            pairs.advance()
-            streams[0].advance(pairs.ring[-1:])
-            if stage == 1:
-                while len(pairs.ring) < layout.z:
-                    pairs.advance()
-            else:
-                pairs.advance()
-            streams[1].advance(pairs.ring[-1:])
-            if stage == 1:
-                planes = jnp.stack(pairs.ring)
-                planes_theirs = layout.shift(planes, db=1)
-        elif stage == 2:
-            planes_theirs, rot_theirs = streams[0].advance((planes_theirs, rot_theirs))
-            turned = transposed(layout, planes, planes_theirs)
-            (turned,) = streams[1].advance((turned,))
+        if stage == layout.z - 1:
+            early = jnp.stack([array[-1] for array, *_ in streams[0].pieces()])
+            early, rot_theirs = streams[0].advance((layout.shift(early, db=1), rot_theirs))
         else:
-            for stream in streams:
-                stream.advance()
-    fulls, inverses = zip(*[inverses_of(layout, turned, stream) for stream in streams])
+            streams[0].advance()
+        streams[1].advance()
+    late = layout.shift(streams[0].across[-1][-1:], db=1)
+    turned = transposed(layout, streams[0], (early, late))
+    fulls, inverses = zip(
+        *[inverses_of(layout, turned, stream, size) for stream, size in zip(streams, sizes)]
+    )
     total = bias_of(chunks, inverses, rotated, rot_theirs)
     parts = [total] + [layout.shift(total, dz=dz) for dz in range(1, layout.z)]
     while len(parts) > 1:
         far = len(parts) // 2
         parts = [parts[at] + parts[at + far] for at in range(far)]
     parts = [parts[0]] + [layout.shift(parts[0], dy=dy, db=db) for dy, db in ((1, 0), (0, 1), (1, 1))]
-    force_bias, weights = weights_of(order, fields, parts)
-    kept, *sent = potential_of(weights, cholesky)
+    force_bias, kept, *sent = potential_of(order, fields, parts, cholesky)
     received = [layout.shift(part, db=1) for part in sent]
 
     rounded, base = first_of([kept], fulls, 0)
@@ -539,8 +560,9 @@
     for _ in range(layout.z):
         for stream in streams:
             stream.advance()
-    mine, sent = second_of(layout, (kept, *received), (base, base_theirs), streams)
-    return place(order, mine, layout.shift(sent, db=1)), force_bias
+    sent, full = second_of(layout, received, base_theirs, streams)
+    theirs = layout.shift(sent, db=1)
+    return place(order, theirs, finish(order, kept, base, full)), force_bias
 
 
 def solution(mesh):

time: 148 us -> 143 us (0.966)
  waiting for transfers between devices: 102 us -> 75.4 us
  starting transfers between devices: 26 us -> 45.9 us
    ppermute x44 -> x27, waiting for transfers between devices: 102 us -> 27.9 us  [shift(): return lax.ppermute(array, 'chol', pairs)]
    ppermute x0 -> x14, waiting for transfers between devices: none -> 46.2 us  [step(): return lax.ppermute(array, 'chol', pairs)]
    ppermute x0 -> x14, starting transfers between devices: none -> 24.6 us  [step(): return lax.ppermute(array, 'chol', pairs)]
    ppermute x44 -> x27, starting transfers between devices: 24.3 us -> 18.7 us  [shift(): return lax.ppermute(array, 'chol', pairs)]
    pallas_call x4, Pallas kernels: 5.32 us -> 6.89 us  [the longest x1 3.17 us: potential_of(): pl.pallas_call(potential_kernel, out_shape=[jax.ShapeDtypeStruct((per_gro...]
  transfers between devices with their start and end apart: 46 -> 43, of which waited for: 31 -> 31; matrix products, arithmetic and copies ran while one was open for 1% -> 1% of each run, Pallas kernels for 4% -> 4%
where the time goes in v7:
time: 143 us
  waiting for transfers between devices  75.4 us (53%)
  starting transfers between devices  45.9 us (32%)
  Pallas kernels  17.7 us (12%)
  local copies, waits for them, and re-layouts  1.75 us (1%)
    ppermute x14, waiting for transfers between devices, step(): return lax.ppermute(array, 'chol', pairs)  46.2 us
    ppermute x27, waiting for transfers between devices, shift(): return lax.ppermute(array, 'chol', pairs)  27.9 us
    ppermute x14, starting transfers between devices, step(): return lax.ppermute(array, 'chol', pairs)  24.6 us
    ppermute x27, starting transfers between devices, shift(): return lax.ppermute(array, 'chol', pairs)  18.7 us
    pallas_call x2, Pallas kernels, inverses_of(): pl.pallas_call(functools.partial(inverse_kernel, layout, places), out_sha...  4.53 us
    pallas_call x1, Pallas kernels, potential_of(): pl.pallas_call(potential_kernel, out_shape=[jax.ShapeDtypeStruct((per_gro...  3.17 us
  transfers between devices with their start and end apart: 43, of which 31 were waited for; matrix products, arithmetic and copies ran while one was open for 1% of the time, Pallas kernels for 4%

profile of v7, /device:TPU:0, one launch (start us, length us, event | category | flops | bytes accessed | tf_op | source)
XLA Modules:
  0.0 142.6 jit_solution(11678971100874760023)
XLA Ops:
  0.6 1.0 copy-done.2
  1.7 0.7 copy-done.4
  2.3 2.0 %shard_map.77 = (bf16[2,128,256]{2,1,0:T(8,128)(2,1)S(1)}, bf16[2,128,256]{2,1,0:T(8,128)(2,1)S(1)}, bf16[2,128,256]{2,1,0:T(8,128)(2,1)S(1)}, bf16[2,128,256]{2,1,0:T(8,128)(2,1)S(1)}, s32[8]{0:T(128)S(1)}) custom-call(s32[16]{0:T(128)S(1)} %copy-done.4, bf16[8,128,256]{2,1,0:T(8,128)(2,1)S(1)} %copy-done.2), custom_call_target="tpu_custom_call" | custom-call | tf_op jit(solution)/shard_map/pallas_call | solution.py:465
  4.4 0.5 collective-permute-start
  4.9 2.6 %collective-permute-start.10 = (bf16[2,128,256]{2,1,0:T(8,128)(2,1)S(1)}, bf16[2,128,256]{2,1,0:T(8,128)(2,1)S(1)}, u32[]{:S(2)}, u32[]{:S(2)}) collective-permute-start(bf16[2,128,256]{2,1,0:T(8,128)(2,1)S(1)} %get-tuple-element.58), channel_id=1, source_target_pairs={{0,16},{1,17},{2,18},{3,19},{4,20},{5,21},{6,22},{7,23},{8,24},{9,... | collective-permute-start | bytes 393224 | tf_op jit(solution)/shard_map/ppermute | solution.py:494
  7.6 0.9 pad_maximum_fusion.refs_0_
  8.5 2.9 %collective-permute-start.2 = (bf16[5,128,256]{2,1,0:T(8,128)(2,1)S(1)}, bf16[5,128,256]{2,1,0:T(8,128)(2,1)S(1)}, u32[]{:S(2)}, u32[]{:S(2)}) collective-permute-start(bf16[5,128,256]{2,1,0:T(8,128)(2,1)S(1)} %pad_maximum_fusion.refs_0_), channel_id=1, source_target_pairs={{0,8},{1,9},{2,10},{3,11},{4,0},{5,1},{6,2},{7,3},{8,12},{9,13},{1... | collective-permute-start | bytes 983048 | tf_op jit(solution)/shard_map/ppermute | solution.py:46
  11.3 1.5 %collective-permute-start.1 = (bf16[5,128,256]{2,1,0:T(8,128)(2,1)S(1)}, bf16[5,128,256]{2,1,0:T(8,128)(2,1)S(1)}, u32[]{:S(2)}, u32[]{:S(2)}) collective-permute-start(bf16[5,128,256]{2,1,0:T(8,128)(2,1)S(1)} %pad_maximum_fusion.refs_0_), channel_id=1, source_target_pairs={{0,2},{1,3},{2,0},{3,1},{4,6},{5,7},{6,4},{7,5},{8,10},{9,11},{10,... | collective-permute-start | bytes 983048 | tf_op jit(solution)/shard_map/ppermute | solution.py:40
  12.9 1.2 collective-permute-done.11
  14.1 4.7 %collective-permute-done.2.refs_1_ = bf16[5,128,256]{2,1,0:T(8,128)(2,1)S(1)} collective-permute-done((bf16[5,128,256]{2,1,0:T(8,128)(2,1)S(1)}, bf16[5,128,256]{2,1,0:T(8,128)(2,1)S(1)}, u32[]{:S(2)}, u32[]{:S(2)}) %collective-permute-start.2) | collective-permute-done | bytes 327712 | tf_op jit(solution)/shard_map/ppermute | solution.py:46
  18.8 2.2 %collective-permute-done.1.refs_4_ = bf16[5,128,256]{2,1,0:T(8,128)(2,1)S(1)} collective-permute-done((bf16[5,128,256]{2,1,0:T(8,128)(2,1)S(1)}, bf16[5,128,256]{2,1,0:T(8,128)(2,1)S(1)}, u32[]{:S(2)}, u32[]{:S(2)}) %collective-permute-start.1) | collective-permute-done | bytes 327712 | tf_op jit(solution)/shard_map/ppermute | solution.py:40
  21.0 1.6 %collective-permute-start.4 = (bf16[5,128,256]{2,1,0:T(8,128)(2,1)S(1)}, bf16[5,128,256]{2,1,0:T(8,128)(2,1)S(1)}, u32[]{:S(2)}, u32[]{:S(2)}) collective-permute-start(bf16[5,128,256]{2,1,0:T(8,128)(2,1)S(1)} %collective-permute-done.2.refs_1_), channel_id=1, source_target_pairs={{0,8},{1,9},{2,10},{3,11},{4,0},{5,1},{6,2},{7,3},{8,12},{9,13},{1... | collective-permute-start | bytes 983048 | tf_op jit(solution)/shard_map/ppermute | solution.py:46
  22.6 1.5 %collective-permute-start.3 = (bf16[5,128,256]{2,1,0:T(8,128)(2,1)S(1)}, bf16[5,128,256]{2,1,0:T(8,128)(2,1)S(1)}, u32[]{:S(2)}, u32[]{:S(2)}) collective-permute-start(bf16[5,128,256]{2,1,0:T(8,128)(2,1)S(1)} %collective-permute-done.2.refs_1_), channel_id=1, source_target_pairs={{0,2},{1,3},{2,0},{3,1},{4,6},{5,7},{6,4},{7,5},{8,10},{9,11},{10,... | collective-permute-start | bytes 983048 | tf_op jit(solution)/shard_map/ppermute | solution.py:40
  24.6 0.5 collective-permute-start.13
  25.1 10.4 %collective-permute-done.14.refs_1_ = bf16[4,128,256]{2,1,0:T(8,128)(2,1)S(1)} collective-permute-done((bf16[4,128,256]{2,1,0:T(8,128)(2,1)S(1)}, bf16[4,128,256]{2,1,0:T(8,128)(2,1)S(1)}, u32[]{:S(2)}, u32[]{:S(2)}) %collective-permute-start.14) | collective-permute-done | bytes 262176 | tf_op jit(solution)/shard_map/ppermute | solution.py:46
  35.5 1.3 collective-permute-done.13.refs_4_
  36.8 1.2 collective-permute-start.16
  38.0 1.5 %collective-permute-start.15 = (bf16[4,128,256]{2,1,0:T(8,128)(2,1)S(1)}, bf16[4,128,256]{2,1,0:T(8,128)(2,1)S(1)}, u32[]{:S(2)}, u32[]{:S(2)}) collective-permute-start(bf16[4,128,256]{2,1,0:T(8,128)(2,1)S(1)} %collective-permute-done.14.refs_1_), channel_id=1, source_target_pairs={{0,2},{1,3},{2,0},{3,1},{4,6},{5,7},{6,4},{7,5},{8,10},{9,11},{10,... | collective-permute-start | bytes 786440 | tf_op jit(solution)/shard_map/ppermute | solution.py:40
  39.5 0.7 collective-permute-start.6
  40.1 0.5 collective-permute-start.5
  40.7 9.4 %collective-permute-done.6.refs_3_ = bf16[5,128,256]{2,1,0:T(8,128)(2,1)S(1)} collective-permute-done((bf16[5,128,256]{2,1,0:T(8,128)(2,1)S(1)}, bf16[5,128,256]{2,1,0:T(8,128)(2,1)S(1)}, u32[]{:S(2)}, u32[]{:S(2)}) %collective-permute-start.6) | collective-permute-done | bytes 327712 | tf_op jit(solution)/shard_map/ppermute | solution.py:46
  50.0 1.2 collective-permute-done.5.refs_6_
  51.4 1.2 collective-permute-start.18
  52.6 1.6 %collective-permute-start.17 = (bf16[4,128,256]{2,1,0:T(8,128)(2,1)S(1)}, bf16[4,128,256]{2,1,0:T(8,128)(2,1)S(1)}, u32[]{:S(2)}, u32[]{:S(2)}) collective-permute-start(bf16[4,128,256]{2,1,0:T(8,128)(2,1)S(1)} %collective-permute-done.16.refs_2_), channel_id=1, source_target_pairs={{0,2},{1,3},{2,0},{3,1},{4,6},{5,7},{6,4},{7,5},{8,10},{9,11},{10,... | collective-permute-start | bytes 786440 | tf_op jit(solution)/shard_map/ppermute | solution.py:40
  54.6 5.4 %collective-permute-done.18.refs_3_ = bf16[4,128,256]{2,1,0:T(8,128)(2,1)S(1)} collective-permute-done((bf16[4,128,256]{2,1,0:T(8,128)(2,1)S(1)}, bf16[4,128,256]{2,1,0:T(8,128)(2,1)S(1)}, u32[]{:S(2)}, u32[]{:S(2)}) %collective-permute-start.18) | collective-permute-done | bytes 262176 | tf_op jit(solution)/shard_map/ppermute | solution.py:46
  60.1 1.7 %collective-permute-done.17.refs_6_ = bf16[4,128,256]{2,1,0:T(8,128)(2,1)S(1)} collective-permute-done((bf16[4,128,256]{2,1,0:T(8,128)(2,1)S(1)}, bf16[4,128,256]{2,1,0:T(8,128)(2,1)S(1)}, u32[]{:S(2)}, u32[]{:S(2)}) %collective-permute-start.17) | collective-permute-done | bytes 262176 | tf_op jit(solution)/shard_map/ppermute | solution.py:40
  61.8 1.0 collective-permute-start.19
  62.7 5.3 %collective-permute-done.9.refs_7_ = bf16[5,128,256]{2,1,0:T(8,128)(2,1)S(1)} collective-permute-done((bf16[5,128,256]{2,1,0:T(8,128)(2,1)S(1)}, bf16[5,128,256]{2,1,0:T(8,128)(2,1)S(1)}, u32[]{:S(2)}, u32[]{:S(2)}) %collective-permute-start.9) | collective-permute-done | bytes 327712 | tf_op jit(solution)/shard_map/ppermute | solution.py:40
  68.1 1.2 collective-permute-done.12.refs_9_
  69.8 2.3 %shard_map.79 = (bf16[2,8,2,128,256]{4,3,2,1,0:T(8,128)(2,1)S(1)}, bf16[2,256,256]{2,1,0:T(8,128)(2,1)S(1)}) custom-call(bf16[256,2048]{1,0:T(8,128)(2,1)S(1)} %shard_map.78.trial, bf16[5,128,256]{2,1,0:T(8,128)(2,1)S(1)} %pad_maximum_fusion.refs_0_, bf16[5,128,256]{2,1,0:T(8,128)(2,1)S(1)} %collective-permute-done.2.refs_1_, ...), custom_call_target="tpu_custom_call" | custom-call | flops 1342177280 | bytes 6291456 | tf_op jit(solution)/shard_map/pallas_call | solution.py:150
  72.1 2.3 %shard_map.80 = (bf16[2,8,2,128,256]{4,3,2,1,0:T(8,128)(2,1)S(1)}, bf16[2,256,256]{2,1,0:T(8,128)(2,1)S(1)}) custom-call(bf16[256,2048]{1,0:T(8,128)(2,1)S(1)} %shard_map.78.trial, bf16[4,128,256]{2,1,0:T(8,128)(2,1)S(1)} %pad_maximum_fusion.1.refs_0_.refs_1_, bf16[4,128,256]{2,1,0:T(8,128)(2,1)S(1)} %collective-permute-done.14.refs_1_, ...), custom_call_target="tpu_custom_call" | custom-call | flops 1342177280 | bytes 6291456 | tf_op jit(solution)/shard_map/pallas_call | solution.py:150
  74.4 1.7 %shard_map.81 = f32[4,32]{1,0:T(4,128)S(1)} custom-call(bf16[32,128,256]{2,1,0:T(8,128)(2,1)S(1)} %copy-done.1, bf16[32,128,256]{2,1,0:T(8,128)(2,1)S(1)} %collective-permute-done.8.rot_theirs, bf16[5,128,256]{2,1,0:T(8,128)(2,1)S(1)} %pad_maximum_fusion.refs_0_, bf16[4,128,256]{2,1,0:T(8,128)(2,1)S(1)} %pad_maximum_fusion.1.refs_0_.refs_1_, ...), custom_call_target="tpu_custom_call" | custom-call | flops 402653184 | bytes 4718592 | tf_op jit(solution)/shard_map/pallas_call | solution.py:208
  76.1 1.8 %collective-permute-start.22 = (f32[4,32]{1,0:T(4,128)S(1)}, f32[4,32]{1,0:T(4,128)S(1)}, u32[]{:S(2)}, u32[]{:S(2)}) collective-permute-start(f32[4,32]{1,0:T(4,128)S(1)} %shard_map.81), channel_id=1, source_target_pairs={{0,12},{1,13},{2,14},{3,15},{4,0},{5,1},{6,2},{7,3},{8,4},{9,5},{1... | collective-permute-start | bytes 1544 | tf_op jit(solution)/shard_map/ppermute | solution.py:40
  78.1 1.0 collective-permute-start.20
  79.1 0.6 collective-permute-done.22
  79.7 3.5 %collective-permute-done.21 = f32[4,32]{1,0:T(4,128)S(1)} collective-permute-done((f32[4,32]{1,0:T(4,128)S(1)}, f32[4,32]{1,0:T(4,128)S(1)}, u32[]{:S(2)}, u32[]{:S(2)}) %collective-permute-start.21) | collective-permute-done | bytes 544 | tf_op jit(solution)/shard_map/ppermute | solution.py:40
  83.3 1.6 %collective-permute-start.24 = (f32[4,32]{1,0:T(4,128)S(1)}, f32[4,32]{1,0:T(4,128)S(1)}, u32[]{:S(2)}, u32[]{:S(2)}) collective-permute-start(f32[4,32]{1,0:T(4,128)S(1)} %add_add_fusion.mine), channel_id=1, source_target_pairs={{0,1},{1,0},{2,3},{3,2},{4,5},{5,4},{6,7},{7,6},{8,9},{9,8},{10,11... | collective-permute-start | bytes 1544 | tf_op jit(solution)/shard_map/ppermute | solution.py:40
  85.4 0.9 collective-permute-done.25.theirs_across
  86.3 2.2 %collective-permute-done.23.mine_across = f32[4,32]{1,0:T(4,128)S(1)} collective-permute-done((f32[4,32]{1,0:T(4,128)S(1)}, f32[4,32]{1,0:T(4,128)S(1)}, u32[]{:S(2)}, u32[]{:S(2)}) %collective-permute-start.23) | collective-permute-done | bytes 544 | tf_op jit(solution)/shard_map/ppermute | solution.py:40
  88.5 3.2 %shard_map.82 = (f32[8,32]{1,0:T(8,128)}, bf16[4,128,2048]{2,1,0:T(8,128)(2,1)S(1)}, bf16[4,64,2048]{2,1,0:T(8,128)(2,1)S(1)}, bf16[4,64,2048]{2,1,0:T(8,128)(2,1)S(1)}) custom-call(s32[8]{0:T(128)S(1)} %get-tuple-element.48.order, f32[8,32]{1,0:T(8,128)S(1)} %copy-done.3, f32[4,32]{1,0:T(4,128)S(1)} %add_add_fusion.mine, ...), custom_call_target="tpu_custom_call" | custom-call | tf_op jit(solution)/shard_map/pallas_call | solution.py:270
  92.3 0.7 shard_map.84
  93.4 0.5 collective-permute-start.28
  93.9 0.6 collective-permute-done.26.refs_0_
  94.4 1.5 %collective-permute-done.27.refs_1_ = bf16[4,64,2048]{2,1,0:T(8,128)(2,1)S(1)} collective-permute-done((bf16[4,64,2048]{2,1,0:T(8,128)(2,1)S(1)}, bf16[4,64,2048]{2,1,0:T(8,128)(2,1)S(1)}, u32[]{:S(2)}, u32[]{:S(2)}) %collective-permute-start.27) | collective-permute-done | bytes 1048608 | tf_op jit(solution)/shard_map/ppermute | solution.py:40
  95.9 0.7 shard_map.83
  96.7 1.1 collective-permute-start.36
  97.8 1.5 %collective-permute-start.35 = (bf16[4,128,256]{2,1,0:T(8,128)(2,1)S(1)}, bf16[4,128,256]{2,1,0:T(8,128)(2,1)S(1)}, u32[]{:S(2)}, u32[]{:S(2)}) collective-permute-start(bf16[4,128,256]{2,1,0:T(8,128)(2,1)S(1)} %get-tuple-element.83.refs_11_), channel_id=1, source_target_pairs={{0,2},{1,3},{2,0},{3,1},{4,6},{5,7},{6,4},{7,5},{8,10},{9,11},{10,... | collective-permute-start | bytes 786440 | tf_op jit(solution)/shard_map/ppermute | solution.py:40
  99.3 2.9 %collective-permute-done.29.refs_4_ = bf16[4,128,256]{2,1,0:T(8,128)(2,1)S(1)} collective-permute-done((bf16[4,128,256]{2,1,0:T(8,128)(2,1)S(1)}, bf16[4,128,256]{2,1,0:T(8,128)(2,1)S(1)}, u32[]{:S(2)}, u32[]{:S(2)}) %collective-permute-start.29) | collective-permute-done | bytes 262176 | tf_op jit(solution)/shard_map/ppermute | solution.py:46
  102.6 3.1 %collective-permute-start.31 = (bf16[4,128,256]{2,1,0:T(8,128)(2,1)S(1)}, bf16[4,128,256]{2,1,0:T(8,128)(2,1)S(1)}, u32[]{:S(2)}, u32[]{:S(2)}) collective-permute-start(bf16[4,128,256]{2,1,0:T(8,128)(2,1)S(1)} %collective-permute-done.29.refs_4_), channel_id=1, source_target_pairs={{0,8},{1,9},{2,10},{3,11},{4,0},{5,1},{6,2},{7,3},{8,12},{9,13},{1... | collective-permute-start | bytes 786440 | tf_op jit(solution)/shard_map/ppermute | solution.py:46
  106.2 1.7 %collective-permute-done.36.refs_12_ = bf16[4,128,256]{2,1,0:T(8,128)(2,1)S(1)} collective-permute-done((bf16[4,128,256]{2,1,0:T(8,128)(2,1)S(1)}, bf16[4,128,256]{2,1,0:T(8,128)(2,1)S(1)}, u32[]{:S(2)}, u32[]{:S(2)}) %collective-permute-start.36) | collective-permute-done | bytes 262176 | tf_op jit(solution)/shard_map/ppermute | solution.py:46
  108.2 3.1 %collective-permute-start.38 = (bf16[4,128,256]{2,1,0:T(8,128)(2,1)S(1)}, bf16[4,128,256]{2,1,0:T(8,128)(2,1)S(1)}, u32[]{:S(2)}, u32[]{:S(2)}) collective-permute-start(bf16[4,128,256]{2,1,0:T(8,128)(2,1)S(1)} %collective-permute-done.36.refs_12_), channel_id=1, source_target_pairs={{0,8},{1,9},{2,10},{3,11},{4,0},{5,1},{6,2},{7,3},{8,12},{9,13},{1... | collective-permute-start | bytes 786440 | tf_op jit(solution)/shard_map/ppermute | solution.py:46
  111.8 1.7 %collective-permute-done.31.refs_5_ = bf16[4,128,256]{2,1,0:T(8,128)(2,1)S(1)} collective-permute-done((bf16[4,128,256]{2,1,0:T(8,128)(2,1)S(1)}, bf16[4,128,256]{2,1,0:T(8,128)(2,1)S(1)}, u32[]{:S(2)}, u32[]{:S(2)}) %collective-permute-start.31) | collective-permute-done | bytes 262176 | tf_op jit(solution)/shard_map/ppermute | solution.py:46
  113.9 3.0 %collective-permute-start.33 = (bf16[4,128,256]{2,1,0:T(8,128)(2,1)S(1)}, bf16[4,128,256]{2,1,0:T(8,128)(2,1)S(1)}, u32[]{:S(2)}, u32[]{:S(2)}) collective-permute-start(bf16[4,128,256]{2,1,0:T(8,128)(2,1)S(1)} %collective-permute-done.31.refs_5_), channel_id=1, source_target_pairs={{0,8},{1,9},{2,10},{3,11},{4,0},{5,1},{6,2},{7,3},{8,12},{9,13},{1... | collective-permute-start | bytes 786440 | tf_op jit(solution)/shard_map/ppermute | solution.py:46
  117.4 1.7 %collective-permute-done.38.refs_13_ = bf16[4,128,256]{2,1,0:T(8,128)(2,1)S(1)} collective-permute-done((bf16[4,128,256]{2,1,0:T(8,128)(2,1)S(1)}, bf16[4,128,256]{2,1,0:T(8,128)(2,1)S(1)}, u32[]{:S(2)}, u32[]{:S(2)}) %collective-permute-start.38) | collective-permute-done | bytes 262176 | tf_op jit(solution)/shard_map/ppermute | solution.py:46
  119.5 3.0 %collective-permute-start.40 = (bf16[4,128,256]{2,1,0:T(8,128)(2,1)S(1)}, bf16[4,128,256]{2,1,0:T(8,128)(2,1)S(1)}, u32[]{:S(2)}, u32[]{:S(2)}) collective-permute-start(bf16[4,128,256]{2,1,0:T(8,128)(2,1)S(1)} %collective-permute-done.38.refs_13_), channel_id=1, source_target_pairs={{0,8},{1,9},{2,10},{3,11},{4,0},{5,1},{6,2},{7,3},{8,12},{9,13},{1... | collective-permute-start | bytes 786440 | tf_op jit(solution)/shard_map/ppermute | solution.py:46
  123.0 1.7 %collective-permute-done.33.refs_6_ = bf16[4,128,256]{2,1,0:T(8,128)(2,1)S(1)} collective-permute-done((bf16[4,128,256]{2,1,0:T(8,128)(2,1)S(1)}, bf16[4,128,256]{2,1,0:T(8,128)(2,1)S(1)}, u32[]{:S(2)}, u32[]{:S(2)}) %collective-permute-start.33) | collective-permute-done | bytes 262176 | tf_op jit(solution)/shard_map/ppermute | solution.py:46
  125.7 3.8 %collective-permute-done.40.refs_14_ = bf16[4,128,256]{2,1,0:T(8,128)(2,1)S(1)} collective-permute-done((bf16[4,128,256]{2,1,0:T(8,128)(2,1)S(1)}, bf16[4,128,256]{2,1,0:T(8,128)(2,1)S(1)}, u32[]{:S(2)}, u32[]{:S(2)}) %collective-permute-start.40) | collective-permute-done | bytes 262176 | tf_op jit(solution)/shard_map/ppermute | solution.py:46
  129.4 2.3 %collective-permute-done.39.refs_17_ = bf16[4,128,256]{2,1,0:T(8,128)(2,1)S(1)} collective-permute-done((bf16[4,128,256]{2,1,0:T(8,128)(2,1)S(1)}, bf16[4,128,256]{2,1,0:T(8,128)(2,1)S(1)}, u32[]{:S(2)}, u32[]{:S(2)}) %collective-permute-start.39) | collective-permute-done | bytes 262176 | tf_op jit(solution)/shard_map/ppermute | solution.py:40
  131.8 2.0 %collective-permute-start.41 = (bf16[4,128,256]{2,1,0:T(8,128)(2,1)S(1)}, bf16[4,128,256]{2,1,0:T(8,128)(2,1)S(1)}, u32[]{:S(2)}, u32[]{:S(2)}) collective-permute-start(bf16[4,128,256]{2,1,0:T(8,128)(2,1)S(1)} %collective-permute-done.39.refs_17_), channel_id=1, source_target_pairs={{0,8},{1,9},{2,10},{3,11},{4,0},{5,1},{6,2},{7,3},{8,12},{9,13},{1... | collective-permute-start | bytes 786440 | tf_op jit(solution)/shard_map/ppermute | solution.py:46
  133.8 1.4 collective-permute-done.34.refs_10_
  135.1 3.0 %collective-permute-done.41.refs_18_ = bf16[4,128,256]{2,1,0:T(8,128)(2,1)S(1)} collective-permute-done((bf16[4,128,256]{2,1,0:T(8,128)(2,1)S(1)}, bf16[4,128,256]{2,1,0:T(8,128)(2,1)S(1)}, u32[]{:S(2)}, u32[]{:S(2)}) %collective-permute-start.41) | collective-permute-done | bytes 262176 | tf_op jit(solution)/shard_map/ppermute | solution.py:46
  138.1 1.0 shard_map.85
  139.3 2.0 %shard_map.86._ = bf16[8,128,256]{2,1,0:T(8,128)(2,1)} custom-call(s32[8]{0:T(128)S(1)} %get-tuple-element.48.order, bf16[4,128,2048]{2,1,0:T(8,128)(2,1)S(1)} %get-tuple-element.75.refs_0_.potential, f32[4,128,256]{2,1,0:T(8,128)S(1)} %get-tuple-element.91.base, bf16[4,8,2,128,256]{4,3,2,1,0:T(8,128)(2,1)S(1)} %get-tuple-element.92.full), custom_call_target="tpu_custom_call" | custom-call | flops 536870912 | bytes 6291456 | tf_op jit(solution)/shard_map/pallas_call | solution.py:379
  141.3 1.3 shard_map.87
  (58 shorter events, 8.2 us)
Async XLA Ops:
  0.6 1.0 copy-start.2
  1.7 0.7 copy-start.4
  2.3 22.7 %copy-start.5 = (bf16[128,256]{1,0:T(8,128)(2,1)S(1)}, bf16[128,256]{1,0:T(8,128)(2,1)}, u32[]{:S(2)}) copy-start(bf16[128,256]{1,0:T(8,128)(2,1)} %param.7) | copy-start | bytes 196612
  4.4 3.2 %collective-permute-start = (bf16[2,128,256]{2,1,0:T(8,128)(2,1)S(1)}, bf16[2,128,256]{2,1,0:T(8,128)(2,1)S(1)}, u32[]{:S(2)}, u32[]{:S(2)}) collective-permute-start(bf16[2,128,256]{2,1,0:T(8,128)(2,1)S(1)} %get-tuple-element.50), channel_id=1, source_target_pairs={{0,1},{1,0},{2,3},{3,2},{4,5},{5,4},{6,7},{7,6},{8,9},{9,8},{10,11... | collective-permute-start | bytes 393224 | tf_op jit(solution)/shard_map/ppermute | solution.py:40
  4.9 8.0 %collective-permute-start.10 = (bf16[2,128,256]{2,1,0:T(8,128)(2,1)S(1)}, bf16[2,128,256]{2,1,0:T(8,128)(2,1)S(1)}, u32[]{:S(2)}, u32[]{:S(2)}) collective-permute-start(bf16[2,128,256]{2,1,0:T(8,128)(2,1)S(1)} %get-tuple-element.58), channel_id=1, source_target_pairs={{0,16},{1,17},{2,18},{3,19},{4,20},{5,21},{6,22},{7,23},{8,24},{9,... | collective-permute-start | bytes 393224 | tf_op jit(solution)/shard_map/ppermute | solution.py:494
  7.5 6.6 %collective-permute-start.11 = (bf16[2,128,256]{2,1,0:T(8,128)(2,1)S(1)}, bf16[2,128,256]{2,1,0:T(8,128)(2,1)S(1)}, u32[]{:S(2)}, u32[]{:S(2)}) collective-permute-start(bf16[2,128,256]{2,1,0:T(8,128)(2,1)S(1)} %get-tuple-element.59), channel_id=1, source_target_pairs={{0,17},{1,16},{2,19},{3,18},{4,21},{5,20},{6,23},{7,22},{8,25},{9,... | collective-permute-start | bytes 393224 | tf_op jit(solution)/shard_map/ppermute | solution.py:495
  8.5 10.4 %collective-permute-start.2 = (bf16[5,128,256]{2,1,0:T(8,128)(2,1)S(1)}, bf16[5,128,256]{2,1,0:T(8,128)(2,1)S(1)}, u32[]{:S(2)}, u32[]{:S(2)}) collective-permute-start(bf16[5,128,256]{2,1,0:T(8,128)(2,1)S(1)} %pad_maximum_fusion.refs_0_), channel_id=1, source_target_pairs={{0,8},{1,9},{2,10},{3,11},{4,0},{5,1},{6,2},{7,3},{8,12},{9,13},{1... | collective-permute-start | bytes 983048 | tf_op jit(solution)/shard_map/ppermute | solution.py:46
  11.3 9.7 %collective-permute-start.1 = (bf16[5,128,256]{2,1,0:T(8,128)(2,1)S(1)}, bf16[5,128,256]{2,1,0:T(8,128)(2,1)S(1)}, u32[]{:S(2)}, u32[]{:S(2)}) collective-permute-start(bf16[5,128,256]{2,1,0:T(8,128)(2,1)S(1)} %pad_maximum_fusion.refs_0_), channel_id=1, source_target_pairs={{0,2},{1,3},{2,0},{3,1},{4,6},{5,7},{6,4},{7,5},{8,10},{9,11},{10,... | collective-permute-start | bytes 983048 | tf_op jit(solution)/shard_map/ppermute | solution.py:40
  12.9 55.2 %collective-permute-start.8 = (bf16[32,128,256]{2,1,0:T(8,128)(2,1)}, bf16[32,128,256]{2,1,0:T(8,128)(2,1)S(1)}, u32[]{:S(2)}, u32[]{:S(2)}) collective-permute-start(bf16[32,128,256]{2,1,0:T(8,128)(2,1)} %rot_mine.1), channel_id=1, source_target_pairs={{0,1},{1,0},{2,3},{3,2},{4,5},{5,4},{6,7},{7,6},{8,9},{9,8},{10,11... | collective-permute-start | bytes 6291464 | tf_op jit(solution)/shard_map/ppermute | solution.py:40
  21.0 18.5 %collective-permute-start.4 = (bf16[5,128,256]{2,1,0:T(8,128)(2,1)S(1)}, bf16[5,128,256]{2,1,0:T(8,128)(2,1)S(1)}, u32[]{:S(2)}, u32[]{:S(2)}) collective-permute-start(bf16[5,128,256]{2,1,0:T(8,128)(2,1)S(1)} %collective-permute-done.2.refs_1_), channel_id=1, source_target_pairs={{0,8},{1,9},{2,10},{3,11},{4,0},{5,1},{6,2},{7,3},{8,12},{9,13},{1... | collective-permute-start | bytes 983048 | tf_op jit(solution)/shard_map/ppermute | solution.py:46
  22.6 16.9 %collective-permute-start.3 = (bf16[5,128,256]{2,1,0:T(8,128)(2,1)S(1)}, bf16[5,128,256]{2,1,0:T(8,128)(2,1)S(1)}, u32[]{:S(2)}, u32[]{:S(2)}) collective-permute-start(bf16[5,128,256]{2,1,0:T(8,128)(2,1)S(1)} %collective-permute-done.2.refs_1_), channel_id=1, source_target_pairs={{0,2},{1,3},{2,0},{3,1},{4,6},{5,7},{6,4},{7,5},{8,10},{9,11},{10,... | collective-permute-start | bytes 983048 | tf_op jit(solution)/shard_map/ppermute | solution.py:40
  24.1 11.3 %collective-permute-start.14 = (bf16[4,128,256]{2,1,0:T(8,128)(2,1)S(1)}, bf16[4,128,256]{2,1,0:T(8,128)(2,1)S(1)}, u32[]{:S(2)}, u32[]{:S(2)}) collective-permute-start(bf16[4,128,256]{2,1,0:T(8,128)(2,1)S(1)} %pad_maximum_fusion.1.refs_0_.refs_1_), channel_id=1, source_target_pairs={{0,8},{1,9},{2,10},{3,11},{4,0},{5,1},{6,2},{7,3},{8,12},{9,13},{1... | collective-permute-start | bytes 786440 | tf_op jit(solution)/shard_map/ppermute | solution.py:46
  24.6 12.2 %collective-permute-start.13 = (bf16[4,128,256]{2,1,0:T(8,128)(2,1)S(1)}, bf16[4,128,256]{2,1,0:T(8,128)(2,1)S(1)}, u32[]{:S(2)}, u32[]{:S(2)}) collective-permute-start(bf16[4,128,256]{2,1,0:T(8,128)(2,1)S(1)} %pad_maximum_fusion.1.refs_0_.refs_1_), channel_id=1, source_target_pairs={{0,2},{1,3},{2,0},{3,1},{4,6},{5,7},{6,4},{7,5},{8,10},{9,11},{10,... | collective-permute-start | bytes 786440 | tf_op jit(solution)/shard_map/ppermute | solution.py:40
  36.8 14.6 %collective-permute-start.16 = (bf16[4,128,256]{2,1,0:T(8,128)(2,1)S(1)}, bf16[4,128,256]{2,1,0:T(8,128)(2,1)S(1)}, u32[]{:S(2)}, u32[]{:S(2)}) collective-permute-start(bf16[4,128,256]{2,1,0:T(8,128)(2,1)S(1)} %collective-permute-done.14.refs_1_), channel_id=1, source_target_pairs={{0,8},{1,9},{2,10},{3,11},{4,0},{5,1},{6,2},{7,3},{8,12},{9,13},{1... | collective-permute-start | bytes 786440 | tf_op jit(solution)/shard_map/ppermute | solution.py:46
  38.0 13.4 %collective-permute-start.15 = (bf16[4,128,256]{2,1,0:T(8,128)(2,1)S(1)}, bf16[4,128,256]{2,1,0:T(8,128)(2,1)S(1)}, u32[]{:S(2)}, u32[]{:S(2)}) collective-permute-start(bf16[4,128,256]{2,1,0:T(8,128)(2,1)S(1)} %collective-permute-done.14.refs_1_), channel_id=1, source_target_pairs={{0,2},{1,3},{2,0},{3,1},{4,6},{5,7},{6,4},{7,5},{8,10},{9,11},{10,... | collective-permute-start | bytes 786440 | tf_op jit(solution)/shard_map/ppermute | solution.py:40
  39.5 10.5 %collective-permute-start.6 = (bf16[5,128,256]{2,1,0:T(8,128)(2,1)S(1)}, bf16[5,128,256]{2,1,0:T(8,128)(2,1)S(1)}, u32[]{:S(2)}, u32[]{:S(2)}) collective-permute-start(bf16[5,128,256]{2,1,0:T(8,128)(2,1)S(1)} %collective-permute-done.4.refs_2_), channel_id=1, source_target_pairs={{0,8},{1,9},{2,10},{3,11},{4,0},{5,1},{6,2},{7,3},{8,12},{9,13},{1... | collective-permute-start | bytes 983048 | tf_op jit(solution)/shard_map/ppermute | solution.py:46
  40.1 11.1 %collective-permute-start.5 = (bf16[5,128,256]{2,1,0:T(8,128)(2,1)S(1)}, bf16[5,128,256]{2,1,0:T(8,128)(2,1)S(1)}, u32[]{:S(2)}, u32[]{:S(2)}) collective-permute-start(bf16[5,128,256]{2,1,0:T(8,128)(2,1)S(1)} %collective-permute-done.4.refs_2_), channel_id=1, source_target_pairs={{0,2},{1,3},{2,0},{3,1},{4,6},{5,7},{6,4},{7,5},{8,10},{9,11},{10,... | collective-permute-start | bytes 983048 | tf_op jit(solution)/shard_map/ppermute | solution.py:40
  51.2 23.1 %copy-start.1 = (bf16[32,128,256]{2,1,0:T(8,128)(2,1)S(1)}, bf16[32,128,256]{2,1,0:T(8,128)(2,1)}, u32[]{:S(2)}) copy-start(bf16[32,128,256]{2,1,0:T(8,128)(2,1)} %rot_mine.1) | copy-start | bytes 6291460
  51.3 16.7 %collective-permute-start.7 = (bf16[7,128,256]{2,1,0:T(8,128)(2,1)S(1)}, bf16[7,128,256]{2,1,0:T(8,128)(2,1)S(1)}, u32[]{:S(2)}, u32[]{:S(2)}) collective-permute-start(bf16[7,128,256]{2,1,0:T(8,128)(2,1)S(1)} %slice_dynamic-update-slice_fusion), channel_id=1, source_target_pairs={{0,1},{1,0},{2,3},{3,2},{4,5},{5,4},{6,7},{7,6},{8,9},{9,8},{10,11... | collective-permute-start | bytes 1376264 | tf_op jit(solution)/shard_map/ppermute | solution.py:40
  51.4 8.7 %collective-permute-start.18 = (bf16[4,128,256]{2,1,0:T(8,128)(2,1)S(1)}, bf16[4,128,256]{2,1,0:T(8,128)(2,1)S(1)}, u32[]{:S(2)}, u32[]{:S(2)}) collective-permute-start(bf16[4,128,256]{2,1,0:T(8,128)(2,1)S(1)} %collective-permute-done.16.refs_2_), channel_id=1, source_target_pairs={{0,8},{1,9},{2,10},{3,11},{4,0},{5,1},{6,2},{7,3},{8,12},{9,13},{1... | collective-permute-start | bytes 786440 | tf_op jit(solution)/shard_map/ppermute | solution.py:46
  52.6 9.2 %collective-permute-start.17 = (bf16[4,128,256]{2,1,0:T(8,128)(2,1)S(1)}, bf16[4,128,256]{2,1,0:T(8,128)(2,1)S(1)}, u32[]{:S(2)}, u32[]{:S(2)}) collective-permute-start(bf16[4,128,256]{2,1,0:T(8,128)(2,1)S(1)} %collective-permute-done.16.refs_2_), channel_id=1, source_target_pairs={{0,2},{1,3},{2,0},{3,1},{4,6},{5,7},{6,4},{7,5},{8,10},{9,11},{10,... | collective-permute-start | bytes 786440 | tf_op jit(solution)/shard_map/ppermute | solution.py:40
  54.2 13.8 %collective-permute-start.9 = (bf16[5,128,256]{2,1,0:T(8,128)(2,1)S(1)}, bf16[5,128,256]{2,1,0:T(8,128)(2,1)S(1)}, u32[]{:S(2)}, u32[]{:S(2)}) collective-permute-start(bf16[5,128,256]{2,1,0:T(8,128)(2,1)S(1)} %collective-permute-done.6.refs_3_), channel_id=1, source_target_pairs={{0,2},{1,3},{2,0},{3,1},{4,6},{5,7},{6,4},{7,5},{8,10},{9,11},{10,... | collective-permute-start | bytes 983048 | tf_op jit(solution)/shard_map/ppermute | solution.py:40
  61.8 10.3 %collective-permute-start.19 = (bf16[4,128,256]{2,1,0:T(8,128)(2,1)S(1)}, bf16[4,128,256]{2,1,0:T(8,128)(2,1)S(1)}, u32[]{:S(2)}, u32[]{:S(2)}) collective-permute-start(bf16[4,128,256]{2,1,0:T(8,128)(2,1)S(1)} %collective-permute-done.17.refs_6_), channel_id=1, source_target_pairs={{0,8},{1,9},{2,10},{3,11},{4,0},{5,1},{6,2},{7,3},{8,12},{9,13},{1... | collective-permute-start | bytes 786440 | tf_op jit(solution)/shard_map/ppermute | solution.py:46
  68.0 1.3 collective-permute-start.12
  69.3 19.2 %copy-start = (bf16[32,128,2048]{2,1,0:T(8,128)(2,1)S(1)}, bf16[32,128,2048]{2,1,0:T(8,128)(2,1)}, u32[]{:S(2)}) copy-start(bf16[32,128,2048]{2,1,0:T(8,128)(2,1)} %cholesky.1) | copy-start | bytes 50331652
  74.4 14.2 %copy-start.3 = (f32[8,32]{1,0:T(8,128)S(1)}, f32[8,32]{1,0:T(8,128)}, u32[]{:S(2)}) copy-start(f32[8,32]{1,0:T(8,128)} %fields.1) | copy-start | bytes 3076
  76.1 3.6 %collective-permute-start.22 = (f32[4,32]{1,0:T(4,128)S(1)}, f32[4,32]{1,0:T(4,128)S(1)}, u32[]{:S(2)}, u32[]{:S(2)}) collective-permute-start(f32[4,32]{1,0:T(4,128)S(1)} %shard_map.81), channel_id=1, source_target_pairs={{0,12},{1,13},{2,14},{3,15},{4,0},{5,1},{6,2},{7,3},{8,4},{9,5},{1... | collective-permute-start | bytes 1544 | tf_op jit(solution)/shard_map/ppermute | solution.py:40
  77.8 5.4 %collective-permute-start.21 = (f32[4,32]{1,0:T(4,128)S(1)}, f32[4,32]{1,0:T(4,128)S(1)}, u32[]{:S(2)}, u32[]{:S(2)}) collective-permute-start(f32[4,32]{1,0:T(4,128)S(1)} %shard_map.81), channel_id=1, source_target_pairs={{0,4},{1,5},{2,6},{3,7},{4,8},{5,9},{6,10},{7,11},{8,12},{9,13},{1... | collective-permute-start | bytes 1544 | tf_op jit(solution)/shard_map/ppermute | solution.py:40
  78.1 5.1 %collective-permute-start.20 = (f32[4,32]{1,0:T(4,128)S(1)}, f32[4,32]{1,0:T(4,128)S(1)}, u32[]{:S(2)}, u32[]{:S(2)}) collective-permute-start(f32[4,32]{1,0:T(4,128)S(1)} %shard_map.81), channel_id=1, source_target_pairs={{0,8},{1,9},{2,10},{3,11},{4,12},{5,13},{6,14},{7,15},{8,0},{9,1},... | collective-permute-start | bytes 1544 | tf_op jit(solution)/shard_map/ppermute | solution.py:40
  83.2 3.1 %collective-permute-start.25 = (f32[4,32]{1,0:T(4,128)S(1)}, f32[4,32]{1,0:T(4,128)S(1)}, u32[]{:S(2)}, u32[]{:S(2)}) collective-permute-start(f32[4,32]{1,0:T(4,128)S(1)} %add_add_fusion.mine), channel_id=1, source_target_pairs={{0,3},{1,2},{2,1},{3,0},{4,7},{5,6},{6,5},{7,4},{8,11},{9,10},{10,... | collective-permute-start | bytes 1544 | tf_op jit(solution)/shard_map/ppermute | solution.py:40
  83.3 3.0 %collective-permute-start.24 = (f32[4,32]{1,0:T(4,128)S(1)}, f32[4,32]{1,0:T(4,128)S(1)}, u32[]{:S(2)}, u32[]{:S(2)}) collective-permute-start(f32[4,32]{1,0:T(4,128)S(1)} %add_add_fusion.mine), channel_id=1, source_target_pairs={{0,1},{1,0},{2,3},{3,2},{4,5},{5,4},{6,7},{7,6},{8,9},{9,8},{10,11... | collective-permute-start | bytes 1544 | tf_op jit(solution)/shard_map/ppermute | solution.py:40
  84.9 3.6 %collective-permute-start.23 = (f32[4,32]{1,0:T(4,128)S(1)}, f32[4,32]{1,0:T(4,128)S(1)}, u32[]{:S(2)}, u32[]{:S(2)}) collective-permute-start(f32[4,32]{1,0:T(4,128)S(1)} %add_add_fusion.mine), channel_id=1, source_target_pairs={{0,2},{1,3},{2,0},{3,1},{4,6},{5,7},{6,4},{7,5},{8,10},{9,11},{10,... | collective-permute-start | bytes 1544 | tf_op jit(solution)/shard_map/ppermute | solution.py:40
  91.7 2.7 %collective-permute-start.26 = (bf16[4,64,2048]{2,1,0:T(8,128)(2,1)S(1)}, bf16[4,64,2048]{2,1,0:T(8,128)(2,1)S(1)}, u32[]{:S(2)}, u32[]{:S(2)}) collective-permute-start(bf16[4,64,2048]{2,1,0:T(8,128)(2,1)S(1)} %get-tuple-element.70), channel_id=1, source_target_pairs={{0,1},{1,0},{2,3},{3,2},{4,5},{5,4},{6,7},{7,6},{8,9},{9,8},{10,11... | collective-permute-start | bytes 3145736 | tf_op jit(solution)/shard_map/ppermute | solution.py:40
  91.8 4.1 %collective-permute-start.27 = (bf16[4,64,2048]{2,1,0:T(8,128)(2,1)S(1)}, bf16[4,64,2048]{2,1,0:T(8,128)(2,1)S(1)}, u32[]{:S(2)}, u32[]{:S(2)}) collective-permute-start(bf16[4,64,2048]{2,1,0:T(8,128)(2,1)S(1)} %get-tuple-element.71), channel_id=1, source_target_pairs={{0,1},{1,0},{2,3},{3,2},{4,5},{5,4},{6,7},{7,6},{8,9},{9,8},{10,11... | collective-permute-start | bytes 3145736 | tf_op jit(solution)/shard_map/ppermute | solution.py:40
  93.0 9.2 %collective-permute-start.29 = (bf16[4,128,256]{2,1,0:T(8,128)(2,1)S(1)}, bf16[4,128,256]{2,1,0:T(8,128)(2,1)S(1)}, u32[]{:S(2)}, u32[]{:S(2)}) collective-permute-start(bf16[4,128,256]{2,1,0:T(8,128)(2,1)S(1)} %get-tuple-element.76.refs_3_), channel_id=1, source_target_pairs={{0,8},{1,9},{2,10},{3,11},{4,0},{5,1},{6,2},{7,3},{8,12},{9,13},{1... | collective-permute-start | bytes 786440 | tf_op jit(solution)/shard_map/ppermute | solution.py:46
  93.4 9.2 %collective-permute-start.28 = (bf16[4,128,256]{2,1,0:T(8,128)(2,1)S(1)}, bf16[4,128,256]{2,1,0:T(8,128)(2,1)S(1)}, u32[]{:S(2)}, u32[]{:S(2)}) collective-permute-start(bf16[4,128,256]{2,1,0:T(8,128)(2,1)S(1)} %get-tuple-element.76.refs_3_), channel_id=1, source_target_pairs={{0,2},{1,3},{2,0},{3,1},{4,6},{5,7},{6,4},{7,5},{8,10},{9,11},{10,... | collective-permute-start | bytes 786440 | tf_op jit(solution)/shard_map/ppermute | solution.py:40
  96.7 11.2 %collective-permute-start.36 = (bf16[4,128,256]{2,1,0:T(8,128)(2,1)S(1)}, bf16[4,128,256]{2,1,0:T(8,128)(2,1)S(1)}, u32[]{:S(2)}, u32[]{:S(2)}) collective-permute-start(bf16[4,128,256]{2,1,0:T(8,128)(2,1)S(1)} %get-tuple-element.83.refs_11_), channel_id=1, source_target_pairs={{0,8},{1,9},{2,10},{3,11},{4,0},{5,1},{6,2},{7,3},{8,12},{9,13},{1... | collective-permute-start | bytes 786440 | tf_op jit(solution)/shard_map/ppermute | solution.py:46
  97.8 10.4 %collective-permute-start.35 = (bf16[4,128,256]{2,1,0:T(8,128)(2,1)S(1)}, bf16[4,128,256]{2,1,0:T(8,128)(2,1)S(1)}, u32[]{:S(2)}, u32[]{:S(2)}) collective-permute-start(bf16[4,128,256]{2,1,0:T(8,128)(2,1)S(1)} %get-tuple-element.83.refs_11_), channel_id=1, source_target_pairs={{0,2},{1,3},{2,0},{3,1},{4,6},{5,7},{6,4},{7,5},{8,10},{9,11},{10,... | collective-permute-start | bytes 786440 | tf_op jit(solution)/shard_map/ppermute | solution.py:40
  102.6 10.9 %collective-permute-start.31 = (bf16[4,128,256]{2,1,0:T(8,128)(2,1)S(1)}, bf16[4,128,256]{2,1,0:T(8,128)(2,1)S(1)}, u32[]{:S(2)}, u32[]{:S(2)}) collective-permute-start(bf16[4,128,256]{2,1,0:T(8,128)(2,1)S(1)} %collective-permute-done.29.refs_4_), channel_id=1, source_target_pairs={{0,8},{1,9},{2,10},{3,11},{4,0},{5,1},{6,2},{7,3},{8,12},{9,13},{1... | collective-permute-start | bytes 786440 | tf_op jit(solution)/shard_map/ppermute | solution.py:46
  105.7 8.2 %collective-permute-start.30 = (bf16[4,128,256]{2,1,0:T(8,128)(2,1)S(1)}, bf16[4,128,256]{2,1,0:T(8,128)(2,1)S(1)}, u32[]{:S(2)}, u32[]{:S(2)}) collective-permute-start(bf16[4,128,256]{2,1,0:T(8,128)(2,1)S(1)} %collective-permute-done.29.refs_4_), channel_id=1, source_target_pairs={{0,2},{1,3},{2,0},{3,1},{4,6},{5,7},{6,4},{7,5},{8,10},{9,11},{10,... | collective-permute-start | bytes 786440 | tf_op jit(solution)/shard_map/ppermute | solution.py:40
  108.2 10.9 %collective-permute-start.38 = (bf16[4,128,256]{2,1,0:T(8,128)(2,1)S(1)}, bf16[4,128,256]{2,1,0:T(8,128)(2,1)S(1)}, u32[]{:S(2)}, u32[]{:S(2)}) collective-permute-start(bf16[4,128,256]{2,1,0:T(8,128)(2,1)S(1)} %collective-permute-done.36.refs_12_), channel_id=1, source_target_pairs={{0,8},{1,9},{2,10},{3,11},{4,0},{5,1},{6,2},{7,3},{8,12},{9,13},{1... | collective-permute-start | bytes 786440 | tf_op jit(solution)/shard_map/ppermute | solution.py:46
  111.3 8.2 %collective-permute-start.37 = (bf16[4,128,256]{2,1,0:T(8,128)(2,1)S(1)}, bf16[4,128,256]{2,1,0:T(8,128)(2,1)S(1)}, u32[]{:S(2)}, u32[]{:S(2)}) collective-permute-start(bf16[4,128,256]{2,1,0:T(8,128)(2,1)S(1)} %collective-permute-done.36.refs_12_), channel_id=1, source_target_pairs={{0,2},{1,3},{2,0},{3,1},{4,6},{5,7},{6,4},{7,5},{8,10},{9,11},{10,... | collective-permute-start | bytes 786440 | tf_op jit(solution)/shard_map/ppermute | solution.py:40
  113.9 10.8 %collective-permute-start.33 = (bf16[4,128,256]{2,1,0:T(8,128)(2,1)S(1)}, bf16[4,128,256]{2,1,0:T(8,128)(2,1)S(1)}, u32[]{:S(2)}, u32[]{:S(2)}) collective-permute-start(bf16[4,128,256]{2,1,0:T(8,128)(2,1)S(1)} %collective-permute-done.31.refs_5_), channel_id=1, source_target_pairs={{0,8},{1,9},{2,10},{3,11},{4,0},{5,1},{6,2},{7,3},{8,12},{9,13},{1... | collective-permute-start | bytes 786440 | tf_op jit(solution)/shard_map/ppermute | solution.py:46
  116.9 8.2 %collective-permute-start.32 = (bf16[4,128,256]{2,1,0:T(8,128)(2,1)S(1)}, bf16[4,128,256]{2,1,0:T(8,128)(2,1)S(1)}, u32[]{:S(2)}, u32[]{:S(2)}) collective-permute-start(bf16[4,128,256]{2,1,0:T(8,128)(2,1)S(1)} %collective-permute-done.31.refs_5_), channel_id=1, source_target_pairs={{0,2},{1,3},{2,0},{3,1},{4,6},{5,7},{6,4},{7,5},{8,10},{9,11},{10,... | collective-permute-start | bytes 786440 | tf_op jit(solution)/shard_map/ppermute | solution.py:40
  119.5 9.9 %collective-permute-start.40 = (bf16[4,128,256]{2,1,0:T(8,128)(2,1)S(1)}, bf16[4,128,256]{2,1,0:T(8,128)(2,1)S(1)}, u32[]{:S(2)}, u32[]{:S(2)}) collective-permute-start(bf16[4,128,256]{2,1,0:T(8,128)(2,1)S(1)} %collective-permute-done.38.refs_13_), channel_id=1, source_target_pairs={{0,8},{1,9},{2,10},{3,11},{4,0},{5,1},{6,2},{7,3},{8,12},{9,13},{1... | collective-permute-start | bytes 786440 | tf_op jit(solution)/shard_map/ppermute | solution.py:46
  122.5 9.2 %collective-permute-start.39 = (bf16[4,128,256]{2,1,0:T(8,128)(2,1)S(1)}, bf16[4,128,256]{2,1,0:T(8,128)(2,1)S(1)}, u32[]{:S(2)}, u32[]{:S(2)}) collective-permute-start(bf16[4,128,256]{2,1,0:T(8,128)(2,1)S(1)} %collective-permute-done.38.refs_13_), channel_id=1, source_target_pairs={{0,2},{1,3},{2,0},{3,1},{4,6},{5,7},{6,4},{7,5},{8,10},{9,11},{10,... | collective-permute-start | bytes 786440 | tf_op jit(solution)/shard_map/ppermute | solution.py:40
  125.2 10.0 %collective-permute-start.34 = (bf16[4,128,256]{2,1,0:T(8,128)(2,1)S(1)}, bf16[4,128,256]{2,1,0:T(8,128)(2,1)S(1)}, u32[]{:S(2)}, u32[]{:S(2)}) collective-permute-start(bf16[4,128,256]{2,1,0:T(8,128)(2,1)S(1)} %collective-permute-done.33.refs_6_), channel_id=1, source_target_pairs={{0,2},{1,3},{2,0},{3,1},{4,6},{5,7},{6,4},{7,5},{8,10},{9,11},{10,... | collective-permute-start | bytes 786440 | tf_op jit(solution)/shard_map/ppermute | solution.py:40
  131.8 6.4 %collective-permute-start.41 = (bf16[4,128,256]{2,1,0:T(8,128)(2,1)S(1)}, bf16[4,128,256]{2,1,0:T(8,128)(2,1)S(1)}, u32[]{:S(2)}, u32[]{:S(2)}) collective-permute-start(bf16[4,128,256]{2,1,0:T(8,128)(2,1)S(1)} %collective-permute-done.39.refs_17_), channel_id=1, source_target_pairs={{0,8},{1,9},{2,10},{3,11},{4,0},{5,1},{6,2},{7,3},{8,12},{9,13},{1... | collective-permute-start | bytes 786440 | tf_op jit(solution)/shard_map/ppermute | solution.py:46
  139.2 2.1 %collective-permute-start.42 = (bf16[4,128,256]{2,1,0:T(8,128)(2,1)S(1)}, bf16[4,128,256]{2,1,0:T(8,128)(2,1)S(1)}, u32[]{:S(2)}, u32[]{:S(2)}) collective-permute-start(bf16[4,128,256]{2,1,0:T(8,128)(2,1)S(1)} %get-tuple-element.90), channel_id=1, source_target_pairs={{0,1},{1,0},{2,3},{3,2},{4,5},{5,4},{6,7},{7,6},{8,9},{9,8},{10,11... | collective-permute-start | bytes 786440 | tf_op jit(solution)/shard_map/ppermute | solution.py:40

commit v8 on v7

--- a/solution.py
+++ b/solution.py
@@ -55,55 +55,53 @@
 
 
 class Stream:
-    def __init__(self, layout, piece, last_along_z=False):
+    def __init__(self, layout, piece):
         self.layout = layout
         self.ring = [piece]
         self.across = []
-        self.last_along_z = last_along_z
+        self.last = []
+
+    def moves(self):
+        latest = self.ring[-1]
+        if len(self.ring) < self.layout.z:
+            return [self.layout.shift(latest, dy=1), self.layout.step(latest)]
+        half = (latest.shape[0] + 1) // 2
+        return [
+            self.layout.shift(latest[:half], dy=1),
+            self.layout.step(self.across[-1][half:]),
+        ]
+
+    def accept(self, moved):
+        if len(self.ring) < self.layout.z:
+            self.across.append(moved[0])
+            self.ring.append(moved[1])
+        else:
+            self.last = moved
 
     def advance(self, anchors=()):
-        latest = self.ring[-1]
-        last = len(self.ring) == self.layout.z
-        if last and self.last_along_z:
-            moved = [self.layout.step(self.across[-1])]
-        else:
-            moved = [self.layout.shift(latest, dy=1)]
-        if not last:
-            moved.append(self.layout.step(latest))
-        if anchors or not last:
+        moved = self.moves()
+        if anchors or len(self.ring) < self.layout.z:
             anchors, moved = lax.optimization_barrier((anchors, moved))
-        self.across.append(moved[0])
-        self.ring.extend(moved[1:])
+        self.accept(moved)
         return anchors
 
     def pieces(self):
-        ring = [(array, steps, 0) for steps, array in enumerate(self.ring)]
-        return ring + [(array, steps, 1) for steps, array in enumerate(self.across)]
-
-
-def transpose_kernel(layout, places, *refs):
-    arrays, theirs, (out, buffer) = refs[: len(places)], refs[len(places) : -2], refs[-2:]
-    b = lax.rem(lax.axis_index("chol"), 2)
-    slabs = [(part, at) for part in theirs for at in range(part.shape[0])]
-    for array, (steps, dy), (part, at) in zip(arrays, places, slabs):
-        chip = layout.origin(steps, dy)
-        buffer[chip, b] = array[array.shape[0] - 1]
-        buffer[chip, 1 - b] = part[at]
-    out[...] = buffer[...].reshape(-1, buffer.shape[-1]).T
-
-
-def transposed(layout, stream, theirs):
-    arrays = [array for array, *_ in stream.pieces()]
-    places = [place for _, *place in stream.pieces()]
-    _, rows, electrons = arrays[0].shape
-    return pl.pallas_call(
-        functools.partial(transpose_kernel, layout, places),
-        out_shape=jax.ShapeDtypeStruct((electrons, layout.chol * rows), BF16),
-        in_specs=vmem_specs(len(arrays) + len(theirs)),
-        out_specs=pl.BlockSpec(memory_space=pltpu.VMEM),
-        scratch_shapes=[pltpu.VMEM((layout.chol // 2, 2, rows, electrons), BF16)],
-        compiler_params=params(8),
-    )(*arrays, *theirs)
+        ring = [(array, 0, steps, 0) for steps, array in enumerate(self.ring)]
+        across = [(array, 0, steps, 1) for steps, array in enumerate(self.across)]
+        lower, upper = self.last
+        steps = self.layout.z - 1
+        return ring + across + [(lower, 0, steps, 1), (upper, lower.shape[0], steps, 1)]
+
+
+def operands(streams):
+    arrays, slabs = [], []
+    for stream in streams:
+        slabs.append([])
+        for array, first, steps, dy in stream.pieces():
+            for at in range(array.shape[0]):
+                slabs[-1].append((len(arrays), at, first + at, steps, dy))
+            arrays.append(array)
+    return arrays, slabs
 
 
 def product(left, right):
@@ -128,70 +126,51 @@
     return estimates
 
 
-def inverse_kernel(layout, places, trial, *refs):
-    pieces, (full, out) = refs[:-2], refs[-2:]
-    count = out.shape[0]
+def bias_kernel(layout, slabs, counts, rot_mine, rot_theirs, early, late, *refs):
+    fulls, (out, buffer, turned, greens) = refs[-4 - len(counts) : -4], refs[-4:]
+    pieces = refs[: -4 - len(counts)]
+    vectors, rows, electrons = rot_mine.shape
+    index = lax.axis_index("chol")
+    chip, b = index // 2, lax.rem(index, 2)
+
+    theirs = [(early, at) for at in range(early.shape[0])] + [(late, 0)]
+    trial = [slab for slab in slabs[0] if slab[2] == 2 * counts[0]]
+    for (operand, at, _, steps, dy), (part, place) in zip(trial, theirs):
+        origin = layout.origin(steps, dy)
+        buffer[origin, b] = pieces[operand][at]
+        buffer[origin, 1 - b] = part[place]
+    turned[...] = buffer[...].reshape(-1, electrons).T
+
     matrices = []
-    for walker in range(count):
-        for piece, (steps, dy) in zip(pieces, places):
-            chip = layout.origin(steps, dy)
-            for block in range(2):
-                full[walker, chip, block] = piece[block * count + walker]
-        rows = full[walker].reshape(-1, full.shape[-1])
-        matrices.append(jnp.dot(trial[...], rows, preferred_element_type=F32))
-    for walker, inverse in enumerate(newton_inverses(matrices)):
-        out[walker] = inverse.astype(out.dtype)
-
-
-def inverses_of(layout, trial, stream, count):
-    arrays = [array for array, *_ in stream.pieces()]
-    places = [place for _, *place in stream.pieces()]
-    _, rows, electrons = arrays[0].shape
-    return pl.pallas_call(
-        functools.partial(inverse_kernel, layout, places),
-        out_shape=[
-            jax.ShapeDtypeStruct((count, layout.chol // 2, 2, rows, electrons), BF16),
-            jax.ShapeDtypeStruct((count, electrons, electrons), BF16),
-        ],
-        in_specs=vmem_specs(1 + len(arrays)),
-        out_specs=vmem_specs(2),
-        compiler_params=params(8),
-        cost_estimate=pl.CostEstimate(
-            flops=2 * count * electrons**2 * (trial.shape[1] + 6 * (ITERS - 1) * electrons),
-            bytes_accessed=4 * (count + 1) * trial.shape[1] * electrons,
-            transcendentals=0,
-        ),
-    )(trial, *arrays)
-
-
-def bias_kernel(sizes, rot_mine, rot_theirs, *refs):
-    streams = len(sizes)
-    chunks, inverses, (out, greens) = refs[:streams], refs[streams : 2 * streams], refs[-2:]
-    vectors, rows, electrons = rot_mine.shape
-    b = lax.rem(lax.axis_index("chol"), 2)
-    count = 0
-    for chunk, inverse, size in zip(chunks, inverses, sizes):
-        for walker in range(size):
-            both = jnp.concatenate([chunk[walker], chunk[size + walker]], axis=0)
-            product = jnp.dot(both, inverse[walker], preferred_element_type=F32).astype(BF16)
-            greens[:, :, count] = product.reshape(2, rows // BLOCK, BLOCK, electrons)
-            count += 1
-    total = jnp.zeros((vectors * BLOCK, count * BLOCK), F32)
+    for full, count, stream in zip(fulls, counts, slabs):
+        for operand, at, slab, steps, dy in stream:
+            if slab < 2 * count:
+                full[slab % count, layout.origin(steps, dy), slab // count] = pieces[operand][at]
+        for walker in range(count):
+            columns = full[walker].reshape(-1, electrons)
+            matrices.append(jnp.dot(turned[...], columns, preferred_element_type=F32))
+    inverses = [inverse.astype(BF16) for inverse in newton_inverses(matrices)]
+
+    walkers = [(full, at) for full, count in zip(fulls, counts) for at in range(count)]
+    for number, (full, walker) in enumerate(walkers):
+        both = full[walker, chip].reshape(2 * rows, electrons)
+        green = jnp.dot(both, inverses[number], preferred_element_type=F32).astype(BF16)
+        greens[:, :, number] = green.reshape(2, rows // BLOCK, BLOCK, electrons)
+    width = len(walkers) * BLOCK
+    total = jnp.zeros((vectors * BLOCK, width), F32)
     for half, rot in ((b, rot_mine), (1 - b, rot_theirs)):
         for block in range(rows // BLOCK):
             total += lax.dot_general(
                 rot[:, block * BLOCK : (block + 1) * BLOCK, :].reshape(vectors * BLOCK, electrons),
-                greens[half, block].reshape(count * BLOCK, electrons),
+                greens[half, block].reshape(width, electrons),
                 (((1,), (1,)), ((), ())),
                 preferred_element_type=F32,
             )
     same = lax.rem(lax.broadcasted_iota(jnp.int32, total.shape, 0), BLOCK) == lax.rem(
         lax.broadcasted_iota(jnp.int32, total.shape, 1), BLOCK
     )
-    summed = jnp.sum(
-        jnp.where(same, total, 0.0).reshape(vectors, BLOCK, count * BLOCK), axis=1
-    )
-    shape = (count, count * BLOCK)
+    summed = jnp.sum(jnp.where(same, total, 0.0).reshape(vectors, BLOCK, width), axis=1)
+    shape = (len(walkers), width)
     pick = (
         lax.broadcasted_iota(jnp.int32, shape, 1) // BLOCK
         == lax.broadcasted_iota(jnp.int32, shape, 0)
@@ -201,23 +180,33 @@
     )
 
 
-def bias_of(chunks, inverses, rot_mine, rot_theirs):
+def bias_of(layout, streams, counts, early, late, rot_mine, rot_theirs):
+    arrays, slabs = operands(streams)
     vectors, rows, electrons = rot_mine.shape
-    sizes = [inverse.shape[0] for inverse in inverses]
-    count = sum(sizes)
-    return pl.pallas_call(
-        functools.partial(bias_kernel, sizes),
-        out_shape=jax.ShapeDtypeStruct((count, vectors), F32),
-        in_specs=vmem_specs(2 + 2 * len(sizes)),
-        out_specs=pl.BlockSpec(memory_space=pltpu.VMEM),
-        scratch_shapes=[pltpu.VMEM((2, rows // BLOCK, count, BLOCK, electrons), BF16)],
-        compiler_params=params(12),
+    chips = layout.chol // 2
+    total = sum(counts)
+    return pl.pallas_call(
+        functools.partial(bias_kernel, layout, slabs, counts),
+        out_shape=[
+            jax.ShapeDtypeStruct((count, chips, 2, rows, electrons), BF16) for count in counts
+        ]
+        + [jax.ShapeDtypeStruct((total, vectors), F32)],
+        in_specs=vmem_specs(4 + len(arrays)),
+        out_specs=vmem_specs(len(counts) + 1),
+        scratch_shapes=[
+            pltpu.VMEM((chips, 2, rows, electrons), BF16),
+            pltpu.VMEM((electrons, 2 * chips * rows), BF16),
+            pltpu.VMEM((2, rows // BLOCK, total, BLOCK, electrons), BF16),
+        ],
+        compiler_params=params(20),
         cost_estimate=pl.CostEstimate(
-            flops=4 * count * rows * electrons * (electrons + vectors * BLOCK),
-            bytes_accessed=4 * (vectors + count) * rows * electrons,
+            flops=2 * total * electrons**2 * (2 * chips * rows + 6 * (ITERS - 1) * electrons)
+            + 4 * total * rows * electrons * (electrons + vectors * BLOCK),
+            bytes_accessed=4 * (vectors + total) * rows * electrons
+            + 4 * (total + 1) * 2 * chips * rows * electrons,
             transcendentals=0,
         ),
-    )(rot_mine, rot_theirs, *chunks, *inverses)
+    )(rot_mine, rot_theirs, early, late, *arrays)
 
 
 def potential_kernel(order, fields, mine, mine_across, theirs, theirs_across, cholesky, *refs):
@@ -316,14 +305,14 @@
     )(*potential, *fulls)
 
 
-def second_kernel(layout, places, parts, *refs):
+def second_kernel(layout, slabs, parts, *refs):
     potential, base, pieces = refs[:parts], refs[parts], refs[parts + 1 : -2]
     out, full = refs[-2:]
     b = lax.rem(lax.axis_index("chol"), 2)
+    for block, stream in zip((b, 1 - b), slabs):
+        for operand, at, walker, steps, dy in stream:
+            full[walker, layout.origin(steps, dy), block] = pieces[operand][at]
     for walker in range(out.shape[0]):
-        for piece, (sibling, steps, dy) in zip(pieces, places):
-            block = 1 - b if sibling else b
-            full[walker, layout.origin(steps, dy), block] = piece[walker]
         rows = jnp.concatenate([part[walker] for part in potential], axis=0)
         columns = full[walker].reshape(-1, full.shape[-1])
         term = jnp.dot(rows, columns, preferred_element_type=F32)
@@ -331,15 +320,11 @@
 
 
 def second_of(layout, potential, base, streams):
-    arrays, places = [], []
-    for sibling, stream in enumerate(streams):
-        for array, steps, dy in stream.pieces():
-            arrays.append(array)
-            places.append((sibling, steps, dy))
+    arrays, slabs = operands(streams)
     orbitals = potential[0].shape[2]
     half, rows, electrons = base.shape
     return pl.pallas_call(
-        functools.partial(second_kernel, layout, places, len(potential)),
+        functools.partial(second_kernel, layout, slabs, len(potential)),
         out_shape=[
             jax.ShapeDtypeStruct((half, rows, electrons), BF16),
             jax.ShapeDtypeStruct((half, layout.chol // 2, 2, rows, electrons), BF16),
@@ -531,21 +516,20 @@
         jnp.concatenate([jnp.where(b == 0, own, other), jnp.where(b == 0, other, own), *extra])
         for (own, other), extra in zip(shares, ([trial[None]], []))
     ]
-    streams = [Stream(layout, chunks[0]), Stream(layout, chunks[1], last_along_z=True)]
+    streams = [Stream(layout, chunk) for chunk in chunks]
     rot_theirs = layout.shift(rotated, db=1)
-    for stage in range(layout.z):
-        if stage == layout.z - 1:
-            early = jnp.stack([array[-1] for array, *_ in streams[0].pieces()])
-            early, rot_theirs = streams[0].advance((layout.shift(early, db=1), rot_theirs))
-        else:
-            streams[0].advance()
-        streams[1].advance()
-    late = layout.shift(streams[0].across[-1][-1:], db=1)
-    turned = transposed(layout, streams[0], (early, late))
-    fulls, inverses = zip(
-        *[inverses_of(layout, turned, stream, size) for stream, size in zip(streams, sizes)]
-    )
-    total = bias_of(chunks, inverses, rotated, rot_theirs)
+    moved = lax.optimization_barrier([stream.moves() for stream in streams])
+    for stream, arrays in zip(streams, moved):
+        stream.accept(arrays)
+    for _ in range(layout.z - 2):
+        for stream in streams:
+            stream.advance()
+    slabs = [array[-1:] for array in (*streams[0].ring, *streams[0].across)]
+    early = layout.shift(jnp.concatenate(slabs), db=1)
+    late = layout.shift(early[layout.z - 1 : layout.z], dy=1)
+    early, rot_theirs = streams[0].advance((early, rot_theirs))
+    streams[1].advance()
+    *fulls, total = bias_of(layout, streams, sizes, early, late, rotated, rot_theirs)
     parts = [total] + [layout.shift(total, dz=dz) for dz in range(1, layout.z)]
     while len(parts) > 1:
         far = len(parts) // 2
@@ -556,7 +540,7 @@
 
     rounded, base = first_of([kept], fulls, 0)
     rounded_theirs, base_theirs = first_of(received, fulls, 1)
-    streams = [Stream(layout, rounded), Stream(layout, rounded_theirs, last_along_z=True)]
+    streams = [Stream(layout, rounded), Stream(layout, rounded_theirs)]
     for _ in range(layout.z):
         for stream in streams:
             stream.advance()

time: 143 us -> 147 us (1.028)
  local copies, waits for them, and re-layouts: 1.75 us -> 7.6 us
  waiting for transfers between devices: 75.4 us -> 71.6 us
  starting transfers between devices: 45.9 us -> 49.6 us
  Pallas kernels: 17.7 us -> 16.1 us
    ppermute x27 -> x29, starting transfers between devices: 18.7 us -> 24.5 us  [shift(): return lax.ppermute(array, 'chol', pairs)]
    unnamed x18, local copies, waits for them, and re-layouts: 1.74 us -> 7.5 us
    ppermute x14 -> x16, waiting for transfers between devices: 46.2 us -> 43.8 us  [step(): return lax.ppermute(array, 'chol', pairs)]
    ppermute x14 -> x16, starting transfers between devices: 24.6 us -> 22.4 us  [step(): return lax.ppermute(array, 'chol', pairs)]
    pallas_call x5 -> x2, Pallas kernels: 7.7 us -> 6.05 us  [the longest x1 4.93 us: bias_of(): pl.pallas_call(functools.partial(bias_kernel, layout, slabs, counts), out...]
    ppermute x27 -> x29, waiting for transfers between devices: 27.9 us -> 26.5 us  [shift(): return lax.ppermute(array, 'chol', pairs)]
  transfers between devices with their start and end apart: 43 -> 47, of which waited for: 31 -> 30; matrix products, arithmetic and copies ran while one was open for 1% -> 1% of each run, Pallas kernels for 4% -> 2%
where the time goes in v8:
time: 147 us
  waiting for transfers between devices  71.6 us (49%)
  starting transfers between devices  49.6 us (34%)
  Pallas kernels  16.1 us (11%)
  local copies, waits for them, and re-layouts  7.6 us (5%)
    ppermute x16, waiting for transfers between devices, step(): return lax.ppermute(array, 'chol', pairs)  43.8 us
    ppermute x29, waiting for transfers between devices, shift(): return lax.ppermute(array, 'chol', pairs)  26.5 us
    ppermute x29, starting transfers between devices, shift(): return lax.ppermute(array, 'chol', pairs)  24.5 us
    ppermute x16, starting transfers between devices, step(): return lax.ppermute(array, 'chol', pairs)  22.4 us
    unnamed x18, local copies, waits for them, and re-layouts  7.5 us
    pallas_call x1, Pallas kernels, bias_of(): pl.pallas_call(functools.partial(bias_kernel, layout, slabs, counts), out...  4.93 us
    pallas_call x1, Pallas kernels, potential_of(): pl.pallas_call(potential_kernel, out_shape=[jax.ShapeDtypeStruct((per_gro...  3.18 us
  transfers between devices with their start and end apart: 47, of which 30 were waited for; matrix products, arithmetic and copies ran while one was open for 1% of the time, Pallas kernels for 2%

profile of v8, /device:TPU:0, one launch (start us, length us, event | category | flops | bytes accessed | tf_op | source)
XLA Modules:
  0.0 146.8 jit_solution(4572476311499480606)
XLA Ops:
  0.6 1.0 copy-done.1
  2.3 2.0 %shard_map.77 = (bf16[2,128,256]{2,1,0:T(8,128)(2,1)S(1)}, bf16[2,128,256]{2,1,0:T(8,128)(2,1)S(1)}, bf16[2,128,256]{2,1,0:T(8,128)(2,1)S(1)}, bf16[2,128,256]{2,1,0:T(8,128)(2,1)S(1)}, s32[8]{0:T(128)S(1)}) custom-call(s32[16]{0:T(128)S(1)} %copy-done.3, bf16[8,128,256]{2,1,0:T(8,128)(2,1)S(1)} %copy-done.1), custom_call_target="tpu_custom_call" | custom-call | tf_op jit(solution)/shard_map/pallas_call | solution.py:450
  4.9 2.6 %collective-permute-start.3 = (bf16[2,128,256]{2,1,0:T(8,128)(2,1)S(1)}, bf16[2,128,256]{2,1,0:T(8,128)(2,1)S(1)}, u32[]{:S(2)}, u32[]{:S(2)}) collective-permute-start(bf16[2,128,256]{2,1,0:T(8,128)(2,1)S(1)} %get-tuple-element.51), channel_id=1, source_target_pairs={{0,16},{1,17},{2,18},{3,19},{4,20},{5,21},{6,22},{7,23},{8,24},{9,... | collective-permute-start | bytes 393224 | tf_op jit(solution)/shard_map/ppermute | solution.py:479
  7.6 0.9 pad_maximum_fusion.refs_0_
  8.5 2.9 %collective-permute-start.2 = (bf16[5,128,256]{2,1,0:T(8,128)(2,1)S(1)}, bf16[5,128,256]{2,1,0:T(8,128)(2,1)S(1)}, u32[]{:S(2)}, u32[]{:S(2)}) collective-permute-start(bf16[5,128,256]{2,1,0:T(8,128)(2,1)S(1)} %pad_maximum_fusion.refs_0_), channel_id=1, source_target_pairs={{0,8},{1,9},{2,10},{3,11},{4,0},{5,1},{6,2},{7,3},{8,12},{9,13},{1... | collective-permute-start | bytes 983048 | tf_op jit(solution)/shard_map/ppermute | solution.py:46
  11.3 1.5 %collective-permute-start.1 = (bf16[5,128,256]{2,1,0:T(8,128)(2,1)S(1)}, bf16[5,128,256]{2,1,0:T(8,128)(2,1)S(1)}, u32[]{:S(2)}, u32[]{:S(2)}) collective-permute-start(bf16[5,128,256]{2,1,0:T(8,128)(2,1)S(1)} %pad_maximum_fusion.refs_0_), channel_id=1, source_target_pairs={{0,2},{1,3},{2,0},{3,1},{4,6},{5,7},{6,4},{7,5},{8,10},{9,11},{10,... | collective-permute-start | bytes 983048 | tf_op jit(solution)/shard_map/ppermute | solution.py:40
  12.9 1.2 collective-permute-done.4
  14.2 2.7 %collective-permute-start.6 = (bf16[4,128,256]{2,1,0:T(8,128)(2,1)S(1)}, bf16[4,128,256]{2,1,0:T(8,128)(2,1)S(1)}, u32[]{:S(2)}, u32[]{:S(2)}) collective-permute-start(bf16[4,128,256]{2,1,0:T(8,128)(2,1)S(1)} %pad_maximum_fusion.1.refs_9_), channel_id=1, source_target_pairs={{0,8},{1,9},{2,10},{3,11},{4,0},{5,1},{6,2},{7,3},{8,12},{9,13},{1... | collective-permute-start | bytes 786440 | tf_op jit(solution)/shard_map/ppermute | solution.py:46
  16.9 1.5 %collective-permute-start.5 = (bf16[4,128,256]{2,1,0:T(8,128)(2,1)S(1)}, bf16[4,128,256]{2,1,0:T(8,128)(2,1)S(1)}, u32[]{:S(2)}, u32[]{:S(2)}) collective-permute-start(bf16[4,128,256]{2,1,0:T(8,128)(2,1)S(1)} %pad_maximum_fusion.1.refs_9_), channel_id=1, source_target_pairs={{0,2},{1,3},{2,0},{3,1},{4,6},{5,7},{6,4},{7,5},{8,10},{9,11},{10,... | collective-permute-start | bytes 786440 | tf_op jit(solution)/shard_map/ppermute | solution.py:40
  18.4 6.0 %collective-permute-done.6.refs_10_ = bf16[4,128,256]{2,1,0:T(8,128)(2,1)S(1)} collective-permute-done((bf16[4,128,256]{2,1,0:T(8,128)(2,1)S(1)}, bf16[4,128,256]{2,1,0:T(8,128)(2,1)S(1)}, u32[]{:S(2)}, u32[]{:S(2)}) %collective-permute-start.6) | collective-permute-done | bytes 262176 | tf_op jit(solution)/shard_map/ppermute | solution.py:46
  24.4 2.2 %collective-permute-done.5.refs_13_ = bf16[4,128,256]{2,1,0:T(8,128)(2,1)S(1)} collective-permute-done((bf16[4,128,256]{2,1,0:T(8,128)(2,1)S(1)}, bf16[4,128,256]{2,1,0:T(8,128)(2,1)S(1)}, u32[]{:S(2)}, u32[]{:S(2)}) %collective-permute-start.5) | collective-permute-done | bytes 262176 | tf_op jit(solution)/shard_map/ppermute | solution.py:40
  26.6 1.6 %collective-permute-start.8 = (bf16[5,128,256]{2,1,0:T(8,128)(2,1)S(1)}, bf16[5,128,256]{2,1,0:T(8,128)(2,1)S(1)}, u32[]{:S(2)}, u32[]{:S(2)}) collective-permute-start(bf16[5,128,256]{2,1,0:T(8,128)(2,1)S(1)} %collective-permute-done.2.refs_1_), channel_id=1, source_target_pairs={{0,8},{1,9},{2,10},{3,11},{4,0},{5,1},{6,2},{7,3},{8,12},{9,13},{1... | collective-permute-start | bytes 983048 | tf_op jit(solution)/shard_map/ppermute | solution.py:46
  28.2 1.5 %collective-permute-start.7 = (bf16[5,128,256]{2,1,0:T(8,128)(2,1)S(1)}, bf16[5,128,256]{2,1,0:T(8,128)(2,1)S(1)}, u32[]{:S(2)}, u32[]{:S(2)}) collective-permute-start(bf16[5,128,256]{2,1,0:T(8,128)(2,1)S(1)} %collective-permute-done.2.refs_1_), channel_id=1, source_target_pairs={{0,2},{1,3},{2,0},{3,1},{4,6},{5,7},{6,4},{7,5},{8,10},{9,11},{10,... | collective-permute-start | bytes 983048 | tf_op jit(solution)/shard_map/ppermute | solution.py:40
  30.7 6.6 %collective-permute-done.8.refs_2_ = bf16[5,128,256]{2,1,0:T(8,128)(2,1)S(1)} collective-permute-done((bf16[5,128,256]{2,1,0:T(8,128)(2,1)S(1)}, bf16[5,128,256]{2,1,0:T(8,128)(2,1)S(1)}, u32[]{:S(2)}, u32[]{:S(2)}) %collective-permute-start.8) | collective-permute-done | bytes 327712 | tf_op jit(solution)/shard_map/ppermute | solution.py:46
  37.3 1.6 %collective-permute-done.7.refs_5_ = bf16[5,128,256]{2,1,0:T(8,128)(2,1)S(1)} collective-permute-done((bf16[5,128,256]{2,1,0:T(8,128)(2,1)S(1)}, bf16[5,128,256]{2,1,0:T(8,128)(2,1)S(1)}, u32[]{:S(2)}, u32[]{:S(2)}) %collective-permute-start.7) | collective-permute-done | bytes 327712 | tf_op jit(solution)/shard_map/ppermute | solution.py:40
  38.9 0.9 collective-permute-start.10
  39.8 1.5 %collective-permute-start.9 = (bf16[5,128,256]{2,1,0:T(8,128)(2,1)S(1)}, bf16[5,128,256]{2,1,0:T(8,128)(2,1)S(1)}, u32[]{:S(2)}, u32[]{:S(2)}) collective-permute-start(bf16[5,128,256]{2,1,0:T(8,128)(2,1)S(1)} %collective-permute-done.8.refs_2_), channel_id=1, source_target_pairs={{0,2},{1,3},{2,0},{3,1},{4,6},{5,7},{6,4},{7,5},{8,10},{9,11},{10,... | collective-permute-start | bytes 983048 | tf_op jit(solution)/shard_map/ppermute | solution.py:40
  41.3 6.8 %collective-permute-done.10.refs_3_ = bf16[5,128,256]{2,1,0:T(8,128)(2,1)S(1)} collective-permute-done((bf16[5,128,256]{2,1,0:T(8,128)(2,1)S(1)}, bf16[5,128,256]{2,1,0:T(8,128)(2,1)S(1)}, u32[]{:S(2)}, u32[]{:S(2)}) %collective-permute-start.10) | collective-permute-done | bytes 327712 | tf_op jit(solution)/shard_map/ppermute | solution.py:46
  48.1 1.3 collective-permute-done.9.refs_6_
  49.6 1.2 collective-permute-start.19
  50.8 1.5 %collective-permute-start.18 = (bf16[4,128,256]{2,1,0:T(8,128)(2,1)S(1)}, bf16[4,128,256]{2,1,0:T(8,128)(2,1)S(1)}, u32[]{:S(2)}, u32[]{:S(2)}) collective-permute-start(bf16[4,128,256]{2,1,0:T(8,128)(2,1)S(1)} %collective-permute-done.17.refs_11_), channel_id=1, source_target_pairs={{0,2},{1,3},{2,0},{3,1},{4,6},{5,7},{6,4},{7,5},{8,10},{9,11},{10,... | collective-permute-start | bytes 786440 | tf_op jit(solution)/shard_map/ppermute | solution.py:40
  52.9 5.3 %collective-permute-done.19.refs_12_ = bf16[4,128,256]{2,1,0:T(8,128)(2,1)S(1)} collective-permute-done((bf16[4,128,256]{2,1,0:T(8,128)(2,1)S(1)}, bf16[4,128,256]{2,1,0:T(8,128)(2,1)S(1)}, u32[]{:S(2)}, u32[]{:S(2)}) %collective-permute-start.19) | collective-permute-done | bytes 262176 | tf_op jit(solution)/shard_map/ppermute | solution.py:46
  58.3 2.1 %collective-permute-start.14 = (bf16[2,128,256]{2,1,0:T(8,128)(2,1)S(1)}, bf16[2,128,256]{2,1,0:T(8,128)(2,1)S(1)}, u32[]{:S(2)}, u32[]{:S(2)}) collective-permute-start(bf16[2,128,256]{2,1,0:T(8,128)(2,1)S(1)} %slice.52), channel_id=1, source_target_pairs={{0,8},{1,9},{2,10},{3,11},{4,0},{5,1},{6,2},{7,3},{8,12},{9,13},{1... | collective-permute-start | bytes 393224 | tf_op jit(solution)/shard_map/ppermute | solution.py:46
  60.8 1.5 %collective-permute-start.20 = (bf16[2,128,256]{2,1,0:T(8,128)(2,1)S(1)}, bf16[2,128,256]{2,1,0:T(8,128)(2,1)S(1)}, u32[]{:S(2)}, u32[]{:S(2)}) collective-permute-start(bf16[2,128,256]{2,1,0:T(8,128)(2,1)S(1)} %slice.54), channel_id=1, source_target_pairs={{0,2},{1,3},{2,0},{3,1},{4,6},{5,7},{6,4},{7,5},{8,10},{9,11},{10,... | collective-permute-start | bytes 393224 | tf_op jit(solution)/shard_map/ppermute | solution.py:40
  62.3 2.0 %collective-permute-done.14.refs_8_ = bf16[2,128,256]{2,1,0:T(8,128)(2,1)S(1)} collective-permute-done((bf16[2,128,256]{2,1,0:T(8,128)(2,1)S(1)}, bf16[2,128,256]{2,1,0:T(8,128)(2,1)S(1)}, u32[]{:S(2)}, u32[]{:S(2)}) %collective-permute-start.14) | collective-permute-done | bytes 131104 | tf_op jit(solution)/shard_map/ppermute | solution.py:46
  64.3 1.5 %collective-permute-start.15 = (bf16[1,128,256]{2,1,0:T(8,128)(2,1)S(1)}, bf16[1,128,256]{2,1,0:T(8,128)(2,1)S(1)}, u32[]{:S(2)}, u32[]{:S(2)}) collective-permute-start(bf16[1,128,256]{2,1,0:T(8,128)(2,1)S(1)} %slice.60), channel_id=1, source_target_pairs={{0,2},{1,3},{2,0},{3,1},{4,6},{5,7},{6,4},{7,5},{8,10},{9,11},{10,... | collective-permute-start | bytes 196616 | tf_op jit(solution)/shard_map/ppermute | solution.py:40
  66.2 0.8 collective-permute-done.20.refs_16_
  66.9 1.7 %collective-permute-done.15.late = bf16[1,128,256]{2,1,0:T(8,128)(2,1)S(1)} collective-permute-done((bf16[1,128,256]{2,1,0:T(8,128)(2,1)S(1)}, bf16[1,128,256]{2,1,0:T(8,128)(2,1)S(1)}, u32[]{:S(2)}, u32[]{:S(2)}) %collective-permute-start.15) | collective-permute-done | bytes 65568 | tf_op jit(solution)/shard_map/ppermute | solution.py:40
  68.6 4.9 %shard_map.78 = (bf16[2,8,2,128,256]{4,3,2,1,0:T(8,128)(2,1)S(1)}, bf16[2,8,2,128,256]{4,3,2,1,0:T(8,128)(2,1)S(1)}, f32[4,32]{1,0:T(4,128)S(1)}) custom-call(bf16[32,128,256]{2,1,0:T(8,128)(2,1)S(1)} %copy-done.4, bf16[32,128,256]{2,1,0:T(8,128)(2,1)S(1)} %collective-permute-done.12.rot_theirs, bf16[7,128,256]{2,1,0:T(8,128)(2,1)S(1)} %collective-permute-done.11.early, ...), custom_call_target="tpu_custom_call" | custom-call | flops 3087007744 | bytes 15204352 | tf_op jit(solution)/shard_map/pallas_call | solution.py:188
  73.5 1.9 %collective-permute-start.24 = (f32[4,32]{1,0:T(4,128)S(1)}, f32[4,32]{1,0:T(4,128)S(1)}, u32[]{:S(2)}, u32[]{:S(2)}) collective-permute-start(f32[4,32]{1,0:T(4,128)S(1)} %get-tuple-element.69), channel_id=1, source_target_pairs={{0,12},{1,13},{2,14},{3,15},{4,0},{5,1},{6,2},{7,3},{8,4},{9,5},{1... | collective-permute-start | bytes 1544 | tf_op jit(solution)/shard_map/ppermute | solution.py:40
  76.2 2.8 %collective-permute-start.22 = (f32[4,32]{1,0:T(4,128)S(1)}, f32[4,32]{1,0:T(4,128)S(1)}, u32[]{:S(2)}, u32[]{:S(2)}) collective-permute-start(f32[4,32]{1,0:T(4,128)S(1)} %get-tuple-element.69), channel_id=1, source_target_pairs={{0,8},{1,9},{2,10},{3,11},{4,12},{5,13},{6,14},{7,15},{8,0},{9,1},... | collective-permute-start | bytes 1544 | tf_op jit(solution)/shard_map/ppermute | solution.py:40
  78.9 1.9 %collective-permute-done.23 = f32[4,32]{1,0:T(4,128)S(1)} collective-permute-done((f32[4,32]{1,0:T(4,128)S(1)}, f32[4,32]{1,0:T(4,128)S(1)}, u32[]{:S(2)}, u32[]{:S(2)}) %collective-permute-start.23) | collective-permute-done | bytes 544 | tf_op jit(solution)/shard_map/ppermute | solution.py:40
  80.9 1.6 %collective-permute-start.26 = (f32[4,32]{1,0:T(4,128)S(1)}, f32[4,32]{1,0:T(4,128)S(1)}, u32[]{:S(2)}, u32[]{:S(2)}) collective-permute-start(f32[4,32]{1,0:T(4,128)S(1)} %add_add_fusion.mine), channel_id=1, source_target_pairs={{0,1},{1,0},{2,3},{3,2},{4,5},{5,4},{6,7},{7,6},{8,9},{9,8},{10,11... | collective-permute-start | bytes 1544 | tf_op jit(solution)/shard_map/ppermute | solution.py:40
  83.0 0.9 collective-permute-done.27.theirs_across
  83.9 2.2 %collective-permute-done.25.mine_across = f32[4,32]{1,0:T(4,128)S(1)} collective-permute-done((f32[4,32]{1,0:T(4,128)S(1)}, f32[4,32]{1,0:T(4,128)S(1)}, u32[]{:S(2)}, u32[]{:S(2)}) %collective-permute-start.25) | collective-permute-done | bytes 544 | tf_op jit(solution)/shard_map/ppermute | solution.py:40
  86.1 5.8 %copy-done = bf16[32,128,2048]{2,1,0:T(8,128)(2,1)S(1)} copy-done((bf16[32,128,2048]{2,1,0:T(8,128)(2,1)S(1)}, bf16[32,128,2048]{2,1,0:T(8,128)(2,1)}, u32[]{:S(2)}) %copy-start) | copy-done | bytes 16777240
  91.9 3.2 %shard_map.79 = (f32[8,32]{1,0:T(8,128)}, bf16[4,128,2048]{2,1,0:T(8,128)(2,1)S(1)}, bf16[4,64,2048]{2,1,0:T(8,128)(2,1)S(1)}, bf16[4,64,2048]{2,1,0:T(8,128)(2,1)S(1)}) custom-call(s32[8]{0:T(128)S(1)} %get-tuple-element.48.order, f32[8,32]{1,0:T(8,128)S(1)} %copy-done.2, f32[4,32]{1,0:T(4,128)S(1)} %add_add_fusion.mine, ...), custom_call_target="tpu_custom_call" | custom-call | tf_op jit(solution)/shard_map/pallas_call | solution.py:259
  95.6 0.8 shard_map.81
  96.4 2.6 %collective-permute-start.31 = (bf16[4,128,256]{2,1,0:T(8,128)(2,1)S(1)}, bf16[4,128,256]{2,1,0:T(8,128)(2,1)S(1)}, u32[]{:S(2)}, u32[]{:S(2)}) collective-permute-start(bf16[4,128,256]{2,1,0:T(8,128)(2,1)S(1)} %get-tuple-element.76.refs_3_), channel_id=1, source_target_pairs={{0,8},{1,9},{2,10},{3,11},{4,0},{5,1},{6,2},{7,3},{8,12},{9,13},{1... | collective-permute-start | bytes 786440 | tf_op jit(solution)/shard_map/ppermute | solution.py:46
  99.5 0.8 shard_map.80
  100.3 2.4 %collective-permute-start.39 = (bf16[4,128,256]{2,1,0:T(8,128)(2,1)S(1)}, bf16[4,128,256]{2,1,0:T(8,128)(2,1)S(1)}, u32[]{:S(2)}, u32[]{:S(2)}) collective-permute-start(bf16[4,128,256]{2,1,0:T(8,128)(2,1)S(1)} %get-tuple-element.83.refs_12_), channel_id=1, source_target_pairs={{0,8},{1,9},{2,10},{3,11},{4,0},{5,1},{6,2},{7,3},{8,12},{9,13},{1... | collective-permute-start | bytes 786440 | tf_op jit(solution)/shard_map/ppermute | solution.py:46
  103.2 2.5 %collective-permute-done.31.refs_4_ = bf16[4,128,256]{2,1,0:T(8,128)(2,1)S(1)} collective-permute-done((bf16[4,128,256]{2,1,0:T(8,128)(2,1)S(1)}, bf16[4,128,256]{2,1,0:T(8,128)(2,1)S(1)}, u32[]{:S(2)}, u32[]{:S(2)}) %collective-permute-start.31) | collective-permute-done | bytes 262176 | tf_op jit(solution)/shard_map/ppermute | solution.py:46
  105.7 2.5 %collective-permute-done.30.refs_7_ = bf16[4,128,256]{2,1,0:T(8,128)(2,1)S(1)} collective-permute-done((bf16[4,128,256]{2,1,0:T(8,128)(2,1)S(1)}, bf16[4,128,256]{2,1,0:T(8,128)(2,1)S(1)}, u32[]{:S(2)}, u32[]{:S(2)}) %collective-permute-start.30) | collective-permute-done | bytes 262176 | tf_op jit(solution)/shard_map/ppermute | solution.py:40
  108.2 0.9 collective-permute-start.33
  109.6 1.7 %collective-permute-done.39.refs_13_ = bf16[4,128,256]{2,1,0:T(8,128)(2,1)S(1)} collective-permute-done((bf16[4,128,256]{2,1,0:T(8,128)(2,1)S(1)}, bf16[4,128,256]{2,1,0:T(8,128)(2,1)S(1)}, u32[]{:S(2)}, u32[]{:S(2)}) %collective-permute-start.39) | collective-permute-done | bytes 262176 | tf_op jit(solution)/shard_map/ppermute | solution.py:46
  111.3 2.5 %collective-permute-done.38.refs_16_ = bf16[4,128,256]{2,1,0:T(8,128)(2,1)S(1)} collective-permute-done((bf16[4,128,256]{2,1,0:T(8,128)(2,1)S(1)}, bf16[4,128,256]{2,1,0:T(8,128)(2,1)S(1)}, u32[]{:S(2)}, u32[]{:S(2)}) %collective-permute-start.38) | collective-permute-done | bytes 262176 | tf_op jit(solution)/shard_map/ppermute | solution.py:40
  113.8 0.9 collective-permute-start.41
  115.2 2.3 %collective-permute-done.33.refs_5_ = bf16[4,128,256]{2,1,0:T(8,128)(2,1)S(1)} collective-permute-done((bf16[4,128,256]{2,1,0:T(8,128)(2,1)S(1)}, bf16[4,128,256]{2,1,0:T(8,128)(2,1)S(1)}, u32[]{:S(2)}, u32[]{:S(2)}) %collective-permute-start.33) | collective-permute-done | bytes 262176 | tf_op jit(solution)/shard_map/ppermute | solution.py:46
  117.5 2.0 %collective-permute-done.32.refs_8_ = bf16[4,128,256]{2,1,0:T(8,128)(2,1)S(1)} collective-permute-done((bf16[4,128,256]{2,1,0:T(8,128)(2,1)S(1)}, bf16[4,128,256]{2,1,0:T(8,128)(2,1)S(1)}, u32[]{:S(2)}, u32[]{:S(2)}) %collective-permute-start.32) | collective-permute-done | bytes 262176 | tf_op jit(solution)/shard_map/ppermute | solution.py:40
  119.5 0.9 collective-permute-start.35
  120.8 2.3 %collective-permute-done.41.refs_14_ = bf16[4,128,256]{2,1,0:T(8,128)(2,1)S(1)} collective-permute-done((bf16[4,128,256]{2,1,0:T(8,128)(2,1)S(1)}, bf16[4,128,256]{2,1,0:T(8,128)(2,1)S(1)}, u32[]{:S(2)}, u32[]{:S(2)}) %collective-permute-start.41) | collective-permute-done | bytes 262176 | tf_op jit(solution)/shard_map/ppermute | solution.py:46
  123.1 2.0 %collective-permute-done.40.refs_17_ = bf16[4,128,256]{2,1,0:T(8,128)(2,1)S(1)} collective-permute-done((bf16[4,128,256]{2,1,0:T(8,128)(2,1)S(1)}, bf16[4,128,256]{2,1,0:T(8,128)(2,1)S(1)}, u32[]{:S(2)}, u32[]{:S(2)}) %collective-permute-start.40) | collective-permute-done | bytes 262176 | tf_op jit(solution)/shard_map/ppermute | solution.py:40
  125.1 0.9 collective-permute-start.43
  126.4 2.3 %collective-permute-done.35.refs_6_ = bf16[4,128,256]{2,1,0:T(8,128)(2,1)S(1)} collective-permute-done((bf16[4,128,256]{2,1,0:T(8,128)(2,1)S(1)}, bf16[4,128,256]{2,1,0:T(8,128)(2,1)S(1)}, u32[]{:S(2)}, u32[]{:S(2)}) %collective-permute-start.35) | collective-permute-done | bytes 262176 | tf_op jit(solution)/shard_map/ppermute | solution.py:46
  128.7 2.0 %collective-permute-done.34.refs_9_ = bf16[4,128,256]{2,1,0:T(8,128)(2,1)S(1)} collective-permute-done((bf16[4,128,256]{2,1,0:T(8,128)(2,1)S(1)}, bf16[4,128,256]{2,1,0:T(8,128)(2,1)S(1)}, u32[]{:S(2)}, u32[]{:S(2)}) %collective-permute-start.34) | collective-permute-done | bytes 262176 | tf_op jit(solution)/shard_map/ppermute | solution.py:40
  130.7 0.9 collective-permute-start.37
  132.1 2.2 %collective-permute-done.43.refs_15_ = bf16[4,128,256]{2,1,0:T(8,128)(2,1)S(1)} collective-permute-done((bf16[4,128,256]{2,1,0:T(8,128)(2,1)S(1)}, bf16[4,128,256]{2,1,0:T(8,128)(2,1)S(1)}, u32[]{:S(2)}, u32[]{:S(2)}) %collective-permute-start.43) | collective-permute-done | bytes 262176 | tf_op jit(solution)/shard_map/ppermute | solution.py:46
  134.3 2.0 %collective-permute-done.42.refs_18_ = bf16[4,128,256]{2,1,0:T(8,128)(2,1)S(1)} collective-permute-done((bf16[4,128,256]{2,1,0:T(8,128)(2,1)S(1)}, bf16[4,128,256]{2,1,0:T(8,128)(2,1)S(1)}, u32[]{:S(2)}, u32[]{:S(2)}) %collective-permute-start.42) | collective-permute-done | bytes 262176 | tf_op jit(solution)/shard_map/ppermute | solution.py:40
  136.3 0.9 collective-permute-start.45
  137.9 3.4 %collective-permute-done.45.refs_20_ = bf16[2,128,256]{2,1,0:T(8,128)(2,1)S(1)} collective-permute-done((bf16[2,128,256]{2,1,0:T(8,128)(2,1)S(1)}, bf16[2,128,256]{2,1,0:T(8,128)(2,1)S(1)}, u32[]{:S(2)}, u32[]{:S(2)}) %collective-permute-start.45) | collective-permute-done | bytes 131104 | tf_op jit(solution)/shard_map/ppermute | solution.py:46
  141.4 0.9 collective-permute-done.44.refs_19_
  142.2 1.1 shard_map.82
  143.4 2.0 %shard_map.83._ = bf16[8,128,256]{2,1,0:T(8,128)(2,1)} custom-call(s32[8]{0:T(128)S(1)} %get-tuple-element.48.order, bf16[4,128,2048]{2,1,0:T(8,128)(2,1)S(1)} %get-tuple-element.75.refs_0_.potential, f32[4,128,256]{2,1,0:T(8,128)S(1)} %get-tuple-element.91.base, bf16[4,8,2,128,256]{4,3,2,1,0:T(8,128)(2,1)S(1)} %get-tuple-element.92.full), custom_call_target="tpu_custom_call" | custom-call | flops 536870912 | bytes 6291456 | tf_op jit(solution)/shard_map/pallas_call | solution.py:364
  145.5 1.3 shard_map.84
  (71 shorter events, 9.8 us)
Async XLA Ops:
  0.6 1.0 copy-start.1
  1.7 0.7 copy-start.3
  2.3 27.4 %copy-start.4 = (bf16[32,128,256]{2,1,0:T(8,128)(2,1)S(1)}, bf16[32,128,256]{2,1,0:T(8,128)(2,1)}, u32[]{:S(2)}) copy-start(bf16[32,128,256]{2,1,0:T(8,128)(2,1)} %rot_mine.1) | copy-start | bytes 6291460
  2.3 27.4 %copy-start.5 = (bf16[128,256]{1,0:T(8,128)(2,1)S(1)}, bf16[128,256]{1,0:T(8,128)(2,1)}, u32[]{:S(2)}) copy-start(bf16[128,256]{1,0:T(8,128)(2,1)} %param.7) | copy-start | bytes 196612
  4.4 3.2 %collective-permute-start = (bf16[2,128,256]{2,1,0:T(8,128)(2,1)S(1)}, bf16[2,128,256]{2,1,0:T(8,128)(2,1)S(1)}, u32[]{:S(2)}, u32[]{:S(2)}) collective-permute-start(bf16[2,128,256]{2,1,0:T(8,128)(2,1)S(1)} %get-tuple-element.50), channel_id=1, source_target_pairs={{0,1},{1,0},{2,3},{3,2},{4,5},{5,4},{6,7},{7,6},{8,9},{9,8},{10,11... | collective-permute-start | bytes 393224 | tf_op jit(solution)/shard_map/ppermute | solution.py:40
  4.9 8.0 %collective-permute-start.3 = (bf16[2,128,256]{2,1,0:T(8,128)(2,1)S(1)}, bf16[2,128,256]{2,1,0:T(8,128)(2,1)S(1)}, u32[]{:S(2)}, u32[]{:S(2)}) collective-permute-start(bf16[2,128,256]{2,1,0:T(8,128)(2,1)S(1)} %get-tuple-element.51), channel_id=1, source_target_pairs={{0,16},{1,17},{2,18},{3,19},{4,20},{5,21},{6,22},{7,23},{8,24},{9,... | collective-permute-start | bytes 393224 | tf_op jit(solution)/shard_map/ppermute | solution.py:479
  7.5 6.6 %collective-permute-start.4 = (bf16[2,128,256]{2,1,0:T(8,128)(2,1)S(1)}, bf16[2,128,256]{2,1,0:T(8,128)(2,1)S(1)}, u32[]{:S(2)}, u32[]{:S(2)}) collective-permute-start(bf16[2,128,256]{2,1,0:T(8,128)(2,1)S(1)} %get-tuple-element.52), channel_id=1, source_target_pairs={{0,17},{1,16},{2,19},{3,18},{4,21},{5,20},{6,23},{7,22},{8,25},{9,... | collective-permute-start | bytes 393224 | tf_op jit(solution)/shard_map/ppermute | solution.py:480
  8.5 18.2 %collective-permute-start.2 = (bf16[5,128,256]{2,1,0:T(8,128)(2,1)S(1)}, bf16[5,128,256]{2,1,0:T(8,128)(2,1)S(1)}, u32[]{:S(2)}, u32[]{:S(2)}) collective-permute-start(bf16[5,128,256]{2,1,0:T(8,128)(2,1)S(1)} %pad_maximum_fusion.refs_0_), channel_id=1, source_target_pairs={{0,8},{1,9},{2,10},{3,11},{4,0},{5,1},{6,2},{7,3},{8,12},{9,13},{1... | collective-permute-start | bytes 983048 | tf_op jit(solution)/shard_map/ppermute | solution.py:46
  11.3 15.3 %collective-permute-start.1 = (bf16[5,128,256]{2,1,0:T(8,128)(2,1)S(1)}, bf16[5,128,256]{2,1,0:T(8,128)(2,1)S(1)}, u32[]{:S(2)}, u32[]{:S(2)}) collective-permute-start(bf16[5,128,256]{2,1,0:T(8,128)(2,1)S(1)} %pad_maximum_fusion.refs_0_), channel_id=1, source_target_pairs={{0,2},{1,3},{2,0},{3,1},{4,6},{5,7},{6,4},{7,5},{8,10},{9,11},{10,... | collective-permute-start | bytes 983048 | tf_op jit(solution)/shard_map/ppermute | solution.py:40
  14.2 10.3 %collective-permute-start.6 = (bf16[4,128,256]{2,1,0:T(8,128)(2,1)S(1)}, bf16[4,128,256]{2,1,0:T(8,128)(2,1)S(1)}, u32[]{:S(2)}, u32[]{:S(2)}) collective-permute-start(bf16[4,128,256]{2,1,0:T(8,128)(2,1)S(1)} %pad_maximum_fusion.1.refs_9_), channel_id=1, source_target_pairs={{0,8},{1,9},{2,10},{3,11},{4,0},{5,1},{6,2},{7,3},{8,12},{9,13},{1... | collective-permute-start | bytes 786440 | tf_op jit(solution)/shard_map/ppermute | solution.py:46
  16.9 9.8 %collective-permute-start.5 = (bf16[4,128,256]{2,1,0:T(8,128)(2,1)S(1)}, bf16[4,128,256]{2,1,0:T(8,128)(2,1)S(1)}, u32[]{:S(2)}, u32[]{:S(2)}) collective-permute-start(bf16[4,128,256]{2,1,0:T(8,128)(2,1)S(1)} %pad_maximum_fusion.1.refs_9_), channel_id=1, source_target_pairs={{0,2},{1,3},{2,0},{3,1},{4,6},{5,7},{6,4},{7,5},{8,10},{9,11},{10,... | collective-permute-start | bytes 786440 | tf_op jit(solution)/shard_map/ppermute | solution.py:40
  26.6 10.6 %collective-permute-start.8 = (bf16[5,128,256]{2,1,0:T(8,128)(2,1)S(1)}, bf16[5,128,256]{2,1,0:T(8,128)(2,1)S(1)}, u32[]{:S(2)}, u32[]{:S(2)}) collective-permute-start(bf16[5,128,256]{2,1,0:T(8,128)(2,1)S(1)} %collective-permute-done.2.refs_1_), channel_id=1, source_target_pairs={{0,8},{1,9},{2,10},{3,11},{4,0},{5,1},{6,2},{7,3},{8,12},{9,13},{1... | collective-permute-start | bytes 983048 | tf_op jit(solution)/shard_map/ppermute | solution.py:46
  28.2 10.6 %collective-permute-start.7 = (bf16[5,128,256]{2,1,0:T(8,128)(2,1)S(1)}, bf16[5,128,256]{2,1,0:T(8,128)(2,1)S(1)}, u32[]{:S(2)}, u32[]{:S(2)}) collective-permute-start(bf16[5,128,256]{2,1,0:T(8,128)(2,1)S(1)} %collective-permute-done.2.refs_1_), channel_id=1, source_target_pairs={{0,2},{1,3},{2,0},{3,1},{4,6},{5,7},{6,4},{7,5},{8,10},{9,11},{10,... | collective-permute-start | bytes 983048 | tf_op jit(solution)/shard_map/ppermute | solution.py:40
  29.7 36.1 %collective-permute-start.12 = (bf16[32,128,256]{2,1,0:T(8,128)(2,1)S(1)}, bf16[32,128,256]{2,1,0:T(8,128)(2,1)S(1)}, u32[]{:S(2)}, u32[]{:S(2)}) collective-permute-start(bf16[32,128,256]{2,1,0:T(8,128)(2,1)S(1)} %copy-done.4), channel_id=1, source_target_pairs={{0,1},{1,0},{2,3},{3,2},{4,5},{5,4},{6,7},{7,6},{8,9},{9,8},{10,11... | collective-permute-start | bytes 6291464 | tf_op jit(solution)/shard_map/ppermute | solution.py:40
  29.8 19.8 %collective-permute-start.17 = (bf16[4,128,256]{2,1,0:T(8,128)(2,1)S(1)}, bf16[4,128,256]{2,1,0:T(8,128)(2,1)S(1)}, u32[]{:S(2)}, u32[]{:S(2)}) collective-permute-start(bf16[4,128,256]{2,1,0:T(8,128)(2,1)S(1)} %collective-permute-done.6.refs_10_), channel_id=1, source_target_pairs={{0,8},{1,9},{2,10},{3,11},{4,0},{5,1},{6,2},{7,3},{8,12},{9,13},{1... | collective-permute-start | bytes 786440 | tf_op jit(solution)/shard_map/ppermute | solution.py:46
  30.2 19.4 %collective-permute-start.16 = (bf16[4,128,256]{2,1,0:T(8,128)(2,1)S(1)}, bf16[4,128,256]{2,1,0:T(8,128)(2,1)S(1)}, u32[]{:S(2)}, u32[]{:S(2)}) collective-permute-start(bf16[4,128,256]{2,1,0:T(8,128)(2,1)S(1)} %collective-permute-done.6.refs_10_), channel_id=1, source_target_pairs={{0,2},{1,3},{2,0},{3,1},{4,6},{5,7},{6,4},{7,5},{8,10},{9,11},{10,... | collective-permute-start | bytes 786440 | tf_op jit(solution)/shard_map/ppermute | solution.py:40
  38.9 9.3 %collective-permute-start.10 = (bf16[5,128,256]{2,1,0:T(8,128)(2,1)S(1)}, bf16[5,128,256]{2,1,0:T(8,128)(2,1)S(1)}, u32[]{:S(2)}, u32[]{:S(2)}) collective-permute-start(bf16[5,128,256]{2,1,0:T(8,128)(2,1)S(1)} %collective-permute-done.8.refs_2_), channel_id=1, source_target_pairs={{0,8},{1,9},{2,10},{3,11},{4,0},{5,1},{6,2},{7,3},{8,12},{9,13},{1... | collective-permute-start | bytes 983048 | tf_op jit(solution)/shard_map/ppermute | solution.py:46
  39.8 9.7 %collective-permute-start.9 = (bf16[5,128,256]{2,1,0:T(8,128)(2,1)S(1)}, bf16[5,128,256]{2,1,0:T(8,128)(2,1)S(1)}, u32[]{:S(2)}, u32[]{:S(2)}) collective-permute-start(bf16[5,128,256]{2,1,0:T(8,128)(2,1)S(1)} %collective-permute-done.8.refs_2_), channel_id=1, source_target_pairs={{0,2},{1,3},{2,0},{3,1},{4,6},{5,7},{6,4},{7,5},{8,10},{9,11},{10,... | collective-permute-start | bytes 983048 | tf_op jit(solution)/shard_map/ppermute | solution.py:40
  49.5 11.3 %collective-permute-start.11 = (bf16[7,128,256]{2,1,0:T(8,128)(2,1)S(1)}, bf16[7,128,256]{2,1,0:T(8,128)(2,1)S(1)}, u32[]{:S(2)}, u32[]{:S(2)}) collective-permute-start(bf16[7,128,256]{2,1,0:T(8,128)(2,1)S(1)} %slice_dynamic-update-slice_fusion), channel_id=1, source_target_pairs={{0,1},{1,0},{2,3},{3,2},{4,5},{5,4},{6,7},{7,6},{8,9},{9,8},{10,11... | collective-permute-start | bytes 1376264 | tf_op jit(solution)/shard_map/ppermute | solution.py:40
  49.6 8.7 %collective-permute-start.19 = (bf16[4,128,256]{2,1,0:T(8,128)(2,1)S(1)}, bf16[4,128,256]{2,1,0:T(8,128)(2,1)S(1)}, u32[]{:S(2)}, u32[]{:S(2)}) collective-permute-start(bf16[4,128,256]{2,1,0:T(8,128)(2,1)S(1)} %collective-permute-done.17.refs_11_), channel_id=1, source_target_pairs={{0,8},{1,9},{2,10},{3,11},{4,0},{5,1},{6,2},{7,3},{8,12},{9,13},{1... | collective-permute-start | bytes 786440 | tf_op jit(solution)/shard_map/ppermute | solution.py:46
  50.8 9.6 %collective-permute-start.18 = (bf16[4,128,256]{2,1,0:T(8,128)(2,1)S(1)}, bf16[4,128,256]{2,1,0:T(8,128)(2,1)S(1)}, u32[]{:S(2)}, u32[]{:S(2)}) collective-permute-start(bf16[4,128,256]{2,1,0:T(8,128)(2,1)S(1)} %collective-permute-done.17.refs_11_), channel_id=1, source_target_pairs={{0,2},{1,3},{2,0},{3,1},{4,6},{5,7},{6,4},{7,5},{8,10},{9,11},{10,... | collective-permute-start | bytes 786440 | tf_op jit(solution)/shard_map/ppermute | solution.py:40
  52.4 13.5 %collective-permute-start.13 = (bf16[3,128,256]{2,1,0:T(8,128)(2,1)S(1)}, bf16[3,128,256]{2,1,0:T(8,128)(2,1)S(1)}, u32[]{:S(2)}, u32[]{:S(2)}) collective-permute-start(bf16[3,128,256]{2,1,0:T(8,128)(2,1)S(1)} %slice.51), channel_id=1, source_target_pairs={{0,2},{1,3},{2,0},{3,1},{4,6},{5,7},{6,4},{7,5},{8,10},{9,11},{10,... | collective-permute-start | bytes 589832 | tf_op jit(solution)/shard_map/ppermute | solution.py:40
  58.3 6.0 %collective-permute-start.14 = (bf16[2,128,256]{2,1,0:T(8,128)(2,1)S(1)}, bf16[2,128,256]{2,1,0:T(8,128)(2,1)S(1)}, u32[]{:S(2)}, u32[]{:S(2)}) collective-permute-start(bf16[2,128,256]{2,1,0:T(8,128)(2,1)S(1)} %slice.52), channel_id=1, source_target_pairs={{0,8},{1,9},{2,10},{3,11},{4,0},{5,1},{6,2},{7,3},{8,12},{9,13},{1... | collective-permute-start | bytes 393224 | tf_op jit(solution)/shard_map/ppermute | solution.py:46
  60.4 5.7 %collective-permute-start.21 = (bf16[2,128,256]{2,1,0:T(8,128)(2,1)S(1)}, bf16[2,128,256]{2,1,0:T(8,128)(2,1)S(1)}, u32[]{:S(2)}, u32[]{:S(2)}) collective-permute-start(bf16[2,128,256]{2,1,0:T(8,128)(2,1)S(1)} %slice.55), channel_id=1, source_target_pairs={{0,8},{1,9},{2,10},{3,11},{4,0},{5,1},{6,2},{7,3},{8,12},{9,13},{1... | collective-permute-start | bytes 393224 | tf_op jit(solution)/shard_map/ppermute | solution.py:46
  60.8 6.2 %collective-permute-start.20 = (bf16[2,128,256]{2,1,0:T(8,128)(2,1)S(1)}, bf16[2,128,256]{2,1,0:T(8,128)(2,1)S(1)}, u32[]{:S(2)}, u32[]{:S(2)}) collective-permute-start(bf16[2,128,256]{2,1,0:T(8,128)(2,1)S(1)} %slice.54), channel_id=1, source_target_pairs={{0,2},{1,3},{2,0},{3,1},{4,6},{5,7},{6,4},{7,5},{8,10},{9,11},{10,... | collective-permute-start | bytes 393224 | tf_op jit(solution)/shard_map/ppermute | solution.py:40
  62.3 23.8 %copy-start.2 = (f32[8,32]{1,0:T(8,128)S(1)}, f32[8,32]{1,0:T(8,128)}, u32[]{:S(2)}) copy-start(f32[8,32]{1,0:T(8,128)} %fields.1) | copy-start | bytes 3076
  64.3 4.3 %collective-permute-start.15 = (bf16[1,128,256]{2,1,0:T(8,128)(2,1)S(1)}, bf16[1,128,256]{2,1,0:T(8,128)(2,1)S(1)}, u32[]{:S(2)}, u32[]{:S(2)}) collective-permute-start(bf16[1,128,256]{2,1,0:T(8,128)(2,1)S(1)} %slice.60), channel_id=1, source_target_pairs={{0,2},{1,3},{2,0},{3,1},{4,6},{5,7},{6,4},{7,5},{8,10},{9,11},{10,... | collective-permute-start | bytes 196616 | tf_op jit(solution)/shard_map/ppermute | solution.py:40
  73.5 5.4 %collective-permute-start.24 = (f32[4,32]{1,0:T(4,128)S(1)}, f32[4,32]{1,0:T(4,128)S(1)}, u32[]{:S(2)}, u32[]{:S(2)}) collective-permute-start(f32[4,32]{1,0:T(4,128)S(1)} %get-tuple-element.69), channel_id=1, source_target_pairs={{0,12},{1,13},{2,14},{3,15},{4,0},{5,1},{6,2},{7,3},{8,4},{9,5},{1... | collective-permute-start | bytes 1544 | tf_op jit(solution)/shard_map/ppermute | solution.py:40
  75.4 5.4 %collective-permute-start.23 = (f32[4,32]{1,0:T(4,128)S(1)}, f32[4,32]{1,0:T(4,128)S(1)}, u32[]{:S(2)}, u32[]{:S(2)}) collective-permute-start(f32[4,32]{1,0:T(4,128)S(1)} %get-tuple-element.69), channel_id=1, source_target_pairs={{0,4},{1,5},{2,6},{3,7},{4,8},{5,9},{6,10},{7,11},{8,12},{9,13},{1... | collective-permute-start | bytes 1544 | tf_op jit(solution)/shard_map/ppermute | solution.py:40
  76.2 4.6 %collective-permute-start.22 = (f32[4,32]{1,0:T(4,128)S(1)}, f32[4,32]{1,0:T(4,128)S(1)}, u32[]{:S(2)}, u32[]{:S(2)}) collective-permute-start(f32[4,32]{1,0:T(4,128)S(1)} %get-tuple-element.69), channel_id=1, source_target_pairs={{0,8},{1,9},{2,10},{3,11},{4,12},{5,13},{6,14},{7,15},{8,0},{9,1},... | collective-permute-start | bytes 1544 | tf_op jit(solution)/shard_map/ppermute | solution.py:40
  80.8 3.1 %collective-permute-start.27 = (f32[4,32]{1,0:T(4,128)S(1)}, f32[4,32]{1,0:T(4,128)S(1)}, u32[]{:S(2)}, u32[]{:S(2)}) collective-permute-start(f32[4,32]{1,0:T(4,128)S(1)} %add_add_fusion.mine), channel_id=1, source_target_pairs={{0,3},{1,2},{2,1},{3,0},{4,7},{5,6},{6,5},{7,4},{8,11},{9,10},{10,... | collective-permute-start | bytes 1544 | tf_op jit(solution)/shard_map/ppermute | solution.py:40
  80.9 3.0 %collective-permute-start.26 = (f32[4,32]{1,0:T(4,128)S(1)}, f32[4,32]{1,0:T(4,128)S(1)}, u32[]{:S(2)}, u32[]{:S(2)}) collective-permute-start(f32[4,32]{1,0:T(4,128)S(1)} %add_add_fusion.mine), channel_id=1, source_target_pairs={{0,1},{1,0},{2,3},{3,2},{4,5},{5,4},{6,7},{7,6},{8,9},{9,8},{10,11... | collective-permute-start | bytes 1544 | tf_op jit(solution)/shard_map/ppermute | solution.py:40
  82.5 3.6 %collective-permute-start.25 = (f32[4,32]{1,0:T(4,128)S(1)}, f32[4,32]{1,0:T(4,128)S(1)}, u32[]{:S(2)}, u32[]{:S(2)}) collective-permute-start(f32[4,32]{1,0:T(4,128)S(1)} %add_add_fusion.mine), channel_id=1, source_target_pairs={{0,2},{1,3},{2,0},{3,1},{4,6},{5,7},{6,4},{7,5},{8,10},{9,11},{10,... | collective-permute-start | bytes 1544 | tf_op jit(solution)/shard_map/ppermute | solution.py:40
  86.1 5.8 %copy-start = (bf16[32,128,2048]{2,1,0:T(8,128)(2,1)S(1)}, bf16[32,128,2048]{2,1,0:T(8,128)(2,1)}, u32[]{:S(2)}) copy-start(bf16[32,128,2048]{2,1,0:T(8,128)(2,1)} %cholesky.1) | copy-start | bytes 50331652
  95.0 4.5 %collective-permute-start.28 = (bf16[4,64,2048]{2,1,0:T(8,128)(2,1)S(1)}, bf16[4,64,2048]{2,1,0:T(8,128)(2,1)S(1)}, u32[]{:S(2)}, u32[]{:S(2)}) collective-permute-start(bf16[4,64,2048]{2,1,0:T(8,128)(2,1)S(1)} %get-tuple-element.70), channel_id=1, source_target_pairs={{0,1},{1,0},{2,3},{3,2},{4,5},{5,4},{6,7},{7,6},{8,9},{9,8},{10,11... | collective-permute-start | bytes 3145736 | tf_op jit(solution)/shard_map/ppermute | solution.py:40
  95.1 4.4 %collective-permute-start.29 = (bf16[4,64,2048]{2,1,0:T(8,128)(2,1)S(1)}, bf16[4,64,2048]{2,1,0:T(8,128)(2,1)S(1)}, u32[]{:S(2)}, u32[]{:S(2)}) collective-permute-start(bf16[4,64,2048]{2,1,0:T(8,128)(2,1)S(1)} %get-tuple-element.71), channel_id=1, source_target_pairs={{0,1},{1,0},{2,3},{3,2},{4,5},{5,4},{6,7},{7,6},{8,9},{9,8},{10,11... | collective-permute-start | bytes 3145736 | tf_op jit(solution)/shard_map/ppermute | solution.py:40
  96.4 9.3 %collective-permute-start.31 = (bf16[4,128,256]{2,1,0:T(8,128)(2,1)S(1)}, bf16[4,128,256]{2,1,0:T(8,128)(2,1)S(1)}, u32[]{:S(2)}, u32[]{:S(2)}) collective-permute-start(bf16[4,128,256]{2,1,0:T(8,128)(2,1)S(1)} %get-tuple-element.76.refs_3_), channel_id=1, source_target_pairs={{0,8},{1,9},{2,10},{3,11},{4,0},{5,1},{6,2},{7,3},{8,12},{9,13},{1... | collective-permute-start | bytes 786440 | tf_op jit(solution)/shard_map/ppermute | solution.py:46
  99.0 9.2 %collective-permute-start.30 = (bf16[4,128,256]{2,1,0:T(8,128)(2,1)S(1)}, bf16[4,128,256]{2,1,0:T(8,128)(2,1)S(1)}, u32[]{:S(2)}, u32[]{:S(2)}) collective-permute-start(bf16[4,128,256]{2,1,0:T(8,128)(2,1)S(1)} %get-tuple-element.76.refs_3_), channel_id=1, source_target_pairs={{0,2},{1,3},{2,0},{3,1},{4,6},{5,7},{6,4},{7,5},{8,10},{9,11},{10,... | collective-permute-start | bytes 786440 | tf_op jit(solution)/shard_map/ppermute | solution.py:40
  100.3 11.0 %collective-permute-start.39 = (bf16[4,128,256]{2,1,0:T(8,128)(2,1)S(1)}, bf16[4,128,256]{2,1,0:T(8,128)(2,1)S(1)}, u32[]{:S(2)}, u32[]{:S(2)}) collective-permute-start(bf16[4,128,256]{2,1,0:T(8,128)(2,1)S(1)} %get-tuple-element.83.refs_12_), channel_id=1, source_target_pairs={{0,8},{1,9},{2,10},{3,11},{4,0},{5,1},{6,2},{7,3},{8,12},{9,13},{1... | collective-permute-start | bytes 786440 | tf_op jit(solution)/shard_map/ppermute | solution.py:46
  102.7 11.2 %collective-permute-start.38 = (bf16[4,128,256]{2,1,0:T(8,128)(2,1)S(1)}, bf16[4,128,256]{2,1,0:T(8,128)(2,1)S(1)}, u32[]{:S(2)}, u32[]{:S(2)}) collective-permute-start(bf16[4,128,256]{2,1,0:T(8,128)(2,1)S(1)} %get-tuple-element.83.refs_12_), channel_id=1, source_target_pairs={{0,2},{1,3},{2,0},{3,1},{4,6},{5,7},{6,4},{7,5},{8,10},{9,11},{10,... | collective-permute-start | bytes 786440 | tf_op jit(solution)/shard_map/ppermute | solution.py:40
  108.2 9.2 %collective-permute-start.33 = (bf16[4,128,256]{2,1,0:T(8,128)(2,1)S(1)}, bf16[4,128,256]{2,1,0:T(8,128)(2,1)S(1)}, u32[]{:S(2)}, u32[]{:S(2)}) collective-permute-start(bf16[4,128,256]{2,1,0:T(8,128)(2,1)S(1)} %collective-permute-done.31.refs_4_), channel_id=1, source_target_pairs={{0,8},{1,9},{2,10},{3,11},{4,0},{5,1},{6,2},{7,3},{8,12},{9,13},{1... | collective-permute-start | bytes 786440 | tf_op jit(solution)/shard_map/ppermute | solution.py:46
  109.1 10.4 %collective-permute-start.32 = (bf16[4,128,256]{2,1,0:T(8,128)(2,1)S(1)}, bf16[4,128,256]{2,1,0:T(8,128)(2,1)S(1)}, u32[]{:S(2)}, u32[]{:S(2)}) collective-permute-start(bf16[4,128,256]{2,1,0:T(8,128)(2,1)S(1)} %collective-permute-done.31.refs_4_), channel_id=1, source_target_pairs={{0,2},{1,3},{2,0},{3,1},{4,6},{5,7},{6,4},{7,5},{8,10},{9,11},{10,... | collective-permute-start | bytes 786440 | tf_op jit(solution)/shard_map/ppermute | solution.py:40
  113.8 9.2 %collective-permute-start.41 = (bf16[4,128,256]{2,1,0:T(8,128)(2,1)S(1)}, bf16[4,128,256]{2,1,0:T(8,128)(2,1)S(1)}, u32[]{:S(2)}, u32[]{:S(2)}) collective-permute-start(bf16[4,128,256]{2,1,0:T(8,128)(2,1)S(1)} %collective-permute-done.39.refs_13_), channel_id=1, source_target_pairs={{0,8},{1,9},{2,10},{3,11},{4,0},{5,1},{6,2},{7,3},{8,12},{9,13},{1... | collective-permute-start | bytes 786440 | tf_op jit(solution)/shard_map/ppermute | solution.py:46
  114.7 10.4 %collective-permute-start.40 = (bf16[4,128,256]{2,1,0:T(8,128)(2,1)S(1)}, bf16[4,128,256]{2,1,0:T(8,128)(2,1)S(1)}, u32[]{:S(2)}, u32[]{:S(2)}) collective-permute-start(bf16[4,128,256]{2,1,0:T(8,128)(2,1)S(1)} %collective-permute-done.39.refs_13_), channel_id=1, source_target_pairs={{0,2},{1,3},{2,0},{3,1},{4,6},{5,7},{6,4},{7,5},{8,10},{9,11},{10,... | collective-permute-start | bytes 786440 | tf_op jit(solution)/shard_map/ppermute | solution.py:40
  119.5 9.2 %collective-permute-start.35 = (bf16[4,128,256]{2,1,0:T(8,128)(2,1)S(1)}, bf16[4,128,256]{2,1,0:T(8,128)(2,1)S(1)}, u32[]{:S(2)}, u32[]{:S(2)}) collective-permute-start(bf16[4,128,256]{2,1,0:T(8,128)(2,1)S(1)} %collective-permute-done.33.refs_5_), channel_id=1, source_target_pairs={{0,8},{1,9},{2,10},{3,11},{4,0},{5,1},{6,2},{7,3},{8,12},{9,13},{1... | collective-permute-start | bytes 786440 | tf_op jit(solution)/shard_map/ppermute | solution.py:46
  120.3 10.4 %collective-permute-start.34 = (bf16[4,128,256]{2,1,0:T(8,128)(2,1)S(1)}, bf16[4,128,256]{2,1,0:T(8,128)(2,1)S(1)}, u32[]{:S(2)}, u32[]{:S(2)}) collective-permute-start(bf16[4,128,256]{2,1,0:T(8,128)(2,1)S(1)} %collective-permute-done.33.refs_5_), channel_id=1, source_target_pairs={{0,2},{1,3},{2,0},{3,1},{4,6},{5,7},{6,4},{7,5},{8,10},{9,11},{10,... | collective-permute-start | bytes 786440 | tf_op jit(solution)/shard_map/ppermute | solution.py:40
  125.1 9.2 %collective-permute-start.43 = (bf16[4,128,256]{2,1,0:T(8,128)(2,1)S(1)}, bf16[4,128,256]{2,1,0:T(8,128)(2,1)S(1)}, u32[]{:S(2)}, u32[]{:S(2)}) collective-permute-start(bf16[4,128,256]{2,1,0:T(8,128)(2,1)S(1)} %collective-permute-done.41.refs_14_), channel_id=1, source_target_pairs={{0,8},{1,9},{2,10},{3,11},{4,0},{5,1},{6,2},{7,3},{8,12},{9,13},{1... | collective-permute-start | bytes 786440 | tf_op jit(solution)/shard_map/ppermute | solution.py:46
  125.9 10.4 %collective-permute-start.42 = (bf16[4,128,256]{2,1,0:T(8,128)(2,1)S(1)}, bf16[4,128,256]{2,1,0:T(8,128)(2,1)S(1)}, u32[]{:S(2)}, u32[]{:S(2)}) collective-permute-start(bf16[4,128,256]{2,1,0:T(8,128)(2,1)S(1)} %collective-permute-done.41.refs_14_), channel_id=1, source_target_pairs={{0,2},{1,3},{2,0},{3,1},{4,6},{5,7},{6,4},{7,5},{8,10},{9,11},{10,... | collective-permute-start | bytes 786440 | tf_op jit(solution)/shard_map/ppermute | solution.py:40
  130.7 7.0 %collective-permute-start.37 = (bf16[2,128,256]{2,1,0:T(8,128)(2,1)S(1)}, bf16[2,128,256]{2,1,0:T(8,128)(2,1)S(1)}, u32[]{:S(2)}, u32[]{:S(2)}) collective-permute-start(bf16[2,128,256]{2,1,0:T(8,128)(2,1)S(1)} %slice.57), channel_id=1, source_target_pairs={{0,8},{1,9},{2,10},{3,11},{4,0},{5,1},{6,2},{7,3},{8,12},{9,13},{1... | collective-permute-start | bytes 393224 | tf_op jit(solution)/shard_map/ppermute | solution.py:46
  131.6 6.3 %collective-permute-start.36 = (bf16[2,128,256]{2,1,0:T(8,128)(2,1)S(1)}, bf16[2,128,256]{2,1,0:T(8,128)(2,1)S(1)}, u32[]{:S(2)}, u32[]{:S(2)}) collective-permute-start(bf16[2,128,256]{2,1,0:T(8,128)(2,1)S(1)} %slice.56), channel_id=1, source_target_pairs={{0,2},{1,3},{2,0},{3,1},{4,6},{5,7},{6,4},{7,5},{8,10},{9,11},{10,... | collective-permute-start | bytes 393224 | tf_op jit(solution)/shard_map/ppermute | solution.py:40
  136.3 5.0 %collective-permute-start.45 = (bf16[2,128,256]{2,1,0:T(8,128)(2,1)S(1)}, bf16[2,128,256]{2,1,0:T(8,128)(2,1)S(1)}, u32[]{:S(2)}, u32[]{:S(2)}) collective-permute-start(bf16[2,128,256]{2,1,0:T(8,128)(2,1)S(1)} %slice.59), channel_id=1, source_target_pairs={{0,8},{1,9},{2,10},{3,11},{4,0},{5,1},{6,2},{7,3},{8,12},{9,13},{1... | collective-permute-start | bytes 393224 | tf_op jit(solution)/shard_map/ppermute | solution.py:46
  137.3 5.0 %collective-permute-start.44 = (bf16[2,128,256]{2,1,0:T(8,128)(2,1)S(1)}, bf16[2,128,256]{2,1,0:T(8,128)(2,1)S(1)}, u32[]{:S(2)}, u32[]{:S(2)}) collective-permute-start(bf16[2,128,256]{2,1,0:T(8,128)(2,1)S(1)} %slice.58), channel_id=1, source_target_pairs={{0,2},{1,3},{2,0},{3,1},{4,6},{5,7},{6,4},{7,5},{8,10},{9,11},{10,... | collective-permute-start | bytes 393224 | tf_op jit(solution)/shard_map/ppermute | solution.py:40
  143.3 2.1 %collective-permute-start.46 = (bf16[4,128,256]{2,1,0:T(8,128)(2,1)S(1)}, bf16[4,128,256]{2,1,0:T(8,128)(2,1)S(1)}, u32[]{:S(2)}, u32[]{:S(2)}) collective-permute-start(bf16[4,128,256]{2,1,0:T(8,128)(2,1)S(1)} %get-tuple-element.90), channel_id=1, source_target_pairs={{0,1},{1,0},{2,3},{3,2},{4,5},{5,4},{6,7},{7,6},{8,9},{9,8},{10,11... | collective-permute-start | bytes 786440 | tf_op jit(solution)/shard_map/ppermute | solution.py:40

commit v9 on v8

--- a/solution.py
+++ b/solution.py
@@ -38,6 +38,9 @@
             target = (((z + dz) % self.z) * 2 + (y ^ dy)) * 2 + (b ^ db)
             pairs.append((index, target))
         return lax.ppermute(array, "chol", pairs)
+
+    def flip(self, array, mask):
+        return lax.ppermute(array, "chol", [(i, i ^ mask) for i in range(self.chol)])
 
     def step(self, array):
         ring = [*range(0, self.z, 2), *reversed(range(1, self.z, 2))]
@@ -126,29 +129,34 @@
     return estimates
 
 
-def bias_kernel(layout, slabs, counts, rot_mine, rot_theirs, early, late, *refs):
-    fulls, (out, buffer, turned, greens) = refs[-4 - len(counts) : -4], refs[-4:]
-    pieces = refs[: -4 - len(counts)]
+def transpose_kernel(matrix, out):
+    out[...] = matrix[...].T
+
+
+def transposed(matrix):
+    return pl.pallas_call(
+        transpose_kernel,
+        out_shape=jax.ShapeDtypeStruct(matrix.shape[::-1], matrix.dtype),
+        in_specs=vmem_specs(1),
+        out_specs=pl.BlockSpec(memory_space=pltpu.VMEM),
+        compiler_params=params(8),
+    )(matrix)
+
+
+def bias_kernel(layout, slabs, counts, rot_mine, rot_theirs, trial, *refs):
+    fulls, (out, greens) = refs[-2 - len(counts) : -2], refs[-2:]
+    pieces = refs[: -2 - len(counts)]
     vectors, rows, electrons = rot_mine.shape
     index = lax.axis_index("chol")
     chip, b = index // 2, lax.rem(index, 2)
 
-    theirs = [(early, at) for at in range(early.shape[0])] + [(late, 0)]
-    trial = [slab for slab in slabs[0] if slab[2] == 2 * counts[0]]
-    for (operand, at, _, steps, dy), (part, place) in zip(trial, theirs):
-        origin = layout.origin(steps, dy)
-        buffer[origin, b] = pieces[operand][at]
-        buffer[origin, 1 - b] = part[place]
-    turned[...] = buffer[...].reshape(-1, electrons).T
-
     matrices = []
     for full, count, stream in zip(fulls, counts, slabs):
         for operand, at, slab, steps, dy in stream:
-            if slab < 2 * count:
-                full[slab % count, layout.origin(steps, dy), slab // count] = pieces[operand][at]
+            full[slab % count, layout.origin(steps, dy), slab // count] = pieces[operand][at]
         for walker in range(count):
             columns = full[walker].reshape(-1, electrons)
-            matrices.append(jnp.dot(turned[...], columns, preferred_element_type=F32))
+            matrices.append(jnp.dot(trial[...], columns, preferred_element_type=F32))
     inverses = [inverse.astype(BF16) for inverse in newton_inverses(matrices)]
 
     walkers = [(full, at) for full, count in zip(fulls, counts) for at in range(count)]
@@ -180,7 +188,7 @@
     )
 
 
-def bias_of(layout, streams, counts, early, late, rot_mine, rot_theirs):
+def bias_of(layout, streams, counts, trial, rot_mine, rot_theirs):
     arrays, slabs = operands(streams)
     vectors, rows, electrons = rot_mine.shape
     chips = layout.chol // 2
@@ -191,14 +199,12 @@
             jax.ShapeDtypeStruct((count, chips, 2, rows, electrons), BF16) for count in counts
         ]
         + [jax.ShapeDtypeStruct((total, vectors), F32)],
-        in_specs=vmem_specs(4 + len(arrays)),
+        in_specs=vmem_specs(3 + len(arrays)),
         out_specs=vmem_specs(len(counts) + 1),
         scratch_shapes=[
-            pltpu.VMEM((chips, 2, rows, electrons), BF16),
-            pltpu.VMEM((electrons, 2 * chips * rows), BF16),
             pltpu.VMEM((2, rows // BLOCK, total, BLOCK, electrons), BF16),
         ],
-        compiler_params=params(20),
+        compiler_params=params(12),
         cost_estimate=pl.CostEstimate(
             flops=2 * total * electrons**2 * (2 * chips * rows + 6 * (ITERS - 1) * electrons)
             + 4 * total * rows * electrons * (electrons + vectors * BLOCK),
@@ -206,7 +212,7 @@
             + 4 * (total + 1) * 2 * chips * rows * electrons,
             transcendentals=0,
         ),
-    )(rot_mine, rot_theirs, early, late, *arrays)
+    )(rot_mine, rot_theirs, trial, *arrays)
 
 
 def potential_kernel(order, fields, mine, mine_across, theirs, theirs_across, cholesky, *refs):
@@ -513,28 +519,30 @@
     shares, order = migrate(layout, walkers, source)
     sizes = [own.shape[0] for own, _ in shares]
     chunks = [
-        jnp.concatenate([jnp.where(b == 0, own, other), jnp.where(b == 0, other, own), *extra])
-        for (own, other), extra in zip(shares, ([trial[None]], []))
+        jnp.concatenate([jnp.where(b == 0, own, other), jnp.where(b == 0, other, own)])
+        for own, other in shares
     ]
     streams = [Stream(layout, chunk) for chunk in chunks]
     rot_theirs = layout.shift(rotated, db=1)
-    moved = lax.optimization_barrier([stream.moves() for stream in streams])
-    for stream, arrays in zip(streams, moved):
+    turned = transposed(lax.all_gather(trial, "chol", axis=0, tiled=True))
+    moved = lax.optimization_barrier([stream.moves() for stream in reversed(streams)])
+    for stream, arrays in zip(reversed(streams), moved):
         stream.accept(arrays)
     for _ in range(layout.z - 2):
         for stream in streams:
             stream.advance()
-    slabs = [array[-1:] for array in (*streams[0].ring, *streams[0].across)]
-    early = layout.shift(jnp.concatenate(slabs), db=1)
-    late = layout.shift(early[layout.z - 1 : layout.z], dy=1)
-    early, rot_theirs = streams[0].advance((early, rot_theirs))
+    turned, rot_theirs = streams[0].advance((turned, rot_theirs))
     streams[1].advance()
-    *fulls, total = bias_of(layout, streams, sizes, early, late, rotated, rot_theirs)
-    parts = [total] + [layout.shift(total, dz=dz) for dz in range(1, layout.z)]
-    while len(parts) > 1:
-        far = len(parts) // 2
-        parts = [parts[at] + parts[at + far] for at in range(far)]
-    parts = [parts[0]] + [layout.shift(parts[0], dy=dy, db=db) for dy, db in ((1, 0), (0, 1), (1, 1))]
+    *fulls, total = bias_of(layout, streams, sizes, turned, rotated, rot_theirs)
+    bits = [2] + [4 << at for at in range(layout.z.bit_length() - 1)]
+    while len(bits) > 1:
+        first, second, *rest = bits if len(bits) % 2 else (bits[0], 0, *bits[1:])
+        sums = [total + layout.flip(total, first)]
+        if second:
+            sums.append(layout.flip(total, second) + layout.flip(total, first + second))
+        total = sum(sums[1:], sums[0])
+        bits = rest
+    parts = [total] + [layout.flip(total, mask) for mask in (bits[0], 1, bits[0] + 1)]
     force_bias, kept, *sent = potential_of(order, fields, parts, cholesky)
     received = [layout.shift(part, db=1) for part in sent]
 

time: 147 us -> 162 us (1.10)
  between operations: 0.89 us -> 14.3 us
  waiting for transfers between devices: 71.6 us -> 62.4 us
  local copies, waits for them, and re-layouts: 7.6 us -> 14.6 us
  starting transfers between devices: 49.6 us -> 51.8 us
  Pallas kernels: 16.1 us -> 18.1 us
    ppermute x16, waiting for transfers between devices: 43.8 us -> 31 us  [step(): return lax.ppermute(array, 'chol', pairs)]
    ppermute x29 -> x21, starting transfers between devices: 24.5 us -> 17.4 us  [shift(): return lax.ppermute(array, 'chol', pairs)]
    ppermute x0 -> x6, starting transfers between devices: none -> 6.56 us  [flip(): lax.ppermute(array, 'chol', [(i, i ^ mask) for i in range(self.chol)])]
    ppermute x0 -> x6, waiting for transfers between devices: none -> 5.64 us  [flip(): lax.ppermute(array, 'chol', [(i, i ^ mask) for i in range(self.chol)])]
    unnamed x18 -> x16, local copies, waits for them, and re-layouts: 7.5 us -> 11.9 us
    ppermute x29 -> x21, waiting for transfers between devices: 26.5 us -> 23.5 us  [shift(): return lax.ppermute(array, 'chol', pairs)]
    ppermute x16, starting transfers between devices: 22.4 us -> 25.2 us  [step(): return lax.ppermute(array, 'chol', pairs)]
    pallas_call x1, Pallas kernels: 4.93 us -> 6.7 us  [bias_of(): pl.pallas_call(functools.partial(bias_kernel, layout, slabs, counts), out...]
  transfers between devices with their start and end apart: 47 -> 46, of which waited for: 30 -> 32; matrix products, arithmetic and copies ran while one was open for 1% -> 2% of each run, Pallas kernels for 2% -> 4%
where the time goes in v9:
time: 162 us; the launch traced here: 161 us
  waiting for transfers between devices  62.4 us (39%)
  starting transfers between devices  51.8 us (32%)
  Pallas kernels  18.1 us (11%)
  local copies, waits for them, and re-layouts  14.6 us (9%)
  between operations  14.3 us (9%)
    ppermute x16, waiting for transfers between devices, step(): return lax.ppermute(array, 'chol', pairs)  31 us
    ppermute x16, starting transfers between devices, step(): return lax.ppermute(array, 'chol', pairs)  25.2 us
    ppermute x21, waiting for transfers between devices, shift(): return lax.ppermute(array, 'chol', pairs)  23.5 us
    ppermute x21, starting transfers between devices, shift(): return lax.ppermute(array, 'chol', pairs)  17.4 us
    unnamed x16, local copies, waits for them, and re-layouts  11.9 us
    pallas_call x1, Pallas kernels, bias_of(): pl.pallas_call(functools.partial(bias_kernel, layout, slabs, counts), out...  6.7 us
    ppermute x6, starting transfers between devices, flip(): lax.ppermute(array, 'chol', [(i, i ^ mask) for i in range(self.chol)])  6.56 us
    ppermute x6, waiting for transfers between devices, flip(): lax.ppermute(array, 'chol', [(i, i ^ mask) for i in range(self.chol)])  5.64 us
  transfers between devices with their start and end apart: 46, of which 32 were waited for; matrix products, arithmetic and copies ran while one was open for 2% of the time, Pallas kernels for 4%

profile of v9, /device:TPU:0, one launch (start us, length us, event | category | flops | bytes accessed | tf_op | source)
XLA Modules:
  0.0 161.3 jit_solution(7543600461367286286)
XLA Ops:
  7.9 1.0 copy-done.2
  9.6 2.0 %shard_map.77 = (bf16[2,128,256]{2,1,0:T(8,128)(2,1)S(1)}, bf16[2,128,256]{2,1,0:T(8,128)(2,1)S(1)}, bf16[2,128,256]{2,1,0:T(8,128)(2,1)S(1)}, bf16[2,128,256]{2,1,0:T(8,128)(2,1)S(1)}, s32[8]{0:T(128)S(1)}) custom-call(s32[16]{0:T(128)S(1)} %copy-done.4, bf16[8,128,256]{2,1,0:T(8,128)(2,1)S(1)} %copy-done.2), custom_call_target="tpu_custom_call" | custom-call | tf_op jit(solution)/shard_map/pallas_call | solution.py:456
  12.2 2.6 %collective-permute-start.1 = (bf16[2,128,256]{2,1,0:T(8,128)(2,1)S(1)}, bf16[2,128,256]{2,1,0:T(8,128)(2,1)S(1)}, u32[]{:S(2)}, u32[]{:S(2)}) collective-permute-start(bf16[2,128,256]{2,1,0:T(8,128)(2,1)S(1)} %get-tuple-element.49), channel_id=1, source_target_pairs={{0,16},{1,17},{2,18},{3,19},{4,20},{5,21},{6,22},{7,23},{8,24},{9,... | collective-permute-start | bytes 393224 | tf_op jit(solution)/shard_map/ppermute | solution.py:485
  14.9 2.9 %collective-permute-start.7 = (bf16[4,128,256]{2,1,0:T(8,128)(2,1)S(1)}, bf16[4,128,256]{2,1,0:T(8,128)(2,1)S(1)}, u32[]{:S(2)}, u32[]{:S(2)}) collective-permute-start(bf16[4,128,256]{2,1,0:T(8,128)(2,1)S(1)} %pad_maximum_fusion.1.refs_0_), channel_id=1, source_target_pairs={{0,8},{1,9},{2,10},{3,11},{4,0},{5,1},{6,2},{7,3},{8,12},{9,13},{1... | collective-permute-start | bytes 786440 | tf_op jit(solution)/shard_map/ppermute | solution.py:49
  17.7 1.5 collective-permute-start.6
  19.3 2.1 %collective-permute-done.2 = bf16[2,128,256]{2,1,0:T(8,128)(2,1)S(1)} collective-permute-done((bf16[2,128,256]{2,1,0:T(8,128)(2,1)S(1)}, bf16[2,128,256]{2,1,0:T(8,128)(2,1)S(1)}, u32[]{:S(2)}, u32[]{:S(2)}) %collective-permute-start.2) | collective-permute-done | bytes 131104 | tf_op jit(solution)/shard_map/ppermute | solution.py:486
  21.4 2.7 %collective-permute-start.4 = (bf16[4,128,256]{2,1,0:T(8,128)(2,1)S(1)}, bf16[4,128,256]{2,1,0:T(8,128)(2,1)S(1)}, u32[]{:S(2)}, u32[]{:S(2)}) collective-permute-start(bf16[4,128,256]{2,1,0:T(8,128)(2,1)S(1)} %pad_maximum_fusion.refs_9_), channel_id=1, source_target_pairs={{0,8},{1,9},{2,10},{3,11},{4,0},{5,1},{6,2},{7,3},{8,12},{9,13},{1... | collective-permute-start | bytes 786440 | tf_op jit(solution)/shard_map/ppermute | solution.py:49
  24.1 1.5 collective-permute-start.3
  25.7 1.1 collective-permute-done.6.refs_4_
  26.7 5.0 %collective-permute-done.4.refs_10_ = bf16[4,128,256]{2,1,0:T(8,128)(2,1)S(1)} collective-permute-done((bf16[4,128,256]{2,1,0:T(8,128)(2,1)S(1)}, bf16[4,128,256]{2,1,0:T(8,128)(2,1)S(1)}, u32[]{:S(2)}, u32[]{:S(2)}) %collective-permute-start.4) | collective-permute-done | bytes 262176 | tf_op jit(solution)/shard_map/ppermute | solution.py:49
  31.7 0.9 collective-permute-done.3.refs_13_
  32.6 2.5 %collective-permute-start.9 = (bf16[4,128,256]{2,1,0:T(8,128)(2,1)S(1)}, bf16[4,128,256]{2,1,0:T(8,128)(2,1)S(1)}, u32[]{:S(2)}, u32[]{:S(2)}) collective-permute-start(bf16[4,128,256]{2,1,0:T(8,128)(2,1)S(1)} %collective-permute-done.7.refs_1_), channel_id=1, source_target_pairs={{0,8},{1,9},{2,10},{3,11},{4,0},{5,1},{6,2},{7,3},{8,12},{9,13},{1... | collective-permute-start | bytes 786440 | tf_op jit(solution)/shard_map/ppermute | solution.py:49
  35.1 1.6 %collective-permute-start.8 = (bf16[4,128,256]{2,1,0:T(8,128)(2,1)S(1)}, bf16[4,128,256]{2,1,0:T(8,128)(2,1)S(1)}, u32[]{:S(2)}, u32[]{:S(2)}) collective-permute-start(bf16[4,128,256]{2,1,0:T(8,128)(2,1)S(1)} %collective-permute-done.7.refs_1_), channel_id=1, source_target_pairs={{0,2},{1,3},{2,0},{3,1},{4,6},{5,7},{6,4},{7,5},{8,10},{9,11},{10,... | collective-permute-start | bytes 786440 | tf_op jit(solution)/shard_map/ppermute | solution.py:40
  37.8 5.4 %collective-permute-done.9.refs_2_ = bf16[4,128,256]{2,1,0:T(8,128)(2,1)S(1)} collective-permute-done((bf16[4,128,256]{2,1,0:T(8,128)(2,1)S(1)}, bf16[4,128,256]{2,1,0:T(8,128)(2,1)S(1)}, u32[]{:S(2)}, u32[]{:S(2)}) %collective-permute-start.9) | collective-permute-done | bytes 262176 | tf_op jit(solution)/shard_map/ppermute | solution.py:49
  43.2 3.1 %collective-permute-done.8.refs_5_ = bf16[4,128,256]{2,1,0:T(8,128)(2,1)S(1)} collective-permute-done((bf16[4,128,256]{2,1,0:T(8,128)(2,1)S(1)}, bf16[4,128,256]{2,1,0:T(8,128)(2,1)S(1)}, u32[]{:S(2)}, u32[]{:S(2)}) %collective-permute-start.8) | collective-permute-done | bytes 262176 | tf_op jit(solution)/shard_map/ppermute | solution.py:40
  46.6 2.2 %collective-permute-start.10 = (bf16[4,128,256]{2,1,0:T(8,128)(2,1)S(1)}, bf16[4,128,256]{2,1,0:T(8,128)(2,1)S(1)}, u32[]{:S(2)}, u32[]{:S(2)}) collective-permute-start(bf16[4,128,256]{2,1,0:T(8,128)(2,1)S(1)} %collective-permute-done.9.refs_2_), channel_id=1, source_target_pairs={{0,2},{1,3},{2,0},{3,1},{4,6},{5,7},{6,4},{7,5},{8,10},{9,11},{10,... | collective-permute-start | bytes 786440 | tf_op jit(solution)/shard_map/ppermute | solution.py:40
  48.8 2.4 %collective-permute-done.15.refs_11_ = bf16[4,128,256]{2,1,0:T(8,128)(2,1)S(1)} collective-permute-done((bf16[4,128,256]{2,1,0:T(8,128)(2,1)S(1)}, bf16[4,128,256]{2,1,0:T(8,128)(2,1)S(1)}, u32[]{:S(2)}, u32[]{:S(2)}) %collective-permute-start.15) | collective-permute-done | bytes 262176 | tf_op jit(solution)/shard_map/ppermute | solution.py:49
  51.1 1.6 %collective-permute-done.14.refs_14_ = bf16[4,128,256]{2,1,0:T(8,128)(2,1)S(1)} collective-permute-done((bf16[4,128,256]{2,1,0:T(8,128)(2,1)S(1)}, bf16[4,128,256]{2,1,0:T(8,128)(2,1)S(1)}, u32[]{:S(2)}, u32[]{:S(2)}) %collective-permute-start.14) | collective-permute-done | bytes 262176 | tf_op jit(solution)/shard_map/ppermute | solution.py:40
  53.5 1.7 %collective-permute-start.17 = (bf16[4,128,256]{2,1,0:T(8,128)(2,1)S(1)}, bf16[4,128,256]{2,1,0:T(8,128)(2,1)S(1)}, u32[]{:S(2)}, u32[]{:S(2)}) collective-permute-start(bf16[4,128,256]{2,1,0:T(8,128)(2,1)S(1)} %collective-permute-done.15.refs_11_), channel_id=1, source_target_pairs={{0,8},{1,9},{2,10},{3,11},{4,0},{5,1},{6,2},{7,3},{8,12},{9,13},{1... | collective-permute-start | bytes 786440 | tf_op jit(solution)/shard_map/ppermute | solution.py:49
  55.2 2.0 %collective-permute-start.16 = (bf16[4,128,256]{2,1,0:T(8,128)(2,1)S(1)}, bf16[4,128,256]{2,1,0:T(8,128)(2,1)S(1)}, u32[]{:S(2)}, u32[]{:S(2)}) collective-permute-start(bf16[4,128,256]{2,1,0:T(8,128)(2,1)S(1)} %collective-permute-done.15.refs_11_), channel_id=1, source_target_pairs={{0,2},{1,3},{2,0},{3,1},{4,6},{5,7},{6,4},{7,5},{8,10},{9,11},{10,... | collective-permute-start | bytes 786440 | tf_op jit(solution)/shard_map/ppermute | solution.py:40
  57.3 1.1 collective-permute-done.10.refs_6_
  59.7 2.3 %collective-permute-start.13 = (bf16[2,128,256]{2,1,0:T(8,128)(2,1)}, bf16[2,128,256]{2,1,0:T(8,128)(2,1)S(1)}, u32[]{:S(2)}, u32[]{:S(2)}) collective-permute-start(bf16[2,128,256]{2,1,0:T(8,128)(2,1)} %slice.25), channel_id=1, source_target_pairs={{0,8},{1,9},{2,10},{3,11},{4,0},{5,1},{6,2},{7,3},{8,12},{9,13},{1... | collective-permute-start | bytes 393224 | tf_op jit(solution)/shard_map/ppermute | solution.py:49
  62.0 1.6 %collective-permute-start.12 = (bf16[2,128,256]{2,1,0:T(8,128)(2,1)}, bf16[2,128,256]{2,1,0:T(8,128)(2,1)}, u32[]{:S(2)}, u32[]{:S(2)}) collective-permute-start(bf16[2,128,256]{2,1,0:T(8,128)(2,1)} %slice.24), channel_id=1, source_target_pairs={{0,2},{1,3},{2,0},{3,1},{4,6},{5,7},{6,4},{7,5},{8,10},{9,11},{10,... | collective-permute-start | bytes 393224 | tf_op jit(solution)/shard_map/ppermute | solution.py:40
  64.9 2.7 %collective-permute-start.19 = (bf16[2,128,256]{2,1,0:T(8,128)(2,1)}, bf16[2,128,256]{2,1,0:T(8,128)(2,1)}, u32[]{:S(2)}, u32[]{:S(2)}) collective-permute-start(bf16[2,128,256]{2,1,0:T(8,128)(2,1)} %slice.27), channel_id=1, source_target_pairs={{0,8},{1,9},{2,10},{3,11},{4,0},{5,1},{6,2},{7,3},{8,12},{9,13},{1... | collective-permute-start | bytes 393224 | tf_op jit(solution)/shard_map/ppermute | solution.py:49
  67.6 1.6 %collective-permute-start.18 = (bf16[2,128,256]{2,1,0:T(8,128)(2,1)}, bf16[2,128,256]{2,1,0:T(8,128)(2,1)}, u32[]{:S(2)}, u32[]{:S(2)}) collective-permute-start(bf16[2,128,256]{2,1,0:T(8,128)(2,1)} %slice.26), channel_id=1, source_target_pairs={{0,2},{1,3},{2,0},{3,1},{4,6},{5,7},{6,4},{7,5},{8,10},{9,11},{10,... | collective-permute-start | bytes 393224 | tf_op jit(solution)/shard_map/ppermute | solution.py:40
  69.2 1.2 copy-done.1
  70.8 2.0 %collective-permute-done.18.refs_16_ = bf16[2,128,256]{2,1,0:T(8,128)(2,1)} collective-permute-done((bf16[2,128,256]{2,1,0:T(8,128)(2,1)}, bf16[2,128,256]{2,1,0:T(8,128)(2,1)}, u32[]{:S(2)}, u32[]{:S(2)}) %collective-permute-start.18) | collective-permute-done | bytes 131104 | tf_op jit(solution)/shard_map/ppermute | solution.py:40
  72.9 1.6 copy-done.5
  74.5 0.9 copy-done.7
  75.4 6.7 %shard_map.79 = (bf16[2,8,2,128,256]{4,3,2,1,0:T(8,128)(2,1)S(1)}, bf16[2,8,2,128,256]{4,3,2,1,0:T(8,128)(2,1)S(1)}, f32[4,32]{1,0:T(4,128)S(1)}) custom-call(bf16[32,128,256]{2,1,0:T(8,128)(2,1)S(1)} %copy-done.5, bf16[32,128,256]{2,1,0:T(8,128)(2,1)} %collective-permute-done.rot_theirs, bf16[256,2048]{1,0:T(8,128)(2,1)S(1)} %shard_map.78.trial, ...), custom_call_target="tpu_custom_call" | custom-call | flops 3087007744 | bytes 15204352 | tf_op jit(solution)/shard_map/pallas_call | solution.py:196
  82.8 2.4 %collective-permute-start.21 = (f32[4,32]{1,0:T(4,128)S(1)}, f32[4,32]{1,0:T(4,128)S(1)}, u32[]{:S(2)}, u32[]{:S(2)}) collective-permute-start(f32[4,32]{1,0:T(4,128)S(1)} %get-tuple-element.69), channel_id=1, source_target_pairs={{0,4},{1,5},{2,6},{3,7},{4,0},{5,1},{6,2},{7,3},{8,12},{9,13},{10,... | collective-permute-start | bytes 1544 | tf_op jit(solution)/shard_map/ppermute | solution.py:43
  85.6 1.0 collective-permute-done.22
  86.8 2.0 %collective-permute-done.20 = f32[4,32]{1,0:T(4,128)S(1)} collective-permute-done((f32[4,32]{1,0:T(4,128)S(1)}, f32[4,32]{1,0:T(4,128)S(1)}, u32[]{:S(2)}, u32[]{:S(2)}) %collective-permute-start.20) | collective-permute-done | bytes 544 | tf_op jit(solution)/shard_map/ppermute | solution.py:43
  88.8 1.0 collective-permute-start.24
  89.9 2.0 %collective-permute-start.23 = (f32[4,32]{1,0:T(4,128)S(1)}, f32[4,32]{1,0:T(4,128)S(1)}, u32[]{:S(2)}, u32[]{:S(2)}) collective-permute-start(f32[4,32]{1,0:T(4,128)S(1)} %add_add_fusion.mine), channel_id=1, source_target_pairs={{0,8},{1,9},{2,10},{3,11},{4,12},{5,13},{6,14},{7,15},{8,0},{9,1},... | collective-permute-start | bytes 1544 | tf_op jit(solution)/shard_map/ppermute | solution.py:43
  91.9 0.9 collective-permute-done.25.theirs_across
  92.7 1.6 collective-permute-done.23.mine_across
  94.3 5.8 %copy-done = bf16[32,128,2048]{2,1,0:T(8,128)(2,1)S(1)} copy-done((bf16[32,128,2048]{2,1,0:T(8,128)(2,1)S(1)}, bf16[32,128,2048]{2,1,0:T(8,128)(2,1)}, u32[]{:S(2)}) %copy-start) | copy-done | bytes 16777240
  100.1 3.2 %shard_map.80 = (f32[8,32]{1,0:T(8,128)}, bf16[4,128,2048]{2,1,0:T(8,128)(2,1)S(1)}, bf16[4,64,2048]{2,1,0:T(8,128)(2,1)S(1)}, bf16[4,64,2048]{2,1,0:T(8,128)(2,1)S(1)}) custom-call(s32[8]{0:T(128)S(1)} %get-tuple-element.48.order, f32[8,32]{1,0:T(8,128)S(1)} %copy-done.3, f32[4,32]{1,0:T(4,128)S(1)} %add_add_fusion.mine, ...), custom_call_target="tpu_custom_call" | custom-call | tf_op jit(solution)/shard_map/pallas_call | solution.py:265
  104.6 2.1 %collective-permute-start.29 = (bf16[4,128,256]{2,1,0:T(8,128)(2,1)S(1)}, bf16[4,128,256]{2,1,0:T(8,128)(2,1)S(1)}, u32[]{:S(2)}, u32[]{:S(2)}) collective-permute-start(bf16[4,128,256]{2,1,0:T(8,128)(2,1)S(1)} %get-tuple-element.76.refs_3_), channel_id=1, source_target_pairs={{0,8},{1,9},{2,10},{3,11},{4,0},{5,1},{6,2},{7,3},{8,12},{9,13},{1... | collective-permute-start | bytes 786440 | tf_op jit(solution)/shard_map/ppermute | solution.py:49
  108.2 2.1 %collective-permute-start.37 = (bf16[4,128,256]{2,1,0:T(8,128)(2,1)S(1)}, bf16[4,128,256]{2,1,0:T(8,128)(2,1)S(1)}, u32[]{:S(2)}, u32[]{:S(2)}) collective-permute-start(bf16[4,128,256]{2,1,0:T(8,128)(2,1)S(1)} %get-tuple-element.83.refs_12_), channel_id=1, source_target_pairs={{0,8},{1,9},{2,10},{3,11},{4,0},{5,1},{6,2},{7,3},{8,12},{9,13},{1... | collective-permute-start | bytes 786440 | tf_op jit(solution)/shard_map/ppermute | solution.py:49
  110.7 3.1 %collective-permute-done.29.refs_4_ = bf16[4,128,256]{2,1,0:T(8,128)(2,1)S(1)} collective-permute-done((bf16[4,128,256]{2,1,0:T(8,128)(2,1)S(1)}, bf16[4,128,256]{2,1,0:T(8,128)(2,1)S(1)}, u32[]{:S(2)}, u32[]{:S(2)}) %collective-permute-start.29) | collective-permute-done | bytes 262176 | tf_op jit(solution)/shard_map/ppermute | solution.py:49
  113.8 2.1 %collective-permute-done.28.refs_7_ = bf16[4,128,256]{2,1,0:T(8,128)(2,1)S(1)} collective-permute-done((bf16[4,128,256]{2,1,0:T(8,128)(2,1)S(1)}, bf16[4,128,256]{2,1,0:T(8,128)(2,1)S(1)}, u32[]{:S(2)}, u32[]{:S(2)}) %collective-permute-start.28) | collective-permute-done | bytes 262176 | tf_op jit(solution)/shard_map/ppermute | solution.py:40
  115.9 0.9 collective-permute-start.31
  117.1 2.3 %collective-permute-done.37.refs_13_ = bf16[4,128,256]{2,1,0:T(8,128)(2,1)S(1)} collective-permute-done((bf16[4,128,256]{2,1,0:T(8,128)(2,1)S(1)}, bf16[4,128,256]{2,1,0:T(8,128)(2,1)S(1)}, u32[]{:S(2)}, u32[]{:S(2)}) %collective-permute-start.37) | collective-permute-done | bytes 262176 | tf_op jit(solution)/shard_map/ppermute | solution.py:49
  119.4 2.1 %collective-permute-done.36.refs_16_ = bf16[4,128,256]{2,1,0:T(8,128)(2,1)S(1)} collective-permute-done((bf16[4,128,256]{2,1,0:T(8,128)(2,1)S(1)}, bf16[4,128,256]{2,1,0:T(8,128)(2,1)S(1)}, u32[]{:S(2)}, u32[]{:S(2)}) %collective-permute-start.36) | collective-permute-done | bytes 262176 | tf_op jit(solution)/shard_map/ppermute | solution.py:40
  121.5 0.9 collective-permute-start.39
  122.7 2.4 %collective-permute-done.31.refs_5_ = bf16[4,128,256]{2,1,0:T(8,128)(2,1)S(1)} collective-permute-done((bf16[4,128,256]{2,1,0:T(8,128)(2,1)S(1)}, bf16[4,128,256]{2,1,0:T(8,128)(2,1)S(1)}, u32[]{:S(2)}, u32[]{:S(2)}) %collective-permute-start.31) | collective-permute-done | bytes 262176 | tf_op jit(solution)/shard_map/ppermute | solution.py:49
  125.1 2.0 %collective-permute-done.30.refs_8_ = bf16[4,128,256]{2,1,0:T(8,128)(2,1)S(1)} collective-permute-done((bf16[4,128,256]{2,1,0:T(8,128)(2,1)S(1)}, bf16[4,128,256]{2,1,0:T(8,128)(2,1)S(1)}, u32[]{:S(2)}, u32[]{:S(2)}) %collective-permute-start.30) | collective-permute-done | bytes 262176 | tf_op jit(solution)/shard_map/ppermute | solution.py:40
  127.1 0.9 collective-permute-start.33
  128.4 2.4 %collective-permute-done.39.refs_14_ = bf16[4,128,256]{2,1,0:T(8,128)(2,1)S(1)} collective-permute-done((bf16[4,128,256]{2,1,0:T(8,128)(2,1)S(1)}, bf16[4,128,256]{2,1,0:T(8,128)(2,1)S(1)}, u32[]{:S(2)}, u32[]{:S(2)}) %collective-permute-start.39) | collective-permute-done | bytes 262176 | tf_op jit(solution)/shard_map/ppermute | solution.py:49
  130.7 2.0 %collective-permute-done.38.refs_17_ = bf16[4,128,256]{2,1,0:T(8,128)(2,1)S(1)} collective-permute-done((bf16[4,128,256]{2,1,0:T(8,128)(2,1)S(1)}, bf16[4,128,256]{2,1,0:T(8,128)(2,1)S(1)}, u32[]{:S(2)}, u32[]{:S(2)}) %collective-permute-start.38) | collective-permute-done | bytes 262176 | tf_op jit(solution)/shard_map/ppermute | solution.py:40
  132.7 0.9 collective-permute-start.41
  134.0 2.4 %collective-permute-done.33.refs_6_ = bf16[4,128,256]{2,1,0:T(8,128)(2,1)S(1)} collective-permute-done((bf16[4,128,256]{2,1,0:T(8,128)(2,1)S(1)}, bf16[4,128,256]{2,1,0:T(8,128)(2,1)S(1)}, u32[]{:S(2)}, u32[]{:S(2)}) %collective-permute-start.33) | collective-permute-done | bytes 262176 | tf_op jit(solution)/shard_map/ppermute | solution.py:49
  136.3 2.0 %collective-permute-done.32.refs_9_ = bf16[4,128,256]{2,1,0:T(8,128)(2,1)S(1)} collective-permute-done((bf16[4,128,256]{2,1,0:T(8,128)(2,1)S(1)}, bf16[4,128,256]{2,1,0:T(8,128)(2,1)S(1)}, u32[]{:S(2)}, u32[]{:S(2)}) %collective-permute-start.32) | collective-permute-done | bytes 262176 | tf_op jit(solution)/shard_map/ppermute | solution.py:40
  138.4 0.9 collective-permute-start.35
  139.7 2.3 %collective-permute-done.41.refs_15_ = bf16[4,128,256]{2,1,0:T(8,128)(2,1)S(1)} collective-permute-done((bf16[4,128,256]{2,1,0:T(8,128)(2,1)S(1)}, bf16[4,128,256]{2,1,0:T(8,128)(2,1)S(1)}, u32[]{:S(2)}, u32[]{:S(2)}) %collective-permute-start.41) | collective-permute-done | bytes 262176 | tf_op jit(solution)/shard_map/ppermute | solution.py:49
  142.0 2.0 %collective-permute-done.40.refs_18_ = bf16[4,128,256]{2,1,0:T(8,128)(2,1)S(1)} collective-permute-done((bf16[4,128,256]{2,1,0:T(8,128)(2,1)S(1)}, bf16[4,128,256]{2,1,0:T(8,128)(2,1)S(1)}, u32[]{:S(2)}, u32[]{:S(2)}) %collective-permute-start.40) | collective-permute-done | bytes 262176 | tf_op jit(solution)/shard_map/ppermute | solution.py:40
  144.0 0.9 collective-permute-start.43
  145.6 3.4 %collective-permute-done.43.refs_20_ = bf16[2,128,256]{2,1,0:T(8,128)(2,1)S(1)} collective-permute-done((bf16[2,128,256]{2,1,0:T(8,128)(2,1)S(1)}, bf16[2,128,256]{2,1,0:T(8,128)(2,1)S(1)}, u32[]{:S(2)}, u32[]{:S(2)}) %collective-permute-start.43) | collective-permute-done | bytes 131104 | tf_op jit(solution)/shard_map/ppermute | solution.py:49
  149.0 0.9 collective-permute-done.42.refs_19_
  149.9 1.1 shard_map.83
  151.1 2.0 %shard_map.84._ = bf16[8,128,256]{2,1,0:T(8,128)(2,1)} custom-call(s32[8]{0:T(128)S(1)} %get-tuple-element.48.order, bf16[4,128,2048]{2,1,0:T(8,128)(2,1)S(1)} %get-tuple-element.75.refs_0_.potential, f32[4,128,256]{2,1,0:T(8,128)S(1)} %get-tuple-element.91.base, bf16[4,8,2,128,256]{4,3,2,1,0:T(8,128)(2,1)S(1)} %get-tuple-element.92.full), custom_call_target="tpu_custom_call" | custom-call | flops 536870912 | bytes 6291456 | tf_op jit(solution)/shard_map/pallas_call | solution.py:370
  153.1 1.3 shard_map.85
  (67 shorter events, 14.6 us)
Async XLA Ops:
  7.2 62.1 %all-gather.2.cloned.1.call-start = ((), (), s32[]{:S(2)}) async-start(), calls=%async_computation | async-start | bytes 1114112 | tf_op jit(solution)/shard_map/all_gather | solution.py:527
  7.2 63.6 %collective-permute-start = (bf16[32,128,256]{2,1,0:T(8,128)(2,1)}, bf16[32,128,256]{2,1,0:T(8,128)(2,1)}, u32[]{:S(2)}, u32[]{:S(2)}) collective-permute-start(bf16[32,128,256]{2,1,0:T(8,128)(2,1)} %rot_mine.1), channel_id=1, source_target_pairs={{0,1},{1,0},{2,3},{3,2},{4,5},{5,4},{6,7},{7,6},{8,9},{9,8},{10,11... | collective-permute-start | bytes 6291464 | tf_op jit(solution)/shard_map/ppermute | solution.py:40
  7.9 1.0 copy-start.2
  8.9 0.7 copy-start.4
  11.7 3.2 %collective-permute-start.5 = (bf16[2,128,256]{2,1,0:T(8,128)(2,1)S(1)}, bf16[2,128,256]{2,1,0:T(8,128)(2,1)S(1)}, u32[]{:S(2)}, u32[]{:S(2)}) collective-permute-start(bf16[2,128,256]{2,1,0:T(8,128)(2,1)S(1)} %get-tuple-element.52), channel_id=1, source_target_pairs={{0,1},{1,0},{2,3},{3,2},{4,5},{5,4},{6,7},{7,6},{8,9},{9,8},{10,11... | collective-permute-start | bytes 393224 | tf_op jit(solution)/shard_map/ppermute | solution.py:40
  12.2 7.1 %collective-permute-start.1 = (bf16[2,128,256]{2,1,0:T(8,128)(2,1)S(1)}, bf16[2,128,256]{2,1,0:T(8,128)(2,1)S(1)}, u32[]{:S(2)}, u32[]{:S(2)}) collective-permute-start(bf16[2,128,256]{2,1,0:T(8,128)(2,1)S(1)} %get-tuple-element.49), channel_id=1, source_target_pairs={{0,16},{1,17},{2,18},{3,19},{4,20},{5,21},{6,22},{7,23},{8,24},{9,... | collective-permute-start | bytes 393224 | tf_op jit(solution)/shard_map/ppermute | solution.py:485
  14.7 6.6 %collective-permute-start.2 = (bf16[2,128,256]{2,1,0:T(8,128)(2,1)S(1)}, bf16[2,128,256]{2,1,0:T(8,128)(2,1)S(1)}, u32[]{:S(2)}, u32[]{:S(2)}) collective-permute-start(bf16[2,128,256]{2,1,0:T(8,128)(2,1)S(1)} %get-tuple-element.50), channel_id=1, source_target_pairs={{0,17},{1,16},{2,19},{3,18},{4,21},{5,20},{6,23},{7,22},{8,25},{9,... | collective-permute-start | bytes 393224 | tf_op jit(solution)/shard_map/ppermute | solution.py:486
  14.9 10.8 %collective-permute-start.7 = (bf16[4,128,256]{2,1,0:T(8,128)(2,1)S(1)}, bf16[4,128,256]{2,1,0:T(8,128)(2,1)S(1)}, u32[]{:S(2)}, u32[]{:S(2)}) collective-permute-start(bf16[4,128,256]{2,1,0:T(8,128)(2,1)S(1)} %pad_maximum_fusion.1.refs_0_), channel_id=1, source_target_pairs={{0,8},{1,9},{2,10},{3,11},{4,0},{5,1},{6,2},{7,3},{8,12},{9,13},{1... | collective-permute-start | bytes 786440 | tf_op jit(solution)/shard_map/ppermute | solution.py:49
  17.7 9.0 %collective-permute-start.6 = (bf16[4,128,256]{2,1,0:T(8,128)(2,1)S(1)}, bf16[4,128,256]{2,1,0:T(8,128)(2,1)S(1)}, u32[]{:S(2)}, u32[]{:S(2)}) collective-permute-start(bf16[4,128,256]{2,1,0:T(8,128)(2,1)S(1)} %pad_maximum_fusion.1.refs_0_), channel_id=1, source_target_pairs={{0,2},{1,3},{2,0},{3,1},{4,6},{5,7},{6,4},{7,5},{8,10},{9,11},{10,... | collective-permute-start | bytes 786440 | tf_op jit(solution)/shard_map/ppermute | solution.py:40
  21.4 10.3 %collective-permute-start.4 = (bf16[4,128,256]{2,1,0:T(8,128)(2,1)S(1)}, bf16[4,128,256]{2,1,0:T(8,128)(2,1)S(1)}, u32[]{:S(2)}, u32[]{:S(2)}) collective-permute-start(bf16[4,128,256]{2,1,0:T(8,128)(2,1)S(1)} %pad_maximum_fusion.refs_9_), channel_id=1, source_target_pairs={{0,8},{1,9},{2,10},{3,11},{4,0},{5,1},{6,2},{7,3},{8,12},{9,13},{1... | collective-permute-start | bytes 786440 | tf_op jit(solution)/shard_map/ppermute | solution.py:49
  24.1 8.5 %collective-permute-start.3 = (bf16[4,128,256]{2,1,0:T(8,128)(2,1)S(1)}, bf16[4,128,256]{2,1,0:T(8,128)(2,1)S(1)}, u32[]{:S(2)}, u32[]{:S(2)}) collective-permute-start(bf16[4,128,256]{2,1,0:T(8,128)(2,1)S(1)} %pad_maximum_fusion.refs_9_), channel_id=1, source_target_pairs={{0,2},{1,3},{2,0},{3,1},{4,6},{5,7},{6,4},{7,5},{8,10},{9,11},{10,... | collective-permute-start | bytes 786440 | tf_op jit(solution)/shard_map/ppermute | solution.py:40
  32.6 10.6 %collective-permute-start.9 = (bf16[4,128,256]{2,1,0:T(8,128)(2,1)S(1)}, bf16[4,128,256]{2,1,0:T(8,128)(2,1)S(1)}, u32[]{:S(2)}, u32[]{:S(2)}) collective-permute-start(bf16[4,128,256]{2,1,0:T(8,128)(2,1)S(1)} %collective-permute-done.7.refs_1_), channel_id=1, source_target_pairs={{0,8},{1,9},{2,10},{3,11},{4,0},{5,1},{6,2},{7,3},{8,12},{9,13},{1... | collective-permute-start | bytes 786440 | tf_op jit(solution)/shard_map/ppermute | solution.py:49
  35.1 11.2 %collective-permute-start.8 = (bf16[4,128,256]{2,1,0:T(8,128)(2,1)S(1)}, bf16[4,128,256]{2,1,0:T(8,128)(2,1)S(1)}, u32[]{:S(2)}, u32[]{:S(2)}) collective-permute-start(bf16[4,128,256]{2,1,0:T(8,128)(2,1)S(1)} %collective-permute-done.7.refs_1_), channel_id=1, source_target_pairs={{0,2},{1,3},{2,0},{3,1},{4,6},{5,7},{6,4},{7,5},{8,10},{9,11},{10,... | collective-permute-start | bytes 786440 | tf_op jit(solution)/shard_map/ppermute | solution.py:40
  36.7 14.4 %collective-permute-start.15 = (bf16[4,128,256]{2,1,0:T(8,128)(2,1)S(1)}, bf16[4,128,256]{2,1,0:T(8,128)(2,1)S(1)}, u32[]{:S(2)}, u32[]{:S(2)}) collective-permute-start(bf16[4,128,256]{2,1,0:T(8,128)(2,1)S(1)} %collective-permute-done.4.refs_10_), channel_id=1, source_target_pairs={{0,8},{1,9},{2,10},{3,11},{4,0},{5,1},{6,2},{7,3},{8,12},{9,13},{1... | collective-permute-start | bytes 786440 | tf_op jit(solution)/shard_map/ppermute | solution.py:49
  37.4 15.4 %collective-permute-start.14 = (bf16[4,128,256]{2,1,0:T(8,128)(2,1)S(1)}, bf16[4,128,256]{2,1,0:T(8,128)(2,1)S(1)}, u32[]{:S(2)}, u32[]{:S(2)}) collective-permute-start(bf16[4,128,256]{2,1,0:T(8,128)(2,1)S(1)} %collective-permute-done.4.refs_10_), channel_id=1, source_target_pairs={{0,2},{1,3},{2,0},{3,1},{4,6},{5,7},{6,4},{7,5},{8,10},{9,11},{10,... | collective-permute-start | bytes 786440 | tf_op jit(solution)/shard_map/ppermute | solution.py:40
  46.3 11.0 %collective-permute-start.11 = (bf16[4,128,256]{2,1,0:T(8,128)(2,1)S(1)}, bf16[4,128,256]{2,1,0:T(8,128)(2,1)S(1)}, u32[]{:S(2)}, u32[]{:S(2)}) collective-permute-start(bf16[4,128,256]{2,1,0:T(8,128)(2,1)S(1)} %collective-permute-done.9.refs_2_), channel_id=1, source_target_pairs={{0,8},{1,9},{2,10},{3,11},{4,0},{5,1},{6,2},{7,3},{8,12},{9,13},{1... | collective-permute-start | bytes 786440 | tf_op jit(solution)/shard_map/ppermute | solution.py:49
  46.6 11.8 %collective-permute-start.10 = (bf16[4,128,256]{2,1,0:T(8,128)(2,1)S(1)}, bf16[4,128,256]{2,1,0:T(8,128)(2,1)S(1)}, u32[]{:S(2)}, u32[]{:S(2)}) collective-permute-start(bf16[4,128,256]{2,1,0:T(8,128)(2,1)S(1)} %collective-permute-done.9.refs_2_), channel_id=1, source_target_pairs={{0,2},{1,3},{2,0},{3,1},{4,6},{5,7},{6,4},{7,5},{8,10},{9,11},{10,... | collective-permute-start | bytes 786440 | tf_op jit(solution)/shard_map/ppermute | solution.py:40
  52.8 0.7 copy-start.6
  53.5 10.1 %collective-permute-start.17 = (bf16[4,128,256]{2,1,0:T(8,128)(2,1)S(1)}, bf16[4,128,256]{2,1,0:T(8,128)(2,1)S(1)}, u32[]{:S(2)}, u32[]{:S(2)}) collective-permute-start(bf16[4,128,256]{2,1,0:T(8,128)(2,1)S(1)} %collective-permute-done.15.refs_11_), channel_id=1, source_target_pairs={{0,8},{1,9},{2,10},{3,11},{4,0},{5,1},{6,2},{7,3},{8,12},{9,13},{1... | collective-permute-start | bytes 786440 | tf_op jit(solution)/shard_map/ppermute | solution.py:49
  55.2 8.4 %collective-permute-start.16 = (bf16[4,128,256]{2,1,0:T(8,128)(2,1)S(1)}, bf16[4,128,256]{2,1,0:T(8,128)(2,1)S(1)}, u32[]{:S(2)}, u32[]{:S(2)}) collective-permute-start(bf16[4,128,256]{2,1,0:T(8,128)(2,1)S(1)} %collective-permute-done.15.refs_11_), channel_id=1, source_target_pairs={{0,2},{1,3},{2,0},{3,1},{4,6},{5,7},{6,4},{7,5},{8,10},{9,11},{10,... | collective-permute-start | bytes 786440 | tf_op jit(solution)/shard_map/ppermute | solution.py:40
  59.7 11.1 %collective-permute-start.13 = (bf16[2,128,256]{2,1,0:T(8,128)(2,1)}, bf16[2,128,256]{2,1,0:T(8,128)(2,1)S(1)}, u32[]{:S(2)}, u32[]{:S(2)}) collective-permute-start(bf16[2,128,256]{2,1,0:T(8,128)(2,1)} %slice.25), channel_id=1, source_target_pairs={{0,8},{1,9},{2,10},{3,11},{4,0},{5,1},{6,2},{7,3},{8,12},{9,13},{1... | collective-permute-start | bytes 393224 | tf_op jit(solution)/shard_map/ppermute | solution.py:49
  62.0 8.8 %collective-permute-start.12 = (bf16[2,128,256]{2,1,0:T(8,128)(2,1)}, bf16[2,128,256]{2,1,0:T(8,128)(2,1)}, u32[]{:S(2)}, u32[]{:S(2)}) collective-permute-start(bf16[2,128,256]{2,1,0:T(8,128)(2,1)} %slice.24), channel_id=1, source_target_pairs={{0,2},{1,3},{2,0},{3,1},{4,6},{5,7},{6,4},{7,5},{8,10},{9,11},{10,... | collective-permute-start | bytes 393224 | tf_op jit(solution)/shard_map/ppermute | solution.py:40
  64.9 5.9 %collective-permute-start.19 = (bf16[2,128,256]{2,1,0:T(8,128)(2,1)}, bf16[2,128,256]{2,1,0:T(8,128)(2,1)}, u32[]{:S(2)}, u32[]{:S(2)}) collective-permute-start(bf16[2,128,256]{2,1,0:T(8,128)(2,1)} %slice.27), channel_id=1, source_target_pairs={{0,8},{1,9},{2,10},{3,11},{4,0},{5,1},{6,2},{7,3},{8,12},{9,13},{1... | collective-permute-start | bytes 393224 | tf_op jit(solution)/shard_map/ppermute | solution.py:49
  67.6 5.3 %collective-permute-start.18 = (bf16[2,128,256]{2,1,0:T(8,128)(2,1)}, bf16[2,128,256]{2,1,0:T(8,128)(2,1)}, u32[]{:S(2)}, u32[]{:S(2)}) collective-permute-start(bf16[2,128,256]{2,1,0:T(8,128)(2,1)} %slice.26), channel_id=1, source_target_pairs={{0,2},{1,3},{2,0},{3,1},{4,6},{5,7},{6,4},{7,5},{8,10},{9,11},{10,... | collective-permute-start | bytes 393224 | tf_op jit(solution)/shard_map/ppermute | solution.py:40
  69.2 1.2 copy-start.1
  70.8 23.5 %copy-start.3 = (f32[8,32]{1,0:T(8,128)S(1)}, f32[8,32]{1,0:T(8,128)}, u32[]{:S(2)}) copy-start(f32[8,32]{1,0:T(8,128)} %fields.1) | copy-start | bytes 3076
  72.9 1.6 copy-start.5
  74.5 0.9 copy-start.7
  82.1 4.5 %collective-permute-start.22 = (f32[4,32]{1,0:T(4,128)S(1)}, f32[4,32]{1,0:T(4,128)S(1)}, u32[]{:S(2)}, u32[]{:S(2)}) collective-permute-start(f32[4,32]{1,0:T(4,128)S(1)} %get-tuple-element.69), channel_id=1, source_target_pairs={{0,6},{1,7},{2,4},{3,5},{4,2},{5,3},{6,0},{7,1},{8,14},{9,15},{10,... | collective-permute-start | bytes 1544 | tf_op jit(solution)/shard_map/ppermute | solution.py:43
  82.8 4.0 %collective-permute-start.21 = (f32[4,32]{1,0:T(4,128)S(1)}, f32[4,32]{1,0:T(4,128)S(1)}, u32[]{:S(2)}, u32[]{:S(2)}) collective-permute-start(f32[4,32]{1,0:T(4,128)S(1)} %get-tuple-element.69), channel_id=1, source_target_pairs={{0,4},{1,5},{2,6},{3,7},{4,0},{5,1},{6,2},{7,3},{8,12},{9,13},{10,... | collective-permute-start | bytes 1544 | tf_op jit(solution)/shard_map/ppermute | solution.py:43
  85.2 3.6 %collective-permute-start.20 = (f32[4,32]{1,0:T(4,128)S(1)}, f32[4,32]{1,0:T(4,128)S(1)}, u32[]{:S(2)}, u32[]{:S(2)}) collective-permute-start(f32[4,32]{1,0:T(4,128)S(1)} %get-tuple-element.69), channel_id=1, source_target_pairs={{0,2},{1,3},{2,0},{3,1},{4,6},{5,7},{6,4},{7,5},{8,10},{9,11},{10,... | collective-permute-start | bytes 1544 | tf_op jit(solution)/shard_map/ppermute | solution.py:43
  88.8 3.9 %collective-permute-start.25 = (f32[4,32]{1,0:T(4,128)S(1)}, f32[4,32]{1,0:T(4,128)S(1)}, u32[]{:S(2)}, u32[]{:S(2)}) collective-permute-start(f32[4,32]{1,0:T(4,128)S(1)} %add_add_fusion.mine), channel_id=1, source_target_pairs={{0,9},{1,8},{2,11},{3,10},{4,13},{5,12},{6,15},{7,14},{8,1},{9,0},... | collective-permute-start | bytes 1544 | tf_op jit(solution)/shard_map/ppermute | solution.py:43
  88.8 3.9 %collective-permute-start.24 = (f32[4,32]{1,0:T(4,128)S(1)}, f32[4,32]{1,0:T(4,128)S(1)}, u32[]{:S(2)}, u32[]{:S(2)}) collective-permute-start(f32[4,32]{1,0:T(4,128)S(1)} %add_add_fusion.mine), channel_id=1, source_target_pairs={{0,1},{1,0},{2,3},{3,2},{4,5},{5,4},{6,7},{7,6},{8,9},{9,8},{10,11... | collective-permute-start | bytes 1544 | tf_op jit(solution)/shard_map/ppermute | solution.py:43
  89.9 4.5 %collective-permute-start.23 = (f32[4,32]{1,0:T(4,128)S(1)}, f32[4,32]{1,0:T(4,128)S(1)}, u32[]{:S(2)}, u32[]{:S(2)}) collective-permute-start(f32[4,32]{1,0:T(4,128)S(1)} %add_add_fusion.mine), channel_id=1, source_target_pairs={{0,8},{1,9},{2,10},{3,11},{4,12},{5,13},{6,14},{7,15},{8,0},{9,1},... | collective-permute-start | bytes 1544 | tf_op jit(solution)/shard_map/ppermute | solution.py:43
  94.3 5.8 %copy-start = (bf16[32,128,2048]{2,1,0:T(8,128)(2,1)S(1)}, bf16[32,128,2048]{2,1,0:T(8,128)(2,1)}, u32[]{:S(2)}) copy-start(bf16[32,128,2048]{2,1,0:T(8,128)(2,1)} %cholesky.1) | copy-start | bytes 50331652
  103.3 3.8 %collective-permute-start.26 = (bf16[4,64,2048]{2,1,0:T(8,128)(2,1)S(1)}, bf16[4,64,2048]{2,1,0:T(8,128)(2,1)S(1)}, u32[]{:S(2)}, u32[]{:S(2)}) collective-permute-start(bf16[4,64,2048]{2,1,0:T(8,128)(2,1)S(1)} %get-tuple-element.70), channel_id=1, source_target_pairs={{0,1},{1,0},{2,3},{3,2},{4,5},{5,4},{6,7},{7,6},{8,9},{9,8},{10,11... | collective-permute-start | bytes 3145736 | tf_op jit(solution)/shard_map/ppermute | solution.py:40
  103.4 4.1 %collective-permute-start.27 = (bf16[4,64,2048]{2,1,0:T(8,128)(2,1)S(1)}, bf16[4,64,2048]{2,1,0:T(8,128)(2,1)S(1)}, u32[]{:S(2)}, u32[]{:S(2)}) collective-permute-start(bf16[4,64,2048]{2,1,0:T(8,128)(2,1)S(1)} %get-tuple-element.71), channel_id=1, source_target_pairs={{0,1},{1,0},{2,3},{3,2},{4,5},{5,4},{6,7},{7,6},{8,9},{9,8},{10,11... | collective-permute-start | bytes 3145736 | tf_op jit(solution)/shard_map/ppermute | solution.py:40
  104.6 9.2 %collective-permute-start.29 = (bf16[4,128,256]{2,1,0:T(8,128)(2,1)S(1)}, bf16[4,128,256]{2,1,0:T(8,128)(2,1)S(1)}, u32[]{:S(2)}, u32[]{:S(2)}) collective-permute-start(bf16[4,128,256]{2,1,0:T(8,128)(2,1)S(1)} %get-tuple-element.76.refs_3_), channel_id=1, source_target_pairs={{0,8},{1,9},{2,10},{3,11},{4,0},{5,1},{6,2},{7,3},{8,12},{9,13},{1... | collective-permute-start | bytes 786440 | tf_op jit(solution)/shard_map/ppermute | solution.py:49
  106.7 9.2 %collective-permute-start.28 = (bf16[4,128,256]{2,1,0:T(8,128)(2,1)S(1)}, bf16[4,128,256]{2,1,0:T(8,128)(2,1)S(1)}, u32[]{:S(2)}, u32[]{:S(2)}) collective-permute-start(bf16[4,128,256]{2,1,0:T(8,128)(2,1)S(1)} %get-tuple-element.76.refs_3_), channel_id=1, source_target_pairs={{0,2},{1,3},{2,0},{3,1},{4,6},{5,7},{6,4},{7,5},{8,10},{9,11},{10,... | collective-permute-start | bytes 786440 | tf_op jit(solution)/shard_map/ppermute | solution.py:40
  108.2 11.2 %collective-permute-start.37 = (bf16[4,128,256]{2,1,0:T(8,128)(2,1)S(1)}, bf16[4,128,256]{2,1,0:T(8,128)(2,1)S(1)}, u32[]{:S(2)}, u32[]{:S(2)}) collective-permute-start(bf16[4,128,256]{2,1,0:T(8,128)(2,1)S(1)} %get-tuple-element.83.refs_12_), channel_id=1, source_target_pairs={{0,8},{1,9},{2,10},{3,11},{4,0},{5,1},{6,2},{7,3},{8,12},{9,13},{1... | collective-permute-start | bytes 786440 | tf_op jit(solution)/shard_map/ppermute | solution.py:49
  110.3 11.2 %collective-permute-start.36 = (bf16[4,128,256]{2,1,0:T(8,128)(2,1)S(1)}, bf16[4,128,256]{2,1,0:T(8,128)(2,1)S(1)}, u32[]{:S(2)}, u32[]{:S(2)}) collective-permute-start(bf16[4,128,256]{2,1,0:T(8,128)(2,1)S(1)} %get-tuple-element.83.refs_12_), channel_id=1, source_target_pairs={{0,2},{1,3},{2,0},{3,1},{4,6},{5,7},{6,4},{7,5},{8,10},{9,11},{10,... | collective-permute-start | bytes 786440 | tf_op jit(solution)/shard_map/ppermute | solution.py:40
  115.9 9.2 %collective-permute-start.31 = (bf16[4,128,256]{2,1,0:T(8,128)(2,1)S(1)}, bf16[4,128,256]{2,1,0:T(8,128)(2,1)S(1)}, u32[]{:S(2)}, u32[]{:S(2)}) collective-permute-start(bf16[4,128,256]{2,1,0:T(8,128)(2,1)S(1)} %collective-permute-done.29.refs_4_), channel_id=1, source_target_pairs={{0,8},{1,9},{2,10},{3,11},{4,0},{5,1},{6,2},{7,3},{8,12},{9,13},{1... | collective-permute-start | bytes 786440 | tf_op jit(solution)/shard_map/ppermute | solution.py:49
  116.7 10.4 %collective-permute-start.30 = (bf16[4,128,256]{2,1,0:T(8,128)(2,1)S(1)}, bf16[4,128,256]{2,1,0:T(8,128)(2,1)S(1)}, u32[]{:S(2)}, u32[]{:S(2)}) collective-permute-start(bf16[4,128,256]{2,1,0:T(8,128)(2,1)S(1)} %collective-permute-done.29.refs_4_), channel_id=1, source_target_pairs={{0,2},{1,3},{2,0},{3,1},{4,6},{5,7},{6,4},{7,5},{8,10},{9,11},{10,... | collective-permute-start | bytes 786440 | tf_op jit(solution)/shard_map/ppermute | solution.py:40
  121.5 9.2 %collective-permute-start.39 = (bf16[4,128,256]{2,1,0:T(8,128)(2,1)S(1)}, bf16[4,128,256]{2,1,0:T(8,128)(2,1)S(1)}, u32[]{:S(2)}, u32[]{:S(2)}) collective-permute-start(bf16[4,128,256]{2,1,0:T(8,128)(2,1)S(1)} %collective-permute-done.37.refs_13_), channel_id=1, source_target_pairs={{0,8},{1,9},{2,10},{3,11},{4,0},{5,1},{6,2},{7,3},{8,12},{9,13},{1... | collective-permute-start | bytes 786440 | tf_op jit(solution)/shard_map/ppermute | solution.py:49
  122.3 10.4 %collective-permute-start.38 = (bf16[4,128,256]{2,1,0:T(8,128)(2,1)S(1)}, bf16[4,128,256]{2,1,0:T(8,128)(2,1)S(1)}, u32[]{:S(2)}, u32[]{:S(2)}) collective-permute-start(bf16[4,128,256]{2,1,0:T(8,128)(2,1)S(1)} %collective-permute-done.37.refs_13_), channel_id=1, source_target_pairs={{0,2},{1,3},{2,0},{3,1},{4,6},{5,7},{6,4},{7,5},{8,10},{9,11},{10,... | collective-permute-start | bytes 786440 | tf_op jit(solution)/shard_map/ppermute | solution.py:40
  127.1 9.2 %collective-permute-start.33 = (bf16[4,128,256]{2,1,0:T(8,128)(2,1)S(1)}, bf16[4,128,256]{2,1,0:T(8,128)(2,1)S(1)}, u32[]{:S(2)}, u32[]{:S(2)}) collective-permute-start(bf16[4,128,256]{2,1,0:T(8,128)(2,1)S(1)} %collective-permute-done.31.refs_5_), channel_id=1, source_target_pairs={{0,8},{1,9},{2,10},{3,11},{4,0},{5,1},{6,2},{7,3},{8,12},{9,13},{1... | collective-permute-start | bytes 786440 | tf_op jit(solution)/shard_map/ppermute | solution.py:49
  128.0 10.4 %collective-permute-start.32 = (bf16[4,128,256]{2,1,0:T(8,128)(2,1)S(1)}, bf16[4,128,256]{2,1,0:T(8,128)(2,1)S(1)}, u32[]{:S(2)}, u32[]{:S(2)}) collective-permute-start(bf16[4,128,256]{2,1,0:T(8,128)(2,1)S(1)} %collective-permute-done.31.refs_5_), channel_id=1, source_target_pairs={{0,2},{1,3},{2,0},{3,1},{4,6},{5,7},{6,4},{7,5},{8,10},{9,11},{10,... | collective-permute-start | bytes 786440 | tf_op jit(solution)/shard_map/ppermute | solution.py:40
  132.7 9.2 %collective-permute-start.41 = (bf16[4,128,256]{2,1,0:T(8,128)(2,1)S(1)}, bf16[4,128,256]{2,1,0:T(8,128)(2,1)S(1)}, u32[]{:S(2)}, u32[]{:S(2)}) collective-permute-start(bf16[4,128,256]{2,1,0:T(8,128)(2,1)S(1)} %collective-permute-done.39.refs_14_), channel_id=1, source_target_pairs={{0,8},{1,9},{2,10},{3,11},{4,0},{5,1},{6,2},{7,3},{8,12},{9,13},{1... | collective-permute-start | bytes 786440 | tf_op jit(solution)/shard_map/ppermute | solution.py:49
  133.6 10.4 %collective-permute-start.40 = (bf16[4,128,256]{2,1,0:T(8,128)(2,1)S(1)}, bf16[4,128,256]{2,1,0:T(8,128)(2,1)S(1)}, u32[]{:S(2)}, u32[]{:S(2)}) collective-permute-start(bf16[4,128,256]{2,1,0:T(8,128)(2,1)S(1)} %collective-permute-done.39.refs_14_), channel_id=1, source_target_pairs={{0,2},{1,3},{2,0},{3,1},{4,6},{5,7},{6,4},{7,5},{8,10},{9,11},{10,... | collective-permute-start | bytes 786440 | tf_op jit(solution)/shard_map/ppermute | solution.py:40
  138.4 6.9 %collective-permute-start.35 = (bf16[2,128,256]{2,1,0:T(8,128)(2,1)S(1)}, bf16[2,128,256]{2,1,0:T(8,128)(2,1)S(1)}, u32[]{:S(2)}, u32[]{:S(2)}) collective-permute-start(bf16[2,128,256]{2,1,0:T(8,128)(2,1)S(1)} %slice.29), channel_id=1, source_target_pairs={{0,8},{1,9},{2,10},{3,11},{4,0},{5,1},{6,2},{7,3},{8,12},{9,13},{1... | collective-permute-start | bytes 393224 | tf_op jit(solution)/shard_map/ppermute | solution.py:49
  139.3 6.3 %collective-permute-start.34 = (bf16[2,128,256]{2,1,0:T(8,128)(2,1)S(1)}, bf16[2,128,256]{2,1,0:T(8,128)(2,1)S(1)}, u32[]{:S(2)}, u32[]{:S(2)}) collective-permute-start(bf16[2,128,256]{2,1,0:T(8,128)(2,1)S(1)} %slice.28), channel_id=1, source_target_pairs={{0,2},{1,3},{2,0},{3,1},{4,6},{5,7},{6,4},{7,5},{8,10},{9,11},{10,... | collective-permute-start | bytes 393224 | tf_op jit(solution)/shard_map/ppermute | solution.py:40
  144.0 5.0 %collective-permute-start.43 = (bf16[2,128,256]{2,1,0:T(8,128)(2,1)S(1)}, bf16[2,128,256]{2,1,0:T(8,128)(2,1)S(1)}, u32[]{:S(2)}, u32[]{:S(2)}) collective-permute-start(bf16[2,128,256]{2,1,0:T(8,128)(2,1)S(1)} %slice.31), channel_id=1, source_target_pairs={{0,8},{1,9},{2,10},{3,11},{4,0},{5,1},{6,2},{7,3},{8,12},{9,13},{1... | collective-permute-start | bytes 393224 | tf_op jit(solution)/shard_map/ppermute | solution.py:49
  144.9 5.0 %collective-permute-start.42 = (bf16[2,128,256]{2,1,0:T(8,128)(2,1)S(1)}, bf16[2,128,256]{2,1,0:T(8,128)(2,1)S(1)}, u32[]{:S(2)}, u32[]{:S(2)}) collective-permute-start(bf16[2,128,256]{2,1,0:T(8,128)(2,1)S(1)} %slice.30), channel_id=1, source_target_pairs={{0,2},{1,3},{2,0},{3,1},{4,6},{5,7},{6,4},{7,5},{8,10},{9,11},{10,... | collective-permute-start | bytes 393224 | tf_op jit(solution)/shard_map/ppermute | solution.py:40
  151.0 2.1 %collective-permute-start.44 = (bf16[4,128,256]{2,1,0:T(8,128)(2,1)S(1)}, bf16[4,128,256]{2,1,0:T(8,128)(2,1)S(1)}, u32[]{:S(2)}, u32[]{:S(2)}) collective-permute-start(bf16[4,128,256]{2,1,0:T(8,128)(2,1)S(1)} %get-tuple-element.90), channel_id=1, source_target_pairs={{0,1},{1,0},{2,3},{3,2},{4,5},{5,4},{6,7},{7,6},{8,9},{9,8},{10,11... | collective-permute-start | bytes 786440 | tf_op jit(solution)/shard_map/ppermute | solution.py:40
Sparse Core Ops, SparseCore 0:
  10.2 47.0 all-gather.1

commit v10 on v8

--- a/solution.py
+++ b/solution.py
@@ -38,6 +38,9 @@
             target = (((z + dz) % self.z) * 2 + (y ^ dy)) * 2 + (b ^ db)
             pairs.append((index, target))
         return lax.ppermute(array, "chol", pairs)
+
+    def flip(self, array, mask):
+        return lax.ppermute(array, "chol", [(i, i ^ mask) for i in range(self.chol)])
 
     def step(self, array):
         ring = [*range(0, self.z, 2), *reversed(range(1, self.z, 2))]
@@ -126,12 +129,11 @@
     return estimates
 
 
-def bias_kernel(layout, slabs, counts, rot_mine, rot_theirs, early, late, *refs):
-    fulls, (out, buffer, turned, greens) = refs[-4 - len(counts) : -4], refs[-4:]
-    pieces = refs[: -4 - len(counts)]
-    vectors, rows, electrons = rot_mine.shape
-    index = lax.axis_index("chol")
-    chip, b = index // 2, lax.rem(index, 2)
+def inverse_kernel(layout, slabs, counts, early, late, *refs):
+    fulls, (out, buffer, turned) = refs[-3 - len(counts) : -3], refs[-3:]
+    pieces = refs[: -3 - len(counts)]
+    electrons = early.shape[-1]
+    b = lax.rem(lax.axis_index("chol"), 2)
 
     theirs = [(early, at) for at in range(early.shape[0])] + [(late, 0)]
     trial = [slab for slab in slabs[0] if slab[2] == 2 * counts[0]]
@@ -149,8 +151,41 @@
         for walker in range(count):
             columns = full[walker].reshape(-1, electrons)
             matrices.append(jnp.dot(turned[...], columns, preferred_element_type=F32))
-    inverses = [inverse.astype(BF16) for inverse in newton_inverses(matrices)]
-
+    for number, inverse in enumerate(newton_inverses(matrices)):
+        out[number] = inverse.astype(BF16)
+
+
+def inverses_of(layout, streams, counts, early, late):
+    arrays, slabs = operands(streams)
+    _, rows, electrons = early.shape
+    chips = layout.chol // 2
+    total = sum(counts)
+    return pl.pallas_call(
+        functools.partial(inverse_kernel, layout, slabs, counts),
+        out_shape=[
+            jax.ShapeDtypeStruct((count, chips, 2, rows, electrons), BF16) for count in counts
+        ]
+        + [jax.ShapeDtypeStruct((total, electrons, electrons), BF16)],
+        in_specs=vmem_specs(2 + len(arrays)),
+        out_specs=vmem_specs(len(counts) + 1),
+        scratch_shapes=[
+            pltpu.VMEM((chips, 2, rows, electrons), BF16),
+            pltpu.VMEM((electrons, 2 * chips * rows), BF16),
+        ],
+        compiler_params=params(8),
+        cost_estimate=pl.CostEstimate(
+            flops=2 * total * electrons**2 * (2 * chips * rows + 6 * (ITERS - 1) * electrons),
+            bytes_accessed=4 * (total + 1) * 2 * chips * rows * electrons,
+            transcendentals=0,
+        ),
+    )(early, late, *arrays)
+
+
+def bias_kernel(counts, rot_mine, rot_theirs, inverses, *refs):
+    fulls, (out, greens) = refs[:-2], refs[-2:]
+    vectors, rows, electrons = rot_mine.shape
+    index = lax.axis_index("chol")
+    chip, b = index // 2, lax.rem(index, 2)
     walkers = [(full, at) for full, count in zip(fulls, counts) for at in range(count)]
     for number, (full, walker) in enumerate(walkers):
         both = full[walker, chip].reshape(2 * rows, electrons)
@@ -180,33 +215,23 @@
     )
 
 
-def bias_of(layout, streams, counts, early, late, rot_mine, rot_theirs):
-    arrays, slabs = operands(streams)
+def bias_of(fulls, inverses, rot_mine, rot_theirs):
     vectors, rows, electrons = rot_mine.shape
-    chips = layout.chol // 2
+    counts = [full.shape[0] for full in fulls]
     total = sum(counts)
     return pl.pallas_call(
-        functools.partial(bias_kernel, layout, slabs, counts),
-        out_shape=[
-            jax.ShapeDtypeStruct((count, chips, 2, rows, electrons), BF16) for count in counts
-        ]
-        + [jax.ShapeDtypeStruct((total, vectors), F32)],
-        in_specs=vmem_specs(4 + len(arrays)),
-        out_specs=vmem_specs(len(counts) + 1),
-        scratch_shapes=[
-            pltpu.VMEM((chips, 2, rows, electrons), BF16),
-            pltpu.VMEM((electrons, 2 * chips * rows), BF16),
-            pltpu.VMEM((2, rows // BLOCK, total, BLOCK, electrons), BF16),
-        ],
-        compiler_params=params(20),
+        functools.partial(bias_kernel, counts),
+        out_shape=jax.ShapeDtypeStruct((total, vectors), F32),
+        in_specs=vmem_specs(3 + len(fulls)),
+        out_specs=pl.BlockSpec(memory_space=pltpu.VMEM),
+        scratch_shapes=[pltpu.VMEM((2, rows // BLOCK, total, BLOCK, electrons), BF16)],
+        compiler_params=params(8),
         cost_estimate=pl.CostEstimate(
-            flops=2 * total * electrons**2 * (2 * chips * rows + 6 * (ITERS - 1) * electrons)
-            + 4 * total * rows * electrons * (electrons + vectors * BLOCK),
-            bytes_accessed=4 * (vectors + total) * rows * electrons
-            + 4 * (total + 1) * 2 * chips * rows * electrons,
+            flops=4 * total * rows * electrons * (electrons + vectors * BLOCK),
+            bytes_accessed=4 * (vectors + total) * rows * electrons,
             transcendentals=0,
         ),
-    )(rot_mine, rot_theirs, early, late, *arrays)
+    )(rot_mine, rot_theirs, inverses, *fulls)
 
 
 def potential_kernel(order, fields, mine, mine_across, theirs, theirs_across, cholesky, *refs):
@@ -529,12 +554,17 @@
     late = layout.shift(early[layout.z - 1 : layout.z], dy=1)
     early, rot_theirs = streams[0].advance((early, rot_theirs))
     streams[1].advance()
-    *fulls, total = bias_of(layout, streams, sizes, early, late, rotated, rot_theirs)
-    parts = [total] + [layout.shift(total, dz=dz) for dz in range(1, layout.z)]
-    while len(parts) > 1:
-        far = len(parts) // 2
-        parts = [parts[at] + parts[at + far] for at in range(far)]
-    parts = [parts[0]] + [layout.shift(parts[0], dy=dy, db=db) for dy, db in ((1, 0), (0, 1), (1, 1))]
+    *fulls, inverses = inverses_of(layout, streams, sizes, early, late)
+    total = bias_of(fulls, inverses, rotated, rot_theirs)
+    bits = [2] + [4 << at for at in range(layout.z.bit_length() - 1)]
+    while len(bits) > 1:
+        first, second, *rest = bits if len(bits) % 2 else (bits[0], 0, *bits[1:])
+        sums = [total + layout.flip(total, first)]
+        if second:
+            sums.append(layout.flip(total, second) + layout.flip(total, first + second))
+        total = sum(sums[1:], sums[0])
+        bits = rest
+    parts = [total] + [layout.flip(total, mask) for mask in (bits[0], 1, bits[0] + 1)]
     force_bias, kept, *sent = potential_of(order, fields, parts, cholesky)
     received = [layout.shift(part, db=1) for part in sent]
 

time: 147 us -> 142 us (0.966)
  local copies, waits for them, and re-layouts: 7.6 us -> 1.98 us
  starting transfers between devices: 49.6 us -> 52.1 us
  waiting for transfers between devices: 71.6 us -> 69.8 us
    ppermute x29 -> x23, waiting for transfers between devices: 26.5 us -> 13.1 us  [shift(): return lax.ppermute(array, 'chol', pairs)]
    ppermute x0 -> x6, starting transfers between devices: none -> 7.27 us  [flip(): lax.ppermute(array, 'chol', [(i, i ^ mask) for i in range(self.chol)])]
    ppermute x0 -> x6, waiting for transfers between devices: none -> 7.27 us  [flip(): lax.ppermute(array, 'chol', [(i, i ^ mask) for i in range(self.chol)])]
    ppermute x29 -> x23, starting transfers between devices: 24.5 us -> 17.6 us  [shift(): return lax.ppermute(array, 'chol', pairs)]
    unnamed x18, local copies, waits for them, and re-layouts: 7.5 us -> 1.89 us
    ppermute x16, waiting for transfers between devices: 43.8 us -> 48.2 us  [step(): return lax.ppermute(array, 'chol', pairs)]
    ppermute x16, starting transfers between devices: 22.4 us -> 24.6 us  [step(): return lax.ppermute(array, 'chol', pairs)]
    pallas_call x1 -> x2, Pallas kernels: 4.93 us -> 5.04 us  [the longest x1 3.32 us: inverses_of(): pl.pallas_call(functools.partial(inverse_kernel, layout, slabs, counts),...]
  transfers between devices with their start and end apart: 47 -> 47, of which waited for: 30 -> 32; matrix products, arithmetic and copies ran while one was open for 1% -> 1% of each run, Pallas kernels for 2% -> 3%
where the time goes in v10:
time: 142 us
  waiting for transfers between devices  69.8 us (49%)
  starting transfers between devices  52.1 us (37%)
  Pallas kernels  16.1 us (11%)
  local copies, waits for them, and re-layouts  1.98 us (1%)
    ppermute x16, waiting for transfers between devices, step(): return lax.ppermute(array, 'chol', pairs)  48.2 us
    ppermute x16, starting transfers between devices, step(): return lax.ppermute(array, 'chol', pairs)  24.6 us
    ppermute x23, starting transfers between devices, shift(): return lax.ppermute(array, 'chol', pairs)  17.6 us
    ppermute x23, waiting for transfers between devices, shift(): return lax.ppermute(array, 'chol', pairs)  13.1 us
    ppermute x6, starting transfers between devices, flip(): lax.ppermute(array, 'chol', [(i, i ^ mask) for i in range(self.chol)])  7.27 us
    ppermute x6, waiting for transfers between devices, flip(): lax.ppermute(array, 'chol', [(i, i ^ mask) for i in range(self.chol)])  7.27 us
    pallas_call x1, Pallas kernels, inverses_of(): pl.pallas_call(functools.partial(inverse_kernel, layout, slabs, counts),...  3.32 us
    pallas_call x1, Pallas kernels, potential_of(): pl.pallas_call(potential_kernel, out_shape=[jax.ShapeDtypeStruct((per_gro...  3.18 us
  transfers between devices with their start and end apart: 47, of which 32 were waited for; matrix products, arithmetic and copies ran while one was open for 1% of the time, Pallas kernels for 3%

profile of v10, /device:TPU:0, one launch (start us, length us, event | category | flops | bytes accessed | tf_op | source)
XLA Modules:
  0.0 141.9 jit_solution(12347095669339807214)
XLA Ops:
  0.6 1.2 copy-done.2
  1.8 0.7 copy-done.4
  2.5 2.0 %shard_map.77 = (bf16[2,128,256]{2,1,0:T(8,128)(2,1)S(1)}, bf16[2,128,256]{2,1,0:T(8,128)(2,1)S(1)}, bf16[2,128,256]{2,1,0:T(8,128)(2,1)S(1)}, bf16[2,128,256]{2,1,0:T(8,128)(2,1)S(1)}, s32[8]{0:T(128)S(1)}) custom-call(s32[16]{0:T(128)S(1)} %copy-done.4, bf16[8,128,256]{2,1,0:T(8,128)(2,1)S(1)} %copy-done.2), custom_call_target="tpu_custom_call" | custom-call | tf_op jit(solution)/shard_map/pallas_call | solution.py:475
  4.5 0.5 collective-permute-start
  5.1 2.6 %collective-permute-start.3 = (bf16[2,128,256]{2,1,0:T(8,128)(2,1)S(1)}, bf16[2,128,256]{2,1,0:T(8,128)(2,1)S(1)}, u32[]{:S(2)}, u32[]{:S(2)}) collective-permute-start(bf16[2,128,256]{2,1,0:T(8,128)(2,1)S(1)} %get-tuple-element.51), channel_id=1, source_target_pairs={{0,16},{1,17},{2,18},{3,19},{4,20},{5,21},{6,22},{7,23},{8,24},{9,... | collective-permute-start | bytes 393224 | tf_op jit(solution)/shard_map/ppermute | solution.py:504
  7.7 0.9 pad_maximum_fusion.refs_0_
  8.6 2.9 %collective-permute-start.2 = (bf16[5,128,256]{2,1,0:T(8,128)(2,1)S(1)}, bf16[5,128,256]{2,1,0:T(8,128)(2,1)S(1)}, u32[]{:S(2)}, u32[]{:S(2)}) collective-permute-start(bf16[5,128,256]{2,1,0:T(8,128)(2,1)S(1)} %pad_maximum_fusion.refs_0_), channel_id=1, source_target_pairs={{0,8},{1,9},{2,10},{3,11},{4,0},{5,1},{6,2},{7,3},{8,12},{9,13},{1... | collective-permute-start | bytes 983048 | tf_op jit(solution)/shard_map/ppermute | solution.py:49
  11.5 1.5 %collective-permute-start.1 = (bf16[5,128,256]{2,1,0:T(8,128)(2,1)S(1)}, bf16[5,128,256]{2,1,0:T(8,128)(2,1)S(1)}, u32[]{:S(2)}, u32[]{:S(2)}) collective-permute-start(bf16[5,128,256]{2,1,0:T(8,128)(2,1)S(1)} %pad_maximum_fusion.refs_0_), channel_id=1, source_target_pairs={{0,2},{1,3},{2,0},{3,1},{4,6},{5,7},{6,4},{7,5},{8,10},{9,11},{10,... | collective-permute-start | bytes 983048 | tf_op jit(solution)/shard_map/ppermute | solution.py:40
  13.0 1.2 collective-permute-done.4
  14.3 2.7 %collective-permute-start.6 = (bf16[4,128,256]{2,1,0:T(8,128)(2,1)S(1)}, bf16[4,128,256]{2,1,0:T(8,128)(2,1)S(1)}, u32[]{:S(2)}, u32[]{:S(2)}) collective-permute-start(bf16[4,128,256]{2,1,0:T(8,128)(2,1)S(1)} %pad_maximum_fusion.1.refs_9_), channel_id=1, source_target_pairs={{0,8},{1,9},{2,10},{3,11},{4,0},{5,1},{6,2},{7,3},{8,12},{9,13},{1... | collective-permute-start | bytes 786440 | tf_op jit(solution)/shard_map/ppermute | solution.py:49
  17.0 1.5 %collective-permute-start.5 = (bf16[4,128,256]{2,1,0:T(8,128)(2,1)S(1)}, bf16[4,128,256]{2,1,0:T(8,128)(2,1)S(1)}, u32[]{:S(2)}, u32[]{:S(2)}) collective-permute-start(bf16[4,128,256]{2,1,0:T(8,128)(2,1)S(1)} %pad_maximum_fusion.1.refs_9_), channel_id=1, source_target_pairs={{0,2},{1,3},{2,0},{3,1},{4,6},{5,7},{6,4},{7,5},{8,10},{9,11},{10,... | collective-permute-start | bytes 786440 | tf_op jit(solution)/shard_map/ppermute | solution.py:40
  18.6 6.0 %collective-permute-done.6.refs_10_ = bf16[4,128,256]{2,1,0:T(8,128)(2,1)S(1)} collective-permute-done((bf16[4,128,256]{2,1,0:T(8,128)(2,1)S(1)}, bf16[4,128,256]{2,1,0:T(8,128)(2,1)S(1)}, u32[]{:S(2)}, u32[]{:S(2)}) %collective-permute-start.6) | collective-permute-done | bytes 262176 | tf_op jit(solution)/shard_map/ppermute | solution.py:49
  24.6 2.2 %collective-permute-done.5.refs_13_ = bf16[4,128,256]{2,1,0:T(8,128)(2,1)S(1)} collective-permute-done((bf16[4,128,256]{2,1,0:T(8,128)(2,1)S(1)}, bf16[4,128,256]{2,1,0:T(8,128)(2,1)S(1)}, u32[]{:S(2)}, u32[]{:S(2)}) %collective-permute-start.5) | collective-permute-done | bytes 262176 | tf_op jit(solution)/shard_map/ppermute | solution.py:40
  26.8 1.6 %collective-permute-start.8 = (bf16[5,128,256]{2,1,0:T(8,128)(2,1)S(1)}, bf16[5,128,256]{2,1,0:T(8,128)(2,1)S(1)}, u32[]{:S(2)}, u32[]{:S(2)}) collective-permute-start(bf16[5,128,256]{2,1,0:T(8,128)(2,1)S(1)} %collective-permute-done.2.refs_1_), channel_id=1, source_target_pairs={{0,8},{1,9},{2,10},{3,11},{4,0},{5,1},{6,2},{7,3},{8,12},{9,13},{1... | collective-permute-start | bytes 983048 | tf_op jit(solution)/shard_map/ppermute | solution.py:49
  28.4 1.5 %collective-permute-start.7 = (bf16[5,128,256]{2,1,0:T(8,128)(2,1)S(1)}, bf16[5,128,256]{2,1,0:T(8,128)(2,1)S(1)}, u32[]{:S(2)}, u32[]{:S(2)}) collective-permute-start(bf16[5,128,256]{2,1,0:T(8,128)(2,1)S(1)} %collective-permute-done.2.refs_1_), channel_id=1, source_target_pairs={{0,2},{1,3},{2,0},{3,1},{4,6},{5,7},{6,4},{7,5},{8,10},{9,11},{10,... | collective-permute-start | bytes 983048 | tf_op jit(solution)/shard_map/ppermute | solution.py:40
  30.3 0.5 collective-permute-start.16
  30.9 6.6 %collective-permute-done.8.refs_2_ = bf16[5,128,256]{2,1,0:T(8,128)(2,1)S(1)} collective-permute-done((bf16[5,128,256]{2,1,0:T(8,128)(2,1)S(1)}, bf16[5,128,256]{2,1,0:T(8,128)(2,1)S(1)}, u32[]{:S(2)}, u32[]{:S(2)}) %collective-permute-start.8) | collective-permute-done | bytes 327712 | tf_op jit(solution)/shard_map/ppermute | solution.py:49
  37.5 1.6 %collective-permute-done.7.refs_5_ = bf16[5,128,256]{2,1,0:T(8,128)(2,1)S(1)} collective-permute-done((bf16[5,128,256]{2,1,0:T(8,128)(2,1)S(1)}, bf16[5,128,256]{2,1,0:T(8,128)(2,1)S(1)}, u32[]{:S(2)}, u32[]{:S(2)}) %collective-permute-start.7) | collective-permute-done | bytes 327712 | tf_op jit(solution)/shard_map/ppermute | solution.py:40
  39.0 0.9 collective-permute-start.10
  39.9 1.5 %collective-permute-start.9 = (bf16[5,128,256]{2,1,0:T(8,128)(2,1)S(1)}, bf16[5,128,256]{2,1,0:T(8,128)(2,1)S(1)}, u32[]{:S(2)}, u32[]{:S(2)}) collective-permute-start(bf16[5,128,256]{2,1,0:T(8,128)(2,1)S(1)} %collective-permute-done.8.refs_2_), channel_id=1, source_target_pairs={{0,2},{1,3},{2,0},{3,1},{4,6},{5,7},{6,4},{7,5},{8,10},{9,11},{10,... | collective-permute-start | bytes 983048 | tf_op jit(solution)/shard_map/ppermute | solution.py:40
  41.5 6.8 %collective-permute-done.10.refs_3_ = bf16[5,128,256]{2,1,0:T(8,128)(2,1)S(1)} collective-permute-done((bf16[5,128,256]{2,1,0:T(8,128)(2,1)S(1)}, bf16[5,128,256]{2,1,0:T(8,128)(2,1)S(1)}, u32[]{:S(2)}, u32[]{:S(2)}) %collective-permute-start.10) | collective-permute-done | bytes 327712 | tf_op jit(solution)/shard_map/ppermute | solution.py:49
  48.3 1.3 collective-permute-done.9.refs_6_
  49.7 1.2 collective-permute-start.19
  51.0 1.5 %collective-permute-start.18 = (bf16[4,128,256]{2,1,0:T(8,128)(2,1)S(1)}, bf16[4,128,256]{2,1,0:T(8,128)(2,1)S(1)}, u32[]{:S(2)}, u32[]{:S(2)}) collective-permute-start(bf16[4,128,256]{2,1,0:T(8,128)(2,1)S(1)} %collective-permute-done.17.refs_11_), channel_id=1, source_target_pairs={{0,2},{1,3},{2,0},{3,1},{4,6},{5,7},{6,4},{7,5},{8,10},{9,11},{10,... | collective-permute-start | bytes 786440 | tf_op jit(solution)/shard_map/ppermute | solution.py:40
  52.5 0.6 collective-permute-start.13
  53.1 5.3 %collective-permute-done.19.refs_12_ = bf16[4,128,256]{2,1,0:T(8,128)(2,1)S(1)} collective-permute-done((bf16[4,128,256]{2,1,0:T(8,128)(2,1)S(1)}, bf16[4,128,256]{2,1,0:T(8,128)(2,1)S(1)}, u32[]{:S(2)}, u32[]{:S(2)}) %collective-permute-start.19) | collective-permute-done | bytes 262176 | tf_op jit(solution)/shard_map/ppermute | solution.py:49
  58.4 2.1 %collective-permute-start.14 = (bf16[2,128,256]{2,1,0:T(8,128)(2,1)S(1)}, bf16[2,128,256]{2,1,0:T(8,128)(2,1)S(1)}, u32[]{:S(2)}, u32[]{:S(2)}) collective-permute-start(bf16[2,128,256]{2,1,0:T(8,128)(2,1)S(1)} %slice.52), channel_id=1, source_target_pairs={{0,8},{1,9},{2,10},{3,11},{4,0},{5,1},{6,2},{7,3},{8,12},{9,13},{1... | collective-permute-start | bytes 393224 | tf_op jit(solution)/shard_map/ppermute | solution.py:49
  60.9 1.5 %collective-permute-start.20 = (bf16[2,128,256]{2,1,0:T(8,128)(2,1)S(1)}, bf16[2,128,256]{2,1,0:T(8,128)(2,1)S(1)}, u32[]{:S(2)}, u32[]{:S(2)}) collective-permute-start(bf16[2,128,256]{2,1,0:T(8,128)(2,1)S(1)} %slice.54), channel_id=1, source_target_pairs={{0,2},{1,3},{2,0},{3,1},{4,6},{5,7},{6,4},{7,5},{8,10},{9,11},{10,... | collective-permute-start | bytes 393224 | tf_op jit(solution)/shard_map/ppermute | solution.py:40
  62.4 2.0 %collective-permute-done.14.refs_8_ = bf16[2,128,256]{2,1,0:T(8,128)(2,1)S(1)} collective-permute-done((bf16[2,128,256]{2,1,0:T(8,128)(2,1)S(1)}, bf16[2,128,256]{2,1,0:T(8,128)(2,1)S(1)}, u32[]{:S(2)}, u32[]{:S(2)}) %collective-permute-start.14) | collective-permute-done | bytes 131104 | tf_op jit(solution)/shard_map/ppermute | solution.py:49
  64.5 1.5 %collective-permute-start.15 = (bf16[1,128,256]{2,1,0:T(8,128)(2,1)S(1)}, bf16[1,128,256]{2,1,0:T(8,128)(2,1)S(1)}, u32[]{:S(2)}, u32[]{:S(2)}) collective-permute-start(bf16[1,128,256]{2,1,0:T(8,128)(2,1)S(1)} %slice.60), channel_id=1, source_target_pairs={{0,2},{1,3},{2,0},{3,1},{4,6},{5,7},{6,4},{7,5},{8,10},{9,11},{10,... | collective-permute-start | bytes 196616 | tf_op jit(solution)/shard_map/ppermute | solution.py:40
  66.3 0.8 collective-permute-done.20.refs_16_
  67.1 1.7 %collective-permute-done.15.late = bf16[1,128,256]{2,1,0:T(8,128)(2,1)S(1)} collective-permute-done((bf16[1,128,256]{2,1,0:T(8,128)(2,1)S(1)}, bf16[1,128,256]{2,1,0:T(8,128)(2,1)S(1)}, u32[]{:S(2)}, u32[]{:S(2)}) %collective-permute-start.15) | collective-permute-done | bytes 65568 | tf_op jit(solution)/shard_map/ppermute | solution.py:40
  68.7 3.3 %shard_map.78 = (bf16[2,8,2,128,256]{4,3,2,1,0:T(8,128)(2,1)S(1)}, bf16[2,8,2,128,256]{4,3,2,1,0:T(8,128)(2,1)S(1)}, bf16[4,256,256]{2,1,0:T(8,128)(2,1)S(1)}) custom-call(bf16[7,128,256]{2,1,0:T(8,128)(2,1)S(1)} %collective-permute-done.11.early, bf16[1,128,256]{2,1,0:T(8,128)(2,1)S(1)} %collective-permute-done.15.late, ...), custom_call_target="tpu_custom_call" | custom-call | flops 2684354560 | bytes 10485760 | tf_op jit(solution)/shard_map/pallas_call | solution.py:163
  72.1 1.7 %shard_map.79 = f32[4,32]{1,0:T(4,128)S(1)} custom-call(bf16[32,128,256]{2,1,0:T(8,128)(2,1)S(1)} %copy-done.1, bf16[32,128,256]{2,1,0:T(8,128)(2,1)S(1)} %collective-permute-done.12.rot_theirs, bf16[4,256,256]{2,1,0:T(8,128)(2,1)S(1)} %get-tuple-element.69.inverses, bf16[2,8,2,128,256]{4,3,2,1,0:T(8,128)(2,1)S(1)} %get-tuple-element.70.refs_0_.refs_2_.refs_1_, ...), custom_call_target="tpu_custom_call" | custom-call | flops 402653184 | bytes 4718592 | tf_op jit(solution)/shard_map/pallas_call | solution.py:222
  73.8 3.6 %collective-permute-start.24 = (f32[4,32]{1,0:T(4,128)S(1)}, f32[4,32]{1,0:T(4,128)S(1)}, u32[]{:S(2)}, u32[]{:S(2)}) collective-permute-start(f32[4,32]{1,0:T(4,128)S(1)} %shard_map.79), channel_id=1, source_target_pairs={{0,6},{1,7},{2,4},{3,5},{4,2},{5,3},{6,0},{7,1},{8,14},{9,15},{10,... | collective-permute-start | bytes 1544 | tf_op jit(solution)/shard_map/ppermute | solution.py:43
  77.4 0.6 collective-permute-start.22
  78.0 1.0 collective-permute-done.24
  79.0 2.0 %collective-permute-done.23 = f32[4,32]{1,0:T(4,128)S(1)} collective-permute-done((f32[4,32]{1,0:T(4,128)S(1)}, f32[4,32]{1,0:T(4,128)S(1)}, u32[]{:S(2)}, u32[]{:S(2)}) %collective-permute-start.23) | collective-permute-done | bytes 544 | tf_op jit(solution)/shard_map/ppermute | solution.py:43
  81.1 2.8 %collective-permute-start.26 = (f32[4,32]{1,0:T(4,128)S(1)}, f32[4,32]{1,0:T(4,128)S(1)}, u32[]{:S(2)}, u32[]{:S(2)}) collective-permute-start(f32[4,32]{1,0:T(4,128)S(1)} %add_add_fusion.mine), channel_id=1, source_target_pairs={{0,1},{1,0},{2,3},{3,2},{4,5},{5,4},{6,7},{7,6},{8,9},{9,8},{10,11... | collective-permute-start | bytes 1544 | tf_op jit(solution)/shard_map/ppermute | solution.py:43
  84.1 0.9 collective-permute-done.27.theirs_across
  85.0 3.4 %collective-permute-done.25.mine_across = f32[4,32]{1,0:T(4,128)S(1)} collective-permute-done((f32[4,32]{1,0:T(4,128)S(1)}, f32[4,32]{1,0:T(4,128)S(1)}, u32[]{:S(2)}, u32[]{:S(2)}) %collective-permute-start.25) | collective-permute-done | bytes 544 | tf_op jit(solution)/shard_map/ppermute | solution.py:43
  88.4 3.2 %shard_map.80 = (f32[8,32]{1,0:T(8,128)}, bf16[4,128,2048]{2,1,0:T(8,128)(2,1)S(1)}, bf16[4,64,2048]{2,1,0:T(8,128)(2,1)S(1)}, bf16[4,64,2048]{2,1,0:T(8,128)(2,1)S(1)}) custom-call(s32[8]{0:T(128)S(1)} %get-tuple-element.48.order, f32[8,32]{1,0:T(8,128)S(1)} %copy-done.3, f32[4,32]{1,0:T(4,128)S(1)} %add_add_fusion.mine, ...), custom_call_target="tpu_custom_call" | custom-call | tf_op jit(solution)/shard_map/pallas_call | solution.py:284
  92.1 0.8 shard_map.82
  93.7 0.6 collective-permute-done.28.refs_0_
  94.3 1.5 %collective-permute-done.29.refs_1_ = bf16[4,64,2048]{2,1,0:T(8,128)(2,1)S(1)} collective-permute-done((bf16[4,64,2048]{2,1,0:T(8,128)(2,1)S(1)}, bf16[4,64,2048]{2,1,0:T(8,128)(2,1)S(1)}, u32[]{:S(2)}, u32[]{:S(2)}) %collective-permute-start.29) | collective-permute-done | bytes 1048608 | tf_op jit(solution)/shard_map/ppermute | solution.py:40
  95.8 0.8 shard_map.81
  96.9 1.2 collective-permute-start.38
  98.1 4.1 %collective-permute-done.31.refs_4_ = bf16[4,128,256]{2,1,0:T(8,128)(2,1)S(1)} collective-permute-done((bf16[4,128,256]{2,1,0:T(8,128)(2,1)S(1)}, bf16[4,128,256]{2,1,0:T(8,128)(2,1)S(1)}, u32[]{:S(2)}, u32[]{:S(2)}) %collective-permute-start.31) | collective-permute-done | bytes 262176 | tf_op jit(solution)/shard_map/ppermute | solution.py:49
  102.4 2.0 %collective-permute-start.33 = (bf16[4,128,256]{2,1,0:T(8,128)(2,1)S(1)}, bf16[4,128,256]{2,1,0:T(8,128)(2,1)S(1)}, u32[]{:S(2)}, u32[]{:S(2)}) collective-permute-start(bf16[4,128,256]{2,1,0:T(8,128)(2,1)S(1)} %collective-permute-done.31.refs_4_), channel_id=1, source_target_pairs={{0,8},{1,9},{2,10},{3,11},{4,0},{5,1},{6,2},{7,3},{8,12},{9,13},{1... | collective-permute-start | bytes 786440 | tf_op jit(solution)/shard_map/ppermute | solution.py:49
  104.9 2.9 %collective-permute-done.39.refs_13_ = bf16[4,128,256]{2,1,0:T(8,128)(2,1)S(1)} collective-permute-done((bf16[4,128,256]{2,1,0:T(8,128)(2,1)S(1)}, bf16[4,128,256]{2,1,0:T(8,128)(2,1)S(1)}, u32[]{:S(2)}, u32[]{:S(2)}) %collective-permute-start.39) | collective-permute-done | bytes 262176 | tf_op jit(solution)/shard_map/ppermute | solution.py:49
  108.0 2.0 %collective-permute-start.41 = (bf16[4,128,256]{2,1,0:T(8,128)(2,1)S(1)}, bf16[4,128,256]{2,1,0:T(8,128)(2,1)S(1)}, u32[]{:S(2)}, u32[]{:S(2)}) collective-permute-start(bf16[4,128,256]{2,1,0:T(8,128)(2,1)S(1)} %collective-permute-done.39.refs_13_), channel_id=1, source_target_pairs={{0,8},{1,9},{2,10},{3,11},{4,0},{5,1},{6,2},{7,3},{8,12},{9,13},{1... | collective-permute-start | bytes 786440 | tf_op jit(solution)/shard_map/ppermute | solution.py:49
  110.5 2.9 %collective-permute-done.33.refs_5_ = bf16[4,128,256]{2,1,0:T(8,128)(2,1)S(1)} collective-permute-done((bf16[4,128,256]{2,1,0:T(8,128)(2,1)S(1)}, bf16[4,128,256]{2,1,0:T(8,128)(2,1)S(1)}, u32[]{:S(2)}, u32[]{:S(2)}) %collective-permute-start.33) | collective-permute-done | bytes 262176 | tf_op jit(solution)/shard_map/ppermute | solution.py:49
  113.7 2.0 %collective-permute-start.35 = (bf16[4,128,256]{2,1,0:T(8,128)(2,1)S(1)}, bf16[4,128,256]{2,1,0:T(8,128)(2,1)S(1)}, u32[]{:S(2)}, u32[]{:S(2)}) collective-permute-start(bf16[4,128,256]{2,1,0:T(8,128)(2,1)S(1)} %collective-permute-done.33.refs_5_), channel_id=1, source_target_pairs={{0,8},{1,9},{2,10},{3,11},{4,0},{5,1},{6,2},{7,3},{8,12},{9,13},{1... | collective-permute-start | bytes 786440 | tf_op jit(solution)/shard_map/ppermute | solution.py:49
  116.1 2.9 %collective-permute-done.41.refs_14_ = bf16[4,128,256]{2,1,0:T(8,128)(2,1)S(1)} collective-permute-done((bf16[4,128,256]{2,1,0:T(8,128)(2,1)S(1)}, bf16[4,128,256]{2,1,0:T(8,128)(2,1)S(1)}, u32[]{:S(2)}, u32[]{:S(2)}) %collective-permute-start.41) | collective-permute-done | bytes 262176 | tf_op jit(solution)/shard_map/ppermute | solution.py:49
  119.3 2.0 %collective-permute-start.43 = (bf16[4,128,256]{2,1,0:T(8,128)(2,1)S(1)}, bf16[4,128,256]{2,1,0:T(8,128)(2,1)S(1)}, u32[]{:S(2)}, u32[]{:S(2)}) collective-permute-start(bf16[4,128,256]{2,1,0:T(8,128)(2,1)S(1)} %collective-permute-done.41.refs_14_), channel_id=1, source_target_pairs={{0,8},{1,9},{2,10},{3,11},{4,0},{5,1},{6,2},{7,3},{8,12},{9,13},{1... | collective-permute-start | bytes 786440 | tf_op jit(solution)/shard_map/ppermute | solution.py:49
  121.7 2.9 %collective-permute-done.35.refs_6_ = bf16[4,128,256]{2,1,0:T(8,128)(2,1)S(1)} collective-permute-done((bf16[4,128,256]{2,1,0:T(8,128)(2,1)S(1)}, bf16[4,128,256]{2,1,0:T(8,128)(2,1)S(1)}, u32[]{:S(2)}, u32[]{:S(2)}) %collective-permute-start.35) | collective-permute-done | bytes 262176 | tf_op jit(solution)/shard_map/ppermute | solution.py:49
  124.9 2.0 %collective-permute-start.37 = (bf16[2,128,256]{2,1,0:T(8,128)(2,1)S(1)}, bf16[2,128,256]{2,1,0:T(8,128)(2,1)S(1)}, u32[]{:S(2)}, u32[]{:S(2)}) collective-permute-start(bf16[2,128,256]{2,1,0:T(8,128)(2,1)S(1)} %slice.57), channel_id=1, source_target_pairs={{0,8},{1,9},{2,10},{3,11},{4,0},{5,1},{6,2},{7,3},{8,12},{9,13},{1... | collective-permute-start | bytes 393224 | tf_op jit(solution)/shard_map/ppermute | solution.py:49
  127.4 2.8 %collective-permute-done.43.refs_15_ = bf16[4,128,256]{2,1,0:T(8,128)(2,1)S(1)} collective-permute-done((bf16[4,128,256]{2,1,0:T(8,128)(2,1)S(1)}, bf16[4,128,256]{2,1,0:T(8,128)(2,1)S(1)}, u32[]{:S(2)}, u32[]{:S(2)}) %collective-permute-start.43) | collective-permute-done | bytes 262176 | tf_op jit(solution)/shard_map/ppermute | solution.py:49
  130.5 2.0 %collective-permute-start.45 = (bf16[2,128,256]{2,1,0:T(8,128)(2,1)S(1)}, bf16[2,128,256]{2,1,0:T(8,128)(2,1)S(1)}, u32[]{:S(2)}, u32[]{:S(2)}) collective-permute-start(bf16[2,128,256]{2,1,0:T(8,128)(2,1)S(1)} %slice.59), channel_id=1, source_target_pairs={{0,8},{1,9},{2,10},{3,11},{4,0},{5,1},{6,2},{7,3},{8,12},{9,13},{1... | collective-permute-start | bytes 393224 | tf_op jit(solution)/shard_map/ppermute | solution.py:49
  133.1 2.5 %collective-permute-done.45.refs_20_ = bf16[2,128,256]{2,1,0:T(8,128)(2,1)S(1)} collective-permute-done((bf16[2,128,256]{2,1,0:T(8,128)(2,1)S(1)}, bf16[2,128,256]{2,1,0:T(8,128)(2,1)S(1)}, u32[]{:S(2)}, u32[]{:S(2)}) %collective-permute-start.45) | collective-permute-done | bytes 131104 | tf_op jit(solution)/shard_map/ppermute | solution.py:49
  135.6 2.0 %collective-permute-done.44.refs_19_ = bf16[2,128,256]{2,1,0:T(8,128)(2,1)S(1)} collective-permute-done((bf16[2,128,256]{2,1,0:T(8,128)(2,1)S(1)}, bf16[2,128,256]{2,1,0:T(8,128)(2,1)S(1)}, u32[]{:S(2)}, u32[]{:S(2)}) %collective-permute-start.44) | collective-permute-done | bytes 131104 | tf_op jit(solution)/shard_map/ppermute | solution.py:40
  137.5 1.0 shard_map.83
  138.6 1.9 %shard_map.84._ = bf16[8,128,256]{2,1,0:T(8,128)(2,1)} custom-call(s32[8]{0:T(128)S(1)} %get-tuple-element.48.order, bf16[4,128,2048]{2,1,0:T(8,128)(2,1)S(1)} %get-tuple-element.75.refs_0_.potential, f32[4,128,256]{2,1,0:T(8,128)S(1)} %get-tuple-element.91.base, bf16[4,8,2,128,256]{4,3,2,1,0:T(8,128)(2,1)S(1)} %get-tuple-element.92.full), custom_call_target="tpu_custom_call" | custom-call | flops 536870912 | bytes 6291456 | tf_op jit(solution)/shard_map/pallas_call | solution.py:389
  140.6 1.3 shard_map.85
  (72 shorter events, 7.9 us)
Async XLA Ops:
  0.6 29.3 %copy-start.1 = (bf16[32,128,256]{2,1,0:T(8,128)(2,1)S(1)}, bf16[32,128,256]{2,1,0:T(8,128)(2,1)}, u32[]{:S(2)}) copy-start(bf16[32,128,256]{2,1,0:T(8,128)(2,1)} %rot_mine.1) | copy-start | bytes 6291460
  0.6 1.2 copy-start.2
  1.8 0.7 copy-start.4
  2.5 27.4 %copy-start.5 = (bf16[128,256]{1,0:T(8,128)(2,1)S(1)}, bf16[128,256]{1,0:T(8,128)(2,1)}, u32[]{:S(2)}) copy-start(bf16[128,256]{1,0:T(8,128)(2,1)} %param.7) | copy-start | bytes 196612
  4.5 3.2 %collective-permute-start = (bf16[2,128,256]{2,1,0:T(8,128)(2,1)S(1)}, bf16[2,128,256]{2,1,0:T(8,128)(2,1)S(1)}, u32[]{:S(2)}, u32[]{:S(2)}) collective-permute-start(bf16[2,128,256]{2,1,0:T(8,128)(2,1)S(1)} %get-tuple-element.50), channel_id=1, source_target_pairs={{0,1},{1,0},{2,3},{3,2},{4,5},{5,4},{6,7},{7,6},{8,9},{9,8},{10,11... | collective-permute-start | bytes 393224 | tf_op jit(solution)/shard_map/ppermute | solution.py:40
  5.1 8.0 %collective-permute-start.3 = (bf16[2,128,256]{2,1,0:T(8,128)(2,1)S(1)}, bf16[2,128,256]{2,1,0:T(8,128)(2,1)S(1)}, u32[]{:S(2)}, u32[]{:S(2)}) collective-permute-start(bf16[2,128,256]{2,1,0:T(8,128)(2,1)S(1)} %get-tuple-element.51), channel_id=1, source_target_pairs={{0,16},{1,17},{2,18},{3,19},{4,20},{5,21},{6,22},{7,23},{8,24},{9,... | collective-permute-start | bytes 393224 | tf_op jit(solution)/shard_map/ppermute | solution.py:504
  7.6 6.6 %collective-permute-start.4 = (bf16[2,128,256]{2,1,0:T(8,128)(2,1)S(1)}, bf16[2,128,256]{2,1,0:T(8,128)(2,1)S(1)}, u32[]{:S(2)}, u32[]{:S(2)}) collective-permute-start(bf16[2,128,256]{2,1,0:T(8,128)(2,1)S(1)} %get-tuple-element.52), channel_id=1, source_target_pairs={{0,17},{1,16},{2,19},{3,18},{4,21},{5,20},{6,23},{7,22},{8,25},{9,... | collective-permute-start | bytes 393224 | tf_op jit(solution)/shard_map/ppermute | solution.py:505
  8.6 18.2 %collective-permute-start.2 = (bf16[5,128,256]{2,1,0:T(8,128)(2,1)S(1)}, bf16[5,128,256]{2,1,0:T(8,128)(2,1)S(1)}, u32[]{:S(2)}, u32[]{:S(2)}) collective-permute-start(bf16[5,128,256]{2,1,0:T(8,128)(2,1)S(1)} %pad_maximum_fusion.refs_0_), channel_id=1, source_target_pairs={{0,8},{1,9},{2,10},{3,11},{4,0},{5,1},{6,2},{7,3},{8,12},{9,13},{1... | collective-permute-start | bytes 983048 | tf_op jit(solution)/shard_map/ppermute | solution.py:49
  11.5 15.3 %collective-permute-start.1 = (bf16[5,128,256]{2,1,0:T(8,128)(2,1)S(1)}, bf16[5,128,256]{2,1,0:T(8,128)(2,1)S(1)}, u32[]{:S(2)}, u32[]{:S(2)}) collective-permute-start(bf16[5,128,256]{2,1,0:T(8,128)(2,1)S(1)} %pad_maximum_fusion.refs_0_), channel_id=1, source_target_pairs={{0,2},{1,3},{2,0},{3,1},{4,6},{5,7},{6,4},{7,5},{8,10},{9,11},{10,... | collective-permute-start | bytes 983048 | tf_op jit(solution)/shard_map/ppermute | solution.py:40
  14.3 10.3 %collective-permute-start.6 = (bf16[4,128,256]{2,1,0:T(8,128)(2,1)S(1)}, bf16[4,128,256]{2,1,0:T(8,128)(2,1)S(1)}, u32[]{:S(2)}, u32[]{:S(2)}) collective-permute-start(bf16[4,128,256]{2,1,0:T(8,128)(2,1)S(1)} %pad_maximum_fusion.1.refs_9_), channel_id=1, source_target_pairs={{0,8},{1,9},{2,10},{3,11},{4,0},{5,1},{6,2},{7,3},{8,12},{9,13},{1... | collective-permute-start | bytes 786440 | tf_op jit(solution)/shard_map/ppermute | solution.py:49
  17.0 9.8 %collective-permute-start.5 = (bf16[4,128,256]{2,1,0:T(8,128)(2,1)S(1)}, bf16[4,128,256]{2,1,0:T(8,128)(2,1)S(1)}, u32[]{:S(2)}, u32[]{:S(2)}) collective-permute-start(bf16[4,128,256]{2,1,0:T(8,128)(2,1)S(1)} %pad_maximum_fusion.1.refs_9_), channel_id=1, source_target_pairs={{0,2},{1,3},{2,0},{3,1},{4,6},{5,7},{6,4},{7,5},{8,10},{9,11},{10,... | collective-permute-start | bytes 786440 | tf_op jit(solution)/shard_map/ppermute | solution.py:40
  26.8 10.6 %collective-permute-start.8 = (bf16[5,128,256]{2,1,0:T(8,128)(2,1)S(1)}, bf16[5,128,256]{2,1,0:T(8,128)(2,1)S(1)}, u32[]{:S(2)}, u32[]{:S(2)}) collective-permute-start(bf16[5,128,256]{2,1,0:T(8,128)(2,1)S(1)} %collective-permute-done.2.refs_1_), channel_id=1, source_target_pairs={{0,8},{1,9},{2,10},{3,11},{4,0},{5,1},{6,2},{7,3},{8,12},{9,13},{1... | collective-permute-start | bytes 983048 | tf_op jit(solution)/shard_map/ppermute | solution.py:49
  28.4 10.6 %collective-permute-start.7 = (bf16[5,128,256]{2,1,0:T(8,128)(2,1)S(1)}, bf16[5,128,256]{2,1,0:T(8,128)(2,1)S(1)}, u32[]{:S(2)}, u32[]{:S(2)}) collective-permute-start(bf16[5,128,256]{2,1,0:T(8,128)(2,1)S(1)} %collective-permute-done.2.refs_1_), channel_id=1, source_target_pairs={{0,2},{1,3},{2,0},{3,1},{4,6},{5,7},{6,4},{7,5},{8,10},{9,11},{10,... | collective-permute-start | bytes 983048 | tf_op jit(solution)/shard_map/ppermute | solution.py:40
  29.9 36.1 %collective-permute-start.12 = (bf16[32,128,256]{2,1,0:T(8,128)(2,1)S(1)}, bf16[32,128,256]{2,1,0:T(8,128)(2,1)S(1)}, u32[]{:S(2)}, u32[]{:S(2)}) collective-permute-start(bf16[32,128,256]{2,1,0:T(8,128)(2,1)S(1)} %copy-done.1), channel_id=1, source_target_pairs={{0,1},{1,0},{2,3},{3,2},{4,5},{5,4},{6,7},{7,6},{8,9},{9,8},{10,11... | collective-permute-start | bytes 6291464 | tf_op jit(solution)/shard_map/ppermute | solution.py:40
  29.9 19.8 %collective-permute-start.17 = (bf16[4,128,256]{2,1,0:T(8,128)(2,1)S(1)}, bf16[4,128,256]{2,1,0:T(8,128)(2,1)S(1)}, u32[]{:S(2)}, u32[]{:S(2)}) collective-permute-start(bf16[4,128,256]{2,1,0:T(8,128)(2,1)S(1)} %collective-permute-done.6.refs_10_), channel_id=1, source_target_pairs={{0,8},{1,9},{2,10},{3,11},{4,0},{5,1},{6,2},{7,3},{8,12},{9,13},{1... | collective-permute-start | bytes 786440 | tf_op jit(solution)/shard_map/ppermute | solution.py:49
  30.3 19.4 %collective-permute-start.16 = (bf16[4,128,256]{2,1,0:T(8,128)(2,1)S(1)}, bf16[4,128,256]{2,1,0:T(8,128)(2,1)S(1)}, u32[]{:S(2)}, u32[]{:S(2)}) collective-permute-start(bf16[4,128,256]{2,1,0:T(8,128)(2,1)S(1)} %collective-permute-done.6.refs_10_), channel_id=1, source_target_pairs={{0,2},{1,3},{2,0},{3,1},{4,6},{5,7},{6,4},{7,5},{8,10},{9,11},{10,... | collective-permute-start | bytes 786440 | tf_op jit(solution)/shard_map/ppermute | solution.py:40
  39.0 9.3 %collective-permute-start.10 = (bf16[5,128,256]{2,1,0:T(8,128)(2,1)S(1)}, bf16[5,128,256]{2,1,0:T(8,128)(2,1)S(1)}, u32[]{:S(2)}, u32[]{:S(2)}) collective-permute-start(bf16[5,128,256]{2,1,0:T(8,128)(2,1)S(1)} %collective-permute-done.8.refs_2_), channel_id=1, source_target_pairs={{0,8},{1,9},{2,10},{3,11},{4,0},{5,1},{6,2},{7,3},{8,12},{9,13},{1... | collective-permute-start | bytes 983048 | tf_op jit(solution)/shard_map/ppermute | solution.py:49
  39.9 9.7 %collective-permute-start.9 = (bf16[5,128,256]{2,1,0:T(8,128)(2,1)S(1)}, bf16[5,128,256]{2,1,0:T(8,128)(2,1)S(1)}, u32[]{:S(2)}, u32[]{:S(2)}) collective-permute-start(bf16[5,128,256]{2,1,0:T(8,128)(2,1)S(1)} %collective-permute-done.8.refs_2_), channel_id=1, source_target_pairs={{0,2},{1,3},{2,0},{3,1},{4,6},{5,7},{6,4},{7,5},{8,10},{9,11},{10,... | collective-permute-start | bytes 983048 | tf_op jit(solution)/shard_map/ppermute | solution.py:40
  49.6 11.3 %collective-permute-start.11 = (bf16[7,128,256]{2,1,0:T(8,128)(2,1)S(1)}, bf16[7,128,256]{2,1,0:T(8,128)(2,1)S(1)}, u32[]{:S(2)}, u32[]{:S(2)}) collective-permute-start(bf16[7,128,256]{2,1,0:T(8,128)(2,1)S(1)} %slice_dynamic-update-slice_fusion), channel_id=1, source_target_pairs={{0,1},{1,0},{2,3},{3,2},{4,5},{5,4},{6,7},{7,6},{8,9},{9,8},{10,11... | collective-permute-start | bytes 1376264 | tf_op jit(solution)/shard_map/ppermute | solution.py:40
  49.7 8.7 %collective-permute-start.19 = (bf16[4,128,256]{2,1,0:T(8,128)(2,1)S(1)}, bf16[4,128,256]{2,1,0:T(8,128)(2,1)S(1)}, u32[]{:S(2)}, u32[]{:S(2)}) collective-permute-start(bf16[4,128,256]{2,1,0:T(8,128)(2,1)S(1)} %collective-permute-done.17.refs_11_), channel_id=1, source_target_pairs={{0,8},{1,9},{2,10},{3,11},{4,0},{5,1},{6,2},{7,3},{8,12},{9,13},{1... | collective-permute-start | bytes 786440 | tf_op jit(solution)/shard_map/ppermute | solution.py:49
  51.0 9.6 %collective-permute-start.18 = (bf16[4,128,256]{2,1,0:T(8,128)(2,1)S(1)}, bf16[4,128,256]{2,1,0:T(8,128)(2,1)S(1)}, u32[]{:S(2)}, u32[]{:S(2)}) collective-permute-start(bf16[4,128,256]{2,1,0:T(8,128)(2,1)S(1)} %collective-permute-done.17.refs_11_), channel_id=1, source_target_pairs={{0,2},{1,3},{2,0},{3,1},{4,6},{5,7},{6,4},{7,5},{8,10},{9,11},{10,... | collective-permute-start | bytes 786440 | tf_op jit(solution)/shard_map/ppermute | solution.py:40
  52.5 13.5 %collective-permute-start.13 = (bf16[3,128,256]{2,1,0:T(8,128)(2,1)S(1)}, bf16[3,128,256]{2,1,0:T(8,128)(2,1)S(1)}, u32[]{:S(2)}, u32[]{:S(2)}) collective-permute-start(bf16[3,128,256]{2,1,0:T(8,128)(2,1)S(1)} %slice.51), channel_id=1, source_target_pairs={{0,2},{1,3},{2,0},{3,1},{4,6},{5,7},{6,4},{7,5},{8,10},{9,11},{10,... | collective-permute-start | bytes 589832 | tf_op jit(solution)/shard_map/ppermute | solution.py:40
  58.4 6.0 %collective-permute-start.14 = (bf16[2,128,256]{2,1,0:T(8,128)(2,1)S(1)}, bf16[2,128,256]{2,1,0:T(8,128)(2,1)S(1)}, u32[]{:S(2)}, u32[]{:S(2)}) collective-permute-start(bf16[2,128,256]{2,1,0:T(8,128)(2,1)S(1)} %slice.52), channel_id=1, source_target_pairs={{0,8},{1,9},{2,10},{3,11},{4,0},{5,1},{6,2},{7,3},{8,12},{9,13},{1... | collective-permute-start | bytes 393224 | tf_op jit(solution)/shard_map/ppermute | solution.py:49
  60.6 5.7 %collective-permute-start.21 = (bf16[2,128,256]{2,1,0:T(8,128)(2,1)S(1)}, bf16[2,128,256]{2,1,0:T(8,128)(2,1)S(1)}, u32[]{:S(2)}, u32[]{:S(2)}) collective-permute-start(bf16[2,128,256]{2,1,0:T(8,128)(2,1)S(1)} %slice.55), channel_id=1, source_target_pairs={{0,8},{1,9},{2,10},{3,11},{4,0},{5,1},{6,2},{7,3},{8,12},{9,13},{1... | collective-permute-start | bytes 393224 | tf_op jit(solution)/shard_map/ppermute | solution.py:49
  60.9 6.2 %collective-permute-start.20 = (bf16[2,128,256]{2,1,0:T(8,128)(2,1)S(1)}, bf16[2,128,256]{2,1,0:T(8,128)(2,1)S(1)}, u32[]{:S(2)}, u32[]{:S(2)}) collective-permute-start(bf16[2,128,256]{2,1,0:T(8,128)(2,1)S(1)} %slice.54), channel_id=1, source_target_pairs={{0,2},{1,3},{2,0},{3,1},{4,6},{5,7},{6,4},{7,5},{8,10},{9,11},{10,... | collective-permute-start | bytes 393224 | tf_op jit(solution)/shard_map/ppermute | solution.py:40
  64.5 4.3 %collective-permute-start.15 = (bf16[1,128,256]{2,1,0:T(8,128)(2,1)S(1)}, bf16[1,128,256]{2,1,0:T(8,128)(2,1)S(1)}, u32[]{:S(2)}, u32[]{:S(2)}) collective-permute-start(bf16[1,128,256]{2,1,0:T(8,128)(2,1)S(1)} %slice.60), channel_id=1, source_target_pairs={{0,2},{1,3},{2,0},{3,1},{4,6},{5,7},{6,4},{7,5},{8,10},{9,11},{10,... | collective-permute-start | bytes 196616 | tf_op jit(solution)/shard_map/ppermute | solution.py:40
  68.7 19.6 %copy-start = (bf16[32,128,2048]{2,1,0:T(8,128)(2,1)S(1)}, bf16[32,128,2048]{2,1,0:T(8,128)(2,1)}, u32[]{:S(2)}) copy-start(bf16[32,128,2048]{2,1,0:T(8,128)(2,1)} %cholesky.1) | copy-start | bytes 50331652
  72.1 16.3 %copy-start.3 = (f32[8,32]{1,0:T(8,128)S(1)}, f32[8,32]{1,0:T(8,128)}, u32[]{:S(2)}) copy-start(f32[8,32]{1,0:T(8,128)} %fields.1) | copy-start | bytes 3076
  73.8 5.2 %collective-permute-start.24 = (f32[4,32]{1,0:T(4,128)S(1)}, f32[4,32]{1,0:T(4,128)S(1)}, u32[]{:S(2)}, u32[]{:S(2)}) collective-permute-start(f32[4,32]{1,0:T(4,128)S(1)} %shard_map.79), channel_id=1, source_target_pairs={{0,6},{1,7},{2,4},{3,5},{4,2},{5,3},{6,0},{7,1},{8,14},{9,15},{10,... | collective-permute-start | bytes 1544 | tf_op jit(solution)/shard_map/ppermute | solution.py:43
  77.4 3.6 %collective-permute-start.23 = (f32[4,32]{1,0:T(4,128)S(1)}, f32[4,32]{1,0:T(4,128)S(1)}, u32[]{:S(2)}, u32[]{:S(2)}) collective-permute-start(f32[4,32]{1,0:T(4,128)S(1)} %shard_map.79), channel_id=1, source_target_pairs={{0,4},{1,5},{2,6},{3,7},{4,0},{5,1},{6,2},{7,3},{8,12},{9,13},{10,... | collective-permute-start | bytes 1544 | tf_op jit(solution)/shard_map/ppermute | solution.py:43
  77.4 3.6 %collective-permute-start.22 = (f32[4,32]{1,0:T(4,128)S(1)}, f32[4,32]{1,0:T(4,128)S(1)}, u32[]{:S(2)}, u32[]{:S(2)}) collective-permute-start(f32[4,32]{1,0:T(4,128)S(1)} %shard_map.79), channel_id=1, source_target_pairs={{0,2},{1,3},{2,0},{3,1},{4,6},{5,7},{6,4},{7,5},{8,10},{9,11},{10,... | collective-permute-start | bytes 1544 | tf_op jit(solution)/shard_map/ppermute | solution.py:43
  81.0 4.0 %collective-permute-start.27 = (f32[4,32]{1,0:T(4,128)S(1)}, f32[4,32]{1,0:T(4,128)S(1)}, u32[]{:S(2)}, u32[]{:S(2)}) collective-permute-start(f32[4,32]{1,0:T(4,128)S(1)} %add_add_fusion.mine), channel_id=1, source_target_pairs={{0,9},{1,8},{2,11},{3,10},{4,13},{5,12},{6,15},{7,14},{8,1},{9,0},... | collective-permute-start | bytes 1544 | tf_op jit(solution)/shard_map/ppermute | solution.py:43
  81.1 3.9 %collective-permute-start.26 = (f32[4,32]{1,0:T(4,128)S(1)}, f32[4,32]{1,0:T(4,128)S(1)}, u32[]{:S(2)}, u32[]{:S(2)}) collective-permute-start(f32[4,32]{1,0:T(4,128)S(1)} %add_add_fusion.mine), channel_id=1, source_target_pairs={{0,1},{1,0},{2,3},{3,2},{4,5},{5,4},{6,7},{7,6},{8,9},{9,8},{10,11... | collective-permute-start | bytes 1544 | tf_op jit(solution)/shard_map/ppermute | solution.py:43
  83.9 4.5 %collective-permute-start.25 = (f32[4,32]{1,0:T(4,128)S(1)}, f32[4,32]{1,0:T(4,128)S(1)}, u32[]{:S(2)}, u32[]{:S(2)}) collective-permute-start(f32[4,32]{1,0:T(4,128)S(1)} %add_add_fusion.mine), channel_id=1, source_target_pairs={{0,8},{1,9},{2,10},{3,11},{4,12},{5,13},{6,14},{7,15},{8,0},{9,1},... | collective-permute-start | bytes 1544 | tf_op jit(solution)/shard_map/ppermute | solution.py:43
  91.6 2.7 %collective-permute-start.28 = (bf16[4,64,2048]{2,1,0:T(8,128)(2,1)S(1)}, bf16[4,64,2048]{2,1,0:T(8,128)(2,1)S(1)}, u32[]{:S(2)}, u32[]{:S(2)}) collective-permute-start(bf16[4,64,2048]{2,1,0:T(8,128)(2,1)S(1)} %get-tuple-element.72), channel_id=1, source_target_pairs={{0,1},{1,0},{2,3},{3,2},{4,5},{5,4},{6,7},{7,6},{8,9},{9,8},{10,11... | collective-permute-start | bytes 3145736 | tf_op jit(solution)/shard_map/ppermute | solution.py:40
  91.6 4.1 %collective-permute-start.29 = (bf16[4,64,2048]{2,1,0:T(8,128)(2,1)S(1)}, bf16[4,64,2048]{2,1,0:T(8,128)(2,1)S(1)}, u32[]{:S(2)}, u32[]{:S(2)}) collective-permute-start(bf16[4,64,2048]{2,1,0:T(8,128)(2,1)S(1)} %get-tuple-element.73), channel_id=1, source_target_pairs={{0,1},{1,0},{2,3},{3,2},{4,5},{5,4},{6,7},{7,6},{8,9},{9,8},{10,11... | collective-permute-start | bytes 3145736 | tf_op jit(solution)/shard_map/ppermute | solution.py:40
  93.0 9.2 %collective-permute-start.31 = (bf16[4,128,256]{2,1,0:T(8,128)(2,1)S(1)}, bf16[4,128,256]{2,1,0:T(8,128)(2,1)S(1)}, u32[]{:S(2)}, u32[]{:S(2)}) collective-permute-start(bf16[4,128,256]{2,1,0:T(8,128)(2,1)S(1)} %get-tuple-element.76.refs_3_), channel_id=1, source_target_pairs={{0,8},{1,9},{2,10},{3,11},{4,0},{5,1},{6,2},{7,3},{8,12},{9,13},{1... | collective-permute-start | bytes 786440 | tf_op jit(solution)/shard_map/ppermute | solution.py:49
  93.2 9.2 %collective-permute-start.30 = (bf16[4,128,256]{2,1,0:T(8,128)(2,1)S(1)}, bf16[4,128,256]{2,1,0:T(8,128)(2,1)S(1)}, u32[]{:S(2)}, u32[]{:S(2)}) collective-permute-start(bf16[4,128,256]{2,1,0:T(8,128)(2,1)S(1)} %get-tuple-element.76.refs_3_), channel_id=1, source_target_pairs={{0,2},{1,3},{2,0},{3,1},{4,6},{5,7},{6,4},{7,5},{8,10},{9,11},{10,... | collective-permute-start | bytes 786440 | tf_op jit(solution)/shard_map/ppermute | solution.py:40
  96.6 11.2 %collective-permute-start.39 = (bf16[4,128,256]{2,1,0:T(8,128)(2,1)S(1)}, bf16[4,128,256]{2,1,0:T(8,128)(2,1)S(1)}, u32[]{:S(2)}, u32[]{:S(2)}) collective-permute-start(bf16[4,128,256]{2,1,0:T(8,128)(2,1)S(1)} %get-tuple-element.83.refs_12_), channel_id=1, source_target_pairs={{0,8},{1,9},{2,10},{3,11},{4,0},{5,1},{6,2},{7,3},{8,12},{9,13},{1... | collective-permute-start | bytes 786440 | tf_op jit(solution)/shard_map/ppermute | solution.py:49
  96.9 11.2 %collective-permute-start.38 = (bf16[4,128,256]{2,1,0:T(8,128)(2,1)S(1)}, bf16[4,128,256]{2,1,0:T(8,128)(2,1)S(1)}, u32[]{:S(2)}, u32[]{:S(2)}) collective-permute-start(bf16[4,128,256]{2,1,0:T(8,128)(2,1)S(1)} %get-tuple-element.83.refs_12_), channel_id=1, source_target_pairs={{0,2},{1,3},{2,0},{3,1},{4,6},{5,7},{6,4},{7,5},{8,10},{9,11},{10,... | collective-permute-start | bytes 786440 | tf_op jit(solution)/shard_map/ppermute | solution.py:40
  102.4 11.0 %collective-permute-start.33 = (bf16[4,128,256]{2,1,0:T(8,128)(2,1)S(1)}, bf16[4,128,256]{2,1,0:T(8,128)(2,1)S(1)}, u32[]{:S(2)}, u32[]{:S(2)}) collective-permute-start(bf16[4,128,256]{2,1,0:T(8,128)(2,1)S(1)} %collective-permute-done.31.refs_4_), channel_id=1, source_target_pairs={{0,8},{1,9},{2,10},{3,11},{4,0},{5,1},{6,2},{7,3},{8,12},{9,13},{1... | collective-permute-start | bytes 786440 | tf_op jit(solution)/shard_map/ppermute | solution.py:49
  104.4 9.3 %collective-permute-start.32 = (bf16[4,128,256]{2,1,0:T(8,128)(2,1)S(1)}, bf16[4,128,256]{2,1,0:T(8,128)(2,1)S(1)}, u32[]{:S(2)}, u32[]{:S(2)}) collective-permute-start(bf16[4,128,256]{2,1,0:T(8,128)(2,1)S(1)} %collective-permute-done.31.refs_4_), channel_id=1, source_target_pairs={{0,2},{1,3},{2,0},{3,1},{4,6},{5,7},{6,4},{7,5},{8,10},{9,11},{10,... | collective-permute-start | bytes 786440 | tf_op jit(solution)/shard_map/ppermute | solution.py:40
  108.0 11.0 %collective-permute-start.41 = (bf16[4,128,256]{2,1,0:T(8,128)(2,1)S(1)}, bf16[4,128,256]{2,1,0:T(8,128)(2,1)S(1)}, u32[]{:S(2)}, u32[]{:S(2)}) collective-permute-start(bf16[4,128,256]{2,1,0:T(8,128)(2,1)S(1)} %collective-permute-done.39.refs_13_), channel_id=1, source_target_pairs={{0,8},{1,9},{2,10},{3,11},{4,0},{5,1},{6,2},{7,3},{8,12},{9,13},{1... | collective-permute-start | bytes 786440 | tf_op jit(solution)/shard_map/ppermute | solution.py:49
  110.0 9.3 %collective-permute-start.40 = (bf16[4,128,256]{2,1,0:T(8,128)(2,1)S(1)}, bf16[4,128,256]{2,1,0:T(8,128)(2,1)S(1)}, u32[]{:S(2)}, u32[]{:S(2)}) collective-permute-start(bf16[4,128,256]{2,1,0:T(8,128)(2,1)S(1)} %collective-permute-done.39.refs_13_), channel_id=1, source_target_pairs={{0,2},{1,3},{2,0},{3,1},{4,6},{5,7},{6,4},{7,5},{8,10},{9,11},{10,... | collective-permute-start | bytes 786440 | tf_op jit(solution)/shard_map/ppermute | solution.py:40
  113.7 11.0 %collective-permute-start.35 = (bf16[4,128,256]{2,1,0:T(8,128)(2,1)S(1)}, bf16[4,128,256]{2,1,0:T(8,128)(2,1)S(1)}, u32[]{:S(2)}, u32[]{:S(2)}) collective-permute-start(bf16[4,128,256]{2,1,0:T(8,128)(2,1)S(1)} %collective-permute-done.33.refs_5_), channel_id=1, source_target_pairs={{0,8},{1,9},{2,10},{3,11},{4,0},{5,1},{6,2},{7,3},{8,12},{9,13},{1... | collective-permute-start | bytes 786440 | tf_op jit(solution)/shard_map/ppermute | solution.py:49
  115.6 9.3 %collective-permute-start.34 = (bf16[4,128,256]{2,1,0:T(8,128)(2,1)S(1)}, bf16[4,128,256]{2,1,0:T(8,128)(2,1)S(1)}, u32[]{:S(2)}, u32[]{:S(2)}) collective-permute-start(bf16[4,128,256]{2,1,0:T(8,128)(2,1)S(1)} %collective-permute-done.33.refs_5_), channel_id=1, source_target_pairs={{0,2},{1,3},{2,0},{3,1},{4,6},{5,7},{6,4},{7,5},{8,10},{9,11},{10,... | collective-permute-start | bytes 786440 | tf_op jit(solution)/shard_map/ppermute | solution.py:40
  119.3 11.0 %collective-permute-start.43 = (bf16[4,128,256]{2,1,0:T(8,128)(2,1)S(1)}, bf16[4,128,256]{2,1,0:T(8,128)(2,1)S(1)}, u32[]{:S(2)}, u32[]{:S(2)}) collective-permute-start(bf16[4,128,256]{2,1,0:T(8,128)(2,1)S(1)} %collective-permute-done.41.refs_14_), channel_id=1, source_target_pairs={{0,8},{1,9},{2,10},{3,11},{4,0},{5,1},{6,2},{7,3},{8,12},{9,13},{1... | collective-permute-start | bytes 786440 | tf_op jit(solution)/shard_map/ppermute | solution.py:49
  121.2 9.3 %collective-permute-start.42 = (bf16[4,128,256]{2,1,0:T(8,128)(2,1)S(1)}, bf16[4,128,256]{2,1,0:T(8,128)(2,1)S(1)}, u32[]{:S(2)}, u32[]{:S(2)}) collective-permute-start(bf16[4,128,256]{2,1,0:T(8,128)(2,1)S(1)} %collective-permute-done.41.refs_14_), channel_id=1, source_target_pairs={{0,2},{1,3},{2,0},{3,1},{4,6},{5,7},{6,4},{7,5},{8,10},{9,11},{10,... | collective-permute-start | bytes 786440 | tf_op jit(solution)/shard_map/ppermute | solution.py:40
  124.9 8.1 %collective-permute-start.37 = (bf16[2,128,256]{2,1,0:T(8,128)(2,1)S(1)}, bf16[2,128,256]{2,1,0:T(8,128)(2,1)S(1)}, u32[]{:S(2)}, u32[]{:S(2)}) collective-permute-start(bf16[2,128,256]{2,1,0:T(8,128)(2,1)S(1)} %slice.57), channel_id=1, source_target_pairs={{0,8},{1,9},{2,10},{3,11},{4,0},{5,1},{6,2},{7,3},{8,12},{9,13},{1... | collective-permute-start | bytes 393224 | tf_op jit(solution)/shard_map/ppermute | solution.py:49
  126.9 6.1 %collective-permute-start.36 = (bf16[2,128,256]{2,1,0:T(8,128)(2,1)S(1)}, bf16[2,128,256]{2,1,0:T(8,128)(2,1)S(1)}, u32[]{:S(2)}, u32[]{:S(2)}) collective-permute-start(bf16[2,128,256]{2,1,0:T(8,128)(2,1)S(1)} %slice.56), channel_id=1, source_target_pairs={{0,2},{1,3},{2,0},{3,1},{4,6},{5,7},{6,4},{7,5},{8,10},{9,11},{10,... | collective-permute-start | bytes 393224 | tf_op jit(solution)/shard_map/ppermute | solution.py:40
  130.5 5.0 %collective-permute-start.45 = (bf16[2,128,256]{2,1,0:T(8,128)(2,1)S(1)}, bf16[2,128,256]{2,1,0:T(8,128)(2,1)S(1)}, u32[]{:S(2)}, u32[]{:S(2)}) collective-permute-start(bf16[2,128,256]{2,1,0:T(8,128)(2,1)S(1)} %slice.59), channel_id=1, source_target_pairs={{0,8},{1,9},{2,10},{3,11},{4,0},{5,1},{6,2},{7,3},{8,12},{9,13},{1... | collective-permute-start | bytes 393224 | tf_op jit(solution)/shard_map/ppermute | solution.py:49
  132.6 5.0 %collective-permute-start.44 = (bf16[2,128,256]{2,1,0:T(8,128)(2,1)S(1)}, bf16[2,128,256]{2,1,0:T(8,128)(2,1)S(1)}, u32[]{:S(2)}, u32[]{:S(2)}) collective-permute-start(bf16[2,128,256]{2,1,0:T(8,128)(2,1)S(1)} %slice.58), channel_id=1, source_target_pairs={{0,2},{1,3},{2,0},{3,1},{4,6},{5,7},{6,4},{7,5},{8,10},{9,11},{10,... | collective-permute-start | bytes 393224 | tf_op jit(solution)/shard_map/ppermute | solution.py:40
  138.5 2.0 %collective-permute-start.46 = (bf16[4,128,256]{2,1,0:T(8,128)(2,1)S(1)}, bf16[4,128,256]{2,1,0:T(8,128)(2,1)S(1)}, u32[]{:S(2)}, u32[]{:S(2)}) collective-permute-start(bf16[4,128,256]{2,1,0:T(8,128)(2,1)S(1)} %get-tuple-element.90), channel_id=1, source_target_pairs={{0,1},{1,0},{2,3},{3,2},{4,5},{5,4},{6,7},{7,6},{8,9},{9,8},{10,11... | collective-permute-start | bytes 786440 | tf_op jit(solution)/shard_map/ppermute | solution.py:40

commit v11 on v10

--- a/solution.py
+++ b/solution.py
@@ -129,25 +129,31 @@
     return estimates
 
 
-def inverse_kernel(layout, slabs, counts, early, late, *refs):
-    fulls, (out, buffer, turned) = refs[-3 - len(counts) : -3], refs[-3:]
-    pieces = refs[: -3 - len(counts)]
-    electrons = early.shape[-1]
+def inverse_kernel(layout, slabs, counts, *refs):
+    streams = len(counts)
+    early, late, refs = refs[:streams], refs[streams : 2 * streams], refs[2 * streams :]
+    fulls, (out, buffer, turned) = refs[-3 - streams : -3], refs[-3:]
+    pieces = refs[: -3 - streams]
+    rows, electrons = early[0].shape[1:]
     b = lax.rem(lax.axis_index("chol"), 2)
 
-    theirs = [(early, at) for at in range(early.shape[0])] + [(late, 0)]
-    trial = [slab for slab in slabs[0] if slab[2] == 2 * counts[0]]
-    for (operand, at, _, steps, dy), (part, place) in zip(trial, theirs):
-        origin = layout.origin(steps, dy)
-        buffer[origin, b] = pieces[operand][at]
-        buffer[origin, 1 - b] = part[place]
+    for half, stream in enumerate(slabs):
+        place = slice(half * rows, (half + 1) * rows)
+        theirs = [(early[half], at) for at in range(early[half].shape[0])] + [(late[half], 0)]
+        trial = [slab for slab in stream if slab[2] == 4 * counts[half]]
+        for (operand, at, _, steps, dy), (part, number) in zip(trial, theirs):
+            origin = layout.origin(steps, dy)
+            buffer[origin, b, place] = pieces[operand][at]
+            buffer[origin, 1 - b, place] = part[number]
     turned[...] = buffer[...].reshape(-1, electrons).T
 
     matrices = []
     for full, count, stream in zip(fulls, counts, slabs):
         for operand, at, slab, steps, dy in stream:
-            if slab < 2 * count:
-                full[slab % count, layout.origin(steps, dy), slab // count] = pieces[operand][at]
+            if slab < 4 * count:
+                block, walker, half = slab // (2 * count), slab // 2 % count, slab % 2
+                place = slice(half * rows, (half + 1) * rows)
+                full[walker, layout.origin(steps, dy), block, place] = pieces[operand][at]
         for walker in range(count):
             columns = full[walker].reshape(-1, electrons)
             matrices.append(jnp.dot(turned[...], columns, preferred_element_type=F32))
@@ -157,7 +163,8 @@
 
 def inverses_of(layout, streams, counts, early, late):
     arrays, slabs = operands(streams)
-    _, rows, electrons = early.shape
+    _, rows, electrons = early[0].shape
+    rows = 2 * rows
     chips = layout.chol // 2
     total = sum(counts)
     return pl.pallas_call(
@@ -166,7 +173,7 @@
             jax.ShapeDtypeStruct((count, chips, 2, rows, electrons), BF16) for count in counts
         ]
         + [jax.ShapeDtypeStruct((total, electrons, electrons), BF16)],
-        in_specs=vmem_specs(2 + len(arrays)),
+        in_specs=vmem_specs(2 * len(counts) + len(arrays)),
         out_specs=vmem_specs(len(counts) + 1),
         scratch_shapes=[
             pltpu.VMEM((chips, 2, rows, electrons), BF16),
@@ -178,7 +185,7 @@
             bytes_accessed=4 * (total + 1) * 2 * chips * rows * electrons,
             transcendentals=0,
         ),
-    )(early, late, *arrays)
+    )(*early, *late, *arrays)
 
 
 def bias_kernel(counts, rot_mine, rot_theirs, inverses, *refs):
@@ -234,16 +241,15 @@
     )(rot_mine, rot_theirs, inverses, *fulls)
 
 
-def potential_kernel(order, fields, mine, mine_across, theirs, theirs_across, cholesky, *refs):
+def potential_kernel(order, fields, mine, theirs, cholesky, *refs):
     bias_out, kept, *sent, weights = refs
     per_group, vectors = fields.shape
     half, piece = kept.shape[0], sent[0].shape[1]
-    sums = (mine[...] + mine_across[...], theirs[...] + theirs_across[...])
     b = lax.rem(lax.axis_index("chol"), 2)
     row = lax.broadcasted_iota(jnp.int32, (per_group, vectors), 0)
     bias = jnp.zeros((per_group, vectors), F32)
     for walker in range(half):
-        for part, core in zip(sums, (b, 1 - b)):
+        for part, core in ((mine, b), (theirs, 1 - b)):
             slot = order[core * half + walker]
             bias += jnp.where(row == slot, part[walker : walker + 1, :], 0.0)
     bias = TAU_ROOT * bias
@@ -289,7 +295,7 @@
             sent,
             sent,
         ],
-        in_specs=[pl.BlockSpec(memory_space=pltpu.SMEM)] + vmem_specs(6),
+        in_specs=[pl.BlockSpec(memory_space=pltpu.SMEM)] + vmem_specs(4),
         out_specs=vmem_specs(4),
         scratch_shapes=[pltpu.VMEM((per_group * BLOCK, vectors * BLOCK), BF16)],
         compiler_params=params(12),
@@ -537,34 +543,41 @@
     b = lax.axis_index("chol") % 2
     shares, order = migrate(layout, walkers, source)
     sizes = [own.shape[0] for own, _ in shares]
-    chunks = [
-        jnp.concatenate([jnp.where(b == 0, own, other), jnp.where(b == 0, other, own), *extra])
-        for (own, other), extra in zip(shares, ([trial[None]], []))
-    ]
-    streams = [Stream(layout, chunk) for chunk in chunks]
+    halves = trial.reshape(2, -1, trial.shape[1])
+    streams = []
+    for at, (own, other) in enumerate(shares):
+        both = (jnp.where(b == 0, own, other), jnp.where(b == 0, other, own))
+        slabs = jnp.concatenate(both).reshape(-1, *halves.shape[1:])
+        streams.append(Stream(layout, jnp.concatenate([slabs, halves[at : at + 1]])))
     rot_theirs = layout.shift(rotated, db=1)
-    moved = lax.optimization_barrier([stream.moves() for stream in streams])
-    for stream, arrays in zip(streams, moved):
+    moved = lax.optimization_barrier([stream.moves() for stream in reversed(streams)])
+    for stream, arrays in zip(reversed(streams), moved):
         stream.accept(arrays)
     for _ in range(layout.z - 2):
         for stream in streams:
             stream.advance()
-    slabs = [array[-1:] for array in (*streams[0].ring, *streams[0].across)]
-    early = layout.shift(jnp.concatenate(slabs), db=1)
-    late = layout.shift(early[layout.z - 1 : layout.z], dy=1)
-    early, rot_theirs = streams[0].advance((early, rot_theirs))
-    streams[1].advance()
+    early, late = [], []
+    for at, stream in enumerate(streams):
+        slabs = [array[-1:] for array in (*stream.ring, *stream.across)]
+        received = layout.shift(jnp.concatenate(slabs), db=1)
+        if at == 0:
+            (received,) = stream.advance((received,))
+        else:
+            stream.advance()
+        early.append(received)
+        late.append(layout.shift(received[layout.z - 1 : layout.z], dy=1))
     *fulls, inverses = inverses_of(layout, streams, sizes, early, late)
     total = bias_of(fulls, inverses, rotated, rot_theirs)
     bits = [2] + [4 << at for at in range(layout.z.bit_length() - 1)]
-    while len(bits) > 1:
-        first, second, *rest = bits if len(bits) % 2 else (bits[0], 0, *bits[1:])
-        sums = [total + layout.flip(total, first)]
-        if second:
-            sums.append(layout.flip(total, second) + layout.flip(total, first + second))
-        total = sum(sums[1:], sums[0])
-        bits = rest
-    parts = [total] + [layout.flip(total, mask) for mask in (bits[0], 1, bits[0] + 1)]
+    while bits:
+        masks = [0]
+        for bit in bits[:3]:
+            masks += [mask + bit for mask in masks]
+        sums = [layout.flip(total, mask) if mask else total for mask in masks]
+        while len(sums) > 1:
+            sums = [one + two for one, two in zip(sums[::2], sums[1::2])]
+        total, bits = sums[0], bits[3:]
+    parts = [total, layout.flip(total, 1)]
     force_bias, kept, *sent = potential_of(order, fields, parts, cholesky)
     received = [layout.shift(part, db=1) for part in sent]
 

time: 142 us -> 140 us (0.986)
  waiting for transfers between devices: 69.8 us -> 59.8 us
  starting transfers between devices: 52.1 us -> 59.7 us
    ppermute x16, waiting for transfers between devices: 48.2 us -> 38.9 us  [step(): return lax.ppermute(array, 'chol', pairs)]
    ppermute x23 -> x25, starting transfers between devices: 17.6 us -> 22.2 us  [shift(): return lax.ppermute(array, 'chol', pairs)]
    ppermute x6 -> x8, starting transfers between devices: 7.27 us -> 11.2 us  [flip(): lax.ppermute(array, 'chol', [(i, i ^ mask) for i in range(self.chol)])]
    ppermute x23 -> x25, waiting for transfers between devices: 13.1 us -> 16.6 us  [shift(): return lax.ppermute(array, 'chol', pairs)]
    ppermute x6 -> x8, waiting for transfers between devices: 7.27 us -> 4.22 us  [flip(): lax.ppermute(array, 'chol', [(i, i ^ mask) for i in range(self.chol)])]
  transfers between devices with their start and end apart: 47 -> 51, of which waited for: 32 -> 36; matrix products, arithmetic and copies ran while one was open for 1% -> 1% of each run, Pallas kernels for 3% -> 5%
where the time goes in v11:
time: 140 us; the launch traced here: 139 us
  waiting for transfers between devices  59.8 us (43%)
  starting transfers between devices  59.7 us (43%)
  Pallas kernels  15.9 us (11%)
  local copies, waits for them, and re-layouts  2.77 us (2%)
    ppermute x16, waiting for transfers between devices, step(): return lax.ppermute(array, 'chol', pairs)  38.9 us
    ppermute x16, starting transfers between devices, step(): return lax.ppermute(array, 'chol', pairs)  23.2 us
    ppermute x25, starting transfers between devices, shift(): return lax.ppermute(array, 'chol', pairs)  22.2 us
    ppermute x25, waiting for transfers between devices, shift(): return lax.ppermute(array, 'chol', pairs)  16.6 us
    ppermute x8, starting transfers between devices, flip(): lax.ppermute(array, 'chol', [(i, i ^ mask) for i in range(self.chol)])  11.2 us
    ppermute x8, waiting for transfers between devices, flip(): lax.ppermute(array, 'chol', [(i, i ^ mask) for i in range(self.chol)])  4.22 us
    pallas_call x1, Pallas kernels, inverses_of(): pl.pallas_call(functools.partial(inverse_kernel, layout, slabs, counts),...  3.27 us
    pallas_call x1, Pallas kernels, potential_of(): pl.pallas_call(potential_kernel, out_shape=[jax.ShapeDtypeStruct((per_gro...  3.16 us
  transfers between devices with their start and end apart: 51, of which 36 were waited for; matrix products, arithmetic and copies ran while one was open for 1% of the time, Pallas kernels for 5%

profile of v11, /device:TPU:0, one launch (start us, length us, event | category | flops | bytes accessed | tf_op | source)
XLA Modules:
  0.0 139.4 jit_solution(3467023007536255068)
XLA Ops:
  0.6 1.2 copy-done.2
  2.5 2.0 %shard_map.77 = (bf16[2,128,256]{2,1,0:T(8,128)(2,1)S(1)}, bf16[2,128,256]{2,1,0:T(8,128)(2,1)S(1)}, bf16[2,128,256]{2,1,0:T(8,128)(2,1)S(1)}, bf16[2,128,256]{2,1,0:T(8,128)(2,1)S(1)}, s32[8]{0:T(128)S(1)}) custom-call(s32[16]{0:T(128)S(1)} %copy-done.4, bf16[8,128,256]{2,1,0:T(8,128)(2,1)S(1)} %copy-done.2), custom_call_target="tpu_custom_call" | custom-call | tf_op jit(solution)/shard_map/pallas_call | solution.py:481
  4.5 3.0 %collective-permute-start.1 = (bf16[2,128,256]{2,1,0:T(8,128)(2,1)S(1)}, bf16[2,128,256]{2,1,0:T(8,128)(2,1)S(1)}, u32[]{:S(2)}, u32[]{:S(2)}) collective-permute-start(bf16[2,128,256]{2,1,0:T(8,128)(2,1)S(1)} %get-tuple-element.48), channel_id=1, source_target_pairs={{0,16},{1,17},{2,18},{3,19},{4,20},{5,21},{6,22},{7,23},{8,24},{9,... | collective-permute-start | bytes 393224 | tf_op jit(solution)/shard_map/ppermute | solution.py:510
  9.0 2.9 %collective-permute-start.7 = (bf16[9,64,256]{2,1,0:T(8,128)(2,1)S(1)}, bf16[9,64,256]{2,1,0:T(8,128)(2,1)S(1)}, u32[]{:S(2)}, u32[]{:S(2)}) collective-permute-start(bf16[9,64,256]{2,1,0:T(8,128)(2,1)S(1)} %pad_maximum_fusion.1.refs_4_), channel_id=1, source_target_pairs={{0,8},{1,9},{2,10},{3,11},{4,0},{5,1},{6,2},{7,3},{8,12},{9,13},{1... | collective-permute-start | bytes 884744 | tf_op jit(solution)/shard_map/ppermute | solution.py:49
  11.9 1.5 %collective-permute-start.6 = (bf16[9,64,256]{2,1,0:T(8,128)(2,1)S(1)}, bf16[9,64,256]{2,1,0:T(8,128)(2,1)S(1)}, u32[]{:S(2)}, u32[]{:S(2)}) collective-permute-start(bf16[9,64,256]{2,1,0:T(8,128)(2,1)S(1)} %pad_maximum_fusion.1.refs_4_), channel_id=1, source_target_pairs={{0,2},{1,3},{2,0},{3,1},{4,6},{5,7},{6,4},{7,5},{8,10},{9,11},{10,... | collective-permute-start | bytes 884744 | tf_op jit(solution)/shard_map/ppermute | solution.py:40
  13.6 2.5 %collective-permute-start.4 = (bf16[9,64,256]{2,1,0:T(8,128)(2,1)S(1)}, bf16[9,64,256]{2,1,0:T(8,128)(2,1)S(1)}, u32[]{:S(2)}, u32[]{:S(2)}) collective-permute-start(bf16[9,64,256]{2,1,0:T(8,128)(2,1)S(1)} %pad_maximum_fusion.refs_13_), channel_id=1, source_target_pairs={{0,8},{1,9},{2,10},{3,11},{4,0},{5,1},{6,2},{7,3},{8,12},{9,13},{1... | collective-permute-start | bytes 884744 | tf_op jit(solution)/shard_map/ppermute | solution.py:49
  16.1 1.5 %collective-permute-start.3 = (bf16[9,64,256]{2,1,0:T(8,128)(2,1)S(1)}, bf16[9,64,256]{2,1,0:T(8,128)(2,1)S(1)}, u32[]{:S(2)}, u32[]{:S(2)}) collective-permute-start(bf16[9,64,256]{2,1,0:T(8,128)(2,1)S(1)} %pad_maximum_fusion.refs_13_), channel_id=1, source_target_pairs={{0,2},{1,3},{2,0},{3,1},{4,6},{5,7},{6,4},{7,5},{8,10},{9,11},{10,... | collective-permute-start | bytes 884744 | tf_op jit(solution)/shard_map/ppermute | solution.py:40
  17.9 1.4 collective-permute-done.7.refs_5_
  19.3 2.5 %collective-permute-done.6.refs_8_ = bf16[9,64,256]{2,1,0:T(8,128)(2,1)S(1)} collective-permute-done((bf16[9,64,256]{2,1,0:T(8,128)(2,1)S(1)}, bf16[9,64,256]{2,1,0:T(8,128)(2,1)S(1)}, u32[]{:S(2)}, u32[]{:S(2)}) %collective-permute-start.6) | collective-permute-done | bytes 294944 | tf_op jit(solution)/shard_map/ppermute | solution.py:40
  21.8 3.2 %collective-permute-done.4.refs_14_ = bf16[9,64,256]{2,1,0:T(8,128)(2,1)S(1)} collective-permute-done((bf16[9,64,256]{2,1,0:T(8,128)(2,1)S(1)}, bf16[9,64,256]{2,1,0:T(8,128)(2,1)S(1)}, u32[]{:S(2)}, u32[]{:S(2)}) %collective-permute-start.4) | collective-permute-done | bytes 294944 | tf_op jit(solution)/shard_map/ppermute | solution.py:49
  25.0 2.2 %collective-permute-done.3.refs_17_ = bf16[9,64,256]{2,1,0:T(8,128)(2,1)S(1)} collective-permute-done((bf16[9,64,256]{2,1,0:T(8,128)(2,1)S(1)}, bf16[9,64,256]{2,1,0:T(8,128)(2,1)S(1)}, u32[]{:S(2)}, u32[]{:S(2)}) %collective-permute-start.3) | collective-permute-done | bytes 294944 | tf_op jit(solution)/shard_map/ppermute | solution.py:40
  27.2 1.6 %collective-permute-start.9 = (bf16[9,64,256]{2,1,0:T(8,128)(2,1)S(1)}, bf16[9,64,256]{2,1,0:T(8,128)(2,1)S(1)}, u32[]{:S(2)}, u32[]{:S(2)}) collective-permute-start(bf16[9,64,256]{2,1,0:T(8,128)(2,1)S(1)} %collective-permute-done.7.refs_5_), channel_id=1, source_target_pairs={{0,8},{1,9},{2,10},{3,11},{4,0},{5,1},{6,2},{7,3},{8,12},{9,13},{1... | collective-permute-start | bytes 884744 | tf_op jit(solution)/shard_map/ppermute | solution.py:49
  28.8 1.5 %collective-permute-start.8 = (bf16[9,64,256]{2,1,0:T(8,128)(2,1)S(1)}, bf16[9,64,256]{2,1,0:T(8,128)(2,1)S(1)}, u32[]{:S(2)}, u32[]{:S(2)}) collective-permute-start(bf16[9,64,256]{2,1,0:T(8,128)(2,1)S(1)} %collective-permute-done.7.refs_5_), channel_id=1, source_target_pairs={{0,2},{1,3},{2,0},{3,1},{4,6},{5,7},{6,4},{7,5},{8,10},{9,11},{10,... | collective-permute-start | bytes 884744 | tf_op jit(solution)/shard_map/ppermute | solution.py:40
  31.2 6.0 %collective-permute-done.9.refs_6_ = bf16[9,64,256]{2,1,0:T(8,128)(2,1)S(1)} collective-permute-done((bf16[9,64,256]{2,1,0:T(8,128)(2,1)S(1)}, bf16[9,64,256]{2,1,0:T(8,128)(2,1)S(1)}, u32[]{:S(2)}, u32[]{:S(2)}) %collective-permute-start.9) | collective-permute-done | bytes 294944 | tf_op jit(solution)/shard_map/ppermute | solution.py:49
  37.2 1.6 %collective-permute-done.8.refs_9_ = bf16[9,64,256]{2,1,0:T(8,128)(2,1)S(1)} collective-permute-done((bf16[9,64,256]{2,1,0:T(8,128)(2,1)S(1)}, bf16[9,64,256]{2,1,0:T(8,128)(2,1)S(1)}, u32[]{:S(2)}, u32[]{:S(2)}) %collective-permute-start.8) | collective-permute-done | bytes 294944 | tf_op jit(solution)/shard_map/ppermute | solution.py:40
  39.7 1.5 %collective-permute-start.10 = (bf16[9,64,256]{2,1,0:T(8,128)(2,1)S(1)}, bf16[9,64,256]{2,1,0:T(8,128)(2,1)S(1)}, u32[]{:S(2)}, u32[]{:S(2)}) collective-permute-start(bf16[9,64,256]{2,1,0:T(8,128)(2,1)S(1)} %collective-permute-done.9.refs_6_), channel_id=1, source_target_pairs={{0,2},{1,3},{2,0},{3,1},{4,6},{5,7},{6,4},{7,5},{8,10},{9,11},{10,... | collective-permute-start | bytes 884744 | tf_op jit(solution)/shard_map/ppermute | solution.py:40
  41.2 2.3 %collective-permute-done.16.refs_15_ = bf16[9,64,256]{2,1,0:T(8,128)(2,1)S(1)} collective-permute-done((bf16[9,64,256]{2,1,0:T(8,128)(2,1)S(1)}, bf16[9,64,256]{2,1,0:T(8,128)(2,1)S(1)}, u32[]{:S(2)}, u32[]{:S(2)}) %collective-permute-start.16) | collective-permute-done | bytes 294944 | tf_op jit(solution)/shard_map/ppermute | solution.py:49
  43.5 1.6 %collective-permute-done.15.refs_18_ = bf16[9,64,256]{2,1,0:T(8,128)(2,1)S(1)} collective-permute-done((bf16[9,64,256]{2,1,0:T(8,128)(2,1)S(1)}, bf16[9,64,256]{2,1,0:T(8,128)(2,1)S(1)}, u32[]{:S(2)}, u32[]{:S(2)}) %collective-permute-start.15) | collective-permute-done | bytes 294944 | tf_op jit(solution)/shard_map/ppermute | solution.py:40
  46.0 1.5 %collective-permute-start.17 = (bf16[9,64,256]{2,1,0:T(8,128)(2,1)S(1)}, bf16[9,64,256]{2,1,0:T(8,128)(2,1)S(1)}, u32[]{:S(2)}, u32[]{:S(2)}) collective-permute-start(bf16[9,64,256]{2,1,0:T(8,128)(2,1)S(1)} %collective-permute-done.16.refs_15_), channel_id=1, source_target_pairs={{0,2},{1,3},{2,0},{3,1},{4,6},{5,7},{6,4},{7,5},{8,10},{9,11},{10,... | collective-permute-start | bytes 884744 | tf_op jit(solution)/shard_map/ppermute | solution.py:40
  47.5 2.3 %collective-permute-done.11.refs_7_ = bf16[9,64,256]{2,1,0:T(8,128)(2,1)S(1)} collective-permute-done((bf16[9,64,256]{2,1,0:T(8,128)(2,1)S(1)}, bf16[9,64,256]{2,1,0:T(8,128)(2,1)S(1)}, u32[]{:S(2)}, u32[]{:S(2)}) %collective-permute-start.11) | collective-permute-done | bytes 294944 | tf_op jit(solution)/shard_map/ppermute | solution.py:49
  49.8 1.6 %collective-permute-done.10.refs_10_ = bf16[9,64,256]{2,1,0:T(8,128)(2,1)S(1)} collective-permute-done((bf16[9,64,256]{2,1,0:T(8,128)(2,1)S(1)}, bf16[9,64,256]{2,1,0:T(8,128)(2,1)S(1)}, u32[]{:S(2)}, u32[]{:S(2)}) %collective-permute-start.10) | collective-permute-done | bytes 294944 | tf_op jit(solution)/shard_map/ppermute | solution.py:40
  51.4 1.0 collective-permute-start.14
  52.4 1.5 %collective-permute-start.13 = (bf16[5,64,256]{2,1,0:T(8,128)(2,1)S(1)}, bf16[5,64,256]{2,1,0:T(8,128)(2,1)S(1)}, u32[]{:S(2)}, u32[]{:S(2)}) collective-permute-start(bf16[5,64,256]{2,1,0:T(8,128)(2,1)S(1)} %slice.88), channel_id=1, source_target_pairs={{0,2},{1,3},{2,0},{3,1},{4,6},{5,7},{6,4},{7,5},{8,10},{9,11},{10,... | collective-permute-start | bytes 491528 | tf_op jit(solution)/shard_map/ppermute | solution.py:40
  53.9 1.8 %collective-permute-done.18.refs_16_ = bf16[9,64,256]{2,1,0:T(8,128)(2,1)S(1)} collective-permute-done((bf16[9,64,256]{2,1,0:T(8,128)(2,1)S(1)}, bf16[9,64,256]{2,1,0:T(8,128)(2,1)S(1)}, u32[]{:S(2)}, u32[]{:S(2)}) %collective-permute-start.18) | collective-permute-done | bytes 294944 | tf_op jit(solution)/shard_map/ppermute | solution.py:49
  55.8 1.6 %collective-permute-done.17.refs_19_ = bf16[9,64,256]{2,1,0:T(8,128)(2,1)S(1)} collective-permute-done((bf16[9,64,256]{2,1,0:T(8,128)(2,1)S(1)}, bf16[9,64,256]{2,1,0:T(8,128)(2,1)S(1)}, u32[]{:S(2)}, u32[]{:S(2)}) %collective-permute-start.17) | collective-permute-done | bytes 294944 | tf_op jit(solution)/shard_map/ppermute | solution.py:40
  57.5 1.6 %collective-permute-start.22 = (bf16[5,64,256]{2,1,0:T(8,128)(2,1)S(1)}, bf16[5,64,256]{2,1,0:T(8,128)(2,1)S(1)}, u32[]{:S(2)}, u32[]{:S(2)}) collective-permute-start(bf16[5,64,256]{2,1,0:T(8,128)(2,1)S(1)} %slice.98), channel_id=1, source_target_pairs={{0,2},{1,3},{2,0},{3,1},{4,6},{5,7},{6,4},{7,5},{8,10},{9,11},{10,... | collective-permute-start | bytes 491528 | tf_op jit(solution)/shard_map/ppermute | solution.py:40
  59.2 2.1 %collective-permute-start.23 = (bf16[4,64,256]{2,1,0:T(8,128)(2,1)S(1)}, bf16[4,64,256]{2,1,0:T(8,128)(2,1)S(1)}, u32[]{:S(2)}, u32[]{:S(2)}) collective-permute-start(bf16[4,64,256]{2,1,0:T(8,128)(2,1)S(1)} %slice.99), channel_id=1, source_target_pairs={{0,8},{1,9},{2,10},{3,11},{4,0},{5,1},{6,2},{7,3},{8,12},{9,13},{1... | collective-permute-start | bytes 393224 | tf_op jit(solution)/shard_map/ppermute | solution.py:49
  61.7 1.5 %collective-permute-start.21 = (bf16[1,64,256]{2,1,0:T(8,128)(2,1)S(1)}, bf16[1,64,256]{2,1,0:T(8,128)(2,1)S(1)}, u32[]{:S(2)}, u32[]{:S(2)}) collective-permute-start(bf16[1,64,256]{2,1,0:T(8,128)(2,1)S(1)} %slice.104), channel_id=1, source_target_pairs={{0,2},{1,3},{2,0},{3,1},{4,6},{5,7},{6,4},{7,5},{8,10},{9,11},{10,... | collective-permute-start | bytes 98312 | tf_op jit(solution)/shard_map/ppermute | solution.py:40
  63.3 1.5 %collective-permute-done.23.refs_21_ = bf16[4,64,256]{2,1,0:T(8,128)(2,1)S(1)} collective-permute-done((bf16[4,64,256]{2,1,0:T(8,128)(2,1)S(1)}, bf16[4,64,256]{2,1,0:T(8,128)(2,1)S(1)}, u32[]{:S(2)}, u32[]{:S(2)}) %collective-permute-start.23) | collective-permute-done | bytes 131104 | tf_op jit(solution)/shard_map/ppermute | solution.py:49
  65.7 3.3 %shard_map.78 = (bf16[2,8,2,128,256]{4,3,2,1,0:T(8,128)(2,1)S(1)}, bf16[2,8,2,128,256]{4,3,2,1,0:T(8,128)(2,1)S(1)}, bf16[4,256,256]{2,1,0:T(8,128)(2,1)S(1)}) custom-call(bf16[7,64,256]{2,1,0:T(8,128)(2,1)S(1)} %collective-permute-done.12.refs_0_, bf16[7,64,256]{2,1,0:T(8,128)(2,1)S(1)} %collective-permute-done.19.refs_1_, ...), custom_call_target="tpu_custom_call" | custom-call | flops 2684354560 | bytes 10485760 | tf_op jit(solution)/shard_map/pallas_call | solution.py:170
  69.0 1.7 %shard_map.79 = f32[4,32]{1,0:T(4,128)S(1)} custom-call(bf16[32,128,256]{2,1,0:T(8,128)(2,1)S(1)} %copy-done.1, bf16[32,128,256]{2,1,0:T(8,128)(2,1)S(1)} %collective-permute-done.rot_theirs, bf16[4,256,256]{2,1,0:T(8,128)(2,1)S(1)} %get-tuple-element.67.inverses, bf16[2,8,2,128,256]{4,3,2,1,0:T(8,128)(2,1)S(1)} %get-tuple-element.68.refs_0_.refs_2_.refs_1_, ...), custom_call_target="tpu_custom_call" | custom-call | flops 402653184 | bytes 4718592 | tf_op jit(solution)/shard_map/pallas_call | solution.py:229
  70.7 2.3 %collective-permute-start.30 = (f32[4,32]{1,0:T(4,128)S(1)}, f32[4,32]{1,0:T(4,128)S(1)}, u32[]{:S(2)}, u32[]{:S(2)}) collective-permute-start(f32[4,32]{1,0:T(4,128)S(1)} %shard_map.79), channel_id=1, source_target_pairs={{0,14},{1,15},{2,12},{3,13},{4,10},{5,11},{6,8},{7,9},{8,6},{9,7},... | collective-permute-start | bytes 1544 | tf_op jit(solution)/shard_map/ppermute | solution.py:43
  72.9 2.6 %collective-permute-start.29 = (f32[4,32]{1,0:T(4,128)S(1)}, f32[4,32]{1,0:T(4,128)S(1)}, u32[]{:S(2)}, u32[]{:S(2)}) collective-permute-start(f32[4,32]{1,0:T(4,128)S(1)} %shard_map.79), channel_id=1, source_target_pairs={{0,12},{1,13},{2,14},{3,15},{4,8},{5,9},{6,10},{7,11},{8,4},{9,5},... | collective-permute-start | bytes 1544 | tf_op jit(solution)/shard_map/ppermute | solution.py:43
  75.5 2.9 %collective-permute-start.27 = (f32[4,32]{1,0:T(4,128)S(1)}, f32[4,32]{1,0:T(4,128)S(1)}, u32[]{:S(2)}, u32[]{:S(2)}) collective-permute-start(f32[4,32]{1,0:T(4,128)S(1)} %shard_map.79), channel_id=1, source_target_pairs={{0,8},{1,9},{2,10},{3,11},{4,12},{5,13},{6,14},{7,15},{8,0},{9,1},... | collective-permute-start | bytes 1544 | tf_op jit(solution)/shard_map/ppermute | solution.py:43
  78.4 3.0 %collective-permute-start.25 = (f32[4,32]{1,0:T(4,128)S(1)}, f32[4,32]{1,0:T(4,128)S(1)}, u32[]{:S(2)}, u32[]{:S(2)}) collective-permute-start(f32[4,32]{1,0:T(4,128)S(1)} %shard_map.79), channel_id=1, source_target_pairs={{0,4},{1,5},{2,6},{3,7},{4,0},{5,1},{6,2},{7,3},{8,12},{9,13},{10,... | collective-permute-start | bytes 1544 | tf_op jit(solution)/shard_map/ppermute | solution.py:43
  81.9 1.0 collective-permute-done.26
  82.9 2.0 %collective-permute-done.24 = f32[4,32]{1,0:T(4,128)S(1)} collective-permute-done((f32[4,32]{1,0:T(4,128)S(1)}, f32[4,32]{1,0:T(4,128)S(1)}, u32[]{:S(2)}, u32[]{:S(2)}) %collective-permute-start.24) | collective-permute-done | bytes 544 | tf_op jit(solution)/shard_map/ppermute | solution.py:43
  85.0 1.1 collective-permute-done.31.theirs
  86.2 3.2 %shard_map.80 = (f32[8,32]{1,0:T(8,128)}, bf16[4,128,2048]{2,1,0:T(8,128)(2,1)S(1)}, bf16[4,64,2048]{2,1,0:T(8,128)(2,1)S(1)}, bf16[4,64,2048]{2,1,0:T(8,128)(2,1)S(1)}) custom-call(s32[8]{0:T(128)S(1)} %get-tuple-element.47.order, f32[8,32]{1,0:T(8,128)S(1)} %copy-done.3, f32[4,32]{1,0:T(4,128)S(1)} %add_add_fusion.mine, ...), custom_call_target="tpu_custom_call" | custom-call | tf_op jit(solution)/shard_map/pallas_call | solution.py:290
  92.1 1.5 %collective-permute-done.33.refs_1_ = bf16[4,64,2048]{2,1,0:T(8,128)(2,1)S(1)} collective-permute-done((bf16[4,64,2048]{2,1,0:T(8,128)(2,1)S(1)}, bf16[4,64,2048]{2,1,0:T(8,128)(2,1)S(1)}, u32[]{:S(2)}, u32[]{:S(2)}) %collective-permute-start.33) | collective-permute-done | bytes 1048608 | tf_op jit(solution)/shard_map/ppermute | solution.py:40
  94.3 1.0 collective-permute-start.42
  95.3 4.5 %collective-permute-done.35.refs_4_ = bf16[4,128,256]{2,1,0:T(8,128)(2,1)S(1)} collective-permute-done((bf16[4,128,256]{2,1,0:T(8,128)(2,1)S(1)}, bf16[4,128,256]{2,1,0:T(8,128)(2,1)S(1)}, u32[]{:S(2)}, u32[]{:S(2)}) %collective-permute-start.35) | collective-permute-done | bytes 262176 | tf_op jit(solution)/shard_map/ppermute | solution.py:49
  99.9 1.8 %collective-permute-start.37 = (bf16[4,128,256]{2,1,0:T(8,128)(2,1)S(1)}, bf16[4,128,256]{2,1,0:T(8,128)(2,1)S(1)}, u32[]{:S(2)}, u32[]{:S(2)}) collective-permute-start(bf16[4,128,256]{2,1,0:T(8,128)(2,1)S(1)} %collective-permute-done.35.refs_4_), channel_id=1, source_target_pairs={{0,8},{1,9},{2,10},{3,11},{4,0},{5,1},{6,2},{7,3},{8,12},{9,13},{1... | collective-permute-start | bytes 786440 | tf_op jit(solution)/shard_map/ppermute | solution.py:49
  101.7 1.0 collective-permute-start.36
  102.7 2.8 %collective-permute-done.43.refs_13_ = bf16[4,128,256]{2,1,0:T(8,128)(2,1)S(1)} collective-permute-done((bf16[4,128,256]{2,1,0:T(8,128)(2,1)S(1)}, bf16[4,128,256]{2,1,0:T(8,128)(2,1)S(1)}, u32[]{:S(2)}, u32[]{:S(2)}) %collective-permute-start.43) | collective-permute-done | bytes 262176 | tf_op jit(solution)/shard_map/ppermute | solution.py:49
  105.5 1.8 %collective-permute-start.45 = (bf16[4,128,256]{2,1,0:T(8,128)(2,1)S(1)}, bf16[4,128,256]{2,1,0:T(8,128)(2,1)S(1)}, u32[]{:S(2)}, u32[]{:S(2)}) collective-permute-start(bf16[4,128,256]{2,1,0:T(8,128)(2,1)S(1)} %collective-permute-done.43.refs_13_), channel_id=1, source_target_pairs={{0,8},{1,9},{2,10},{3,11},{4,0},{5,1},{6,2},{7,3},{8,12},{9,13},{1... | collective-permute-start | bytes 786440 | tf_op jit(solution)/shard_map/ppermute | solution.py:49
  107.3 1.0 collective-permute-start.44
  108.3 2.8 %collective-permute-done.37.refs_5_ = bf16[4,128,256]{2,1,0:T(8,128)(2,1)S(1)} collective-permute-done((bf16[4,128,256]{2,1,0:T(8,128)(2,1)S(1)}, bf16[4,128,256]{2,1,0:T(8,128)(2,1)S(1)}, u32[]{:S(2)}, u32[]{:S(2)}) %collective-permute-start.37) | collective-permute-done | bytes 262176 | tf_op jit(solution)/shard_map/ppermute | solution.py:49
  111.1 1.8 %collective-permute-start.39 = (bf16[4,128,256]{2,1,0:T(8,128)(2,1)S(1)}, bf16[4,128,256]{2,1,0:T(8,128)(2,1)S(1)}, u32[]{:S(2)}, u32[]{:S(2)}) collective-permute-start(bf16[4,128,256]{2,1,0:T(8,128)(2,1)S(1)} %collective-permute-done.37.refs_5_), channel_id=1, source_target_pairs={{0,8},{1,9},{2,10},{3,11},{4,0},{5,1},{6,2},{7,3},{8,12},{9,13},{1... | collective-permute-start | bytes 786440 | tf_op jit(solution)/shard_map/ppermute | solution.py:49
  112.9 1.0 collective-permute-start.38
  113.9 2.8 %collective-permute-done.45.refs_14_ = bf16[4,128,256]{2,1,0:T(8,128)(2,1)S(1)} collective-permute-done((bf16[4,128,256]{2,1,0:T(8,128)(2,1)S(1)}, bf16[4,128,256]{2,1,0:T(8,128)(2,1)S(1)}, u32[]{:S(2)}, u32[]{:S(2)}) %collective-permute-start.45) | collective-permute-done | bytes 262176 | tf_op jit(solution)/shard_map/ppermute | solution.py:49
  116.8 1.8 %collective-permute-start.47 = (bf16[4,128,256]{2,1,0:T(8,128)(2,1)S(1)}, bf16[4,128,256]{2,1,0:T(8,128)(2,1)S(1)}, u32[]{:S(2)}, u32[]{:S(2)}) collective-permute-start(bf16[4,128,256]{2,1,0:T(8,128)(2,1)S(1)} %collective-permute-done.45.refs_14_), channel_id=1, source_target_pairs={{0,8},{1,9},{2,10},{3,11},{4,0},{5,1},{6,2},{7,3},{8,12},{9,13},{1... | collective-permute-start | bytes 786440 | tf_op jit(solution)/shard_map/ppermute | solution.py:49
  118.6 1.0 collective-permute-start.46
  119.5 2.8 %collective-permute-done.39.refs_6_ = bf16[4,128,256]{2,1,0:T(8,128)(2,1)S(1)} collective-permute-done((bf16[4,128,256]{2,1,0:T(8,128)(2,1)S(1)}, bf16[4,128,256]{2,1,0:T(8,128)(2,1)S(1)}, u32[]{:S(2)}, u32[]{:S(2)}) %collective-permute-start.39) | collective-permute-done | bytes 262176 | tf_op jit(solution)/shard_map/ppermute | solution.py:49
  122.4 1.9 %collective-permute-start.41 = (bf16[2,128,256]{2,1,0:T(8,128)(2,1)S(1)}, bf16[2,128,256]{2,1,0:T(8,128)(2,1)S(1)}, u32[]{:S(2)}, u32[]{:S(2)}) collective-permute-start(bf16[2,128,256]{2,1,0:T(8,128)(2,1)S(1)} %slice.101), channel_id=1, source_target_pairs={{0,8},{1,9},{2,10},{3,11},{4,0},{5,1},{6,2},{7,3},{8,12},{9,13},{1... | collective-permute-start | bytes 393224 | tf_op jit(solution)/shard_map/ppermute | solution.py:49
  124.3 1.0 collective-permute-start.40
  125.2 2.7 %collective-permute-done.47.refs_15_ = bf16[4,128,256]{2,1,0:T(8,128)(2,1)S(1)} collective-permute-done((bf16[4,128,256]{2,1,0:T(8,128)(2,1)S(1)}, bf16[4,128,256]{2,1,0:T(8,128)(2,1)S(1)}, u32[]{:S(2)}, u32[]{:S(2)}) %collective-permute-start.47) | collective-permute-done | bytes 262176 | tf_op jit(solution)/shard_map/ppermute | solution.py:49
  128.0 1.9 %collective-permute-start.49 = (bf16[2,128,256]{2,1,0:T(8,128)(2,1)S(1)}, bf16[2,128,256]{2,1,0:T(8,128)(2,1)S(1)}, u32[]{:S(2)}, u32[]{:S(2)}) collective-permute-start(bf16[2,128,256]{2,1,0:T(8,128)(2,1)S(1)} %slice.103), channel_id=1, source_target_pairs={{0,8},{1,9},{2,10},{3,11},{4,0},{5,1},{6,2},{7,3},{8,12},{9,13},{1... | collective-permute-start | bytes 393224 | tf_op jit(solution)/shard_map/ppermute | solution.py:49
  129.9 1.0 collective-permute-start.48
  130.9 2.2 %collective-permute-done.49.refs_20_ = bf16[2,128,256]{2,1,0:T(8,128)(2,1)S(1)} collective-permute-done((bf16[2,128,256]{2,1,0:T(8,128)(2,1)S(1)}, bf16[2,128,256]{2,1,0:T(8,128)(2,1)S(1)}, u32[]{:S(2)}, u32[]{:S(2)}) %collective-permute-start.49) | collective-permute-done | bytes 131104 | tf_op jit(solution)/shard_map/ppermute | solution.py:49
  133.0 1.8 %collective-permute-done.48.refs_19_ = bf16[2,128,256]{2,1,0:T(8,128)(2,1)S(1)} collective-permute-done((bf16[2,128,256]{2,1,0:T(8,128)(2,1)S(1)}, bf16[2,128,256]{2,1,0:T(8,128)(2,1)S(1)}, u32[]{:S(2)}, u32[]{:S(2)}) %collective-permute-start.48) | collective-permute-done | bytes 131104 | tf_op jit(solution)/shard_map/ppermute | solution.py:40
  134.8 1.0 shard_map.83
  135.9 1.9 %shard_map.84._ = bf16[8,128,256]{2,1,0:T(8,128)(2,1)} custom-call(s32[8]{0:T(128)S(1)} %get-tuple-element.47.order, bf16[4,128,2048]{2,1,0:T(8,128)(2,1)S(1)} %get-tuple-element.73.refs_0_.potential, f32[4,128,256]{2,1,0:T(8,128)S(1)} %get-tuple-element.89.base, bf16[4,8,2,128,256]{4,3,2,1,0:T(8,128)(2,1)S(1)} %get-tuple-element.90.full), custom_call_target="tpu_custom_call" | custom-call | flops 536870912 | bytes 6291456 | tf_op jit(solution)/shard_map/pallas_call | solution.py:395
  137.9 1.3 shard_map.85
  (90 shorter events, 11.5 us)
Async XLA Ops:
  0.6 17.0 %copy-start.1 = (bf16[32,128,256]{2,1,0:T(8,128)(2,1)S(1)}, bf16[32,128,256]{2,1,0:T(8,128)(2,1)}, u32[]{:S(2)}) copy-start(bf16[32,128,256]{2,1,0:T(8,128)(2,1)} %rot_mine.1) | copy-start | bytes 6291460
  0.6 1.2 copy-start.2
  1.8 0.7 copy-start.4
  2.5 15.4 %copy-start.5 = (bf16[128,256]{1,0:T(8,128)(2,1)S(1)}, bf16[128,256]{1,0:T(8,128)(2,1)}, u32[]{:S(2)}) copy-start(bf16[128,256]{1,0:T(8,128)(2,1)} %param.7) | copy-start | bytes 196612
  4.5 8.9 %collective-permute-start.1 = (bf16[2,128,256]{2,1,0:T(8,128)(2,1)S(1)}, bf16[2,128,256]{2,1,0:T(8,128)(2,1)S(1)}, u32[]{:S(2)}, u32[]{:S(2)}) collective-permute-start(bf16[2,128,256]{2,1,0:T(8,128)(2,1)S(1)} %get-tuple-element.48), channel_id=1, source_target_pairs={{0,16},{1,17},{2,18},{3,19},{4,20},{5,21},{6,22},{7,23},{8,24},{9,... | collective-permute-start | bytes 393224 | tf_op jit(solution)/shard_map/ppermute | solution.py:510
  7.5 5.9 %collective-permute-start.2 = (bf16[2,128,256]{2,1,0:T(8,128)(2,1)S(1)}, bf16[2,128,256]{2,1,0:T(8,128)(2,1)S(1)}, u32[]{:S(2)}, u32[]{:S(2)}) collective-permute-start(bf16[2,128,256]{2,1,0:T(8,128)(2,1)S(1)} %get-tuple-element.49), channel_id=1, source_target_pairs={{0,17},{1,16},{2,19},{3,18},{4,21},{5,20},{6,23},{7,22},{8,25},{9,... | collective-permute-start | bytes 393224 | tf_op jit(solution)/shard_map/ppermute | solution.py:511
  7.6 1.3 collective-permute-start.5
  9.0 10.3 %collective-permute-start.7 = (bf16[9,64,256]{2,1,0:T(8,128)(2,1)S(1)}, bf16[9,64,256]{2,1,0:T(8,128)(2,1)S(1)}, u32[]{:S(2)}, u32[]{:S(2)}) collective-permute-start(bf16[9,64,256]{2,1,0:T(8,128)(2,1)S(1)} %pad_maximum_fusion.1.refs_4_), channel_id=1, source_target_pairs={{0,8},{1,9},{2,10},{3,11},{4,0},{5,1},{6,2},{7,3},{8,12},{9,13},{1... | collective-permute-start | bytes 884744 | tf_op jit(solution)/shard_map/ppermute | solution.py:49
  11.9 9.9 %collective-permute-start.6 = (bf16[9,64,256]{2,1,0:T(8,128)(2,1)S(1)}, bf16[9,64,256]{2,1,0:T(8,128)(2,1)S(1)}, u32[]{:S(2)}, u32[]{:S(2)}) collective-permute-start(bf16[9,64,256]{2,1,0:T(8,128)(2,1)S(1)} %pad_maximum_fusion.1.refs_4_), channel_id=1, source_target_pairs={{0,2},{1,3},{2,0},{3,1},{4,6},{5,7},{6,4},{7,5},{8,10},{9,11},{10,... | collective-permute-start | bytes 884744 | tf_op jit(solution)/shard_map/ppermute | solution.py:40
  13.6 11.5 %collective-permute-start.4 = (bf16[9,64,256]{2,1,0:T(8,128)(2,1)S(1)}, bf16[9,64,256]{2,1,0:T(8,128)(2,1)S(1)}, u32[]{:S(2)}, u32[]{:S(2)}) collective-permute-start(bf16[9,64,256]{2,1,0:T(8,128)(2,1)S(1)} %pad_maximum_fusion.refs_13_), channel_id=1, source_target_pairs={{0,8},{1,9},{2,10},{3,11},{4,0},{5,1},{6,2},{7,3},{8,12},{9,13},{1... | collective-permute-start | bytes 884744 | tf_op jit(solution)/shard_map/ppermute | solution.py:49
  16.1 11.2 %collective-permute-start.3 = (bf16[9,64,256]{2,1,0:T(8,128)(2,1)S(1)}, bf16[9,64,256]{2,1,0:T(8,128)(2,1)S(1)}, u32[]{:S(2)}, u32[]{:S(2)}) collective-permute-start(bf16[9,64,256]{2,1,0:T(8,128)(2,1)S(1)} %pad_maximum_fusion.refs_13_), channel_id=1, source_target_pairs={{0,2},{1,3},{2,0},{3,1},{4,6},{5,7},{6,4},{7,5},{8,10},{9,11},{10,... | collective-permute-start | bytes 884744 | tf_op jit(solution)/shard_map/ppermute | solution.py:40
  17.6 51.4 %collective-permute-start = (bf16[32,128,256]{2,1,0:T(8,128)(2,1)S(1)}, bf16[32,128,256]{2,1,0:T(8,128)(2,1)S(1)}, u32[]{:S(2)}, u32[]{:S(2)}) collective-permute-start(bf16[32,128,256]{2,1,0:T(8,128)(2,1)S(1)} %copy-done.1), channel_id=1, source_target_pairs={{0,1},{1,0},{2,3},{3,2},{4,5},{5,4},{6,7},{7,6},{8,9},{9,8},{10,11... | collective-permute-start | bytes 6291464 | tf_op jit(solution)/shard_map/ppermute | solution.py:40
  27.2 9.9 %collective-permute-start.9 = (bf16[9,64,256]{2,1,0:T(8,128)(2,1)S(1)}, bf16[9,64,256]{2,1,0:T(8,128)(2,1)S(1)}, u32[]{:S(2)}, u32[]{:S(2)}) collective-permute-start(bf16[9,64,256]{2,1,0:T(8,128)(2,1)S(1)} %collective-permute-done.7.refs_5_), channel_id=1, source_target_pairs={{0,8},{1,9},{2,10},{3,11},{4,0},{5,1},{6,2},{7,3},{8,12},{9,13},{1... | collective-permute-start | bytes 884744 | tf_op jit(solution)/shard_map/ppermute | solution.py:49
  28.8 9.9 %collective-permute-start.8 = (bf16[9,64,256]{2,1,0:T(8,128)(2,1)S(1)}, bf16[9,64,256]{2,1,0:T(8,128)(2,1)S(1)}, u32[]{:S(2)}, u32[]{:S(2)}) collective-permute-start(bf16[9,64,256]{2,1,0:T(8,128)(2,1)S(1)} %collective-permute-done.7.refs_5_), channel_id=1, source_target_pairs={{0,2},{1,3},{2,0},{3,1},{4,6},{5,7},{6,4},{7,5},{8,10},{9,11},{10,... | collective-permute-start | bytes 884744 | tf_op jit(solution)/shard_map/ppermute | solution.py:40
  30.3 13.2 %collective-permute-start.16 = (bf16[9,64,256]{2,1,0:T(8,128)(2,1)S(1)}, bf16[9,64,256]{2,1,0:T(8,128)(2,1)S(1)}, u32[]{:S(2)}, u32[]{:S(2)}) collective-permute-start(bf16[9,64,256]{2,1,0:T(8,128)(2,1)S(1)} %collective-permute-done.4.refs_14_), channel_id=1, source_target_pairs={{0,8},{1,9},{2,10},{3,11},{4,0},{5,1},{6,2},{7,3},{8,12},{9,13},{1... | collective-permute-start | bytes 884744 | tf_op jit(solution)/shard_map/ppermute | solution.py:49
  30.7 14.4 %collective-permute-start.15 = (bf16[9,64,256]{2,1,0:T(8,128)(2,1)S(1)}, bf16[9,64,256]{2,1,0:T(8,128)(2,1)S(1)}, u32[]{:S(2)}, u32[]{:S(2)}) collective-permute-start(bf16[9,64,256]{2,1,0:T(8,128)(2,1)S(1)} %collective-permute-done.4.refs_14_), channel_id=1, source_target_pairs={{0,2},{1,3},{2,0},{3,1},{4,6},{5,7},{6,4},{7,5},{8,10},{9,11},{10,... | collective-permute-start | bytes 884744 | tf_op jit(solution)/shard_map/ppermute | solution.py:40
  38.8 11.1 %collective-permute-start.11 = (bf16[9,64,256]{2,1,0:T(8,128)(2,1)S(1)}, bf16[9,64,256]{2,1,0:T(8,128)(2,1)S(1)}, u32[]{:S(2)}, u32[]{:S(2)}) collective-permute-start(bf16[9,64,256]{2,1,0:T(8,128)(2,1)S(1)} %collective-permute-done.9.refs_6_), channel_id=1, source_target_pairs={{0,8},{1,9},{2,10},{3,11},{4,0},{5,1},{6,2},{7,3},{8,12},{9,13},{1... | collective-permute-start | bytes 884744 | tf_op jit(solution)/shard_map/ppermute | solution.py:49
  39.7 11.7 %collective-permute-start.10 = (bf16[9,64,256]{2,1,0:T(8,128)(2,1)S(1)}, bf16[9,64,256]{2,1,0:T(8,128)(2,1)S(1)}, u32[]{:S(2)}, u32[]{:S(2)}) collective-permute-start(bf16[9,64,256]{2,1,0:T(8,128)(2,1)S(1)} %collective-permute-done.9.refs_6_), channel_id=1, source_target_pairs={{0,2},{1,3},{2,0},{3,1},{4,6},{5,7},{6,4},{7,5},{8,10},{9,11},{10,... | collective-permute-start | bytes 884744 | tf_op jit(solution)/shard_map/ppermute | solution.py:40
  45.1 10.7 %collective-permute-start.18 = (bf16[9,64,256]{2,1,0:T(8,128)(2,1)S(1)}, bf16[9,64,256]{2,1,0:T(8,128)(2,1)S(1)}, u32[]{:S(2)}, u32[]{:S(2)}) collective-permute-start(bf16[9,64,256]{2,1,0:T(8,128)(2,1)S(1)} %collective-permute-done.16.refs_15_), channel_id=1, source_target_pairs={{0,8},{1,9},{2,10},{3,11},{4,0},{5,1},{6,2},{7,3},{8,12},{9,13},{1... | collective-permute-start | bytes 884744 | tf_op jit(solution)/shard_map/ppermute | solution.py:49
  46.0 11.4 %collective-permute-start.17 = (bf16[9,64,256]{2,1,0:T(8,128)(2,1)S(1)}, bf16[9,64,256]{2,1,0:T(8,128)(2,1)S(1)}, u32[]{:S(2)}, u32[]{:S(2)}) collective-permute-start(bf16[9,64,256]{2,1,0:T(8,128)(2,1)S(1)} %collective-permute-done.16.refs_15_), channel_id=1, source_target_pairs={{0,2},{1,3},{2,0},{3,1},{4,6},{5,7},{6,4},{7,5},{8,10},{9,11},{10,... | collective-permute-start | bytes 884744 | tf_op jit(solution)/shard_map/ppermute | solution.py:40
  51.4 6.1 %collective-permute-start.14 = (bf16[4,64,256]{2,1,0:T(8,128)(2,1)S(1)}, bf16[4,64,256]{2,1,0:T(8,128)(2,1)S(1)}, u32[]{:S(2)}, u32[]{:S(2)}) collective-permute-start(bf16[4,64,256]{2,1,0:T(8,128)(2,1)S(1)} %slice.89), channel_id=1, source_target_pairs={{0,8},{1,9},{2,10},{3,11},{4,0},{5,1},{6,2},{7,3},{8,12},{9,13},{1... | collective-permute-start | bytes 393224 | tf_op jit(solution)/shard_map/ppermute | solution.py:49
  52.4 6.8 %collective-permute-start.13 = (bf16[5,64,256]{2,1,0:T(8,128)(2,1)S(1)}, bf16[5,64,256]{2,1,0:T(8,128)(2,1)S(1)}, u32[]{:S(2)}, u32[]{:S(2)}) collective-permute-start(bf16[5,64,256]{2,1,0:T(8,128)(2,1)S(1)} %slice.88), channel_id=1, source_target_pairs={{0,2},{1,3},{2,0},{3,1},{4,6},{5,7},{6,4},{7,5},{8,10},{9,11},{10,... | collective-permute-start | bytes 491528 | tf_op jit(solution)/shard_map/ppermute | solution.py:40
  55.8 5.5 %collective-permute-start.12 = (bf16[7,64,256]{2,1,0:T(8,128)(2,1)S(1)}, bf16[7,64,256]{2,1,0:T(8,128)(2,1)S(1)}, u32[]{:S(2)}, u32[]{:S(2)}) collective-permute-start(bf16[7,64,256]{2,1,0:T(8,128)(2,1)S(1)} %slice_dynamic-update-slice_fusion.6), channel_id=1, source_target_pairs={{0,1},{1,0},{2,3},{3,2},{4,5},{5,4},{6,7},{7,6},{8,9},{9,8},{10,11... | collective-permute-start | bytes 688136 | tf_op jit(solution)/shard_map/ppermute | solution.py:40
  57.4 4.3 %collective-permute-start.19 = (bf16[7,64,256]{2,1,0:T(8,128)(2,1)S(1)}, bf16[7,64,256]{2,1,0:T(8,128)(2,1)S(1)}, u32[]{:S(2)}, u32[]{:S(2)}) collective-permute-start(bf16[7,64,256]{2,1,0:T(8,128)(2,1)S(1)} %slice_dynamic-update-slice_fusion), channel_id=1, source_target_pairs={{0,1},{1,0},{2,3},{3,2},{4,5},{5,4},{6,7},{7,6},{8,9},{9,8},{10,11... | collective-permute-start | bytes 688136 | tf_op jit(solution)/shard_map/ppermute | solution.py:40
  57.5 7.3 %collective-permute-start.22 = (bf16[5,64,256]{2,1,0:T(8,128)(2,1)S(1)}, bf16[5,64,256]{2,1,0:T(8,128)(2,1)S(1)}, u32[]{:S(2)}, u32[]{:S(2)}) collective-permute-start(bf16[5,64,256]{2,1,0:T(8,128)(2,1)S(1)} %slice.98), channel_id=1, source_target_pairs={{0,2},{1,3},{2,0},{3,1},{4,6},{5,7},{6,4},{7,5},{8,10},{9,11},{10,... | collective-permute-start | bytes 491528 | tf_op jit(solution)/shard_map/ppermute | solution.py:40
  59.2 5.7 %collective-permute-start.23 = (bf16[4,64,256]{2,1,0:T(8,128)(2,1)S(1)}, bf16[4,64,256]{2,1,0:T(8,128)(2,1)S(1)}, u32[]{:S(2)}, u32[]{:S(2)}) collective-permute-start(bf16[4,64,256]{2,1,0:T(8,128)(2,1)S(1)} %slice.99), channel_id=1, source_target_pairs={{0,8},{1,9},{2,10},{3,11},{4,0},{5,1},{6,2},{7,3},{8,12},{9,13},{1... | collective-permute-start | bytes 393224 | tf_op jit(solution)/shard_map/ppermute | solution.py:49
  61.2 4.0 %collective-permute-start.20 = (bf16[1,64,256]{2,1,0:T(8,128)(2,1)S(1)}, bf16[1,64,256]{2,1,0:T(8,128)(2,1)S(1)}, u32[]{:S(2)}, u32[]{:S(2)}) collective-permute-start(bf16[1,64,256]{2,1,0:T(8,128)(2,1)S(1)} %slice.96), channel_id=1, source_target_pairs={{0,2},{1,3},{2,0},{3,1},{4,6},{5,7},{6,4},{7,5},{8,10},{9,11},{10,... | collective-permute-start | bytes 98312 | tf_op jit(solution)/shard_map/ppermute | solution.py:40
  61.7 3.9 %collective-permute-start.21 = (bf16[1,64,256]{2,1,0:T(8,128)(2,1)S(1)}, bf16[1,64,256]{2,1,0:T(8,128)(2,1)S(1)}, u32[]{:S(2)}, u32[]{:S(2)}) collective-permute-start(bf16[1,64,256]{2,1,0:T(8,128)(2,1)S(1)} %slice.104), channel_id=1, source_target_pairs={{0,2},{1,3},{2,0},{3,1},{4,6},{5,7},{6,4},{7,5},{8,10},{9,11},{10,... | collective-permute-start | bytes 98312 | tf_op jit(solution)/shard_map/ppermute | solution.py:40
  65.7 20.5 %copy-start = (bf16[32,128,2048]{2,1,0:T(8,128)(2,1)S(1)}, bf16[32,128,2048]{2,1,0:T(8,128)(2,1)}, u32[]{:S(2)}) copy-start(bf16[32,128,2048]{2,1,0:T(8,128)(2,1)} %cholesky.1) | copy-start | bytes 50331652
  69.0 17.2 %copy-start.3 = (f32[8,32]{1,0:T(8,128)S(1)}, f32[8,32]{1,0:T(8,128)}, u32[]{:S(2)}) copy-start(f32[8,32]{1,0:T(8,128)} %fields.1) | copy-start | bytes 3076
  70.7 7.7 %collective-permute-start.30 = (f32[4,32]{1,0:T(4,128)S(1)}, f32[4,32]{1,0:T(4,128)S(1)}, u32[]{:S(2)}, u32[]{:S(2)}) collective-permute-start(f32[4,32]{1,0:T(4,128)S(1)} %shard_map.79), channel_id=1, source_target_pairs={{0,14},{1,15},{2,12},{3,13},{4,10},{5,11},{6,8},{7,9},{8,6},{9,7},... | collective-permute-start | bytes 1544 | tf_op jit(solution)/shard_map/ppermute | solution.py:43
  72.9 8.4 %collective-permute-start.29 = (f32[4,32]{1,0:T(4,128)S(1)}, f32[4,32]{1,0:T(4,128)S(1)}, u32[]{:S(2)}, u32[]{:S(2)}) collective-permute-start(f32[4,32]{1,0:T(4,128)S(1)} %shard_map.79), channel_id=1, source_target_pairs={{0,12},{1,13},{2,14},{3,15},{4,8},{5,9},{6,10},{7,11},{8,4},{9,5},... | collective-permute-start | bytes 1544 | tf_op jit(solution)/shard_map/ppermute | solution.py:43
  75.5 6.4 %collective-permute-start.28 = (f32[4,32]{1,0:T(4,128)S(1)}, f32[4,32]{1,0:T(4,128)S(1)}, u32[]{:S(2)}, u32[]{:S(2)}) collective-permute-start(f32[4,32]{1,0:T(4,128)S(1)} %shard_map.79), channel_id=1, source_target_pairs={{0,10},{1,11},{2,8},{3,9},{4,14},{5,15},{6,12},{7,13},{8,2},{9,3},... | collective-permute-start | bytes 1544 | tf_op jit(solution)/shard_map/ppermute | solution.py:43
  75.5 6.4 %collective-permute-start.27 = (f32[4,32]{1,0:T(4,128)S(1)}, f32[4,32]{1,0:T(4,128)S(1)}, u32[]{:S(2)}, u32[]{:S(2)}) collective-permute-start(f32[4,32]{1,0:T(4,128)S(1)} %shard_map.79), channel_id=1, source_target_pairs={{0,8},{1,9},{2,10},{3,11},{4,12},{5,13},{6,14},{7,15},{8,0},{9,1},... | collective-permute-start | bytes 1544 | tf_op jit(solution)/shard_map/ppermute | solution.py:43
  78.4 4.5 %collective-permute-start.26 = (f32[4,32]{1,0:T(4,128)S(1)}, f32[4,32]{1,0:T(4,128)S(1)}, u32[]{:S(2)}, u32[]{:S(2)}) collective-permute-start(f32[4,32]{1,0:T(4,128)S(1)} %shard_map.79), channel_id=1, source_target_pairs={{0,6},{1,7},{2,4},{3,5},{4,2},{5,3},{6,0},{7,1},{8,14},{9,15},{10,... | collective-permute-start | bytes 1544 | tf_op jit(solution)/shard_map/ppermute | solution.py:43
  78.4 4.6 %collective-permute-start.25 = (f32[4,32]{1,0:T(4,128)S(1)}, f32[4,32]{1,0:T(4,128)S(1)}, u32[]{:S(2)}, u32[]{:S(2)}) collective-permute-start(f32[4,32]{1,0:T(4,128)S(1)} %shard_map.79), channel_id=1, source_target_pairs={{0,4},{1,5},{2,6},{3,7},{4,0},{5,1},{6,2},{7,3},{8,12},{9,13},{10,... | collective-permute-start | bytes 1544 | tf_op jit(solution)/shard_map/ppermute | solution.py:43
  81.3 3.6 %collective-permute-start.24 = (f32[4,32]{1,0:T(4,128)S(1)}, f32[4,32]{1,0:T(4,128)S(1)}, u32[]{:S(2)}, u32[]{:S(2)}) collective-permute-start(f32[4,32]{1,0:T(4,128)S(1)} %shard_map.79), channel_id=1, source_target_pairs={{0,2},{1,3},{2,0},{3,1},{4,6},{5,7},{6,4},{7,5},{8,10},{9,11},{10,... | collective-permute-start | bytes 1544 | tf_op jit(solution)/shard_map/ppermute | solution.py:43
  84.9 1.2 collective-permute-start.31
  89.3 2.7 %collective-permute-start.32 = (bf16[4,64,2048]{2,1,0:T(8,128)(2,1)S(1)}, bf16[4,64,2048]{2,1,0:T(8,128)(2,1)S(1)}, u32[]{:S(2)}, u32[]{:S(2)}) collective-permute-start(bf16[4,64,2048]{2,1,0:T(8,128)(2,1)S(1)} %get-tuple-element.70), channel_id=1, source_target_pairs={{0,1},{1,0},{2,3},{3,2},{4,5},{5,4},{6,7},{7,6},{8,9},{9,8},{10,11... | collective-permute-start | bytes 3145736 | tf_op jit(solution)/shard_map/ppermute | solution.py:40
  89.6 4.0 %collective-permute-start.33 = (bf16[4,64,2048]{2,1,0:T(8,128)(2,1)S(1)}, bf16[4,64,2048]{2,1,0:T(8,128)(2,1)S(1)}, u32[]{:S(2)}, u32[]{:S(2)}) collective-permute-start(bf16[4,64,2048]{2,1,0:T(8,128)(2,1)S(1)} %get-tuple-element.71), channel_id=1, source_target_pairs={{0,1},{1,0},{2,3},{3,2},{4,5},{5,4},{6,7},{7,6},{8,9},{9,8},{10,11... | collective-permute-start | bytes 3145736 | tf_op jit(solution)/shard_map/ppermute | solution.py:40
  90.6 9.2 %collective-permute-start.35 = (bf16[4,128,256]{2,1,0:T(8,128)(2,1)S(1)}, bf16[4,128,256]{2,1,0:T(8,128)(2,1)S(1)}, u32[]{:S(2)}, u32[]{:S(2)}) collective-permute-start(bf16[4,128,256]{2,1,0:T(8,128)(2,1)S(1)} %get-tuple-element.74.refs_3_), channel_id=1, source_target_pairs={{0,8},{1,9},{2,10},{3,11},{4,0},{5,1},{6,2},{7,3},{8,12},{9,13},{1... | collective-permute-start | bytes 786440 | tf_op jit(solution)/shard_map/ppermute | solution.py:49
  90.7 9.2 %collective-permute-start.34 = (bf16[4,128,256]{2,1,0:T(8,128)(2,1)S(1)}, bf16[4,128,256]{2,1,0:T(8,128)(2,1)S(1)}, u32[]{:S(2)}, u32[]{:S(2)}) collective-permute-start(bf16[4,128,256]{2,1,0:T(8,128)(2,1)S(1)} %get-tuple-element.74.refs_3_), channel_id=1, source_target_pairs={{0,2},{1,3},{2,0},{3,1},{4,6},{5,7},{6,4},{7,5},{8,10},{9,11},{10,... | collective-permute-start | bytes 786440 | tf_op jit(solution)/shard_map/ppermute | solution.py:40
  94.3 11.2 %collective-permute-start.43 = (bf16[4,128,256]{2,1,0:T(8,128)(2,1)S(1)}, bf16[4,128,256]{2,1,0:T(8,128)(2,1)S(1)}, u32[]{:S(2)}, u32[]{:S(2)}) collective-permute-start(bf16[4,128,256]{2,1,0:T(8,128)(2,1)S(1)} %get-tuple-element.81.refs_12_), channel_id=1, source_target_pairs={{0,8},{1,9},{2,10},{3,11},{4,0},{5,1},{6,2},{7,3},{8,12},{9,13},{1... | collective-permute-start | bytes 786440 | tf_op jit(solution)/shard_map/ppermute | solution.py:49
  94.3 11.2 %collective-permute-start.42 = (bf16[4,128,256]{2,1,0:T(8,128)(2,1)S(1)}, bf16[4,128,256]{2,1,0:T(8,128)(2,1)S(1)}, u32[]{:S(2)}, u32[]{:S(2)}) collective-permute-start(bf16[4,128,256]{2,1,0:T(8,128)(2,1)S(1)} %get-tuple-element.81.refs_12_), channel_id=1, source_target_pairs={{0,2},{1,3},{2,0},{3,1},{4,6},{5,7},{6,4},{7,5},{8,10},{9,11},{10,... | collective-permute-start | bytes 786440 | tf_op jit(solution)/shard_map/ppermute | solution.py:40
  99.9 11.2 %collective-permute-start.37 = (bf16[4,128,256]{2,1,0:T(8,128)(2,1)S(1)}, bf16[4,128,256]{2,1,0:T(8,128)(2,1)S(1)}, u32[]{:S(2)}, u32[]{:S(2)}) collective-permute-start(bf16[4,128,256]{2,1,0:T(8,128)(2,1)S(1)} %collective-permute-done.35.refs_4_), channel_id=1, source_target_pairs={{0,8},{1,9},{2,10},{3,11},{4,0},{5,1},{6,2},{7,3},{8,12},{9,13},{1... | collective-permute-start | bytes 786440 | tf_op jit(solution)/shard_map/ppermute | solution.py:49
  101.7 9.4 %collective-permute-start.36 = (bf16[4,128,256]{2,1,0:T(8,128)(2,1)S(1)}, bf16[4,128,256]{2,1,0:T(8,128)(2,1)S(1)}, u32[]{:S(2)}, u32[]{:S(2)}) collective-permute-start(bf16[4,128,256]{2,1,0:T(8,128)(2,1)S(1)} %collective-permute-done.35.refs_4_), channel_id=1, source_target_pairs={{0,2},{1,3},{2,0},{3,1},{4,6},{5,7},{6,4},{7,5},{8,10},{9,11},{10,... | collective-permute-start | bytes 786440 | tf_op jit(solution)/shard_map/ppermute | solution.py:40
  105.5 11.2 %collective-permute-start.45 = (bf16[4,128,256]{2,1,0:T(8,128)(2,1)S(1)}, bf16[4,128,256]{2,1,0:T(8,128)(2,1)S(1)}, u32[]{:S(2)}, u32[]{:S(2)}) collective-permute-start(bf16[4,128,256]{2,1,0:T(8,128)(2,1)S(1)} %collective-permute-done.43.refs_13_), channel_id=1, source_target_pairs={{0,8},{1,9},{2,10},{3,11},{4,0},{5,1},{6,2},{7,3},{8,12},{9,13},{1... | collective-permute-start | bytes 786440 | tf_op jit(solution)/shard_map/ppermute | solution.py:49
  107.3 9.4 %collective-permute-start.44 = (bf16[4,128,256]{2,1,0:T(8,128)(2,1)S(1)}, bf16[4,128,256]{2,1,0:T(8,128)(2,1)S(1)}, u32[]{:S(2)}, u32[]{:S(2)}) collective-permute-start(bf16[4,128,256]{2,1,0:T(8,128)(2,1)S(1)} %collective-permute-done.43.refs_13_), channel_id=1, source_target_pairs={{0,2},{1,3},{2,0},{3,1},{4,6},{5,7},{6,4},{7,5},{8,10},{9,11},{10,... | collective-permute-start | bytes 786440 | tf_op jit(solution)/shard_map/ppermute | solution.py:40
  111.1 11.2 %collective-permute-start.39 = (bf16[4,128,256]{2,1,0:T(8,128)(2,1)S(1)}, bf16[4,128,256]{2,1,0:T(8,128)(2,1)S(1)}, u32[]{:S(2)}, u32[]{:S(2)}) collective-permute-start(bf16[4,128,256]{2,1,0:T(8,128)(2,1)S(1)} %collective-permute-done.37.refs_5_), channel_id=1, source_target_pairs={{0,8},{1,9},{2,10},{3,11},{4,0},{5,1},{6,2},{7,3},{8,12},{9,13},{1... | collective-permute-start | bytes 786440 | tf_op jit(solution)/shard_map/ppermute | solution.py:49
  112.9 9.4 %collective-permute-start.38 = (bf16[4,128,256]{2,1,0:T(8,128)(2,1)S(1)}, bf16[4,128,256]{2,1,0:T(8,128)(2,1)S(1)}, u32[]{:S(2)}, u32[]{:S(2)}) collective-permute-start(bf16[4,128,256]{2,1,0:T(8,128)(2,1)S(1)} %collective-permute-done.37.refs_5_), channel_id=1, source_target_pairs={{0,2},{1,3},{2,0},{3,1},{4,6},{5,7},{6,4},{7,5},{8,10},{9,11},{10,... | collective-permute-start | bytes 786440 | tf_op jit(solution)/shard_map/ppermute | solution.py:40
  116.8 11.2 %collective-permute-start.47 = (bf16[4,128,256]{2,1,0:T(8,128)(2,1)S(1)}, bf16[4,128,256]{2,1,0:T(8,128)(2,1)S(1)}, u32[]{:S(2)}, u32[]{:S(2)}) collective-permute-start(bf16[4,128,256]{2,1,0:T(8,128)(2,1)S(1)} %collective-permute-done.45.refs_14_), channel_id=1, source_target_pairs={{0,8},{1,9},{2,10},{3,11},{4,0},{5,1},{6,2},{7,3},{8,12},{9,13},{1... | collective-permute-start | bytes 786440 | tf_op jit(solution)/shard_map/ppermute | solution.py:49
  118.6 9.4 %collective-permute-start.46 = (bf16[4,128,256]{2,1,0:T(8,128)(2,1)S(1)}, bf16[4,128,256]{2,1,0:T(8,128)(2,1)S(1)}, u32[]{:S(2)}, u32[]{:S(2)}) collective-permute-start(bf16[4,128,256]{2,1,0:T(8,128)(2,1)S(1)} %collective-permute-done.45.refs_14_), channel_id=1, source_target_pairs={{0,2},{1,3},{2,0},{3,1},{4,6},{5,7},{6,4},{7,5},{8,10},{9,11},{10,... | collective-permute-start | bytes 786440 | tf_op jit(solution)/shard_map/ppermute | solution.py:40
  122.4 8.5 %collective-permute-start.41 = (bf16[2,128,256]{2,1,0:T(8,128)(2,1)S(1)}, bf16[2,128,256]{2,1,0:T(8,128)(2,1)S(1)}, u32[]{:S(2)}, u32[]{:S(2)}) collective-permute-start(bf16[2,128,256]{2,1,0:T(8,128)(2,1)S(1)} %slice.101), channel_id=1, source_target_pairs={{0,8},{1,9},{2,10},{3,11},{4,0},{5,1},{6,2},{7,3},{8,12},{9,13},{1... | collective-permute-start | bytes 393224 | tf_op jit(solution)/shard_map/ppermute | solution.py:49
  124.3 6.6 %collective-permute-start.40 = (bf16[2,128,256]{2,1,0:T(8,128)(2,1)S(1)}, bf16[2,128,256]{2,1,0:T(8,128)(2,1)S(1)}, u32[]{:S(2)}, u32[]{:S(2)}) collective-permute-start(bf16[2,128,256]{2,1,0:T(8,128)(2,1)S(1)} %slice.100), channel_id=1, source_target_pairs={{0,2},{1,3},{2,0},{3,1},{4,6},{5,7},{6,4},{7,5},{8,10},{9,11},{10,... | collective-permute-start | bytes 393224 | tf_op jit(solution)/shard_map/ppermute | solution.py:40
  128.0 5.0 %collective-permute-start.49 = (bf16[2,128,256]{2,1,0:T(8,128)(2,1)S(1)}, bf16[2,128,256]{2,1,0:T(8,128)(2,1)S(1)}, u32[]{:S(2)}, u32[]{:S(2)}) collective-permute-start(bf16[2,128,256]{2,1,0:T(8,128)(2,1)S(1)} %slice.103), channel_id=1, source_target_pairs={{0,8},{1,9},{2,10},{3,11},{4,0},{5,1},{6,2},{7,3},{8,12},{9,13},{1... | collective-permute-start | bytes 393224 | tf_op jit(solution)/shard_map/ppermute | solution.py:49
  129.9 5.0 %collective-permute-start.48 = (bf16[2,128,256]{2,1,0:T(8,128)(2,1)S(1)}, bf16[2,128,256]{2,1,0:T(8,128)(2,1)S(1)}, u32[]{:S(2)}, u32[]{:S(2)}) collective-permute-start(bf16[2,128,256]{2,1,0:T(8,128)(2,1)S(1)} %slice.102), channel_id=1, source_target_pairs={{0,2},{1,3},{2,0},{3,1},{4,6},{5,7},{6,4},{7,5},{8,10},{9,11},{10,... | collective-permute-start | bytes 393224 | tf_op jit(solution)/shard_map/ppermute | solution.py:40
  135.9 2.0 %collective-permute-start.50 = (bf16[4,128,256]{2,1,0:T(8,128)(2,1)S(1)}, bf16[4,128,256]{2,1,0:T(8,128)(2,1)S(1)}, u32[]{:S(2)}, u32[]{:S(2)}) collective-permute-start(bf16[4,128,256]{2,1,0:T(8,128)(2,1)S(1)} %get-tuple-element.88), channel_id=1, source_target_pairs={{0,1},{1,0},{2,3},{3,2},{4,5},{5,4},{6,7},{7,6},{8,9},{9,8},{10,11... | collective-permute-start | bytes 786440 | tf_op jit(solution)/shard_map/ppermute | solution.py:40

commit v12 on v11

--- a/solution.py
+++ b/solution.py
@@ -241,17 +241,20 @@
     )(rot_mine, rot_theirs, inverses, *fulls)
 
 
-def potential_kernel(order, fields, mine, theirs, cholesky, *refs):
+def potential_kernel(order, fields, parts, cholesky, *refs):
     bias_out, kept, *sent, weights = refs
     per_group, vectors = fields.shape
     half, piece = kept.shape[0], sent[0].shape[1]
     b = lax.rem(lax.axis_index("chol"), 2)
     row = lax.broadcasted_iota(jnp.int32, (per_group, vectors), 0)
     bias = jnp.zeros((per_group, vectors), F32)
-    for walker in range(half):
-        for part, core in ((mine, b), (theirs, 1 - b)):
+    for core in range(2):
+        total = parts[core]
+        for index in range(core + 2, parts.shape[0], 2):
+            total = total + parts[index]
+        for walker in range(half):
             slot = order[core * half + walker]
-            bias += jnp.where(row == slot, part[walker : walker + 1, :], 0.0)
+            bias += jnp.where(row == slot, total[walker : walker + 1, :], 0.0)
     bias = TAU_ROOT * bias
     bias_out[...] = bias
     shifted = (fields[...] - bias).astype(BF16)
@@ -295,11 +298,11 @@
             sent,
             sent,
         ],
-        in_specs=[pl.BlockSpec(memory_space=pltpu.SMEM)] + vmem_specs(4),
+        in_specs=[pl.BlockSpec(memory_space=pltpu.SMEM)] + vmem_specs(3),
         out_specs=vmem_specs(4),
         scratch_shapes=[pltpu.VMEM((per_group * BLOCK, vectors * BLOCK), BF16)],
         compiler_params=params(12),
-    )(order, fields, *parts, cholesky)
+    )(order, fields, parts, cholesky)
 
 
 def first_kernel(sibling, parts, *refs):
@@ -452,7 +455,7 @@
         picked[jnp.where(stays == 1, jnp.minimum(stayed, half - 1), per_group)] = local
         rank = jnp.minimum(jnp.where(stays == 1, stayed, arrived), half - 1)
         core = rank // share
-        order[core * half + (1 - stays) * share + rank - core * share] = jnp.int32(slot)
+        order[core * half + stays * share + rank - core * share] = jnp.int32(slot)
         stayed, arrived = stayed + stays, arrived + 1 - stays
         local = source[(1 - group) * per_group + slot] - group * per_group
         goes = ((local >= 0) & (local < per_group)).astype(jnp.int32)
@@ -509,7 +512,7 @@
         axes = ("walk", "chol")
         near = lax.ppermute(near, axes, list(enumerate(across)))
         cross = lax.ppermute(cross, axes, [(i, j ^ 1) for i, j in enumerate(across)])
-        return [(stay, layout.shift(stay_sent, db=1)), (near, cross)], order
+        return [(near, cross), (stay, layout.shift(stay_sent, db=1))], order
     table = source.reshape(layout.walk, per_group)
     incoming = lax.dynamic_index_in_dim(table, group, 0, keepdims=False)
     incoming_groups = incoming // per_group
@@ -550,17 +553,14 @@
         slabs = jnp.concatenate(both).reshape(-1, *halves.shape[1:])
         streams.append(Stream(layout, jnp.concatenate([slabs, halves[at : at + 1]])))
     rot_theirs = layout.shift(rotated, db=1)
-    moved = lax.optimization_barrier([stream.moves() for stream in reversed(streams)])
-    for stream, arrays in zip(reversed(streams), moved):
-        stream.accept(arrays)
-    for _ in range(layout.z - 2):
+    for _ in range(layout.z - 1):
         for stream in streams:
             stream.advance()
     early, late = [], []
     for at, stream in enumerate(streams):
         slabs = [array[-1:] for array in (*stream.ring, *stream.across)]
         received = layout.shift(jnp.concatenate(slabs), db=1)
-        if at == 0:
+        if at == 1:
             (received,) = stream.advance((received,))
         else:
             stream.advance()
@@ -568,16 +568,9 @@
         late.append(layout.shift(received[layout.z - 1 : layout.z], dy=1))
     *fulls, inverses = inverses_of(layout, streams, sizes, early, late)
     total = bias_of(fulls, inverses, rotated, rot_theirs)
-    bits = [2] + [4 << at for at in range(layout.z.bit_length() - 1)]
-    while bits:
-        masks = [0]
-        for bit in bits[:3]:
-            masks += [mask + bit for mask in masks]
-        sums = [layout.flip(total, mask) if mask else total for mask in masks]
-        while len(sums) > 1:
-            sums = [one + two for one, two in zip(sums[::2], sums[1::2])]
-        total, bits = sums[0], bits[3:]
-    parts = [total, layout.flip(total, 1)]
+    parts = lax.all_to_all(
+        jnp.broadcast_to(total, (layout.chol, *total.shape)), "chol", 0, 0, tiled=True
+    )
     force_bias, kept, *sent = potential_of(order, fields, parts, cholesky)
     received = [layout.shift(part, db=1) for part in sent]
 

time: 140 us -> 140 us (level)
  starting transfers between devices: 59.7 us -> 45.1 us
  blocking collectives: 0 us -> 9.37 us
  local copies, waits for them, and re-layouts: 2.77 us -> 9.1 us
  waiting for transfers between devices: 59.8 us -> 55.8 us
  Pallas kernels: 15.9 us -> 18.5 us
    ppermute x8 -> x0, starting transfers between devices: 11.2 us -> none  [flip(): lax.ppermute(array, 'chol', [(i, i ^ mask) for i in range(self.chol)])]
    all_to_all x0 -> x1, blocking collectives: none -> 9.37 us  [shards(): lax.all_to_all(jnp.broadcast_to(total, (layout.chol, *total.shape)), 'cho...]
    ppermute x25, waiting for transfers between devices: 16.6 us -> 24.4 us  [shift(): return lax.ppermute(array, 'chol', pairs)]
    ppermute x16, waiting for transfers between devices: 38.9 us -> 31.4 us  [step(): return lax.ppermute(array, 'chol', pairs)]
    unnamed x23 -> x27, local copies, waits for them, and re-layouts: 1.89 us -> 7.68 us
    ppermute x8 -> x0, waiting for transfers between devices: 4.22 us -> none  [flip(): lax.ppermute(array, 'chol', [(i, i ^ mask) for i in range(self.chol)])]
    pallas_call x1, Pallas kernels: 1.71 us -> 4.07 us  [bias_of(): pl.pallas_call(functools.partial(bias_kernel, counts), out_shape=jax.Shap...]
    ppermute x25, starting transfers between devices: 22.2 us -> 20 us  [shift(): return lax.ppermute(array, 'chol', pairs)]
  transfers between devices with their start and end apart: 51 -> 43, of which waited for: 36 -> 34; matrix products, arithmetic and copies ran while one was open for 1% -> 1% of each run, Pallas kernels for 5% -> 5%
where the time goes in v12:
time: 140 us
  waiting for transfers between devices  55.8 us (40%)
  starting transfers between devices  45.1 us (32%)
  Pallas kernels  18.5 us (13%)
  blocking collectives  9.37 us (7%)
  local copies, waits for them, and re-layouts  9.1 us (6%)
    ppermute x16, waiting for transfers between devices, step(): return lax.ppermute(array, 'chol', pairs)  31.4 us
    ppermute x25, waiting for transfers between devices, shift(): return lax.ppermute(array, 'chol', pairs)  24.4 us
    ppermute x16, starting transfers between devices, step(): return lax.ppermute(array, 'chol', pairs)  22.1 us
    ppermute x25, starting transfers between devices, shift(): return lax.ppermute(array, 'chol', pairs)  20 us
    all_to_all x1, blocking collectives, shards(): lax.all_to_all(jnp.broadcast_to(total, (layout.chol, *total.shape)), 'cho...  9.37 us
    unnamed x27, local copies, waits for them, and re-layouts  7.68 us
    pallas_call x1, Pallas kernels, bias_of(): pl.pallas_call(functools.partial(bias_kernel, counts), out_shape=jax.Shap...  4.07 us
    pallas_call x1, Pallas kernels, inverses_of(): pl.pallas_call(functools.partial(inverse_kernel, layout, slabs, counts),...  3.28 us
  transfers between devices with their start and end apart: 43, of which 34 were waited for; matrix products, arithmetic and copies ran while one was open for 1% of the time, Pallas kernels for 5%

profile of v12, /device:TPU:0, one launch (start us, length us, event | category | flops | bytes accessed | tf_op | source)
XLA Modules:
  0.0 139.7 jit_solution(5496386302127007011)
XLA Ops:
  0.6 1.0 copy-done.3
  2.3 2.0 %shard_map.77 = (bf16[2,128,256]{2,1,0:T(8,128)(2,1)S(1)}, bf16[2,128,256]{2,1,0:T(8,128)(2,1)S(1)}, bf16[2,128,256]{2,1,0:T(8,128)(2,1)S(1)}, bf16[2,128,256]{2,1,0:T(8,128)(2,1)S(1)}, s32[8]{0:T(128)S(1)}) custom-call(s32[16]{0:T(128)S(1)} %copy-done.5, bf16[8,128,256]{2,1,0:T(8,128)(2,1)S(1)} %copy-done.3), custom_call_target="tpu_custom_call" | custom-call | tf_op jit(solution)/shard_map/pallas_call | solution.py:484
  4.3 3.0 %collective-permute-start.1 = (bf16[2,128,256]{2,1,0:T(8,128)(2,1)S(1)}, bf16[2,128,256]{2,1,0:T(8,128)(2,1)S(1)}, u32[]{:S(2)}, u32[]{:S(2)}) collective-permute-start(bf16[2,128,256]{2,1,0:T(8,128)(2,1)S(1)} %get-tuple-element.48), channel_id=1, source_target_pairs={{0,16},{1,17},{2,18},{3,19},{4,20},{5,21},{6,22},{7,23},{8,24},{9,... | collective-permute-start | bytes 393224 | tf_op jit(solution)/shard_map/ppermute | solution.py:513
  7.5 0.8 slice_bitcast_fusion
  8.8 2.9 %collective-permute-start.12 = (bf16[9,64,256]{2,1,0:T(8,128)(2,1)S(1)}, bf16[9,64,256]{2,1,0:T(8,128)(2,1)S(1)}, u32[]{:S(2)}, u32[]{:S(2)}) collective-permute-start(bf16[9,64,256]{2,1,0:T(8,128)(2,1)S(1)} %pad_maximum_fusion.1.refs_13_), channel_id=1, source_target_pairs={{0,8},{1,9},{2,10},{3,11},{4,0},{5,1},{6,2},{7,3},{8,12},{9,13},{1... | collective-permute-start | bytes 884744 | tf_op jit(solution)/shard_map/ppermute | solution.py:49
  11.7 1.5 %collective-permute-start.11 = (bf16[9,64,256]{2,1,0:T(8,128)(2,1)S(1)}, bf16[9,64,256]{2,1,0:T(8,128)(2,1)S(1)}, u32[]{:S(2)}, u32[]{:S(2)}) collective-permute-start(bf16[9,64,256]{2,1,0:T(8,128)(2,1)S(1)} %pad_maximum_fusion.1.refs_13_), channel_id=1, source_target_pairs={{0,2},{1,3},{2,0},{3,1},{4,6},{5,7},{6,4},{7,5},{8,10},{9,11},{10,... | collective-permute-start | bytes 884744 | tf_op jit(solution)/shard_map/ppermute | solution.py:40
  13.4 2.5 %collective-permute-start.4 = (bf16[9,64,256]{2,1,0:T(8,128)(2,1)S(1)}, bf16[9,64,256]{2,1,0:T(8,128)(2,1)S(1)}, u32[]{:S(2)}, u32[]{:S(2)}) collective-permute-start(bf16[9,64,256]{2,1,0:T(8,128)(2,1)S(1)} %pad_maximum_fusion.refs_4_), channel_id=1, source_target_pairs={{0,8},{1,9},{2,10},{3,11},{4,0},{5,1},{6,2},{7,3},{8,12},{9,13},{1... | collective-permute-start | bytes 884744 | tf_op jit(solution)/shard_map/ppermute | solution.py:49
  15.9 1.5 %collective-permute-start.3 = (bf16[9,64,256]{2,1,0:T(8,128)(2,1)S(1)}, bf16[9,64,256]{2,1,0:T(8,128)(2,1)S(1)}, u32[]{:S(2)}, u32[]{:S(2)}) collective-permute-start(bf16[9,64,256]{2,1,0:T(8,128)(2,1)S(1)} %pad_maximum_fusion.refs_4_), channel_id=1, source_target_pairs={{0,2},{1,3},{2,0},{3,1},{4,6},{5,7},{6,4},{7,5},{8,10},{9,11},{10,... | collective-permute-start | bytes 884744 | tf_op jit(solution)/shard_map/ppermute | solution.py:40
  17.7 1.4 collective-permute-done.12.refs_14_
  19.1 2.5 %collective-permute-done.11.refs_17_ = bf16[9,64,256]{2,1,0:T(8,128)(2,1)S(1)} collective-permute-done((bf16[9,64,256]{2,1,0:T(8,128)(2,1)S(1)}, bf16[9,64,256]{2,1,0:T(8,128)(2,1)S(1)}, u32[]{:S(2)}, u32[]{:S(2)}) %collective-permute-start.11) | collective-permute-done | bytes 294944 | tf_op jit(solution)/shard_map/ppermute | solution.py:40
  21.6 1.6 %collective-permute-start.14 = (bf16[9,64,256]{2,1,0:T(8,128)(2,1)S(1)}, bf16[9,64,256]{2,1,0:T(8,128)(2,1)S(1)}, u32[]{:S(2)}, u32[]{:S(2)}) collective-permute-start(bf16[9,64,256]{2,1,0:T(8,128)(2,1)S(1)} %collective-permute-done.12.refs_14_), channel_id=1, source_target_pairs={{0,8},{1,9},{2,10},{3,11},{4,0},{5,1},{6,2},{7,3},{8,12},{9,13},{1... | collective-permute-start | bytes 884744 | tf_op jit(solution)/shard_map/ppermute | solution.py:49
  23.2 1.5 %collective-permute-start.13 = (bf16[9,64,256]{2,1,0:T(8,128)(2,1)S(1)}, bf16[9,64,256]{2,1,0:T(8,128)(2,1)S(1)}, u32[]{:S(2)}, u32[]{:S(2)}) collective-permute-start(bf16[9,64,256]{2,1,0:T(8,128)(2,1)S(1)} %collective-permute-done.12.refs_14_), channel_id=1, source_target_pairs={{0,2},{1,3},{2,0},{3,1},{4,6},{5,7},{6,4},{7,5},{8,10},{9,11},{10,... | collective-permute-start | bytes 884744 | tf_op jit(solution)/shard_map/ppermute | solution.py:40
  24.7 0.7 collective-permute-done.4.refs_5_
  25.4 2.5 %collective-permute-done.3.refs_8_ = bf16[9,64,256]{2,1,0:T(8,128)(2,1)S(1)} collective-permute-done((bf16[9,64,256]{2,1,0:T(8,128)(2,1)S(1)}, bf16[9,64,256]{2,1,0:T(8,128)(2,1)S(1)}, u32[]{:S(2)}, u32[]{:S(2)}) %collective-permute-start.3) | collective-permute-done | bytes 294944 | tf_op jit(solution)/shard_map/ppermute | solution.py:40
  27.9 1.6 %collective-permute-start.6 = (bf16[9,64,256]{2,1,0:T(8,128)(2,1)S(1)}, bf16[9,64,256]{2,1,0:T(8,128)(2,1)S(1)}, u32[]{:S(2)}, u32[]{:S(2)}) collective-permute-start(bf16[9,64,256]{2,1,0:T(8,128)(2,1)S(1)} %collective-permute-done.4.refs_5_), channel_id=1, source_target_pairs={{0,8},{1,9},{2,10},{3,11},{4,0},{5,1},{6,2},{7,3},{8,12},{9,13},{1... | collective-permute-start | bytes 884744 | tf_op jit(solution)/shard_map/ppermute | solution.py:49
  29.5 1.5 %collective-permute-start.5 = (bf16[9,64,256]{2,1,0:T(8,128)(2,1)S(1)}, bf16[9,64,256]{2,1,0:T(8,128)(2,1)S(1)}, u32[]{:S(2)}, u32[]{:S(2)}) collective-permute-start(bf16[9,64,256]{2,1,0:T(8,128)(2,1)S(1)} %collective-permute-done.4.refs_5_), channel_id=1, source_target_pairs={{0,2},{1,3},{2,0},{3,1},{4,6},{5,7},{6,4},{7,5},{8,10},{9,11},{10,... | collective-permute-start | bytes 884744 | tf_op jit(solution)/shard_map/ppermute | solution.py:40
  31.0 0.7 collective-permute-done.14.refs_15_
  31.7 2.5 %collective-permute-done.13.refs_18_ = bf16[9,64,256]{2,1,0:T(8,128)(2,1)S(1)} collective-permute-done((bf16[9,64,256]{2,1,0:T(8,128)(2,1)S(1)}, bf16[9,64,256]{2,1,0:T(8,128)(2,1)S(1)}, u32[]{:S(2)}, u32[]{:S(2)}) %collective-permute-start.13) | collective-permute-done | bytes 294944 | tf_op jit(solution)/shard_map/ppermute | solution.py:40
  34.2 1.6 %collective-permute-start.16 = (bf16[9,64,256]{2,1,0:T(8,128)(2,1)S(1)}, bf16[9,64,256]{2,1,0:T(8,128)(2,1)S(1)}, u32[]{:S(2)}, u32[]{:S(2)}) collective-permute-start(bf16[9,64,256]{2,1,0:T(8,128)(2,1)S(1)} %collective-permute-done.14.refs_15_), channel_id=1, source_target_pairs={{0,8},{1,9},{2,10},{3,11},{4,0},{5,1},{6,2},{7,3},{8,12},{9,13},{1... | collective-permute-start | bytes 884744 | tf_op jit(solution)/shard_map/ppermute | solution.py:49
  35.8 1.5 %collective-permute-start.15 = (bf16[9,64,256]{2,1,0:T(8,128)(2,1)S(1)}, bf16[9,64,256]{2,1,0:T(8,128)(2,1)S(1)}, u32[]{:S(2)}, u32[]{:S(2)}) collective-permute-start(bf16[9,64,256]{2,1,0:T(8,128)(2,1)S(1)} %collective-permute-done.14.refs_15_), channel_id=1, source_target_pairs={{0,2},{1,3},{2,0},{3,1},{4,6},{5,7},{6,4},{7,5},{8,10},{9,11},{10,... | collective-permute-start | bytes 884744 | tf_op jit(solution)/shard_map/ppermute | solution.py:40
  37.3 0.7 collective-permute-done.6.refs_6_
  38.0 2.5 %collective-permute-done.5.refs_9_ = bf16[9,64,256]{2,1,0:T(8,128)(2,1)S(1)} collective-permute-done((bf16[9,64,256]{2,1,0:T(8,128)(2,1)S(1)}, bf16[9,64,256]{2,1,0:T(8,128)(2,1)S(1)}, u32[]{:S(2)}, u32[]{:S(2)}) %collective-permute-start.5) | collective-permute-done | bytes 294944 | tf_op jit(solution)/shard_map/ppermute | solution.py:40
  40.6 1.6 %collective-permute-start.8 = (bf16[9,64,256]{2,1,0:T(8,128)(2,1)S(1)}, bf16[9,64,256]{2,1,0:T(8,128)(2,1)S(1)}, u32[]{:S(2)}, u32[]{:S(2)}) collective-permute-start(bf16[9,64,256]{2,1,0:T(8,128)(2,1)S(1)} %collective-permute-done.6.refs_6_), channel_id=1, source_target_pairs={{0,8},{1,9},{2,10},{3,11},{4,0},{5,1},{6,2},{7,3},{8,12},{9,13},{1... | collective-permute-start | bytes 884744 | tf_op jit(solution)/shard_map/ppermute | solution.py:49
  42.1 1.5 %collective-permute-start.7 = (bf16[9,64,256]{2,1,0:T(8,128)(2,1)S(1)}, bf16[9,64,256]{2,1,0:T(8,128)(2,1)S(1)}, u32[]{:S(2)}, u32[]{:S(2)}) collective-permute-start(bf16[9,64,256]{2,1,0:T(8,128)(2,1)S(1)} %collective-permute-done.6.refs_6_), channel_id=1, source_target_pairs={{0,2},{1,3},{2,0},{3,1},{4,6},{5,7},{6,4},{7,5},{8,10},{9,11},{10,... | collective-permute-start | bytes 884744 | tf_op jit(solution)/shard_map/ppermute | solution.py:40
  43.7 0.7 collective-permute-done.16.refs_16_
  44.4 2.5 %collective-permute-done.15.refs_19_ = bf16[9,64,256]{2,1,0:T(8,128)(2,1)S(1)} collective-permute-done((bf16[9,64,256]{2,1,0:T(8,128)(2,1)S(1)}, bf16[9,64,256]{2,1,0:T(8,128)(2,1)S(1)}, u32[]{:S(2)}, u32[]{:S(2)}) %collective-permute-start.15) | collective-permute-done | bytes 294944 | tf_op jit(solution)/shard_map/ppermute | solution.py:40
  46.9 1.6 %collective-permute-start.19 = (bf16[4,64,256]{2,1,0:T(8,128)(2,1)S(1)}, bf16[4,64,256]{2,1,0:T(8,128)(2,1)S(1)}, u32[]{:S(2)}, u32[]{:S(2)}) collective-permute-start(bf16[4,64,256]{2,1,0:T(8,128)(2,1)S(1)} %slice.95), channel_id=1, source_target_pairs={{0,8},{1,9},{2,10},{3,11},{4,0},{5,1},{6,2},{7,3},{8,12},{9,13},{1... | collective-permute-start | bytes 393224 | tf_op jit(solution)/shard_map/ppermute | solution.py:49
  48.6 1.5 %collective-permute-start.18 = (bf16[5,64,256]{2,1,0:T(8,128)(2,1)S(1)}, bf16[5,64,256]{2,1,0:T(8,128)(2,1)S(1)}, u32[]{:S(2)}, u32[]{:S(2)}) collective-permute-start(bf16[5,64,256]{2,1,0:T(8,128)(2,1)S(1)} %slice.94), channel_id=1, source_target_pairs={{0,2},{1,3},{2,0},{3,1},{4,6},{5,7},{6,4},{7,5},{8,10},{9,11},{10,... | collective-permute-start | bytes 491528 | tf_op jit(solution)/shard_map/ppermute | solution.py:40
  50.7 2.5 %collective-permute-done.7.refs_10_ = bf16[9,64,256]{2,1,0:T(8,128)(2,1)S(1)} collective-permute-done((bf16[9,64,256]{2,1,0:T(8,128)(2,1)S(1)}, bf16[9,64,256]{2,1,0:T(8,128)(2,1)S(1)}, u32[]{:S(2)}, u32[]{:S(2)}) %collective-permute-start.7) | collective-permute-done | bytes 294944 | tf_op jit(solution)/shard_map/ppermute | solution.py:40
  53.3 1.6 %collective-permute-start.22 = (bf16[5,64,256]{2,1,0:T(8,128)(2,1)S(1)}, bf16[5,64,256]{2,1,0:T(8,128)(2,1)S(1)}, u32[]{:S(2)}, u32[]{:S(2)}) collective-permute-start(bf16[5,64,256]{2,1,0:T(8,128)(2,1)S(1)} %slice.98), channel_id=1, source_target_pairs={{0,2},{1,3},{2,0},{3,1},{4,6},{5,7},{6,4},{7,5},{8,10},{9,11},{10,... | collective-permute-start | bytes 491528 | tf_op jit(solution)/shard_map/ppermute | solution.py:40
  54.9 0.9 collective-permute-done.18.refs_20_
  55.8 2.1 %collective-permute-start.23 = (bf16[4,64,256]{2,1,0:T(8,128)(2,1)S(1)}, bf16[4,64,256]{2,1,0:T(8,128)(2,1)S(1)}, u32[]{:S(2)}, u32[]{:S(2)}) collective-permute-start(bf16[4,64,256]{2,1,0:T(8,128)(2,1)S(1)} %slice.99), channel_id=1, source_target_pairs={{0,8},{1,9},{2,10},{3,11},{4,0},{5,1},{6,2},{7,3},{8,12},{9,13},{1... | collective-permute-start | bytes 393224 | tf_op jit(solution)/shard_map/ppermute | solution.py:49
  57.9 1.0 collective-permute-start.21
  58.9 1.0 collective-permute-start.20
  59.9 0.9 collective-permute-done.23.refs_12_
  60.8 1.0 collective-permute-done.21.refs_3_
  61.8 1.0 collective-permute-done.20.refs_2_
  62.9 3.3 %shard_map.78 = (bf16[2,8,2,128,256]{4,3,2,1,0:T(8,128)(2,1)S(1)}, bf16[2,8,2,128,256]{4,3,2,1,0:T(8,128)(2,1)S(1)}, bf16[4,256,256]{2,1,0:T(8,128)(2,1)S(1)}) custom-call(bf16[7,64,256]{2,1,0:T(8,128)(2,1)S(1)} %collective-permute-done.9.refs_0_, bf16[7,64,256]{2,1,0:T(8,128)(2,1)S(1)} %collective-permute-done.17.refs_1_, ...), custom_call_target="tpu_custom_call" | custom-call | flops 2684354560 | bytes 10485760 | tf_op jit(solution)/shard_map/pallas_call | solution.py:170
  66.2 4.1 %shard_map.79 = f32[4,32]{1,0:T(4,128)S(1)} custom-call(bf16[32,128,256]{2,1,0:T(8,128)(2,1)} %rot_mine.1, bf16[32,128,256]{2,1,0:T(8,128)(2,1)S(1)} %collective-permute-done.rot_theirs, bf16[4,256,256]{2,1,0:T(8,128)(2,1)S(1)} %get-tuple-element.67.inverses, bf16[2,8,2,128,256]{4,3,2,1,0:T(8,128)(2,1)S(1)} %get-tuple-element.68.refs_0_.refs_2_.refs_1_, ...), custom_call_target="tpu_custom_call" | custom-call | flops 402653184 | bytes 4718592 | tf_op jit(solution)/shard_map/pallas_call | solution.py:229
  70.4 9.4 %all_to_all.5 = f32[16,1,128]{2,1,0:T(1,128)S(1)} all-to-all(f32[16,1,128]{2,1,0:T(1,128)S(1)} %reshape.15), channel_id=1, replica_groups=mesh['walk'=2,'chol'=16] {'chol'}, dimensions={0} | all-to-all | bytes 16384 | tf_op jit(solution)/shard_map/all_to_all | solution.py:571
  80.3 0.7 reduce
  81.0 5.8 %copy-done.2 = bf16[32,128,2048]{2,1,0:T(8,128)(2,1)S(1)} copy-done((bf16[32,128,2048]{2,1,0:T(8,128)(2,1)S(1)}, bf16[32,128,2048]{2,1,0:T(8,128)(2,1)}, u32[]{:S(2)}) %copy-start.2) | copy-done | bytes 16777240
  86.8 3.2 %shard_map.80 = (f32[8,32]{1,0:T(8,128)}, bf16[4,128,2048]{2,1,0:T(8,128)(2,1)S(1)}, bf16[4,64,2048]{2,1,0:T(8,128)(2,1)S(1)}, bf16[4,64,2048]{2,1,0:T(8,128)(2,1)S(1)}) custom-call(s32[8]{0:T(128)S(1)} %get-tuple-element.47.order, f32[8,32]{1,0:T(8,128)S(1)} %copy-done.4, f32[16,4,32]{2,1,0:T(4,128)S(1)} %reshape.16.parts, bf16[32,128,2048]{2,1,0:T(8,128)(2,1)S(1)} %copy-done.2), custom_call_target="tpu_custom_call" | custom-call | tf_op jit(solution)/shard_map/pallas_call | solution.py:293
  90.6 0.8 shard_map.82
  92.7 1.5 %collective-permute-done.25.refs_1_ = bf16[4,64,2048]{2,1,0:T(8,128)(2,1)S(1)} collective-permute-done((bf16[4,64,2048]{2,1,0:T(8,128)(2,1)S(1)}, bf16[4,64,2048]{2,1,0:T(8,128)(2,1)S(1)}, u32[]{:S(2)}, u32[]{:S(2)}) %collective-permute-start.25) | collective-permute-done | bytes 1048608 | tf_op jit(solution)/shard_map/ppermute | solution.py:40
  94.2 0.8 shard_map.81
  96.1 4.4 %collective-permute-done.27.refs_4_ = bf16[4,128,256]{2,1,0:T(8,128)(2,1)S(1)} collective-permute-done((bf16[4,128,256]{2,1,0:T(8,128)(2,1)S(1)}, bf16[4,128,256]{2,1,0:T(8,128)(2,1)S(1)}, u32[]{:S(2)}, u32[]{:S(2)}) %collective-permute-start.27) | collective-permute-done | bytes 262176 | tf_op jit(solution)/shard_map/ppermute | solution.py:49
  101.1 0.9 collective-permute-start.29
  102.5 3.6 %collective-permute-done.35.refs_13_ = bf16[4,128,256]{2,1,0:T(8,128)(2,1)S(1)} collective-permute-done((bf16[4,128,256]{2,1,0:T(8,128)(2,1)S(1)}, bf16[4,128,256]{2,1,0:T(8,128)(2,1)S(1)}, u32[]{:S(2)}, u32[]{:S(2)}) %collective-permute-start.35) | collective-permute-done | bytes 262176 | tf_op jit(solution)/shard_map/ppermute | solution.py:49
  106.7 0.9 collective-permute-start.37
  108.2 3.6 %collective-permute-done.29.refs_5_ = bf16[4,128,256]{2,1,0:T(8,128)(2,1)S(1)} collective-permute-done((bf16[4,128,256]{2,1,0:T(8,128)(2,1)S(1)}, bf16[4,128,256]{2,1,0:T(8,128)(2,1)S(1)}, u32[]{:S(2)}, u32[]{:S(2)}) %collective-permute-start.29) | collective-permute-done | bytes 262176 | tf_op jit(solution)/shard_map/ppermute | solution.py:49
  112.3 0.9 collective-permute-start.31
  113.8 3.6 %collective-permute-done.37.refs_14_ = bf16[4,128,256]{2,1,0:T(8,128)(2,1)S(1)} collective-permute-done((bf16[4,128,256]{2,1,0:T(8,128)(2,1)S(1)}, bf16[4,128,256]{2,1,0:T(8,128)(2,1)S(1)}, u32[]{:S(2)}, u32[]{:S(2)}) %collective-permute-start.37) | collective-permute-done | bytes 262176 | tf_op jit(solution)/shard_map/ppermute | solution.py:49
  118.0 0.9 collective-permute-start.39
  119.4 3.6 %collective-permute-done.31.refs_6_ = bf16[4,128,256]{2,1,0:T(8,128)(2,1)S(1)} collective-permute-done((bf16[4,128,256]{2,1,0:T(8,128)(2,1)S(1)}, bf16[4,128,256]{2,1,0:T(8,128)(2,1)S(1)}, u32[]{:S(2)}, u32[]{:S(2)}) %collective-permute-start.31) | collective-permute-done | bytes 262176 | tf_op jit(solution)/shard_map/ppermute | solution.py:49
  123.6 1.0 collective-permute-start.33
  125.1 3.5 %collective-permute-done.39.refs_15_ = bf16[4,128,256]{2,1,0:T(8,128)(2,1)S(1)} collective-permute-done((bf16[4,128,256]{2,1,0:T(8,128)(2,1)S(1)}, bf16[4,128,256]{2,1,0:T(8,128)(2,1)S(1)}, u32[]{:S(2)}, u32[]{:S(2)}) %collective-permute-start.39) | collective-permute-done | bytes 262176 | tf_op jit(solution)/shard_map/ppermute | solution.py:49
  129.2 0.9 collective-permute-start.41
  130.7 0.7 collective-permute-done.33.refs_11_
  131.4 2.8 %collective-permute-done.41.refs_20_ = bf16[2,128,256]{2,1,0:T(8,128)(2,1)S(1)} collective-permute-done((bf16[2,128,256]{2,1,0:T(8,128)(2,1)S(1)}, bf16[2,128,256]{2,1,0:T(8,128)(2,1)S(1)}, u32[]{:S(2)}, u32[]{:S(2)}) %collective-permute-start.41) | collective-permute-done | bytes 131104 | tf_op jit(solution)/shard_map/ppermute | solution.py:49
  134.2 0.9 collective-permute-done.40.refs_19_
  135.1 1.1 shard_map.83
  136.3 2.0 %shard_map.84._ = bf16[8,128,256]{2,1,0:T(8,128)(2,1)} custom-call(s32[8]{0:T(128)S(1)} %get-tuple-element.47.order, bf16[4,128,2048]{2,1,0:T(8,128)(2,1)S(1)} %get-tuple-element.73.refs_0_.potential, f32[4,128,256]{2,1,0:T(8,128)S(1)} %get-tuple-element.89.base, bf16[4,8,2,128,256]{4,3,2,1,0:T(8,128)(2,1)S(1)} %get-tuple-element.90.full), custom_call_target="tpu_custom_call" | custom-call | flops 536870912 | bytes 6291456 | tf_op jit(solution)/shard_map/pallas_call | solution.py:398
  138.4 1.3 shard_map.85
  (81 shorter events, 13.2 us)
Async XLA Ops:
  0.6 1.0 copy-start.3
  1.7 0.7 copy-start.5
  2.3 15.4 %copy-start.6 = (bf16[128,256]{1,0:T(8,128)(2,1)S(1)}, bf16[128,256]{1,0:T(8,128)(2,1)}, u32[]{:S(2)}) copy-start(bf16[128,256]{1,0:T(8,128)(2,1)} %param.7) | copy-start | bytes 196612
  4.3 8.9 %collective-permute-start.1 = (bf16[2,128,256]{2,1,0:T(8,128)(2,1)S(1)}, bf16[2,128,256]{2,1,0:T(8,128)(2,1)S(1)}, u32[]{:S(2)}, u32[]{:S(2)}) collective-permute-start(bf16[2,128,256]{2,1,0:T(8,128)(2,1)S(1)} %get-tuple-element.48), channel_id=1, source_target_pairs={{0,16},{1,17},{2,18},{3,19},{4,20},{5,21},{6,22},{7,23},{8,24},{9,... | collective-permute-start | bytes 393224 | tf_op jit(solution)/shard_map/ppermute | solution.py:513
  7.4 5.9 %collective-permute-start.2 = (bf16[2,128,256]{2,1,0:T(8,128)(2,1)S(1)}, bf16[2,128,256]{2,1,0:T(8,128)(2,1)S(1)}, u32[]{:S(2)}, u32[]{:S(2)}) collective-permute-start(bf16[2,128,256]{2,1,0:T(8,128)(2,1)S(1)} %get-tuple-element.49), channel_id=1, source_target_pairs={{0,17},{1,16},{2,19},{3,18},{4,21},{5,20},{6,23},{7,22},{8,25},{9,... | collective-permute-start | bytes 393224 | tf_op jit(solution)/shard_map/ppermute | solution.py:514
  7.4 1.3 collective-permute-start.10
  8.8 10.3 %collective-permute-start.12 = (bf16[9,64,256]{2,1,0:T(8,128)(2,1)S(1)}, bf16[9,64,256]{2,1,0:T(8,128)(2,1)S(1)}, u32[]{:S(2)}, u32[]{:S(2)}) collective-permute-start(bf16[9,64,256]{2,1,0:T(8,128)(2,1)S(1)} %pad_maximum_fusion.1.refs_13_), channel_id=1, source_target_pairs={{0,8},{1,9},{2,10},{3,11},{4,0},{5,1},{6,2},{7,3},{8,12},{9,13},{1... | collective-permute-start | bytes 884744 | tf_op jit(solution)/shard_map/ppermute | solution.py:49
  11.7 9.9 %collective-permute-start.11 = (bf16[9,64,256]{2,1,0:T(8,128)(2,1)S(1)}, bf16[9,64,256]{2,1,0:T(8,128)(2,1)S(1)}, u32[]{:S(2)}, u32[]{:S(2)}) collective-permute-start(bf16[9,64,256]{2,1,0:T(8,128)(2,1)S(1)} %pad_maximum_fusion.1.refs_13_), channel_id=1, source_target_pairs={{0,2},{1,3},{2,0},{3,1},{4,6},{5,7},{6,4},{7,5},{8,10},{9,11},{10,... | collective-permute-start | bytes 884744 | tf_op jit(solution)/shard_map/ppermute | solution.py:40
  13.4 12.0 %collective-permute-start.4 = (bf16[9,64,256]{2,1,0:T(8,128)(2,1)S(1)}, bf16[9,64,256]{2,1,0:T(8,128)(2,1)S(1)}, u32[]{:S(2)}, u32[]{:S(2)}) collective-permute-start(bf16[9,64,256]{2,1,0:T(8,128)(2,1)S(1)} %pad_maximum_fusion.refs_4_), channel_id=1, source_target_pairs={{0,8},{1,9},{2,10},{3,11},{4,0},{5,1},{6,2},{7,3},{8,12},{9,13},{1... | collective-permute-start | bytes 884744 | tf_op jit(solution)/shard_map/ppermute | solution.py:49
  15.9 12.1 %collective-permute-start.3 = (bf16[9,64,256]{2,1,0:T(8,128)(2,1)S(1)}, bf16[9,64,256]{2,1,0:T(8,128)(2,1)S(1)}, u32[]{:S(2)}, u32[]{:S(2)}) collective-permute-start(bf16[9,64,256]{2,1,0:T(8,128)(2,1)S(1)} %pad_maximum_fusion.refs_4_), channel_id=1, source_target_pairs={{0,2},{1,3},{2,0},{3,1},{4,6},{5,7},{6,4},{7,5},{8,10},{9,11},{10,... | collective-permute-start | bytes 884744 | tf_op jit(solution)/shard_map/ppermute | solution.py:40
  17.4 48.8 %collective-permute-start = (bf16[32,128,256]{2,1,0:T(8,128)(2,1)}, bf16[32,128,256]{2,1,0:T(8,128)(2,1)S(1)}, u32[]{:S(2)}, u32[]{:S(2)}) collective-permute-start(bf16[32,128,256]{2,1,0:T(8,128)(2,1)} %rot_mine.1), channel_id=1, source_target_pairs={{0,1},{1,0},{2,3},{3,2},{4,5},{5,4},{6,7},{7,6},{8,9},{9,8},{10,11... | collective-permute-start | bytes 6291464 | tf_op jit(solution)/shard_map/ppermute | solution.py:40
  21.6 10.1 %collective-permute-start.14 = (bf16[9,64,256]{2,1,0:T(8,128)(2,1)S(1)}, bf16[9,64,256]{2,1,0:T(8,128)(2,1)S(1)}, u32[]{:S(2)}, u32[]{:S(2)}) collective-permute-start(bf16[9,64,256]{2,1,0:T(8,128)(2,1)S(1)} %collective-permute-done.12.refs_14_), channel_id=1, source_target_pairs={{0,8},{1,9},{2,10},{3,11},{4,0},{5,1},{6,2},{7,3},{8,12},{9,13},{1... | collective-permute-start | bytes 884744 | tf_op jit(solution)/shard_map/ppermute | solution.py:49
  23.2 11.1 %collective-permute-start.13 = (bf16[9,64,256]{2,1,0:T(8,128)(2,1)S(1)}, bf16[9,64,256]{2,1,0:T(8,128)(2,1)S(1)}, u32[]{:S(2)}, u32[]{:S(2)}) collective-permute-start(bf16[9,64,256]{2,1,0:T(8,128)(2,1)S(1)} %collective-permute-done.12.refs_14_), channel_id=1, source_target_pairs={{0,2},{1,3},{2,0},{3,1},{4,6},{5,7},{6,4},{7,5},{8,10},{9,11},{10,... | collective-permute-start | bytes 884744 | tf_op jit(solution)/shard_map/ppermute | solution.py:40
  27.9 10.1 %collective-permute-start.6 = (bf16[9,64,256]{2,1,0:T(8,128)(2,1)S(1)}, bf16[9,64,256]{2,1,0:T(8,128)(2,1)S(1)}, u32[]{:S(2)}, u32[]{:S(2)}) collective-permute-start(bf16[9,64,256]{2,1,0:T(8,128)(2,1)S(1)} %collective-permute-done.4.refs_5_), channel_id=1, source_target_pairs={{0,8},{1,9},{2,10},{3,11},{4,0},{5,1},{6,2},{7,3},{8,12},{9,13},{1... | collective-permute-start | bytes 884744 | tf_op jit(solution)/shard_map/ppermute | solution.py:49
  29.5 11.1 %collective-permute-start.5 = (bf16[9,64,256]{2,1,0:T(8,128)(2,1)S(1)}, bf16[9,64,256]{2,1,0:T(8,128)(2,1)S(1)}, u32[]{:S(2)}, u32[]{:S(2)}) collective-permute-start(bf16[9,64,256]{2,1,0:T(8,128)(2,1)S(1)} %collective-permute-done.4.refs_5_), channel_id=1, source_target_pairs={{0,2},{1,3},{2,0},{3,1},{4,6},{5,7},{6,4},{7,5},{8,10},{9,11},{10,... | collective-permute-start | bytes 884744 | tf_op jit(solution)/shard_map/ppermute | solution.py:40
  34.2 10.1 %collective-permute-start.16 = (bf16[9,64,256]{2,1,0:T(8,128)(2,1)S(1)}, bf16[9,64,256]{2,1,0:T(8,128)(2,1)S(1)}, u32[]{:S(2)}, u32[]{:S(2)}) collective-permute-start(bf16[9,64,256]{2,1,0:T(8,128)(2,1)S(1)} %collective-permute-done.14.refs_15_), channel_id=1, source_target_pairs={{0,8},{1,9},{2,10},{3,11},{4,0},{5,1},{6,2},{7,3},{8,12},{9,13},{1... | collective-permute-start | bytes 884744 | tf_op jit(solution)/shard_map/ppermute | solution.py:49
  35.8 11.1 %collective-permute-start.15 = (bf16[9,64,256]{2,1,0:T(8,128)(2,1)S(1)}, bf16[9,64,256]{2,1,0:T(8,128)(2,1)S(1)}, u32[]{:S(2)}, u32[]{:S(2)}) collective-permute-start(bf16[9,64,256]{2,1,0:T(8,128)(2,1)S(1)} %collective-permute-done.14.refs_15_), channel_id=1, source_target_pairs={{0,2},{1,3},{2,0},{3,1},{4,6},{5,7},{6,4},{7,5},{8,10},{9,11},{10,... | collective-permute-start | bytes 884744 | tf_op jit(solution)/shard_map/ppermute | solution.py:40
  40.6 10.1 %collective-permute-start.8 = (bf16[9,64,256]{2,1,0:T(8,128)(2,1)S(1)}, bf16[9,64,256]{2,1,0:T(8,128)(2,1)S(1)}, u32[]{:S(2)}, u32[]{:S(2)}) collective-permute-start(bf16[9,64,256]{2,1,0:T(8,128)(2,1)S(1)} %collective-permute-done.6.refs_6_), channel_id=1, source_target_pairs={{0,8},{1,9},{2,10},{3,11},{4,0},{5,1},{6,2},{7,3},{8,12},{9,13},{1... | collective-permute-start | bytes 884744 | tf_op jit(solution)/shard_map/ppermute | solution.py:49
  42.1 11.1 %collective-permute-start.7 = (bf16[9,64,256]{2,1,0:T(8,128)(2,1)S(1)}, bf16[9,64,256]{2,1,0:T(8,128)(2,1)S(1)}, u32[]{:S(2)}, u32[]{:S(2)}) collective-permute-start(bf16[9,64,256]{2,1,0:T(8,128)(2,1)S(1)} %collective-permute-done.6.refs_6_), channel_id=1, source_target_pairs={{0,2},{1,3},{2,0},{3,1},{4,6},{5,7},{6,4},{7,5},{8,10},{9,11},{10,... | collective-permute-start | bytes 884744 | tf_op jit(solution)/shard_map/ppermute | solution.py:40
  46.9 6.4 %collective-permute-start.19 = (bf16[4,64,256]{2,1,0:T(8,128)(2,1)S(1)}, bf16[4,64,256]{2,1,0:T(8,128)(2,1)S(1)}, u32[]{:S(2)}, u32[]{:S(2)}) collective-permute-start(bf16[4,64,256]{2,1,0:T(8,128)(2,1)S(1)} %slice.95), channel_id=1, source_target_pairs={{0,8},{1,9},{2,10},{3,11},{4,0},{5,1},{6,2},{7,3},{8,12},{9,13},{1... | collective-permute-start | bytes 393224 | tf_op jit(solution)/shard_map/ppermute | solution.py:49
  48.6 7.3 %collective-permute-start.18 = (bf16[5,64,256]{2,1,0:T(8,128)(2,1)S(1)}, bf16[5,64,256]{2,1,0:T(8,128)(2,1)S(1)}, u32[]{:S(2)}, u32[]{:S(2)}) collective-permute-start(bf16[5,64,256]{2,1,0:T(8,128)(2,1)S(1)} %slice.94), channel_id=1, source_target_pairs={{0,2},{1,3},{2,0},{3,1},{4,6},{5,7},{6,4},{7,5},{8,10},{9,11},{10,... | collective-permute-start | bytes 491528 | tf_op jit(solution)/shard_map/ppermute | solution.py:40
  50.7 7.2 %collective-permute-start.17 = (bf16[7,64,256]{2,1,0:T(8,128)(2,1)S(1)}, bf16[7,64,256]{2,1,0:T(8,128)(2,1)S(1)}, u32[]{:S(2)}, u32[]{:S(2)}) collective-permute-start(bf16[7,64,256]{2,1,0:T(8,128)(2,1)S(1)} %slice_dynamic-update-slice_fusion), channel_id=1, source_target_pairs={{0,1},{1,0},{2,3},{3,2},{4,5},{5,4},{6,7},{7,6},{8,9},{9,8},{10,11... | collective-permute-start | bytes 688136 | tf_op jit(solution)/shard_map/ppermute | solution.py:40
  53.2 5.7 %collective-permute-start.9 = (bf16[7,64,256]{2,1,0:T(8,128)(2,1)S(1)}, bf16[7,64,256]{2,1,0:T(8,128)(2,1)S(1)}, u32[]{:S(2)}, u32[]{:S(2)}) collective-permute-start(bf16[7,64,256]{2,1,0:T(8,128)(2,1)S(1)} %slice_dynamic-update-slice_fusion.6), channel_id=1, source_target_pairs={{0,1},{1,0},{2,3},{3,2},{4,5},{5,4},{6,7},{7,6},{8,9},{9,8},{10,11... | collective-permute-start | bytes 688136 | tf_op jit(solution)/shard_map/ppermute | solution.py:40
  53.3 7.5 %collective-permute-start.22 = (bf16[5,64,256]{2,1,0:T(8,128)(2,1)S(1)}, bf16[5,64,256]{2,1,0:T(8,128)(2,1)S(1)}, u32[]{:S(2)}, u32[]{:S(2)}) collective-permute-start(bf16[5,64,256]{2,1,0:T(8,128)(2,1)S(1)} %slice.98), channel_id=1, source_target_pairs={{0,2},{1,3},{2,0},{3,1},{4,6},{5,7},{6,4},{7,5},{8,10},{9,11},{10,... | collective-permute-start | bytes 491528 | tf_op jit(solution)/shard_map/ppermute | solution.py:40
  55.8 5.0 %collective-permute-start.23 = (bf16[4,64,256]{2,1,0:T(8,128)(2,1)S(1)}, bf16[4,64,256]{2,1,0:T(8,128)(2,1)S(1)}, u32[]{:S(2)}, u32[]{:S(2)}) collective-permute-start(bf16[4,64,256]{2,1,0:T(8,128)(2,1)S(1)} %slice.99), channel_id=1, source_target_pairs={{0,8},{1,9},{2,10},{3,11},{4,0},{5,1},{6,2},{7,3},{8,12},{9,13},{1... | collective-permute-start | bytes 393224 | tf_op jit(solution)/shard_map/ppermute | solution.py:49
  57.9 3.9 %collective-permute-start.21 = (bf16[1,64,256]{2,1,0:T(8,128)(2,1)S(1)}, bf16[1,64,256]{2,1,0:T(8,128)(2,1)S(1)}, u32[]{:S(2)}, u32[]{:S(2)}) collective-permute-start(bf16[1,64,256]{2,1,0:T(8,128)(2,1)S(1)} %slice.97), channel_id=1, source_target_pairs={{0,2},{1,3},{2,0},{3,1},{4,6},{5,7},{6,4},{7,5},{8,10},{9,11},{10,... | collective-permute-start | bytes 98312 | tf_op jit(solution)/shard_map/ppermute | solution.py:40
  58.9 3.9 %collective-permute-start.20 = (bf16[1,64,256]{2,1,0:T(8,128)(2,1)S(1)}, bf16[1,64,256]{2,1,0:T(8,128)(2,1)S(1)}, u32[]{:S(2)}, u32[]{:S(2)}) collective-permute-start(bf16[1,64,256]{2,1,0:T(8,128)(2,1)S(1)} %slice.104), channel_id=1, source_target_pairs={{0,2},{1,3},{2,0},{3,1},{4,6},{5,7},{6,4},{7,5},{8,10},{9,11},{10,... | collective-permute-start | bytes 98312 | tf_op jit(solution)/shard_map/ppermute | solution.py:40
  66.1 4.1 %copy-start = (bf16[2,8,2,128,256]{4,3,2,1,0:T(8,128)(2,1)}, bf16[2,8,2,128,256]{4,3,2,1,0:T(8,128)(2,1)S(1)}, u32[]{:S(2)}) copy-start(bf16[2,8,2,128,256]{4,3,2,1,0:T(8,128)(2,1)S(1)} %get-tuple-element.69.refs_1_.refs_3_.refs_2_) | copy-start | bytes 6291460
  66.2 14.9 %copy-start.4 = (f32[8,32]{1,0:T(8,128)S(1)}, f32[8,32]{1,0:T(8,128)}, u32[]{:S(2)}) copy-start(f32[8,32]{1,0:T(8,128)} %fields.1) | copy-start | bytes 3076
  81.0 5.8 %copy-start.2 = (bf16[32,128,2048]{2,1,0:T(8,128)(2,1)S(1)}, bf16[32,128,2048]{2,1,0:T(8,128)(2,1)}, u32[]{:S(2)}) copy-start(bf16[32,128,2048]{2,1,0:T(8,128)(2,1)} %cholesky.1) | copy-start | bytes 50331652
  86.8 3.8 %copy-start.1 = (bf16[2,8,2,128,256]{4,3,2,1,0:T(8,128)(2,1)S(1)}, bf16[2,8,2,128,256]{4,3,2,1,0:T(8,128)(2,1)}, u32[]{:S(2)}) copy-start(bf16[2,8,2,128,256]{4,3,2,1,0:T(8,128)(2,1)} %copy-done) | copy-start | bytes 6291460
  90.0 2.7 %collective-permute-start.24 = (bf16[4,64,2048]{2,1,0:T(8,128)(2,1)S(1)}, bf16[4,64,2048]{2,1,0:T(8,128)(2,1)S(1)}, u32[]{:S(2)}, u32[]{:S(2)}) collective-permute-start(bf16[4,64,2048]{2,1,0:T(8,128)(2,1)S(1)} %get-tuple-element.70), channel_id=1, source_target_pairs={{0,1},{1,0},{2,3},{3,2},{4,5},{5,4},{6,7},{7,6},{8,9},{9,8},{10,11... | collective-permute-start | bytes 3145736 | tf_op jit(solution)/shard_map/ppermute | solution.py:40
  90.1 4.1 %collective-permute-start.25 = (bf16[4,64,2048]{2,1,0:T(8,128)(2,1)S(1)}, bf16[4,64,2048]{2,1,0:T(8,128)(2,1)S(1)}, u32[]{:S(2)}, u32[]{:S(2)}) collective-permute-start(bf16[4,64,2048]{2,1,0:T(8,128)(2,1)S(1)} %get-tuple-element.71), channel_id=1, source_target_pairs={{0,1},{1,0},{2,3},{3,2},{4,5},{5,4},{6,7},{7,6},{8,9},{9,8},{10,11... | collective-permute-start | bytes 3145736 | tf_op jit(solution)/shard_map/ppermute | solution.py:40
  91.3 9.2 %collective-permute-start.27 = (bf16[4,128,256]{2,1,0:T(8,128)(2,1)S(1)}, bf16[4,128,256]{2,1,0:T(8,128)(2,1)S(1)}, u32[]{:S(2)}, u32[]{:S(2)}) collective-permute-start(bf16[4,128,256]{2,1,0:T(8,128)(2,1)S(1)} %get-tuple-element.74.refs_3_), channel_id=1, source_target_pairs={{0,8},{1,9},{2,10},{3,11},{4,0},{5,1},{6,2},{7,3},{8,12},{9,13},{1... | collective-permute-start | bytes 786440 | tf_op jit(solution)/shard_map/ppermute | solution.py:49
  91.9 9.2 %collective-permute-start.26 = (bf16[4,128,256]{2,1,0:T(8,128)(2,1)S(1)}, bf16[4,128,256]{2,1,0:T(8,128)(2,1)S(1)}, u32[]{:S(2)}, u32[]{:S(2)}) collective-permute-start(bf16[4,128,256]{2,1,0:T(8,128)(2,1)S(1)} %get-tuple-element.74.refs_3_), channel_id=1, source_target_pairs={{0,2},{1,3},{2,0},{3,1},{4,6},{5,7},{6,4},{7,5},{8,10},{9,11},{10,... | collective-permute-start | bytes 786440 | tf_op jit(solution)/shard_map/ppermute | solution.py:40
  95.0 11.2 %collective-permute-start.35 = (bf16[4,128,256]{2,1,0:T(8,128)(2,1)S(1)}, bf16[4,128,256]{2,1,0:T(8,128)(2,1)S(1)}, u32[]{:S(2)}, u32[]{:S(2)}) collective-permute-start(bf16[4,128,256]{2,1,0:T(8,128)(2,1)S(1)} %get-tuple-element.81.refs_12_), channel_id=1, source_target_pairs={{0,8},{1,9},{2,10},{3,11},{4,0},{5,1},{6,2},{7,3},{8,12},{9,13},{1... | collective-permute-start | bytes 786440 | tf_op jit(solution)/shard_map/ppermute | solution.py:49
  95.5 11.2 %collective-permute-start.34 = (bf16[4,128,256]{2,1,0:T(8,128)(2,1)S(1)}, bf16[4,128,256]{2,1,0:T(8,128)(2,1)S(1)}, u32[]{:S(2)}, u32[]{:S(2)}) collective-permute-start(bf16[4,128,256]{2,1,0:T(8,128)(2,1)S(1)} %get-tuple-element.81.refs_12_), channel_id=1, source_target_pairs={{0,2},{1,3},{2,0},{3,1},{4,6},{5,7},{6,4},{7,5},{8,10},{9,11},{10,... | collective-permute-start | bytes 786440 | tf_op jit(solution)/shard_map/ppermute | solution.py:40
  101.1 10.7 %collective-permute-start.29 = (bf16[4,128,256]{2,1,0:T(8,128)(2,1)S(1)}, bf16[4,128,256]{2,1,0:T(8,128)(2,1)S(1)}, u32[]{:S(2)}, u32[]{:S(2)}) collective-permute-start(bf16[4,128,256]{2,1,0:T(8,128)(2,1)S(1)} %collective-permute-done.27.refs_4_), channel_id=1, source_target_pairs={{0,8},{1,9},{2,10},{3,11},{4,0},{5,1},{6,2},{7,3},{8,12},{9,13},{1... | collective-permute-start | bytes 786440 | tf_op jit(solution)/shard_map/ppermute | solution.py:49
  102.0 10.4 %collective-permute-start.28 = (bf16[4,128,256]{2,1,0:T(8,128)(2,1)S(1)}, bf16[4,128,256]{2,1,0:T(8,128)(2,1)S(1)}, u32[]{:S(2)}, u32[]{:S(2)}) collective-permute-start(bf16[4,128,256]{2,1,0:T(8,128)(2,1)S(1)} %collective-permute-done.27.refs_4_), channel_id=1, source_target_pairs={{0,2},{1,3},{2,0},{3,1},{4,6},{5,7},{6,4},{7,5},{8,10},{9,11},{10,... | collective-permute-start | bytes 786440 | tf_op jit(solution)/shard_map/ppermute | solution.py:40
  106.7 10.7 %collective-permute-start.37 = (bf16[4,128,256]{2,1,0:T(8,128)(2,1)S(1)}, bf16[4,128,256]{2,1,0:T(8,128)(2,1)S(1)}, u32[]{:S(2)}, u32[]{:S(2)}) collective-permute-start(bf16[4,128,256]{2,1,0:T(8,128)(2,1)S(1)} %collective-permute-done.35.refs_13_), channel_id=1, source_target_pairs={{0,8},{1,9},{2,10},{3,11},{4,0},{5,1},{6,2},{7,3},{8,12},{9,13},{1... | collective-permute-start | bytes 786440 | tf_op jit(solution)/shard_map/ppermute | solution.py:49
  107.6 10.4 %collective-permute-start.36 = (bf16[4,128,256]{2,1,0:T(8,128)(2,1)S(1)}, bf16[4,128,256]{2,1,0:T(8,128)(2,1)S(1)}, u32[]{:S(2)}, u32[]{:S(2)}) collective-permute-start(bf16[4,128,256]{2,1,0:T(8,128)(2,1)S(1)} %collective-permute-done.35.refs_13_), channel_id=1, source_target_pairs={{0,2},{1,3},{2,0},{3,1},{4,6},{5,7},{6,4},{7,5},{8,10},{9,11},{10,... | collective-permute-start | bytes 786440 | tf_op jit(solution)/shard_map/ppermute | solution.py:40
  112.3 10.7 %collective-permute-start.31 = (bf16[4,128,256]{2,1,0:T(8,128)(2,1)S(1)}, bf16[4,128,256]{2,1,0:T(8,128)(2,1)S(1)}, u32[]{:S(2)}, u32[]{:S(2)}) collective-permute-start(bf16[4,128,256]{2,1,0:T(8,128)(2,1)S(1)} %collective-permute-done.29.refs_5_), channel_id=1, source_target_pairs={{0,8},{1,9},{2,10},{3,11},{4,0},{5,1},{6,2},{7,3},{8,12},{9,13},{1... | collective-permute-start | bytes 786440 | tf_op jit(solution)/shard_map/ppermute | solution.py:49
  113.3 10.3 %collective-permute-start.30 = (bf16[4,128,256]{2,1,0:T(8,128)(2,1)S(1)}, bf16[4,128,256]{2,1,0:T(8,128)(2,1)S(1)}, u32[]{:S(2)}, u32[]{:S(2)}) collective-permute-start(bf16[4,128,256]{2,1,0:T(8,128)(2,1)S(1)} %collective-permute-done.29.refs_5_), channel_id=1, source_target_pairs={{0,2},{1,3},{2,0},{3,1},{4,6},{5,7},{6,4},{7,5},{8,10},{9,11},{10,... | collective-permute-start | bytes 786440 | tf_op jit(solution)/shard_map/ppermute | solution.py:40
  118.0 10.7 %collective-permute-start.39 = (bf16[4,128,256]{2,1,0:T(8,128)(2,1)S(1)}, bf16[4,128,256]{2,1,0:T(8,128)(2,1)S(1)}, u32[]{:S(2)}, u32[]{:S(2)}) collective-permute-start(bf16[4,128,256]{2,1,0:T(8,128)(2,1)S(1)} %collective-permute-done.37.refs_14_), channel_id=1, source_target_pairs={{0,8},{1,9},{2,10},{3,11},{4,0},{5,1},{6,2},{7,3},{8,12},{9,13},{1... | collective-permute-start | bytes 786440 | tf_op jit(solution)/shard_map/ppermute | solution.py:49
  118.9 10.3 %collective-permute-start.38 = (bf16[4,128,256]{2,1,0:T(8,128)(2,1)S(1)}, bf16[4,128,256]{2,1,0:T(8,128)(2,1)S(1)}, u32[]{:S(2)}, u32[]{:S(2)}) collective-permute-start(bf16[4,128,256]{2,1,0:T(8,128)(2,1)S(1)} %collective-permute-done.37.refs_14_), channel_id=1, source_target_pairs={{0,2},{1,3},{2,0},{3,1},{4,6},{5,7},{6,4},{7,5},{8,10},{9,11},{10,... | collective-permute-start | bytes 786440 | tf_op jit(solution)/shard_map/ppermute | solution.py:40
  123.6 7.8 %collective-permute-start.33 = (bf16[2,128,256]{2,1,0:T(8,128)(2,1)S(1)}, bf16[2,128,256]{2,1,0:T(8,128)(2,1)S(1)}, u32[]{:S(2)}, u32[]{:S(2)}) collective-permute-start(bf16[2,128,256]{2,1,0:T(8,128)(2,1)S(1)} %slice.101), channel_id=1, source_target_pairs={{0,8},{1,9},{2,10},{3,11},{4,0},{5,1},{6,2},{7,3},{8,12},{9,13},{1... | collective-permute-start | bytes 393224 | tf_op jit(solution)/shard_map/ppermute | solution.py:49
  124.6 6.9 %collective-permute-start.32 = (bf16[2,128,256]{2,1,0:T(8,128)(2,1)S(1)}, bf16[2,128,256]{2,1,0:T(8,128)(2,1)S(1)}, u32[]{:S(2)}, u32[]{:S(2)}) collective-permute-start(bf16[2,128,256]{2,1,0:T(8,128)(2,1)S(1)} %slice.100), channel_id=1, source_target_pairs={{0,2},{1,3},{2,0},{3,1},{4,6},{5,7},{6,4},{7,5},{8,10},{9,11},{10,... | collective-permute-start | bytes 393224 | tf_op jit(solution)/shard_map/ppermute | solution.py:40
  129.2 5.0 %collective-permute-start.41 = (bf16[2,128,256]{2,1,0:T(8,128)(2,1)S(1)}, bf16[2,128,256]{2,1,0:T(8,128)(2,1)S(1)}, u32[]{:S(2)}, u32[]{:S(2)}) collective-permute-start(bf16[2,128,256]{2,1,0:T(8,128)(2,1)S(1)} %slice.103), channel_id=1, source_target_pairs={{0,8},{1,9},{2,10},{3,11},{4,0},{5,1},{6,2},{7,3},{8,12},{9,13},{1... | collective-permute-start | bytes 393224 | tf_op jit(solution)/shard_map/ppermute | solution.py:49
  130.1 5.0 %collective-permute-start.40 = (bf16[2,128,256]{2,1,0:T(8,128)(2,1)S(1)}, bf16[2,128,256]{2,1,0:T(8,128)(2,1)S(1)}, u32[]{:S(2)}, u32[]{:S(2)}) collective-permute-start(bf16[2,128,256]{2,1,0:T(8,128)(2,1)S(1)} %slice.102), channel_id=1, source_target_pairs={{0,2},{1,3},{2,0},{3,1},{4,6},{5,7},{6,4},{7,5},{8,10},{9,11},{10,... | collective-permute-start | bytes 393224 | tf_op jit(solution)/shard_map/ppermute | solution.py:40
  136.2 2.1 %collective-permute-start.42 = (bf16[4,128,256]{2,1,0:T(8,128)(2,1)S(1)}, bf16[4,128,256]{2,1,0:T(8,128)(2,1)S(1)}, u32[]{:S(2)}, u32[]{:S(2)}) collective-permute-start(bf16[4,128,256]{2,1,0:T(8,128)(2,1)S(1)} %get-tuple-element.88), channel_id=1, source_target_pairs={{0,1},{1,0},{2,3},{3,2},{4,5},{5,4},{6,7},{7,6},{8,9},{9,8},{10,11... | collective-permute-start | bytes 786440 | tf_op jit(solution)/shard_map/ppermute | solution.py:40

commit v13 on v12

--- a/solution.py
+++ b/solution.py
@@ -217,18 +217,23 @@
         lax.broadcasted_iota(jnp.int32, shape, 1) // BLOCK
         == lax.broadcasted_iota(jnp.int32, shape, 0)
     ).astype(F32)
-    out[...] = lax.dot_general(
+    bias = lax.dot_general(
         pick, summed, (((1,), (1,)), ((), ())), precision=HIGHEST, preferred_element_type=F32
     )
-
-
-def bias_of(fulls, inverses, rot_mine, rot_theirs):
+    out[...] = jnp.zeros_like(out)
+    for index in range(out.shape[0]):
+        out[index, : len(walkers), :vectors] = bias
+
+
+def bias_of(layout, fulls, inverses, rot_mine, rot_theirs):
     vectors, rows, electrons = rot_mine.shape
     counts = [full.shape[0] for full in fulls]
     total = sum(counts)
     return pl.pallas_call(
         functools.partial(bias_kernel, counts),
-        out_shape=jax.ShapeDtypeStruct((total, vectors), F32),
+        out_shape=jax.ShapeDtypeStruct(
+            (layout.chol, pl.cdiv(total, 8) * 8, pl.cdiv(vectors, 128) * 128), F32
+        ),
         in_specs=vmem_specs(3 + len(fulls)),
         out_specs=pl.BlockSpec(memory_space=pltpu.VMEM),
         scratch_shapes=[pltpu.VMEM((2, rows // BLOCK, total, BLOCK, electrons), BF16)],
@@ -254,7 +259,7 @@
             total = total + parts[index]
         for walker in range(half):
             slot = order[core * half + walker]
-            bias += jnp.where(row == slot, total[walker : walker + 1, :], 0.0)
+            bias += jnp.where(row == slot, total[walker : walker + 1, :vectors], 0.0)
     bias = TAU_ROOT * bias
     bias_out[...] = bias
     shifted = (fields[...] - bias).astype(BF16)
@@ -567,10 +572,8 @@
         early.append(received)
         late.append(layout.shift(received[layout.z - 1 : layout.z], dy=1))
     *fulls, inverses = inverses_of(layout, streams, sizes, early, late)
-    total = bias_of(fulls, inverses, rotated, rot_theirs)
-    parts = lax.all_to_all(
-        jnp.broadcast_to(total, (layout.chol, *total.shape)), "chol", 0, 0, tiled=True
-    )
+    parts = bias_of(layout, fulls, inverses, rotated, rot_theirs)
+    parts = lax.all_to_all(parts, "chol", 0, 0, tiled=True)
     force_bias, kept, *sent = potential_of(order, fields, parts, cholesky)
     received = [layout.shift(part, db=1) for part in sent]
 

time: 140 us -> 131 us (0.936)
  local copies, waits for them, and re-layouts: 9.1 us -> 2.77 us
  Pallas kernels: 18.5 us -> 16.1 us
    unnamed x27 -> x23, local copies, waits for them, and re-layouts: 7.68 us -> 1.89 us
    pallas_call x1, Pallas kernels: 4.07 us -> 1.72 us  [bias_of(): pl.pallas_call(functools.partial(bias_kernel, counts), out_shape=jax.Shap...]
    ppermute x25, waiting for transfers between devices: 24.4 us -> 22.7 us  [shift(): return lax.ppermute(array, 'chol', pairs)]
where the time goes in v13:
time: 131 us; the launch traced here: 130 us
  waiting for transfers between devices  55.3 us (42%)
  starting transfers between devices  45.3 us (35%)
  Pallas kernels  16.1 us (12%)
  blocking collectives  9.88 us (8%)
  local copies, waits for them, and re-layouts  2.77 us (2%)
    ppermute x16, waiting for transfers between devices, step(): return lax.ppermute(array, 'chol', pairs)  32.7 us
    ppermute x25, waiting for transfers between devices, shift(): return lax.ppermute(array, 'chol', pairs)  22.7 us
    ppermute x16, starting transfers between devices, step(): return lax.ppermute(array, 'chol', pairs)  21.6 us
    ppermute x25, starting transfers between devices, shift(): return lax.ppermute(array, 'chol', pairs)  20.7 us
    all_to_all x1, blocking collectives, shards(): parts = lax.all_to_all(parts, 'chol', 0, 0, tiled=True)  9.88 us
    pallas_call x1, Pallas kernels, inverses_of(): pl.pallas_call(functools.partial(inverse_kernel, layout, slabs, counts),...  3.32 us
    pallas_call x1, Pallas kernels, potential_of(): pl.pallas_call(potential_kernel, out_shape=[jax.ShapeDtypeStruct((per_gro...  3.17 us
    ppermute x1, starting transfers between devices, migrate(): near = lax.ppermute(near, axes, list(enumerate(across)))  3 us
  transfers between devices with their start and end apart: 43, of which 34 were waited for; matrix products, arithmetic and copies ran while one was open for 1% of the time, Pallas kernels for 5%

profile of v13, /device:TPU:0, one launch (start us, length us, event | category | flops | bytes accessed | tf_op | source)
XLA Modules:
  0.0 130.4 jit_solution(6374693365966861377)
XLA Ops:
  0.6 1.2 copy-done.2
  1.8 0.7 copy-done.4
  2.5 2.0 %shard_map.77 = (bf16[2,128,256]{2,1,0:T(8,128)(2,1)S(1)}, bf16[2,128,256]{2,1,0:T(8,128)(2,1)S(1)}, bf16[2,128,256]{2,1,0:T(8,128)(2,1)S(1)}, bf16[2,128,256]{2,1,0:T(8,128)(2,1)S(1)}, s32[8]{0:T(128)S(1)}) custom-call(s32[16]{0:T(128)S(1)} %copy-done.4, bf16[8,128,256]{2,1,0:T(8,128)(2,1)S(1)} %copy-done.2), custom_call_target="tpu_custom_call" | custom-call | tf_op jit(solution)/shard_map/pallas_call | solution.py:489
  4.5 3.0 %collective-permute-start.1 = (bf16[2,128,256]{2,1,0:T(8,128)(2,1)S(1)}, bf16[2,128,256]{2,1,0:T(8,128)(2,1)S(1)}, u32[]{:S(2)}, u32[]{:S(2)}) collective-permute-start(bf16[2,128,256]{2,1,0:T(8,128)(2,1)S(1)} %get-tuple-element.48), channel_id=1, source_target_pairs={{0,16},{1,17},{2,18},{3,19},{4,20},{5,21},{6,22},{7,23},{8,24},{9,... | collective-permute-start | bytes 393224 | tf_op jit(solution)/shard_map/ppermute | solution.py:518
  7.7 0.8 slice_bitcast_fusion
  9.0 2.9 %collective-permute-start.12 = (bf16[9,64,256]{2,1,0:T(8,128)(2,1)S(1)}, bf16[9,64,256]{2,1,0:T(8,128)(2,1)S(1)}, u32[]{:S(2)}, u32[]{:S(2)}) collective-permute-start(bf16[9,64,256]{2,1,0:T(8,128)(2,1)S(1)} %pad_maximum_fusion.1.refs_13_), channel_id=1, source_target_pairs={{0,8},{1,9},{2,10},{3,11},{4,0},{5,1},{6,2},{7,3},{8,12},{9,13},{1... | collective-permute-start | bytes 884744 | tf_op jit(solution)/shard_map/ppermute | solution.py:49
  11.9 1.5 %collective-permute-start.11 = (bf16[9,64,256]{2,1,0:T(8,128)(2,1)S(1)}, bf16[9,64,256]{2,1,0:T(8,128)(2,1)S(1)}, u32[]{:S(2)}, u32[]{:S(2)}) collective-permute-start(bf16[9,64,256]{2,1,0:T(8,128)(2,1)S(1)} %pad_maximum_fusion.1.refs_13_), channel_id=1, source_target_pairs={{0,2},{1,3},{2,0},{3,1},{4,6},{5,7},{6,4},{7,5},{8,10},{9,11},{10,... | collective-permute-start | bytes 884744 | tf_op jit(solution)/shard_map/ppermute | solution.py:40
  13.5 2.5 %collective-permute-start.4 = (bf16[9,64,256]{2,1,0:T(8,128)(2,1)S(1)}, bf16[9,64,256]{2,1,0:T(8,128)(2,1)S(1)}, u32[]{:S(2)}, u32[]{:S(2)}) collective-permute-start(bf16[9,64,256]{2,1,0:T(8,128)(2,1)S(1)} %pad_maximum_fusion.refs_4_), channel_id=1, source_target_pairs={{0,8},{1,9},{2,10},{3,11},{4,0},{5,1},{6,2},{7,3},{8,12},{9,13},{1... | collective-permute-start | bytes 884744 | tf_op jit(solution)/shard_map/ppermute | solution.py:49
  16.0 1.5 %collective-permute-start.3 = (bf16[9,64,256]{2,1,0:T(8,128)(2,1)S(1)}, bf16[9,64,256]{2,1,0:T(8,128)(2,1)S(1)}, u32[]{:S(2)}, u32[]{:S(2)}) collective-permute-start(bf16[9,64,256]{2,1,0:T(8,128)(2,1)S(1)} %pad_maximum_fusion.refs_4_), channel_id=1, source_target_pairs={{0,2},{1,3},{2,0},{3,1},{4,6},{5,7},{6,4},{7,5},{8,10},{9,11},{10,... | collective-permute-start | bytes 884744 | tf_op jit(solution)/shard_map/ppermute | solution.py:40
  17.9 1.4 %collective-permute-done.12.refs_14_ = bf16[9,64,256]{2,1,0:T(8,128)(2,1)S(1)} collective-permute-done((bf16[9,64,256]{2,1,0:T(8,128)(2,1)S(1)}, bf16[9,64,256]{2,1,0:T(8,128)(2,1)S(1)}, u32[]{:S(2)}, u32[]{:S(2)}) %collective-permute-start.12) | collective-permute-done | bytes 294944 | tf_op jit(solution)/shard_map/ppermute | solution.py:49
  19.3 2.5 %collective-permute-done.11.refs_17_ = bf16[9,64,256]{2,1,0:T(8,128)(2,1)S(1)} collective-permute-done((bf16[9,64,256]{2,1,0:T(8,128)(2,1)S(1)}, bf16[9,64,256]{2,1,0:T(8,128)(2,1)S(1)}, u32[]{:S(2)}, u32[]{:S(2)}) %collective-permute-start.11) | collective-permute-done | bytes 294944 | tf_op jit(solution)/shard_map/ppermute | solution.py:40
  21.8 1.6 %collective-permute-start.14 = (bf16[9,64,256]{2,1,0:T(8,128)(2,1)S(1)}, bf16[9,64,256]{2,1,0:T(8,128)(2,1)S(1)}, u32[]{:S(2)}, u32[]{:S(2)}) collective-permute-start(bf16[9,64,256]{2,1,0:T(8,128)(2,1)S(1)} %collective-permute-done.12.refs_14_), channel_id=1, source_target_pairs={{0,8},{1,9},{2,10},{3,11},{4,0},{5,1},{6,2},{7,3},{8,12},{9,13},{1... | collective-permute-start | bytes 884744 | tf_op jit(solution)/shard_map/ppermute | solution.py:49
  23.3 1.5 %collective-permute-start.13 = (bf16[9,64,256]{2,1,0:T(8,128)(2,1)S(1)}, bf16[9,64,256]{2,1,0:T(8,128)(2,1)S(1)}, u32[]{:S(2)}, u32[]{:S(2)}) collective-permute-start(bf16[9,64,256]{2,1,0:T(8,128)(2,1)S(1)} %collective-permute-done.12.refs_14_), channel_id=1, source_target_pairs={{0,2},{1,3},{2,0},{3,1},{4,6},{5,7},{6,4},{7,5},{8,10},{9,11},{10,... | collective-permute-start | bytes 884744 | tf_op jit(solution)/shard_map/ppermute | solution.py:40
  24.9 0.7 collective-permute-done.4.refs_5_
  25.6 2.5 %collective-permute-done.3.refs_8_ = bf16[9,64,256]{2,1,0:T(8,128)(2,1)S(1)} collective-permute-done((bf16[9,64,256]{2,1,0:T(8,128)(2,1)S(1)}, bf16[9,64,256]{2,1,0:T(8,128)(2,1)S(1)}, u32[]{:S(2)}, u32[]{:S(2)}) %collective-permute-start.3) | collective-permute-done | bytes 294944 | tf_op jit(solution)/shard_map/ppermute | solution.py:40
  28.1 1.6 %collective-permute-start.6 = (bf16[9,64,256]{2,1,0:T(8,128)(2,1)S(1)}, bf16[9,64,256]{2,1,0:T(8,128)(2,1)S(1)}, u32[]{:S(2)}, u32[]{:S(2)}) collective-permute-start(bf16[9,64,256]{2,1,0:T(8,128)(2,1)S(1)} %collective-permute-done.4.refs_5_), channel_id=1, source_target_pairs={{0,8},{1,9},{2,10},{3,11},{4,0},{5,1},{6,2},{7,3},{8,12},{9,13},{1... | collective-permute-start | bytes 884744 | tf_op jit(solution)/shard_map/ppermute | solution.py:49
  29.7 1.5 %collective-permute-start.5 = (bf16[9,64,256]{2,1,0:T(8,128)(2,1)S(1)}, bf16[9,64,256]{2,1,0:T(8,128)(2,1)S(1)}, u32[]{:S(2)}, u32[]{:S(2)}) collective-permute-start(bf16[9,64,256]{2,1,0:T(8,128)(2,1)S(1)} %collective-permute-done.4.refs_5_), channel_id=1, source_target_pairs={{0,2},{1,3},{2,0},{3,1},{4,6},{5,7},{6,4},{7,5},{8,10},{9,11},{10,... | collective-permute-start | bytes 884744 | tf_op jit(solution)/shard_map/ppermute | solution.py:40
  31.2 0.7 collective-permute-done.14.refs_15_
  31.9 2.5 %collective-permute-done.13.refs_18_ = bf16[9,64,256]{2,1,0:T(8,128)(2,1)S(1)} collective-permute-done((bf16[9,64,256]{2,1,0:T(8,128)(2,1)S(1)}, bf16[9,64,256]{2,1,0:T(8,128)(2,1)S(1)}, u32[]{:S(2)}, u32[]{:S(2)}) %collective-permute-start.13) | collective-permute-done | bytes 294944 | tf_op jit(solution)/shard_map/ppermute | solution.py:40
  34.4 1.6 %collective-permute-start.16 = (bf16[9,64,256]{2,1,0:T(8,128)(2,1)S(1)}, bf16[9,64,256]{2,1,0:T(8,128)(2,1)S(1)}, u32[]{:S(2)}, u32[]{:S(2)}) collective-permute-start(bf16[9,64,256]{2,1,0:T(8,128)(2,1)S(1)} %collective-permute-done.14.refs_15_), channel_id=1, source_target_pairs={{0,8},{1,9},{2,10},{3,11},{4,0},{5,1},{6,2},{7,3},{8,12},{9,13},{1... | collective-permute-start | bytes 884744 | tf_op jit(solution)/shard_map/ppermute | solution.py:49
  36.0 1.5 %collective-permute-start.15 = (bf16[9,64,256]{2,1,0:T(8,128)(2,1)S(1)}, bf16[9,64,256]{2,1,0:T(8,128)(2,1)S(1)}, u32[]{:S(2)}, u32[]{:S(2)}) collective-permute-start(bf16[9,64,256]{2,1,0:T(8,128)(2,1)S(1)} %collective-permute-done.14.refs_15_), channel_id=1, source_target_pairs={{0,2},{1,3},{2,0},{3,1},{4,6},{5,7},{6,4},{7,5},{8,10},{9,11},{10,... | collective-permute-start | bytes 884744 | tf_op jit(solution)/shard_map/ppermute | solution.py:40
  37.5 0.7 collective-permute-done.6.refs_6_
  38.2 2.5 %collective-permute-done.5.refs_9_ = bf16[9,64,256]{2,1,0:T(8,128)(2,1)S(1)} collective-permute-done((bf16[9,64,256]{2,1,0:T(8,128)(2,1)S(1)}, bf16[9,64,256]{2,1,0:T(8,128)(2,1)S(1)}, u32[]{:S(2)}, u32[]{:S(2)}) %collective-permute-start.5) | collective-permute-done | bytes 294944 | tf_op jit(solution)/shard_map/ppermute | solution.py:40
  40.7 1.6 %collective-permute-start.8 = (bf16[9,64,256]{2,1,0:T(8,128)(2,1)S(1)}, bf16[9,64,256]{2,1,0:T(8,128)(2,1)S(1)}, u32[]{:S(2)}, u32[]{:S(2)}) collective-permute-start(bf16[9,64,256]{2,1,0:T(8,128)(2,1)S(1)} %collective-permute-done.6.refs_6_), channel_id=1, source_target_pairs={{0,8},{1,9},{2,10},{3,11},{4,0},{5,1},{6,2},{7,3},{8,12},{9,13},{1... | collective-permute-start | bytes 884744 | tf_op jit(solution)/shard_map/ppermute | solution.py:49
  42.3 1.5 %collective-permute-start.7 = (bf16[9,64,256]{2,1,0:T(8,128)(2,1)S(1)}, bf16[9,64,256]{2,1,0:T(8,128)(2,1)S(1)}, u32[]{:S(2)}, u32[]{:S(2)}) collective-permute-start(bf16[9,64,256]{2,1,0:T(8,128)(2,1)S(1)} %collective-permute-done.6.refs_6_), channel_id=1, source_target_pairs={{0,2},{1,3},{2,0},{3,1},{4,6},{5,7},{6,4},{7,5},{8,10},{9,11},{10,... | collective-permute-start | bytes 884744 | tf_op jit(solution)/shard_map/ppermute | solution.py:40
  43.8 0.7 collective-permute-done.16.refs_16_
  44.5 2.5 %collective-permute-done.15.refs_19_ = bf16[9,64,256]{2,1,0:T(8,128)(2,1)S(1)} collective-permute-done((bf16[9,64,256]{2,1,0:T(8,128)(2,1)S(1)}, bf16[9,64,256]{2,1,0:T(8,128)(2,1)S(1)}, u32[]{:S(2)}, u32[]{:S(2)}) %collective-permute-start.15) | collective-permute-done | bytes 294944 | tf_op jit(solution)/shard_map/ppermute | solution.py:40
  47.1 1.6 %collective-permute-start.19 = (bf16[4,64,256]{2,1,0:T(8,128)(2,1)S(1)}, bf16[4,64,256]{2,1,0:T(8,128)(2,1)S(1)}, u32[]{:S(2)}, u32[]{:S(2)}) collective-permute-start(bf16[4,64,256]{2,1,0:T(8,128)(2,1)S(1)} %slice.95), channel_id=1, source_target_pairs={{0,8},{1,9},{2,10},{3,11},{4,0},{5,1},{6,2},{7,3},{8,12},{9,13},{1... | collective-permute-start | bytes 393224 | tf_op jit(solution)/shard_map/ppermute | solution.py:49
  48.7 1.5 %collective-permute-start.18 = (bf16[5,64,256]{2,1,0:T(8,128)(2,1)S(1)}, bf16[5,64,256]{2,1,0:T(8,128)(2,1)S(1)}, u32[]{:S(2)}, u32[]{:S(2)}) collective-permute-start(bf16[5,64,256]{2,1,0:T(8,128)(2,1)S(1)} %slice.94), channel_id=1, source_target_pairs={{0,2},{1,3},{2,0},{3,1},{4,6},{5,7},{6,4},{7,5},{8,10},{9,11},{10,... | collective-permute-start | bytes 491528 | tf_op jit(solution)/shard_map/ppermute | solution.py:40
  50.9 2.5 %collective-permute-done.7.refs_10_ = bf16[9,64,256]{2,1,0:T(8,128)(2,1)S(1)} collective-permute-done((bf16[9,64,256]{2,1,0:T(8,128)(2,1)S(1)}, bf16[9,64,256]{2,1,0:T(8,128)(2,1)S(1)}, u32[]{:S(2)}, u32[]{:S(2)}) %collective-permute-start.7) | collective-permute-done | bytes 294944 | tf_op jit(solution)/shard_map/ppermute | solution.py:40
  53.5 1.6 %collective-permute-start.22 = (bf16[5,64,256]{2,1,0:T(8,128)(2,1)S(1)}, bf16[5,64,256]{2,1,0:T(8,128)(2,1)S(1)}, u32[]{:S(2)}, u32[]{:S(2)}) collective-permute-start(bf16[5,64,256]{2,1,0:T(8,128)(2,1)S(1)} %slice.98), channel_id=1, source_target_pairs={{0,2},{1,3},{2,0},{3,1},{4,6},{5,7},{6,4},{7,5},{8,10},{9,11},{10,... | collective-permute-start | bytes 491528 | tf_op jit(solution)/shard_map/ppermute | solution.py:40
  55.1 0.9 collective-permute-done.18.refs_20_
  56.0 2.1 %collective-permute-start.23 = (bf16[4,64,256]{2,1,0:T(8,128)(2,1)S(1)}, bf16[4,64,256]{2,1,0:T(8,128)(2,1)S(1)}, u32[]{:S(2)}, u32[]{:S(2)}) collective-permute-start(bf16[4,64,256]{2,1,0:T(8,128)(2,1)S(1)} %slice.99), channel_id=1, source_target_pairs={{0,8},{1,9},{2,10},{3,11},{4,0},{5,1},{6,2},{7,3},{8,12},{9,13},{1... | collective-permute-start | bytes 393224 | tf_op jit(solution)/shard_map/ppermute | solution.py:49
  58.1 1.0 collective-permute-start.21
  59.1 1.0 collective-permute-start.20
  60.1 0.9 collective-permute-done.23.refs_12_
  61.0 1.0 collective-permute-done.21.refs_3_
  62.0 1.0 collective-permute-done.20.refs_2_
  63.0 3.3 %shard_map.78 = (bf16[2,8,2,128,256]{4,3,2,1,0:T(8,128)(2,1)S(1)}, bf16[2,8,2,128,256]{4,3,2,1,0:T(8,128)(2,1)S(1)}, bf16[4,256,256]{2,1,0:T(8,128)(2,1)S(1)}) custom-call(bf16[7,64,256]{2,1,0:T(8,128)(2,1)S(1)} %collective-permute-done.9.refs_0_, bf16[7,64,256]{2,1,0:T(8,128)(2,1)S(1)} %collective-permute-done.17.refs_1_, ...), custom_call_target="tpu_custom_call" | custom-call | flops 2684354560 | bytes 10485760 | tf_op jit(solution)/shard_map/pallas_call | solution.py:170
  66.4 1.7 %shard_map.79 = f32[16,8,128]{2,1,0:T(8,128)S(1)} custom-call(bf16[32,128,256]{2,1,0:T(8,128)(2,1)S(1)} %copy-done.1, bf16[32,128,256]{2,1,0:T(8,128)(2,1)S(1)} %collective-permute-done.rot_theirs, bf16[4,256,256]{2,1,0:T(8,128)(2,1)S(1)} %get-tuple-element.67.inverses, bf16[2,8,2,128,256]{4,3,2,1,0:T(8,128)(2,1)S(1)} %get-tuple-element.68.refs_0_.refs_2_.refs_1_, ...), custom_call_target="tpu_custom_call" | custom-call | flops 402653184 | bytes 4718592 | tf_op jit(solution)/shard_map/pallas_call | solution.py:232
  68.1 9.9 %all_to_all.5.parts = f32[16,8,128]{2,1,0:T(8,128)S(1)} all-to-all(f32[16,8,128]{2,1,0:T(8,128)S(1)} %shard_map.79), channel_id=1, replica_groups=mesh['walk'=2,'chol'=16] {'chol'}, dimensions={0} | all-to-all | bytes 131072 | tf_op jit(solution)/shard_map/all_to_all | solution.py:576
  78.0 3.2 %shard_map.80 = (f32[8,32]{1,0:T(8,128)}, bf16[4,128,2048]{2,1,0:T(8,128)(2,1)S(1)}, bf16[4,64,2048]{2,1,0:T(8,128)(2,1)S(1)}, bf16[4,64,2048]{2,1,0:T(8,128)(2,1)S(1)}) custom-call(s32[8]{0:T(128)S(1)} %get-tuple-element.47.order, f32[8,32]{1,0:T(8,128)S(1)} %copy-done.3, f32[16,8,128]{2,1,0:T(8,128)S(1)} %all_to_all.5.parts, bf16[32,128,2048]{2,1,0:T(8,128)(2,1)S(1)} %copy-done), custom_call_target="tpu_custom_call" | custom-call | tf_op jit(solution)/shard_map/pallas_call | solution.py:298
  81.7 0.8 shard_map.82
  82.8 0.7 collective-permute-start.26
  83.9 1.5 %collective-permute-done.25.refs_1_ = bf16[4,64,2048]{2,1,0:T(8,128)(2,1)S(1)} collective-permute-done((bf16[4,64,2048]{2,1,0:T(8,128)(2,1)S(1)}, bf16[4,64,2048]{2,1,0:T(8,128)(2,1)S(1)}, u32[]{:S(2)}, u32[]{:S(2)}) %collective-permute-start.25) | collective-permute-done | bytes 1048608 | tf_op jit(solution)/shard_map/ppermute | solution.py:40
  85.4 0.8 shard_map.81
  87.1 4.6 %collective-permute-done.27.refs_4_ = bf16[4,128,256]{2,1,0:T(8,128)(2,1)S(1)} collective-permute-done((bf16[4,128,256]{2,1,0:T(8,128)(2,1)S(1)}, bf16[4,128,256]{2,1,0:T(8,128)(2,1)S(1)}, u32[]{:S(2)}, u32[]{:S(2)}) %collective-permute-start.27) | collective-permute-done | bytes 262176 | tf_op jit(solution)/shard_map/ppermute | solution.py:49
  92.0 0.9 collective-permute-start.29
  93.6 3.8 %collective-permute-done.35.refs_13_ = bf16[4,128,256]{2,1,0:T(8,128)(2,1)S(1)} collective-permute-done((bf16[4,128,256]{2,1,0:T(8,128)(2,1)S(1)}, bf16[4,128,256]{2,1,0:T(8,128)(2,1)S(1)}, u32[]{:S(2)}, u32[]{:S(2)}) %collective-permute-start.35) | collective-permute-done | bytes 262176 | tf_op jit(solution)/shard_map/ppermute | solution.py:49
  97.6 0.9 collective-permute-start.37
  99.2 3.8 %collective-permute-done.29.refs_5_ = bf16[4,128,256]{2,1,0:T(8,128)(2,1)S(1)} collective-permute-done((bf16[4,128,256]{2,1,0:T(8,128)(2,1)S(1)}, bf16[4,128,256]{2,1,0:T(8,128)(2,1)S(1)}, u32[]{:S(2)}, u32[]{:S(2)}) %collective-permute-start.29) | collective-permute-done | bytes 262176 | tf_op jit(solution)/shard_map/ppermute | solution.py:49
  103.2 0.9 collective-permute-start.31
  104.8 3.8 %collective-permute-done.37.refs_14_ = bf16[4,128,256]{2,1,0:T(8,128)(2,1)S(1)} collective-permute-done((bf16[4,128,256]{2,1,0:T(8,128)(2,1)S(1)}, bf16[4,128,256]{2,1,0:T(8,128)(2,1)S(1)}, u32[]{:S(2)}, u32[]{:S(2)}) %collective-permute-start.37) | collective-permute-done | bytes 262176 | tf_op jit(solution)/shard_map/ppermute | solution.py:49
  108.9 0.9 collective-permute-start.39
  110.4 3.8 %collective-permute-done.31.refs_6_ = bf16[4,128,256]{2,1,0:T(8,128)(2,1)S(1)} collective-permute-done((bf16[4,128,256]{2,1,0:T(8,128)(2,1)S(1)}, bf16[4,128,256]{2,1,0:T(8,128)(2,1)S(1)}, u32[]{:S(2)}, u32[]{:S(2)}) %collective-permute-start.31) | collective-permute-done | bytes 262176 | tf_op jit(solution)/shard_map/ppermute | solution.py:49
  114.5 1.0 collective-permute-start.33
  116.1 3.7 %collective-permute-done.39.refs_15_ = bf16[4,128,256]{2,1,0:T(8,128)(2,1)S(1)} collective-permute-done((bf16[4,128,256]{2,1,0:T(8,128)(2,1)S(1)}, bf16[4,128,256]{2,1,0:T(8,128)(2,1)S(1)}, u32[]{:S(2)}, u32[]{:S(2)}) %collective-permute-start.39) | collective-permute-done | bytes 262176 | tf_op jit(solution)/shard_map/ppermute | solution.py:49
  120.1 1.0 collective-permute-start.41
  121.7 0.9 collective-permute-done.33.refs_11_
  122.7 2.5 %collective-permute-done.41.refs_20_ = bf16[2,128,256]{2,1,0:T(8,128)(2,1)S(1)} collective-permute-done((bf16[2,128,256]{2,1,0:T(8,128)(2,1)S(1)}, bf16[2,128,256]{2,1,0:T(8,128)(2,1)S(1)}, u32[]{:S(2)}, u32[]{:S(2)}) %collective-permute-start.41) | collective-permute-done | bytes 131104 | tf_op jit(solution)/shard_map/ppermute | solution.py:49
  125.1 0.9 collective-permute-done.40.refs_19_
  126.1 1.0 shard_map.83
  127.2 1.9 %shard_map.84._ = bf16[8,128,256]{2,1,0:T(8,128)(2,1)} custom-call(s32[8]{0:T(128)S(1)} %get-tuple-element.47.order, bf16[4,128,2048]{2,1,0:T(8,128)(2,1)S(1)} %get-tuple-element.73.refs_0_.potential, f32[4,128,256]{2,1,0:T(8,128)S(1)} %get-tuple-element.89.base, bf16[4,8,2,128,256]{4,3,2,1,0:T(8,128)(2,1)S(1)} %get-tuple-element.90.full), custom_call_target="tpu_custom_call" | custom-call | flops 536870912 | bytes 6291456 | tf_op jit(solution)/shard_map/pallas_call | solution.py:403
  129.1 1.3 shard_map.85
  (74 shorter events, 9.5 us)
Async XLA Ops:
  0.6 16.9 %copy-start.1 = (bf16[32,128,256]{2,1,0:T(8,128)(2,1)S(1)}, bf16[32,128,256]{2,1,0:T(8,128)(2,1)}, u32[]{:S(2)}) copy-start(bf16[32,128,256]{2,1,0:T(8,128)(2,1)} %rot_mine.1) | copy-start | bytes 6291460
  0.6 1.2 copy-start.2
  1.8 0.7 copy-start.4
  2.5 15.4 %copy-start.5 = (bf16[128,256]{1,0:T(8,128)(2,1)S(1)}, bf16[128,256]{1,0:T(8,128)(2,1)}, u32[]{:S(2)}) copy-start(bf16[128,256]{1,0:T(8,128)(2,1)} %param.7) | copy-start | bytes 196612
  4.5 8.9 %collective-permute-start.1 = (bf16[2,128,256]{2,1,0:T(8,128)(2,1)S(1)}, bf16[2,128,256]{2,1,0:T(8,128)(2,1)S(1)}, u32[]{:S(2)}, u32[]{:S(2)}) collective-permute-start(bf16[2,128,256]{2,1,0:T(8,128)(2,1)S(1)} %get-tuple-element.48), channel_id=1, source_target_pairs={{0,16},{1,17},{2,18},{3,19},{4,20},{5,21},{6,22},{7,23},{8,24},{9,... | collective-permute-start | bytes 393224 | tf_op jit(solution)/shard_map/ppermute | solution.py:518
  7.5 5.9 %collective-permute-start.2 = (bf16[2,128,256]{2,1,0:T(8,128)(2,1)S(1)}, bf16[2,128,256]{2,1,0:T(8,128)(2,1)S(1)}, u32[]{:S(2)}, u32[]{:S(2)}) collective-permute-start(bf16[2,128,256]{2,1,0:T(8,128)(2,1)S(1)} %get-tuple-element.49), channel_id=1, source_target_pairs={{0,17},{1,16},{2,19},{3,18},{4,21},{5,20},{6,23},{7,22},{8,25},{9,... | collective-permute-start | bytes 393224 | tf_op jit(solution)/shard_map/ppermute | solution.py:519
  7.5 1.3 %collective-permute-start.10 = (bf16[2,128,256]{2,1,0:T(8,128)(2,1)S(1)}, bf16[2,128,256]{2,1,0:T(8,128)(2,1)S(1)}, u32[]{:S(2)}, u32[]{:S(2)}) collective-permute-start(bf16[2,128,256]{2,1,0:T(8,128)(2,1)S(1)} %get-tuple-element.57), channel_id=1, source_target_pairs={{0,1},{1,0},{2,3},{3,2},{4,5},{5,4},{6,7},{7,6},{8,9},{9,8},{10,11... | collective-permute-start | bytes 393224 | tf_op jit(solution)/shard_map/ppermute | solution.py:40
  9.0 10.3 %collective-permute-start.12 = (bf16[9,64,256]{2,1,0:T(8,128)(2,1)S(1)}, bf16[9,64,256]{2,1,0:T(8,128)(2,1)S(1)}, u32[]{:S(2)}, u32[]{:S(2)}) collective-permute-start(bf16[9,64,256]{2,1,0:T(8,128)(2,1)S(1)} %pad_maximum_fusion.1.refs_13_), channel_id=1, source_target_pairs={{0,8},{1,9},{2,10},{3,11},{4,0},{5,1},{6,2},{7,3},{8,12},{9,13},{1... | collective-permute-start | bytes 884744 | tf_op jit(solution)/shard_map/ppermute | solution.py:49
  11.9 9.9 %collective-permute-start.11 = (bf16[9,64,256]{2,1,0:T(8,128)(2,1)S(1)}, bf16[9,64,256]{2,1,0:T(8,128)(2,1)S(1)}, u32[]{:S(2)}, u32[]{:S(2)}) collective-permute-start(bf16[9,64,256]{2,1,0:T(8,128)(2,1)S(1)} %pad_maximum_fusion.1.refs_13_), channel_id=1, source_target_pairs={{0,2},{1,3},{2,0},{3,1},{4,6},{5,7},{6,4},{7,5},{8,10},{9,11},{10,... | collective-permute-start | bytes 884744 | tf_op jit(solution)/shard_map/ppermute | solution.py:40
  13.5 12.0 %collective-permute-start.4 = (bf16[9,64,256]{2,1,0:T(8,128)(2,1)S(1)}, bf16[9,64,256]{2,1,0:T(8,128)(2,1)S(1)}, u32[]{:S(2)}, u32[]{:S(2)}) collective-permute-start(bf16[9,64,256]{2,1,0:T(8,128)(2,1)S(1)} %pad_maximum_fusion.refs_4_), channel_id=1, source_target_pairs={{0,8},{1,9},{2,10},{3,11},{4,0},{5,1},{6,2},{7,3},{8,12},{9,13},{1... | collective-permute-start | bytes 884744 | tf_op jit(solution)/shard_map/ppermute | solution.py:49
  16.0 12.1 %collective-permute-start.3 = (bf16[9,64,256]{2,1,0:T(8,128)(2,1)S(1)}, bf16[9,64,256]{2,1,0:T(8,128)(2,1)S(1)}, u32[]{:S(2)}, u32[]{:S(2)}) collective-permute-start(bf16[9,64,256]{2,1,0:T(8,128)(2,1)S(1)} %pad_maximum_fusion.refs_4_), channel_id=1, source_target_pairs={{0,2},{1,3},{2,0},{3,1},{4,6},{5,7},{6,4},{7,5},{8,10},{9,11},{10,... | collective-permute-start | bytes 884744 | tf_op jit(solution)/shard_map/ppermute | solution.py:40
  17.6 48.8 %collective-permute-start = (bf16[32,128,256]{2,1,0:T(8,128)(2,1)S(1)}, bf16[32,128,256]{2,1,0:T(8,128)(2,1)S(1)}, u32[]{:S(2)}, u32[]{:S(2)}) collective-permute-start(bf16[32,128,256]{2,1,0:T(8,128)(2,1)S(1)} %copy-done.1), channel_id=1, source_target_pairs={{0,1},{1,0},{2,3},{3,2},{4,5},{5,4},{6,7},{7,6},{8,9},{9,8},{10,11... | collective-permute-start | bytes 6291464 | tf_op jit(solution)/shard_map/ppermute | solution.py:40
  21.8 10.1 %collective-permute-start.14 = (bf16[9,64,256]{2,1,0:T(8,128)(2,1)S(1)}, bf16[9,64,256]{2,1,0:T(8,128)(2,1)S(1)}, u32[]{:S(2)}, u32[]{:S(2)}) collective-permute-start(bf16[9,64,256]{2,1,0:T(8,128)(2,1)S(1)} %collective-permute-done.12.refs_14_), channel_id=1, source_target_pairs={{0,8},{1,9},{2,10},{3,11},{4,0},{5,1},{6,2},{7,3},{8,12},{9,13},{1... | collective-permute-start | bytes 884744 | tf_op jit(solution)/shard_map/ppermute | solution.py:49
  23.3 11.1 %collective-permute-start.13 = (bf16[9,64,256]{2,1,0:T(8,128)(2,1)S(1)}, bf16[9,64,256]{2,1,0:T(8,128)(2,1)S(1)}, u32[]{:S(2)}, u32[]{:S(2)}) collective-permute-start(bf16[9,64,256]{2,1,0:T(8,128)(2,1)S(1)} %collective-permute-done.12.refs_14_), channel_id=1, source_target_pairs={{0,2},{1,3},{2,0},{3,1},{4,6},{5,7},{6,4},{7,5},{8,10},{9,11},{10,... | collective-permute-start | bytes 884744 | tf_op jit(solution)/shard_map/ppermute | solution.py:40
  28.1 10.1 %collective-permute-start.6 = (bf16[9,64,256]{2,1,0:T(8,128)(2,1)S(1)}, bf16[9,64,256]{2,1,0:T(8,128)(2,1)S(1)}, u32[]{:S(2)}, u32[]{:S(2)}) collective-permute-start(bf16[9,64,256]{2,1,0:T(8,128)(2,1)S(1)} %collective-permute-done.4.refs_5_), channel_id=1, source_target_pairs={{0,8},{1,9},{2,10},{3,11},{4,0},{5,1},{6,2},{7,3},{8,12},{9,13},{1... | collective-permute-start | bytes 884744 | tf_op jit(solution)/shard_map/ppermute | solution.py:49
  29.7 11.1 %collective-permute-start.5 = (bf16[9,64,256]{2,1,0:T(8,128)(2,1)S(1)}, bf16[9,64,256]{2,1,0:T(8,128)(2,1)S(1)}, u32[]{:S(2)}, u32[]{:S(2)}) collective-permute-start(bf16[9,64,256]{2,1,0:T(8,128)(2,1)S(1)} %collective-permute-done.4.refs_5_), channel_id=1, source_target_pairs={{0,2},{1,3},{2,0},{3,1},{4,6},{5,7},{6,4},{7,5},{8,10},{9,11},{10,... | collective-permute-start | bytes 884744 | tf_op jit(solution)/shard_map/ppermute | solution.py:40
  34.4 10.1 %collective-permute-start.16 = (bf16[9,64,256]{2,1,0:T(8,128)(2,1)S(1)}, bf16[9,64,256]{2,1,0:T(8,128)(2,1)S(1)}, u32[]{:S(2)}, u32[]{:S(2)}) collective-permute-start(bf16[9,64,256]{2,1,0:T(8,128)(2,1)S(1)} %collective-permute-done.14.refs_15_), channel_id=1, source_target_pairs={{0,8},{1,9},{2,10},{3,11},{4,0},{5,1},{6,2},{7,3},{8,12},{9,13},{1... | collective-permute-start | bytes 884744 | tf_op jit(solution)/shard_map/ppermute | solution.py:49
  36.0 11.1 %collective-permute-start.15 = (bf16[9,64,256]{2,1,0:T(8,128)(2,1)S(1)}, bf16[9,64,256]{2,1,0:T(8,128)(2,1)S(1)}, u32[]{:S(2)}, u32[]{:S(2)}) collective-permute-start(bf16[9,64,256]{2,1,0:T(8,128)(2,1)S(1)} %collective-permute-done.14.refs_15_), channel_id=1, source_target_pairs={{0,2},{1,3},{2,0},{3,1},{4,6},{5,7},{6,4},{7,5},{8,10},{9,11},{10,... | collective-permute-start | bytes 884744 | tf_op jit(solution)/shard_map/ppermute | solution.py:40
  40.7 10.1 %collective-permute-start.8 = (bf16[9,64,256]{2,1,0:T(8,128)(2,1)S(1)}, bf16[9,64,256]{2,1,0:T(8,128)(2,1)S(1)}, u32[]{:S(2)}, u32[]{:S(2)}) collective-permute-start(bf16[9,64,256]{2,1,0:T(8,128)(2,1)S(1)} %collective-permute-done.6.refs_6_), channel_id=1, source_target_pairs={{0,8},{1,9},{2,10},{3,11},{4,0},{5,1},{6,2},{7,3},{8,12},{9,13},{1... | collective-permute-start | bytes 884744 | tf_op jit(solution)/shard_map/ppermute | solution.py:49
  42.3 11.1 %collective-permute-start.7 = (bf16[9,64,256]{2,1,0:T(8,128)(2,1)S(1)}, bf16[9,64,256]{2,1,0:T(8,128)(2,1)S(1)}, u32[]{:S(2)}, u32[]{:S(2)}) collective-permute-start(bf16[9,64,256]{2,1,0:T(8,128)(2,1)S(1)} %collective-permute-done.6.refs_6_), channel_id=1, source_target_pairs={{0,2},{1,3},{2,0},{3,1},{4,6},{5,7},{6,4},{7,5},{8,10},{9,11},{10,... | collective-permute-start | bytes 884744 | tf_op jit(solution)/shard_map/ppermute | solution.py:40
  47.1 6.4 %collective-permute-start.19 = (bf16[4,64,256]{2,1,0:T(8,128)(2,1)S(1)}, bf16[4,64,256]{2,1,0:T(8,128)(2,1)S(1)}, u32[]{:S(2)}, u32[]{:S(2)}) collective-permute-start(bf16[4,64,256]{2,1,0:T(8,128)(2,1)S(1)} %slice.95), channel_id=1, source_target_pairs={{0,8},{1,9},{2,10},{3,11},{4,0},{5,1},{6,2},{7,3},{8,12},{9,13},{1... | collective-permute-start | bytes 393224 | tf_op jit(solution)/shard_map/ppermute | solution.py:49
  48.7 7.3 %collective-permute-start.18 = (bf16[5,64,256]{2,1,0:T(8,128)(2,1)S(1)}, bf16[5,64,256]{2,1,0:T(8,128)(2,1)S(1)}, u32[]{:S(2)}, u32[]{:S(2)}) collective-permute-start(bf16[5,64,256]{2,1,0:T(8,128)(2,1)S(1)} %slice.94), channel_id=1, source_target_pairs={{0,2},{1,3},{2,0},{3,1},{4,6},{5,7},{6,4},{7,5},{8,10},{9,11},{10,... | collective-permute-start | bytes 491528 | tf_op jit(solution)/shard_map/ppermute | solution.py:40
  50.9 7.2 %collective-permute-start.17 = (bf16[7,64,256]{2,1,0:T(8,128)(2,1)S(1)}, bf16[7,64,256]{2,1,0:T(8,128)(2,1)S(1)}, u32[]{:S(2)}, u32[]{:S(2)}) collective-permute-start(bf16[7,64,256]{2,1,0:T(8,128)(2,1)S(1)} %slice_dynamic-update-slice_fusion), channel_id=1, source_target_pairs={{0,1},{1,0},{2,3},{3,2},{4,5},{5,4},{6,7},{7,6},{8,9},{9,8},{10,11... | collective-permute-start | bytes 688136 | tf_op jit(solution)/shard_map/ppermute | solution.py:40
  53.4 5.7 %collective-permute-start.9 = (bf16[7,64,256]{2,1,0:T(8,128)(2,1)S(1)}, bf16[7,64,256]{2,1,0:T(8,128)(2,1)S(1)}, u32[]{:S(2)}, u32[]{:S(2)}) collective-permute-start(bf16[7,64,256]{2,1,0:T(8,128)(2,1)S(1)} %slice_dynamic-update-slice_fusion.6), channel_id=1, source_target_pairs={{0,1},{1,0},{2,3},{3,2},{4,5},{5,4},{6,7},{7,6},{8,9},{9,8},{10,11... | collective-permute-start | bytes 688136 | tf_op jit(solution)/shard_map/ppermute | solution.py:40
  53.5 7.5 %collective-permute-start.22 = (bf16[5,64,256]{2,1,0:T(8,128)(2,1)S(1)}, bf16[5,64,256]{2,1,0:T(8,128)(2,1)S(1)}, u32[]{:S(2)}, u32[]{:S(2)}) collective-permute-start(bf16[5,64,256]{2,1,0:T(8,128)(2,1)S(1)} %slice.98), channel_id=1, source_target_pairs={{0,2},{1,3},{2,0},{3,1},{4,6},{5,7},{6,4},{7,5},{8,10},{9,11},{10,... | collective-permute-start | bytes 491528 | tf_op jit(solution)/shard_map/ppermute | solution.py:40
  56.0 5.0 %collective-permute-start.23 = (bf16[4,64,256]{2,1,0:T(8,128)(2,1)S(1)}, bf16[4,64,256]{2,1,0:T(8,128)(2,1)S(1)}, u32[]{:S(2)}, u32[]{:S(2)}) collective-permute-start(bf16[4,64,256]{2,1,0:T(8,128)(2,1)S(1)} %slice.99), channel_id=1, source_target_pairs={{0,8},{1,9},{2,10},{3,11},{4,0},{5,1},{6,2},{7,3},{8,12},{9,13},{1... | collective-permute-start | bytes 393224 | tf_op jit(solution)/shard_map/ppermute | solution.py:49
  58.1 3.9 %collective-permute-start.21 = (bf16[1,64,256]{2,1,0:T(8,128)(2,1)S(1)}, bf16[1,64,256]{2,1,0:T(8,128)(2,1)S(1)}, u32[]{:S(2)}, u32[]{:S(2)}) collective-permute-start(bf16[1,64,256]{2,1,0:T(8,128)(2,1)S(1)} %slice.97), channel_id=1, source_target_pairs={{0,2},{1,3},{2,0},{3,1},{4,6},{5,7},{6,4},{7,5},{8,10},{9,11},{10,... | collective-permute-start | bytes 98312 | tf_op jit(solution)/shard_map/ppermute | solution.py:40
  59.1 3.9 %collective-permute-start.20 = (bf16[1,64,256]{2,1,0:T(8,128)(2,1)S(1)}, bf16[1,64,256]{2,1,0:T(8,128)(2,1)S(1)}, u32[]{:S(2)}, u32[]{:S(2)}) collective-permute-start(bf16[1,64,256]{2,1,0:T(8,128)(2,1)S(1)} %slice.104), channel_id=1, source_target_pairs={{0,2},{1,3},{2,0},{3,1},{4,6},{5,7},{6,4},{7,5},{8,10},{9,11},{10,... | collective-permute-start | bytes 98312 | tf_op jit(solution)/shard_map/ppermute | solution.py:40
  63.0 15.0 %copy-start = (bf16[32,128,2048]{2,1,0:T(8,128)(2,1)S(1)}, bf16[32,128,2048]{2,1,0:T(8,128)(2,1)}, u32[]{:S(2)}) copy-start(bf16[32,128,2048]{2,1,0:T(8,128)(2,1)} %cholesky.1) | copy-start | bytes 50331652
  66.4 11.6 %copy-start.3 = (f32[8,32]{1,0:T(8,128)S(1)}, f32[8,32]{1,0:T(8,128)}, u32[]{:S(2)}) copy-start(f32[8,32]{1,0:T(8,128)} %fields.1) | copy-start | bytes 3076
  81.2 2.7 %collective-permute-start.24 = (bf16[4,64,2048]{2,1,0:T(8,128)(2,1)S(1)}, bf16[4,64,2048]{2,1,0:T(8,128)(2,1)S(1)}, u32[]{:S(2)}, u32[]{:S(2)}) collective-permute-start(bf16[4,64,2048]{2,1,0:T(8,128)(2,1)S(1)} %get-tuple-element.70), channel_id=1, source_target_pairs={{0,1},{1,0},{2,3},{3,2},{4,5},{5,4},{6,7},{7,6},{8,9},{9,8},{10,11... | collective-permute-start | bytes 3145736 | tf_op jit(solution)/shard_map/ppermute | solution.py:40
  81.2 4.1 %collective-permute-start.25 = (bf16[4,64,2048]{2,1,0:T(8,128)(2,1)S(1)}, bf16[4,64,2048]{2,1,0:T(8,128)(2,1)S(1)}, u32[]{:S(2)}, u32[]{:S(2)}) collective-permute-start(bf16[4,64,2048]{2,1,0:T(8,128)(2,1)S(1)} %get-tuple-element.71), channel_id=1, source_target_pairs={{0,1},{1,0},{2,3},{3,2},{4,5},{5,4},{6,7},{7,6},{8,9},{9,8},{10,11... | collective-permute-start | bytes 3145736 | tf_op jit(solution)/shard_map/ppermute | solution.py:40
  82.6 9.2 %collective-permute-start.27 = (bf16[4,128,256]{2,1,0:T(8,128)(2,1)S(1)}, bf16[4,128,256]{2,1,0:T(8,128)(2,1)S(1)}, u32[]{:S(2)}, u32[]{:S(2)}) collective-permute-start(bf16[4,128,256]{2,1,0:T(8,128)(2,1)S(1)} %get-tuple-element.74.refs_3_), channel_id=1, source_target_pairs={{0,8},{1,9},{2,10},{3,11},{4,0},{5,1},{6,2},{7,3},{8,12},{9,13},{1... | collective-permute-start | bytes 786440 | tf_op jit(solution)/shard_map/ppermute | solution.py:49
  82.8 9.2 %collective-permute-start.26 = (bf16[4,128,256]{2,1,0:T(8,128)(2,1)S(1)}, bf16[4,128,256]{2,1,0:T(8,128)(2,1)S(1)}, u32[]{:S(2)}, u32[]{:S(2)}) collective-permute-start(bf16[4,128,256]{2,1,0:T(8,128)(2,1)S(1)} %get-tuple-element.74.refs_3_), channel_id=1, source_target_pairs={{0,2},{1,3},{2,0},{3,1},{4,6},{5,7},{6,4},{7,5},{8,10},{9,11},{10,... | collective-permute-start | bytes 786440 | tf_op jit(solution)/shard_map/ppermute | solution.py:40
  86.2 11.2 %collective-permute-start.35 = (bf16[4,128,256]{2,1,0:T(8,128)(2,1)S(1)}, bf16[4,128,256]{2,1,0:T(8,128)(2,1)S(1)}, u32[]{:S(2)}, u32[]{:S(2)}) collective-permute-start(bf16[4,128,256]{2,1,0:T(8,128)(2,1)S(1)} %get-tuple-element.81.refs_12_), channel_id=1, source_target_pairs={{0,8},{1,9},{2,10},{3,11},{4,0},{5,1},{6,2},{7,3},{8,12},{9,13},{1... | collective-permute-start | bytes 786440 | tf_op jit(solution)/shard_map/ppermute | solution.py:49
  86.5 11.1 %collective-permute-start.34 = (bf16[4,128,256]{2,1,0:T(8,128)(2,1)S(1)}, bf16[4,128,256]{2,1,0:T(8,128)(2,1)S(1)}, u32[]{:S(2)}, u32[]{:S(2)}) collective-permute-start(bf16[4,128,256]{2,1,0:T(8,128)(2,1)S(1)} %get-tuple-element.81.refs_12_), channel_id=1, source_target_pairs={{0,2},{1,3},{2,0},{3,1},{4,6},{5,7},{6,4},{7,5},{8,10},{9,11},{10,... | collective-permute-start | bytes 786440 | tf_op jit(solution)/shard_map/ppermute | solution.py:40
  92.0 11.0 %collective-permute-start.29 = (bf16[4,128,256]{2,1,0:T(8,128)(2,1)S(1)}, bf16[4,128,256]{2,1,0:T(8,128)(2,1)S(1)}, u32[]{:S(2)}, u32[]{:S(2)}) collective-permute-start(bf16[4,128,256]{2,1,0:T(8,128)(2,1)S(1)} %collective-permute-done.27.refs_4_), channel_id=1, source_target_pairs={{0,8},{1,9},{2,10},{3,11},{4,0},{5,1},{6,2},{7,3},{8,12},{9,13},{1... | collective-permute-start | bytes 786440 | tf_op jit(solution)/shard_map/ppermute | solution.py:49
  92.9 10.3 %collective-permute-start.28 = (bf16[4,128,256]{2,1,0:T(8,128)(2,1)S(1)}, bf16[4,128,256]{2,1,0:T(8,128)(2,1)S(1)}, u32[]{:S(2)}, u32[]{:S(2)}) collective-permute-start(bf16[4,128,256]{2,1,0:T(8,128)(2,1)S(1)} %collective-permute-done.27.refs_4_), channel_id=1, source_target_pairs={{0,2},{1,3},{2,0},{3,1},{4,6},{5,7},{6,4},{7,5},{8,10},{9,11},{10,... | collective-permute-start | bytes 786440 | tf_op jit(solution)/shard_map/ppermute | solution.py:40
  97.6 11.0 %collective-permute-start.37 = (bf16[4,128,256]{2,1,0:T(8,128)(2,1)S(1)}, bf16[4,128,256]{2,1,0:T(8,128)(2,1)S(1)}, u32[]{:S(2)}, u32[]{:S(2)}) collective-permute-start(bf16[4,128,256]{2,1,0:T(8,128)(2,1)S(1)} %collective-permute-done.35.refs_13_), channel_id=1, source_target_pairs={{0,8},{1,9},{2,10},{3,11},{4,0},{5,1},{6,2},{7,3},{8,12},{9,13},{1... | collective-permute-start | bytes 786440 | tf_op jit(solution)/shard_map/ppermute | solution.py:49
  98.5 10.3 %collective-permute-start.36 = (bf16[4,128,256]{2,1,0:T(8,128)(2,1)S(1)}, bf16[4,128,256]{2,1,0:T(8,128)(2,1)S(1)}, u32[]{:S(2)}, u32[]{:S(2)}) collective-permute-start(bf16[4,128,256]{2,1,0:T(8,128)(2,1)S(1)} %collective-permute-done.35.refs_13_), channel_id=1, source_target_pairs={{0,2},{1,3},{2,0},{3,1},{4,6},{5,7},{6,4},{7,5},{8,10},{9,11},{10,... | collective-permute-start | bytes 786440 | tf_op jit(solution)/shard_map/ppermute | solution.py:40
  103.2 11.0 %collective-permute-start.31 = (bf16[4,128,256]{2,1,0:T(8,128)(2,1)S(1)}, bf16[4,128,256]{2,1,0:T(8,128)(2,1)S(1)}, u32[]{:S(2)}, u32[]{:S(2)}) collective-permute-start(bf16[4,128,256]{2,1,0:T(8,128)(2,1)S(1)} %collective-permute-done.29.refs_5_), channel_id=1, source_target_pairs={{0,8},{1,9},{2,10},{3,11},{4,0},{5,1},{6,2},{7,3},{8,12},{9,13},{1... | collective-permute-start | bytes 786440 | tf_op jit(solution)/shard_map/ppermute | solution.py:49
  104.2 10.3 %collective-permute-start.30 = (bf16[4,128,256]{2,1,0:T(8,128)(2,1)S(1)}, bf16[4,128,256]{2,1,0:T(8,128)(2,1)S(1)}, u32[]{:S(2)}, u32[]{:S(2)}) collective-permute-start(bf16[4,128,256]{2,1,0:T(8,128)(2,1)S(1)} %collective-permute-done.29.refs_5_), channel_id=1, source_target_pairs={{0,2},{1,3},{2,0},{3,1},{4,6},{5,7},{6,4},{7,5},{8,10},{9,11},{10,... | collective-permute-start | bytes 786440 | tf_op jit(solution)/shard_map/ppermute | solution.py:40
  108.9 11.0 %collective-permute-start.39 = (bf16[4,128,256]{2,1,0:T(8,128)(2,1)S(1)}, bf16[4,128,256]{2,1,0:T(8,128)(2,1)S(1)}, u32[]{:S(2)}, u32[]{:S(2)}) collective-permute-start(bf16[4,128,256]{2,1,0:T(8,128)(2,1)S(1)} %collective-permute-done.37.refs_14_), channel_id=1, source_target_pairs={{0,8},{1,9},{2,10},{3,11},{4,0},{5,1},{6,2},{7,3},{8,12},{9,13},{1... | collective-permute-start | bytes 786440 | tf_op jit(solution)/shard_map/ppermute | solution.py:49
  109.8 10.3 %collective-permute-start.38 = (bf16[4,128,256]{2,1,0:T(8,128)(2,1)S(1)}, bf16[4,128,256]{2,1,0:T(8,128)(2,1)S(1)}, u32[]{:S(2)}, u32[]{:S(2)}) collective-permute-start(bf16[4,128,256]{2,1,0:T(8,128)(2,1)S(1)} %collective-permute-done.37.refs_14_), channel_id=1, source_target_pairs={{0,2},{1,3},{2,0},{3,1},{4,6},{5,7},{6,4},{7,5},{8,10},{9,11},{10,... | collective-permute-start | bytes 786440 | tf_op jit(solution)/shard_map/ppermute | solution.py:40
  114.5 8.2 %collective-permute-start.33 = (bf16[2,128,256]{2,1,0:T(8,128)(2,1)S(1)}, bf16[2,128,256]{2,1,0:T(8,128)(2,1)S(1)}, u32[]{:S(2)}, u32[]{:S(2)}) collective-permute-start(bf16[2,128,256]{2,1,0:T(8,128)(2,1)S(1)} %slice.101), channel_id=1, source_target_pairs={{0,8},{1,9},{2,10},{3,11},{4,0},{5,1},{6,2},{7,3},{8,12},{9,13},{1... | collective-permute-start | bytes 393224 | tf_op jit(solution)/shard_map/ppermute | solution.py:49
  115.5 7.2 %collective-permute-start.32 = (bf16[2,128,256]{2,1,0:T(8,128)(2,1)S(1)}, bf16[2,128,256]{2,1,0:T(8,128)(2,1)S(1)}, u32[]{:S(2)}, u32[]{:S(2)}) collective-permute-start(bf16[2,128,256]{2,1,0:T(8,128)(2,1)S(1)} %slice.100), channel_id=1, source_target_pairs={{0,2},{1,3},{2,0},{3,1},{4,6},{5,7},{6,4},{7,5},{8,10},{9,11},{10,... | collective-permute-start | bytes 393224 | tf_op jit(solution)/shard_map/ppermute | solution.py:40
  120.1 5.0 %collective-permute-start.41 = (bf16[2,128,256]{2,1,0:T(8,128)(2,1)S(1)}, bf16[2,128,256]{2,1,0:T(8,128)(2,1)S(1)}, u32[]{:S(2)}, u32[]{:S(2)}) collective-permute-start(bf16[2,128,256]{2,1,0:T(8,128)(2,1)S(1)} %slice.103), channel_id=1, source_target_pairs={{0,8},{1,9},{2,10},{3,11},{4,0},{5,1},{6,2},{7,3},{8,12},{9,13},{1... | collective-permute-start | bytes 393224 | tf_op jit(solution)/shard_map/ppermute | solution.py:49
  121.1 5.0 %collective-permute-start.40 = (bf16[2,128,256]{2,1,0:T(8,128)(2,1)S(1)}, bf16[2,128,256]{2,1,0:T(8,128)(2,1)S(1)}, u32[]{:S(2)}, u32[]{:S(2)}) collective-permute-start(bf16[2,128,256]{2,1,0:T(8,128)(2,1)S(1)} %slice.102), channel_id=1, source_target_pairs={{0,2},{1,3},{2,0},{3,1},{4,6},{5,7},{6,4},{7,5},{8,10},{9,11},{10,... | collective-permute-start | bytes 393224 | tf_op jit(solution)/shard_map/ppermute | solution.py:40
  127.1 2.0 %collective-permute-start.42 = (bf16[4,128,256]{2,1,0:T(8,128)(2,1)S(1)}, bf16[4,128,256]{2,1,0:T(8,128)(2,1)S(1)}, u32[]{:S(2)}, u32[]{:S(2)}) collective-permute-start(bf16[4,128,256]{2,1,0:T(8,128)(2,1)S(1)} %get-tuple-element.88), channel_id=1, source_target_pairs={{0,1},{1,0},{2,3},{3,2},{4,5},{5,4},{6,7},{7,6},{8,9},{9,8},{10,11... | collective-permute-start | bytes 786440 | tf_op jit(solution)/shard_map/ppermute | solution.py:40

commit v14 on v13

--- a/solution.py
+++ b/solution.py
@@ -379,71 +379,56 @@
     )(*potential, base, *arrays)
 
 
-def finish_kernel(order, potential, base, full, out, results, semaphores):
-    half = base.shape[0]
-    b = lax.rem(lax.axis_index("chol"), 2)
-    copies = []
-    for walker in range(half):
+def finish_kernel(potential, base, full, out):
+    for walker in range(out.shape[0]):
         columns = full[walker].reshape(-1, full.shape[-1])
         term = jnp.dot(potential[walker], columns, preferred_element_type=F32)
-        results[walker] = (base[walker] + 0.5 * term).astype(BF16)
-        copies.append(
-            pltpu.make_async_copy(
-                results.at[walker], out.at[order[b * half + walker]], semaphores.at[walker]
-            )
-        )
-        copies[-1].start()
-    for copy in copies:
-        copy.wait()
-
-
-def finish(order, potential, base, full):
+        out[walker] = (base[walker] + 0.5 * term).astype(BF16)
+
+
+def finish(potential, base, full):
     half, rows, electrons = base.shape
     orbitals = potential.shape[2]
     return pl.pallas_call(
         finish_kernel,
-        out_shape=jax.ShapeDtypeStruct((2 * half, rows, electrons), BF16),
-        in_specs=[pl.BlockSpec(memory_space=pltpu.SMEM)] + vmem_specs(3),
-        out_specs=pl.BlockSpec(memory_space=pl.ANY),
-        scratch_shapes=[
-            pltpu.VMEM((half, rows, electrons), BF16),
-            pltpu.SemaphoreType.DMA((half,)),
-        ],
+        out_shape=jax.ShapeDtypeStruct((half, rows, electrons), BF16),
+        in_specs=vmem_specs(3),
+        out_specs=pl.BlockSpec(memory_space=pltpu.VMEM),
         compiler_params=params(8),
         cost_estimate=pl.CostEstimate(
             flops=2 * half * rows * orbitals * electrons,
             bytes_accessed=2 * half * orbitals * (rows + electrons),
             transcendentals=0,
         ),
-    )(order, potential, base, full)
-
-
-def place_kernel(order, theirs, _, out, semaphores):
-    half = theirs.shape[0]
+    )(potential, base, full)
+
+
+def place_kernel(order, mine, theirs, out, semaphores):
+    half = mine.shape[0]
     b = lax.rem(lax.axis_index("chol"), 2)
-    copies = [
-        pltpu.make_async_copy(
-            theirs.at[walker], out.at[order[(1 - b) * half + walker]], semaphores.at[walker]
-        )
-        for walker in range(half)
-    ]
+    copies = []
+    for part, core in ((mine, b), (theirs, 1 - b)):
+        for walker in range(half):
+            target = out.at[order[core * half + walker]]
+            copies.append(
+                pltpu.make_async_copy(part.at[walker], target, semaphores.at[len(copies)])
+            )
     for copy in copies:
         copy.start()
     for copy in copies:
         copy.wait()
 
 
-def place(order, theirs, out):
+def place(order, mine, theirs):
+    half, rows, electrons = mine.shape
     return pl.pallas_call(
         place_kernel,
-        out_shape=jax.ShapeDtypeStruct(out.shape, out.dtype),
-        in_specs=[pl.BlockSpec(memory_space=pltpu.SMEM)] + vmem_specs(1)
-        + [pl.BlockSpec(memory_space=pl.ANY)],
+        out_shape=jax.ShapeDtypeStruct((2 * half, rows, electrons), BF16),
+        in_specs=[pl.BlockSpec(memory_space=pltpu.SMEM)] + vmem_specs(2),
         out_specs=pl.BlockSpec(memory_space=pl.ANY),
-        scratch_shapes=[pltpu.SemaphoreType.DMA((theirs.shape[0],))],
-        input_output_aliases={2: 0},
+        scratch_shapes=[pltpu.SemaphoreType.DMA((2 * half,))],
         compiler_params=params(4),
-    )(order, theirs, out)
+    )(order, mine, theirs)
 
 
 def split_kernel(source, walkers, *refs):
@@ -496,7 +481,7 @@
             pltpu.SMEM((per_group + 1,), jnp.int32),
             pltpu.SemaphoreType.DMA((per_group,)),
         ],
-        compiler_params=params(4),
+        compiler_params=params(60),
     )(source, walkers)
 
 
@@ -585,7 +570,7 @@
             stream.advance()
     sent, full = second_of(layout, received, base_theirs, streams)
     theirs = layout.shift(sent, db=1)
-    return place(order, theirs, finish(order, kept, base, full)), force_bias
+    return place(order, finish(kept, base, full), theirs), force_bias
 
 
 def solution(mesh):

time: 131 us -> 146 us (1.11)
  Pallas kernels: 16.1 us -> 31.5 us
  waiting for transfers between devices: 55.3 us -> 57.5 us
  local copies, waits for them, and re-layouts: 2.77 us -> 0.94 us
    pallas_call x1, Pallas kernels: 2.01 us -> 18.5 us  [split_walkers(): pl.pallas_call(split_kernel, out_shape=[share] * 4 + [jax.ShapeDtypeStruc...]
    unnamed x23 -> x21, local copies, waits for them, and re-layouts: 1.89 us -> 0.06 us
  transfers between devices with their start and end apart: 43 -> 43, of which waited for: 34 -> 35; matrix products, arithmetic and copies ran while one was open for 1% -> 1% of each run, Pallas kernels for 5% -> 4%
where the time goes in v14:
time: 146 us
  waiting for transfers between devices  57.5 us (39%)
  starting transfers between devices  44.1 us (30%)
  Pallas kernels  31.5 us (22%)
  blocking collectives  9.88 us (7%)
    ppermute x16, waiting for transfers between devices, step(): return lax.ppermute(array, 'chol', pairs)  33.8 us
    ppermute x25, waiting for transfers between devices, shift(): return lax.ppermute(array, 'chol', pairs)  23.7 us
    ppermute x16, starting transfers between devices, step(): return lax.ppermute(array, 'chol', pairs)  20.8 us
    ppermute x25, starting transfers between devices, shift(): return lax.ppermute(array, 'chol', pairs)  20.4 us
    pallas_call x1, Pallas kernels, split_walkers(): pl.pallas_call(split_kernel, out_shape=[share] * 4 + [jax.ShapeDtypeStruc...  18.5 us
    all_to_all x1, blocking collectives, shards(): parts = lax.all_to_all(parts, 'chol', 0, 0, tiled=True)  9.88 us
    pallas_call x1, Pallas kernels, inverses_of(): pl.pallas_call(functools.partial(inverse_kernel, layout, slabs, counts),...  3.32 us
    pallas_call x1, Pallas kernels, potential_of(): pl.pallas_call(potential_kernel, out_shape=[jax.ShapeDtypeStruct((per_gro...  3.18 us
  transfers between devices with their start and end apart: 43, of which 35 were waited for; matrix products, arithmetic and copies ran while one was open for 1% of the time, Pallas kernels for 4%

profile of v14, /device:TPU:0, one launch (start us, length us, event | category | flops | bytes accessed | tf_op | source)
XLA Modules:
  0.0 145.9 jit_solution(5340248593295005468)
XLA Ops:
  0.7 18.5 %shard_map.77 = (bf16[2,128,256]{2,1,0:T(8,128)(2,1)}, bf16[2,128,256]{2,1,0:T(8,128)(2,1)}, bf16[2,128,256]{2,1,0:T(8,128)(2,1)}, bf16[2,128,256]{2,1,0:T(8,128)(2,1)}, s32[8]{0:T(128)}) custom-call(s32[16]{0:T(128)} %source.1, bf16[8,128,256]{2,1,0:T(8,128)(2,1)} %walkers.1), custom_call_target="tpu_custom_call" | custom-call | tf_op jit(solution)/shard_map/pallas_call | solution.py:474
  19.1 3.0 %collective-permute-start.1 = (bf16[2,128,256]{2,1,0:T(8,128)(2,1)}, bf16[2,128,256]{2,1,0:T(8,128)(2,1)S(1)}, u32[]{:S(2)}, u32[]{:S(2)}) collective-permute-start(bf16[2,128,256]{2,1,0:T(8,128)(2,1)} %get-tuple-element.48), channel_id=1, source_target_pairs={{0,16},{1,17},{2,18},{3,19},{4,20},{5,21},{6,22},{7,23},{8,24},{9,... | collective-permute-start | bytes 393224 | tf_op jit(solution)/shard_map/ppermute | solution.py:503
  22.3 0.8 slice_bitcast_fusion
  23.7 0.9 broadcast_select_fusion.1
  24.7 2.9 %collective-permute-start.12 = (bf16[9,64,256]{2,1,0:T(8,128)(2,1)S(1)}, bf16[9,64,256]{2,1,0:T(8,128)(2,1)S(1)}, u32[]{:S(2)}, u32[]{:S(2)}) collective-permute-start(bf16[9,64,256]{2,1,0:T(8,128)(2,1)S(1)} %pad_maximum_fusion.1.refs_13_), channel_id=1, source_target_pairs={{0,8},{1,9},{2,10},{3,11},{4,0},{5,1},{6,2},{7,3},{8,12},{9,13},{1... | collective-permute-start | bytes 884744 | tf_op jit(solution)/shard_map/ppermute | solution.py:49
  27.6 1.5 %collective-permute-start.11 = (bf16[9,64,256]{2,1,0:T(8,128)(2,1)S(1)}, bf16[9,64,256]{2,1,0:T(8,128)(2,1)S(1)}, u32[]{:S(2)}, u32[]{:S(2)}) collective-permute-start(bf16[9,64,256]{2,1,0:T(8,128)(2,1)S(1)} %pad_maximum_fusion.1.refs_13_), channel_id=1, source_target_pairs={{0,2},{1,3},{2,0},{3,1},{4,6},{5,7},{6,4},{7,5},{8,10},{9,11},{10,... | collective-permute-start | bytes 884744 | tf_op jit(solution)/shard_map/ppermute | solution.py:40
  29.3 1.6 %collective-permute-start.4 = (bf16[9,64,256]{2,1,0:T(8,128)(2,1)S(1)}, bf16[9,64,256]{2,1,0:T(8,128)(2,1)S(1)}, u32[]{:S(2)}, u32[]{:S(2)}) collective-permute-start(bf16[9,64,256]{2,1,0:T(8,128)(2,1)S(1)} %pad_maximum_fusion.refs_4_), channel_id=1, source_target_pairs={{0,8},{1,9},{2,10},{3,11},{4,0},{5,1},{6,2},{7,3},{8,12},{9,13},{1... | collective-permute-start | bytes 884744 | tf_op jit(solution)/shard_map/ppermute | solution.py:49
  30.9 1.5 %collective-permute-start.3 = (bf16[9,64,256]{2,1,0:T(8,128)(2,1)S(1)}, bf16[9,64,256]{2,1,0:T(8,128)(2,1)S(1)}, u32[]{:S(2)}, u32[]{:S(2)}) collective-permute-start(bf16[9,64,256]{2,1,0:T(8,128)(2,1)S(1)} %pad_maximum_fusion.refs_4_), channel_id=1, source_target_pairs={{0,2},{1,3},{2,0},{3,1},{4,6},{5,7},{6,4},{7,5},{8,10},{9,11},{10,... | collective-permute-start | bytes 884744 | tf_op jit(solution)/shard_map/ppermute | solution.py:40
  32.4 2.5 %collective-permute-done.12.refs_14_ = bf16[9,64,256]{2,1,0:T(8,128)(2,1)S(1)} collective-permute-done((bf16[9,64,256]{2,1,0:T(8,128)(2,1)S(1)}, bf16[9,64,256]{2,1,0:T(8,128)(2,1)S(1)}, u32[]{:S(2)}, u32[]{:S(2)}) %collective-permute-start.12) | collective-permute-done | bytes 294944 | tf_op jit(solution)/shard_map/ppermute | solution.py:49
  35.0 2.5 %collective-permute-done.11.refs_17_ = bf16[9,64,256]{2,1,0:T(8,128)(2,1)S(1)} collective-permute-done((bf16[9,64,256]{2,1,0:T(8,128)(2,1)S(1)}, bf16[9,64,256]{2,1,0:T(8,128)(2,1)S(1)}, u32[]{:S(2)}, u32[]{:S(2)}) %collective-permute-start.11) | collective-permute-done | bytes 294944 | tf_op jit(solution)/shard_map/ppermute | solution.py:40
  37.5 1.6 %collective-permute-start.14 = (bf16[9,64,256]{2,1,0:T(8,128)(2,1)S(1)}, bf16[9,64,256]{2,1,0:T(8,128)(2,1)S(1)}, u32[]{:S(2)}, u32[]{:S(2)}) collective-permute-start(bf16[9,64,256]{2,1,0:T(8,128)(2,1)S(1)} %collective-permute-done.12.refs_14_), channel_id=1, source_target_pairs={{0,8},{1,9},{2,10},{3,11},{4,0},{5,1},{6,2},{7,3},{8,12},{9,13},{1... | collective-permute-start | bytes 884744 | tf_op jit(solution)/shard_map/ppermute | solution.py:49
  39.1 1.5 %collective-permute-start.13 = (bf16[9,64,256]{2,1,0:T(8,128)(2,1)S(1)}, bf16[9,64,256]{2,1,0:T(8,128)(2,1)S(1)}, u32[]{:S(2)}, u32[]{:S(2)}) collective-permute-start(bf16[9,64,256]{2,1,0:T(8,128)(2,1)S(1)} %collective-permute-done.12.refs_14_), channel_id=1, source_target_pairs={{0,2},{1,3},{2,0},{3,1},{4,6},{5,7},{6,4},{7,5},{8,10},{9,11},{10,... | collective-permute-start | bytes 884744 | tf_op jit(solution)/shard_map/ppermute | solution.py:40
  40.6 0.7 collective-permute-done.4.refs_5_
  41.3 2.5 %collective-permute-done.3.refs_8_ = bf16[9,64,256]{2,1,0:T(8,128)(2,1)S(1)} collective-permute-done((bf16[9,64,256]{2,1,0:T(8,128)(2,1)S(1)}, bf16[9,64,256]{2,1,0:T(8,128)(2,1)S(1)}, u32[]{:S(2)}, u32[]{:S(2)}) %collective-permute-start.3) | collective-permute-done | bytes 294944 | tf_op jit(solution)/shard_map/ppermute | solution.py:40
  43.8 1.6 %collective-permute-start.6 = (bf16[9,64,256]{2,1,0:T(8,128)(2,1)S(1)}, bf16[9,64,256]{2,1,0:T(8,128)(2,1)S(1)}, u32[]{:S(2)}, u32[]{:S(2)}) collective-permute-start(bf16[9,64,256]{2,1,0:T(8,128)(2,1)S(1)} %collective-permute-done.4.refs_5_), channel_id=1, source_target_pairs={{0,8},{1,9},{2,10},{3,11},{4,0},{5,1},{6,2},{7,3},{8,12},{9,13},{1... | collective-permute-start | bytes 884744 | tf_op jit(solution)/shard_map/ppermute | solution.py:49
  45.4 1.5 %collective-permute-start.5 = (bf16[9,64,256]{2,1,0:T(8,128)(2,1)S(1)}, bf16[9,64,256]{2,1,0:T(8,128)(2,1)S(1)}, u32[]{:S(2)}, u32[]{:S(2)}) collective-permute-start(bf16[9,64,256]{2,1,0:T(8,128)(2,1)S(1)} %collective-permute-done.4.refs_5_), channel_id=1, source_target_pairs={{0,2},{1,3},{2,0},{3,1},{4,6},{5,7},{6,4},{7,5},{8,10},{9,11},{10,... | collective-permute-start | bytes 884744 | tf_op jit(solution)/shard_map/ppermute | solution.py:40
  46.9 0.7 collective-permute-done.14.refs_15_
  47.6 2.5 %collective-permute-done.13.refs_18_ = bf16[9,64,256]{2,1,0:T(8,128)(2,1)S(1)} collective-permute-done((bf16[9,64,256]{2,1,0:T(8,128)(2,1)S(1)}, bf16[9,64,256]{2,1,0:T(8,128)(2,1)S(1)}, u32[]{:S(2)}, u32[]{:S(2)}) %collective-permute-start.13) | collective-permute-done | bytes 294944 | tf_op jit(solution)/shard_map/ppermute | solution.py:40
  50.2 1.6 %collective-permute-start.16 = (bf16[9,64,256]{2,1,0:T(8,128)(2,1)S(1)}, bf16[9,64,256]{2,1,0:T(8,128)(2,1)S(1)}, u32[]{:S(2)}, u32[]{:S(2)}) collective-permute-start(bf16[9,64,256]{2,1,0:T(8,128)(2,1)S(1)} %collective-permute-done.14.refs_15_), channel_id=1, source_target_pairs={{0,8},{1,9},{2,10},{3,11},{4,0},{5,1},{6,2},{7,3},{8,12},{9,13},{1... | collective-permute-start | bytes 884744 | tf_op jit(solution)/shard_map/ppermute | solution.py:49
  51.7 1.5 %collective-permute-start.15 = (bf16[9,64,256]{2,1,0:T(8,128)(2,1)S(1)}, bf16[9,64,256]{2,1,0:T(8,128)(2,1)S(1)}, u32[]{:S(2)}, u32[]{:S(2)}) collective-permute-start(bf16[9,64,256]{2,1,0:T(8,128)(2,1)S(1)} %collective-permute-done.14.refs_15_), channel_id=1, source_target_pairs={{0,2},{1,3},{2,0},{3,1},{4,6},{5,7},{6,4},{7,5},{8,10},{9,11},{10,... | collective-permute-start | bytes 884744 | tf_op jit(solution)/shard_map/ppermute | solution.py:40
  53.3 0.7 collective-permute-done.6.refs_6_
  54.0 2.5 %collective-permute-done.5.refs_9_ = bf16[9,64,256]{2,1,0:T(8,128)(2,1)S(1)} collective-permute-done((bf16[9,64,256]{2,1,0:T(8,128)(2,1)S(1)}, bf16[9,64,256]{2,1,0:T(8,128)(2,1)S(1)}, u32[]{:S(2)}, u32[]{:S(2)}) %collective-permute-start.5) | collective-permute-done | bytes 294944 | tf_op jit(solution)/shard_map/ppermute | solution.py:40
  56.5 1.6 %collective-permute-start.8 = (bf16[9,64,256]{2,1,0:T(8,128)(2,1)S(1)}, bf16[9,64,256]{2,1,0:T(8,128)(2,1)S(1)}, u32[]{:S(2)}, u32[]{:S(2)}) collective-permute-start(bf16[9,64,256]{2,1,0:T(8,128)(2,1)S(1)} %collective-permute-done.6.refs_6_), channel_id=1, source_target_pairs={{0,8},{1,9},{2,10},{3,11},{4,0},{5,1},{6,2},{7,3},{8,12},{9,13},{1... | collective-permute-start | bytes 884744 | tf_op jit(solution)/shard_map/ppermute | solution.py:49
  58.1 1.5 %collective-permute-start.7 = (bf16[9,64,256]{2,1,0:T(8,128)(2,1)S(1)}, bf16[9,64,256]{2,1,0:T(8,128)(2,1)S(1)}, u32[]{:S(2)}, u32[]{:S(2)}) collective-permute-start(bf16[9,64,256]{2,1,0:T(8,128)(2,1)S(1)} %collective-permute-done.6.refs_6_), channel_id=1, source_target_pairs={{0,2},{1,3},{2,0},{3,1},{4,6},{5,7},{6,4},{7,5},{8,10},{9,11},{10,... | collective-permute-start | bytes 884744 | tf_op jit(solution)/shard_map/ppermute | solution.py:40
  59.6 0.7 collective-permute-done.16.refs_16_
  60.3 2.5 %collective-permute-done.15.refs_19_ = bf16[9,64,256]{2,1,0:T(8,128)(2,1)S(1)} collective-permute-done((bf16[9,64,256]{2,1,0:T(8,128)(2,1)S(1)}, bf16[9,64,256]{2,1,0:T(8,128)(2,1)S(1)}, u32[]{:S(2)}, u32[]{:S(2)}) %collective-permute-start.15) | collective-permute-done | bytes 294944 | tf_op jit(solution)/shard_map/ppermute | solution.py:40
  62.8 1.6 %collective-permute-start.19 = (bf16[4,64,256]{2,1,0:T(8,128)(2,1)S(1)}, bf16[4,64,256]{2,1,0:T(8,128)(2,1)S(1)}, u32[]{:S(2)}, u32[]{:S(2)}) collective-permute-start(bf16[4,64,256]{2,1,0:T(8,128)(2,1)S(1)} %slice.95), channel_id=1, source_target_pairs={{0,8},{1,9},{2,10},{3,11},{4,0},{5,1},{6,2},{7,3},{8,12},{9,13},{1... | collective-permute-start | bytes 393224 | tf_op jit(solution)/shard_map/ppermute | solution.py:49
  64.5 1.5 %collective-permute-start.18 = (bf16[5,64,256]{2,1,0:T(8,128)(2,1)S(1)}, bf16[5,64,256]{2,1,0:T(8,128)(2,1)S(1)}, u32[]{:S(2)}, u32[]{:S(2)}) collective-permute-start(bf16[5,64,256]{2,1,0:T(8,128)(2,1)S(1)} %slice.94), channel_id=1, source_target_pairs={{0,2},{1,3},{2,0},{3,1},{4,6},{5,7},{6,4},{7,5},{8,10},{9,11},{10,... | collective-permute-start | bytes 491528 | tf_op jit(solution)/shard_map/ppermute | solution.py:40
  66.6 2.5 %collective-permute-done.7.refs_10_ = bf16[9,64,256]{2,1,0:T(8,128)(2,1)S(1)} collective-permute-done((bf16[9,64,256]{2,1,0:T(8,128)(2,1)S(1)}, bf16[9,64,256]{2,1,0:T(8,128)(2,1)S(1)}, u32[]{:S(2)}, u32[]{:S(2)}) %collective-permute-start.7) | collective-permute-done | bytes 294944 | tf_op jit(solution)/shard_map/ppermute | solution.py:40
  69.3 1.6 %collective-permute-start.22 = (bf16[5,64,256]{2,1,0:T(8,128)(2,1)S(1)}, bf16[5,64,256]{2,1,0:T(8,128)(2,1)S(1)}, u32[]{:S(2)}, u32[]{:S(2)}) collective-permute-start(bf16[5,64,256]{2,1,0:T(8,128)(2,1)S(1)} %slice.98), channel_id=1, source_target_pairs={{0,2},{1,3},{2,0},{3,1},{4,6},{5,7},{6,4},{7,5},{8,10},{9,11},{10,... | collective-permute-start | bytes 491528 | tf_op jit(solution)/shard_map/ppermute | solution.py:40
  70.9 0.9 collective-permute-done.18.refs_20_
  71.7 2.1 %collective-permute-start.23 = (bf16[4,64,256]{2,1,0:T(8,128)(2,1)S(1)}, bf16[4,64,256]{2,1,0:T(8,128)(2,1)S(1)}, u32[]{:S(2)}, u32[]{:S(2)}) collective-permute-start(bf16[4,64,256]{2,1,0:T(8,128)(2,1)S(1)} %slice.99), channel_id=1, source_target_pairs={{0,8},{1,9},{2,10},{3,11},{4,0},{5,1},{6,2},{7,3},{8,12},{9,13},{1... | collective-permute-start | bytes 393224 | tf_op jit(solution)/shard_map/ppermute | solution.py:49
  73.8 1.0 collective-permute-start.21
  74.9 1.0 collective-permute-start.20
  75.9 0.9 collective-permute-done.23.refs_12_
  76.7 1.0 collective-permute-done.21.refs_3_
  77.7 1.0 collective-permute-done.20.refs_2_
  78.8 3.3 %shard_map.78 = (bf16[2,8,2,128,256]{4,3,2,1,0:T(8,128)(2,1)S(1)}, bf16[2,8,2,128,256]{4,3,2,1,0:T(8,128)(2,1)S(1)}, bf16[4,256,256]{2,1,0:T(8,128)(2,1)S(1)}) custom-call(bf16[7,64,256]{2,1,0:T(8,128)(2,1)S(1)} %collective-permute-done.9.refs_0_, bf16[7,64,256]{2,1,0:T(8,128)(2,1)S(1)} %collective-permute-done.17.refs_1_, ...), custom_call_target="tpu_custom_call" | custom-call | flops 2684354560 | bytes 10485760 | tf_op jit(solution)/shard_map/pallas_call | solution.py:170
  82.1 1.7 %shard_map.79 = f32[16,8,128]{2,1,0:T(8,128)S(1)} custom-call(bf16[32,128,256]{2,1,0:T(8,128)(2,1)S(1)} %copy-done.1, bf16[32,128,256]{2,1,0:T(8,128)(2,1)S(1)} %collective-permute-done.rot_theirs, bf16[4,256,256]{2,1,0:T(8,128)(2,1)S(1)} %get-tuple-element.67.inverses, bf16[2,8,2,128,256]{4,3,2,1,0:T(8,128)(2,1)S(1)} %get-tuple-element.68.refs_0_.refs_1_.refs_2_, ...), custom_call_target="tpu_custom_call" | custom-call | flops 402653184 | bytes 4718592 | tf_op jit(solution)/shard_map/pallas_call | solution.py:232
  83.9 9.9 %all_to_all.5.parts = f32[16,8,128]{2,1,0:T(8,128)S(1)} all-to-all(f32[16,8,128]{2,1,0:T(8,128)S(1)} %shard_map.79), channel_id=1, replica_groups=mesh['walk'=2,'chol'=16] {'chol'}, dimensions={0} | all-to-all | bytes 131072 | tf_op jit(solution)/shard_map/all_to_all | solution.py:561
  93.7 3.2 %shard_map.80 = (f32[8,32]{1,0:T(8,128)}, bf16[4,128,2048]{2,1,0:T(8,128)(2,1)S(1)}, bf16[4,64,2048]{2,1,0:T(8,128)(2,1)S(1)}, bf16[4,64,2048]{2,1,0:T(8,128)(2,1)S(1)}) custom-call(s32[8]{0:T(128)S(1)} %copy-done.3, f32[8,32]{1,0:T(8,128)S(1)} %copy-done.2, f32[16,8,128]{2,1,0:T(8,128)S(1)} %all_to_all.5.parts, bf16[32,128,2048]{2,1,0:T(8,128)(2,1)S(1)} %copy-done), custom_call_target="tpu_custom_call" | custom-call | tf_op jit(solution)/shard_map/pallas_call | solution.py:298
  97.5 0.8 shard_map.81
  99.7 1.5 %collective-permute-done.25.refs_1_ = bf16[4,64,2048]{2,1,0:T(8,128)(2,1)S(1)} collective-permute-done((bf16[4,64,2048]{2,1,0:T(8,128)(2,1)S(1)}, bf16[4,64,2048]{2,1,0:T(8,128)(2,1)S(1)}, u32[]{:S(2)}, u32[]{:S(2)}) %collective-permute-start.25) | collective-permute-done | bytes 1048608 | tf_op jit(solution)/shard_map/ppermute | solution.py:40
  101.2 0.8 shard_map.82
  102.9 4.7 %collective-permute-done.27.refs_4_ = bf16[4,128,256]{2,1,0:T(8,128)(2,1)S(1)} collective-permute-done((bf16[4,128,256]{2,1,0:T(8,128)(2,1)S(1)}, bf16[4,128,256]{2,1,0:T(8,128)(2,1)S(1)}, u32[]{:S(2)}, u32[]{:S(2)}) %collective-permute-start.27) | collective-permute-done | bytes 262176 | tf_op jit(solution)/shard_map/ppermute | solution.py:49
  107.8 0.9 collective-permute-start.29
  108.7 0.7 collective-permute-start.28
  109.3 3.8 %collective-permute-done.35.refs_13_ = bf16[4,128,256]{2,1,0:T(8,128)(2,1)S(1)} collective-permute-done((bf16[4,128,256]{2,1,0:T(8,128)(2,1)S(1)}, bf16[4,128,256]{2,1,0:T(8,128)(2,1)S(1)}, u32[]{:S(2)}, u32[]{:S(2)}) %collective-permute-start.35) | collective-permute-done | bytes 262176 | tf_op jit(solution)/shard_map/ppermute | solution.py:49
  113.4 0.9 collective-permute-start.37
  115.0 3.8 %collective-permute-done.29.refs_5_ = bf16[4,128,256]{2,1,0:T(8,128)(2,1)S(1)} collective-permute-done((bf16[4,128,256]{2,1,0:T(8,128)(2,1)S(1)}, bf16[4,128,256]{2,1,0:T(8,128)(2,1)S(1)}, u32[]{:S(2)}, u32[]{:S(2)}) %collective-permute-start.29) | collective-permute-done | bytes 262176 | tf_op jit(solution)/shard_map/ppermute | solution.py:49
  119.0 0.9 collective-permute-start.31
  120.6 3.8 %collective-permute-done.37.refs_14_ = bf16[4,128,256]{2,1,0:T(8,128)(2,1)S(1)} collective-permute-done((bf16[4,128,256]{2,1,0:T(8,128)(2,1)S(1)}, bf16[4,128,256]{2,1,0:T(8,128)(2,1)S(1)}, u32[]{:S(2)}, u32[]{:S(2)}) %collective-permute-start.37) | collective-permute-done | bytes 262176 | tf_op jit(solution)/shard_map/ppermute | solution.py:49
  124.6 0.9 collective-permute-start.39
  126.2 3.8 %collective-permute-done.31.refs_6_ = bf16[4,128,256]{2,1,0:T(8,128)(2,1)S(1)} collective-permute-done((bf16[4,128,256]{2,1,0:T(8,128)(2,1)S(1)}, bf16[4,128,256]{2,1,0:T(8,128)(2,1)S(1)}, u32[]{:S(2)}, u32[]{:S(2)}) %collective-permute-start.31) | collective-permute-done | bytes 262176 | tf_op jit(solution)/shard_map/ppermute | solution.py:49
  130.3 1.0 collective-permute-start.33
  131.9 3.7 %collective-permute-done.39.refs_15_ = bf16[4,128,256]{2,1,0:T(8,128)(2,1)S(1)} collective-permute-done((bf16[4,128,256]{2,1,0:T(8,128)(2,1)S(1)}, bf16[4,128,256]{2,1,0:T(8,128)(2,1)S(1)}, u32[]{:S(2)}, u32[]{:S(2)}) %collective-permute-start.39) | collective-permute-done | bytes 262176 | tf_op jit(solution)/shard_map/ppermute | solution.py:49
  135.9 1.0 collective-permute-start.41
  137.5 0.9 collective-permute-done.33.refs_11_
  138.4 2.5 %collective-permute-done.41.refs_20_ = bf16[2,128,256]{2,1,0:T(8,128)(2,1)S(1)} collective-permute-done((bf16[2,128,256]{2,1,0:T(8,128)(2,1)S(1)}, bf16[2,128,256]{2,1,0:T(8,128)(2,1)S(1)}, u32[]{:S(2)}, u32[]{:S(2)}) %collective-permute-start.41) | collective-permute-done | bytes 131104 | tf_op jit(solution)/shard_map/ppermute | solution.py:49
  140.9 0.9 collective-permute-done.40.refs_19_
  141.8 1.0 shard_map.83
  142.9 0.7 shard_map.84.mine
  143.7 0.8 collective-permute-done.42.theirs
  144.5 1.4 shard_map.85
  (72 shorter events, 9.3 us)
Async XLA Ops:
  0.6 31.8 %copy-start.4 = (bf16[128,256]{1,0:T(8,128)(2,1)S(1)}, bf16[128,256]{1,0:T(8,128)(2,1)}, u32[]{:S(2)}) copy-start(bf16[128,256]{1,0:T(8,128)(2,1)} %param.7) | copy-start | bytes 196612
  0.6 31.8 %copy-start.1 = (bf16[32,128,256]{2,1,0:T(8,128)(2,1)S(1)}, bf16[32,128,256]{2,1,0:T(8,128)(2,1)}, u32[]{:S(2)}) copy-start(bf16[32,128,256]{2,1,0:T(8,128)(2,1)} %rot_mine.1) | copy-start | bytes 6291460
  19.1 10.0 %collective-permute-start.1 = (bf16[2,128,256]{2,1,0:T(8,128)(2,1)}, bf16[2,128,256]{2,1,0:T(8,128)(2,1)S(1)}, u32[]{:S(2)}, u32[]{:S(2)}) collective-permute-start(bf16[2,128,256]{2,1,0:T(8,128)(2,1)} %get-tuple-element.48), channel_id=1, source_target_pairs={{0,16},{1,17},{2,18},{3,19},{4,20},{5,21},{6,22},{7,23},{8,24},{9,... | collective-permute-start | bytes 393224 | tf_op jit(solution)/shard_map/ppermute | solution.py:503
  22.1 7.0 %collective-permute-start.2 = (bf16[2,128,256]{2,1,0:T(8,128)(2,1)}, bf16[2,128,256]{2,1,0:T(8,128)(2,1)S(1)}, u32[]{:S(2)}, u32[]{:S(2)}) collective-permute-start(bf16[2,128,256]{2,1,0:T(8,128)(2,1)} %get-tuple-element.49), channel_id=1, source_target_pairs={{0,17},{1,16},{2,19},{3,18},{4,21},{5,20},{6,23},{7,22},{8,25},{9,... | collective-permute-start | bytes 393224 | tf_op jit(solution)/shard_map/ppermute | solution.py:504
  22.1 1.6 %collective-permute-start.10 = (bf16[2,128,256]{2,1,0:T(8,128)(2,1)}, bf16[2,128,256]{2,1,0:T(8,128)(2,1)S(1)}, u32[]{:S(2)}, u32[]{:S(2)}) collective-permute-start(bf16[2,128,256]{2,1,0:T(8,128)(2,1)} %get-tuple-element.57), channel_id=1, source_target_pairs={{0,1},{1,0},{2,3},{3,2},{4,5},{5,4},{6,7},{7,6},{8,9},{9,8},{10,11... | collective-permute-start | bytes 393224 | tf_op jit(solution)/shard_map/ppermute | solution.py:40
  24.7 10.3 %collective-permute-start.12 = (bf16[9,64,256]{2,1,0:T(8,128)(2,1)S(1)}, bf16[9,64,256]{2,1,0:T(8,128)(2,1)S(1)}, u32[]{:S(2)}, u32[]{:S(2)}) collective-permute-start(bf16[9,64,256]{2,1,0:T(8,128)(2,1)S(1)} %pad_maximum_fusion.1.refs_13_), channel_id=1, source_target_pairs={{0,8},{1,9},{2,10},{3,11},{4,0},{5,1},{6,2},{7,3},{8,12},{9,13},{1... | collective-permute-start | bytes 884744 | tf_op jit(solution)/shard_map/ppermute | solution.py:49
  27.6 9.9 %collective-permute-start.11 = (bf16[9,64,256]{2,1,0:T(8,128)(2,1)S(1)}, bf16[9,64,256]{2,1,0:T(8,128)(2,1)S(1)}, u32[]{:S(2)}, u32[]{:S(2)}) collective-permute-start(bf16[9,64,256]{2,1,0:T(8,128)(2,1)S(1)} %pad_maximum_fusion.1.refs_13_), channel_id=1, source_target_pairs={{0,2},{1,3},{2,0},{3,1},{4,6},{5,7},{6,4},{7,5},{8,10},{9,11},{10,... | collective-permute-start | bytes 884744 | tf_op jit(solution)/shard_map/ppermute | solution.py:40
  29.3 12.0 %collective-permute-start.4 = (bf16[9,64,256]{2,1,0:T(8,128)(2,1)S(1)}, bf16[9,64,256]{2,1,0:T(8,128)(2,1)S(1)}, u32[]{:S(2)}, u32[]{:S(2)}) collective-permute-start(bf16[9,64,256]{2,1,0:T(8,128)(2,1)S(1)} %pad_maximum_fusion.refs_4_), channel_id=1, source_target_pairs={{0,8},{1,9},{2,10},{3,11},{4,0},{5,1},{6,2},{7,3},{8,12},{9,13},{1... | collective-permute-start | bytes 884744 | tf_op jit(solution)/shard_map/ppermute | solution.py:49
  30.9 12.9 %collective-permute-start.3 = (bf16[9,64,256]{2,1,0:T(8,128)(2,1)S(1)}, bf16[9,64,256]{2,1,0:T(8,128)(2,1)S(1)}, u32[]{:S(2)}, u32[]{:S(2)}) collective-permute-start(bf16[9,64,256]{2,1,0:T(8,128)(2,1)S(1)} %pad_maximum_fusion.refs_4_), channel_id=1, source_target_pairs={{0,2},{1,3},{2,0},{3,1},{4,6},{5,7},{6,4},{7,5},{8,10},{9,11},{10,... | collective-permute-start | bytes 884744 | tf_op jit(solution)/shard_map/ppermute | solution.py:40
  32.4 49.7 %collective-permute-start = (bf16[32,128,256]{2,1,0:T(8,128)(2,1)S(1)}, bf16[32,128,256]{2,1,0:T(8,128)(2,1)S(1)}, u32[]{:S(2)}, u32[]{:S(2)}) collective-permute-start(bf16[32,128,256]{2,1,0:T(8,128)(2,1)S(1)} %copy-done.1), channel_id=1, source_target_pairs={{0,1},{1,0},{2,3},{3,2},{4,5},{5,4},{6,7},{7,6},{8,9},{9,8},{10,11... | collective-permute-start | bytes 6291464 | tf_op jit(solution)/shard_map/ppermute | solution.py:40
  37.5 10.1 %collective-permute-start.14 = (bf16[9,64,256]{2,1,0:T(8,128)(2,1)S(1)}, bf16[9,64,256]{2,1,0:T(8,128)(2,1)S(1)}, u32[]{:S(2)}, u32[]{:S(2)}) collective-permute-start(bf16[9,64,256]{2,1,0:T(8,128)(2,1)S(1)} %collective-permute-done.12.refs_14_), channel_id=1, source_target_pairs={{0,8},{1,9},{2,10},{3,11},{4,0},{5,1},{6,2},{7,3},{8,12},{9,13},{1... | collective-permute-start | bytes 884744 | tf_op jit(solution)/shard_map/ppermute | solution.py:49
  39.1 11.1 %collective-permute-start.13 = (bf16[9,64,256]{2,1,0:T(8,128)(2,1)S(1)}, bf16[9,64,256]{2,1,0:T(8,128)(2,1)S(1)}, u32[]{:S(2)}, u32[]{:S(2)}) collective-permute-start(bf16[9,64,256]{2,1,0:T(8,128)(2,1)S(1)} %collective-permute-done.12.refs_14_), channel_id=1, source_target_pairs={{0,2},{1,3},{2,0},{3,1},{4,6},{5,7},{6,4},{7,5},{8,10},{9,11},{10,... | collective-permute-start | bytes 884744 | tf_op jit(solution)/shard_map/ppermute | solution.py:40
  43.8 10.1 %collective-permute-start.6 = (bf16[9,64,256]{2,1,0:T(8,128)(2,1)S(1)}, bf16[9,64,256]{2,1,0:T(8,128)(2,1)S(1)}, u32[]{:S(2)}, u32[]{:S(2)}) collective-permute-start(bf16[9,64,256]{2,1,0:T(8,128)(2,1)S(1)} %collective-permute-done.4.refs_5_), channel_id=1, source_target_pairs={{0,8},{1,9},{2,10},{3,11},{4,0},{5,1},{6,2},{7,3},{8,12},{9,13},{1... | collective-permute-start | bytes 884744 | tf_op jit(solution)/shard_map/ppermute | solution.py:49
  45.4 11.1 %collective-permute-start.5 = (bf16[9,64,256]{2,1,0:T(8,128)(2,1)S(1)}, bf16[9,64,256]{2,1,0:T(8,128)(2,1)S(1)}, u32[]{:S(2)}, u32[]{:S(2)}) collective-permute-start(bf16[9,64,256]{2,1,0:T(8,128)(2,1)S(1)} %collective-permute-done.4.refs_5_), channel_id=1, source_target_pairs={{0,2},{1,3},{2,0},{3,1},{4,6},{5,7},{6,4},{7,5},{8,10},{9,11},{10,... | collective-permute-start | bytes 884744 | tf_op jit(solution)/shard_map/ppermute | solution.py:40
  50.2 10.1 %collective-permute-start.16 = (bf16[9,64,256]{2,1,0:T(8,128)(2,1)S(1)}, bf16[9,64,256]{2,1,0:T(8,128)(2,1)S(1)}, u32[]{:S(2)}, u32[]{:S(2)}) collective-permute-start(bf16[9,64,256]{2,1,0:T(8,128)(2,1)S(1)} %collective-permute-done.14.refs_15_), channel_id=1, source_target_pairs={{0,8},{1,9},{2,10},{3,11},{4,0},{5,1},{6,2},{7,3},{8,12},{9,13},{1... | collective-permute-start | bytes 884744 | tf_op jit(solution)/shard_map/ppermute | solution.py:49
  51.7 11.1 %collective-permute-start.15 = (bf16[9,64,256]{2,1,0:T(8,128)(2,1)S(1)}, bf16[9,64,256]{2,1,0:T(8,128)(2,1)S(1)}, u32[]{:S(2)}, u32[]{:S(2)}) collective-permute-start(bf16[9,64,256]{2,1,0:T(8,128)(2,1)S(1)} %collective-permute-done.14.refs_15_), channel_id=1, source_target_pairs={{0,2},{1,3},{2,0},{3,1},{4,6},{5,7},{6,4},{7,5},{8,10},{9,11},{10,... | collective-permute-start | bytes 884744 | tf_op jit(solution)/shard_map/ppermute | solution.py:40
  56.5 10.1 %collective-permute-start.8 = (bf16[9,64,256]{2,1,0:T(8,128)(2,1)S(1)}, bf16[9,64,256]{2,1,0:T(8,128)(2,1)S(1)}, u32[]{:S(2)}, u32[]{:S(2)}) collective-permute-start(bf16[9,64,256]{2,1,0:T(8,128)(2,1)S(1)} %collective-permute-done.6.refs_6_), channel_id=1, source_target_pairs={{0,8},{1,9},{2,10},{3,11},{4,0},{5,1},{6,2},{7,3},{8,12},{9,13},{1... | collective-permute-start | bytes 884744 | tf_op jit(solution)/shard_map/ppermute | solution.py:49
  58.1 11.1 %collective-permute-start.7 = (bf16[9,64,256]{2,1,0:T(8,128)(2,1)S(1)}, bf16[9,64,256]{2,1,0:T(8,128)(2,1)S(1)}, u32[]{:S(2)}, u32[]{:S(2)}) collective-permute-start(bf16[9,64,256]{2,1,0:T(8,128)(2,1)S(1)} %collective-permute-done.6.refs_6_), channel_id=1, source_target_pairs={{0,2},{1,3},{2,0},{3,1},{4,6},{5,7},{6,4},{7,5},{8,10},{9,11},{10,... | collective-permute-start | bytes 884744 | tf_op jit(solution)/shard_map/ppermute | solution.py:40
  62.8 6.4 %collective-permute-start.19 = (bf16[4,64,256]{2,1,0:T(8,128)(2,1)S(1)}, bf16[4,64,256]{2,1,0:T(8,128)(2,1)S(1)}, u32[]{:S(2)}, u32[]{:S(2)}) collective-permute-start(bf16[4,64,256]{2,1,0:T(8,128)(2,1)S(1)} %slice.95), channel_id=1, source_target_pairs={{0,8},{1,9},{2,10},{3,11},{4,0},{5,1},{6,2},{7,3},{8,12},{9,13},{1... | collective-permute-start | bytes 393224 | tf_op jit(solution)/shard_map/ppermute | solution.py:49
  64.5 7.3 %collective-permute-start.18 = (bf16[5,64,256]{2,1,0:T(8,128)(2,1)S(1)}, bf16[5,64,256]{2,1,0:T(8,128)(2,1)S(1)}, u32[]{:S(2)}, u32[]{:S(2)}) collective-permute-start(bf16[5,64,256]{2,1,0:T(8,128)(2,1)S(1)} %slice.94), channel_id=1, source_target_pairs={{0,2},{1,3},{2,0},{3,1},{4,6},{5,7},{6,4},{7,5},{8,10},{9,11},{10,... | collective-permute-start | bytes 491528 | tf_op jit(solution)/shard_map/ppermute | solution.py:40
  66.6 7.2 %collective-permute-start.17 = (bf16[7,64,256]{2,1,0:T(8,128)(2,1)S(1)}, bf16[7,64,256]{2,1,0:T(8,128)(2,1)S(1)}, u32[]{:S(2)}, u32[]{:S(2)}) collective-permute-start(bf16[7,64,256]{2,1,0:T(8,128)(2,1)S(1)} %slice_dynamic-update-slice_fusion), channel_id=1, source_target_pairs={{0,1},{1,0},{2,3},{3,2},{4,5},{5,4},{6,7},{7,6},{8,9},{9,8},{10,11... | collective-permute-start | bytes 688136 | tf_op jit(solution)/shard_map/ppermute | solution.py:40
  69.1 5.7 %collective-permute-start.9 = (bf16[7,64,256]{2,1,0:T(8,128)(2,1)S(1)}, bf16[7,64,256]{2,1,0:T(8,128)(2,1)S(1)}, u32[]{:S(2)}, u32[]{:S(2)}) collective-permute-start(bf16[7,64,256]{2,1,0:T(8,128)(2,1)S(1)} %slice_dynamic-update-slice_fusion.6), channel_id=1, source_target_pairs={{0,1},{1,0},{2,3},{3,2},{4,5},{5,4},{6,7},{7,6},{8,9},{9,8},{10,11... | collective-permute-start | bytes 688136 | tf_op jit(solution)/shard_map/ppermute | solution.py:40
  69.3 7.5 %collective-permute-start.22 = (bf16[5,64,256]{2,1,0:T(8,128)(2,1)S(1)}, bf16[5,64,256]{2,1,0:T(8,128)(2,1)S(1)}, u32[]{:S(2)}, u32[]{:S(2)}) collective-permute-start(bf16[5,64,256]{2,1,0:T(8,128)(2,1)S(1)} %slice.98), channel_id=1, source_target_pairs={{0,2},{1,3},{2,0},{3,1},{4,6},{5,7},{6,4},{7,5},{8,10},{9,11},{10,... | collective-permute-start | bytes 491528 | tf_op jit(solution)/shard_map/ppermute | solution.py:40
  71.7 5.0 %collective-permute-start.23 = (bf16[4,64,256]{2,1,0:T(8,128)(2,1)S(1)}, bf16[4,64,256]{2,1,0:T(8,128)(2,1)S(1)}, u32[]{:S(2)}, u32[]{:S(2)}) collective-permute-start(bf16[4,64,256]{2,1,0:T(8,128)(2,1)S(1)} %slice.99), channel_id=1, source_target_pairs={{0,8},{1,9},{2,10},{3,11},{4,0},{5,1},{6,2},{7,3},{8,12},{9,13},{1... | collective-permute-start | bytes 393224 | tf_op jit(solution)/shard_map/ppermute | solution.py:49
  73.8 3.9 %collective-permute-start.21 = (bf16[1,64,256]{2,1,0:T(8,128)(2,1)S(1)}, bf16[1,64,256]{2,1,0:T(8,128)(2,1)S(1)}, u32[]{:S(2)}, u32[]{:S(2)}) collective-permute-start(bf16[1,64,256]{2,1,0:T(8,128)(2,1)S(1)} %slice.97), channel_id=1, source_target_pairs={{0,2},{1,3},{2,0},{3,1},{4,6},{5,7},{6,4},{7,5},{8,10},{9,11},{10,... | collective-permute-start | bytes 98312 | tf_op jit(solution)/shard_map/ppermute | solution.py:40
  74.9 3.9 %collective-permute-start.20 = (bf16[1,64,256]{2,1,0:T(8,128)(2,1)S(1)}, bf16[1,64,256]{2,1,0:T(8,128)(2,1)S(1)}, u32[]{:S(2)}, u32[]{:S(2)}) collective-permute-start(bf16[1,64,256]{2,1,0:T(8,128)(2,1)S(1)} %slice.104), channel_id=1, source_target_pairs={{0,2},{1,3},{2,0},{3,1},{4,6},{5,7},{6,4},{7,5},{8,10},{9,11},{10,... | collective-permute-start | bytes 98312 | tf_op jit(solution)/shard_map/ppermute | solution.py:40
  78.8 15.0 %copy-start = (bf16[32,128,2048]{2,1,0:T(8,128)(2,1)S(1)}, bf16[32,128,2048]{2,1,0:T(8,128)(2,1)}, u32[]{:S(2)}) copy-start(bf16[32,128,2048]{2,1,0:T(8,128)(2,1)} %cholesky.1) | copy-start | bytes 50331652
  82.1 11.6 %copy-start.2 = (f32[8,32]{1,0:T(8,128)S(1)}, f32[8,32]{1,0:T(8,128)}, u32[]{:S(2)}) copy-start(f32[8,32]{1,0:T(8,128)} %fields.1) | copy-start | bytes 3076
  82.1 11.6 %copy-start.3 = (s32[8]{0:T(128)S(1)}, s32[8]{0:T(128)}, u32[]{:S(2)}) copy-start(s32[8]{0:T(128)} %get-tuple-element.47.order) | copy-start | bytes 100
  96.9 2.7 %collective-permute-start.24 = (bf16[4,64,2048]{2,1,0:T(8,128)(2,1)S(1)}, bf16[4,64,2048]{2,1,0:T(8,128)(2,1)S(1)}, u32[]{:S(2)}, u32[]{:S(2)}) collective-permute-start(bf16[4,64,2048]{2,1,0:T(8,128)(2,1)S(1)} %get-tuple-element.72), channel_id=1, source_target_pairs={{0,1},{1,0},{2,3},{3,2},{4,5},{5,4},{6,7},{7,6},{8,9},{9,8},{10,11... | collective-permute-start | bytes 3145736 | tf_op jit(solution)/shard_map/ppermute | solution.py:40
  97.0 4.1 %collective-permute-start.25 = (bf16[4,64,2048]{2,1,0:T(8,128)(2,1)S(1)}, bf16[4,64,2048]{2,1,0:T(8,128)(2,1)S(1)}, u32[]{:S(2)}, u32[]{:S(2)}) collective-permute-start(bf16[4,64,2048]{2,1,0:T(8,128)(2,1)S(1)} %get-tuple-element.73), channel_id=1, source_target_pairs={{0,1},{1,0},{2,3},{3,2},{4,5},{5,4},{6,7},{7,6},{8,9},{9,8},{10,11... | collective-permute-start | bytes 3145736 | tf_op jit(solution)/shard_map/ppermute | solution.py:40
  98.3 9.2 %collective-permute-start.27 = (bf16[4,128,256]{2,1,0:T(8,128)(2,1)S(1)}, bf16[4,128,256]{2,1,0:T(8,128)(2,1)S(1)}, u32[]{:S(2)}, u32[]{:S(2)}) collective-permute-start(bf16[4,128,256]{2,1,0:T(8,128)(2,1)S(1)} %get-tuple-element.75.refs_3_), channel_id=1, source_target_pairs={{0,8},{1,9},{2,10},{3,11},{4,0},{5,1},{6,2},{7,3},{8,12},{9,13},{1... | collective-permute-start | bytes 786440 | tf_op jit(solution)/shard_map/ppermute | solution.py:49
  98.6 9.2 %collective-permute-start.26 = (bf16[4,128,256]{2,1,0:T(8,128)(2,1)S(1)}, bf16[4,128,256]{2,1,0:T(8,128)(2,1)S(1)}, u32[]{:S(2)}, u32[]{:S(2)}) collective-permute-start(bf16[4,128,256]{2,1,0:T(8,128)(2,1)S(1)} %get-tuple-element.75.refs_3_), channel_id=1, source_target_pairs={{0,2},{1,3},{2,0},{3,1},{4,6},{5,7},{6,4},{7,5},{8,10},{9,11},{10,... | collective-permute-start | bytes 786440 | tf_op jit(solution)/shard_map/ppermute | solution.py:40
  102.0 11.2 %collective-permute-start.35 = (bf16[4,128,256]{2,1,0:T(8,128)(2,1)S(1)}, bf16[4,128,256]{2,1,0:T(8,128)(2,1)S(1)}, u32[]{:S(2)}, u32[]{:S(2)}) collective-permute-start(bf16[4,128,256]{2,1,0:T(8,128)(2,1)S(1)} %get-tuple-element.82.refs_12_), channel_id=1, source_target_pairs={{0,8},{1,9},{2,10},{3,11},{4,0},{5,1},{6,2},{7,3},{8,12},{9,13},{1... | collective-permute-start | bytes 786440 | tf_op jit(solution)/shard_map/ppermute | solution.py:49
  102.2 11.1 %collective-permute-start.34 = (bf16[4,128,256]{2,1,0:T(8,128)(2,1)S(1)}, bf16[4,128,256]{2,1,0:T(8,128)(2,1)S(1)}, u32[]{:S(2)}, u32[]{:S(2)}) collective-permute-start(bf16[4,128,256]{2,1,0:T(8,128)(2,1)S(1)} %get-tuple-element.82.refs_12_), channel_id=1, source_target_pairs={{0,2},{1,3},{2,0},{3,1},{4,6},{5,7},{6,4},{7,5},{8,10},{9,11},{10,... | collective-permute-start | bytes 786440 | tf_op jit(solution)/shard_map/ppermute | solution.py:40
  107.8 11.0 %collective-permute-start.29 = (bf16[4,128,256]{2,1,0:T(8,128)(2,1)S(1)}, bf16[4,128,256]{2,1,0:T(8,128)(2,1)S(1)}, u32[]{:S(2)}, u32[]{:S(2)}) collective-permute-start(bf16[4,128,256]{2,1,0:T(8,128)(2,1)S(1)} %collective-permute-done.27.refs_4_), channel_id=1, source_target_pairs={{0,8},{1,9},{2,10},{3,11},{4,0},{5,1},{6,2},{7,3},{8,12},{9,13},{1... | collective-permute-start | bytes 786440 | tf_op jit(solution)/shard_map/ppermute | solution.py:49
  108.7 10.3 %collective-permute-start.28 = (bf16[4,128,256]{2,1,0:T(8,128)(2,1)S(1)}, bf16[4,128,256]{2,1,0:T(8,128)(2,1)S(1)}, u32[]{:S(2)}, u32[]{:S(2)}) collective-permute-start(bf16[4,128,256]{2,1,0:T(8,128)(2,1)S(1)} %collective-permute-done.27.refs_4_), channel_id=1, source_target_pairs={{0,2},{1,3},{2,0},{3,1},{4,6},{5,7},{6,4},{7,5},{8,10},{9,11},{10,... | collective-permute-start | bytes 786440 | tf_op jit(solution)/shard_map/ppermute | solution.py:40
  113.4 11.0 %collective-permute-start.37 = (bf16[4,128,256]{2,1,0:T(8,128)(2,1)S(1)}, bf16[4,128,256]{2,1,0:T(8,128)(2,1)S(1)}, u32[]{:S(2)}, u32[]{:S(2)}) collective-permute-start(bf16[4,128,256]{2,1,0:T(8,128)(2,1)S(1)} %collective-permute-done.35.refs_13_), channel_id=1, source_target_pairs={{0,8},{1,9},{2,10},{3,11},{4,0},{5,1},{6,2},{7,3},{8,12},{9,13},{1... | collective-permute-start | bytes 786440 | tf_op jit(solution)/shard_map/ppermute | solution.py:49
  114.3 10.3 %collective-permute-start.36 = (bf16[4,128,256]{2,1,0:T(8,128)(2,1)S(1)}, bf16[4,128,256]{2,1,0:T(8,128)(2,1)S(1)}, u32[]{:S(2)}, u32[]{:S(2)}) collective-permute-start(bf16[4,128,256]{2,1,0:T(8,128)(2,1)S(1)} %collective-permute-done.35.refs_13_), channel_id=1, source_target_pairs={{0,2},{1,3},{2,0},{3,1},{4,6},{5,7},{6,4},{7,5},{8,10},{9,11},{10,... | collective-permute-start | bytes 786440 | tf_op jit(solution)/shard_map/ppermute | solution.py:40
  119.0 11.0 %collective-permute-start.31 = (bf16[4,128,256]{2,1,0:T(8,128)(2,1)S(1)}, bf16[4,128,256]{2,1,0:T(8,128)(2,1)S(1)}, u32[]{:S(2)}, u32[]{:S(2)}) collective-permute-start(bf16[4,128,256]{2,1,0:T(8,128)(2,1)S(1)} %collective-permute-done.29.refs_5_), channel_id=1, source_target_pairs={{0,8},{1,9},{2,10},{3,11},{4,0},{5,1},{6,2},{7,3},{8,12},{9,13},{1... | collective-permute-start | bytes 786440 | tf_op jit(solution)/shard_map/ppermute | solution.py:49
  119.9 10.3 %collective-permute-start.30 = (bf16[4,128,256]{2,1,0:T(8,128)(2,1)S(1)}, bf16[4,128,256]{2,1,0:T(8,128)(2,1)S(1)}, u32[]{:S(2)}, u32[]{:S(2)}) collective-permute-start(bf16[4,128,256]{2,1,0:T(8,128)(2,1)S(1)} %collective-permute-done.29.refs_5_), channel_id=1, source_target_pairs={{0,2},{1,3},{2,0},{3,1},{4,6},{5,7},{6,4},{7,5},{8,10},{9,11},{10,... | collective-permute-start | bytes 786440 | tf_op jit(solution)/shard_map/ppermute | solution.py:40
  124.6 11.0 %collective-permute-start.39 = (bf16[4,128,256]{2,1,0:T(8,128)(2,1)S(1)}, bf16[4,128,256]{2,1,0:T(8,128)(2,1)S(1)}, u32[]{:S(2)}, u32[]{:S(2)}) collective-permute-start(bf16[4,128,256]{2,1,0:T(8,128)(2,1)S(1)} %collective-permute-done.37.refs_14_), channel_id=1, source_target_pairs={{0,8},{1,9},{2,10},{3,11},{4,0},{5,1},{6,2},{7,3},{8,12},{9,13},{1... | collective-permute-start | bytes 786440 | tf_op jit(solution)/shard_map/ppermute | solution.py:49
  125.5 10.3 %collective-permute-start.38 = (bf16[4,128,256]{2,1,0:T(8,128)(2,1)S(1)}, bf16[4,128,256]{2,1,0:T(8,128)(2,1)S(1)}, u32[]{:S(2)}, u32[]{:S(2)}) collective-permute-start(bf16[4,128,256]{2,1,0:T(8,128)(2,1)S(1)} %collective-permute-done.37.refs_14_), channel_id=1, source_target_pairs={{0,2},{1,3},{2,0},{3,1},{4,6},{5,7},{6,4},{7,5},{8,10},{9,11},{10,... | collective-permute-start | bytes 786440 | tf_op jit(solution)/shard_map/ppermute | solution.py:40
  130.3 8.2 %collective-permute-start.33 = (bf16[2,128,256]{2,1,0:T(8,128)(2,1)S(1)}, bf16[2,128,256]{2,1,0:T(8,128)(2,1)S(1)}, u32[]{:S(2)}, u32[]{:S(2)}) collective-permute-start(bf16[2,128,256]{2,1,0:T(8,128)(2,1)S(1)} %slice.101), channel_id=1, source_target_pairs={{0,8},{1,9},{2,10},{3,11},{4,0},{5,1},{6,2},{7,3},{8,12},{9,13},{1... | collective-permute-start | bytes 393224 | tf_op jit(solution)/shard_map/ppermute | solution.py:49
  131.2 7.2 %collective-permute-start.32 = (bf16[2,128,256]{2,1,0:T(8,128)(2,1)S(1)}, bf16[2,128,256]{2,1,0:T(8,128)(2,1)S(1)}, u32[]{:S(2)}, u32[]{:S(2)}) collective-permute-start(bf16[2,128,256]{2,1,0:T(8,128)(2,1)S(1)} %slice.100), channel_id=1, source_target_pairs={{0,2},{1,3},{2,0},{3,1},{4,6},{5,7},{6,4},{7,5},{8,10},{9,11},{10,... | collective-permute-start | bytes 393224 | tf_op jit(solution)/shard_map/ppermute | solution.py:40
  135.9 5.0 %collective-permute-start.41 = (bf16[2,128,256]{2,1,0:T(8,128)(2,1)S(1)}, bf16[2,128,256]{2,1,0:T(8,128)(2,1)S(1)}, u32[]{:S(2)}, u32[]{:S(2)}) collective-permute-start(bf16[2,128,256]{2,1,0:T(8,128)(2,1)S(1)} %slice.103), channel_id=1, source_target_pairs={{0,8},{1,9},{2,10},{3,11},{4,0},{5,1},{6,2},{7,3},{8,12},{9,13},{1... | collective-permute-start | bytes 393224 | tf_op jit(solution)/shard_map/ppermute | solution.py:49
  136.9 5.0 %collective-permute-start.40 = (bf16[2,128,256]{2,1,0:T(8,128)(2,1)S(1)}, bf16[2,128,256]{2,1,0:T(8,128)(2,1)S(1)}, u32[]{:S(2)}, u32[]{:S(2)}) collective-permute-start(bf16[2,128,256]{2,1,0:T(8,128)(2,1)S(1)} %slice.102), channel_id=1, source_target_pairs={{0,2},{1,3},{2,0},{3,1},{4,6},{5,7},{6,4},{7,5},{8,10},{9,11},{10,... | collective-permute-start | bytes 393224 | tf_op jit(solution)/shard_map/ppermute | solution.py:40
  142.9 1.6 %collective-permute-start.42 = (bf16[4,128,256]{2,1,0:T(8,128)(2,1)S(1)}, bf16[4,128,256]{2,1,0:T(8,128)(2,1)S(1)}, u32[]{:S(2)}, u32[]{:S(2)}) collective-permute-start(bf16[4,128,256]{2,1,0:T(8,128)(2,1)S(1)} %get-tuple-element.90), channel_id=1, source_target_pairs={{0,1},{1,0},{2,3},{3,2},{4,5},{5,4},{6,7},{7,6},{8,9},{9,8},{10,11... | collective-permute-start | bytes 786440 | tf_op jit(solution)/shard_map/ppermute | solution.py:40

commit v15 on v14

--- a/solution.py
+++ b/solution.py
@@ -105,6 +105,28 @@
                 slabs[-1].append((len(arrays), at, first + at, steps, dy))
             arrays.append(array)
     return arrays, slabs
+
+
+def lay_out_kernel(half, own, other, trial, out):
+    count, rows = own.shape[0], own.shape[1] // 2
+    b = lax.rem(lax.axis_index("chol"), 2)
+    for block, part in ((b, own), (1 - b, other)):
+        for walker in range(count):
+            for at in range(2):
+                place = slice(at * rows, (at + 1) * rows)
+                out[(block * count + walker) * 2 + at] = part[walker, place]
+    out[4 * count] = trial[half * rows : (half + 1) * rows]
+
+
+def laid_out(own, other, trial, half):
+    count, rows, electrons = own.shape
+    return pl.pallas_call(
+        functools.partial(lay_out_kernel, half),
+        out_shape=jax.ShapeDtypeStruct((4 * count + 1, rows // 2, electrons), own.dtype),
+        in_specs=vmem_specs(3),
+        out_specs=pl.BlockSpec(memory_space=pltpu.VMEM),
+        compiler_params=params(4),
+    )(own, other, trial)
 
 
 def product(left, right):
@@ -481,7 +503,7 @@
             pltpu.SMEM((per_group + 1,), jnp.int32),
             pltpu.SemaphoreType.DMA((per_group,)),
         ],
-        compiler_params=params(60),
+        compiler_params=params(4),
     )(source, walkers)
 
 
@@ -533,15 +555,12 @@
 
 
 def shards(layout, walkers, trial, cholesky, rotated, fields, source):
-    b = lax.axis_index("chol") % 2
     shares, order = migrate(layout, walkers, source)
     sizes = [own.shape[0] for own, _ in shares]
-    halves = trial.reshape(2, -1, trial.shape[1])
-    streams = []
-    for at, (own, other) in enumerate(shares):
-        both = (jnp.where(b == 0, own, other), jnp.where(b == 0, other, own))
-        slabs = jnp.concatenate(both).reshape(-1, *halves.shape[1:])
-        streams.append(Stream(layout, jnp.concatenate([slabs, halves[at : at + 1]])))
+    streams = [
+        Stream(layout, laid_out(own, other, trial, half))
+        for half, (own, other) in enumerate(shares)
+    ]
     rot_theirs = layout.shift(rotated, db=1)
     for _ in range(layout.z - 1):
         for stream in streams:

time: 146 us -> 130 us (0.89)
  Pallas kernels: 31.5 us -> 15 us
  local copies, waits for them, and re-layouts: 0.94 us -> 3.52 us
  waiting for transfers between devices: 57.5 us -> 55.1 us
    pallas_call x1, Pallas kernels: 18.5 us -> 2.01 us  [split_walkers(): pl.pallas_call(split_kernel, out_shape=[share] * 4 + [jax.ShapeDtypeStruc...]
    unnamed x21 -> x26, local copies, waits for them, and re-layouts: 0.06 us -> 3.42 us
    ppermute x16, waiting for transfers between devices: 33.8 us -> 32 us  [step(): return lax.ppermute(array, 'chol', pairs)]
    ppermute x25, waiting for transfers between devices: 23.7 us -> 22.2 us  [shift(): return lax.ppermute(array, 'chol', pairs)]
  transfers between devices with their start and end apart: 43 -> 43, of which waited for: 35 -> 34; matrix products, arithmetic and copies ran while one was open for 1% -> 0% of each run, Pallas kernels for 4% -> 4%
where the time goes in v15:
time: 130 us
  waiting for transfers between devices  55.1 us (42%)
  starting transfers between devices  45.4 us (35%)
  Pallas kernels  15 us (12%)
  blocking collectives  9.88 us (8%)
  local copies, waits for them, and re-layouts  3.52 us (3%)
    ppermute x16, waiting for transfers between devices, step(): return lax.ppermute(array, 'chol', pairs)  32 us
    ppermute x25, waiting for transfers between devices, shift(): return lax.ppermute(array, 'chol', pairs)  22.2 us
    ppermute x16, starting transfers between devices, step(): return lax.ppermute(array, 'chol', pairs)  21.9 us
    ppermute x25, starting transfers between devices, shift(): return lax.ppermute(array, 'chol', pairs)  20.9 us
    all_to_all x1, blocking collectives, shards(): parts = lax.all_to_all(parts, 'chol', 0, 0, tiled=True)  9.88 us
    unnamed x26, local copies, waits for them, and re-layouts  3.42 us
    pallas_call x1, Pallas kernels, inverses_of(): pl.pallas_call(functools.partial(inverse_kernel, layout, slabs, counts),...  3.34 us
    pallas_call x1, Pallas kernels, potential_of(): pl.pallas_call(potential_kernel, out_shape=[jax.ShapeDtypeStruct((per_gro...  3.17 us
  transfers between devices with their start and end apart: 43, of which 34 were waited for; matrix products, arithmetic and copies ran while one was open for 0% of the time, Pallas kernels for 4%

profile of v15, /device:TPU:0, one launch (start us, length us, event | category | flops | bytes accessed | tf_op | source)
XLA Modules:
  0.0 129.8 jit_solution(1909172709482115031)
XLA Ops:
  0.6 1.0 copy-done.2
  2.3 2.0 %shard_map.77 = (bf16[2,128,256]{2,1,0:T(8,128)(2,1)S(1)}, bf16[2,128,256]{2,1,0:T(8,128)(2,1)S(1)}, bf16[2,128,256]{2,1,0:T(8,128)(2,1)S(1)}, bf16[2,128,256]{2,1,0:T(8,128)(2,1)S(1)}, s32[8]{0:T(128)S(1)}) custom-call(s32[16]{0:T(128)S(1)} %copy-done.6, bf16[8,128,256]{2,1,0:T(8,128)(2,1)S(1)} %copy-done.2), custom_call_target="tpu_custom_call" | custom-call | tf_op jit(solution)/shard_map/pallas_call | solution.py:496
  4.9 2.6 %collective-permute-start.1 = (bf16[2,128,256]{2,1,0:T(8,128)(2,1)S(1)}, bf16[2,128,256]{2,1,0:T(8,128)(2,1)S(1)}, u32[]{:S(2)}, u32[]{:S(2)}) collective-permute-start(bf16[2,128,256]{2,1,0:T(8,128)(2,1)S(1)} %get-tuple-element.48), channel_id=1, source_target_pairs={{0,16},{1,17},{2,18},{3,19},{4,20},{5,21},{6,22},{7,23},{8,24},{9,... | collective-permute-start | bytes 393224 | tf_op jit(solution)/shard_map/ppermute | solution.py:525
  7.6 0.8 copy-done.3
  8.5 3.1 %collective-permute-start.12 = (bf16[9,64,256]{2,1,0:T(8,128)(2,1)S(1)}, bf16[9,64,256]{2,1,0:T(8,128)(2,1)S(1)}, u32[]{:S(2)}, u32[]{:S(2)}) collective-permute-start(bf16[9,64,256]{2,1,0:T(8,128)(2,1)S(1)} %shard_map.79.refs_13_), channel_id=1, source_target_pairs={{0,8},{1,9},{2,10},{3,11},{4,0},{5,1},{6,2},{7,3},{8,12},{9,13},{1... | collective-permute-start | bytes 884744 | tf_op jit(solution)/shard_map/ppermute | solution.py:49
  11.6 1.5 %collective-permute-start.11 = (bf16[9,64,256]{2,1,0:T(8,128)(2,1)S(1)}, bf16[9,64,256]{2,1,0:T(8,128)(2,1)S(1)}, u32[]{:S(2)}, u32[]{:S(2)}) collective-permute-start(bf16[9,64,256]{2,1,0:T(8,128)(2,1)S(1)} %shard_map.79.refs_13_), channel_id=1, source_target_pairs={{0,2},{1,3},{2,0},{3,1},{4,6},{5,7},{6,4},{7,5},{8,10},{9,11},{10,... | collective-permute-start | bytes 884744 | tf_op jit(solution)/shard_map/ppermute | solution.py:40
  13.1 0.9 collective-permute-done.2.other
  14.1 0.8 copy-done.4
  14.9 2.7 %collective-permute-start.4 = (bf16[9,64,256]{2,1,0:T(8,128)(2,1)S(1)}, bf16[9,64,256]{2,1,0:T(8,128)(2,1)S(1)}, u32[]{:S(2)}, u32[]{:S(2)}) collective-permute-start(bf16[9,64,256]{2,1,0:T(8,128)(2,1)S(1)} %shard_map.78.refs_4_), channel_id=1, source_target_pairs={{0,8},{1,9},{2,10},{3,11},{4,0},{5,1},{6,2},{7,3},{8,12},{9,13},{1... | collective-permute-start | bytes 884744 | tf_op jit(solution)/shard_map/ppermute | solution.py:49
  17.7 1.5 %collective-permute-start.3 = (bf16[9,64,256]{2,1,0:T(8,128)(2,1)S(1)}, bf16[9,64,256]{2,1,0:T(8,128)(2,1)S(1)}, u32[]{:S(2)}, u32[]{:S(2)}) collective-permute-start(bf16[9,64,256]{2,1,0:T(8,128)(2,1)S(1)} %shard_map.78.refs_4_), channel_id=1, source_target_pairs={{0,2},{1,3},{2,0},{3,1},{4,6},{5,7},{6,4},{7,5},{8,10},{9,11},{10,... | collective-permute-start | bytes 884744 | tf_op jit(solution)/shard_map/ppermute | solution.py:40
  19.2 1.2 collective-permute-done.11.refs_17_
  20.4 1.6 %collective-permute-start.14 = (bf16[9,64,256]{2,1,0:T(8,128)(2,1)S(1)}, bf16[9,64,256]{2,1,0:T(8,128)(2,1)S(1)}, u32[]{:S(2)}, u32[]{:S(2)}) collective-permute-start(bf16[9,64,256]{2,1,0:T(8,128)(2,1)S(1)} %collective-permute-done.12.refs_14_), channel_id=1, source_target_pairs={{0,8},{1,9},{2,10},{3,11},{4,0},{5,1},{6,2},{7,3},{8,12},{9,13},{1... | collective-permute-start | bytes 884744 | tf_op jit(solution)/shard_map/ppermute | solution.py:49
  22.0 1.5 %collective-permute-start.13 = (bf16[9,64,256]{2,1,0:T(8,128)(2,1)S(1)}, bf16[9,64,256]{2,1,0:T(8,128)(2,1)S(1)}, u32[]{:S(2)}, u32[]{:S(2)}) collective-permute-start(bf16[9,64,256]{2,1,0:T(8,128)(2,1)S(1)} %collective-permute-done.12.refs_14_), channel_id=1, source_target_pairs={{0,2},{1,3},{2,0},{3,1},{4,6},{5,7},{6,4},{7,5},{8,10},{9,11},{10,... | collective-permute-start | bytes 884744 | tf_op jit(solution)/shard_map/ppermute | solution.py:40
  23.5 1.5 %collective-permute-done.4.refs_5_ = bf16[9,64,256]{2,1,0:T(8,128)(2,1)S(1)} collective-permute-done((bf16[9,64,256]{2,1,0:T(8,128)(2,1)S(1)}, bf16[9,64,256]{2,1,0:T(8,128)(2,1)S(1)}, u32[]{:S(2)}, u32[]{:S(2)}) %collective-permute-start.4) | collective-permute-done | bytes 294944 | tf_op jit(solution)/shard_map/ppermute | solution.py:49
  25.0 2.5 %collective-permute-done.3.refs_8_ = bf16[9,64,256]{2,1,0:T(8,128)(2,1)S(1)} collective-permute-done((bf16[9,64,256]{2,1,0:T(8,128)(2,1)S(1)}, bf16[9,64,256]{2,1,0:T(8,128)(2,1)S(1)}, u32[]{:S(2)}, u32[]{:S(2)}) %collective-permute-start.3) | collective-permute-done | bytes 294944 | tf_op jit(solution)/shard_map/ppermute | solution.py:40
  27.5 1.6 %collective-permute-start.6 = (bf16[9,64,256]{2,1,0:T(8,128)(2,1)S(1)}, bf16[9,64,256]{2,1,0:T(8,128)(2,1)S(1)}, u32[]{:S(2)}, u32[]{:S(2)}) collective-permute-start(bf16[9,64,256]{2,1,0:T(8,128)(2,1)S(1)} %collective-permute-done.4.refs_5_), channel_id=1, source_target_pairs={{0,8},{1,9},{2,10},{3,11},{4,0},{5,1},{6,2},{7,3},{8,12},{9,13},{1... | collective-permute-start | bytes 884744 | tf_op jit(solution)/shard_map/ppermute | solution.py:49
  29.1 1.5 %collective-permute-start.5 = (bf16[9,64,256]{2,1,0:T(8,128)(2,1)S(1)}, bf16[9,64,256]{2,1,0:T(8,128)(2,1)S(1)}, u32[]{:S(2)}, u32[]{:S(2)}) collective-permute-start(bf16[9,64,256]{2,1,0:T(8,128)(2,1)S(1)} %collective-permute-done.4.refs_5_), channel_id=1, source_target_pairs={{0,2},{1,3},{2,0},{3,1},{4,6},{5,7},{6,4},{7,5},{8,10},{9,11},{10,... | collective-permute-start | bytes 884744 | tf_op jit(solution)/shard_map/ppermute | solution.py:40
  30.6 0.7 collective-permute-done.14.refs_15_
  31.3 2.5 %collective-permute-done.13.refs_18_ = bf16[9,64,256]{2,1,0:T(8,128)(2,1)S(1)} collective-permute-done((bf16[9,64,256]{2,1,0:T(8,128)(2,1)S(1)}, bf16[9,64,256]{2,1,0:T(8,128)(2,1)S(1)}, u32[]{:S(2)}, u32[]{:S(2)}) %collective-permute-start.13) | collective-permute-done | bytes 294944 | tf_op jit(solution)/shard_map/ppermute | solution.py:40
  33.8 1.6 %collective-permute-start.16 = (bf16[9,64,256]{2,1,0:T(8,128)(2,1)S(1)}, bf16[9,64,256]{2,1,0:T(8,128)(2,1)S(1)}, u32[]{:S(2)}, u32[]{:S(2)}) collective-permute-start(bf16[9,64,256]{2,1,0:T(8,128)(2,1)S(1)} %collective-permute-done.14.refs_15_), channel_id=1, source_target_pairs={{0,8},{1,9},{2,10},{3,11},{4,0},{5,1},{6,2},{7,3},{8,12},{9,13},{1... | collective-permute-start | bytes 884744 | tf_op jit(solution)/shard_map/ppermute | solution.py:49
  35.4 1.5 %collective-permute-start.15 = (bf16[9,64,256]{2,1,0:T(8,128)(2,1)S(1)}, bf16[9,64,256]{2,1,0:T(8,128)(2,1)S(1)}, u32[]{:S(2)}, u32[]{:S(2)}) collective-permute-start(bf16[9,64,256]{2,1,0:T(8,128)(2,1)S(1)} %collective-permute-done.14.refs_15_), channel_id=1, source_target_pairs={{0,2},{1,3},{2,0},{3,1},{4,6},{5,7},{6,4},{7,5},{8,10},{9,11},{10,... | collective-permute-start | bytes 884744 | tf_op jit(solution)/shard_map/ppermute | solution.py:40
  36.9 0.7 collective-permute-done.6.refs_6_
  37.6 2.5 %collective-permute-done.5.refs_9_ = bf16[9,64,256]{2,1,0:T(8,128)(2,1)S(1)} collective-permute-done((bf16[9,64,256]{2,1,0:T(8,128)(2,1)S(1)}, bf16[9,64,256]{2,1,0:T(8,128)(2,1)S(1)}, u32[]{:S(2)}, u32[]{:S(2)}) %collective-permute-start.5) | collective-permute-done | bytes 294944 | tf_op jit(solution)/shard_map/ppermute | solution.py:40
  40.1 1.6 %collective-permute-start.8 = (bf16[9,64,256]{2,1,0:T(8,128)(2,1)S(1)}, bf16[9,64,256]{2,1,0:T(8,128)(2,1)S(1)}, u32[]{:S(2)}, u32[]{:S(2)}) collective-permute-start(bf16[9,64,256]{2,1,0:T(8,128)(2,1)S(1)} %collective-permute-done.6.refs_6_), channel_id=1, source_target_pairs={{0,8},{1,9},{2,10},{3,11},{4,0},{5,1},{6,2},{7,3},{8,12},{9,13},{1... | collective-permute-start | bytes 884744 | tf_op jit(solution)/shard_map/ppermute | solution.py:49
  41.7 1.5 %collective-permute-start.7 = (bf16[9,64,256]{2,1,0:T(8,128)(2,1)S(1)}, bf16[9,64,256]{2,1,0:T(8,128)(2,1)S(1)}, u32[]{:S(2)}, u32[]{:S(2)}) collective-permute-start(bf16[9,64,256]{2,1,0:T(8,128)(2,1)S(1)} %collective-permute-done.6.refs_6_), channel_id=1, source_target_pairs={{0,2},{1,3},{2,0},{3,1},{4,6},{5,7},{6,4},{7,5},{8,10},{9,11},{10,... | collective-permute-start | bytes 884744 | tf_op jit(solution)/shard_map/ppermute | solution.py:40
  43.2 0.7 collective-permute-done.16.refs_16_
  43.9 2.5 %collective-permute-done.15.refs_19_ = bf16[9,64,256]{2,1,0:T(8,128)(2,1)S(1)} collective-permute-done((bf16[9,64,256]{2,1,0:T(8,128)(2,1)S(1)}, bf16[9,64,256]{2,1,0:T(8,128)(2,1)S(1)}, u32[]{:S(2)}, u32[]{:S(2)}) %collective-permute-start.15) | collective-permute-done | bytes 294944 | tf_op jit(solution)/shard_map/ppermute | solution.py:40
  46.5 1.6 %collective-permute-start.19 = (bf16[4,64,256]{2,1,0:T(8,128)(2,1)S(1)}, bf16[4,64,256]{2,1,0:T(8,128)(2,1)S(1)}, u32[]{:S(2)}, u32[]{:S(2)}) collective-permute-start(bf16[4,64,256]{2,1,0:T(8,128)(2,1)S(1)} %slice.87), channel_id=1, source_target_pairs={{0,8},{1,9},{2,10},{3,11},{4,0},{5,1},{6,2},{7,3},{8,12},{9,13},{1... | collective-permute-start | bytes 393224 | tf_op jit(solution)/shard_map/ppermute | solution.py:49
  48.1 1.5 %collective-permute-start.18 = (bf16[5,64,256]{2,1,0:T(8,128)(2,1)S(1)}, bf16[5,64,256]{2,1,0:T(8,128)(2,1)S(1)}, u32[]{:S(2)}, u32[]{:S(2)}) collective-permute-start(bf16[5,64,256]{2,1,0:T(8,128)(2,1)S(1)} %slice.86), channel_id=1, source_target_pairs={{0,2},{1,3},{2,0},{3,1},{4,6},{5,7},{6,4},{7,5},{8,10},{9,11},{10,... | collective-permute-start | bytes 491528 | tf_op jit(solution)/shard_map/ppermute | solution.py:40
  50.2 2.5 %collective-permute-done.7.refs_10_ = bf16[9,64,256]{2,1,0:T(8,128)(2,1)S(1)} collective-permute-done((bf16[9,64,256]{2,1,0:T(8,128)(2,1)S(1)}, bf16[9,64,256]{2,1,0:T(8,128)(2,1)S(1)}, u32[]{:S(2)}, u32[]{:S(2)}) %collective-permute-start.7) | collective-permute-done | bytes 294944 | tf_op jit(solution)/shard_map/ppermute | solution.py:40
  52.9 1.6 %collective-permute-start.22 = (bf16[5,64,256]{2,1,0:T(8,128)(2,1)S(1)}, bf16[5,64,256]{2,1,0:T(8,128)(2,1)S(1)}, u32[]{:S(2)}, u32[]{:S(2)}) collective-permute-start(bf16[5,64,256]{2,1,0:T(8,128)(2,1)S(1)} %slice.90), channel_id=1, source_target_pairs={{0,2},{1,3},{2,0},{3,1},{4,6},{5,7},{6,4},{7,5},{8,10},{9,11},{10,... | collective-permute-start | bytes 491528 | tf_op jit(solution)/shard_map/ppermute | solution.py:40
  54.5 1.1 collective-permute-done.18.refs_20_
  55.6 2.1 %collective-permute-start.23 = (bf16[4,64,256]{2,1,0:T(8,128)(2,1)S(1)}, bf16[4,64,256]{2,1,0:T(8,128)(2,1)S(1)}, u32[]{:S(2)}, u32[]{:S(2)}) collective-permute-start(bf16[4,64,256]{2,1,0:T(8,128)(2,1)S(1)} %slice.91), channel_id=1, source_target_pairs={{0,8},{1,9},{2,10},{3,11},{4,0},{5,1},{6,2},{7,3},{8,12},{9,13},{1... | collective-permute-start | bytes 393224 | tf_op jit(solution)/shard_map/ppermute | solution.py:49
  57.7 1.0 collective-permute-start.21
  58.8 1.1 collective-permute-start.20
  59.8 0.8 collective-permute-done.23.refs_12_
  60.6 1.0 collective-permute-done.21.refs_3_
  61.6 1.1 collective-permute-done.20.refs_2_
  62.7 3.3 %shard_map.80 = (bf16[2,8,2,128,256]{4,3,2,1,0:T(8,128)(2,1)S(1)}, bf16[2,8,2,128,256]{4,3,2,1,0:T(8,128)(2,1)S(1)}, bf16[4,256,256]{2,1,0:T(8,128)(2,1)S(1)}) custom-call(bf16[7,64,256]{2,1,0:T(8,128)(2,1)S(1)} %collective-permute-done.9.refs_0_, bf16[7,64,256]{2,1,0:T(8,128)(2,1)S(1)} %collective-permute-done.17.refs_1_, ...), custom_call_target="tpu_custom_call" | custom-call | flops 2684354560 | bytes 10485760 | tf_op jit(solution)/shard_map/pallas_call | solution.py:192
  66.1 1.7 %shard_map.81 = f32[16,8,128]{2,1,0:T(8,128)S(1)} custom-call(bf16[32,128,256]{2,1,0:T(8,128)(2,1)S(1)} %copy-done.1, bf16[32,128,256]{2,1,0:T(8,128)(2,1)S(1)} %collective-permute-done.rot_theirs, bf16[4,256,256]{2,1,0:T(8,128)(2,1)S(1)} %get-tuple-element.67.inverses, bf16[2,8,2,128,256]{4,3,2,1,0:T(8,128)(2,1)S(1)} %get-tuple-element.68.refs_0_.refs_1_.refs_2_, ...), custom_call_target="tpu_custom_call" | custom-call | flops 402653184 | bytes 4718592 | tf_op jit(solution)/shard_map/pallas_call | solution.py:254
  67.8 9.9 %all_to_all.5.parts = f32[16,8,128]{2,1,0:T(8,128)S(1)} all-to-all(f32[16,8,128]{2,1,0:T(8,128)S(1)} %shard_map.81), channel_id=1, replica_groups=mesh['walk'=2,'chol'=16] {'chol'}, dimensions={0} | all-to-all | bytes 131072 | tf_op jit(solution)/shard_map/all_to_all | solution.py:580
  77.7 3.2 %shard_map.82 = (f32[8,32]{1,0:T(8,128)}, bf16[4,128,2048]{2,1,0:T(8,128)(2,1)S(1)}, bf16[4,64,2048]{2,1,0:T(8,128)(2,1)S(1)}, bf16[4,64,2048]{2,1,0:T(8,128)(2,1)S(1)}) custom-call(s32[8]{0:T(128)S(1)} %get-tuple-element.47.order, f32[8,32]{1,0:T(8,128)S(1)} %copy-done.5, f32[16,8,128]{2,1,0:T(8,128)S(1)} %all_to_all.5.parts, bf16[32,128,2048]{2,1,0:T(8,128)(2,1)S(1)} %copy-done), custom_call_target="tpu_custom_call" | custom-call | tf_op jit(solution)/shard_map/pallas_call | solution.py:320
  81.5 0.8 shard_map.83
  83.6 1.5 %collective-permute-done.25.refs_1_ = bf16[4,64,2048]{2,1,0:T(8,128)(2,1)S(1)} collective-permute-done((bf16[4,64,2048]{2,1,0:T(8,128)(2,1)S(1)}, bf16[4,64,2048]{2,1,0:T(8,128)(2,1)S(1)}, u32[]{:S(2)}, u32[]{:S(2)}) %collective-permute-start.25) | collective-permute-done | bytes 1048608 | tf_op jit(solution)/shard_map/ppermute | solution.py:40
  85.1 0.8 shard_map.84
  86.9 4.6 %collective-permute-done.27.refs_4_ = bf16[4,128,256]{2,1,0:T(8,128)(2,1)S(1)} collective-permute-done((bf16[4,128,256]{2,1,0:T(8,128)(2,1)S(1)}, bf16[4,128,256]{2,1,0:T(8,128)(2,1)S(1)}, u32[]{:S(2)}, u32[]{:S(2)}) %collective-permute-start.27) | collective-permute-done | bytes 262176 | tf_op jit(solution)/shard_map/ppermute | solution.py:49
  91.8 0.9 collective-permute-start.29
  93.3 3.8 %collective-permute-done.35.refs_13_ = bf16[4,128,256]{2,1,0:T(8,128)(2,1)S(1)} collective-permute-done((bf16[4,128,256]{2,1,0:T(8,128)(2,1)S(1)}, bf16[4,128,256]{2,1,0:T(8,128)(2,1)S(1)}, u32[]{:S(2)}, u32[]{:S(2)}) %collective-permute-start.35) | collective-permute-done | bytes 262176 | tf_op jit(solution)/shard_map/ppermute | solution.py:49
  97.4 0.9 collective-permute-start.37
  98.9 3.8 %collective-permute-done.29.refs_5_ = bf16[4,128,256]{2,1,0:T(8,128)(2,1)S(1)} collective-permute-done((bf16[4,128,256]{2,1,0:T(8,128)(2,1)S(1)}, bf16[4,128,256]{2,1,0:T(8,128)(2,1)S(1)}, u32[]{:S(2)}, u32[]{:S(2)}) %collective-permute-start.29) | collective-permute-done | bytes 262176 | tf_op jit(solution)/shard_map/ppermute | solution.py:49
  103.0 0.9 collective-permute-start.31
  104.6 3.8 %collective-permute-done.37.refs_14_ = bf16[4,128,256]{2,1,0:T(8,128)(2,1)S(1)} collective-permute-done((bf16[4,128,256]{2,1,0:T(8,128)(2,1)S(1)}, bf16[4,128,256]{2,1,0:T(8,128)(2,1)S(1)}, u32[]{:S(2)}, u32[]{:S(2)}) %collective-permute-start.37) | collective-permute-done | bytes 262176 | tf_op jit(solution)/shard_map/ppermute | solution.py:49
  108.6 0.9 collective-permute-start.39
  110.2 3.8 %collective-permute-done.31.refs_6_ = bf16[4,128,256]{2,1,0:T(8,128)(2,1)S(1)} collective-permute-done((bf16[4,128,256]{2,1,0:T(8,128)(2,1)S(1)}, bf16[4,128,256]{2,1,0:T(8,128)(2,1)S(1)}, u32[]{:S(2)}, u32[]{:S(2)}) %collective-permute-start.31) | collective-permute-done | bytes 262176 | tf_op jit(solution)/shard_map/ppermute | solution.py:49
  114.3 1.0 collective-permute-start.33
  115.9 3.7 %collective-permute-done.39.refs_15_ = bf16[4,128,256]{2,1,0:T(8,128)(2,1)S(1)} collective-permute-done((bf16[4,128,256]{2,1,0:T(8,128)(2,1)S(1)}, bf16[4,128,256]{2,1,0:T(8,128)(2,1)S(1)}, u32[]{:S(2)}, u32[]{:S(2)}) %collective-permute-start.39) | collective-permute-done | bytes 262176 | tf_op jit(solution)/shard_map/ppermute | solution.py:49
  119.9 1.0 collective-permute-start.41
  121.5 0.9 collective-permute-done.33.refs_11_
  122.4 2.5 %collective-permute-done.41.refs_20_ = bf16[2,128,256]{2,1,0:T(8,128)(2,1)S(1)} collective-permute-done((bf16[2,128,256]{2,1,0:T(8,128)(2,1)S(1)}, bf16[2,128,256]{2,1,0:T(8,128)(2,1)S(1)}, u32[]{:S(2)}, u32[]{:S(2)}) %collective-permute-start.41) | collective-permute-done | bytes 131104 | tf_op jit(solution)/shard_map/ppermute | solution.py:49
  124.9 0.9 collective-permute-done.40.refs_19_
  125.8 1.0 shard_map.85
  126.9 0.7 shard_map.86.mine
  127.6 0.8 collective-permute-done.42.theirs
  128.4 1.4 %shard_map.87 = bf16[8,128,256]{2,1,0:T(8,128)(2,1)} custom-call(s32[8]{0:T(128)S(1)} %get-tuple-element.47.order, bf16[4,128,256]{2,1,0:T(8,128)(2,1)S(1)} %shard_map.86.mine, bf16[4,128,256]{2,1,0:T(8,128)(2,1)S(1)} %collective-permute-done.42.theirs), custom_call_target="tpu_custom_call" | custom-call | tf_op jit(solution)/shard_map/pallas_call | solution.py:446
  (72 shorter events, 10.6 us)
Async XLA Ops:
  0.6 1.0 copy-start.2
  1.7 0.7 copy-start.6
  4.3 3.3 %collective-permute-start.10 = (bf16[2,128,256]{2,1,0:T(8,128)(2,1)S(1)}, bf16[2,128,256]{2,1,0:T(8,128)(2,1)S(1)}, u32[]{:S(2)}, u32[]{:S(2)}) collective-permute-start(bf16[2,128,256]{2,1,0:T(8,128)(2,1)S(1)} %get-tuple-element.57), channel_id=1, source_target_pairs={{0,1},{1,0},{2,3},{3,2},{4,5},{5,4},{6,7},{7,6},{8,9},{9,8},{10,11... | collective-permute-start | bytes 393224 | tf_op jit(solution)/shard_map/ppermute | solution.py:40
  4.9 8.3 %collective-permute-start.1 = (bf16[2,128,256]{2,1,0:T(8,128)(2,1)S(1)}, bf16[2,128,256]{2,1,0:T(8,128)(2,1)S(1)}, u32[]{:S(2)}, u32[]{:S(2)}) collective-permute-start(bf16[2,128,256]{2,1,0:T(8,128)(2,1)S(1)} %get-tuple-element.48), channel_id=1, source_target_pairs={{0,16},{1,17},{2,18},{3,19},{4,20},{5,21},{6,22},{7,23},{8,24},{9,... | collective-permute-start | bytes 393224 | tf_op jit(solution)/shard_map/ppermute | solution.py:525
  7.4 6.6 %collective-permute-start.2 = (bf16[2,128,256]{2,1,0:T(8,128)(2,1)S(1)}, bf16[2,128,256]{2,1,0:T(8,128)(2,1)S(1)}, u32[]{:S(2)}, u32[]{:S(2)}) collective-permute-start(bf16[2,128,256]{2,1,0:T(8,128)(2,1)S(1)} %get-tuple-element.49), channel_id=1, source_target_pairs={{0,17},{1,16},{2,19},{3,18},{4,21},{5,20},{6,23},{7,22},{8,25},{9,... | collective-permute-start | bytes 393224 | tf_op jit(solution)/shard_map/ppermute | solution.py:526
  7.5 58.6 %collective-permute-start = (bf16[32,128,256]{2,1,0:T(8,128)(2,1)}, bf16[32,128,256]{2,1,0:T(8,128)(2,1)S(1)}, u32[]{:S(2)}, u32[]{:S(2)}) collective-permute-start(bf16[32,128,256]{2,1,0:T(8,128)(2,1)} %rot_mine.1), channel_id=1, source_target_pairs={{0,1},{1,0},{2,3},{3,2},{4,5},{5,4},{6,7},{7,6},{8,9},{9,8},{10,11... | collective-permute-start | bytes 6291464 | tf_op jit(solution)/shard_map/ppermute | solution.py:40
  7.6 0.8 copy-start.3
  8.5 10.7 %collective-permute-start.12 = (bf16[9,64,256]{2,1,0:T(8,128)(2,1)S(1)}, bf16[9,64,256]{2,1,0:T(8,128)(2,1)S(1)}, u32[]{:S(2)}, u32[]{:S(2)}) collective-permute-start(bf16[9,64,256]{2,1,0:T(8,128)(2,1)S(1)} %shard_map.79.refs_13_), channel_id=1, source_target_pairs={{0,8},{1,9},{2,10},{3,11},{4,0},{5,1},{6,2},{7,3},{8,12},{9,13},{1... | collective-permute-start | bytes 884744 | tf_op jit(solution)/shard_map/ppermute | solution.py:49
  11.6 8.8 %collective-permute-start.11 = (bf16[9,64,256]{2,1,0:T(8,128)(2,1)S(1)}, bf16[9,64,256]{2,1,0:T(8,128)(2,1)S(1)}, u32[]{:S(2)}, u32[]{:S(2)}) collective-permute-start(bf16[9,64,256]{2,1,0:T(8,128)(2,1)S(1)} %shard_map.79.refs_13_), channel_id=1, source_target_pairs={{0,2},{1,3},{2,0},{3,1},{4,6},{5,7},{6,4},{7,5},{8,10},{9,11},{10,... | collective-permute-start | bytes 884744 | tf_op jit(solution)/shard_map/ppermute | solution.py:40
  14.1 0.8 copy-start.4
  14.9 10.0 %collective-permute-start.4 = (bf16[9,64,256]{2,1,0:T(8,128)(2,1)S(1)}, bf16[9,64,256]{2,1,0:T(8,128)(2,1)S(1)}, u32[]{:S(2)}, u32[]{:S(2)}) collective-permute-start(bf16[9,64,256]{2,1,0:T(8,128)(2,1)S(1)} %shard_map.78.refs_4_), channel_id=1, source_target_pairs={{0,8},{1,9},{2,10},{3,11},{4,0},{5,1},{6,2},{7,3},{8,12},{9,13},{1... | collective-permute-start | bytes 884744 | tf_op jit(solution)/shard_map/ppermute | solution.py:49
  17.7 9.8 %collective-permute-start.3 = (bf16[9,64,256]{2,1,0:T(8,128)(2,1)S(1)}, bf16[9,64,256]{2,1,0:T(8,128)(2,1)S(1)}, u32[]{:S(2)}, u32[]{:S(2)}) collective-permute-start(bf16[9,64,256]{2,1,0:T(8,128)(2,1)S(1)} %shard_map.78.refs_4_), channel_id=1, source_target_pairs={{0,2},{1,3},{2,0},{3,1},{4,6},{5,7},{6,4},{7,5},{8,10},{9,11},{10,... | collective-permute-start | bytes 884744 | tf_op jit(solution)/shard_map/ppermute | solution.py:40
  20.4 10.9 %collective-permute-start.14 = (bf16[9,64,256]{2,1,0:T(8,128)(2,1)S(1)}, bf16[9,64,256]{2,1,0:T(8,128)(2,1)S(1)}, u32[]{:S(2)}, u32[]{:S(2)}) collective-permute-start(bf16[9,64,256]{2,1,0:T(8,128)(2,1)S(1)} %collective-permute-done.12.refs_14_), channel_id=1, source_target_pairs={{0,8},{1,9},{2,10},{3,11},{4,0},{5,1},{6,2},{7,3},{8,12},{9,13},{1... | collective-permute-start | bytes 884744 | tf_op jit(solution)/shard_map/ppermute | solution.py:49
  22.0 11.8 %collective-permute-start.13 = (bf16[9,64,256]{2,1,0:T(8,128)(2,1)S(1)}, bf16[9,64,256]{2,1,0:T(8,128)(2,1)S(1)}, u32[]{:S(2)}, u32[]{:S(2)}) collective-permute-start(bf16[9,64,256]{2,1,0:T(8,128)(2,1)S(1)} %collective-permute-done.12.refs_14_), channel_id=1, source_target_pairs={{0,2},{1,3},{2,0},{3,1},{4,6},{5,7},{6,4},{7,5},{8,10},{9,11},{10,... | collective-permute-start | bytes 884744 | tf_op jit(solution)/shard_map/ppermute | solution.py:40
  27.5 10.1 %collective-permute-start.6 = (bf16[9,64,256]{2,1,0:T(8,128)(2,1)S(1)}, bf16[9,64,256]{2,1,0:T(8,128)(2,1)S(1)}, u32[]{:S(2)}, u32[]{:S(2)}) collective-permute-start(bf16[9,64,256]{2,1,0:T(8,128)(2,1)S(1)} %collective-permute-done.4.refs_5_), channel_id=1, source_target_pairs={{0,8},{1,9},{2,10},{3,11},{4,0},{5,1},{6,2},{7,3},{8,12},{9,13},{1... | collective-permute-start | bytes 884744 | tf_op jit(solution)/shard_map/ppermute | solution.py:49
  29.1 11.1 %collective-permute-start.5 = (bf16[9,64,256]{2,1,0:T(8,128)(2,1)S(1)}, bf16[9,64,256]{2,1,0:T(8,128)(2,1)S(1)}, u32[]{:S(2)}, u32[]{:S(2)}) collective-permute-start(bf16[9,64,256]{2,1,0:T(8,128)(2,1)S(1)} %collective-permute-done.4.refs_5_), channel_id=1, source_target_pairs={{0,2},{1,3},{2,0},{3,1},{4,6},{5,7},{6,4},{7,5},{8,10},{9,11},{10,... | collective-permute-start | bytes 884744 | tf_op jit(solution)/shard_map/ppermute | solution.py:40
  33.8 10.1 %collective-permute-start.16 = (bf16[9,64,256]{2,1,0:T(8,128)(2,1)S(1)}, bf16[9,64,256]{2,1,0:T(8,128)(2,1)S(1)}, u32[]{:S(2)}, u32[]{:S(2)}) collective-permute-start(bf16[9,64,256]{2,1,0:T(8,128)(2,1)S(1)} %collective-permute-done.14.refs_15_), channel_id=1, source_target_pairs={{0,8},{1,9},{2,10},{3,11},{4,0},{5,1},{6,2},{7,3},{8,12},{9,13},{1... | collective-permute-start | bytes 884744 | tf_op jit(solution)/shard_map/ppermute | solution.py:49
  35.4 11.1 %collective-permute-start.15 = (bf16[9,64,256]{2,1,0:T(8,128)(2,1)S(1)}, bf16[9,64,256]{2,1,0:T(8,128)(2,1)S(1)}, u32[]{:S(2)}, u32[]{:S(2)}) collective-permute-start(bf16[9,64,256]{2,1,0:T(8,128)(2,1)S(1)} %collective-permute-done.14.refs_15_), channel_id=1, source_target_pairs={{0,2},{1,3},{2,0},{3,1},{4,6},{5,7},{6,4},{7,5},{8,10},{9,11},{10,... | collective-permute-start | bytes 884744 | tf_op jit(solution)/shard_map/ppermute | solution.py:40
  40.1 10.1 %collective-permute-start.8 = (bf16[9,64,256]{2,1,0:T(8,128)(2,1)S(1)}, bf16[9,64,256]{2,1,0:T(8,128)(2,1)S(1)}, u32[]{:S(2)}, u32[]{:S(2)}) collective-permute-start(bf16[9,64,256]{2,1,0:T(8,128)(2,1)S(1)} %collective-permute-done.6.refs_6_), channel_id=1, source_target_pairs={{0,8},{1,9},{2,10},{3,11},{4,0},{5,1},{6,2},{7,3},{8,12},{9,13},{1... | collective-permute-start | bytes 884744 | tf_op jit(solution)/shard_map/ppermute | solution.py:49
  41.7 11.1 %collective-permute-start.7 = (bf16[9,64,256]{2,1,0:T(8,128)(2,1)S(1)}, bf16[9,64,256]{2,1,0:T(8,128)(2,1)S(1)}, u32[]{:S(2)}, u32[]{:S(2)}) collective-permute-start(bf16[9,64,256]{2,1,0:T(8,128)(2,1)S(1)} %collective-permute-done.6.refs_6_), channel_id=1, source_target_pairs={{0,2},{1,3},{2,0},{3,1},{4,6},{5,7},{6,4},{7,5},{8,10},{9,11},{10,... | collective-permute-start | bytes 884744 | tf_op jit(solution)/shard_map/ppermute | solution.py:40
  46.5 6.4 %collective-permute-start.19 = (bf16[4,64,256]{2,1,0:T(8,128)(2,1)S(1)}, bf16[4,64,256]{2,1,0:T(8,128)(2,1)S(1)}, u32[]{:S(2)}, u32[]{:S(2)}) collective-permute-start(bf16[4,64,256]{2,1,0:T(8,128)(2,1)S(1)} %slice.87), channel_id=1, source_target_pairs={{0,8},{1,9},{2,10},{3,11},{4,0},{5,1},{6,2},{7,3},{8,12},{9,13},{1... | collective-permute-start | bytes 393224 | tf_op jit(solution)/shard_map/ppermute | solution.py:49
  48.1 7.5 %collective-permute-start.18 = (bf16[5,64,256]{2,1,0:T(8,128)(2,1)S(1)}, bf16[5,64,256]{2,1,0:T(8,128)(2,1)S(1)}, u32[]{:S(2)}, u32[]{:S(2)}) collective-permute-start(bf16[5,64,256]{2,1,0:T(8,128)(2,1)S(1)} %slice.86), channel_id=1, source_target_pairs={{0,2},{1,3},{2,0},{3,1},{4,6},{5,7},{6,4},{7,5},{8,10},{9,11},{10,... | collective-permute-start | bytes 491528 | tf_op jit(solution)/shard_map/ppermute | solution.py:40
  50.2 7.5 %collective-permute-start.17 = (bf16[7,64,256]{2,1,0:T(8,128)(2,1)S(1)}, bf16[7,64,256]{2,1,0:T(8,128)(2,1)S(1)}, u32[]{:S(2)}, u32[]{:S(2)}) collective-permute-start(bf16[7,64,256]{2,1,0:T(8,128)(2,1)S(1)} %slice_dynamic-update-slice_fusion.2), channel_id=1, source_target_pairs={{0,1},{1,0},{2,3},{3,2},{4,5},{5,4},{6,7},{7,6},{8,9},{9,8},{10,11... | collective-permute-start | bytes 688136 | tf_op jit(solution)/shard_map/ppermute | solution.py:40
  52.8 6.0 %collective-permute-start.9 = (bf16[7,64,256]{2,1,0:T(8,128)(2,1)S(1)}, bf16[7,64,256]{2,1,0:T(8,128)(2,1)S(1)}, u32[]{:S(2)}, u32[]{:S(2)}) collective-permute-start(bf16[7,64,256]{2,1,0:T(8,128)(2,1)S(1)} %slice_dynamic-update-slice_fusion.8), channel_id=1, source_target_pairs={{0,1},{1,0},{2,3},{3,2},{4,5},{5,4},{6,7},{7,6},{8,9},{9,8},{10,11... | collective-permute-start | bytes 688136 | tf_op jit(solution)/shard_map/ppermute | solution.py:40
  52.9 7.7 %collective-permute-start.22 = (bf16[5,64,256]{2,1,0:T(8,128)(2,1)S(1)}, bf16[5,64,256]{2,1,0:T(8,128)(2,1)S(1)}, u32[]{:S(2)}, u32[]{:S(2)}) collective-permute-start(bf16[5,64,256]{2,1,0:T(8,128)(2,1)S(1)} %slice.90), channel_id=1, source_target_pairs={{0,2},{1,3},{2,0},{3,1},{4,6},{5,7},{6,4},{7,5},{8,10},{9,11},{10,... | collective-permute-start | bytes 491528 | tf_op jit(solution)/shard_map/ppermute | solution.py:40
  55.6 5.0 %collective-permute-start.23 = (bf16[4,64,256]{2,1,0:T(8,128)(2,1)S(1)}, bf16[4,64,256]{2,1,0:T(8,128)(2,1)S(1)}, u32[]{:S(2)}, u32[]{:S(2)}) collective-permute-start(bf16[4,64,256]{2,1,0:T(8,128)(2,1)S(1)} %slice.91), channel_id=1, source_target_pairs={{0,8},{1,9},{2,10},{3,11},{4,0},{5,1},{6,2},{7,3},{8,12},{9,13},{1... | collective-permute-start | bytes 393224 | tf_op jit(solution)/shard_map/ppermute | solution.py:49
  57.7 3.9 %collective-permute-start.21 = (bf16[1,64,256]{2,1,0:T(8,128)(2,1)S(1)}, bf16[1,64,256]{2,1,0:T(8,128)(2,1)S(1)}, u32[]{:S(2)}, u32[]{:S(2)}) collective-permute-start(bf16[1,64,256]{2,1,0:T(8,128)(2,1)S(1)} %slice.89), channel_id=1, source_target_pairs={{0,2},{1,3},{2,0},{3,1},{4,6},{5,7},{6,4},{7,5},{8,10},{9,11},{10,... | collective-permute-start | bytes 98312 | tf_op jit(solution)/shard_map/ppermute | solution.py:40
  58.8 7.3 %copy-start.1 = (bf16[32,128,256]{2,1,0:T(8,128)(2,1)S(1)}, bf16[32,128,256]{2,1,0:T(8,128)(2,1)}, u32[]{:S(2)}) copy-start(bf16[32,128,256]{2,1,0:T(8,128)(2,1)} %rot_mine.1) | copy-start | bytes 6291460
  58.8 4.0 %collective-permute-start.20 = (bf16[1,64,256]{2,1,0:T(8,128)(2,1)S(1)}, bf16[1,64,256]{2,1,0:T(8,128)(2,1)S(1)}, u32[]{:S(2)}, u32[]{:S(2)}) collective-permute-start(bf16[1,64,256]{2,1,0:T(8,128)(2,1)S(1)} %slice.98), channel_id=1, source_target_pairs={{0,2},{1,3},{2,0},{3,1},{4,6},{5,7},{6,4},{7,5},{8,10},{9,11},{10,... | collective-permute-start | bytes 98312 | tf_op jit(solution)/shard_map/ppermute | solution.py:40
  62.7 15.0 %copy-start = (bf16[32,128,2048]{2,1,0:T(8,128)(2,1)S(1)}, bf16[32,128,2048]{2,1,0:T(8,128)(2,1)}, u32[]{:S(2)}) copy-start(bf16[32,128,2048]{2,1,0:T(8,128)(2,1)} %cholesky.1) | copy-start | bytes 50331652
  66.1 11.6 %copy-start.5 = (f32[8,32]{1,0:T(8,128)S(1)}, f32[8,32]{1,0:T(8,128)}, u32[]{:S(2)}) copy-start(f32[8,32]{1,0:T(8,128)} %fields.1) | copy-start | bytes 3076
  80.9 2.7 %collective-permute-start.24 = (bf16[4,64,2048]{2,1,0:T(8,128)(2,1)S(1)}, bf16[4,64,2048]{2,1,0:T(8,128)(2,1)S(1)}, u32[]{:S(2)}, u32[]{:S(2)}) collective-permute-start(bf16[4,64,2048]{2,1,0:T(8,128)(2,1)S(1)} %get-tuple-element.72), channel_id=1, source_target_pairs={{0,1},{1,0},{2,3},{3,2},{4,5},{5,4},{6,7},{7,6},{8,9},{9,8},{10,11... | collective-permute-start | bytes 3145736 | tf_op jit(solution)/shard_map/ppermute | solution.py:40
  81.0 4.1 %collective-permute-start.25 = (bf16[4,64,2048]{2,1,0:T(8,128)(2,1)S(1)}, bf16[4,64,2048]{2,1,0:T(8,128)(2,1)S(1)}, u32[]{:S(2)}, u32[]{:S(2)}) collective-permute-start(bf16[4,64,2048]{2,1,0:T(8,128)(2,1)S(1)} %get-tuple-element.73), channel_id=1, source_target_pairs={{0,1},{1,0},{2,3},{3,2},{4,5},{5,4},{6,7},{7,6},{8,9},{9,8},{10,11... | collective-permute-start | bytes 3145736 | tf_op jit(solution)/shard_map/ppermute | solution.py:40
  82.3 9.2 %collective-permute-start.27 = (bf16[4,128,256]{2,1,0:T(8,128)(2,1)S(1)}, bf16[4,128,256]{2,1,0:T(8,128)(2,1)S(1)}, u32[]{:S(2)}, u32[]{:S(2)}) collective-permute-start(bf16[4,128,256]{2,1,0:T(8,128)(2,1)S(1)} %get-tuple-element.75.refs_3_), channel_id=1, source_target_pairs={{0,8},{1,9},{2,10},{3,11},{4,0},{5,1},{6,2},{7,3},{8,12},{9,13},{1... | collective-permute-start | bytes 786440 | tf_op jit(solution)/shard_map/ppermute | solution.py:49
  82.6 9.2 %collective-permute-start.26 = (bf16[4,128,256]{2,1,0:T(8,128)(2,1)S(1)}, bf16[4,128,256]{2,1,0:T(8,128)(2,1)S(1)}, u32[]{:S(2)}, u32[]{:S(2)}) collective-permute-start(bf16[4,128,256]{2,1,0:T(8,128)(2,1)S(1)} %get-tuple-element.75.refs_3_), channel_id=1, source_target_pairs={{0,2},{1,3},{2,0},{3,1},{4,6},{5,7},{6,4},{7,5},{8,10},{9,11},{10,... | collective-permute-start | bytes 786440 | tf_op jit(solution)/shard_map/ppermute | solution.py:40
  85.9 11.2 %collective-permute-start.35 = (bf16[4,128,256]{2,1,0:T(8,128)(2,1)S(1)}, bf16[4,128,256]{2,1,0:T(8,128)(2,1)S(1)}, u32[]{:S(2)}, u32[]{:S(2)}) collective-permute-start(bf16[4,128,256]{2,1,0:T(8,128)(2,1)S(1)} %get-tuple-element.82.refs_12_), channel_id=1, source_target_pairs={{0,8},{1,9},{2,10},{3,11},{4,0},{5,1},{6,2},{7,3},{8,12},{9,13},{1... | collective-permute-start | bytes 786440 | tf_op jit(solution)/shard_map/ppermute | solution.py:49
  86.2 11.2 %collective-permute-start.34 = (bf16[4,128,256]{2,1,0:T(8,128)(2,1)S(1)}, bf16[4,128,256]{2,1,0:T(8,128)(2,1)S(1)}, u32[]{:S(2)}, u32[]{:S(2)}) collective-permute-start(bf16[4,128,256]{2,1,0:T(8,128)(2,1)S(1)} %get-tuple-element.82.refs_12_), channel_id=1, source_target_pairs={{0,2},{1,3},{2,0},{3,1},{4,6},{5,7},{6,4},{7,5},{8,10},{9,11},{10,... | collective-permute-start | bytes 786440 | tf_op jit(solution)/shard_map/ppermute | solution.py:40
  91.8 11.0 %collective-permute-start.29 = (bf16[4,128,256]{2,1,0:T(8,128)(2,1)S(1)}, bf16[4,128,256]{2,1,0:T(8,128)(2,1)S(1)}, u32[]{:S(2)}, u32[]{:S(2)}) collective-permute-start(bf16[4,128,256]{2,1,0:T(8,128)(2,1)S(1)} %collective-permute-done.27.refs_4_), channel_id=1, source_target_pairs={{0,8},{1,9},{2,10},{3,11},{4,0},{5,1},{6,2},{7,3},{8,12},{9,13},{1... | collective-permute-start | bytes 786440 | tf_op jit(solution)/shard_map/ppermute | solution.py:49
  92.7 10.3 %collective-permute-start.28 = (bf16[4,128,256]{2,1,0:T(8,128)(2,1)S(1)}, bf16[4,128,256]{2,1,0:T(8,128)(2,1)S(1)}, u32[]{:S(2)}, u32[]{:S(2)}) collective-permute-start(bf16[4,128,256]{2,1,0:T(8,128)(2,1)S(1)} %collective-permute-done.27.refs_4_), channel_id=1, source_target_pairs={{0,2},{1,3},{2,0},{3,1},{4,6},{5,7},{6,4},{7,5},{8,10},{9,11},{10,... | collective-permute-start | bytes 786440 | tf_op jit(solution)/shard_map/ppermute | solution.py:40
  97.4 11.0 %collective-permute-start.37 = (bf16[4,128,256]{2,1,0:T(8,128)(2,1)S(1)}, bf16[4,128,256]{2,1,0:T(8,128)(2,1)S(1)}, u32[]{:S(2)}, u32[]{:S(2)}) collective-permute-start(bf16[4,128,256]{2,1,0:T(8,128)(2,1)S(1)} %collective-permute-done.35.refs_13_), channel_id=1, source_target_pairs={{0,8},{1,9},{2,10},{3,11},{4,0},{5,1},{6,2},{7,3},{8,12},{9,13},{1... | collective-permute-start | bytes 786440 | tf_op jit(solution)/shard_map/ppermute | solution.py:49
  98.3 10.3 %collective-permute-start.36 = (bf16[4,128,256]{2,1,0:T(8,128)(2,1)S(1)}, bf16[4,128,256]{2,1,0:T(8,128)(2,1)S(1)}, u32[]{:S(2)}, u32[]{:S(2)}) collective-permute-start(bf16[4,128,256]{2,1,0:T(8,128)(2,1)S(1)} %collective-permute-done.35.refs_13_), channel_id=1, source_target_pairs={{0,2},{1,3},{2,0},{3,1},{4,6},{5,7},{6,4},{7,5},{8,10},{9,11},{10,... | collective-permute-start | bytes 786440 | tf_op jit(solution)/shard_map/ppermute | solution.py:40
  103.0 11.0 %collective-permute-start.31 = (bf16[4,128,256]{2,1,0:T(8,128)(2,1)S(1)}, bf16[4,128,256]{2,1,0:T(8,128)(2,1)S(1)}, u32[]{:S(2)}, u32[]{:S(2)}) collective-permute-start(bf16[4,128,256]{2,1,0:T(8,128)(2,1)S(1)} %collective-permute-done.29.refs_5_), channel_id=1, source_target_pairs={{0,8},{1,9},{2,10},{3,11},{4,0},{5,1},{6,2},{7,3},{8,12},{9,13},{1... | collective-permute-start | bytes 786440 | tf_op jit(solution)/shard_map/ppermute | solution.py:49
  103.9 10.3 %collective-permute-start.30 = (bf16[4,128,256]{2,1,0:T(8,128)(2,1)S(1)}, bf16[4,128,256]{2,1,0:T(8,128)(2,1)S(1)}, u32[]{:S(2)}, u32[]{:S(2)}) collective-permute-start(bf16[4,128,256]{2,1,0:T(8,128)(2,1)S(1)} %collective-permute-done.29.refs_5_), channel_id=1, source_target_pairs={{0,2},{1,3},{2,0},{3,1},{4,6},{5,7},{6,4},{7,5},{8,10},{9,11},{10,... | collective-permute-start | bytes 786440 | tf_op jit(solution)/shard_map/ppermute | solution.py:40
  108.6 11.0 %collective-permute-start.39 = (bf16[4,128,256]{2,1,0:T(8,128)(2,1)S(1)}, bf16[4,128,256]{2,1,0:T(8,128)(2,1)S(1)}, u32[]{:S(2)}, u32[]{:S(2)}) collective-permute-start(bf16[4,128,256]{2,1,0:T(8,128)(2,1)S(1)} %collective-permute-done.37.refs_14_), channel_id=1, source_target_pairs={{0,8},{1,9},{2,10},{3,11},{4,0},{5,1},{6,2},{7,3},{8,12},{9,13},{1... | collective-permute-start | bytes 786440 | tf_op jit(solution)/shard_map/ppermute | solution.py:49
  109.5 10.3 %collective-permute-start.38 = (bf16[4,128,256]{2,1,0:T(8,128)(2,1)S(1)}, bf16[4,128,256]{2,1,0:T(8,128)(2,1)S(1)}, u32[]{:S(2)}, u32[]{:S(2)}) collective-permute-start(bf16[4,128,256]{2,1,0:T(8,128)(2,1)S(1)} %collective-permute-done.37.refs_14_), channel_id=1, source_target_pairs={{0,2},{1,3},{2,0},{3,1},{4,6},{5,7},{6,4},{7,5},{8,10},{9,11},{10,... | collective-permute-start | bytes 786440 | tf_op jit(solution)/shard_map/ppermute | solution.py:40
  114.3 8.1 %collective-permute-start.33 = (bf16[2,128,256]{2,1,0:T(8,128)(2,1)S(1)}, bf16[2,128,256]{2,1,0:T(8,128)(2,1)S(1)}, u32[]{:S(2)}, u32[]{:S(2)}) collective-permute-start(bf16[2,128,256]{2,1,0:T(8,128)(2,1)S(1)} %slice.93), channel_id=1, source_target_pairs={{0,8},{1,9},{2,10},{3,11},{4,0},{5,1},{6,2},{7,3},{8,12},{9,13},{1... | collective-permute-start | bytes 393224 | tf_op jit(solution)/shard_map/ppermute | solution.py:49
  115.2 7.2 %collective-permute-start.32 = (bf16[2,128,256]{2,1,0:T(8,128)(2,1)S(1)}, bf16[2,128,256]{2,1,0:T(8,128)(2,1)S(1)}, u32[]{:S(2)}, u32[]{:S(2)}) collective-permute-start(bf16[2,128,256]{2,1,0:T(8,128)(2,1)S(1)} %slice.92), channel_id=1, source_target_pairs={{0,2},{1,3},{2,0},{3,1},{4,6},{5,7},{6,4},{7,5},{8,10},{9,11},{10,... | collective-permute-start | bytes 393224 | tf_op jit(solution)/shard_map/ppermute | solution.py:40
  119.9 5.0 %collective-permute-start.41 = (bf16[2,128,256]{2,1,0:T(8,128)(2,1)S(1)}, bf16[2,128,256]{2,1,0:T(8,128)(2,1)S(1)}, u32[]{:S(2)}, u32[]{:S(2)}) collective-permute-start(bf16[2,128,256]{2,1,0:T(8,128)(2,1)S(1)} %slice.95), channel_id=1, source_target_pairs={{0,8},{1,9},{2,10},{3,11},{4,0},{5,1},{6,2},{7,3},{8,12},{9,13},{1... | collective-permute-start | bytes 393224 | tf_op jit(solution)/shard_map/ppermute | solution.py:49
  120.8 5.0 %collective-permute-start.40 = (bf16[2,128,256]{2,1,0:T(8,128)(2,1)S(1)}, bf16[2,128,256]{2,1,0:T(8,128)(2,1)S(1)}, u32[]{:S(2)}, u32[]{:S(2)}) collective-permute-start(bf16[2,128,256]{2,1,0:T(8,128)(2,1)S(1)} %slice.94), channel_id=1, source_target_pairs={{0,2},{1,3},{2,0},{3,1},{4,6},{5,7},{6,4},{7,5},{8,10},{9,11},{10,... | collective-permute-start | bytes 393224 | tf_op jit(solution)/shard_map/ppermute | solution.py:40
  126.8 1.6 %collective-permute-start.42 = (bf16[4,128,256]{2,1,0:T(8,128)(2,1)S(1)}, bf16[4,128,256]{2,1,0:T(8,128)(2,1)S(1)}, u32[]{:S(2)}, u32[]{:S(2)}) collective-permute-start(bf16[4,128,256]{2,1,0:T(8,128)(2,1)S(1)} %get-tuple-element.90), channel_id=1, source_target_pairs={{0,1},{1,0},{2,3},{3,2},{4,5},{5,4},{6,7},{7,6},{8,9},{9,8},{10,11... | collective-permute-start | bytes 786440 | tf_op jit(solution)/shard_map/ppermute | solution.py:40

commit v16 on v15

--- a/solution.py
+++ b/solution.py
@@ -143,11 +143,12 @@
 def newton_inverses(matrices):
     shape = matrices[0].shape
     same = lax.broadcasted_iota(jnp.int32, shape, 0) == lax.broadcasted_iota(jnp.int32, shape, 1)
-    twice = jnp.where(same, 2.0, 0.0).astype(F32)
-    estimates = [twice - matrix for matrix in matrices]
+    identity = jnp.where(same, 1.0, 0.0).astype(F32)
+    powers = [identity - matrix for matrix in matrices]
+    estimates = [identity + power for power in powers]
     for _ in range(ITERS - 1):
-        steps = [twice - product(a, x) for a, x in zip(matrices, estimates)]
-        estimates = [product(x, step) for x, step in zip(estimates, steps)]
+        powers = [product(power, power) for power in powers]
+        estimates = [x + product(x, power) for x, power in zip(estimates, powers)]
     return estimates
 
 

time: 130 us -> 130 us (level)
  no operation moved by 1% of the time
where the time goes in v16:
time: 130 us
  waiting for transfers between devices  55 us (42%)
  starting transfers between devices  45.5 us (35%)
  Pallas kernels  15 us (12%)
  blocking collectives  9.88 us (8%)
  local copies, waits for them, and re-layouts  3.52 us (3%)
    ppermute x16, waiting for transfers between devices, step(): return lax.ppermute(array, 'chol', pairs)  32 us
    ppermute x25, waiting for transfers between devices, shift(): return lax.ppermute(array, 'chol', pairs)  22.1 us
    ppermute x16, starting transfers between devices, step(): return lax.ppermute(array, 'chol', pairs)  21.9 us
    ppermute x25, starting transfers between devices, shift(): return lax.ppermute(array, 'chol', pairs)  20.9 us
    all_to_all x1, blocking collectives, shards(): parts = lax.all_to_all(parts, 'chol', 0, 0, tiled=True)  9.88 us
    unnamed x26, local copies, waits for them, and re-layouts  3.42 us
    pallas_call x1, Pallas kernels, inverses_of(): pl.pallas_call(functools.partial(inverse_kernel, layout, slabs, counts),...  3.29 us
    pallas_call x1, Pallas kernels, potential_of(): pl.pallas_call(potential_kernel, out_shape=[jax.ShapeDtypeStruct((per_gro...  3.17 us
  transfers between devices with their start and end apart: 43, of which 34 were waited for; matrix products, arithmetic and copies ran while one was open for 0% of the time, Pallas kernels for 4%

profile of v16, /device:TPU:0, one launch (start us, length us, event | category | flops | bytes accessed | tf_op | source)
XLA Modules:
  0.0 129.8 jit_solution(11751473472298592584)
XLA Ops:
  0.6 1.0 copy-done.2
  2.3 2.0 %shard_map.77 = (bf16[2,128,256]{2,1,0:T(8,128)(2,1)S(1)}, bf16[2,128,256]{2,1,0:T(8,128)(2,1)S(1)}, bf16[2,128,256]{2,1,0:T(8,128)(2,1)S(1)}, bf16[2,128,256]{2,1,0:T(8,128)(2,1)S(1)}, s32[8]{0:T(128)S(1)}) custom-call(s32[16]{0:T(128)S(1)} %copy-done.6, bf16[8,128,256]{2,1,0:T(8,128)(2,1)S(1)} %copy-done.2), custom_call_target="tpu_custom_call" | custom-call | tf_op jit(solution)/shard_map/pallas_call | solution.py:497
  4.9 2.6 %collective-permute-start.1 = (bf16[2,128,256]{2,1,0:T(8,128)(2,1)S(1)}, bf16[2,128,256]{2,1,0:T(8,128)(2,1)S(1)}, u32[]{:S(2)}, u32[]{:S(2)}) collective-permute-start(bf16[2,128,256]{2,1,0:T(8,128)(2,1)S(1)} %get-tuple-element.48), channel_id=1, source_target_pairs={{0,16},{1,17},{2,18},{3,19},{4,20},{5,21},{6,22},{7,23},{8,24},{9,... | collective-permute-start | bytes 393224 | tf_op jit(solution)/shard_map/ppermute | solution.py:526
  7.6 0.8 copy-done.3
  8.5 3.1 %collective-permute-start.12 = (bf16[9,64,256]{2,1,0:T(8,128)(2,1)S(1)}, bf16[9,64,256]{2,1,0:T(8,128)(2,1)S(1)}, u32[]{:S(2)}, u32[]{:S(2)}) collective-permute-start(bf16[9,64,256]{2,1,0:T(8,128)(2,1)S(1)} %shard_map.79.refs_13_), channel_id=1, source_target_pairs={{0,8},{1,9},{2,10},{3,11},{4,0},{5,1},{6,2},{7,3},{8,12},{9,13},{1... | collective-permute-start | bytes 884744 | tf_op jit(solution)/shard_map/ppermute | solution.py:49
  11.6 1.5 %collective-permute-start.11 = (bf16[9,64,256]{2,1,0:T(8,128)(2,1)S(1)}, bf16[9,64,256]{2,1,0:T(8,128)(2,1)S(1)}, u32[]{:S(2)}, u32[]{:S(2)}) collective-permute-start(bf16[9,64,256]{2,1,0:T(8,128)(2,1)S(1)} %shard_map.79.refs_13_), channel_id=1, source_target_pairs={{0,2},{1,3},{2,0},{3,1},{4,6},{5,7},{6,4},{7,5},{8,10},{9,11},{10,... | collective-permute-start | bytes 884744 | tf_op jit(solution)/shard_map/ppermute | solution.py:40
  13.1 0.9 collective-permute-done.2.other
  14.1 0.8 copy-done.4
  14.9 2.7 %collective-permute-start.4 = (bf16[9,64,256]{2,1,0:T(8,128)(2,1)S(1)}, bf16[9,64,256]{2,1,0:T(8,128)(2,1)S(1)}, u32[]{:S(2)}, u32[]{:S(2)}) collective-permute-start(bf16[9,64,256]{2,1,0:T(8,128)(2,1)S(1)} %shard_map.78.refs_4_), channel_id=1, source_target_pairs={{0,8},{1,9},{2,10},{3,11},{4,0},{5,1},{6,2},{7,3},{8,12},{9,13},{1... | collective-permute-start | bytes 884744 | tf_op jit(solution)/shard_map/ppermute | solution.py:49
  17.7 1.5 %collective-permute-start.3 = (bf16[9,64,256]{2,1,0:T(8,128)(2,1)S(1)}, bf16[9,64,256]{2,1,0:T(8,128)(2,1)S(1)}, u32[]{:S(2)}, u32[]{:S(2)}) collective-permute-start(bf16[9,64,256]{2,1,0:T(8,128)(2,1)S(1)} %shard_map.78.refs_4_), channel_id=1, source_target_pairs={{0,2},{1,3},{2,0},{3,1},{4,6},{5,7},{6,4},{7,5},{8,10},{9,11},{10,... | collective-permute-start | bytes 884744 | tf_op jit(solution)/shard_map/ppermute | solution.py:40
  19.2 1.2 collective-permute-done.11.refs_17_
  20.4 1.6 %collective-permute-start.14 = (bf16[9,64,256]{2,1,0:T(8,128)(2,1)S(1)}, bf16[9,64,256]{2,1,0:T(8,128)(2,1)S(1)}, u32[]{:S(2)}, u32[]{:S(2)}) collective-permute-start(bf16[9,64,256]{2,1,0:T(8,128)(2,1)S(1)} %collective-permute-done.12.refs_14_), channel_id=1, source_target_pairs={{0,8},{1,9},{2,10},{3,11},{4,0},{5,1},{6,2},{7,3},{8,12},{9,13},{1... | collective-permute-start | bytes 884744 | tf_op jit(solution)/shard_map/ppermute | solution.py:49
  22.0 1.5 %collective-permute-start.13 = (bf16[9,64,256]{2,1,0:T(8,128)(2,1)S(1)}, bf16[9,64,256]{2,1,0:T(8,128)(2,1)S(1)}, u32[]{:S(2)}, u32[]{:S(2)}) collective-permute-start(bf16[9,64,256]{2,1,0:T(8,128)(2,1)S(1)} %collective-permute-done.12.refs_14_), channel_id=1, source_target_pairs={{0,2},{1,3},{2,0},{3,1},{4,6},{5,7},{6,4},{7,5},{8,10},{9,11},{10,... | collective-permute-start | bytes 884744 | tf_op jit(solution)/shard_map/ppermute | solution.py:40
  23.5 1.5 %collective-permute-done.4.refs_5_ = bf16[9,64,256]{2,1,0:T(8,128)(2,1)S(1)} collective-permute-done((bf16[9,64,256]{2,1,0:T(8,128)(2,1)S(1)}, bf16[9,64,256]{2,1,0:T(8,128)(2,1)S(1)}, u32[]{:S(2)}, u32[]{:S(2)}) %collective-permute-start.4) | collective-permute-done | bytes 294944 | tf_op jit(solution)/shard_map/ppermute | solution.py:49
  25.0 2.5 %collective-permute-done.3.refs_8_ = bf16[9,64,256]{2,1,0:T(8,128)(2,1)S(1)} collective-permute-done((bf16[9,64,256]{2,1,0:T(8,128)(2,1)S(1)}, bf16[9,64,256]{2,1,0:T(8,128)(2,1)S(1)}, u32[]{:S(2)}, u32[]{:S(2)}) %collective-permute-start.3) | collective-permute-done | bytes 294944 | tf_op jit(solution)/shard_map/ppermute | solution.py:40
  27.5 1.6 %collective-permute-start.6 = (bf16[9,64,256]{2,1,0:T(8,128)(2,1)S(1)}, bf16[9,64,256]{2,1,0:T(8,128)(2,1)S(1)}, u32[]{:S(2)}, u32[]{:S(2)}) collective-permute-start(bf16[9,64,256]{2,1,0:T(8,128)(2,1)S(1)} %collective-permute-done.4.refs_5_), channel_id=1, source_target_pairs={{0,8},{1,9},{2,10},{3,11},{4,0},{5,1},{6,2},{7,3},{8,12},{9,13},{1... | collective-permute-start | bytes 884744 | tf_op jit(solution)/shard_map/ppermute | solution.py:49
  29.1 1.5 %collective-permute-start.5 = (bf16[9,64,256]{2,1,0:T(8,128)(2,1)S(1)}, bf16[9,64,256]{2,1,0:T(8,128)(2,1)S(1)}, u32[]{:S(2)}, u32[]{:S(2)}) collective-permute-start(bf16[9,64,256]{2,1,0:T(8,128)(2,1)S(1)} %collective-permute-done.4.refs_5_), channel_id=1, source_target_pairs={{0,2},{1,3},{2,0},{3,1},{4,6},{5,7},{6,4},{7,5},{8,10},{9,11},{10,... | collective-permute-start | bytes 884744 | tf_op jit(solution)/shard_map/ppermute | solution.py:40
  30.6 0.7 collective-permute-done.14.refs_15_
  31.3 2.5 %collective-permute-done.13.refs_18_ = bf16[9,64,256]{2,1,0:T(8,128)(2,1)S(1)} collective-permute-done((bf16[9,64,256]{2,1,0:T(8,128)(2,1)S(1)}, bf16[9,64,256]{2,1,0:T(8,128)(2,1)S(1)}, u32[]{:S(2)}, u32[]{:S(2)}) %collective-permute-start.13) | collective-permute-done | bytes 294944 | tf_op jit(solution)/shard_map/ppermute | solution.py:40
  33.8 1.6 %collective-permute-start.16 = (bf16[9,64,256]{2,1,0:T(8,128)(2,1)S(1)}, bf16[9,64,256]{2,1,0:T(8,128)(2,1)S(1)}, u32[]{:S(2)}, u32[]{:S(2)}) collective-permute-start(bf16[9,64,256]{2,1,0:T(8,128)(2,1)S(1)} %collective-permute-done.14.refs_15_), channel_id=1, source_target_pairs={{0,8},{1,9},{2,10},{3,11},{4,0},{5,1},{6,2},{7,3},{8,12},{9,13},{1... | collective-permute-start | bytes 884744 | tf_op jit(solution)/shard_map/ppermute | solution.py:49
  35.4 1.5 %collective-permute-start.15 = (bf16[9,64,256]{2,1,0:T(8,128)(2,1)S(1)}, bf16[9,64,256]{2,1,0:T(8,128)(2,1)S(1)}, u32[]{:S(2)}, u32[]{:S(2)}) collective-permute-start(bf16[9,64,256]{2,1,0:T(8,128)(2,1)S(1)} %collective-permute-done.14.refs_15_), channel_id=1, source_target_pairs={{0,2},{1,3},{2,0},{3,1},{4,6},{5,7},{6,4},{7,5},{8,10},{9,11},{10,... | collective-permute-start | bytes 884744 | tf_op jit(solution)/shard_map/ppermute | solution.py:40
  36.9 0.7 collective-permute-done.6.refs_6_
  37.6 2.5 %collective-permute-done.5.refs_9_ = bf16[9,64,256]{2,1,0:T(8,128)(2,1)S(1)} collective-permute-done((bf16[9,64,256]{2,1,0:T(8,128)(2,1)S(1)}, bf16[9,64,256]{2,1,0:T(8,128)(2,1)S(1)}, u32[]{:S(2)}, u32[]{:S(2)}) %collective-permute-start.5) | collective-permute-done | bytes 294944 | tf_op jit(solution)/shard_map/ppermute | solution.py:40
  40.1 1.6 %collective-permute-start.8 = (bf16[9,64,256]{2,1,0:T(8,128)(2,1)S(1)}, bf16[9,64,256]{2,1,0:T(8,128)(2,1)S(1)}, u32[]{:S(2)}, u32[]{:S(2)}) collective-permute-start(bf16[9,64,256]{2,1,0:T(8,128)(2,1)S(1)} %collective-permute-done.6.refs_6_), channel_id=1, source_target_pairs={{0,8},{1,9},{2,10},{3,11},{4,0},{5,1},{6,2},{7,3},{8,12},{9,13},{1... | collective-permute-start | bytes 884744 | tf_op jit(solution)/shard_map/ppermute | solution.py:49
  41.7 1.5 %collective-permute-start.7 = (bf16[9,64,256]{2,1,0:T(8,128)(2,1)S(1)}, bf16[9,64,256]{2,1,0:T(8,128)(2,1)S(1)}, u32[]{:S(2)}, u32[]{:S(2)}) collective-permute-start(bf16[9,64,256]{2,1,0:T(8,128)(2,1)S(1)} %collective-permute-done.6.refs_6_), channel_id=1, source_target_pairs={{0,2},{1,3},{2,0},{3,1},{4,6},{5,7},{6,4},{7,5},{8,10},{9,11},{10,... | collective-permute-start | bytes 884744 | tf_op jit(solution)/shard_map/ppermute | solution.py:40
  43.2 0.7 collective-permute-done.16.refs_16_
  43.9 2.5 %collective-permute-done.15.refs_19_ = bf16[9,64,256]{2,1,0:T(8,128)(2,1)S(1)} collective-permute-done((bf16[9,64,256]{2,1,0:T(8,128)(2,1)S(1)}, bf16[9,64,256]{2,1,0:T(8,128)(2,1)S(1)}, u32[]{:S(2)}, u32[]{:S(2)}) %collective-permute-start.15) | collective-permute-done | bytes 294944 | tf_op jit(solution)/shard_map/ppermute | solution.py:40
  46.5 1.6 %collective-permute-start.19 = (bf16[4,64,256]{2,1,0:T(8,128)(2,1)S(1)}, bf16[4,64,256]{2,1,0:T(8,128)(2,1)S(1)}, u32[]{:S(2)}, u32[]{:S(2)}) collective-permute-start(bf16[4,64,256]{2,1,0:T(8,128)(2,1)S(1)} %slice.87), channel_id=1, source_target_pairs={{0,8},{1,9},{2,10},{3,11},{4,0},{5,1},{6,2},{7,3},{8,12},{9,13},{1... | collective-permute-start | bytes 393224 | tf_op jit(solution)/shard_map/ppermute | solution.py:49
  48.1 1.5 %collective-permute-start.18 = (bf16[5,64,256]{2,1,0:T(8,128)(2,1)S(1)}, bf16[5,64,256]{2,1,0:T(8,128)(2,1)S(1)}, u32[]{:S(2)}, u32[]{:S(2)}) collective-permute-start(bf16[5,64,256]{2,1,0:T(8,128)(2,1)S(1)} %slice.86), channel_id=1, source_target_pairs={{0,2},{1,3},{2,0},{3,1},{4,6},{5,7},{6,4},{7,5},{8,10},{9,11},{10,... | collective-permute-start | bytes 491528 | tf_op jit(solution)/shard_map/ppermute | solution.py:40
  50.2 2.5 %collective-permute-done.7.refs_10_ = bf16[9,64,256]{2,1,0:T(8,128)(2,1)S(1)} collective-permute-done((bf16[9,64,256]{2,1,0:T(8,128)(2,1)S(1)}, bf16[9,64,256]{2,1,0:T(8,128)(2,1)S(1)}, u32[]{:S(2)}, u32[]{:S(2)}) %collective-permute-start.7) | collective-permute-done | bytes 294944 | tf_op jit(solution)/shard_map/ppermute | solution.py:40
  52.9 1.6 %collective-permute-start.22 = (bf16[5,64,256]{2,1,0:T(8,128)(2,1)S(1)}, bf16[5,64,256]{2,1,0:T(8,128)(2,1)S(1)}, u32[]{:S(2)}, u32[]{:S(2)}) collective-permute-start(bf16[5,64,256]{2,1,0:T(8,128)(2,1)S(1)} %slice.90), channel_id=1, source_target_pairs={{0,2},{1,3},{2,0},{3,1},{4,6},{5,7},{6,4},{7,5},{8,10},{9,11},{10,... | collective-permute-start | bytes 491528 | tf_op jit(solution)/shard_map/ppermute | solution.py:40
  54.5 1.1 collective-permute-done.18.refs_20_
  55.6 2.1 %collective-permute-start.23 = (bf16[4,64,256]{2,1,0:T(8,128)(2,1)S(1)}, bf16[4,64,256]{2,1,0:T(8,128)(2,1)S(1)}, u32[]{:S(2)}, u32[]{:S(2)}) collective-permute-start(bf16[4,64,256]{2,1,0:T(8,128)(2,1)S(1)} %slice.91), channel_id=1, source_target_pairs={{0,8},{1,9},{2,10},{3,11},{4,0},{5,1},{6,2},{7,3},{8,12},{9,13},{1... | collective-permute-start | bytes 393224 | tf_op jit(solution)/shard_map/ppermute | solution.py:49
  57.7 1.0 collective-permute-start.21
  58.8 1.1 collective-permute-start.20
  59.8 0.8 collective-permute-done.23.refs_12_
  60.6 1.0 collective-permute-done.21.refs_3_
  61.6 1.1 collective-permute-done.20.refs_2_
  62.7 3.3 %shard_map.80 = (bf16[2,8,2,128,256]{4,3,2,1,0:T(8,128)(2,1)S(1)}, bf16[2,8,2,128,256]{4,3,2,1,0:T(8,128)(2,1)S(1)}, bf16[4,256,256]{2,1,0:T(8,128)(2,1)S(1)}) custom-call(bf16[7,64,256]{2,1,0:T(8,128)(2,1)S(1)} %collective-permute-done.9.refs_0_, bf16[7,64,256]{2,1,0:T(8,128)(2,1)S(1)} %collective-permute-done.17.refs_1_, ...), custom_call_target="tpu_custom_call" | custom-call | flops 2684354560 | bytes 10485760 | tf_op jit(solution)/shard_map/pallas_call | solution.py:193
  66.1 1.7 %shard_map.81 = f32[16,8,128]{2,1,0:T(8,128)S(1)} custom-call(bf16[32,128,256]{2,1,0:T(8,128)(2,1)S(1)} %copy-done.1, bf16[32,128,256]{2,1,0:T(8,128)(2,1)S(1)} %collective-permute-done.rot_theirs, bf16[4,256,256]{2,1,0:T(8,128)(2,1)S(1)} %get-tuple-element.67.inverses, bf16[2,8,2,128,256]{4,3,2,1,0:T(8,128)(2,1)S(1)} %get-tuple-element.68.refs_0_.refs_1_.refs_2_, ...), custom_call_target="tpu_custom_call" | custom-call | flops 402653184 | bytes 4718592 | tf_op jit(solution)/shard_map/pallas_call | solution.py:255
  67.8 9.9 %all_to_all.5.parts = f32[16,8,128]{2,1,0:T(8,128)S(1)} all-to-all(f32[16,8,128]{2,1,0:T(8,128)S(1)} %shard_map.81), channel_id=1, replica_groups=mesh['walk'=2,'chol'=16] {'chol'}, dimensions={0} | all-to-all | bytes 131072 | tf_op jit(solution)/shard_map/all_to_all | solution.py:581
  77.7 3.2 %shard_map.82 = (f32[8,32]{1,0:T(8,128)}, bf16[4,128,2048]{2,1,0:T(8,128)(2,1)S(1)}, bf16[4,64,2048]{2,1,0:T(8,128)(2,1)S(1)}, bf16[4,64,2048]{2,1,0:T(8,128)(2,1)S(1)}) custom-call(s32[8]{0:T(128)S(1)} %get-tuple-element.47.order, f32[8,32]{1,0:T(8,128)S(1)} %copy-done.5, f32[16,8,128]{2,1,0:T(8,128)S(1)} %all_to_all.5.parts, bf16[32,128,2048]{2,1,0:T(8,128)(2,1)S(1)} %copy-done), custom_call_target="tpu_custom_call" | custom-call | tf_op jit(solution)/shard_map/pallas_call | solution.py:321
  81.4 0.8 shard_map.83
  83.6 1.5 %collective-permute-done.25.refs_1_ = bf16[4,64,2048]{2,1,0:T(8,128)(2,1)S(1)} collective-permute-done((bf16[4,64,2048]{2,1,0:T(8,128)(2,1)S(1)}, bf16[4,64,2048]{2,1,0:T(8,128)(2,1)S(1)}, u32[]{:S(2)}, u32[]{:S(2)}) %collective-permute-start.25) | collective-permute-done | bytes 1048608 | tf_op jit(solution)/shard_map/ppermute | solution.py:40
  85.1 0.8 shard_map.84
  86.8 4.6 %collective-permute-done.27.refs_4_ = bf16[4,128,256]{2,1,0:T(8,128)(2,1)S(1)} collective-permute-done((bf16[4,128,256]{2,1,0:T(8,128)(2,1)S(1)}, bf16[4,128,256]{2,1,0:T(8,128)(2,1)S(1)}, u32[]{:S(2)}, u32[]{:S(2)}) %collective-permute-start.27) | collective-permute-done | bytes 262176 | tf_op jit(solution)/shard_map/ppermute | solution.py:49
  91.7 0.9 collective-permute-start.29
  93.3 3.8 %collective-permute-done.35.refs_13_ = bf16[4,128,256]{2,1,0:T(8,128)(2,1)S(1)} collective-permute-done((bf16[4,128,256]{2,1,0:T(8,128)(2,1)S(1)}, bf16[4,128,256]{2,1,0:T(8,128)(2,1)S(1)}, u32[]{:S(2)}, u32[]{:S(2)}) %collective-permute-start.35) | collective-permute-done | bytes 262176 | tf_op jit(solution)/shard_map/ppermute | solution.py:49
  97.3 0.9 collective-permute-start.37
  98.9 3.8 %collective-permute-done.29.refs_5_ = bf16[4,128,256]{2,1,0:T(8,128)(2,1)S(1)} collective-permute-done((bf16[4,128,256]{2,1,0:T(8,128)(2,1)S(1)}, bf16[4,128,256]{2,1,0:T(8,128)(2,1)S(1)}, u32[]{:S(2)}, u32[]{:S(2)}) %collective-permute-start.29) | collective-permute-done | bytes 262176 | tf_op jit(solution)/shard_map/ppermute | solution.py:49
  102.9 0.9 collective-permute-start.31
  104.5 3.8 %collective-permute-done.37.refs_14_ = bf16[4,128,256]{2,1,0:T(8,128)(2,1)S(1)} collective-permute-done((bf16[4,128,256]{2,1,0:T(8,128)(2,1)S(1)}, bf16[4,128,256]{2,1,0:T(8,128)(2,1)S(1)}, u32[]{:S(2)}, u32[]{:S(2)}) %collective-permute-start.37) | collective-permute-done | bytes 262176 | tf_op jit(solution)/shard_map/ppermute | solution.py:49
  108.6 0.9 collective-permute-start.39
  110.1 3.8 %collective-permute-done.31.refs_6_ = bf16[4,128,256]{2,1,0:T(8,128)(2,1)S(1)} collective-permute-done((bf16[4,128,256]{2,1,0:T(8,128)(2,1)S(1)}, bf16[4,128,256]{2,1,0:T(8,128)(2,1)S(1)}, u32[]{:S(2)}, u32[]{:S(2)}) %collective-permute-start.31) | collective-permute-done | bytes 262176 | tf_op jit(solution)/shard_map/ppermute | solution.py:49
  114.2 1.0 collective-permute-start.33
  115.8 3.7 %collective-permute-done.39.refs_15_ = bf16[4,128,256]{2,1,0:T(8,128)(2,1)S(1)} collective-permute-done((bf16[4,128,256]{2,1,0:T(8,128)(2,1)S(1)}, bf16[4,128,256]{2,1,0:T(8,128)(2,1)S(1)}, u32[]{:S(2)}, u32[]{:S(2)}) %collective-permute-start.39) | collective-permute-done | bytes 262176 | tf_op jit(solution)/shard_map/ppermute | solution.py:49
  119.8 1.0 collective-permute-start.41
  121.4 0.9 collective-permute-done.33.refs_11_
  122.4 2.5 %collective-permute-done.41.refs_20_ = bf16[2,128,256]{2,1,0:T(8,128)(2,1)S(1)} collective-permute-done((bf16[2,128,256]{2,1,0:T(8,128)(2,1)S(1)}, bf16[2,128,256]{2,1,0:T(8,128)(2,1)S(1)}, u32[]{:S(2)}, u32[]{:S(2)}) %collective-permute-start.41) | collective-permute-done | bytes 131104 | tf_op jit(solution)/shard_map/ppermute | solution.py:49
  124.8 0.9 collective-permute-done.40.refs_19_
  125.8 1.0 shard_map.85
  126.9 0.7 shard_map.86.mine
  127.6 0.8 collective-permute-done.42.theirs
  128.4 1.4 %shard_map.87 = bf16[8,128,256]{2,1,0:T(8,128)(2,1)} custom-call(s32[8]{0:T(128)S(1)} %get-tuple-element.47.order, bf16[4,128,256]{2,1,0:T(8,128)(2,1)S(1)} %shard_map.86.mine, bf16[4,128,256]{2,1,0:T(8,128)(2,1)S(1)} %collective-permute-done.42.theirs), custom_call_target="tpu_custom_call" | custom-call | tf_op jit(solution)/shard_map/pallas_call | solution.py:447
  (72 shorter events, 10.5 us)
Async XLA Ops:
  0.6 1.0 copy-start.2
  1.7 0.7 copy-start.6
  4.3 3.3 %collective-permute-start.10 = (bf16[2,128,256]{2,1,0:T(8,128)(2,1)S(1)}, bf16[2,128,256]{2,1,0:T(8,128)(2,1)S(1)}, u32[]{:S(2)}, u32[]{:S(2)}) collective-permute-start(bf16[2,128,256]{2,1,0:T(8,128)(2,1)S(1)} %get-tuple-element.57), channel_id=1, source_target_pairs={{0,1},{1,0},{2,3},{3,2},{4,5},{5,4},{6,7},{7,6},{8,9},{9,8},{10,11... | collective-permute-start | bytes 393224 | tf_op jit(solution)/shard_map/ppermute | solution.py:40
  4.9 8.3 %collective-permute-start.1 = (bf16[2,128,256]{2,1,0:T(8,128)(2,1)S(1)}, bf16[2,128,256]{2,1,0:T(8,128)(2,1)S(1)}, u32[]{:S(2)}, u32[]{:S(2)}) collective-permute-start(bf16[2,128,256]{2,1,0:T(8,128)(2,1)S(1)} %get-tuple-element.48), channel_id=1, source_target_pairs={{0,16},{1,17},{2,18},{3,19},{4,20},{5,21},{6,22},{7,23},{8,24},{9,... | collective-permute-start | bytes 393224 | tf_op jit(solution)/shard_map/ppermute | solution.py:526
  7.4 6.6 %collective-permute-start.2 = (bf16[2,128,256]{2,1,0:T(8,128)(2,1)S(1)}, bf16[2,128,256]{2,1,0:T(8,128)(2,1)S(1)}, u32[]{:S(2)}, u32[]{:S(2)}) collective-permute-start(bf16[2,128,256]{2,1,0:T(8,128)(2,1)S(1)} %get-tuple-element.49), channel_id=1, source_target_pairs={{0,17},{1,16},{2,19},{3,18},{4,21},{5,20},{6,23},{7,22},{8,25},{9,... | collective-permute-start | bytes 393224 | tf_op jit(solution)/shard_map/ppermute | solution.py:527
  7.5 58.5 %collective-permute-start = (bf16[32,128,256]{2,1,0:T(8,128)(2,1)}, bf16[32,128,256]{2,1,0:T(8,128)(2,1)S(1)}, u32[]{:S(2)}, u32[]{:S(2)}) collective-permute-start(bf16[32,128,256]{2,1,0:T(8,128)(2,1)} %rot_mine.1), channel_id=1, source_target_pairs={{0,1},{1,0},{2,3},{3,2},{4,5},{5,4},{6,7},{7,6},{8,9},{9,8},{10,11... | collective-permute-start | bytes 6291464 | tf_op jit(solution)/shard_map/ppermute | solution.py:40
  7.6 0.8 copy-start.3
  8.5 10.7 %collective-permute-start.12 = (bf16[9,64,256]{2,1,0:T(8,128)(2,1)S(1)}, bf16[9,64,256]{2,1,0:T(8,128)(2,1)S(1)}, u32[]{:S(2)}, u32[]{:S(2)}) collective-permute-start(bf16[9,64,256]{2,1,0:T(8,128)(2,1)S(1)} %shard_map.79.refs_13_), channel_id=1, source_target_pairs={{0,8},{1,9},{2,10},{3,11},{4,0},{5,1},{6,2},{7,3},{8,12},{9,13},{1... | collective-permute-start | bytes 884744 | tf_op jit(solution)/shard_map/ppermute | solution.py:49
  11.6 8.8 %collective-permute-start.11 = (bf16[9,64,256]{2,1,0:T(8,128)(2,1)S(1)}, bf16[9,64,256]{2,1,0:T(8,128)(2,1)S(1)}, u32[]{:S(2)}, u32[]{:S(2)}) collective-permute-start(bf16[9,64,256]{2,1,0:T(8,128)(2,1)S(1)} %shard_map.79.refs_13_), channel_id=1, source_target_pairs={{0,2},{1,3},{2,0},{3,1},{4,6},{5,7},{6,4},{7,5},{8,10},{9,11},{10,... | collective-permute-start | bytes 884744 | tf_op jit(solution)/shard_map/ppermute | solution.py:40
  14.1 0.8 copy-start.4
  14.9 10.0 %collective-permute-start.4 = (bf16[9,64,256]{2,1,0:T(8,128)(2,1)S(1)}, bf16[9,64,256]{2,1,0:T(8,128)(2,1)S(1)}, u32[]{:S(2)}, u32[]{:S(2)}) collective-permute-start(bf16[9,64,256]{2,1,0:T(8,128)(2,1)S(1)} %shard_map.78.refs_4_), channel_id=1, source_target_pairs={{0,8},{1,9},{2,10},{3,11},{4,0},{5,1},{6,2},{7,3},{8,12},{9,13},{1... | collective-permute-start | bytes 884744 | tf_op jit(solution)/shard_map/ppermute | solution.py:49
  17.7 9.8 %collective-permute-start.3 = (bf16[9,64,256]{2,1,0:T(8,128)(2,1)S(1)}, bf16[9,64,256]{2,1,0:T(8,128)(2,1)S(1)}, u32[]{:S(2)}, u32[]{:S(2)}) collective-permute-start(bf16[9,64,256]{2,1,0:T(8,128)(2,1)S(1)} %shard_map.78.refs_4_), channel_id=1, source_target_pairs={{0,2},{1,3},{2,0},{3,1},{4,6},{5,7},{6,4},{7,5},{8,10},{9,11},{10,... | collective-permute-start | bytes 884744 | tf_op jit(solution)/shard_map/ppermute | solution.py:40
  20.4 10.9 %collective-permute-start.14 = (bf16[9,64,256]{2,1,0:T(8,128)(2,1)S(1)}, bf16[9,64,256]{2,1,0:T(8,128)(2,1)S(1)}, u32[]{:S(2)}, u32[]{:S(2)}) collective-permute-start(bf16[9,64,256]{2,1,0:T(8,128)(2,1)S(1)} %collective-permute-done.12.refs_14_), channel_id=1, source_target_pairs={{0,8},{1,9},{2,10},{3,11},{4,0},{5,1},{6,2},{7,3},{8,12},{9,13},{1... | collective-permute-start | bytes 884744 | tf_op jit(solution)/shard_map/ppermute | solution.py:49
  22.0 11.8 %collective-permute-start.13 = (bf16[9,64,256]{2,1,0:T(8,128)(2,1)S(1)}, bf16[9,64,256]{2,1,0:T(8,128)(2,1)S(1)}, u32[]{:S(2)}, u32[]{:S(2)}) collective-permute-start(bf16[9,64,256]{2,1,0:T(8,128)(2,1)S(1)} %collective-permute-done.12.refs_14_), channel_id=1, source_target_pairs={{0,2},{1,3},{2,0},{3,1},{4,6},{5,7},{6,4},{7,5},{8,10},{9,11},{10,... | collective-permute-start | bytes 884744 | tf_op jit(solution)/shard_map/ppermute | solution.py:40
  27.5 10.1 %collective-permute-start.6 = (bf16[9,64,256]{2,1,0:T(8,128)(2,1)S(1)}, bf16[9,64,256]{2,1,0:T(8,128)(2,1)S(1)}, u32[]{:S(2)}, u32[]{:S(2)}) collective-permute-start(bf16[9,64,256]{2,1,0:T(8,128)(2,1)S(1)} %collective-permute-done.4.refs_5_), channel_id=1, source_target_pairs={{0,8},{1,9},{2,10},{3,11},{4,0},{5,1},{6,2},{7,3},{8,12},{9,13},{1... | collective-permute-start | bytes 884744 | tf_op jit(solution)/shard_map/ppermute | solution.py:49
  29.1 11.1 %collective-permute-start.5 = (bf16[9,64,256]{2,1,0:T(8,128)(2,1)S(1)}, bf16[9,64,256]{2,1,0:T(8,128)(2,1)S(1)}, u32[]{:S(2)}, u32[]{:S(2)}) collective-permute-start(bf16[9,64,256]{2,1,0:T(8,128)(2,1)S(1)} %collective-permute-done.4.refs_5_), channel_id=1, source_target_pairs={{0,2},{1,3},{2,0},{3,1},{4,6},{5,7},{6,4},{7,5},{8,10},{9,11},{10,... | collective-permute-start | bytes 884744 | tf_op jit(solution)/shard_map/ppermute | solution.py:40
  33.8 10.1 %collective-permute-start.16 = (bf16[9,64,256]{2,1,0:T(8,128)(2,1)S(1)}, bf16[9,64,256]{2,1,0:T(8,128)(2,1)S(1)}, u32[]{:S(2)}, u32[]{:S(2)}) collective-permute-start(bf16[9,64,256]{2,1,0:T(8,128)(2,1)S(1)} %collective-permute-done.14.refs_15_), channel_id=1, source_target_pairs={{0,8},{1,9},{2,10},{3,11},{4,0},{5,1},{6,2},{7,3},{8,12},{9,13},{1... | collective-permute-start | bytes 884744 | tf_op jit(solution)/shard_map/ppermute | solution.py:49
  35.4 11.1 %collective-permute-start.15 = (bf16[9,64,256]{2,1,0:T(8,128)(2,1)S(1)}, bf16[9,64,256]{2,1,0:T(8,128)(2,1)S(1)}, u32[]{:S(2)}, u32[]{:S(2)}) collective-permute-start(bf16[9,64,256]{2,1,0:T(8,128)(2,1)S(1)} %collective-permute-done.14.refs_15_), channel_id=1, source_target_pairs={{0,2},{1,3},{2,0},{3,1},{4,6},{5,7},{6,4},{7,5},{8,10},{9,11},{10,... | collective-permute-start | bytes 884744 | tf_op jit(solution)/shard_map/ppermute | solution.py:40
  40.1 10.1 %collective-permute-start.8 = (bf16[9,64,256]{2,1,0:T(8,128)(2,1)S(1)}, bf16[9,64,256]{2,1,0:T(8,128)(2,1)S(1)}, u32[]{:S(2)}, u32[]{:S(2)}) collective-permute-start(bf16[9,64,256]{2,1,0:T(8,128)(2,1)S(1)} %collective-permute-done.6.refs_6_), channel_id=1, source_target_pairs={{0,8},{1,9},{2,10},{3,11},{4,0},{5,1},{6,2},{7,3},{8,12},{9,13},{1... | collective-permute-start | bytes 884744 | tf_op jit(solution)/shard_map/ppermute | solution.py:49
  41.7 11.1 %collective-permute-start.7 = (bf16[9,64,256]{2,1,0:T(8,128)(2,1)S(1)}, bf16[9,64,256]{2,1,0:T(8,128)(2,1)S(1)}, u32[]{:S(2)}, u32[]{:S(2)}) collective-permute-start(bf16[9,64,256]{2,1,0:T(8,128)(2,1)S(1)} %collective-permute-done.6.refs_6_), channel_id=1, source_target_pairs={{0,2},{1,3},{2,0},{3,1},{4,6},{5,7},{6,4},{7,5},{8,10},{9,11},{10,... | collective-permute-start | bytes 884744 | tf_op jit(solution)/shard_map/ppermute | solution.py:40
  46.5 6.4 %collective-permute-start.19 = (bf16[4,64,256]{2,1,0:T(8,128)(2,1)S(1)}, bf16[4,64,256]{2,1,0:T(8,128)(2,1)S(1)}, u32[]{:S(2)}, u32[]{:S(2)}) collective-permute-start(bf16[4,64,256]{2,1,0:T(8,128)(2,1)S(1)} %slice.87), channel_id=1, source_target_pairs={{0,8},{1,9},{2,10},{3,11},{4,0},{5,1},{6,2},{7,3},{8,12},{9,13},{1... | collective-permute-start | bytes 393224 | tf_op jit(solution)/shard_map/ppermute | solution.py:49
  48.1 7.5 %collective-permute-start.18 = (bf16[5,64,256]{2,1,0:T(8,128)(2,1)S(1)}, bf16[5,64,256]{2,1,0:T(8,128)(2,1)S(1)}, u32[]{:S(2)}, u32[]{:S(2)}) collective-permute-start(bf16[5,64,256]{2,1,0:T(8,128)(2,1)S(1)} %slice.86), channel_id=1, source_target_pairs={{0,2},{1,3},{2,0},{3,1},{4,6},{5,7},{6,4},{7,5},{8,10},{9,11},{10,... | collective-permute-start | bytes 491528 | tf_op jit(solution)/shard_map/ppermute | solution.py:40
  50.2 7.5 %collective-permute-start.17 = (bf16[7,64,256]{2,1,0:T(8,128)(2,1)S(1)}, bf16[7,64,256]{2,1,0:T(8,128)(2,1)S(1)}, u32[]{:S(2)}, u32[]{:S(2)}) collective-permute-start(bf16[7,64,256]{2,1,0:T(8,128)(2,1)S(1)} %slice_dynamic-update-slice_fusion.2), channel_id=1, source_target_pairs={{0,1},{1,0},{2,3},{3,2},{4,5},{5,4},{6,7},{7,6},{8,9},{9,8},{10,11... | collective-permute-start | bytes 688136 | tf_op jit(solution)/shard_map/ppermute | solution.py:40
  52.8 6.0 %collective-permute-start.9 = (bf16[7,64,256]{2,1,0:T(8,128)(2,1)S(1)}, bf16[7,64,256]{2,1,0:T(8,128)(2,1)S(1)}, u32[]{:S(2)}, u32[]{:S(2)}) collective-permute-start(bf16[7,64,256]{2,1,0:T(8,128)(2,1)S(1)} %slice_dynamic-update-slice_fusion.8), channel_id=1, source_target_pairs={{0,1},{1,0},{2,3},{3,2},{4,5},{5,4},{6,7},{7,6},{8,9},{9,8},{10,11... | collective-permute-start | bytes 688136 | tf_op jit(solution)/shard_map/ppermute | solution.py:40
  52.9 7.7 %collective-permute-start.22 = (bf16[5,64,256]{2,1,0:T(8,128)(2,1)S(1)}, bf16[5,64,256]{2,1,0:T(8,128)(2,1)S(1)}, u32[]{:S(2)}, u32[]{:S(2)}) collective-permute-start(bf16[5,64,256]{2,1,0:T(8,128)(2,1)S(1)} %slice.90), channel_id=1, source_target_pairs={{0,2},{1,3},{2,0},{3,1},{4,6},{5,7},{6,4},{7,5},{8,10},{9,11},{10,... | collective-permute-start | bytes 491528 | tf_op jit(solution)/shard_map/ppermute | solution.py:40
  55.6 5.0 %collective-permute-start.23 = (bf16[4,64,256]{2,1,0:T(8,128)(2,1)S(1)}, bf16[4,64,256]{2,1,0:T(8,128)(2,1)S(1)}, u32[]{:S(2)}, u32[]{:S(2)}) collective-permute-start(bf16[4,64,256]{2,1,0:T(8,128)(2,1)S(1)} %slice.91), channel_id=1, source_target_pairs={{0,8},{1,9},{2,10},{3,11},{4,0},{5,1},{6,2},{7,3},{8,12},{9,13},{1... | collective-permute-start | bytes 393224 | tf_op jit(solution)/shard_map/ppermute | solution.py:49
  57.7 3.9 %collective-permute-start.21 = (bf16[1,64,256]{2,1,0:T(8,128)(2,1)S(1)}, bf16[1,64,256]{2,1,0:T(8,128)(2,1)S(1)}, u32[]{:S(2)}, u32[]{:S(2)}) collective-permute-start(bf16[1,64,256]{2,1,0:T(8,128)(2,1)S(1)} %slice.89), channel_id=1, source_target_pairs={{0,2},{1,3},{2,0},{3,1},{4,6},{5,7},{6,4},{7,5},{8,10},{9,11},{10,... | collective-permute-start | bytes 98312 | tf_op jit(solution)/shard_map/ppermute | solution.py:40
  58.8 7.3 %copy-start.1 = (bf16[32,128,256]{2,1,0:T(8,128)(2,1)S(1)}, bf16[32,128,256]{2,1,0:T(8,128)(2,1)}, u32[]{:S(2)}) copy-start(bf16[32,128,256]{2,1,0:T(8,128)(2,1)} %rot_mine.1) | copy-start | bytes 6291460
  58.8 4.0 %collective-permute-start.20 = (bf16[1,64,256]{2,1,0:T(8,128)(2,1)S(1)}, bf16[1,64,256]{2,1,0:T(8,128)(2,1)S(1)}, u32[]{:S(2)}, u32[]{:S(2)}) collective-permute-start(bf16[1,64,256]{2,1,0:T(8,128)(2,1)S(1)} %slice.98), channel_id=1, source_target_pairs={{0,2},{1,3},{2,0},{3,1},{4,6},{5,7},{6,4},{7,5},{8,10},{9,11},{10,... | collective-permute-start | bytes 98312 | tf_op jit(solution)/shard_map/ppermute | solution.py:40
  62.7 14.9 %copy-start = (bf16[32,128,2048]{2,1,0:T(8,128)(2,1)S(1)}, bf16[32,128,2048]{2,1,0:T(8,128)(2,1)}, u32[]{:S(2)}) copy-start(bf16[32,128,2048]{2,1,0:T(8,128)(2,1)} %cholesky.1) | copy-start | bytes 50331652
  66.1 11.6 %copy-start.5 = (f32[8,32]{1,0:T(8,128)S(1)}, f32[8,32]{1,0:T(8,128)}, u32[]{:S(2)}) copy-start(f32[8,32]{1,0:T(8,128)} %fields.1) | copy-start | bytes 3076
  80.9 2.7 %collective-permute-start.24 = (bf16[4,64,2048]{2,1,0:T(8,128)(2,1)S(1)}, bf16[4,64,2048]{2,1,0:T(8,128)(2,1)S(1)}, u32[]{:S(2)}, u32[]{:S(2)}) collective-permute-start(bf16[4,64,2048]{2,1,0:T(8,128)(2,1)S(1)} %get-tuple-element.72), channel_id=1, source_target_pairs={{0,1},{1,0},{2,3},{3,2},{4,5},{5,4},{6,7},{7,6},{8,9},{9,8},{10,11... | collective-permute-start | bytes 3145736 | tf_op jit(solution)/shard_map/ppermute | solution.py:40
  80.9 4.1 %collective-permute-start.25 = (bf16[4,64,2048]{2,1,0:T(8,128)(2,1)S(1)}, bf16[4,64,2048]{2,1,0:T(8,128)(2,1)S(1)}, u32[]{:S(2)}, u32[]{:S(2)}) collective-permute-start(bf16[4,64,2048]{2,1,0:T(8,128)(2,1)S(1)} %get-tuple-element.73), channel_id=1, source_target_pairs={{0,1},{1,0},{2,3},{3,2},{4,5},{5,4},{6,7},{7,6},{8,9},{9,8},{10,11... | collective-permute-start | bytes 3145736 | tf_op jit(solution)/shard_map/ppermute | solution.py:40
  82.3 9.2 %collective-permute-start.27 = (bf16[4,128,256]{2,1,0:T(8,128)(2,1)S(1)}, bf16[4,128,256]{2,1,0:T(8,128)(2,1)S(1)}, u32[]{:S(2)}, u32[]{:S(2)}) collective-permute-start(bf16[4,128,256]{2,1,0:T(8,128)(2,1)S(1)} %get-tuple-element.75.refs_3_), channel_id=1, source_target_pairs={{0,8},{1,9},{2,10},{3,11},{4,0},{5,1},{6,2},{7,3},{8,12},{9,13},{1... | collective-permute-start | bytes 786440 | tf_op jit(solution)/shard_map/ppermute | solution.py:49
  82.5 9.2 %collective-permute-start.26 = (bf16[4,128,256]{2,1,0:T(8,128)(2,1)S(1)}, bf16[4,128,256]{2,1,0:T(8,128)(2,1)S(1)}, u32[]{:S(2)}, u32[]{:S(2)}) collective-permute-start(bf16[4,128,256]{2,1,0:T(8,128)(2,1)S(1)} %get-tuple-element.75.refs_3_), channel_id=1, source_target_pairs={{0,2},{1,3},{2,0},{3,1},{4,6},{5,7},{6,4},{7,5},{8,10},{9,11},{10,... | collective-permute-start | bytes 786440 | tf_op jit(solution)/shard_map/ppermute | solution.py:40
  85.9 11.2 %collective-permute-start.35 = (bf16[4,128,256]{2,1,0:T(8,128)(2,1)S(1)}, bf16[4,128,256]{2,1,0:T(8,128)(2,1)S(1)}, u32[]{:S(2)}, u32[]{:S(2)}) collective-permute-start(bf16[4,128,256]{2,1,0:T(8,128)(2,1)S(1)} %get-tuple-element.82.refs_12_), channel_id=1, source_target_pairs={{0,8},{1,9},{2,10},{3,11},{4,0},{5,1},{6,2},{7,3},{8,12},{9,13},{1... | collective-permute-start | bytes 786440 | tf_op jit(solution)/shard_map/ppermute | solution.py:49
  86.2 11.1 %collective-permute-start.34 = (bf16[4,128,256]{2,1,0:T(8,128)(2,1)S(1)}, bf16[4,128,256]{2,1,0:T(8,128)(2,1)S(1)}, u32[]{:S(2)}, u32[]{:S(2)}) collective-permute-start(bf16[4,128,256]{2,1,0:T(8,128)(2,1)S(1)} %get-tuple-element.82.refs_12_), channel_id=1, source_target_pairs={{0,2},{1,3},{2,0},{3,1},{4,6},{5,7},{6,4},{7,5},{8,10},{9,11},{10,... | collective-permute-start | bytes 786440 | tf_op jit(solution)/shard_map/ppermute | solution.py:40
  91.7 11.0 %collective-permute-start.29 = (bf16[4,128,256]{2,1,0:T(8,128)(2,1)S(1)}, bf16[4,128,256]{2,1,0:T(8,128)(2,1)S(1)}, u32[]{:S(2)}, u32[]{:S(2)}) collective-permute-start(bf16[4,128,256]{2,1,0:T(8,128)(2,1)S(1)} %collective-permute-done.27.refs_4_), channel_id=1, source_target_pairs={{0,8},{1,9},{2,10},{3,11},{4,0},{5,1},{6,2},{7,3},{8,12},{9,13},{1... | collective-permute-start | bytes 786440 | tf_op jit(solution)/shard_map/ppermute | solution.py:49
  92.6 10.3 %collective-permute-start.28 = (bf16[4,128,256]{2,1,0:T(8,128)(2,1)S(1)}, bf16[4,128,256]{2,1,0:T(8,128)(2,1)S(1)}, u32[]{:S(2)}, u32[]{:S(2)}) collective-permute-start(bf16[4,128,256]{2,1,0:T(8,128)(2,1)S(1)} %collective-permute-done.27.refs_4_), channel_id=1, source_target_pairs={{0,2},{1,3},{2,0},{3,1},{4,6},{5,7},{6,4},{7,5},{8,10},{9,11},{10,... | collective-permute-start | bytes 786440 | tf_op jit(solution)/shard_map/ppermute | solution.py:40
  97.3 11.0 %collective-permute-start.37 = (bf16[4,128,256]{2,1,0:T(8,128)(2,1)S(1)}, bf16[4,128,256]{2,1,0:T(8,128)(2,1)S(1)}, u32[]{:S(2)}, u32[]{:S(2)}) collective-permute-start(bf16[4,128,256]{2,1,0:T(8,128)(2,1)S(1)} %collective-permute-done.35.refs_13_), channel_id=1, source_target_pairs={{0,8},{1,9},{2,10},{3,11},{4,0},{5,1},{6,2},{7,3},{8,12},{9,13},{1... | collective-permute-start | bytes 786440 | tf_op jit(solution)/shard_map/ppermute | solution.py:49
  98.2 10.3 %collective-permute-start.36 = (bf16[4,128,256]{2,1,0:T(8,128)(2,1)S(1)}, bf16[4,128,256]{2,1,0:T(8,128)(2,1)S(1)}, u32[]{:S(2)}, u32[]{:S(2)}) collective-permute-start(bf16[4,128,256]{2,1,0:T(8,128)(2,1)S(1)} %collective-permute-done.35.refs_13_), channel_id=1, source_target_pairs={{0,2},{1,3},{2,0},{3,1},{4,6},{5,7},{6,4},{7,5},{8,10},{9,11},{10,... | collective-permute-start | bytes 786440 | tf_op jit(solution)/shard_map/ppermute | solution.py:40
  102.9 11.0 %collective-permute-start.31 = (bf16[4,128,256]{2,1,0:T(8,128)(2,1)S(1)}, bf16[4,128,256]{2,1,0:T(8,128)(2,1)S(1)}, u32[]{:S(2)}, u32[]{:S(2)}) collective-permute-start(bf16[4,128,256]{2,1,0:T(8,128)(2,1)S(1)} %collective-permute-done.29.refs_5_), channel_id=1, source_target_pairs={{0,8},{1,9},{2,10},{3,11},{4,0},{5,1},{6,2},{7,3},{8,12},{9,13},{1... | collective-permute-start | bytes 786440 | tf_op jit(solution)/shard_map/ppermute | solution.py:49
  103.9 10.3 %collective-permute-start.30 = (bf16[4,128,256]{2,1,0:T(8,128)(2,1)S(1)}, bf16[4,128,256]{2,1,0:T(8,128)(2,1)S(1)}, u32[]{:S(2)}, u32[]{:S(2)}) collective-permute-start(bf16[4,128,256]{2,1,0:T(8,128)(2,1)S(1)} %collective-permute-done.29.refs_5_), channel_id=1, source_target_pairs={{0,2},{1,3},{2,0},{3,1},{4,6},{5,7},{6,4},{7,5},{8,10},{9,11},{10,... | collective-permute-start | bytes 786440 | tf_op jit(solution)/shard_map/ppermute | solution.py:40
  108.6 11.0 %collective-permute-start.39 = (bf16[4,128,256]{2,1,0:T(8,128)(2,1)S(1)}, bf16[4,128,256]{2,1,0:T(8,128)(2,1)S(1)}, u32[]{:S(2)}, u32[]{:S(2)}) collective-permute-start(bf16[4,128,256]{2,1,0:T(8,128)(2,1)S(1)} %collective-permute-done.37.refs_14_), channel_id=1, source_target_pairs={{0,8},{1,9},{2,10},{3,11},{4,0},{5,1},{6,2},{7,3},{8,12},{9,13},{1... | collective-permute-start | bytes 786440 | tf_op jit(solution)/shard_map/ppermute | solution.py:49
  109.5 10.3 %collective-permute-start.38 = (bf16[4,128,256]{2,1,0:T(8,128)(2,1)S(1)}, bf16[4,128,256]{2,1,0:T(8,128)(2,1)S(1)}, u32[]{:S(2)}, u32[]{:S(2)}) collective-permute-start(bf16[4,128,256]{2,1,0:T(8,128)(2,1)S(1)} %collective-permute-done.37.refs_14_), channel_id=1, source_target_pairs={{0,2},{1,3},{2,0},{3,1},{4,6},{5,7},{6,4},{7,5},{8,10},{9,11},{10,... | collective-permute-start | bytes 786440 | tf_op jit(solution)/shard_map/ppermute | solution.py:40
  114.2 8.2 %collective-permute-start.33 = (bf16[2,128,256]{2,1,0:T(8,128)(2,1)S(1)}, bf16[2,128,256]{2,1,0:T(8,128)(2,1)S(1)}, u32[]{:S(2)}, u32[]{:S(2)}) collective-permute-start(bf16[2,128,256]{2,1,0:T(8,128)(2,1)S(1)} %slice.93), channel_id=1, source_target_pairs={{0,8},{1,9},{2,10},{3,11},{4,0},{5,1},{6,2},{7,3},{8,12},{9,13},{1... | collective-permute-start | bytes 393224 | tf_op jit(solution)/shard_map/ppermute | solution.py:49
  115.2 7.2 %collective-permute-start.32 = (bf16[2,128,256]{2,1,0:T(8,128)(2,1)S(1)}, bf16[2,128,256]{2,1,0:T(8,128)(2,1)S(1)}, u32[]{:S(2)}, u32[]{:S(2)}) collective-permute-start(bf16[2,128,256]{2,1,0:T(8,128)(2,1)S(1)} %slice.92), channel_id=1, source_target_pairs={{0,2},{1,3},{2,0},{3,1},{4,6},{5,7},{6,4},{7,5},{8,10},{9,11},{10,... | collective-permute-start | bytes 393224 | tf_op jit(solution)/shard_map/ppermute | solution.py:40
  119.8 5.0 %collective-permute-start.41 = (bf16[2,128,256]{2,1,0:T(8,128)(2,1)S(1)}, bf16[2,128,256]{2,1,0:T(8,128)(2,1)S(1)}, u32[]{:S(2)}, u32[]{:S(2)}) collective-permute-start(bf16[2,128,256]{2,1,0:T(8,128)(2,1)S(1)} %slice.95), channel_id=1, source_target_pairs={{0,8},{1,9},{2,10},{3,11},{4,0},{5,1},{6,2},{7,3},{8,12},{9,13},{1... | collective-permute-start | bytes 393224 | tf_op jit(solution)/shard_map/ppermute | solution.py:49
  120.8 5.0 %collective-permute-start.40 = (bf16[2,128,256]{2,1,0:T(8,128)(2,1)S(1)}, bf16[2,128,256]{2,1,0:T(8,128)(2,1)S(1)}, u32[]{:S(2)}, u32[]{:S(2)}) collective-permute-start(bf16[2,128,256]{2,1,0:T(8,128)(2,1)S(1)} %slice.94), channel_id=1, source_target_pairs={{0,2},{1,3},{2,0},{3,1},{4,6},{5,7},{6,4},{7,5},{8,10},{9,11},{10,... | collective-permute-start | bytes 393224 | tf_op jit(solution)/shard_map/ppermute | solution.py:40
  126.8 1.6 %collective-permute-start.42 = (bf16[4,128,256]{2,1,0:T(8,128)(2,1)S(1)}, bf16[4,128,256]{2,1,0:T(8,128)(2,1)S(1)}, u32[]{:S(2)}, u32[]{:S(2)}) collective-permute-start(bf16[4,128,256]{2,1,0:T(8,128)(2,1)S(1)} %get-tuple-element.90), channel_id=1, source_target_pairs={{0,1},{1,0},{2,3},{3,2},{4,5},{5,4},{6,7},{7,6},{8,9},{9,8},{10,11... | collective-permute-start | bytes 786440 | tf_op jit(solution)/shard_map/ppermute | solution.py:40
